TPU v7x, 32 devices: a whole 2x2x4 slice. The times are simulated.
32 devices in a mesh: dp: 2 (over y), ctx: 4 (over z), head: 4 (over x, core).
Axes of the slice: x: 2, y: 2, z: 4, core: 2. Of those that a mesh axis runs over, the one named last changes fastest.
Arguments:
- queries: bfloat16 [2, 1024, 8192], P('dp', 'ctx', 'head'), may hold values from -45 to 45
- keys: bfloat16 [2, 1024, 1024], P('dp', 'ctx', 'head'), may hold values from -6 to 6
- values: bfloat16 [2, 1024, 1024], P('dp', 'ctx', 'head'), may hold values from -6 to 6
- doc_ids: int32 [2, 1024], P('dp'), may hold values from 0 to 2, never falling along the last dimension, each value on 1 to 768 neighbouring positions
- inputs: bfloat16 [2, 1024, 8192], P('dp', 'ctx', 'head'), may hold values from -6 to 6
- gate_input: bfloat16 [2, 1024, 8192], P('dp', 'ctx', 'head'), may hold values from -40 to 40
- b_input: bfloat16 [2, 1024, 1024], P('dp', 'ctx', 'head'), may hold values from -0.0625 to 0.0625
- c_input: bfloat16 [2, 1024, 1024], P('dp', 'ctx', 'head'), may hold values from -6 to 6
- dt_raw: float32 [2, 1024, 128], P('dp', 'ctx', 'head'), may hold values from -2 to 2
- dt_bias: float32 [128], P('head'), may hold values from -1 to 1
- decay_log: float32 [128], P('head'), may hold values from -12 to -2
- skip: float32 [128], P('head'), may hold values from 0.5 to 2
- gain: float32 [8192], P('head'), may hold values from 0.5 to 1.5
Outputs:
- teacher_out: bfloat16 [2, 1024, 8192], P('dp', 'ctx', 'head')
- student_out: bfloat16 [2, 1024, 8192], P('dp', 'ctx', 'head')
- grad_gain: float32 [8192], P('head')
- grad_skip: float32 [128], P('head')
Inputs may be any that keep to these rules, and one draw needn't show every extreme that they name: `doc_ids`: three or fewer documents a sequence, numbered from 0 in order; one of them has 768 positions.
All inputs are finite; a program needn't handle non-finite values.
Results may differ from a plain program's by a relative error of at most 0.012.
Values may be sent and summed in bfloat16 or wider, within the bound.
No kernel may reach another device: no remote copies, remote signals or barrier semaphores. Data moves between devices by JAX's collectives and lax.ppermute only.
A program may use at most 64 MiB of HBM per device.

v0:
```python
import jax
import jax.numpy as jnp
from jax import lax
from jax.sharding import PartitionSpec as P

DH = 128
P_SIZE = 64
N = 128


def prefix(array, axis, combine, identity):
    size, mine = (lax.axis_size(axis), lax.axis_index(axis))
    everything = jax.tree.map(
        lambda part, kind: lax.all_gather(part.astype(kind), axis),
        array,
        (jnp.bfloat16, jnp.bfloat16),
    )
    start = jax.tree.map(
        lambda part, zero: jnp.broadcast_to(jnp.asarray(zero, part.dtype), part.shape),
        array,
        identity,
    )

    def prefix_lap(k, before):
        reached = k < mine
        new = combine(
            before, jax.tree.map(lambda part, own: part[k].astype(own.dtype), everything, array)
        )
        return jax.tree.map(lambda a, b: jnp.where(reached, a, b), new, before)

    return lax.fori_loop(0, size, prefix_lap, start)


def entering(array, axis, combine, identity):
    size, mine = (lax.axis_size(axis), lax.axis_index(axis))
    everything = jax.tree.map(
        lambda part, kind: lax.all_gather(part.astype(kind), axis),
        array,
        jax.tree.map(lambda a: jnp.bfloat16 if a.dtype == jnp.float32 else a.dtype, array),
    )
    start = jax.tree.map(
        lambda part, zero: jnp.broadcast_to(jnp.asarray(zero, part.dtype), part.shape),
        array,
        identity,
    )

    def entering_lap(k, before):
        at = size - 1 - k
        reached = at > mine
        new = combine(
            before, jax.tree.map(lambda part, own: part[at].astype(own.dtype), everything, array)
        )
        return jax.tree.map(lambda a, b: jnp.where(reached, a, b), new, before)

    return lax.fori_loop(0, size, entering_lap, start)


def stored_position(rows, count, stretch, tok_dev):
    device = rows // tok_dev
    offset = rows % tok_dev
    block = jnp.where(offset < stretch, device, 2 * count - 1 - device)
    return block * stretch + offset % stretch


def block_terms(xs, bmat, cmat, dt, rate, docs, prior):
    rows, heads, width = xs.shape
    groups, state = (bmat.shape[1], bmat.shape[2])
    per = heads // groups
    cum = jnp.cumsum(rate, axis=0)
    order = jnp.arange(rows, dtype=jnp.int32)
    allowed = (order[:, None] >= order[None, :]) & (docs[:, None] == docs[None, :])
    gram = jnp.einsum("tgn,sgn->gts", cmat, bmat, preferred_element_type=jnp.float32)
    spans = cum.T[:, :, None] - cum.T[:, None, :]
    fading = jnp.exp(jnp.where(allowed[None], spans, -jnp.inf))
    mixing = (
        fading.reshape(groups, per, rows, rows) * gram[:, None] * dt.T.reshape(groups, per, 1, rows)
    ).astype(jnp.bfloat16)
    grouped = xs.reshape(rows, groups, per, width)
    intra = jnp.einsum(
        "gjts,sgjp->tgjp", mixing, grouped, preferred_element_type=jnp.float32
    ).reshape(rows, heads, width)
    final = cum[-1]
    decay = jnp.where(docs[-1] == prior, jnp.exp(final), 0.0)
    tail = jnp.exp(final[None, :] - cum) * dt * (docs == docs[-1]).astype(jnp.float32)[:, None]
    loaded = (
        tail.reshape(rows, groups, per)[..., None] * bmat[:, :, None, :].astype(jnp.float32)
    ).astype(jnp.bfloat16)
    summary = jnp.einsum(
        "sgjp,sgjn->gjpn", grouped, loaded, preferred_element_type=jnp.float32
    ).reshape(heads, width, state)
    reach = jnp.exp(cum) * (docs == prior).astype(jnp.float32)[:, None]
    return (intra, decay, summary, reach)


def inflow(cmat, state, reach):
    rows, groups, width_n = cmat.shape
    heads = state.shape[0]
    per = heads // groups
    grouped = state.reshape(groups, per, state.shape[1], width_n)
    flow = jnp.einsum(
        "tgn,gjpn->tgjp", cmat.astype(jnp.float32), grouped, precision=lax.Precision.HIGHEST
    )
    return flow.reshape(rows, heads, state.shape[1]) * reach[:, :, None]


def combine(earlier, later):
    return (earlier[0] * later[0], later[0][:, None, None] * earlier[1] + later[1])


def gated_norm(mixed, xs, gate, skip, gain, groups):
    rows, heads, width = mixed.shape
    values_out = mixed + skip[None, :, None] * xs.astype(jnp.float32)
    gated = values_out.reshape(rows, heads * width) * jax.nn.silu(gate.astype(jnp.float32))
    gated = gated.reshape(rows, groups, -1)
    normed = gated * lax.rsqrt(jnp.mean(gated * gated, axis=2, keepdims=True) + 1e-05)
    return normed.reshape(rows, heads * width) * gain


def body(
    queries,
    keys,
    values,
    doc_ids,
    inputs,
    gate_input,
    b_input,
    c_input,
    dt_raw,
    dt_bias,
    decay_log,
    skip,
    gain,
):
    count = lax.axis_size("ctx")
    index = lax.axis_index("ctx")
    tok_dev = queries.shape[1]
    stretch = tok_dev // 2
    kv_dev = keys.shape[2] // DH
    per_kv = queries.shape[2] // keys.shape[2]
    docs = doc_ids[0]
    local_rows = index * tok_dev + jnp.arange(tok_dev, dtype=jnp.int32)
    local_pos = stored_position(local_rows, count, stretch, tok_dev)
    local_docs = jnp.take(docs, local_pos)
    query_block = queries[0].reshape(tok_dev, kv_dev, per_kv, DH)
    scale = 1.0 / jnp.sqrt(jnp.float32(DH))
    start_state = (
        jnp.full((tok_dev, kv_dev, per_kv), -1e30, jnp.float32),
        jnp.zeros((tok_dev, kv_dev, per_kv), jnp.float32),
        jnp.zeros((tok_dev, kv_dev, per_kv, DH), jnp.float32),
    )
    carry = start_state
    key_piece = lax.all_gather(keys, "ctx", axis=1, tiled=True)
    value_piece = lax.all_gather(values, "ctx", axis=1, tiled=True)
    size = key_piece.shape[1]
    span = 512
    key_tiles = key_piece[0].reshape(size // span, span, kv_dev, DH)
    value_tiles = value_piece[0].reshape(size // span, span, kv_dev, DH)
    key_pos = stored_position(jnp.arange(size, dtype=jnp.int32), count, stretch, tok_dev)
    key_docs = jnp.take(docs, key_pos).reshape(size // span, span)
    key_pos = key_pos.reshape(size // span, span)

    def inner(state, items):
        top, total, summed = state
        key_now, value_now, pos_now, doc_now = items
        scores = (
            jnp.einsum("tkgd,skd->tkgs", query_block, key_now, preferred_element_type=jnp.float32)
            * scale
        )
        allowed = (
            (local_pos[:, None] >= pos_now[None, :]) & (local_docs[:, None] == doc_now[None, :])
        )[:, None, None, :]
        new_top = jnp.maximum(top, jnp.max(jnp.where(allowed, scores, -1e30), axis=3))
        weights = jnp.where(allowed, jnp.exp(scores - new_top[..., None]), 0.0)
        factor = jnp.exp(top - new_top)
        total = total * factor + jnp.sum(weights, axis=3)
        summed = summed * factor[..., None] + jnp.einsum(
            "tkgs,skd->tkgd",
            weights.astype(jnp.bfloat16),
            value_now,
            preferred_element_type=jnp.float32,
        )
        return ((new_top, total, summed), None)

    carry, _ = lax.scan(inner, carry, (key_tiles, value_tiles, key_pos, key_docs))
    top, total, summed = carry
    teacher = (
        (summed / total[..., None]).reshape(1, tok_dev, kv_dev * per_kv * DH).astype(jnp.bfloat16)
    )
    heads = inputs.shape[2] // P_SIZE
    groups = b_input.shape[2] // N
    dt = jax.nn.softplus(dt_raw[0] + dt_bias)
    rate = -dt * jnp.exp(decay_log)
    xs = inputs[0].reshape(tok_dev, heads, P_SIZE)
    bmat = b_input[0].reshape(tok_dev, groups, N)
    cmat = c_input[0].reshape(tok_dev, groups, N)

    def prior_doc(first):
        return jnp.where(first > 0, jnp.take(docs, jnp.maximum(first - 1, 0)), -1)

    front_first = index * stretch
    back_first = (2 * count - 1 - index) * stretch
    intra_f, decay_f, summ_f, reach_f = block_terms(
        xs[:stretch],
        bmat[:stretch],
        cmat[:stretch],
        dt[:stretch],
        rate[:stretch],
        local_docs[:stretch],
        prior_doc(front_first),
    )
    intra_b, decay_b, summ_b, reach_b = block_terms(
        xs[stretch:],
        bmat[stretch:],
        cmat[stretch:],
        dt[stretch:],
        rate[stretch:],
        local_docs[stretch:],
        prior_doc(back_first),
    )
    identity = (jnp.ones_like(decay_f), jnp.zeros_like(summ_f))
    before_front = prefix((decay_f, summ_f), "ctx", combine, identity)
    through_front = combine(before_front, (decay_f, summ_f))
    last = count - 1
    is_last = index == last
    joined = combine(through_front, (decay_b, summ_b))
    sent = (jnp.where(is_last, joined[0], decay_b), jnp.where(is_last, joined[1], summ_b))
    after = entering(sent, "ctx", combine, identity)
    back_state = jnp.where(is_last, through_front[1], after[1])
    mixed_front = intra_f + inflow(cmat[:stretch], before_front[1], reach_f)
    mixed_back = intra_b + inflow(cmat[stretch:], back_state, reach_b)
    mixed = jnp.concatenate([mixed_front, mixed_back], axis=0)
    target = teacher[0].astype(jnp.float32)
    loss_scale = 1.0 / (lax.axis_size("dp") * count * tok_dev)

    def local_loss(gain_part, skip_part):
        normed = gated_norm(mixed, xs, gate_input[0], skip_part, gain_part, groups)
        diff = normed - target
        return (jnp.sum(diff * diff) * loss_scale, normed)

    (grad_gain, grad_skip), normed = jax.grad(local_loss, argnums=(0, 1), has_aux=True)(gain, skip)
    summed_grads = lax.psum((grad_gain, grad_skip), ("dp", "ctx"))
    student = normed.astype(jnp.bfloat16).reshape(1, tok_dev, heads * P_SIZE)
    return (teacher, student, summed_grads[0], summed_grads[1])


def solution(mesh):
    in_specs = (
        P("dp", "ctx", "head"),
        P("dp", "ctx", "head"),
        P("dp", "ctx", "head"),
        P("dp", None),
        P("dp", "ctx", "head"),
        P("dp", "ctx", "head"),
        P("dp", "ctx", "head"),
        P("dp", "ctx", "head"),
        P("dp", "ctx", "head"),
        P("head"),
        P("head"),
        P("head"),
        P("head"),
    )
    out_specs = (P("dp", "ctx", "head"), P("dp", "ctx", "head"), P("head"), P("head"))
    return jax.shard_map(body, mesh=mesh, in_specs=in_specs, out_specs=out_specs, check_vma=False)
```

profile of v0, /device:TPU:0, one launch (start us, length us, event | category | flops | bytes accessed | tf_op | source)
XLA Modules:
  0.0 227.4 jit_solution(11168301138857354643)
XLA Ops:
  7.3 1.3 constant_dynamic-slice_fusion.4
  8.6 2.0 gather_fusion
  10.6 2.1 fusion.75
  17.1 1.4 compare_convert_fusion.2
  19.3 1.6 bitcast_convert_fusion.2
  21.9 4.5 %gather_fusion.1 = s32[1024]{0:T(1024)S(1)} fusion(s32[1024]{0:T(1024)S(1)} %bitcast.225, s32[1024]{0:T(1024)S(1)} %broadcast_clamp_fusion), kind=kCustom, calls=%fused_computation.1 | custom fusion | bytes 12288 | tf_op jit(solution)/shard_map/jit(_take)/gather | solution.py:159
  26.4 24.0 %all_gather.26 = bf16[1,1024,256]{2,1,0:T(8,128)(2,1)S(1)} all-gather(bf16[1,256,256]{2,1,0:T(8,128)(2,1)S(1)} %copy-done.10), channel_id=1, replica_groups=mesh['dp'=2,'ctx'=4,'head'=4] {'ctx'}, dimensions={1}, use_global_device_ids=true | all-gather | bytes 655360 | tf_op jit(solution)/shard_map/all_gather | solution.py:152
  51.3 2.3 copy.128
  53.5 1.6 copy.130
  55.2 23.2 %all_gather.27 = bf16[1,1024,256]{2,1,0:T(8,128)(2,1)} all-gather(bf16[1,256,256]{2,1,0:T(8,128)(2,1)} %param.21), channel_id=1, replica_groups=mesh['dp'=2,'ctx'=4,'head'=4] {'ctx'}, dimensions={1}, use_global_device_ids=true | all-gather | bytes 655360 | tf_op jit(solution)/shard_map/all_gather | solution.py:153
  78.4 2.0 reshape_squeeze.14
  80.3 2.1 copy.150
  83.3 10.4 %all-gather.2 = bf16[4,1,32]{2,1,0:T(2,128)(2,1)S(1)} all-gather(bf16[1,1,32]{2,1,0:T(2,128)(2,1)S(1)} %get-tuple-element.550), channel_id=1, replica_groups=mesh['dp'=2,'ctx'=4,'head'=4] {'ctx'}, dimensions={0}, use_global_device_ids=true | all-gather | bytes 320 | tf_op jit(solution)/shard_map/all_gather | solution.py:14
  95.4 2.9 %fusion.36 = f32[2,16,128,64]{2,3,1,0:T(8,128)} fusion(bf16[128,2,16,64]{0,3,2,1:T(8,128)(2,1)} %bitcast.243, f32[128,2,128]{2,0,1:T(8,128)} %copy.152, f32[128,2,16]{0,2,1:T(8,128)S(1)} %bitcast.257), kind=kOutput, calls=%fused_computation.81 | convolution fusion | flops 68157440 | bytes 1720320 | tf_op jit(solution)/shard_map/sgjp,sgjn->gjpn/dot_general | solution.py:88
  98.3 5.3 %while.50 = (s32[]{:T(128)}, f32[32]{0:T(128)S(1)}, f32[32,64,128]{2,1,0:T(8,128)S(1)}, s32[]{:T(128)}, bf16[4,32]{1,0:T(4,128)(2,1)S(1)}, /*index=5*/bf16[4,32,64,128]{3,2,1,0:T(8,128)(2,1)}, s32[]{:T(128)}, s32[]{:T(128)}) while((s32[]{:T(128)}, f32[32]{0:T(128)S(1)}, f32[32,64,128]{2,1,0:T(8,128)S(1)}, s32[]{:T(128)}, ...), condition=%wide.region_6.7_spmd.clone, body=%wide.region_5.6_spmd.clone.sunk | while | flops 1310852 | bytes 2622139 | solution.py:31
  98.3 1.3 fusion.114
  99.7 1.3 fusion.114
  101.0 1.3 fusion.114
  102.3 1.3 fusion.114
  104.2 2.3 %fusion.34 = bf16[32,64,128]{2,1,0:T(8,128)(2,1)} fusion(f32[2,16,128,64]{2,3,1,0:T(8,128)} %fusion.36, f32[32]{0:T(128)S(1)} %get-tuple-element.525, pred[]{:T(512)S(6)} %eq.103, f32[2,16,128,64]{2,3,1,0:T(8,128)S(1)} %get-tuple-element.562, f32[32,64,128]{2,1,0:T(8,128)S(1)} %get-tuple-element.306, f32[32]{0:T(128)S(1)} %get-tuple-element.524), kind=kLoop, calls=%fused_computation.79 | loop fusion | flops 1572864 | bytes 3670273 | tf_op jit(solution)/shard_map/convert_element_type | solution.py:37
  106.6 37.3 %while.49 = (s32[]{:T(128)}, f32[256,2,8]{0,2,1:T(8,128)S(1)}, f32[256,2,8]{0,2,1:T(8,128)S(1)}, f32[256,2,8,128]{0,3,2,1:T(8,128)}, s32[2,512]{1,0:T(2,128)S(1)...) while((s32[]{:T(128)}, f32[256,2,8]{0,2,1:T(8,128)S(1)}, ...), condition=%wide.region_3.4_spmd.clone, body=%wide.region_0.3_spmd.clone.sunk | while | flops 1098806272 | bytes 33307804 | solution.py:184
  106.8 1.4 constant_dynamic-slice_fusion.9
  108.2 4.6 %fusion.111 = (f32[256,2,8]{0,2,1:T(8,128)S(1)}, f32[2,512,256,8]{2,1,3,0:T(8,128)}) fusion(pred[256,512]{0,1:T(8,128)(4,1)S(1)} %compare_and_fusion.2, bf16[256,2,8,128]{3,0,2,1:T(8,128)(2,1)S(1)} %get-tuple-element.756, bf16[1,512,2,128]{3,2,1,0:T(2,128)(2,1)S(1)} %get-tuple-element.703), kind=kOutput, calls=%fused_computation.5.clone.1 | convolution fusion | flops 543158272 | bytes 9846784 | tf_op jit(solution)/shard_map/while/body/eval_jaxpr/tkgd,skd->tkgs/dot_general | solution.py:166
  112.9 5.2 %fusion.112 = f32[256,2,8]{0,2,1:T(8,128)S(1)} fusion(f32[2,512,256,8]{2,1,3,0:T(8,128)} %get-tuple-element.705, f32[256,2,8]{0,2,1:T(8,128)S(1)} %select_maximum_fusion.2, pred[256,512]{0,1:T(8,128)(4,1)S(1)} %compare_and_fusion.2), kind=kLoop, calls=%fused_computation.9.clone.1 | loop fusion | flops 8384512 | bytes 8552448 | tf_op jit(solution)/shard_map/while/body/eval_jaxpr/reduce_sum | solution.py:175
  118.3 6.7 %bitcast_add_fusion.4 = f32[256,2,8,128]{0,3,2,1:T(8,128)} fusion(f32[256,2,8,128]{0,3,2,1:T(8,128)} %get-tuple-element.738, f32[2,512,256,8]{2,1,3,0:T(8,128)} %get-tuple-element.705, f32[256,2,8]{0,2,1:T(8,128)S(1)} %select_maximum_fusion.2, pred[256,512]{0,1:T(8,128)(4,1)S(1)} %compare_and_fusion.2, f32[256,2,8]{0,2,1:T(8,128)S(1)} %get-tuple-element.707, ...), kind=kOutput, calls=%fused_computation.12.clone.1 | convolution fusion | flops 546832384 | bytes 13008897 | tf_op jit(solution)/shard_map/while/body/eval_jaxpr/tkgs,skd->tkgd/dot_general | solution.py:176
  125.2 1.4 constant_dynamic-slice_fusion.9
  126.6 4.6 %fusion.111 = (f32[256,2,8]{0,2,1:T(8,128)S(1)}, f32[2,512,256,8]{2,1,3,0:T(8,128)}) fusion(pred[256,512]{0,1:T(8,128)(4,1)S(1)} %compare_and_fusion.2, bf16[256,2,8,128]{3,0,2,1:T(8,128)(2,1)S(1)} %get-tuple-element.756, bf16[1,512,2,128]{3,2,1,0:T(2,128)(2,1)S(1)} %get-tuple-element.703), kind=kOutput, calls=%fused_computation.5.clone.1 | convolution fusion | flops 543158272 | bytes 9846784 | tf_op jit(solution)/shard_map/while/body/eval_jaxpr/tkgd,skd->tkgs/dot_general | solution.py:166
  131.3 5.1 %fusion.112 = f32[256,2,8]{0,2,1:T(8,128)S(1)} fusion(f32[2,512,256,8]{2,1,3,0:T(8,128)} %get-tuple-element.705, f32[256,2,8]{0,2,1:T(8,128)S(1)} %select_maximum_fusion.2, pred[256,512]{0,1:T(8,128)(4,1)S(1)} %compare_and_fusion.2), kind=kLoop, calls=%fused_computation.9.clone.1 | loop fusion | flops 8384512 | bytes 8552448 | tf_op jit(solution)/shard_map/while/body/eval_jaxpr/reduce_sum | solution.py:175
  136.6 7.3 %bitcast_add_fusion.4 = f32[256,2,8,128]{0,3,2,1:T(8,128)} fusion(f32[256,2,8,128]{0,3,2,1:T(8,128)} %get-tuple-element.738, f32[2,512,256,8]{2,1,3,0:T(8,128)} %get-tuple-element.705, f32[256,2,8]{0,2,1:T(8,128)S(1)} %select_maximum_fusion.2, pred[256,512]{0,1:T(8,128)(4,1)S(1)} %compare_and_fusion.2, f32[256,2,8]{0,2,1:T(8,128)S(1)} %get-tuple-element.707, ...), kind=kOutput, calls=%fused_computation.12.clone.1 | convolution fusion | flops 546832384 | bytes 13008897 | tf_op jit(solution)/shard_map/while/body/eval_jaxpr/tkgs,skd->tkgd/dot_general | solution.py:176
  143.9 2.3 copy.155
  146.5 1.8 divide_convert_fusion
  148.3 1.4 copy.157
  149.8 1.6 fusion.76
  153.9 1.5 copy.138
  157.9 2.3 %copy.156 = bf16[1,256,2048]{1,2,0:T(8,128)(2,1)} copy(bf16[1,256,2048]{2,1,0:T(8,128)(2,1)} %param.24) | data formatting | bytes 2097152 | tf_op args[5]
  161.1 1.2 dynamic-slice.8
  163.4 3.0 %fusion.33 = f32[2,16,128,64]{2,3,1,0:T(8,128)} fusion(bf16[128,2,16,64]{0,3,2,1:T(8,128)(2,1)} %bitcast.244, f32[2,16,128]{2,1,0:T(8,128)S(1)} %bitcast.259, f32[2,128,128]{2,1,0:T(8,128)S(1)} %fusion.83, f32[2,16,128]{2,1,0:T(8,128)S(1)} %bitcast.260, pred[128,128]{1,0:T(8,128)(4,1)S(1)} %get-tuple-element.565), kind=kOutput, calls=%fused_computation.78 | convolution fusion | flops 69730304 | bytes 1753088 | tf_op jit(solution)/shard_map/gjts,sgjp->tgjp/dot_general | solution.py:79
  166.4 1.9 fusion.32
  168.5 8.6 %all-reduce = bf16[128]{0:T(256)(128)(2,1)S(1)} all-reduce(bf16[128]{0:T(256)(128)(2,1)S(1)} %dynamic-update-slice.2), channel_id=2, replica_groups=mesh['dp'=2,'ctx'=4,'head'=4] {'ctx'}, use_global_device_ids=true, to_apply=%add | all-reduce | flops 128 | bytes 512
  180.7 5.4 %while.51 = (s32[]{:T(128)}, f32[32,64,128]{2,1,0:T(8,128)S(1)}, s32[]{:T(128)}, bf16[4,32]{1,0:T(4,128)(2,1)S(1)}, bf16[4,32,64,128]{3,2,1,0:T(8,128)(2,1)}, /*index=5*/s32[]{:T(128)}, s32[]{:T(128)}, s32[]{:T(128)}, s32[]{:T(128)}) while((s32[]{:T(128)}, f32[32,64,128]{2,1,0:T(8,128)S(1)}, s32[]{:T(128)}, ...), condition=%wide.region_9.10_spmd.clone, body=%wide.region_8.9_spmd.clone.sunk | while | flops 1310760 | bytes 2621935 | solution.py:55
  180.7 1.3 fusion.115
  182.1 1.3 fusion.115
  183.4 1.3 fusion.115
  184.8 1.3 fusion.115
  186.1 1.4 broadcast_select_fusion.2
  194.2 3.4 %fusion.24 = (f32[2048]{0:T(1024)S(1)}, f32[2048]{0:T(1024)S(1)}, bf16[1,256,2048]{1,2,0:T(8,128)(2,1)S(1)}) fusion(bf16[1,256,2048]{1,2,0:T(8,128)(2,1)S(1)} %bitcast.228, bf16[1,256,2048]{1,2,0:T(8,128)(2,1)S(1)} %copy-done.2, f32[1,128,2048]{1,2,0:T(8,128)S(1)} %add.442, f32[1,128,2048]{1,2,0:T(8,128)S(1)} %copy-done.5, ...), kind=kLoop, calls=%fused_computation.54 | loop fusion | flops 16773120 | bytes 6344704 | tf_op jit(solution)/shard_map/transpose(jvp())/reduce_sum | solution.py:112
  197.6 1.4 copy.158
  199.2 21.3 %all-reduce.1 = (f32[2048]{0:T(1024)}, f32[32]{0:T(128)}) all-reduce(f32[2048]{0:T(1024)S(1)} %get-tuple-element.470, f32[32]{0:T(128)S(1)} %reduce_sum.69), channel_id=1, replica_groups=mesh['dp'=2,'ctx'=4,'head'=4] {'dp','ctx'}, use_global_device_ids=true, to_apply=%region_12.13 | all-reduce | flops 2080 | bytes 16640 | tf_op jit(solution)/shard_map/psum | solution.py:241
  (143 shorter events, 26.0 us)
Async XLA Ops:
  7.2 5.5 %copy-start.20 = (f32[32]{0:T(128)S(1)}, f32[32]{0:T(128)}, u32[]{:S(2)}) copy-start(f32[32]{0:T(128)} %param.29) | copy-start | bytes 388
  7.2 5.5 %copy-start.13 = (f32[1,256,32]{1,2,0:T(8,128)S(1)}, f32[1,256,32]{1,2,0:T(8,128)}, u32[]{:S(2)}) copy-start(f32[1,256,32]{1,2,0:T(8,128)} %param.27) | copy-start | bytes 98308
  7.2 6.3 %copy-start.17 = (f32[32]{0:T(128)S(1)}, f32[32]{0:T(128)}, u32[]{:S(2)}) copy-start(f32[32]{0:T(128)} %param.28) | copy-start | bytes 388
  7.2 91.1 %all-gather.6.cloned.1.call-start = ((), (), s32[]{:S(2)}) async-start(), calls=%async_computation | async-start | bytes 2621440 | tf_op jit(solution)/shard_map/all_gather | solution.py:14
  8.6 5.4 %copy-start.11 = (bf16[1,256,256]{2,1,0:T(8,128)(2,1)S(1)}, bf16[1,256,256]{2,1,0:T(8,128)(2,1)}, u32[]{:S(2)}) copy-start(bf16[1,256,256]{2,1,0:T(8,128)(2,1)} %param.25) | copy-start | bytes 393220
  14.8 11.6 %copy-start.8 = (bf16[1,128,2048]{1,2,0:T(8,128)(2,1)}, bf16[1,128,2048]{1,2,0:T(8,128)(2,1)S(1)}, u32[]{:S(2)}) copy-start(bf16[1,128,2048]{1,2,0:T(8,128)(2,1)S(1)} %copy.139) | copy-start | bytes 1572868
  14.8 7.0 %copy-start = (s32[1,1024]{1,0:T(1,128)S(1)}, s32[1,1024]{1,0:T(1,128)}, u32[]{:S(2)}) copy-start(s32[1,1024]{1,0:T(1,128)} %param.22) | copy-start | bytes 12292
  21.0 83.2 %copy-start.1 = (f32[2,16,128,64]{2,3,1,0:T(8,128)}, f32[2,16,128,64]{2,3,1,0:T(8,128)S(1)}, u32[]{:S(2)}) copy-start(f32[2,16,128,64]{2,3,1,0:T(8,128)S(1)} %get-tuple-element.562) | copy-start | bytes 3145732
  21.0 159.7 %all-gather.8.cloned.1.call-start = ((), (), s32[]{:S(2)}) async-start(), calls=%async_computation.1 | async-start | bytes 2621440 | tf_op jit(solution)/shard_map/all_gather | solution.py:37
  21.8 4.6 %copy-start.10 = (bf16[1,256,256]{2,1,0:T(8,128)(2,1)S(1)}, bf16[1,256,256]{2,1,0:T(8,128)(2,1)}, u32[]{:S(2)}) copy-start(bf16[1,256,256]{2,1,0:T(8,128)(2,1)} %param.20) | copy-start | bytes 393220
  143.9 2.3 %copy-start.18 = (f32[32]{0:T(128)S(1)}, f32[32]{0:T(128)}, u32[]{:S(2)}) copy-start(f32[32]{0:T(128)} %param.30) | copy-start | bytes 388
  148.3 11.9 %copy-start.12 = (f32[2048]{0:T(1024)S(1)}, f32[2048]{0:T(1024)}, u32[]{:S(2)}) copy-start(f32[2048]{0:T(1024)} %param.31) | copy-start | bytes 24580
  157.0 6.4 %copy-start.14 = (f32[32,128]{1,0:T(8,128)S(1)}, f32[32,128]{1,0:T(8,128)}, u32[]{:S(2)}) copy-start(f32[32,128]{1,0:T(8,128)} %copy.144) | copy-start | bytes 49156
  163.1 3.2 %copy-start.9 = (bf16[1,128,2048]{1,2,0:T(8,128)(2,1)S(1)}, bf16[1,128,2048]{1,2,0:T(8,128)(2,1)}, u32[]{:S(2)}) copy-start(bf16[1,128,2048]{1,2,0:T(8,128)(2,1)} %copy-done.8) | copy-start | bytes 1572868
  163.2 3.2 %copy-start.15 = (f32[32,128]{1,0:T(8,128)S(1)}, f32[32,128]{1,0:T(8,128)}, u32[]{:S(2)}) copy-start(f32[32,128]{1,0:T(8,128)} %copy.138) | copy-start | bytes 49156
  163.2 3.2 %copy-start.16 = (f32[32,128]{1,0:T(8,128)S(1)}, f32[32,128]{1,0:T(8,128)}, u32[]{:S(2)}) copy-start(f32[32,128]{1,0:T(8,128)} %copy.133) | copy-start | bytes 49156
  166.4 1.9 copy-start.19
  177.2 1.2 copy-start.6
  188.1 1.2 copy-start.4
  189.4 1.2 copy-start.2
  189.4 1.5 copy-start.3
  189.4 1.9 copy-start.7
  193.0 1.2 copy-start.5
Sparse Core Ops, SparseCore 0:
  21.1 62.8 all-gather.5
  106.7 43.9 all-gather.7
where the time goes:
time: 229 us; the launch traced here: 227 us
  blocking collectives  87.4 us (38%)
  local copies, waits for them, and re-layouts  49.3 us (22%)
  other arithmetic  38.2 us (17%)
  matrix products  34.3 us (15%)
  between operations  17.7 us (8%)
    all_gather x1, blocking collectives, body(): key_piece = lax.all_gather(keys, 'ctx', axis=1, tiled=True)  24 us
    all_gather x1, blocking collectives, body(): value_piece = lax.all_gather(values, 'ctx', axis=1, tiled=True)  23.2 us
    psum x1, blocking collectives, body(): summed_grads = lax.psum((grad_gain, grad_skip), ('dp', 'ctx'))  21.3 us
    unnamed x57, local copies, waits for them, and re-layouts  20.2 us
    dot_general x2, matrix products, inner(): jnp.einsum('tkgs,skd->tkgd', weights.astype(jnp.bfloat16), value_now, pre...  14 us
    all_gather x1, blocking collectives, prefix(): lax.all_gather(part.astype(kind), axis)  10.4 us
    reduce_sum x2, other arithmetic, inner(): total = total * factor + jnp.sum(weights, axis=3)  10.3 us
    dot_general x2, matrix products, inner(): jnp.einsum('tkgd,skd->tkgs', query_block, key_now, preferred_element_type...  9.27 us
  transfers between devices with their start and end apart: 2, of which 0 were waited for; matrix products, arithmetic and copies ran while one was open for 37% of the time, Pallas kernels for 0%

commit v1 on v0

v1 whole, which is shorter than its diff:
```python
import functools
import math

import jax
import jax.numpy as jnp
from jax import lax
from jax.experimental import pallas as pl
from jax.experimental.pallas import tpu as pltpu
from jax.sharding import PartitionSpec as P

DH = 128
P_SIZE = 64
N = 128
EXTRA = 16
EPS = 1e-05
MASKED = -1e30
F32 = jnp.float32
BF16 = jnp.bfloat16
VMEM = pl.BlockSpec(memory_space=pltpu.VMEM)


def params(mib):
    return pltpu.CompilerParams(vmem_limit_bytes=mib << 20)


def cost(flops, size):
    return pl.CostEstimate(flops=flops, bytes_accessed=size, transcendentals=0)


def parts(v):
    hi = v.astype(BF16)
    return hi, (v - hi.astype(F32)).astype(BF16)


def spread_matrix(heads, width, first):
    row = lax.broadcasted_iota(jnp.int32, (heads, width), 0)
    lane = lax.broadcasted_iota(jnp.int32, (heads, width), 1)
    return jnp.where(row == (lane // P_SIZE) + first, 1.0, 0.0).astype(BF16)


def spread(v, matrix):
    hi, lo = parts(v)
    return jnp.dot(hi, matrix, preferred_element_type=F32) + jnp.dot(
        lo, matrix, preferred_element_type=F32
    )


def dot_nt(a, b):
    return lax.dot_general(a, b, (((1,), (1,)), ((), ())), preferred_element_type=F32)


def dot_tn(a, b):
    return lax.dot_general(a, b, (((0,), (0,)), ((), ())), preferred_element_type=F32)


def doc_row(docs_ref, block, stretch):
    return docs_ref[:, pl.ds(pl.multiple_of(block * stretch, stretch), stretch)]


def as_column(row):
    size = row.shape[1]
    r = lax.broadcasted_iota(jnp.int32, (size, size), 0)
    c = lax.broadcasted_iota(jnp.int32, (size, size), 1)
    return jnp.sum(jnp.where(r == c, row.astype(F32), 0.0), axis=1, keepdims=True)


def lower_triangle(size):
    r = lax.broadcasted_iota(jnp.int32, (size, size), 0)
    c = lax.broadcasted_iota(jnp.int32, (size, size), 1)
    return r >= c


def prior_doc(docs_ref, block, stretch):
    before = doc_row(docs_ref, jnp.maximum(block - 1, 0), stretch)[:, stretch - 1 :]
    return jnp.where(block > 0, before, -1)


def pack_kernel(k_ref, v_ref, full_ref, front_ref):
    width = k_ref.shape[1]
    rows = front_ref.shape[0]
    full_ref[:, :width] = k_ref[...]
    full_ref[:, width:] = v_ref[...]
    front_ref[:, :width] = k_ref[:rows, :]
    front_ref[:, width:] = v_ref[:rows, :]


def summary_kernel(
    count, groups, docs_ref, x_ref, b_ref, dt_ref, bias_ref, log_ref, xw_ref, ec_ref, dec_ref, *outs
):
    f_refs, b_refs, q_refs = outs[:groups], outs[groups : 2 * groups], outs[2 * groups :]
    rows, heads = dt_ref.shape
    stretch = rows // 2
    width = x_ref.shape[1] // groups
    index = lax.axis_index("ctx")
    triangle = jnp.where(lower_triangle(stretch), 1.0, 0.0)
    slope = jnp.exp(log_ref[...])
    decays = []
    sums = []
    for half in range(2):
        block = index if half == 0 else 2 * count - 1 - index
        sl = slice(half * stretch, (half + 1) * stretch)
        raw = dt_ref[sl, :] + bias_ref[...]
        dt = jnp.maximum(raw, 0.0) + jnp.log1p(jnp.exp(-jnp.abs(raw)))
        cum = jnp.dot(
            triangle, -dt * slope, precision=lax.Precision.HIGHEST, preferred_element_type=F32
        )
        ec_ref[sl, :] = jnp.exp(cum)
        load = jnp.exp(-cum) * dt
        final = jnp.exp(cum[stretch - 1 :, :])
        row = doc_row(docs_ref, block, stretch)
        last = row[:, stretch - 1 :]
        decays.append(jnp.where(last == prior_doc(docs_ref, block, stretch), final, 0.0))
        same = jnp.where(as_column(row) == last.astype(F32), 1.0, 0.0)
        here = []
        for g in range(groups):
            cols = slice(g * width, (g + 1) * width)
            matrix = spread_matrix(heads, width, g * (heads // groups))
            xw = (x_ref[sl, cols].astype(F32) * spread(load, matrix)).astype(BF16)
            xw_ref[sl, cols] = xw
            proj = (b_ref[sl, g * N : (g + 1) * N].astype(F32) * same).astype(BF16)
            here.append(dot_tn(proj, xw) * spread(final, matrix))
        sums.append(here)
    for g in range(groups):
        cols = slice(g * width, (g + 1) * width)
        matrix = spread_matrix(heads, width, g * (heads // groups))
        both = jnp.concatenate([decays[0], decays[1]], axis=0)
        wide = spread(both, matrix)
        dec_ref[0:2, cols] = wide
        f_refs[g][...] = sums[0][g].astype(BF16)
        b_refs[g][...] = sums[1][g].astype(BF16)
        q_refs[g][:N, :] = (wide[1:2] * sums[0][g] + sums[1][g]).astype(BF16)
        hi, lo = parts(wide[0:1] * wide[1:2])
        q_refs[g][N : N + 1, :] = hi
        q_refs[g][N + 1 : N + 2, :] = lo
        q_refs[g][N + 2 :, :] = jnp.zeros((EXTRA - 2, width), BF16)


def chain_kernel(p_ref, q_ref, f_ref, b_ref, dec_ref, p_out, q_out):
    d_front, d_back = dec_ref[0:1, :], dec_ref[1:2, :]
    f = f_ref[...].astype(F32)
    d_in = q_ref[N : N + 1, :].astype(F32) + q_ref[N + 1 : N + 2, :].astype(F32)
    p_out[...] = (d_front * p_ref[...].astype(F32) + f).astype(BF16)
    q_out[:N, :] = (
        d_back * (d_in * f + q_ref[:N, :].astype(F32)) + b_ref[...].astype(F32)
    ).astype(BF16)
    hi, lo = parts(d_back * d_in * d_front)
    q_out[N : N + 1, :] = hi
    q_out[N + 1 : N + 2, :] = lo
    q_out[N + 2 :, :] = jnp.zeros((EXTRA - 2, p_ref.shape[1]), BF16)


def local_kernel(
    count, docs_ref, x_ref, xw_ref, b_ref, c_ref, ec_ref, skip_ref, pre_ref, reach_ref
):
    rows, heads = ec_ref.shape
    stretch = rows // 2
    width = x_ref.shape[1]
    index = lax.axis_index("ctx")
    g = pl.program_id(0)
    matrix = spread_matrix(heads, width, g * (width // P_SIZE))
    wide_skip = spread(skip_ref[...], matrix)
    triangle = lower_triangle(stretch)
    for half in range(2):
        block = index if half == 0 else 2 * count - 1 - index
        sl = slice(half * stretch, (half + 1) * stretch)
        row = doc_row(docs_ref, block, stretch)
        column = as_column(row)
        gram = dot_nt(c_ref[sl, :], b_ref[sl, :])
        gram = jnp.where(triangle & (column == row.astype(F32)), gram, 0.0).astype(BF16)
        wide = spread(ec_ref[sl, :], matrix)
        inner = jnp.dot(gram, xw_ref[sl, :], preferred_element_type=F32)
        pre_ref[sl, :] = inner * wide + wide_skip * x_ref[sl, :].astype(F32)
        reached = column == prior_doc(docs_ref, block, stretch).astype(F32)
        reach_ref[sl, :] = jnp.where(reached, wide, 0.0)


def attention_kernel(count, per, unroll, docs_ref, q_ref, k_ref, v_ref, *refs):
    others = count - 1
    ups, downs = refs[:others], refs[others : 2 * others]
    out_ref = refs[2 * others]
    kb, vb, ka, va, bias_b, bias_f, bias_a = refs[2 * others + 1 :]
    rows = q_ref.shape[0]
    stretch = rows // 2
    index = lax.axis_index("ctx")
    g = pl.program_id(0)
    kv_width = ups[0].shape[1] // 2
    k_cols = pl.ds(pl.multiple_of(g * DH, DH), DH)
    v_cols = pl.ds(pl.multiple_of(kv_width + g * DH, DH), DH)
    kb[: 2 * stretch, :] = k_ref[...]
    vb[: 2 * stretch, :] = v_ref[...]
    for r in range(1, count):
        at_b = slice((r + 1) * stretch, (r + 2) * stretch)
        at_a = slice((r - 1) * stretch, r * stretch)
        up, down = ups[r - 1], downs[count - r - 1]

        @pl.when(index >= r)
        def _():
            kb[at_b, :] = up[:, k_cols]
            ka[at_a, :] = up[:, k_cols]
            vb[at_b, :] = up[:, v_cols]
            va[at_a, :] = up[:, v_cols]

        @pl.when(index < r)
        def _():
            kb[at_b, :] = down[:stretch, k_cols]
            ka[at_a, :] = down[stretch:, k_cols]
            vb[at_b, :] = down[:stretch, v_cols]
            va[at_a, :] = down[stretch:, v_cols]

    @pl.when(g == 0)
    def _():
        last = 2 * count - 1
        row_f = doc_row(docs_ref, index, stretch).astype(F32)
        row_b = doc_row(docs_ref, last - index, stretch).astype(F32)
        col_f = as_column(row_f)
        col_b = as_column(row_b)
        triangle = lower_triangle(stretch)
        bias_f[...] = jnp.where(triangle & (col_f == row_f), 0.0, MASKED)
        bias_b[:, :stretch] = jnp.where(col_b == row_f, 0.0, MASKED)
        bias_b[:, stretch : 2 * stretch] = jnp.where(triangle & (col_b == row_b), 0.0, MASKED)
        for r in range(1, count):
            up = index >= r
            source = jnp.where(up, index - r, index + count - r)
            key_f = doc_row(docs_ref, source, stretch).astype(F32)
            key_a = doc_row(docs_ref, jnp.where(up, source, last - source), stretch).astype(F32)
            col_a = jnp.where(up, col_f, col_b)
            bias_b[:, (r + 1) * stretch : (r + 2) * stretch] = jnp.where(
                col_b == key_f, 0.0, MASKED
            )
            bias_a[:, (r - 1) * stretch : r * stretch] = jnp.where(col_a == key_a, 0.0, MASKED)

    factor = math.log2(math.e) / math.sqrt(DH)

    def one_head(h):
        cols = pl.ds(pl.multiple_of(h * DH, DH), DH)
        q_f = q_ref[:stretch, cols]
        q_b = q_ref[stretch:, cols]
        s_f = dot_nt(q_f, kb[:stretch, :]) + bias_f[...]
        s_b = dot_nt(q_b, kb[...]) + bias_b[...]
        top_f = jnp.max(s_f, axis=1, keepdims=True)
        top_b = jnp.max(s_b, axis=1, keepdims=True)
        s_a = []
        for r in range(1, count):
            at_a = slice((r - 1) * stretch, r * stretch)
            first = pl.multiple_of(jnp.where(index >= r, 0, stretch), stretch)
            score = dot_nt(q_ref[pl.ds(first, stretch), cols], ka[at_a, :]) + bias_a[:, at_a]
            top = jnp.max(score, axis=1, keepdims=True)
            top_f = jnp.maximum(top_f, jnp.where(index >= r, top, MASKED))
            top_b = jnp.maximum(top_b, jnp.where(index >= r, MASKED, top))
            s_a.append(score)
        w_f = jnp.exp2((s_f - top_f) * factor)
        w_b = jnp.exp2((s_b - top_b) * factor)
        sum_f = jnp.sum(w_f, axis=1, keepdims=True)
        sum_b = jnp.sum(w_b, axis=1, keepdims=True)
        out_f = jnp.dot(w_f.astype(BF16), vb[:stretch, :], preferred_element_type=F32)
        out_b = jnp.dot(w_b.astype(BF16), vb[...], preferred_element_type=F32)
        for r in range(1, count):
            at_a = slice((r - 1) * stretch, r * stretch)
            up = index >= r
            w = jnp.exp2((s_a[r - 1] - jnp.where(up, top_f, top_b)) * factor)
            total = jnp.sum(w, axis=1, keepdims=True)
            out = jnp.dot(w.astype(BF16), va[at_a, :], preferred_element_type=F32)
            sum_f += jnp.where(up, total, 0.0)
            sum_b += jnp.where(up, 0.0, total)
            out_f += jnp.where(up, out, 0.0)
            out_b += jnp.where(up, 0.0, out)
        out_ref[:stretch, cols] = (out_f / sum_f).astype(BF16)
        out_ref[stretch:, cols] = (out_b / sum_b).astype(BF16)

    if unroll:
        for h in range(per):
            one_head(h)
    else:

        @pl.loop(0, per)
        def _(h):
            one_head(h)


def final_kernel(
    count,
    g,
    loss_scale,
    pre_ref,
    reach_ref,
    c_ref,
    x_ref,
    gate_ref,
    teacher_ref,
    gain_ref,
    f_ref,
    dec_ref,
    *refs,
):
    others = count - 1
    p_refs, q_refs = refs[:others], refs[others : 2 * others]
    out_ref, grad_ref, flow_ref, gain_acc, skip_acc = refs[-5:]
    rows, width = pre_ref.shape
    stretch = rows // 2
    index = lax.axis_index("ctx")
    state = p_refs[0][...].astype(F32)
    back = q_refs[0][...].astype(F32)
    for r in range(1, others):
        state += p_refs[r][...].astype(F32)
        back += q_refs[r][...].astype(F32)
    d_in = jnp.where(index == count - 1, 1.0, back[N : N + 1] + back[N + 1 : N + 2])
    after = d_in * (dec_ref[0:1, :] * state + f_ref[...].astype(F32)) + back[:N]
    flow_ref[:stretch, :] = jnp.dot(
        c_ref[:stretch, :], state.astype(BF16), preferred_element_type=F32
    )
    flow_ref[stretch:, :] = jnp.dot(
        c_ref[stretch:, :], after.astype(BF16), preferred_element_type=F32
    )
    gain_acc[...] = jnp.zeros_like(gain_acc)
    skip_acc[...] = jnp.zeros_like(skip_acc)
    gain = gain_ref[...]
    step = 16

    @pl.loop(0, rows // step)
    def _(k):
        sl = pl.ds(pl.multiple_of(k * step, step), step)
        gate = gate_ref[sl, :].astype(F32)
        silu = gate / (1.0 + jnp.exp(-gate))
        gated = (pre_ref[sl, :] + reach_ref[sl, :] * flow_ref[sl, :]) * silu
        scale = lax.rsqrt(jnp.mean(gated * gated, axis=1, keepdims=True) + EPS)
        unit = gated * scale
        normed = unit * gain
        out_ref[sl, :] = normed.astype(BF16)
        push = (normed - teacher_ref[sl, :].astype(F32)) * (2.0 * loss_scale)
        by_gain = push * unit
        pulled = push * gain
        mean = jnp.mean(by_gain * gain, axis=1, keepdims=True)
        by_skip = scale * (pulled - unit * mean) * silu * x_ref[sl, :].astype(F32)
        gain_acc[...] += by_gain[:8] + by_gain[8:]
        skip_acc[...] += by_skip[:8] + by_skip[8:]

    grad_ref[0:1, :] = jnp.sum(gain_acc[...], axis=0, keepdims=True)
    heads = width // P_SIZE
    row = lax.broadcasted_iota(jnp.int32, (128, width), 0)
    lane = lax.broadcasted_iota(jnp.int32, (128, width), 1)
    matrix = jnp.where(row == lane // P_SIZE, 1.0, 0.0).astype(BF16)
    hi, lo = parts(skip_acc[...])
    by_head = jnp.sum(dot_nt(hi, matrix) + dot_nt(lo, matrix), axis=0, keepdims=True)
    grad_ref[1:2, :] = jnp.zeros((1, width), F32)
    grad_ref[1:2, :128] = by_head


def exchange_sum(part, axis):
    size = lax.axis_size(axis)
    step = 1
    while step < size:
        span = 4 if (size // step) % 4 == 0 else 2
        got = [part]
        for k in range(1, span):
            pairs = [(d, d ^ (k * step)) for d in range(size)]
            got.append(lax.ppermute(part, axis, pairs))
        if span == 4:
            part = (got[0] + got[1]) + (got[2] + got[3])
        else:
            part = got[0] + got[1]
        step *= span
    return part


def body(
    queries,
    keys,
    values,
    doc_ids,
    inputs,
    gate_input,
    b_input,
    c_input,
    dt_raw,
    dt_bias,
    decay_log,
    skip,
    gain,
):
    count = lax.axis_size("ctx")
    rows, features = queries.shape[1:]
    stretch = rows // 2
    kv_dev = keys.shape[2] // DH
    per_kv = queries.shape[2] // keys.shape[2]
    groups = b_input.shape[2] // N
    heads = features // P_SIZE
    width = features // groups
    length = doc_ids.shape[1]
    others = count - 1
    last = count - 1
    loss_scale = 1.0 / (lax.axis_size("dp") * count * rows)
    x, gate, bmat, cmat = inputs[0], gate_input[0], b_input[0], c_input[0]
    struct = jax.ShapeDtypeStruct

    full, front = pl.pallas_call(
        pack_kernel,
        out_shape=(
            struct((rows, 2 * kv_dev * DH), BF16),
            struct((stretch, 2 * kv_dev * DH), BF16),
        ),
        in_specs=[VMEM] * 2,
        out_specs=(VMEM,) * 2,
        cost_estimate=cost(0, 3 * keys.size * 2),
        name="pack_kv",
    )(keys[0], values[0])
    ups, downs = [], []
    up, down = front, full
    for r in range(1, count):
        up = lax.ppermute(up, "ctx", [(d, d + 1) for d in range(r - 1, last)])
        down = lax.ppermute(down, "ctx", [(d, d - 1) for d in range(1, count - r + 1)])
        ups.append(up)
        downs.append(down)

    state = struct((N, width), BF16)
    composite = struct((N + EXTRA, width), BF16)
    outs = pl.pallas_call(
        functools.partial(summary_kernel, count, groups),
        out_shape=(
            struct((rows, features), BF16),
            struct((rows, heads), F32),
            struct((8, features), F32),
            *([state] * (2 * groups)),
            *([composite] * groups),
        ),
        in_specs=[VMEM] * 6,
        out_specs=(VMEM,) * (3 + 3 * groups),
        compiler_params=params(32),
        cost_estimate=cost(4 * rows * features * N, 8 * rows * features),
        name="summaries",
    )(doc_ids, x, bmat, dt_raw[0], dt_bias.reshape(1, heads), decay_log.reshape(1, heads))
    xw, ec, dec = outs[:3]
    f_parts, b_parts, q_parts = (
        outs[3 : 3 + groups],
        outs[3 + groups : 3 + 2 * groups],
        outs[3 + 2 * groups :],
    )

    chain = [
        pl.pallas_call(
            chain_kernel,
            out_shape=(state, composite),
            grid=(1,),
            in_specs=[
                pl.BlockSpec((N, width), lambda k: (0, 0)),
                pl.BlockSpec((N + EXTRA, width), lambda k: (0, 0)),
                pl.BlockSpec((N, width), lambda k: (0, 0)),
                pl.BlockSpec((N, width), lambda k: (0, 0)),
                pl.BlockSpec((8, width), lambda k, g=g: (0, g)),
            ],
            out_specs=(
                pl.BlockSpec((N, width), lambda k: (0, 0)),
                pl.BlockSpec((N + EXTRA, width), lambda k: (0, 0)),
            ),
            cost_estimate=cost(8 * N * width, 12 * N * width),
            compiler_params=params(16),
            name="chain",
        )
        for g in range(groups)
    ]
    p_got = [[] for _ in range(groups)]
    q_got = [[] for _ in range(groups)]
    p_send, q_send = list(f_parts), list(q_parts)
    for r in range(1, count):
        for g in range(groups):
            if r > 1:
                p_send[g], q_send[g] = chain[g](
                    p_got[g][-1], q_got[g][-1], f_parts[g], b_parts[g], dec
                )
            p_got[g].append(lax.ppermute(p_send[g], "ctx", [(r - 1, r)]))
            q_got[g].append(lax.ppermute(q_send[g], "ctx", [(count - r, count - r - 1)]))

    by_group = pl.BlockSpec((rows, width), lambda g: (0, g))
    by_proj = pl.BlockSpec((rows, N), lambda g: (0, g))
    pre, reach = pl.pallas_call(
        functools.partial(local_kernel, count),
        out_shape=(struct((rows, features), F32), struct((rows, features), F32)),
        grid=(groups,),
        in_specs=[
            pl.BlockSpec((1, length), lambda g: (0, 0)),
            by_group,
            by_group,
            by_proj,
            by_proj,
            pl.BlockSpec((rows, heads), lambda g: (0, 0)),
            pl.BlockSpec((1, heads), lambda g: (0, 0)),
        ],
        out_specs=(by_group, by_group),
        compiler_params=params(32),
        cost_estimate=cost(4 * rows * features * N, 12 * rows * features),
        name="local",
    )(doc_ids, x, xw, bmat, cmat, ec, skip.reshape(1, heads))

    by_kv = pl.BlockSpec((rows, per_kv * DH), lambda g: (0, g))
    by_key = pl.BlockSpec((rows, DH), lambda g: (0, g))
    teacher = pl.pallas_call(
        functools.partial(attention_kernel, count, per_kv, count <= 4),
        out_shape=struct((rows, features), BF16),
        grid=(kv_dev,),
        in_specs=[
            pl.BlockSpec((1, length), lambda g: (0, 0)),
            by_kv,
            by_key,
            by_key,
            *[pl.BlockSpec((stretch, 2 * kv_dev * DH), lambda g: (0, 0))] * others,
            *[pl.BlockSpec((rows, 2 * kv_dev * DH), lambda g: (0, 0))] * others,
        ],
        out_specs=by_kv,
        scratch_shapes=[
            pltpu.VMEM(((count + 1) * stretch, DH), BF16),
            pltpu.VMEM(((count + 1) * stretch, DH), BF16),
            pltpu.VMEM((others * stretch, DH), BF16),
            pltpu.VMEM((others * stretch, DH), BF16),
            pltpu.VMEM((stretch, (count + 1) * stretch), F32),
            pltpu.VMEM((stretch, stretch), F32),
            pltpu.VMEM((stretch, others * stretch), F32),
        ],
        compiler_params=params(40),
        cost_estimate=cost(
            4 * (2 * count + 1) * stretch * stretch * features, 8 * rows * features
        ),
        name="attention",
    )(doc_ids, queries[0], keys[0], values[0], *ups, *downs)

    student = None
    reduced = []
    for g in range(groups):
        at = lambda k, g=g: (0, g)
        whole = lambda k: (0, 0)
        more = [] if student is None else [student]
        fixed = 9 + 2 * others
        student, grads = pl.pallas_call(
            functools.partial(final_kernel, count, g, loss_scale),
            out_shape=(struct((rows, features), BF16), struct((2, width), F32)),
            grid=(1,),
            in_specs=[
                pl.BlockSpec((rows, width), at),
                pl.BlockSpec((rows, width), at),
                pl.BlockSpec((rows, N), at),
                pl.BlockSpec((rows, width), at),
                pl.BlockSpec((rows, width), at),
                pl.BlockSpec((rows, width), at),
                pl.BlockSpec((1, width), at),
                pl.BlockSpec((N, width), whole),
                pl.BlockSpec((8, width), at),
                *[pl.BlockSpec((N, width), whole)] * others,
                *[pl.BlockSpec((N + EXTRA, width), whole)] * others,
                *[pl.BlockSpec(memory_space=pl.ANY)] * len(more),
            ],
            out_specs=(pl.BlockSpec((rows, width), at), pl.BlockSpec((2, width), whole)),
            scratch_shapes=[
                pltpu.VMEM((rows, width), F32),
                pltpu.VMEM((8, width), F32),
                pltpu.VMEM((8, width), F32),
            ],
            input_output_aliases={fixed: 0} if more else {},
            compiler_params=params(40),
            cost_estimate=cost(2 * rows * width * N, 20 * rows * width),
            name="final",
        )(
            pre,
            reach,
            cmat,
            x,
            gate,
            teacher,
            gain.reshape(1, features),
            f_parts[g],
            dec,
            *p_got[g],
            *q_got[g],
            *more,
        )
        reduced.append(exchange_sum(exchange_sum(grads, "ctx"), "dp"))
    grad_gain = jnp.concatenate([part[0] for part in reduced])
    grad_skip = jnp.concatenate([part[1, : heads // groups] for part in reduced])
    return (teacher[None], student[None], grad_gain, grad_skip)


def solution(mesh):
    rows = P("dp", "ctx", "head")
    in_specs = (
        rows,
        rows,
        rows,
        P("dp", None),
        rows,
        rows,
        rows,
        rows,
        rows,
        P("head"),
        P("head"),
        P("head"),
        P("head"),
    )
    out_specs = (rows, rows, P("head"), P("head"))
    return jax.shard_map(body, mesh=mesh, in_specs=in_specs, out_specs=out_specs, check_vma=False)
```

time: 229 us -> 95.2 us (0.42)
  blocking collectives: 87.4 us -> 0 us
  local copies, waits for them, and re-layouts: 49.3 us -> 6.27 us
  starting transfers between devices: 0.08 us -> 39.4 us
  other arithmetic: 38.2 us -> 1.22 us
  matrix products: 34.3 us -> 0 us
  Pallas kernels: 0 us -> 26.6 us
  waiting for transfers between devices: 0.04 us -> 20.1 us
  between operations: 17.7 us -> 1.08 us
    all_gather x3 -> x0, blocking collectives: 57.5 us -> none  [the longest x1 24 us: body(): key_piece = lax.all_gather(keys, 'ctx', axis=1, tiled=True)]
    ppermute x0 -> x26, starting transfers between devices: none -> 39.4 us  [the longest x8 12.9 us: exchange_sum(): got.append(lax.ppermute(part, axis, pairs))]
    dot_general x12 -> x0, matrix products: 34.3 us -> none  [the longest x2 14 us: inner(): jnp.einsum('tkgs,skd->tkgd', weights.astype(jnp.bfloat16), value_now, pre...]
    pallas_call x0 -> x10, Pallas kernels: none -> 26.6 us  [the longest x2 9.94 us: body(): pl.pallas_call(functools.partial(final_kernel, count, g, loss_scale), out...]
    psum x1 -> x0, blocking collectives: 21.3 us -> none  [body(): summed_grads = lax.psum((grad_gain, grad_skip), ('dp', 'ctx'))]
    ppermute x0 -> x26, waiting for transfers between devices: none -> 20.1 us  [the longest x3 16.4 us: body(): lax.ppermute(down, 'ctx', [(d, d - 1) for d in range(1, count - r + 1)])]
    reduce_sum x6 -> x0, other arithmetic: 15.5 us -> none  [the longest x2 10.3 us: inner(): total = total * factor + jnp.sum(weights, axis=3)]
    unnamed x57 -> x31, local copies, waits for them, and re-layouts: 20.2 us -> 6.25 us
  transfers between devices with their start and end apart: 2 -> 26, of which waited for: 0 -> 5; matrix products, arithmetic and copies ran while one was open for 37% -> 1% of each run, Pallas kernels for 0% -> 26%
where the time goes in v1:
time: 95.2 us; the launch traced here: 94.6 us
  starting transfers between devices  39.4 us (41%)
  Pallas kernels  26.6 us (28%)
  waiting for transfers between devices  20.1 us (21%)
  local copies, waits for them, and re-layouts  6.27 us (7%)
  other arithmetic  1.22 us (1%)
  between operations  1.08 us (1%)
    ppermute x3, waiting for transfers between devices, body(): lax.ppermute(down, 'ctx', [(d, d - 1) for d in range(1, count - r + 1)])  16.4 us
    ppermute x8, starting transfers between devices, exchange_sum(): got.append(lax.ppermute(part, axis, pairs))  12.9 us
    ppermute x6, starting transfers between devices, body(): p_got[g].append(lax.ppermute(p_send[g], 'ctx', [(r - 1, r)]))  10.9 us
    pallas_call x2, Pallas kernels, body(): pl.pallas_call(functools.partial(final_kernel, count, g, loss_scale), out...  9.94 us
    pallas_call x1, Pallas kernels, body(): pl.pallas_call(functools.partial(attention_kernel, count, per_kv, count <...  9.2 us
    unnamed x31, local copies, waits for them, and re-layouts  6.25 us
    ppermute x3, starting transfers between devices, body(): up = lax.ppermute(up, 'ctx', [(d, d + 1) for d in range(r - 1, last)])  6.25 us
    ppermute x6, starting transfers between devices, body(): lax.ppermute(q_send[g], 'ctx', [(count - r, count - r - 1)])  5.43 us
  transfers between devices with their start and end apart: 26, of which 5 were waited for; matrix products, arithmetic and copies ran while one was open for 1% of the time, Pallas kernels for 26%

profile of v1, /device:TPU:0, one launch (start us, length us, event | category | flops | bytes accessed | tf_op | source)
XLA Modules:
  0.0 94.6 jit_solution(2093291609208589601)
XLA Ops:
  0.6 1.7 %pack_kv.1 = (bf16[256,512]{1,0:T(8,128)(2,1)}, bf16[128,512]{1,0:T(8,128)(2,1)}) custom-call(bf16[256,256]{1,0:T(8,128)(2,1)} %bitcast.33, bf16[256,256]{1,0:T(8,128)(2,1)} %bitcast.35), custom_call_target="tpu_custom_call" | custom-call | bytes 393216 | tf_op jit(solution)/shard_map/pack_kv/pallas_call | solution.py:395
  2.4 4.9 %collective-permute-start = (bf16[128,512]{1,0:T(8,128)(2,1)}, bf16[128,512]{1,0:T(8,128)(2,1)S(1)}, u32[]{:S(2)}, u32[]{:S(2)}) collective-permute-start(bf16[128,512]{1,0:T(8,128)(2,1)} %get-tuple-element.29), channel_id=1, source_target_pairs={{0,4},{4,8},{8,12},{1,5},{5,9},{9,13},{2,6},{6,10},{10,14},{3,7},{... | collective-permute-start | bytes 393224 | tf_op jit(solution)/shard_map/ppermute | solution.py:409
  7.3 0.9 copy.18
  8.2 1.2 %copy-done = bf16[1,256,2048]{2,1,0:T(8,128)(2,1)S(1)} copy-done((bf16[1,256,2048]{2,1,0:T(8,128)(2,1)S(1)}, bf16[1,256,2048]{2,1,0:T(8,128)(2,1)}, u32[]{:S(2)}) %copy-start) | copy-done | bytes 1048600
  9.4 0.9 copy-done.5
  10.3 0.7 copy-done.9
  11.0 0.7 copy-done.11
  11.6 0.7 copy-done.12
  12.3 2.3 %summaries.1 = (bf16[256,2048]{1,0:T(8,128)(2,1)S(1)}, f32[256,32]{1,0:T(8,128)S(1)}, f32[8,2048]{1,0:T(8,128)S(1)}, bf16[128,1024]{1,0:T(8,128)(2,1)S(1)}, bf16...) custom-call(s32[1,1024]{1,0:T(1,128)S(1)} %copy-done.9, ...), custom_call_target="tpu_custom_call" | custom-call | flops 268435456 | bytes 4194304 | tf_op jit(solution)/shard_map/summaries/pallas_call | solution.py:416
  14.7 3.5 %collective-permute-start.12 = (bf16[128,1024]{1,0:T(8,128)(2,1)S(1)}, bf16[128,1024]{1,0:T(8,128)(2,1)S(1)}, u32[]{:S(2)}, u32[]{:S(2)}) collective-permute-start(bf16[128,1024]{1,0:T(8,128)(2,1)S(1)} %get-tuple-element.43.f_ref), channel_id=1, source_target_pairs={{0,4},{1,5},{2,6},{3,7},{16,20},{17,21},{18,22},{19,23}} | collective-permute-start | bytes 786440 | tf_op jit(solution)/shard_map/ppermute | solution.py:469
  18.1 0.7 collective-permute-start.13
  18.8 1.3 %collective-permute-start.3 = (bf16[256,512]{1,0:T(8,128)(2,1)}, bf16[256,512]{1,0:T(8,128)(2,1)S(1)}, u32[]{:S(2)}, u32[]{:S(2)}) collective-permute-start(bf16[256,512]{1,0:T(8,128)(2,1)} %get-tuple-element.30), channel_id=1, source_target_pairs={{4,0},{8,4},{12,8},{5,1},{9,5},{13,9},{6,2},{10,6},{14,10},{7,3},{... | collective-permute-start | bytes 786440 | tf_op jit(solution)/shard_map/ppermute | solution.py:410
  20.1 0.7 collective-permute-start.7
  20.8 4.6 %collective-permute-start.6 = (bf16[128,1024]{1,0:T(8,128)(2,1)S(1)}, bf16[128,1024]{1,0:T(8,128)(2,1)S(1)}, u32[]{:S(2)}, u32[]{:S(2)}) collective-permute-start(bf16[128,1024]{1,0:T(8,128)(2,1)S(1)} %get-tuple-element.35.f_ref), channel_id=1, source_target_pairs={{0,4},{1,5},{2,6},{3,7},{16,20},{17,21},{18,22},{19,23}} | collective-permute-start | bytes 786440 | tf_op jit(solution)/shard_map/ppermute | solution.py:469
  25.4 0.7 collective-permute-start.1
  26.1 2.3 %collective-permute-done.3.refs_3_ = bf16[256,512]{1,0:T(8,128)(2,1)S(1)} collective-permute-done((bf16[256,512]{1,0:T(8,128)(2,1)}, bf16[256,512]{1,0:T(8,128)(2,1)S(1)}, u32[]{:S(2)}, u32[]{:S(2)}) %collective-permute-start.3) | collective-permute-done | bytes 262176 | tf_op jit(solution)/shard_map/ppermute | solution.py:410
  28.4 1.3 %collective-permute-start.4 = (bf16[256,512]{1,0:T(8,128)(2,1)S(1)}, bf16[256,512]{1,0:T(8,128)(2,1)S(1)}, u32[]{:S(2)}, u32[]{:S(2)}) collective-permute-start(bf16[256,512]{1,0:T(8,128)(2,1)S(1)} %collective-permute-done.3.refs_3_), channel_id=1, source_target_pairs={{4,0},{8,4},{5,1},{9,5},{6,2},{10,6},{7,3},{11,7},{20,16},{24,20},... | collective-permute-start | bytes 786440 | tf_op jit(solution)/shard_map/ppermute | solution.py:410
  29.8 0.4 chain.6
  30.1 0.7 collective-permute-start.14
  30.8 0.7 collective-permute-start.15
  31.5 0.4 chain.4
  31.9 0.7 collective-permute-start.9
  32.6 0.7 collective-permute-start.8
  33.3 3.6 %collective-permute-done.4.refs_4_ = bf16[256,512]{1,0:T(8,128)(2,1)S(1)} collective-permute-done((bf16[256,512]{1,0:T(8,128)(2,1)S(1)}, bf16[256,512]{1,0:T(8,128)(2,1)S(1)}, u32[]{:S(2)}, u32[]{:S(2)}) %collective-permute-start.4) | collective-permute-done | bytes 262176 | tf_op jit(solution)/shard_map/ppermute | solution.py:410
  36.9 0.7 collective-permute-start.2
  37.6 1.3 %collective-permute-start.5 = (bf16[256,512]{1,0:T(8,128)(2,1)S(1)}, bf16[256,512]{1,0:T(8,128)(2,1)S(1)}, u32[]{:S(2)}, u32[]{:S(2)}) collective-permute-start(bf16[256,512]{1,0:T(8,128)(2,1)S(1)} %collective-permute-done.4.refs_4_), channel_id=1, source_target_pairs={{4,0},{5,1},{6,2},{7,3},{20,16},{21,17},{22,18},{23,19}} | collective-permute-start | bytes 786440 | tf_op jit(solution)/shard_map/ppermute | solution.py:410
  39.3 1.4 %collective-permute-start.17 = (bf16[144,1024]{1,0:T(8,128)(2,1)S(1)}, bf16[144,1024]{1,0:T(8,128)(2,1)S(1)}, u32[]{:S(2)}, u32[]{:S(2)}) collective-permute-start(bf16[144,1024]{1,0:T(8,128)(2,1)S(1)} %get-tuple-element.49), channel_id=1, source_target_pairs={{4,0},{5,1},{6,2},{7,3},{20,16},{21,17},{22,18},{23,19}} | collective-permute-start | bytes 884744 | tf_op jit(solution)/shard_map/ppermute | solution.py:470
  40.7 0.4 chain.5
  41.1 1.3 %collective-permute-start.11 = (bf16[144,1024]{1,0:T(8,128)(2,1)S(1)}, bf16[144,1024]{1,0:T(8,128)(2,1)S(1)}, u32[]{:S(2)}, u32[]{:S(2)}) collective-permute-start(bf16[144,1024]{1,0:T(8,128)(2,1)S(1)} %get-tuple-element.42), channel_id=1, source_target_pairs={{4,0},{5,1},{6,2},{7,3},{20,16},{21,17},{22,18},{23,19}} | collective-permute-start | bytes 884744 | tf_op jit(solution)/shard_map/ppermute | solution.py:470
  42.4 0.7 collective-permute-start.16
  43.1 0.9 collective-permute-start.10
  44.0 1.9 %local.1 = (f32[256,2048]{1,0:T(8,128)S(1)}, f32[256,2048]{1,0:T(8,128)S(1)}) custom-call(s32[1,1024]{1,0:T(1,128)S(1)} %copy-done.9, bf16[256,2048]{1,0:T(8,128)(2,1)S(1)} %bitcast.21, bf16[256,2048]{1,0:T(8,128)(2,1)S(1)} %get-tuple-element.31.xw_ref, bf16[256,256]{1,0:T(8,128)(2,1)S(1)} %bitcast.31, bf16[256,256]{1,0:T(8,128)(2,1)S(1)} %bitcast.27, ...), custom_call_target="tpu_custom_call" | custom-call | flops 268435456 | bytes 6291456 | tf_op jit(solution)/shard_map/local/pallas_call | solution.py:474
  45.9 10.5 %collective-permute-done.5.refs_5_ = bf16[256,512]{1,0:T(8,128)(2,1)S(1)} collective-permute-done((bf16[256,512]{1,0:T(8,128)(2,1)S(1)}, bf16[256,512]{1,0:T(8,128)(2,1)S(1)}, u32[]{:S(2)}, u32[]{:S(2)}) %collective-permute-start.5) | collective-permute-done | bytes 262176 | tf_op jit(solution)/shard_map/ppermute | solution.py:410
  56.4 9.2 %attention.1.teacher_ref = bf16[256,2048]{1,0:T(8,128)(2,1)} custom-call(s32[1,1024]{1,0:T(1,128)S(1)} %copy-done.10, bf16[256,2048]{1,0:T(8,128)(2,1)S(1)} %bitcast.42, bf16[256,256]{1,0:T(8,128)(2,1)S(1)} %bitcast.34, bf16[256,256]{1,0:T(8,128)(2,1)S(1)} %bitcast.36, bf16[128,512]{1,0:T(8,128)(2,1)S(1)} %collective-permute-done.refs_0_, ...), custom_call_target="tpu_custom_call" | custom-call | flops 1207959552 | bytes 4194304 | tf_op jit(solution)/shard_map/attention/pallas_call | solution.py:495
  65.7 1.2 %copy-done.3 = bf16[256,2048]{1,0:T(8,128)(2,1)S(1)} copy-done((bf16[256,2048]{1,0:T(8,128)(2,1)S(1)}, bf16[256,2048]{1,0:T(8,128)(2,1)}, u32[]{:S(2)}) %copy-start.3) | copy-done | bytes 1048600
  66.9 5.0 %final.2 = (bf16[256,2048]{1,0:T(8,128)(2,1)}, f32[2,1024]{1,0:T(2,128)S(1)}) custom-call(f32[256,2048]{1,0:T(8,128)S(1)} %get-tuple-element.33.pre_ref, f32[256,2048]{1,0:T(8,128)S(1)} %get-tuple-element.34.reach_ref, bf16[256,256]{1,0:T(8,128)(2,1)S(1)} %bitcast.28, bf16[256,2048]{1,0:T(8,128)(2,1)S(1)} %bitcast.22, bf16[256,2048]{1,0:T(8,128)(2,1)S(1)} %bitcast.24, ...), custom_call_target="tpu_custom_call" | custom-call | flops 67108864 | bytes 5242880 | tf_op jit(solution)/shard_map/final/pallas_call | solution.py:531
  71.8 3.0 %collective-permute-start.18 = (f32[2,1024]{1,0:T(2,128)S(1)}, f32[2,1024]{1,0:T(2,128)S(1)}, u32[]{:S(2)}, u32[]{:S(2)}) collective-permute-start(f32[2,1024]{1,0:T(2,128)S(1)} %get-tuple-element.52), channel_id=1, source_target_pairs={{0,4},{4,0},{8,12},{12,8},{1,5},{5,1},{9,13},{13,9},{2,6},{6,2},{1... | collective-permute-start | bytes 24584 | tf_op jit(solution)/shard_map/ppermute | solution.py:356
  74.8 2.4 %collective-permute-start.20 = (f32[2,1024]{1,0:T(2,128)S(1)}, f32[2,1024]{1,0:T(2,128)S(1)}, u32[]{:S(2)}, u32[]{:S(2)}) collective-permute-start(f32[2,1024]{1,0:T(2,128)S(1)} %get-tuple-element.52), channel_id=1, source_target_pairs={{0,12},{4,8},{8,4},{12,0},{1,13},{5,9},{9,5},{13,1},{2,14},{6,10},... | collective-permute-start | bytes 24584 | tf_op jit(solution)/shard_map/ppermute | solution.py:356
  77.2 5.0 %final.3 = (bf16[256,2048]{1,0:T(8,128)(2,1)}, f32[2,1024]{1,0:T(2,128)S(1)}) custom-call(f32[256,2048]{1,0:T(8,128)S(1)} %get-tuple-element.33.pre_ref, f32[256,2048]{1,0:T(8,128)S(1)} %get-tuple-element.34.reach_ref, bf16[256,256]{1,0:T(8,128)(2,1)S(1)} %bitcast.29, bf16[256,2048]{1,0:T(8,128)(2,1)S(1)} %bitcast.23, ...), custom_call_target="tpu_custom_call", output_to_operand_aliasing={{0}: (15, {})} | custom-call | flops 67108864 | bytes 5242880 | tf_op jit(solution)/shard_map/final/pallas_call | solution.py:531
  82.2 1.1 %collective-permute-start.22 = (f32[2,1024]{1,0:T(2,128)S(1)}, f32[2,1024]{1,0:T(2,128)S(1)}, u32[]{:S(2)}, u32[]{:S(2)}) collective-permute-start(f32[2,1024]{1,0:T(2,128)S(1)} %get-tuple-element.53), channel_id=1, source_target_pairs={{0,4},{4,0},{8,12},{12,8},{1,5},{5,1},{9,13},{13,9},{2,6},{6,2},{1... | collective-permute-start | bytes 24584 | tf_op jit(solution)/shard_map/ppermute | solution.py:356
  83.3 0.9 collective-permute-start.23
  84.2 2.4 %collective-permute-start.24 = (f32[2,1024]{1,0:T(2,128)S(1)}, f32[2,1024]{1,0:T(2,128)S(1)}, u32[]{:S(2)}, u32[]{:S(2)}) collective-permute-start(f32[2,1024]{1,0:T(2,128)S(1)} %get-tuple-element.53), channel_id=1, source_target_pairs={{0,12},{4,8},{8,4},{12,0},{1,13},{5,9},{9,5},{13,1},{2,14},{6,10},... | collective-permute-start | bytes 24584 | tf_op jit(solution)/shard_map/ppermute | solution.py:356
  86.6 1.6 %collective-permute-start.21 = (f32[2,1024]{1,0:T(2,128)S(1)}, f32[2,1024]{1,0:T(2,128)S(1)}, u32[]{:S(2)}, u32[]{:S(2)}) collective-permute-start(f32[2,1024]{1,0:T(2,128)S(1)} %add_add_fusion.1), channel_id=1, source_target_pairs={{0,16},{16,0},{1,17},{17,1},{2,18},{18,2},{3,19},{19,3},{4,20},{20... | collective-permute-start | bytes 24584 | tf_op jit(solution)/shard_map/ppermute | solution.py:356
  88.2 1.5 %collective-permute-done.24 = f32[2,1024]{1,0:T(2,128)S(1)} collective-permute-done((f32[2,1024]{1,0:T(2,128)S(1)}, f32[2,1024]{1,0:T(2,128)S(1)}, u32[]{:S(2)}, u32[]{:S(2)}) %collective-permute-start.24) | collective-permute-done | bytes 8224 | tf_op jit(solution)/shard_map/ppermute | solution.py:356
  89.7 1.6 %collective-permute-start.25 = (f32[2,1024]{1,0:T(2,128)S(1)}, f32[2,1024]{1,0:T(2,128)S(1)}, u32[]{:S(2)}, u32[]{:S(2)}) collective-permute-start(f32[2,1024]{1,0:T(2,128)S(1)} %add_add_fusion), channel_id=1, source_target_pairs={{0,16},{16,0},{1,17},{17,1},{2,18},{18,2},{3,19},{19,3},{4,20},{20... | collective-permute-start | bytes 24584 | tf_op jit(solution)/shard_map/ppermute | solution.py:356
  91.3 2.1 %collective-permute-done.25 = f32[2,1024]{1,0:T(2,128)S(1)} collective-permute-done((f32[2,1024]{1,0:T(2,128)S(1)}, f32[2,1024]{1,0:T(2,128)S(1)}, u32[]{:S(2)}, u32[]{:S(2)}) %collective-permute-start.25) | collective-permute-done | bytes 8224 | tf_op jit(solution)/shard_map/ppermute | solution.py:356
  93.4 0.6 pad_maximum_fusion.1
  94.0 0.6 pad_maximum_fusion
  (55 shorter events, 0.5 us)
Async XLA Ops:
  2.4 18.5 %collective-permute-start = (bf16[128,512]{1,0:T(8,128)(2,1)}, bf16[128,512]{1,0:T(8,128)(2,1)S(1)}, u32[]{:S(2)}, u32[]{:S(2)}) collective-permute-start(bf16[128,512]{1,0:T(8,128)(2,1)} %get-tuple-element.29), channel_id=1, source_target_pairs={{0,4},{4,8},{8,12},{1,5},{5,9},{9,13},{2,6},{6,10},{10,14},{3,7},{... | collective-permute-start | bytes 393224 | tf_op jit(solution)/shard_map/ppermute | solution.py:409
  8.2 1.2 %copy-start = (bf16[1,256,2048]{2,1,0:T(8,128)(2,1)S(1)}, bf16[1,256,2048]{2,1,0:T(8,128)(2,1)}, u32[]{:S(2)}) copy-start(bf16[1,256,2048]{2,1,0:T(8,128)(2,1)} %param.17) | copy-start | bytes 3145732
  9.4 0.9 copy-start.5
  10.3 0.7 copy-start.9
  11.0 0.7 copy-start.11
  11.6 0.7 copy-start.12
  14.7 10.8 %collective-permute-start.12 = (bf16[128,1024]{1,0:T(8,128)(2,1)S(1)}, bf16[128,1024]{1,0:T(8,128)(2,1)S(1)}, u32[]{:S(2)}, u32[]{:S(2)}) collective-permute-start(bf16[128,1024]{1,0:T(8,128)(2,1)S(1)} %get-tuple-element.43.f_ref), channel_id=1, source_target_pairs={{0,4},{1,5},{2,6},{3,7},{16,20},{17,21},{18,22},{19,23}} | collective-permute-start | bytes 786440 | tf_op jit(solution)/shard_map/ppermute | solution.py:469
  18.1 11.6 %collective-permute-start.13 = (bf16[144,1024]{1,0:T(8,128)(2,1)S(1)}, bf16[144,1024]{1,0:T(8,128)(2,1)S(1)}, u32[]{:S(2)}, u32[]{:S(2)}) collective-permute-start(bf16[144,1024]{1,0:T(8,128)(2,1)S(1)} %get-tuple-element.44), channel_id=1, source_target_pairs={{12,8},{13,9},{14,10},{15,11},{28,24},{29,25},{30,26},{31,27}} | collective-permute-start | bytes 884744 | tf_op jit(solution)/shard_map/ppermute | solution.py:470
  18.8 9.6 %collective-permute-start.3 = (bf16[256,512]{1,0:T(8,128)(2,1)}, bf16[256,512]{1,0:T(8,128)(2,1)S(1)}, u32[]{:S(2)}, u32[]{:S(2)}) collective-permute-start(bf16[256,512]{1,0:T(8,128)(2,1)} %get-tuple-element.30), channel_id=1, source_target_pairs={{4,0},{8,4},{12,8},{5,1},{9,5},{13,9},{6,2},{10,6},{14,10},{7,3},{... | collective-permute-start | bytes 786440 | tf_op jit(solution)/shard_map/ppermute | solution.py:410
  20.1 11.4 %collective-permute-start.7 = (bf16[144,1024]{1,0:T(8,128)(2,1)S(1)}, bf16[144,1024]{1,0:T(8,128)(2,1)S(1)}, u32[]{:S(2)}, u32[]{:S(2)}) collective-permute-start(bf16[144,1024]{1,0:T(8,128)(2,1)S(1)} %get-tuple-element.37), channel_id=1, source_target_pairs={{12,8},{13,9},{14,10},{15,11},{28,24},{29,25},{30,26},{31,27}} | collective-permute-start | bytes 884744 | tf_op jit(solution)/shard_map/ppermute | solution.py:470
  20.8 10.0 %collective-permute-start.6 = (bf16[128,1024]{1,0:T(8,128)(2,1)S(1)}, bf16[128,1024]{1,0:T(8,128)(2,1)S(1)}, u32[]{:S(2)}, u32[]{:S(2)}) collective-permute-start(bf16[128,1024]{1,0:T(8,128)(2,1)S(1)} %get-tuple-element.35.f_ref), channel_id=1, source_target_pairs={{0,4},{1,5},{2,6},{3,7},{16,20},{17,21},{18,22},{19,23}} | collective-permute-start | bytes 786440 | tf_op jit(solution)/shard_map/ppermute | solution.py:469
  25.4 7.2 %collective-permute-start.1 = (bf16[128,512]{1,0:T(8,128)(2,1)S(1)}, bf16[128,512]{1,0:T(8,128)(2,1)S(1)}, u32[]{:S(2)}, u32[]{:S(2)}) collective-permute-start(bf16[128,512]{1,0:T(8,128)(2,1)S(1)} %collective-permute-done.refs_0_), channel_id=1, source_target_pairs={{4,8},{8,12},{5,9},{9,13},{6,10},{10,14},{7,11},{11,15},{20,24},{2... | collective-permute-start | bytes 393224 | tf_op jit(solution)/shard_map/ppermute | solution.py:409
  28.4 8.4 %collective-permute-start.4 = (bf16[256,512]{1,0:T(8,128)(2,1)S(1)}, bf16[256,512]{1,0:T(8,128)(2,1)S(1)}, u32[]{:S(2)}, u32[]{:S(2)}) collective-permute-start(bf16[256,512]{1,0:T(8,128)(2,1)S(1)} %collective-permute-done.3.refs_3_), channel_id=1, source_target_pairs={{4,0},{8,4},{5,1},{9,5},{6,2},{10,6},{7,3},{11,7},{20,16},{24,20},... | collective-permute-start | bytes 786440 | tf_op jit(solution)/shard_map/ppermute | solution.py:410
  29.7 14.2 %copy-start.4 = (bf16[1,256,256]{2,1,0:T(8,128)(2,1)S(1)}, bf16[1,256,256]{2,1,0:T(8,128)(2,1)}, u32[]{:S(2)}) copy-start(bf16[1,256,256]{2,1,0:T(8,128)(2,1)} %param.20) | copy-start | bytes 393220
  29.7 14.2 %copy-start.13 = (f32[32]{0:T(128)S(1)}, f32[32]{0:T(128)}, u32[]{:S(2)}) copy-start(f32[32]{0:T(128)} %param.24) | copy-start | bytes 388
  30.1 7.4 %collective-permute-start.14 = (bf16[128,1024]{1,0:T(8,128)(2,1)S(1)}, bf16[128,1024]{1,0:T(8,128)(2,1)S(1)}, u32[]{:S(2)}, u32[]{:S(2)}) collective-permute-start(bf16[128,1024]{1,0:T(8,128)(2,1)S(1)} %get-tuple-element.46), channel_id=1, source_target_pairs={{4,8},{5,9},{6,10},{7,11},{20,24},{21,25},{22,26},{23,27}} | collective-permute-start | bytes 786440 | tf_op jit(solution)/shard_map/ppermute | solution.py:469
  30.8 8.0 %collective-permute-start.15 = (bf16[144,1024]{1,0:T(8,128)(2,1)S(1)}, bf16[144,1024]{1,0:T(8,128)(2,1)S(1)}, u32[]{:S(2)}, u32[]{:S(2)}) collective-permute-start(bf16[144,1024]{1,0:T(8,128)(2,1)S(1)} %get-tuple-element.47), channel_id=1, source_target_pairs={{8,4},{9,5},{10,6},{11,7},{24,20},{25,21},{26,22},{27,23}} | collective-permute-start | bytes 884744 | tf_op jit(solution)/shard_map/ppermute | solution.py:470
  31.9 8.8 %collective-permute-start.9 = (bf16[144,1024]{1,0:T(8,128)(2,1)S(1)}, bf16[144,1024]{1,0:T(8,128)(2,1)S(1)}, u32[]{:S(2)}, u32[]{:S(2)}) collective-permute-start(bf16[144,1024]{1,0:T(8,128)(2,1)S(1)} %get-tuple-element.40), channel_id=1, source_target_pairs={{8,4},{9,5},{10,6},{11,7},{24,20},{25,21},{26,22},{27,23}} | collective-permute-start | bytes 884744 | tf_op jit(solution)/shard_map/ppermute | solution.py:470
  32.6 8.1 %collective-permute-start.8 = (bf16[128,1024]{1,0:T(8,128)(2,1)S(1)}, bf16[128,1024]{1,0:T(8,128)(2,1)S(1)}, u32[]{:S(2)}, u32[]{:S(2)}) collective-permute-start(bf16[128,1024]{1,0:T(8,128)(2,1)S(1)} %get-tuple-element.39), channel_id=1, source_target_pairs={{4,8},{5,9},{6,10},{7,11},{20,24},{21,25},{22,26},{23,27}} | collective-permute-start | bytes 786440 | tf_op jit(solution)/shard_map/ppermute | solution.py:469
  36.9 6.2 %collective-permute-start.2 = (bf16[128,512]{1,0:T(8,128)(2,1)S(1)}, bf16[128,512]{1,0:T(8,128)(2,1)S(1)}, u32[]{:S(2)}, u32[]{:S(2)}) collective-permute-start(bf16[128,512]{1,0:T(8,128)(2,1)S(1)} %collective-permute-done.1.refs_1_), channel_id=1, source_target_pairs={{8,12},{9,13},{10,14},{11,15},{24,28},{25,29},{26,30},{27,31}} | collective-permute-start | bytes 393224 | tf_op jit(solution)/shard_map/ppermute | solution.py:409
  37.6 18.8 %collective-permute-start.5 = (bf16[256,512]{1,0:T(8,128)(2,1)S(1)}, bf16[256,512]{1,0:T(8,128)(2,1)S(1)}, u32[]{:S(2)}, u32[]{:S(2)}) collective-permute-start(bf16[256,512]{1,0:T(8,128)(2,1)S(1)} %collective-permute-done.4.refs_4_), channel_id=1, source_target_pairs={{4,0},{5,1},{6,2},{7,3},{20,16},{21,17},{22,18},{23,19}} | collective-permute-start | bytes 786440 | tf_op jit(solution)/shard_map/ppermute | solution.py:410
  39.2 17.1 %copy-start.6 = (bf16[1,256,256]{2,1,0:T(8,128)(2,1)S(1)}, bf16[1,256,256]{2,1,0:T(8,128)(2,1)}, u32[]{:S(2)}) copy-start(bf16[1,256,256]{2,1,0:T(8,128)(2,1)} %param.14) | copy-start | bytes 393220
  39.2 17.1 %copy-start.7 = (bf16[1,256,256]{2,1,0:T(8,128)(2,1)S(1)}, bf16[1,256,256]{2,1,0:T(8,128)(2,1)}, u32[]{:S(2)}) copy-start(bf16[1,256,256]{2,1,0:T(8,128)(2,1)} %param.15) | copy-start | bytes 393220
  39.3 17.1 %copy-start.10 = (s32[1,1024]{1,0:T(1,128)S(1)}, s32[1,1024]{1,0:T(1,128)}, u32[]{:S(2)}) copy-start(s32[1,1024]{1,0:T(1,128)} %docs_ref.5) | copy-start | bytes 12292
  39.3 17.1 %copy-start.14 = (bf16[1,256,2048]{2,1,0:T(8,128)(2,1)S(1)}, bf16[1,256,2048]{2,1,0:T(8,128)(2,1)}, u32[]{:S(2)}) copy-start(bf16[1,256,2048]{2,1,0:T(8,128)(2,1)} %param.13) | copy-start | bytes 3145732
  39.3 26.3 %collective-permute-start.17 = (bf16[144,1024]{1,0:T(8,128)(2,1)S(1)}, bf16[144,1024]{1,0:T(8,128)(2,1)S(1)}, u32[]{:S(2)}, u32[]{:S(2)}) collective-permute-start(bf16[144,1024]{1,0:T(8,128)(2,1)S(1)} %get-tuple-element.49), channel_id=1, source_target_pairs={{4,0},{5,1},{6,2},{7,3},{20,16},{21,17},{22,18},{23,19}} | collective-permute-start | bytes 884744 | tf_op jit(solution)/shard_map/ppermute | solution.py:470
  41.1 36.1 %collective-permute-start.11 = (bf16[144,1024]{1,0:T(8,128)(2,1)S(1)}, bf16[144,1024]{1,0:T(8,128)(2,1)S(1)}, u32[]{:S(2)}, u32[]{:S(2)}) collective-permute-start(bf16[144,1024]{1,0:T(8,128)(2,1)S(1)} %get-tuple-element.42), channel_id=1, source_target_pairs={{4,0},{5,1},{6,2},{7,3},{20,16},{21,17},{22,18},{23,19}} | collective-permute-start | bytes 884744 | tf_op jit(solution)/shard_map/ppermute | solution.py:470
  42.4 23.2 %collective-permute-start.16 = (bf16[128,1024]{1,0:T(8,128)(2,1)S(1)}, bf16[128,1024]{1,0:T(8,128)(2,1)S(1)}, u32[]{:S(2)}, u32[]{:S(2)}) collective-permute-start(bf16[128,1024]{1,0:T(8,128)(2,1)S(1)} %get-tuple-element.48), channel_id=1, source_target_pairs={{8,12},{9,13},{10,14},{11,15},{24,28},{25,29},{26,30},{27,31}} | collective-permute-start | bytes 786440 | tf_op jit(solution)/shard_map/ppermute | solution.py:469
  43.1 34.1 %collective-permute-start.10 = (bf16[128,1024]{1,0:T(8,128)(2,1)S(1)}, bf16[128,1024]{1,0:T(8,128)(2,1)S(1)}, u32[]{:S(2)}, u32[]{:S(2)}) collective-permute-start(bf16[128,1024]{1,0:T(8,128)(2,1)S(1)} %get-tuple-element.41), channel_id=1, source_target_pairs={{8,12},{9,13},{10,14},{11,15},{24,28},{25,29},{26,30},{27,31}} | collective-permute-start | bytes 786440 | tf_op jit(solution)/shard_map/ppermute | solution.py:469
  56.4 9.2 %copy-start.1 = (bf16[1,256,2048]{2,1,0:T(8,128)(2,1)S(1)}, bf16[1,256,2048]{2,1,0:T(8,128)(2,1)}, u32[]{:S(2)}) copy-start(bf16[1,256,2048]{2,1,0:T(8,128)(2,1)} %param.17) | copy-start | bytes 3145732
  56.4 9.2 %copy-start.2 = (bf16[1,256,2048]{2,1,0:T(8,128)(2,1)S(1)}, bf16[1,256,2048]{2,1,0:T(8,128)(2,1)}, u32[]{:S(2)}) copy-start(bf16[1,256,2048]{2,1,0:T(8,128)(2,1)} %param.18) | copy-start | bytes 3145732
  56.4 9.2 %copy-start.8 = (f32[2048]{0:T(1024)S(1)}, f32[2048]{0:T(1024)}, u32[]{:S(2)}) copy-start(f32[2048]{0:T(1024)} %param.25) | copy-start | bytes 24580
  65.6 1.2 %copy-start.3 = (bf16[256,2048]{1,0:T(8,128)(2,1)S(1)}, bf16[256,2048]{1,0:T(8,128)(2,1)}, u32[]{:S(2)}) copy-start(bf16[256,2048]{1,0:T(8,128)(2,1)} %attention.1.teacher_ref) | copy-start | bytes 3145732
  71.8 12.4 %collective-permute-start.18 = (f32[2,1024]{1,0:T(2,128)S(1)}, f32[2,1024]{1,0:T(2,128)S(1)}, u32[]{:S(2)}, u32[]{:S(2)}) collective-permute-start(f32[2,1024]{1,0:T(2,128)S(1)} %get-tuple-element.52), channel_id=1, source_target_pairs={{0,4},{4,0},{8,12},{12,8},{1,5},{5,1},{9,13},{13,9},{2,6},{6,2},{1... | collective-permute-start | bytes 24584 | tf_op jit(solution)/shard_map/ppermute | solution.py:356
  74.8 11.7 %collective-permute-start.19 = (f32[2,1024]{1,0:T(2,128)S(1)}, f32[2,1024]{1,0:T(2,128)S(1)}, u32[]{:S(2)}, u32[]{:S(2)}) collective-permute-start(f32[2,1024]{1,0:T(2,128)S(1)} %get-tuple-element.52), channel_id=1, source_target_pairs={{0,8},{4,12},{8,0},{12,4},{1,9},{5,13},{9,1},{13,5},{2,10},{6,14},... | collective-permute-start | bytes 24584 | tf_op jit(solution)/shard_map/ppermute | solution.py:356
  74.8 11.7 %collective-permute-start.20 = (f32[2,1024]{1,0:T(2,128)S(1)}, f32[2,1024]{1,0:T(2,128)S(1)}, u32[]{:S(2)}, u32[]{:S(2)}) collective-permute-start(f32[2,1024]{1,0:T(2,128)S(1)} %get-tuple-element.52), channel_id=1, source_target_pairs={{0,12},{4,8},{8,4},{12,0},{1,13},{5,9},{9,5},{13,1},{2,14},{6,10},... | collective-permute-start | bytes 24584 | tf_op jit(solution)/shard_map/ppermute | solution.py:356
  82.2 6.0 %collective-permute-start.22 = (f32[2,1024]{1,0:T(2,128)S(1)}, f32[2,1024]{1,0:T(2,128)S(1)}, u32[]{:S(2)}, u32[]{:S(2)}) collective-permute-start(f32[2,1024]{1,0:T(2,128)S(1)} %get-tuple-element.53), channel_id=1, source_target_pairs={{0,4},{4,0},{8,12},{12,8},{1,5},{5,1},{9,13},{13,9},{2,6},{6,2},{1... | collective-permute-start | bytes 24584 | tf_op jit(solution)/shard_map/ppermute | solution.py:356
  83.3 4.9 %collective-permute-start.23 = (f32[2,1024]{1,0:T(2,128)S(1)}, f32[2,1024]{1,0:T(2,128)S(1)}, u32[]{:S(2)}, u32[]{:S(2)}) collective-permute-start(f32[2,1024]{1,0:T(2,128)S(1)} %get-tuple-element.53), channel_id=1, source_target_pairs={{0,8},{4,12},{8,0},{12,4},{1,9},{5,13},{9,1},{13,5},{2,10},{6,14},... | collective-permute-start | bytes 24584 | tf_op jit(solution)/shard_map/ppermute | solution.py:356
  84.2 5.4 %collective-permute-start.24 = (f32[2,1024]{1,0:T(2,128)S(1)}, f32[2,1024]{1,0:T(2,128)S(1)}, u32[]{:S(2)}, u32[]{:S(2)}) collective-permute-start(f32[2,1024]{1,0:T(2,128)S(1)} %get-tuple-element.53), channel_id=1, source_target_pairs={{0,12},{4,8},{8,4},{12,0},{1,13},{5,9},{9,5},{13,1},{2,14},{6,10},... | collective-permute-start | bytes 24584 | tf_op jit(solution)/shard_map/ppermute | solution.py:356
  86.6 4.7 %collective-permute-start.21 = (f32[2,1024]{1,0:T(2,128)S(1)}, f32[2,1024]{1,0:T(2,128)S(1)}, u32[]{:S(2)}, u32[]{:S(2)}) collective-permute-start(f32[2,1024]{1,0:T(2,128)S(1)} %add_add_fusion.1), channel_id=1, source_target_pairs={{0,16},{16,0},{1,17},{17,1},{2,18},{18,2},{3,19},{19,3},{4,20},{20... | collective-permute-start | bytes 24584 | tf_op jit(solution)/shard_map/ppermute | solution.py:356
  89.7 3.7 %collective-permute-start.25 = (f32[2,1024]{1,0:T(2,128)S(1)}, f32[2,1024]{1,0:T(2,128)S(1)}, u32[]{:S(2)}, u32[]{:S(2)}) collective-permute-start(f32[2,1024]{1,0:T(2,128)S(1)} %add_add_fusion), channel_id=1, source_target_pairs={{0,16},{16,0},{1,17},{17,1},{2,18},{18,2},{3,19},{19,3},{4,20},{20... | collective-permute-start | bytes 24584 | tf_op jit(solution)/shard_map/ppermute | solution.py:356

commit v2 on v0

v2 whole, which is shorter than its diff:
```python
import functools
import math

import jax
import jax.numpy as jnp
from jax import lax
from jax.experimental import pallas as pl
from jax.experimental.pallas import tpu as pltpu
from jax.sharding import PartitionSpec as P

DH = 128
P_SIZE = 64
N = 128
EXTRA = 16
EPS = 1e-05
MASKED = -1e30
F32 = jnp.float32
BF16 = jnp.bfloat16
VMEM = pl.BlockSpec(memory_space=pltpu.VMEM)


def params(mib):
    return pltpu.CompilerParams(vmem_limit_bytes=mib << 20)


def cost(flops, size):
    return pl.CostEstimate(flops=flops, bytes_accessed=size, transcendentals=0)


def parts(v):
    hi = v.astype(BF16)
    return hi, (v - hi.astype(F32)).astype(BF16)


def spread_matrix(heads, width, first):
    row = lax.broadcasted_iota(jnp.int32, (heads, width), 0)
    lane = lax.broadcasted_iota(jnp.int32, (heads, width), 1)
    return jnp.where(row == (lane // P_SIZE) + first, 1.0, 0.0).astype(BF16)


def dot_nt(a, b):
    return lax.dot_general(a, b, (((1,), (1,)), ((), ())), preferred_element_type=F32)


def dot_tn(a, b):
    return lax.dot_general(a, b, (((0,), (0,)), ((), ())), preferred_element_type=F32)


def spread(v, matrix):
    hi, lo = parts(v)
    return dot_tn(hi, matrix) + dot_tn(lo, matrix)


def doc_row(docs_ref, block, stretch):
    return docs_ref[:, pl.ds(pl.multiple_of(block * stretch, stretch), stretch)]


def as_column(row):
    size = row.shape[1]
    r = lax.broadcasted_iota(jnp.int32, (size, size), 0)
    c = lax.broadcasted_iota(jnp.int32, (size, size), 1)
    return jnp.sum(jnp.where(r == c, row.astype(F32), 0.0), axis=1, keepdims=True)


def lower_triangle(size):
    r = lax.broadcasted_iota(jnp.int32, (size, size), 0)
    c = lax.broadcasted_iota(jnp.int32, (size, size), 1)
    return r >= c


def prior_doc(docs_ref, block, stretch):
    before = doc_row(docs_ref, jnp.maximum(block - 1, 0), stretch)[:, stretch - 1 :]
    return jnp.where(block > 0, before, -1)


def own_block(index, count, half):
    return index if half == 0 else 2 * count - 1 - index


def ring_order(count):
    return [0] + list(range(1, count, 2)) + list(range(2, count, 2))[::-1]


def ring_source(index, count, steps):
    order = ring_order(count)
    source = jnp.int32(0)
    for place, member in enumerate(order):
        source = jnp.where(index == member, order[(place - steps) % count], source)
    return source


def put_state(ref, state):
    ref[:N, :] = state.astype(BF16)
    ref[N:, :] = jnp.zeros((EXTRA, ref.shape[1]), BF16)


def put_composite(ref, state, decay):
    hi, lo = parts(decay)
    ref[:N, :] = state.astype(BF16)
    ref[N:, :] = jnp.concatenate(
        [hi, lo, jnp.zeros((EXTRA - 2, ref.shape[1]), BF16)], axis=0
    )


def opening_kernel(
    count,
    groups,
    docs_ref,
    k_ref,
    v_ref,
    x_ref,
    b_ref,
    dt_ref,
    bias_ref,
    log_ref,
    kv_ref,
    ec_ref,
    *outs,
):
    xw_refs, dec_refs, f_refs, b_refs, send_refs = (
        outs[k * groups : (k + 1) * groups] for k in range(5)
    )
    heads, rows = dt_ref.shape
    stretch = rows // 2
    width = x_ref.shape[1] // groups
    kv_width = k_ref.shape[1]
    index = lax.axis_index("ctx")
    kv_ref[:, :kv_width] = k_ref[...]
    kv_ref[:, kv_width:] = v_ref[...]
    triangle = jnp.where(lower_triangle(stretch), 1.0, 0.0)
    slope = jnp.exp(as_column(log_ref[...]))
    bias = as_column(bias_ref[...])
    lane = lax.broadcasted_iota(jnp.int32, (heads, 8), 1)
    ends = jnp.zeros((heads, 8), F32)
    loads = []
    projs = []
    for half in range(2):
        block = own_block(index, count, half)
        sl = slice(half * stretch, (half + 1) * stretch)
        raw = dt_ref[:, sl] + bias
        dt = jnp.maximum(raw, 0.0) + jnp.log1p(jnp.exp(-jnp.abs(raw)))
        cum = lax.dot_general(
            -dt * slope,
            triangle,
            (((1,), (1,)), ((), ())),
            precision=lax.Precision.HIGHEST,
            preferred_element_type=F32,
        )
        ec_ref[:, sl] = jnp.exp(cum)
        loads.append(jnp.exp(-cum) * dt)
        final = jnp.exp(cum[:, stretch - 1 :])
        row = doc_row(docs_ref, block, stretch)
        last = row[:, stretch - 1 :]
        kept = jnp.where(last == prior_doc(docs_ref, block, stretch), 1.0, 0.0)
        ends = jnp.where(lane == half, final * kept, ends)
        ends = jnp.where(lane == 2 + half, final, ends)
        same = jnp.where(as_column(row) == last.astype(F32), 1.0, 0.0)
        projs.append((b_ref[sl, :].astype(F32) * same).astype(BF16))
    for g in range(groups):
        cols = slice(g * width, (g + 1) * width)
        matrix = spread_matrix(heads, width, g * (heads // groups))
        wide = spread(ends, matrix)
        dec_refs[g][...] = wide
        sums = []
        for half in range(2):
            sl = slice(half * stretch, (half + 1) * stretch)
            xw = (x_ref[sl, cols].astype(F32) * spread(loads[half], matrix)).astype(BF16)
            xw_refs[g][sl, :] = xw
            sums.append(dot_tn(projs[half][:, g * N : (g + 1) * N], xw) * wide[2 + half : 3 + half])
        f_refs[g][...] = sums[0].astype(BF16)
        b_refs[g][...] = sums[1].astype(BF16)

        @pl.when(index == 0)
        def _():
            put_state(send_refs[g], sums[0])

        @pl.when(index != 0)
        def _():
            put_composite(send_refs[g], wide[1:2] * sums[0] + sums[1], wide[0:1] * wide[1:2])


def chain_kernel(count, stage, got_ref, f_ref, b_ref, dec_ref, send_ref):
    index = lax.axis_index("ctx")

    @pl.when(index == stage)
    def _():
        state = dec_ref[0:1, :] * got_ref[:N, :].astype(F32) + f_ref[...].astype(F32)
        put_state(send_ref, state)

    @pl.when(index == count - 1 - stage)
    def _():
        decay = got_ref[N : N + 1, :].astype(F32) + got_ref[N + 1 : N + 2, :].astype(F32)
        inner = decay * f_ref[...].astype(F32) + got_ref[:N, :].astype(F32)
        state = dec_ref[1:2, :] * inner + b_ref[...].astype(F32)
        put_composite(send_ref, state, dec_ref[1:2, :] * decay * dec_ref[0:1, :])


def local_kernel(
    count,
    first,
    docs_ref,
    x_ref,
    gate_ref,
    b_ref,
    c_ref,
    ec_ref,
    skip_ref,
    xw_ref,
    pre_ref,
    reach_ref,
    sx_ref,
):
    heads, rows = ec_ref.shape
    stretch = rows // 2
    width = x_ref.shape[1]
    index = lax.axis_index("ctx")
    matrix = spread_matrix(heads, width, first)
    wide_skip = spread(as_column(skip_ref[...]), matrix)
    triangle = lower_triangle(stretch)
    step = 16
    for half in range(2):
        block = own_block(index, count, half)
        sl = slice(half * stretch, (half + 1) * stretch)
        row = doc_row(docs_ref, block, stretch)
        column = as_column(row)
        gram = dot_nt(c_ref[sl, :], b_ref[sl, :])
        gram = jnp.where(triangle & (column == row.astype(F32)), gram, 0.0).astype(BF16)
        wide = spread(ec_ref[:, sl], matrix)
        inner = jnp.dot(gram, xw_ref[sl, :], preferred_element_type=F32)
        reached = jnp.where(column == prior_doc(docs_ref, block, stretch).astype(F32), 1.0, 0.0)
        for k in range(0, stretch, step):
            at = slice(half * stretch + k, half * stretch + k + step)
            here = slice(k, k + step)
            x = x_ref[at, :].astype(F32)
            gate = gate_ref[at, :].astype(F32)
            silu = gate / (1.0 + jnp.exp(-gate))
            fade = wide[here] * silu
            sx = silu * x
            sx_ref[at, :] = sx
            pre_ref[at, :] = inner[here] * fade + wide_skip * sx
            reach_ref[at, :] = reached[here] * fade


def attention_kernel(count, per, stack, g, docs_ref, q_ref, k_ref, v_ref, *refs):
    others = count - 1
    got = refs[:others]
    out_ref, copy_ref = refs[-10:-8]
    kb, vb, ka, va, bias_b, bias_f, bias_a, best = refs[-8:]
    rows = q_ref.shape[0]
    stretch = rows // 2
    index = lax.axis_index("ctx")
    last = 2 * count - 1
    kv_width = got[0].shape[1] // 2
    k_cols = slice(g * DH, (g + 1) * DH)
    v_cols = slice(kv_width + g * DH, kv_width + (g + 1) * DH)
    row_f = doc_row(docs_ref, index, stretch).astype(F32)
    row_b = doc_row(docs_ref, last - index, stretch).astype(F32)
    col_f = as_column(row_f)
    col_b = as_column(row_b)
    triangle = lower_triangle(stretch)
    bias_f[...] = jnp.where(triangle & (col_f == row_f), 0.0, MASKED)
    bias_b[:, :stretch] = jnp.where(col_b == row_f, 0.0, MASKED)
    bias_b[:, stretch:rows] = jnp.where(triangle & (col_b == row_b), 0.0, MASKED)
    vb[:, DH:] = jnp.ones((vb.shape[0], DH), BF16)
    va[:, DH:] = jnp.ones((va.shape[0], DH), BF16)
    kb[:rows, :] = k_ref[...]
    vb[:rows, :DH] = v_ref[...]
    lower, at_a, picks = [], [], []
    for r in range(others):
        at_b = slice(rows + r * stretch, rows + (r + 1) * stretch)
        at_a.append(slice(r * stretch, (r + 1) * stretch))
        source = ring_source(index, count, r + 1)
        lower.append(source < index)
        picks.append(jnp.where(lower[r], 0, 1))
        own = pl.ds(pl.multiple_of(picks[r] * stretch, stretch), stretch)
        kb[at_b, :] = got[r][:stretch, k_cols]
        vb[at_b, :DH] = got[r][:stretch, v_cols]
        ka[at_a[r], :] = got[r][own, k_cols]
        va[at_a[r], :DH] = got[r][own, v_cols]
        key_f = doc_row(docs_ref, source, stretch).astype(F32)
        key_a = doc_row(docs_ref, jnp.where(lower[r], source, last - source), stretch).astype(F32)
        bias_b[:, at_b] = jnp.where(col_b == key_f, 0.0, MASKED)
        bias_a[:, at_a[r]] = jnp.where(
            jnp.where(lower[r], col_f, col_b) == key_a, 0.0, MASKED
        )

    factor = math.log2(math.e) / math.sqrt(DH)
    tall = stack * stretch

    def stacked(first, base):
        return jnp.concatenate(
            [q_ref[pl.ds(base, stretch), (first + j) * DH : (first + j + 1) * DH] for j in range(stack)],
            axis=0,
        )

    def biased(score, bias):
        size = score.shape[1]
        return (score.reshape(stack, stretch, size) + bias[None]).reshape(tall, size)

    for first in range(0, per, stack):
        s_f = biased(dot_nt(stacked(first, 0), kb[:stretch, :]), bias_f[...])
        s_b = biased(dot_nt(stacked(first, stretch), kb[...]), bias_b[...])
        best[:tall, :] = s_f
        top = s_b[:, :stretch]
        for k in range(1, count + 1):
            top = jnp.maximum(top, s_b[:, k * stretch : (k + 1) * stretch])
        best[tall:, :] = top
        s_a = []
        places = []
        for r in range(others):
            base = pl.multiple_of(picks[r] * stretch, stretch)
            place = pl.ds(pl.multiple_of(picks[r] * tall, tall), tall)
            s_a.append(biased(dot_nt(stacked(first, base), ka[at_a[r], :]), bias_a[:, at_a[r]]))
            best[place, :] = jnp.maximum(best[place, :], s_a[r])
            places.append(place)
        top_f = jnp.max(best[:tall, :], axis=1, keepdims=True)
        top_b = jnp.max(best[tall:, :], axis=1, keepdims=True)
        w_f = jnp.exp2((s_f - top_f) * factor).astype(BF16)
        w_b = jnp.exp2((s_b - top_b) * factor).astype(BF16)
        out_f = jnp.dot(w_f, vb[:stretch, :], preferred_element_type=F32)
        out_b = jnp.dot(w_b, vb[...], preferred_element_type=F32)
        for r in range(others):
            top = jnp.where(lower[r], top_f, top_b)
            w = jnp.exp2((s_a[r] - top) * factor).astype(BF16)
            out = jnp.dot(w, va[at_a[r], :], preferred_element_type=F32)
            out_f += jnp.where(lower[r], out, 0.0)
            out_b += jnp.where(lower[r], 0.0, out)
        for half, out in enumerate((out_f, out_b)):
            result = (out[:, :DH] / out[:, DH:]).astype(BF16)
            sl = slice(half * stretch, (half + 1) * stretch)
            for j in range(stack):
                cols = slice((first + j) * DH, (first + j + 1) * DH)
                out_ref[sl, cols] = result[j * stretch : (j + 1) * stretch]
                copy_ref[sl, cols] = result[j * stretch : (j + 1) * stretch]


def final_kernel(
    count,
    g,
    groups,
    loss_scale,
    pre_ref,
    reach_ref,
    sx_ref,
    c_ref,
    teacher_ref,
    gain_ref,
    f_ref,
    dec_ref,
    *refs,
):
    others = count - 1
    got = refs[:others]
    before = refs[others] if g else None
    out_ref, grad_ref, front, back, flow, gated_ref, sums, gain_acc, skip_acc = refs[-9:]
    rows, width = pre_ref.shape
    stretch = rows // 2
    index = lax.axis_index("ctx")
    tile = 128
    step = 16

    @pl.when(index == 0)
    def _():
        front[...] = jnp.zeros_like(front)

    @pl.when(index == count - 1)
    def _():
        back[:N, :] = jnp.zeros((N, width), BF16)
        back[N:, :] = jnp.where(
            lax.broadcasted_iota(jnp.int32, (EXTRA, width), 0) == 0, 1.0, 0.0
        ).astype(BF16)

    for r in range(1, count):

        @pl.when(index == r)
        def _():
            front[...] = got[r - 1][:N, :]

        @pl.when(index == count - 1 - r)
        def _():
            back[...] = got[r - 1][...]

    d_in = back[N : N + 1, :].astype(F32) + back[N + 1 : N + 2, :].astype(F32)
    through = dec_ref[0:1, :] * front[...].astype(F32) + f_ref[...].astype(F32)
    entering = (d_in * through + back[:N, :].astype(F32)).astype(BF16)
    flow[:stretch, :] = jnp.dot(c_ref[:stretch, :], front[...], preferred_element_type=F32)
    flow[stretch:, :] = jnp.dot(c_ref[stretch:, :], entering, preferred_element_type=F32)
    gain_acc[...] = jnp.zeros_like(gain_acc)
    skip_acc[...] = jnp.zeros_like(skip_acc)

    @pl.loop(0, rows // step, unroll=2)
    def _(k):
        sl = pl.ds(pl.multiple_of(k * step, step), step)
        totals = [jnp.zeros((step, tile), F32)] * 3
        for j in range(0, width, tile):
            cols = slice(j, j + tile)
            gated = pre_ref[sl, cols] + reach_ref[sl, cols] * flow[sl, cols]
            gated_ref[sl, cols] = gated
            scaled = gated * gain_ref[:, cols]
            totals[0] += gated * gated
            totals[1] += scaled * scaled
            totals[2] += scaled * teacher_ref[sl, cols].astype(F32)
        for k3 in range(3):
            sums[sl, k3 * tile : (k3 + 1) * tile] = totals[k3]

    square, weighted, crossed = (
        jnp.sum(sums[:, k3 * tile : (k3 + 1) * tile], axis=1, keepdims=True) * (1.0 / width)
        for k3 in range(3)
    )
    scale = lax.rsqrt(square + EPS)
    push_scale = 2.0 * loss_scale
    mean = push_scale * scale * (scale * weighted - crossed)
    sums[:, :tile] = jnp.broadcast_to(scale, (rows, tile))
    sums[:, tile : 2 * tile] = jnp.broadcast_to(mean, (rows, tile))

    @pl.loop(0, rows // step, unroll=2)
    def _(k):
        sl = pl.ds(pl.multiple_of(k * step, step), step)
        scale = sums[sl, :tile]
        mean = sums[sl, tile : 2 * tile]
        for j in range(0, width, tile):
            cols = slice(j, j + tile)
            gain = gain_ref[:, cols]
            unit = gated_ref[sl, cols] * scale
            normed = unit * gain
            out_ref[sl, cols] = normed.astype(BF16)
            push = (normed - teacher_ref[sl, cols].astype(F32)) * push_scale
            by_gain = push * unit
            by_skip = (push * gain - unit * mean) * (scale * sx_ref[sl, cols])
            gain_acc[:, cols] += by_gain[:8] + by_gain[8:]
            skip_acc[:, cols] += by_skip[:8] + by_skip[8:]

    row = lax.broadcasted_iota(jnp.int32, (tile, width), 0)
    lane = lax.broadcasted_iota(jnp.int32, (tile, width), 1)
    matrix = jnp.where(row == lane // P_SIZE + g * (width // P_SIZE), 1.0, 0.0).astype(BF16)
    hi, lo = parts(skip_acc[...])
    by_head = jnp.sum(dot_nt(hi, matrix) + dot_nt(lo, matrix), axis=0, keepdims=True)
    grad_ref[...] = jnp.zeros_like(grad_ref)
    if g:
        grad_ref[:g, :] = before[:g, :]
        by_head += before[groups : groups + 1, :tile]
    grad_ref[g : g + 1, :] = jnp.sum(gain_acc[...], axis=0, keepdims=True)
    grad_ref[groups : groups + 1, :tile] = by_head


def closing_kernel(a_ref, b_ref, gain_ref, skip_ref):
    total = a_ref[...] + b_ref[...]
    groups, width = total.shape[0] - 1, total.shape[1]
    for g in range(groups):
        gain_ref[:, g * width : (g + 1) * width] = total[g : g + 1, :]
    skip_ref[...] = total[groups : groups + 1, : skip_ref.shape[1]]


def exchange(part, axis, step):
    size = lax.axis_size(axis)
    return lax.ppermute(part, axis, [(d, d ^ step) for d in range(size)])


def body(
    queries,
    keys,
    values,
    doc_ids,
    inputs,
    gate_input,
    b_input,
    c_input,
    dt_raw,
    dt_bias,
    decay_log,
    skip,
    gain,
):
    count = lax.axis_size("ctx")
    rows, features = queries.shape[1:]
    stretch = rows // 2
    kv_dev = keys.shape[2] // DH
    per_kv = queries.shape[2] // keys.shape[2]
    groups = b_input.shape[2] // N
    heads = features // P_SIZE
    width = features // groups
    length = doc_ids.shape[1]
    others = count - 1
    loss_scale = 1.0 / (lax.axis_size("dp") * count * rows)
    x, gate, bmat, cmat = inputs[0], gate_input[0], b_input[0], c_input[0]
    struct = jax.ShapeDtypeStruct

    def whole(*shape):
        return pl.BlockSpec(shape, lambda k: (0, 0))

    def chosen(size, g):
        return pl.BlockSpec((rows, size), lambda k: (0, g))

    state = struct((N, width), BF16)
    payload = struct((N + EXTRA, width), BF16)
    outs = pl.pallas_call(
        functools.partial(opening_kernel, count, groups),
        out_shape=(
            struct((rows, 2 * kv_dev * DH), BF16),
            struct((heads, rows), F32),
            *([struct((rows, width), BF16)] * groups),
            *([struct((8, width), F32)] * groups),
            *([state] * (2 * groups)),
            *([payload] * groups),
        ),
        in_specs=[VMEM] * 8,
        out_specs=(VMEM,) * (2 + 5 * groups),
        compiler_params=params(32),
        cost_estimate=cost(4 * rows * features * N, 8 * rows * features),
        name="opening",
    )(
        *(
            pltpu.with_memory_space_constraint(array, pltpu.HBM)
            for array in (
                doc_ids,
                keys[0],
                values[0],
                x,
                bmat,
                dt_raw[0].T,
                dt_bias.reshape(1, heads),
                decay_log.reshape(1, heads),
            )
        )
    )
    kv, ec = outs[:2]
    xw, dec, f_parts, b_parts, send = (
        outs[2 + k * groups : 2 + (k + 1) * groups] for k in range(5)
    )

    send = list(send)
    got = [[] for _ in range(groups)]
    ring = ring_order(count)
    ring_pairs = [(ring[d], ring[(d + 1) % count]) for d in range(count)]
    moving = kv
    kv_got = []
    for r in range(1, count):
        for g in range(groups):
            if r > 1:
                send[g] = pl.pallas_call(
                    functools.partial(chain_kernel, count, r - 1),
                    out_shape=payload,
                    in_specs=[VMEM] * 4,
                    out_specs=VMEM,
                    cost_estimate=cost(8 * N * width, 8 * N * width),
                    name="chain",
                )(got[g][-1], f_parts[g], b_parts[g], dec[g])
            pairs = [(r - 1, r), (count - r, count - r - 1)]
            got[g].append(lax.ppermute(send[g], "ctx", pairs))
        moving = lax.ppermute(moving, "ctx", ring_pairs)
        kv_got.append(moving)

    local = []
    for g in range(groups):
        local.append(
            pl.pallas_call(
                functools.partial(local_kernel, count, g * (heads // groups)),
                out_shape=(struct((rows, width), F32),) * 3,
                grid=(1,),
                in_specs=[
                    whole(1, length),
                    chosen(width, g),
                    chosen(width, g),
                    chosen(N, g),
                    chosen(N, g),
                    whole(heads, rows),
                    whole(1, heads),
                    whole(rows, width),
                ],
                out_specs=(whole(rows, width),) * 3,
                compiler_params=params(24),
                cost_estimate=cost(2 * rows * width * N, 16 * rows * width),
                name="local",
            )(doc_ids, x, gate, bmat, cmat, ec, skip.reshape(1, heads), xw[g])
        )

    stack = 4 if per_kv % 4 == 0 and count <= 4 else 1
    teacher = None
    targets = []
    for g in range(kv_dev):
        more = [] if teacher is None else [teacher]
        teacher, target = pl.pallas_call(
            functools.partial(attention_kernel, count, per_kv, stack, g),
            out_shape=(struct((rows, features), BF16), struct((rows, per_kv * DH), BF16)),
            grid=(1,),
            in_specs=[
                whole(1, length),
                chosen(per_kv * DH, g),
                chosen(DH, g),
                chosen(DH, g),
                *[whole(rows, 2 * kv_dev * DH)] * others,
                *[pl.BlockSpec(memory_space=pl.ANY)] * len(more),
            ],
            out_specs=(chosen(per_kv * DH, g), whole(rows, per_kv * DH)),
            scratch_shapes=[
                pltpu.VMEM(((count + 1) * stretch, DH), BF16),
                pltpu.VMEM(((count + 1) * stretch, 2 * DH), BF16),
                pltpu.VMEM((others * stretch, DH), BF16),
                pltpu.VMEM((others * stretch, 2 * DH), BF16),
                pltpu.VMEM((stretch, (count + 1) * stretch), F32),
                pltpu.VMEM((stretch, stretch), F32),
                pltpu.VMEM((stretch, others * stretch), F32),
                pltpu.VMEM((2 * stack * stretch, stretch), F32),
            ],
            input_output_aliases={4 + others: 0} if more else {},
            compiler_params=params(40),
            cost_estimate=cost(
                4 * (2 * count + 1) * stretch * stretch * per_kv * DH, 8 * rows * per_kv * DH
            ),
            name="attention",
        )(doc_ids, queries[0], keys[0], values[0], *kv_got, *more)
        targets.append(target)

    student = grads = None
    for g in range(groups):
        more = [] if student is None else [grads, student]
        student, grads = pl.pallas_call(
            functools.partial(final_kernel, count, g, groups, loss_scale),
            out_shape=(struct((rows, features), BF16), struct((groups + 1, width), F32)),
            grid=(1,),
            in_specs=[
                *[whole(rows, width)] * 3,
                chosen(N, g),
                whole(rows, width),
                pl.BlockSpec((1, width), lambda k, g=g: (0, g)),
                whole(N, width),
                whole(8, width),
                *[whole(N + EXTRA, width)] * others,
                *([whole(groups + 1, width), pl.BlockSpec(memory_space=pl.ANY)] if more else []),
            ],
            out_specs=(chosen(width, g), whole(groups + 1, width)),
            scratch_shapes=[
                pltpu.VMEM((N, width), BF16),
                pltpu.VMEM((N + EXTRA, width), BF16),
                pltpu.VMEM((rows, width), F32),
                pltpu.VMEM((rows, width), F32),
                pltpu.VMEM((rows, 3 * 128), F32),
                pltpu.VMEM((8, width), F32),
                pltpu.VMEM((8, width), F32),
            ],
            input_output_aliases={9 + others: 0} if more else {},
            compiler_params=params(32),
            cost_estimate=cost(2 * rows * width * N, 20 * rows * width),
            name="final",
        )(
            *local[g],
            cmat,
            targets[g],
            gain.reshape(1, features),
            f_parts[g],
            dec[g],
            *got[g],
            *more,
        )
    steps = []
    for axis in ("ctx", "dp"):
        step = 1
        while step < lax.axis_size(axis):
            steps.append((axis, step))
            step *= 2
    for axis, step in steps[:-1]:
        grads = grads + exchange(grads, axis, step)
    grad_gain, grad_skip = pl.pallas_call(
        closing_kernel,
        out_shape=(struct((1, features), F32), struct((1, heads), F32)),
        in_specs=[VMEM] * 2,
        out_specs=(VMEM,) * 2,
        name="closing",
    )(grads, exchange(grads, *steps[-1]))
    return (teacher[None], student[None], grad_gain[0], grad_skip[0])


def solution(mesh):
    rows = P("dp", "ctx", "head")
    in_specs = (
        rows,
        rows,
        rows,
        P("dp", None),
        rows,
        rows,
        rows,
        rows,
        rows,
        P("head"),
        P("head"),
        P("head"),
        P("head"),
    )
    out_specs = (rows, rows, P("head"), P("head"))
    return jax.shard_map(body, mesh=mesh, in_specs=in_specs, out_specs=out_specs, check_vma=False)
```

time: 229 us -> 85.5 us (0.37)
  blocking collectives: 87.4 us -> 0 us
  local copies, waits for them, and re-layouts: 49.3 us -> 11 us
  other arithmetic: 38.2 us -> 0.01 us
  matrix products: 34.3 us -> 0 us
  Pallas kernels: 0 us -> 29.6 us
  starting transfers between devices: 0.08 us -> 28.1 us
  between operations: 17.7 us -> 0.89 us
  waiting for transfers between devices: 0.04 us -> 15.3 us
    all_gather x3 -> x0, blocking collectives: 57.5 us -> none  [the longest x1 24 us: body(): key_piece = lax.all_gather(keys, 'ctx', axis=1, tiled=True)]
    dot_general x12 -> x0, matrix products: 34.3 us -> none  [the longest x2 14 us: inner(): jnp.einsum('tkgs,skd->tkgd', weights.astype(jnp.bfloat16), value_now, pre...]
    pallas_call x0 -> x12, Pallas kernels: none -> 29.6 us  [the longest x2 9.96 us: body(): pl.pallas_call(functools.partial(attention_kernel, count, per_kv, stack,...]
    ppermute x0 -> x12, starting transfers between devices: none -> 28.1 us  [the longest x6 9.95 us: body(): got[g].append(lax.ppermute(send[g], 'ctx', pairs))]
    psum x1 -> x0, blocking collectives: 21.3 us -> none  [body(): summed_grads = lax.psum((grad_gain, grad_skip), ('dp', 'ctx'))]
    reduce_sum x6 -> x0, other arithmetic: 15.5 us -> none  [the longest x2 10.3 us: inner(): total = total * factor + jnp.sum(weights, axis=3)]
    ppermute x0 -> x12, waiting for transfers between devices: none -> 15.3 us  [the longest x6 6.85 us: body(): got[g].append(lax.ppermute(send[g], 'ctx', pairs))]
    select_n x17 -> x0, other arithmetic: 12 us -> none  [the longest x8 5.27 us: prefix_lap(): return jax.tree.map(lambda a, b: jnp.where(reached, a, b), new, before)]
  transfers between devices with their start and end apart: 2 -> 12, of which waited for: 0 -> 7; matrix products, arithmetic and copies ran while one was open for 37% -> 0% of each run, Pallas kernels for 0% -> 26%
where the time goes in v2:
time: 85.5 us; the launch traced here: 84.9 us
  Pallas kernels  29.6 us (35%)
  starting transfers between devices  28.1 us (33%)
  waiting for transfers between devices  15.3 us (18%)
  local copies, waits for them, and re-layouts  11 us (13%)
  between operations  0.89 us (1%)
    unnamed x64, local copies, waits for them, and re-layouts  11 us
    pallas_call x2, Pallas kernels, body(): pl.pallas_call(functools.partial(attention_kernel, count, per_kv, stack,...  9.96 us
    ppermute x6, starting transfers between devices, body(): got[g].append(lax.ppermute(send[g], 'ctx', pairs))  9.95 us
    ppermute x3, starting transfers between devices, body(): moving = lax.ppermute(moving, 'ctx', ring_pairs)  9.34 us
    ppermute x3, starting transfers between devices, exchange(): return lax.ppermute(part, axis, [(d, d ^ step) for d in range(size)])  8.79 us
    pallas_call x4, Pallas kernels, body(): pl.pallas_call(functools.partial(chain_kernel, count, r - 1), out_shape=p...  7.37 us
    ppermute x6, waiting for transfers between devices, body(): got[g].append(lax.ppermute(send[g], 'ctx', pairs))  6.85 us
    pallas_call x2, Pallas kernels, body(): pl.pallas_call(functools.partial(final_kernel, count, g, groups, loss_sca...  5.69 us
  transfers between devices with their start and end apart: 12, of which 7 were waited for; matrix products, arithmetic and copies ran while one was open for 0% of the time, Pallas kernels for 26%

profile of v2, /device:TPU:0, one launch (start us, length us, event | category | flops | bytes accessed | tf_op | source)
XLA Modules:
  0.0 84.9 jit_solution(5645744104451458211)
XLA Ops:
  0.6 3.5 %opening.1 = (bf16[256,512]{1,0:T(8,128)(2,1)S(1)}, f32[32,256]{1,0:T(8,128)S(1)}, bf16[256,1024]{1,0:T(8,128)(2,1)S(1)}, bf16[256,1024]{1,0:T(8,128)(2,1)S(1)},...) custom-call(s32[1,1024]{1,0:T(1,128)} %docs_ref.9, ...), custom_call_target="tpu_custom_call" | custom-call | flops 268435456 | bytes 4194304 | tf_op jit(solution)/shard_map/opening/pallas_call | solution.py:496
  4.2 0.7 copy-done.2
  4.9 0.7 copy-done.4
  5.6 0.7 copy-done.17
  6.3 0.7 copy-done.18
  7.0 0.8 copy-done.19
  7.8 0.6 copy-done.23
  8.4 0.6 copy-done.25
  9.0 3.1 %collective-permute-start = (bf16[256,512]{1,0:T(8,128)(2,1)S(1)}, bf16[256,512]{1,0:T(8,128)(2,1)}, u32[]{:S(2)}, u32[]{:S(2)}) collective-permute-start(bf16[256,512]{1,0:T(8,128)(2,1)S(1)} %get-tuple-element.32), channel_id=1, source_target_pairs={{0,4},{4,12},{12,8},{8,0},{1,5},{5,13},{13,9},{9,1},{2,6},{6,14},{... | collective-permute-start | bytes 786440 | tf_op jit(solution)/shard_map/ppermute | solution.py:550
  12.1 4.5 %collective-permute-start.6 = (bf16[144,1024]{1,0:T(8,128)(2,1)S(1)}, bf16[144,1024]{1,0:T(8,128)(2,1)S(1)}, u32[]{:S(2)}, u32[]{:S(2)}) collective-permute-start(bf16[144,1024]{1,0:T(8,128)(2,1)S(1)} %get-tuple-element.52), channel_id=1, source_target_pairs={{0,4},{12,8},{1,5},{13,9},{2,6},{14,10},{3,7},{15,11},{16,20},{28,... | collective-permute-start | bytes 884744 | tf_op jit(solution)/shard_map/ppermute | solution.py:549
  16.6 1.3 %collective-permute-start.3 = (bf16[144,1024]{1,0:T(8,128)(2,1)S(1)}, bf16[144,1024]{1,0:T(8,128)(2,1)S(1)}, u32[]{:S(2)}, u32[]{:S(2)}) collective-permute-start(bf16[144,1024]{1,0:T(8,128)(2,1)S(1)} %get-tuple-element.43), channel_id=1, source_target_pairs={{0,4},{12,8},{1,5},{13,9},{2,6},{14,10},{3,7},{15,11},{16,20},{28,... | collective-permute-start | bytes 884744 | tf_op jit(solution)/shard_map/ppermute | solution.py:549
  17.9 1.6 %collective-permute-done.refs_0_ = bf16[256,512]{1,0:T(8,128)(2,1)} collective-permute-done((bf16[256,512]{1,0:T(8,128)(2,1)S(1)}, bf16[256,512]{1,0:T(8,128)(2,1)}, u32[]{:S(2)}, u32[]{:S(2)}) %collective-permute-start) | collective-permute-done | bytes 262176 | tf_op jit(solution)/shard_map/ppermute | solution.py:550
  19.5 1.9 %collective-permute-start.1 = (bf16[256,512]{1,0:T(8,128)(2,1)}, bf16[256,512]{1,0:T(8,128)(2,1)}, u32[]{:S(2)}, u32[]{:S(2)}) collective-permute-start(bf16[256,512]{1,0:T(8,128)(2,1)} %collective-permute-done.refs_0_), channel_id=1, source_target_pairs={{0,4},{4,12},{12,8},{8,0},{1,5},{5,13},{13,9},{9,1},{2,6},{6,14},{... | collective-permute-start | bytes 786440 | tf_op jit(solution)/shard_map/ppermute | solution.py:550
  21.4 3.7 %collective-permute-done.6.got_ref.refs_0_ = bf16[144,1024]{1,0:T(8,128)(2,1)S(1)} collective-permute-done((bf16[144,1024]{1,0:T(8,128)(2,1)S(1)}, bf16[144,1024]{1,0:T(8,128)(2,1)S(1)}, u32[]{:S(2)}, u32[]{:S(2)}) %collective-permute-start.6) | collective-permute-done | bytes 294944 | tf_op jit(solution)/shard_map/ppermute | solution.py:549
  25.2 0.7 copy-done.9
  25.9 1.8 %chain.6 = bf16[144,1024]{1,0:T(8,128)(2,1)} custom-call(bf16[144,1024]{1,0:T(8,128)(2,1)} %copy-done.9, bf16[128,1024]{1,0:T(8,128)(2,1)} %copy-done.4, bf16[128,1024]{1,0:T(8,128)(2,1)} %copy-done.18, f32[8,1024]{1,0:T(8,128)} %copy-done.25), custom_call_target="tpu_custom_call" | custom-call | flops 1048576 | bytes 1048576 | tf_op jit(solution)/shard_map/chain/pallas_call | solution.py:540
  27.7 0.7 collective-permute-start.7
  28.4 3.1 %collective-permute-done.3.got_ref.refs_0_ = bf16[144,1024]{1,0:T(8,128)(2,1)S(1)} collective-permute-done((bf16[144,1024]{1,0:T(8,128)(2,1)S(1)}, bf16[144,1024]{1,0:T(8,128)(2,1)S(1)}, u32[]{:S(2)}, u32[]{:S(2)}) %collective-permute-start.3) | collective-permute-done | bytes 294944 | tf_op jit(solution)/shard_map/ppermute | solution.py:549
  31.5 0.7 copy-done.7
  32.2 1.9 %chain.4 = bf16[144,1024]{1,0:T(8,128)(2,1)} custom-call(bf16[144,1024]{1,0:T(8,128)(2,1)} %copy-done.7, bf16[128,1024]{1,0:T(8,128)(2,1)} %copy-done.2, bf16[128,1024]{1,0:T(8,128)(2,1)} %copy-done.17, f32[8,1024]{1,0:T(8,128)} %copy-done.23), custom_call_target="tpu_custom_call" | custom-call | flops 1048576 | bytes 1048576 | tf_op jit(solution)/shard_map/chain/pallas_call | solution.py:540
  34.1 0.8 collective-permute-start.4
  34.9 1.2 %collective-permute-done.1.refs_1_ = bf16[256,512]{1,0:T(8,128)(2,1)} collective-permute-done((bf16[256,512]{1,0:T(8,128)(2,1)}, bf16[256,512]{1,0:T(8,128)(2,1)}, u32[]{:S(2)}, u32[]{:S(2)}) %collective-permute-start.1) | collective-permute-done | bytes 262176 | tf_op jit(solution)/shard_map/ppermute | solution.py:550
  36.1 4.3 %collective-permute-start.2 = (bf16[256,512]{1,0:T(8,128)(2,1)}, bf16[256,512]{1,0:T(8,128)(2,1)}, u32[]{:S(2)}, u32[]{:S(2)}) collective-permute-start(bf16[256,512]{1,0:T(8,128)(2,1)} %collective-permute-done.1.refs_1_), channel_id=1, source_target_pairs={{0,4},{4,12},{12,8},{8,0},{1,5},{5,13},{13,9},{9,1},{2,6},{6,14},{... | collective-permute-start | bytes 786440 | tf_op jit(solution)/shard_map/ppermute | solution.py:550
  40.4 0.7 copy-done.13
  41.1 1.8 %chain.7 = bf16[144,1024]{1,0:T(8,128)(2,1)} custom-call(bf16[144,1024]{1,0:T(8,128)(2,1)} %copy-done.13, bf16[128,1024]{1,0:T(8,128)(2,1)} %copy-done.4, bf16[128,1024]{1,0:T(8,128)(2,1)} %copy-done.18, f32[8,1024]{1,0:T(8,128)} %copy-done.25), custom_call_target="tpu_custom_call" | custom-call | flops 1048576 | bytes 1048576 | tf_op jit(solution)/shard_map/chain/pallas_call | solution.py:540
  42.9 1.4 %collective-permute-start.8 = (bf16[144,1024]{1,0:T(8,128)(2,1)}, bf16[144,1024]{1,0:T(8,128)(2,1)}, u32[]{:S(2)}, u32[]{:S(2)}) collective-permute-start(bf16[144,1024]{1,0:T(8,128)(2,1)} %chain.7), channel_id=1, source_target_pairs={{8,12},{4,0},{9,13},{5,1},{10,14},{6,2},{11,15},{7,3},{24,28},{20,... | collective-permute-start | bytes 884744 | tf_op jit(solution)/shard_map/ppermute | solution.py:549
  44.4 0.7 copy-done.11
  45.1 1.8 %chain.5 = bf16[144,1024]{1,0:T(8,128)(2,1)} custom-call(bf16[144,1024]{1,0:T(8,128)(2,1)} %copy-done.11, bf16[128,1024]{1,0:T(8,128)(2,1)} %copy-done.2, bf16[128,1024]{1,0:T(8,128)(2,1)} %copy-done.17, f32[8,1024]{1,0:T(8,128)} %copy-done.23), custom_call_target="tpu_custom_call" | custom-call | flops 1048576 | bytes 1048576 | tf_op jit(solution)/shard_map/chain/pallas_call | solution.py:540
  46.9 1.3 %collective-permute-start.5 = (bf16[144,1024]{1,0:T(8,128)(2,1)}, bf16[144,1024]{1,0:T(8,128)(2,1)S(1)}, u32[]{:S(2)}, u32[]{:S(2)}) collective-permute-start(bf16[144,1024]{1,0:T(8,128)(2,1)} %chain.5), channel_id=1, source_target_pairs={{8,12},{4,0},{9,13},{5,1},{10,14},{6,2},{11,15},{7,3},{24,28},{20,... | collective-permute-start | bytes 884744 | tf_op jit(solution)/shard_map/ppermute | solution.py:549
  48.3 0.6 copy-done.27
  48.9 1.0 %copy-done.20 = bf16[256,1024]{1,0:T(8,128)(2,1)S(1)} copy-done((bf16[256,1024]{1,0:T(8,128)(2,1)S(1)}, bf16[256,1024]{1,0:T(8,128)(2,1)}, u32[]{:S(2)}) %copy-start.20) | copy-done | bytes 524312
  49.9 0.8 local.3
  50.8 0.9 %local.2 = (f32[256,1024]{1,0:T(8,128)S(1)}, f32[256,1024]{1,0:T(8,128)S(1)}, f32[256,1024]{1,0:T(8,128)S(1)}) custom-call(s32[1,1024]{1,0:T(1,128)S(1)} %copy-done.27, bf16[256,2048]{1,0:T(8,128)(2,1)S(1)} %bitcast.20, bf16[256,2048]{1,0:T(8,128)(2,1)S(1)} %bitcast.22, bf16[256,256]{1,0:T(8,128)(2,1)S(1)} %bitcast.29, bf16[256,256]{1,0:T(8,128)(2,1)S(1)} %bitcast.24, ...), custom_call_target="tpu_custom_call" | custom-call | flops 67108864 | bytes 4194304 | tf_op jit(solution)/shard_map/local/pallas_call | solution.py:556
  51.7 0.3 copy-done.16
  52.0 0.0 copy-done.22
  52.1 4.9 %attention.2 = (bf16[256,2048]{1,0:T(8,128)(2,1)}, bf16[256,1024]{1,0:T(8,128)(2,1)S(1)}) custom-call(s32[1,1024]{1,0:T(1,128)S(1)} %copy-done.27, bf16[256,2048]{1,0:T(8,128)(2,1)S(1)} %bitcast.30, bf16[256,256]{1,0:T(8,128)(2,1)S(1)} %bitcast.33, bf16[256,256]{1,0:T(8,128)(2,1)S(1)} %bitcast.36, bf16[256,512]{1,0:T(8,128)(2,1)} %collective-permute-done.refs_0_, ...), custom_call_target="tpu_custom_call" | custom-call | flops 603979776 | bytes 2097152 | tf_op jit(solution)/shard_map/attention/pallas_call | solution.py:582
  57.0 5.0 %attention.3 = (bf16[256,2048]{1,0:T(8,128)(2,1)}, bf16[256,1024]{1,0:T(8,128)(2,1)S(1)}) custom-call(s32[1,1024]{1,0:T(1,128)S(1)} %copy-done.27, bf16[256,2048]{1,0:T(8,128)(2,1)S(1)} %bitcast.31, bf16[256,256]{1,0:T(8,128)(2,1)S(1)} %bitcast.34, bf16[256,256]{1,0:T(8,128)(2,1)S(1)} %bitcast.37, ...), custom_call_target="tpu_custom_call", output_to_operand_aliasing={{0}: (7, {})} | custom-call | flops 603979776 | bytes 2097152 | tf_op jit(solution)/shard_map/attention/pallas_call | solution.py:582
  62.1 0.7 copy-done.28
  62.7 3.4 %final.2 = (bf16[256,2048]{1,0:T(8,128)(2,1)}, f32[3,1024]{1,0:T(4,128)S(1)}) custom-call(f32[256,1024]{1,0:T(8,128)S(1)} %get-tuple-element.46.pre_ref, f32[256,1024]{1,0:T(8,128)S(1)} %get-tuple-element.47.reach_ref, f32[256,1024]{1,0:T(8,128)S(1)} %get-tuple-element.48.sx_ref, bf16[256,256]{1,0:T(8,128)(2,1)S(1)} %bitcast.25, ...), custom_call_target="tpu_custom_call" | custom-call | flops 67108864 | bytes 5242880 | tf_op jit(solution)/shard_map/final/pallas_call | solution.py:617
  66.1 2.3 %final.3 = (bf16[256,2048]{1,0:T(8,128)(2,1)}, f32[3,1024]{1,0:T(4,128)S(1)}) custom-call(f32[256,1024]{1,0:T(8,128)S(1)} %get-tuple-element.37.pre_ref, f32[256,1024]{1,0:T(8,128)S(1)} %get-tuple-element.38.reach_ref, f32[256,1024]{1,0:T(8,128)S(1)} %get-tuple-element.39.sx_ref, bf16[256,256]{1,0:T(8,128)(2,1)S(1)} %bitcast.26, ...), custom_call_target="tpu_custom_call", output_to_operand_aliasing={{0}: (12, {})} | custom-call | flops 67108864 | bytes 5242880 | tf_op jit(solution)/shard_map/final/pallas_call | solution.py:617
  68.5 4.2 %collective-permute-start.9 = (f32[3,1024]{1,0:T(4,128)S(1)}, f32[3,1024]{1,0:T(4,128)S(1)}, u32[]{:S(2)}, u32[]{:S(2)}) collective-permute-start(f32[3,1024]{1,0:T(4,128)S(1)} %get-tuple-element.57), channel_id=1, source_target_pairs={{0,4},{4,0},{8,12},{12,8},{1,5},{5,1},{9,13},{13,9},{2,6},{6,2},{1... | collective-permute-start | bytes 36872 | tf_op jit(solution)/shard_map/ppermute | solution.py:456
  72.6 1.7 %collective-permute-done.9 = f32[3,1024]{1,0:T(4,128)S(1)} collective-permute-done((f32[3,1024]{1,0:T(4,128)S(1)}, f32[3,1024]{1,0:T(4,128)S(1)}, u32[]{:S(2)}, u32[]{:S(2)}) %collective-permute-start.9) | collective-permute-done | bytes 12320 | tf_op jit(solution)/shard_map/ppermute | solution.py:456
  74.3 3.1 %collective-permute-start.10 = (f32[3,1024]{1,0:T(4,128)S(1)}, f32[3,1024]{1,0:T(4,128)S(1)}, u32[]{:S(2)}, u32[]{:S(2)}) collective-permute-start(f32[3,1024]{1,0:T(4,128)S(1)} %add.6), channel_id=1, source_target_pairs={{0,8},{4,12},{8,0},{12,4},{1,9},{5,13},{9,1},{13,5},{2,10},{6,14},... | collective-permute-start | bytes 36872 | tf_op jit(solution)/shard_map/ppermute | solution.py:456
  77.4 1.7 %collective-permute-done.10 = f32[3,1024]{1,0:T(4,128)S(1)} collective-permute-done((f32[3,1024]{1,0:T(4,128)S(1)}, f32[3,1024]{1,0:T(4,128)S(1)}, u32[]{:S(2)}, u32[]{:S(2)}) %collective-permute-start.10) | collective-permute-done | bytes 12320 | tf_op jit(solution)/shard_map/ppermute | solution.py:456
  79.1 1.6 %collective-permute-start.11 = (f32[3,1024]{1,0:T(4,128)S(1)}, f32[3,1024]{1,0:T(4,128)S(1)}, u32[]{:S(2)}, u32[]{:S(2)}) collective-permute-start(f32[3,1024]{1,0:T(4,128)S(1)} %add.7.a_ref), channel_id=1, source_target_pairs={{0,16},{16,0},{1,17},{17,1},{2,18},{18,2},{3,19},{19,3},{4,20},{20... | collective-permute-start | bytes 36872 | tf_op jit(solution)/shard_map/ppermute | solution.py:456
  80.7 2.2 %collective-permute-done.11.b_ref = f32[3,1024]{1,0:T(4,128)S(1)} collective-permute-done((f32[3,1024]{1,0:T(4,128)S(1)}, f32[3,1024]{1,0:T(4,128)S(1)}, u32[]{:S(2)}, u32[]{:S(2)}) %collective-permute-start.11) | collective-permute-done | bytes 12320 | tf_op jit(solution)/shard_map/ppermute | solution.py:456
  82.9 0.6 copy-done.31
  83.5 1.3 %closing.1 = (f32[1,2048]{1,0:T(1,128)}, f32[1,32]{1,0:T(1,128)}) custom-call(f32[3,1024]{1,0:T(4,128)} %copy-done.30, f32[3,1024]{1,0:T(4,128)} %copy-done.31), custom_call_target="tpu_custom_call" | custom-call | tf_op jit(solution)/shard_map/closing/pallas_call | solution.py:663
  (54 shorter events, 0.1 us)
Async XLA Ops:
  4.2 0.7 copy-start.2
  4.9 0.7 copy-start.4
  5.6 0.7 copy-start.17
  6.3 0.7 copy-start.18
  7.0 0.8 copy-start.19
  7.8 0.6 copy-start.23
  8.4 0.6 copy-start.25
  9.0 10.5 %collective-permute-start = (bf16[256,512]{1,0:T(8,128)(2,1)S(1)}, bf16[256,512]{1,0:T(8,128)(2,1)}, u32[]{:S(2)}, u32[]{:S(2)}) collective-permute-start(bf16[256,512]{1,0:T(8,128)(2,1)S(1)} %get-tuple-element.32), channel_id=1, source_target_pairs={{0,4},{4,12},{12,8},{8,0},{1,5},{5,13},{13,9},{9,1},{2,6},{6,14},{... | collective-permute-start | bytes 786440 | tf_op jit(solution)/shard_map/ppermute | solution.py:550
  12.1 13.0 %collective-permute-start.6 = (bf16[144,1024]{1,0:T(8,128)(2,1)S(1)}, bf16[144,1024]{1,0:T(8,128)(2,1)S(1)}, u32[]{:S(2)}, u32[]{:S(2)}) collective-permute-start(bf16[144,1024]{1,0:T(8,128)(2,1)S(1)} %get-tuple-element.52), channel_id=1, source_target_pairs={{0,4},{12,8},{1,5},{13,9},{2,6},{14,10},{3,7},{15,11},{16,20},{28,... | collective-permute-start | bytes 884744 | tf_op jit(solution)/shard_map/ppermute | solution.py:549
  16.6 14.9 %collective-permute-start.3 = (bf16[144,1024]{1,0:T(8,128)(2,1)S(1)}, bf16[144,1024]{1,0:T(8,128)(2,1)S(1)}, u32[]{:S(2)}, u32[]{:S(2)}) collective-permute-start(bf16[144,1024]{1,0:T(8,128)(2,1)S(1)} %get-tuple-element.43), channel_id=1, source_target_pairs={{0,4},{12,8},{1,5},{13,9},{2,6},{14,10},{3,7},{15,11},{16,20},{28,... | collective-permute-start | bytes 884744 | tf_op jit(solution)/shard_map/ppermute | solution.py:549
  19.5 16.5 %collective-permute-start.1 = (bf16[256,512]{1,0:T(8,128)(2,1)}, bf16[256,512]{1,0:T(8,128)(2,1)}, u32[]{:S(2)}, u32[]{:S(2)}) collective-permute-start(bf16[256,512]{1,0:T(8,128)(2,1)} %collective-permute-done.refs_0_), channel_id=1, source_target_pairs={{0,4},{4,12},{12,8},{8,0},{1,5},{5,13},{13,9},{9,1},{2,6},{6,14},{... | collective-permute-start | bytes 786440 | tf_op jit(solution)/shard_map/ppermute | solution.py:550
  25.2 0.7 copy-start.9
  27.7 12.7 %collective-permute-start.7 = (bf16[144,1024]{1,0:T(8,128)(2,1)}, bf16[144,1024]{1,0:T(8,128)(2,1)S(1)}, u32[]{:S(2)}, u32[]{:S(2)}) collective-permute-start(bf16[144,1024]{1,0:T(8,128)(2,1)} %chain.6), channel_id=1, source_target_pairs={{4,8},{8,4},{5,9},{9,5},{6,10},{10,6},{7,11},{11,7},{20,24},{24,20... | collective-permute-start | bytes 884744 | tf_op jit(solution)/shard_map/ppermute | solution.py:549
  31.5 0.7 copy-start.7
  32.2 16.0 %copy-start.15 = (bf16[1,256,256]{2,1,0:T(8,128)(2,1)S(1)}, bf16[1,256,256]{2,1,0:T(8,128)(2,1)}, u32[]{:S(2)}) copy-start(bf16[1,256,256]{2,1,0:T(8,128)(2,1)} %param.19) | copy-start | bytes 393220
  34.1 14.2 %copy-start = (bf16[1,256,2048]{2,1,0:T(8,128)(2,1)S(1)}, bf16[1,256,2048]{2,1,0:T(8,128)(2,1)}, u32[]{:S(2)}) copy-start(bf16[1,256,2048]{2,1,0:T(8,128)(2,1)} %param.17) | copy-start | bytes 3145732
  34.1 14.2 %copy-start.1 = (bf16[1,256,2048]{2,1,0:T(8,128)(2,1)S(1)}, bf16[1,256,2048]{2,1,0:T(8,128)(2,1)}, u32[]{:S(2)}) copy-start(bf16[1,256,2048]{2,1,0:T(8,128)(2,1)} %param.18) | copy-start | bytes 3145732
  34.1 10.3 %collective-permute-start.4 = (bf16[144,1024]{1,0:T(8,128)(2,1)}, bf16[144,1024]{1,0:T(8,128)(2,1)S(1)}, u32[]{:S(2)}, u32[]{:S(2)}) collective-permute-start(bf16[144,1024]{1,0:T(8,128)(2,1)} %chain.4), channel_id=1, source_target_pairs={{4,8},{8,4},{5,9},{9,5},{6,10},{10,6},{7,11},{11,7},{20,24},{24,20... | collective-permute-start | bytes 884744 | tf_op jit(solution)/shard_map/ppermute | solution.py:549
  36.1 15.6 %collective-permute-start.2 = (bf16[256,512]{1,0:T(8,128)(2,1)}, bf16[256,512]{1,0:T(8,128)(2,1)}, u32[]{:S(2)}, u32[]{:S(2)}) collective-permute-start(bf16[256,512]{1,0:T(8,128)(2,1)} %collective-permute-done.1.refs_1_), channel_id=1, source_target_pairs={{0,4},{4,12},{12,8},{8,0},{1,5},{5,13},{13,9},{9,1},{2,6},{6,14},{... | collective-permute-start | bytes 786440 | tf_op jit(solution)/shard_map/ppermute | solution.py:550
  40.4 0.7 copy-start.13
  42.9 5.3 %copy-start.6 = (bf16[1,256,256]{2,1,0:T(8,128)(2,1)S(1)}, bf16[1,256,256]{2,1,0:T(8,128)(2,1)}, u32[]{:S(2)}) copy-start(bf16[1,256,256]{2,1,0:T(8,128)(2,1)} %param.20) | copy-start | bytes 393220
  42.9 19.1 %collective-permute-start.8 = (bf16[144,1024]{1,0:T(8,128)(2,1)}, bf16[144,1024]{1,0:T(8,128)(2,1)}, u32[]{:S(2)}, u32[]{:S(2)}) collective-permute-start(bf16[144,1024]{1,0:T(8,128)(2,1)} %chain.7), channel_id=1, source_target_pairs={{8,12},{4,0},{9,13},{5,1},{10,14},{6,2},{11,15},{7,3},{24,28},{20,... | collective-permute-start | bytes 884744 | tf_op jit(solution)/shard_map/ppermute | solution.py:549
  44.4 0.7 copy-start.11
  46.9 19.2 %collective-permute-start.5 = (bf16[144,1024]{1,0:T(8,128)(2,1)}, bf16[144,1024]{1,0:T(8,128)(2,1)S(1)}, u32[]{:S(2)}, u32[]{:S(2)}) collective-permute-start(bf16[144,1024]{1,0:T(8,128)(2,1)} %chain.5), channel_id=1, source_target_pairs={{8,12},{4,0},{9,13},{5,1},{10,14},{6,2},{11,15},{7,3},{24,28},{20,... | collective-permute-start | bytes 884744 | tf_op jit(solution)/shard_map/ppermute | solution.py:549
  48.2 0.7 copy-start.27
  48.2 0.7 copy-start.29
  48.9 1.0 %copy-start.20 = (bf16[256,1024]{1,0:T(8,128)(2,1)S(1)}, bf16[256,1024]{1,0:T(8,128)(2,1)}, u32[]{:S(2)}) copy-start(bf16[256,1024]{1,0:T(8,128)(2,1)} %copy-done.19) | copy-start | bytes 1572868
  50.8 1.2 %copy-start.16 = (bf16[1,256,2048]{2,1,0:T(8,128)(2,1)S(1)}, bf16[1,256,2048]{2,1,0:T(8,128)(2,1)}, u32[]{:S(2)}) copy-start(bf16[1,256,2048]{2,1,0:T(8,128)(2,1)} %param.13) | copy-start | bytes 3145732
  50.8 1.2 %copy-start.21 = (bf16[1,256,256]{2,1,0:T(8,128)(2,1)S(1)}, bf16[1,256,256]{2,1,0:T(8,128)(2,1)}, u32[]{:S(2)}) copy-start(bf16[1,256,256]{2,1,0:T(8,128)(2,1)} %param.14) | copy-start | bytes 393220
  50.8 1.3 %copy-start.22 = (bf16[1,256,256]{2,1,0:T(8,128)(2,1)S(1)}, bf16[1,256,256]{2,1,0:T(8,128)(2,1)}, u32[]{:S(2)}) copy-start(bf16[1,256,256]{2,1,0:T(8,128)(2,1)} %param.15) | copy-start | bytes 393220
  57.0 5.0 %copy-start.5 = (bf16[128,1024]{1,0:T(8,128)(2,1)S(1)}, bf16[128,1024]{1,0:T(8,128)(2,1)}, u32[]{:S(2)}) copy-start(bf16[128,1024]{1,0:T(8,128)(2,1)} %copy-done.4) | copy-start | bytes 786436
  57.0 5.0 %copy-start.10 = (bf16[144,1024]{1,0:T(8,128)(2,1)S(1)}, bf16[144,1024]{1,0:T(8,128)(2,1)}, u32[]{:S(2)}) copy-start(bf16[144,1024]{1,0:T(8,128)(2,1)} %copy-done.9) | copy-start | bytes 884740
  57.0 5.0 %copy-start.14 = (bf16[144,1024]{1,0:T(8,128)(2,1)S(1)}, bf16[144,1024]{1,0:T(8,128)(2,1)}, u32[]{:S(2)}) copy-start(bf16[144,1024]{1,0:T(8,128)(2,1)} %copy-done.13) | copy-start | bytes 884740
  57.0 5.0 %copy-start.26 = (f32[8,1024]{1,0:T(8,128)S(1)}, f32[8,1024]{1,0:T(8,128)}, u32[]{:S(2)}) copy-start(f32[8,1024]{1,0:T(8,128)} %copy-done.25) | copy-start | bytes 98308
  62.0 0.7 copy-start.28
  62.7 3.4 %copy-start.3 = (bf16[128,1024]{1,0:T(8,128)(2,1)S(1)}, bf16[128,1024]{1,0:T(8,128)(2,1)}, u32[]{:S(2)}) copy-start(bf16[128,1024]{1,0:T(8,128)(2,1)} %copy-done.2) | copy-start | bytes 786436
  62.7 3.4 %copy-start.8 = (bf16[144,1024]{1,0:T(8,128)(2,1)S(1)}, bf16[144,1024]{1,0:T(8,128)(2,1)}, u32[]{:S(2)}) copy-start(bf16[144,1024]{1,0:T(8,128)(2,1)} %copy-done.7) | copy-start | bytes 884740
  62.7 3.4 %copy-start.12 = (bf16[144,1024]{1,0:T(8,128)(2,1)S(1)}, bf16[144,1024]{1,0:T(8,128)(2,1)}, u32[]{:S(2)}) copy-start(bf16[144,1024]{1,0:T(8,128)(2,1)} %copy-done.11) | copy-start | bytes 884740
  62.7 3.4 %copy-start.24 = (f32[8,1024]{1,0:T(8,128)S(1)}, f32[8,1024]{1,0:T(8,128)}, u32[]{:S(2)}) copy-start(f32[8,1024]{1,0:T(8,128)} %copy-done.23) | copy-start | bytes 98308
  68.5 5.9 %collective-permute-start.9 = (f32[3,1024]{1,0:T(4,128)S(1)}, f32[3,1024]{1,0:T(4,128)S(1)}, u32[]{:S(2)}, u32[]{:S(2)}) collective-permute-start(f32[3,1024]{1,0:T(4,128)S(1)} %get-tuple-element.57), channel_id=1, source_target_pairs={{0,4},{4,0},{8,12},{12,8},{1,5},{5,1},{9,13},{13,9},{2,6},{6,2},{1... | collective-permute-start | bytes 36872 | tf_op jit(solution)/shard_map/ppermute | solution.py:456
  74.3 4.8 %collective-permute-start.10 = (f32[3,1024]{1,0:T(4,128)S(1)}, f32[3,1024]{1,0:T(4,128)S(1)}, u32[]{:S(2)}, u32[]{:S(2)}) collective-permute-start(f32[3,1024]{1,0:T(4,128)S(1)} %add.6), channel_id=1, source_target_pairs={{0,8},{4,12},{8,0},{12,4},{1,9},{5,13},{9,1},{13,5},{2,10},{6,14},... | collective-permute-start | bytes 36872 | tf_op jit(solution)/shard_map/ppermute | solution.py:456
  79.1 3.8 %copy-start.30 = (f32[3,1024]{1,0:T(4,128)}, f32[3,1024]{1,0:T(4,128)S(1)}, u32[]{:S(2)}) copy-start(f32[3,1024]{1,0:T(4,128)S(1)} %add.7.a_ref) | copy-start | bytes 36868
  79.1 3.8 %collective-permute-start.11 = (f32[3,1024]{1,0:T(4,128)S(1)}, f32[3,1024]{1,0:T(4,128)S(1)}, u32[]{:S(2)}, u32[]{:S(2)}) collective-permute-start(f32[3,1024]{1,0:T(4,128)S(1)} %add.7.a_ref), channel_id=1, source_target_pairs={{0,16},{16,0},{1,17},{17,1},{2,18},{18,2},{3,19},{19,3},{4,20},{20... | collective-permute-start | bytes 36872 | tf_op jit(solution)/shard_map/ppermute | solution.py:456
  82.9 0.6 copy-start.31

commit v3 on v2

--- a/solution.py
+++ b/solution.py
@@ -244,8 +244,8 @@
 def attention_kernel(count, per, stack, g, docs_ref, q_ref, k_ref, v_ref, *refs):
     others = count - 1
     got = refs[:others]
-    out_ref, copy_ref = refs[-10:-8]
-    kb, vb, ka, va, bias_b, bias_f, bias_a, best = refs[-8:]
+    out_ref, copy_ref = refs[-11:-9]
+    kb, vb, ka, va, bias_b, bias_f, bias_a, bests, accs = refs[-9:]
     rows = q_ref.shape[0]
     stretch = rows // 2
     index = lax.axis_index("ctx")
@@ -298,6 +298,8 @@
         return (score.reshape(stack, stretch, size) + bias[None]).reshape(tall, size)
 
     for first in range(0, per, stack):
+        best = bests.at[first // stack % 2]
+        acc = accs.at[first // stack % 2]
         s_f = biased(dot_nt(stacked(first, 0), kb[:stretch, :]), bias_f[...])
         s_b = biased(dot_nt(stacked(first, stretch), kb[...]), bias_b[...])
         best[:tall, :] = s_f
@@ -319,13 +321,14 @@
         w_b = jnp.exp2((s_b - top_b) * factor).astype(BF16)
         out_f = jnp.dot(w_f, vb[:stretch, :], preferred_element_type=F32)
         out_b = jnp.dot(w_b, vb[...], preferred_element_type=F32)
+        acc[:tall, :] = out_f
+        acc[tall:, :] = out_b
         for r in range(others):
             top = jnp.where(lower[r], top_f, top_b)
             w = jnp.exp2((s_a[r] - top) * factor).astype(BF16)
-            out = jnp.dot(w, va[at_a[r], :], preferred_element_type=F32)
-            out_f += jnp.where(lower[r], out, 0.0)
-            out_b += jnp.where(lower[r], 0.0, out)
-        for half, out in enumerate((out_f, out_b)):
+            acc[places[r], :] += jnp.dot(w, va[at_a[r], :], preferred_element_type=F32)
+        for half in range(2):
+            out = acc[half * tall : (half + 1) * tall, :]
             result = (out[:, :DH] / out[:, DH:]).astype(BF16)
             sl = slice(half * stretch, (half + 1) * stretch)
             for j in range(stack):
@@ -451,9 +454,10 @@
     skip_ref[...] = total[groups : groups + 1, : skip_ref.shape[1]]
 
 
-def exchange(part, axis, step):
-    size = lax.axis_size(axis)
-    return lax.ppermute(part, axis, [(d, d ^ step) for d in range(size)])
+def exchange(part, shift):
+    axes = ("dp", "ctx")
+    size = lax.axis_size(axes)
+    return lax.ppermute(part, axes, [(d, d ^ shift) for d in range(size)])
 
 
 def body(
@@ -505,7 +509,7 @@
         ),
         in_specs=[VMEM] * 8,
         out_specs=(VMEM,) * (2 + 5 * groups),
-        compiler_params=params(32),
+        compiler_params=params(16),
         cost_estimate=cost(4 * rows * features * N, 8 * rows * features),
         name="opening",
     )(
@@ -528,28 +532,6 @@
         outs[2 + k * groups : 2 + (k + 1) * groups] for k in range(5)
     )
 
-    send = list(send)
-    got = [[] for _ in range(groups)]
-    ring = ring_order(count)
-    ring_pairs = [(ring[d], ring[(d + 1) % count]) for d in range(count)]
-    moving = kv
-    kv_got = []
-    for r in range(1, count):
-        for g in range(groups):
-            if r > 1:
-                send[g] = pl.pallas_call(
-                    functools.partial(chain_kernel, count, r - 1),
-                    out_shape=payload,
-                    in_specs=[VMEM] * 4,
-                    out_specs=VMEM,
-                    cost_estimate=cost(8 * N * width, 8 * N * width),
-                    name="chain",
-                )(got[g][-1], f_parts[g], b_parts[g], dec[g])
-            pairs = [(r - 1, r), (count - r, count - r - 1)]
-            got[g].append(lax.ppermute(send[g], "ctx", pairs))
-        moving = lax.ppermute(moving, "ctx", ring_pairs)
-        kv_got.append(moving)
-
     local = []
     for g in range(groups):
         local.append(
@@ -568,11 +550,36 @@
                     whole(rows, width),
                 ],
                 out_specs=(whole(rows, width),) * 3,
-                compiler_params=params(24),
+                compiler_params=params(16),
                 cost_estimate=cost(2 * rows * width * N, 16 * rows * width),
                 name="local",
             )(doc_ids, x, gate, bmat, cmat, ec, skip.reshape(1, heads), xw[g])
         )
+
+    send = list(send)
+    got = [[] for _ in range(groups)]
+    ring = ring_order(count)
+    ring_pairs = [(ring[d], ring[(d + 1) % count]) for d in range(count)]
+    moving = kv
+    kv_got = []
+    for r in range(1, count):
+        for g in range(groups):
+            if r == 2:
+                got[g][0], *local[g] = lax.optimization_barrier((got[g][0], *local[g]))
+            if r > 1:
+                send[g] = pl.pallas_call(
+                    functools.partial(chain_kernel, count, r - 1),
+                    out_shape=payload,
+                    in_specs=[VMEM] * 4,
+                    out_specs=VMEM,
+                    compiler_params=params(4),
+                    cost_estimate=cost(8 * N * width, 8 * N * width),
+                    name="chain",
+                )(got[g][-1], f_parts[g], b_parts[g], dec[g])
+            pairs = [(r - 1, r), (count - r, count - r - 1)]
+            got[g].append(lax.ppermute(send[g], "ctx", pairs))
+        moving = lax.ppermute(moving, "ctx", ring_pairs)
+        kv_got.append(moving)
 
     stack = 4 if per_kv % 4 == 0 and count <= 4 else 1
     teacher = None
@@ -600,10 +607,11 @@
                 pltpu.VMEM((stretch, (count + 1) * stretch), F32),
                 pltpu.VMEM((stretch, stretch), F32),
                 pltpu.VMEM((stretch, others * stretch), F32),
-                pltpu.VMEM((2 * stack * stretch, stretch), F32),
+                pltpu.VMEM((2, 2 * stack * stretch, stretch), F32),
+                pltpu.VMEM((2, 2 * stack * stretch, 2 * DH), F32),
             ],
             input_output_aliases={4 + others: 0} if more else {},
-            compiler_params=params(40),
+            compiler_params=params(24),
             cost_estimate=cost(
                 4 * (2 * count + 1) * stretch * stretch * per_kv * DH, 8 * rows * per_kv * DH
             ),
@@ -639,7 +647,7 @@
                 pltpu.VMEM((8, width), F32),
             ],
             input_output_aliases={9 + others: 0} if more else {},
-            compiler_params=params(32),
+            compiler_params=params(16),
             cost_estimate=cost(2 * rows * width * N, 20 * rows * width),
             name="final",
         )(
@@ -652,21 +660,22 @@
             *got[g],
             *more,
         )
-    steps = []
-    for axis in ("ctx", "dp"):
-        step = 1
-        while step < lax.axis_size(axis):
-            steps.append((axis, step))
-            step *= 2
-    for axis, step in steps[:-1]:
-        grads = grads + exchange(grads, axis, step)
+    partner = exchange(grads, 1)
+    if lax.axis_size("dp") == 2:
+        grads = (grads + partner) + (exchange(grads, count) + exchange(grads, count + 1))
+    else:
+        grads = grads + partner
+    shifts = [1 << k for k in range(1, count.bit_length() - 1)]
+    for shift in shifts[:-1]:
+        grads = grads + exchange(grads, shift)
     grad_gain, grad_skip = pl.pallas_call(
         closing_kernel,
         out_shape=(struct((1, features), F32), struct((1, heads), F32)),
         in_specs=[VMEM] * 2,
         out_specs=(VMEM,) * 2,
+        compiler_params=params(2),
         name="closing",
-    )(grads, exchange(grads, *steps[-1]))
+    )(grads, exchange(grads, shifts[-1]))
     return (teacher[None], student[None], grad_gain[0], grad_skip[0])
 
 

time: 85.5 us -> 69 us (0.81)
  local copies, waits for them, and re-layouts: 11 us -> 1.92 us
  Pallas kernels: 29.6 us -> 20.7 us
  waiting for transfers between devices: 15.3 us -> 21 us
  starting transfers between devices: 28.1 us -> 24.3 us
    unnamed x64 -> x20, local copies, waits for them, and re-layouts: 11 us -> 1.92 us
    ppermute x3, waiting for transfers between devices: 2.76 us -> 11.7 us  [body(): moving = lax.ppermute(moving, 'ctx', ring_pairs)]
    pallas_call x4, Pallas kernels: 7.37 us -> 0.02 us  [body(): pl.pallas_call(functools.partial(chain_kernel, count, r - 1), out_shape=p...]
    ppermute x3 -> x4, waiting for transfers between devices: 5.67 us -> 3.48 us  [exchange(): return lax.ppermute(part, axes, [(d, d ^ shift) for d in range(size)])]
    ppermute x3 -> x4, starting transfers between devices: 8.79 us -> 6.62 us  [exchange(): return lax.ppermute(part, axes, [(d, d ^ shift) for d in range(size)])]
    ppermute x3, starting transfers between devices: 9.34 us -> 7.51 us  [body(): moving = lax.ppermute(moving, 'ctx', ring_pairs)]
    ppermute x6, waiting for transfers between devices: 6.85 us -> 5.78 us  [body(): got[g].append(lax.ppermute(send[g], 'ctx', pairs))]
  transfers between devices with their start and end apart: 12 -> 13, of which waited for: 7 -> 8; matrix products, arithmetic and copies ran while one was open for 0% -> 0% of each run, Pallas kernels for 26% -> 20%
where the time goes in v3:
time: 69 us; the launch traced here: 68.7 us
  starting transfers between devices  24.3 us (35%)
  waiting for transfers between devices  21 us (30%)
  Pallas kernels  20.7 us (30%)
  local copies, waits for them, and re-layouts  1.92 us (3%)
  between operations  0.79 us (1%)
    ppermute x3, waiting for transfers between devices, body(): moving = lax.ppermute(moving, 'ctx', ring_pairs)  11.7 us
    ppermute x6, starting transfers between devices, body(): got[g].append(lax.ppermute(send[g], 'ctx', pairs))  10.2 us
    pallas_call x2, Pallas kernels, body(): pl.pallas_call(functools.partial(attention_kernel, count, per_kv, stack,...  9.81 us
    ppermute x3, starting transfers between devices, body(): moving = lax.ppermute(moving, 'ctx', ring_pairs)  7.51 us
    ppermute x4, starting transfers between devices, exchange(): return lax.ppermute(part, axes, [(d, d ^ shift) for d in range(size)])  6.62 us
    ppermute x6, waiting for transfers between devices, body(): got[g].append(lax.ppermute(send[g], 'ctx', pairs))  5.78 us
    pallas_call x2, Pallas kernels, body(): pl.pallas_call(functools.partial(final_kernel, count, g, groups, loss_sca...  4.85 us
    pallas_call x1, Pallas kernels, body(): pl.pallas_call(functools.partial(opening_kernel, count, groups), out_shap...  3.62 us
  transfers between devices with their start and end apart: 13, of which 8 were waited for; matrix products, arithmetic and copies ran while one was open for 0% of the time, Pallas kernels for 20%

profile of v3, /device:TPU:0, one launch (start us, length us, event | category | flops | bytes accessed | tf_op | source)
XLA Modules:
  0.0 68.7 jit_solution(2811785921290952501)
XLA Ops:
  0.6 0.0 copy-start
  0.6 0.0 copy-start.2
  0.7 0.0 copy-start.3
  0.7 3.6 %opening.1 = (bf16[256,512]{1,0:T(8,128)(2,1)S(1)}, f32[32,256]{1,0:T(8,128)S(1)}, bf16[256,1024]{1,0:T(8,128)(2,1)S(1)}, bf16[256,1024]{1,0:T(8,128)(2,1)S(1)},...) custom-call(s32[1,1024]{1,0:T(1,128)} %docs_ref.9, ...), custom_call_target="tpu_custom_call" | custom-call | flops 268435456 | bytes 4194304 | tf_op jit(solution)/shard_map/opening/pallas_call | solution.py:500
  4.3 3.2 %collective-permute-start = (bf16[256,512]{1,0:T(8,128)(2,1)S(1)}, bf16[256,512]{1,0:T(8,128)(2,1)S(1)}, u32[]{:S(2)}, u32[]{:S(2)}) collective-permute-start(bf16[256,512]{1,0:T(8,128)(2,1)S(1)} %get-tuple-element.40), channel_id=1, source_target_pairs={{0,4},{4,12},{12,8},{8,0},{1,5},{5,13},{13,9},{9,1},{2,6},{6,14},{... | collective-permute-start | bytes 786440 | tf_op jit(solution)/shard_map/ppermute | solution.py:581
  7.5 4.5 %collective-permute-start.6 = (bf16[144,1024]{1,0:T(8,128)(2,1)S(1)}, bf16[144,1024]{1,0:T(8,128)(2,1)S(1)}, u32[]{:S(2)}, u32[]{:S(2)}) collective-permute-start(bf16[144,1024]{1,0:T(8,128)(2,1)S(1)} %get-tuple-element.57), channel_id=1, source_target_pairs={{0,4},{12,8},{1,5},{13,9},{2,6},{14,10},{3,7},{15,11},{16,20},{28,... | collective-permute-start | bytes 884744 | tf_op jit(solution)/shard_map/ppermute | solution.py:580
  12.0 1.3 %collective-permute-start.3 = (bf16[144,1024]{1,0:T(8,128)(2,1)S(1)}, bf16[144,1024]{1,0:T(8,128)(2,1)S(1)}, u32[]{:S(2)}, u32[]{:S(2)}) collective-permute-start(bf16[144,1024]{1,0:T(8,128)(2,1)S(1)} %get-tuple-element.43), channel_id=1, source_target_pairs={{0,4},{12,8},{1,5},{13,9},{2,6},{14,10},{3,7},{15,11},{16,20},{28,... | collective-permute-start | bytes 884744 | tf_op jit(solution)/shard_map/ppermute | solution.py:580
  13.3 1.5 %collective-permute-done.refs_0_ = bf16[256,512]{1,0:T(8,128)(2,1)S(1)} collective-permute-done((bf16[256,512]{1,0:T(8,128)(2,1)S(1)}, bf16[256,512]{1,0:T(8,128)(2,1)S(1)}, u32[]{:S(2)}, u32[]{:S(2)}) %collective-permute-start) | collective-permute-done | bytes 262176 | tf_op jit(solution)/shard_map/ppermute | solution.py:581
  14.8 1.9 %collective-permute-start.1 = (bf16[256,512]{1,0:T(8,128)(2,1)S(1)}, bf16[256,512]{1,0:T(8,128)(2,1)S(1)}, u32[]{:S(2)}, u32[]{:S(2)}) collective-permute-start(bf16[256,512]{1,0:T(8,128)(2,1)S(1)} %collective-permute-done.refs_0_), channel_id=1, source_target_pairs={{0,4},{4,12},{12,8},{8,0},{1,5},{5,13},{13,9},{9,1},{2,6},{6,14},{... | collective-permute-start | bytes 786440 | tf_op jit(solution)/shard_map/ppermute | solution.py:581
  16.6 0.0 copy-start.7
  16.7 0.0 copy-done
  16.7 0.0 copy-done.2
  16.7 0.0 copy-done.3
  16.7 0.7 copy-done.7
  17.3 0.0 copy-done.9
  17.3 1.2 %copy-done.1 = bf16[1,256,2048]{2,1,0:T(8,128)(2,1)S(1)} copy-done((bf16[1,256,2048]{2,1,0:T(8,128)(2,1)S(1)}, bf16[1,256,2048]{2,1,0:T(8,128)(2,1)}, u32[]{:S(2)}) %copy-start.1) | copy-done | bytes 1048600
  18.6 0.9 %local.3 = (f32[256,1024]{1,0:T(8,128)S(1)}, f32[256,1024]{1,0:T(8,128)S(1)}, f32[256,1024]{1,0:T(8,128)S(1)}) custom-call(s32[1,1024]{1,0:T(1,128)S(1)} %copy-done.7, bf16[256,2048]{1,0:T(8,128)(2,1)S(1)} %bitcast.19, bf16[256,2048]{1,0:T(8,128)(2,1)S(1)} %bitcast.21, bf16[256,256]{1,0:T(8,128)(2,1)S(1)} %bitcast.28, bf16[256,256]{1,0:T(8,128)(2,1)S(1)} %bitcast.23, ...), custom_call_target="tpu_custom_call" | custom-call | flops 67108864 | bytes 4194304 | tf_op jit(solution)/shard_map/local/pallas_call | solution.py:538
  19.4 1.0 %collective-permute-done.6.got_ref.refs_0_ = bf16[144,1024]{1,0:T(8,128)(2,1)S(1)} collective-permute-done((bf16[144,1024]{1,0:T(8,128)(2,1)S(1)}, bf16[144,1024]{1,0:T(8,128)(2,1)S(1)}, u32[]{:S(2)}, u32[]{:S(2)}) %collective-permute-start.6) | collective-permute-done | bytes 294944 | tf_op jit(solution)/shard_map/ppermute | solution.py:580
  20.5 0.7 collective-permute-start.7
  21.2 0.9 %local.2 = (f32[256,1024]{1,0:T(8,128)S(1)}, f32[256,1024]{1,0:T(8,128)S(1)}, f32[256,1024]{1,0:T(8,128)S(1)}) custom-call(s32[1,1024]{1,0:T(1,128)S(1)} %copy-done.7, bf16[256,2048]{1,0:T(8,128)(2,1)S(1)} %bitcast.20, bf16[256,2048]{1,0:T(8,128)(2,1)S(1)} %bitcast.22, bf16[256,256]{1,0:T(8,128)(2,1)S(1)} %bitcast.29, bf16[256,256]{1,0:T(8,128)(2,1)S(1)} %bitcast.24, ...), custom_call_target="tpu_custom_call" | custom-call | flops 67108864 | bytes 4194304 | tf_op jit(solution)/shard_map/local/pallas_call | solution.py:538
  22.1 4.7 %collective-permute-done.3.got_ref.refs_0_ = bf16[144,1024]{1,0:T(8,128)(2,1)S(1)} collective-permute-done((bf16[144,1024]{1,0:T(8,128)(2,1)S(1)}, bf16[144,1024]{1,0:T(8,128)(2,1)S(1)}, u32[]{:S(2)}, u32[]{:S(2)}) %collective-permute-start.3) | collective-permute-done | bytes 294944 | tf_op jit(solution)/shard_map/ppermute | solution.py:580
  26.8 0.8 %collective-permute-start.4 = (bf16[144,1024]{1,0:T(8,128)(2,1)S(1)}, bf16[144,1024]{1,0:T(8,128)(2,1)S(1)}, u32[]{:S(2)}, u32[]{:S(2)}) collective-permute-start(bf16[144,1024]{1,0:T(8,128)(2,1)S(1)} %chain.4), channel_id=1, source_target_pairs={{4,8},{8,4},{5,9},{9,5},{6,10},{10,6},{7,11},{11,7},{20,24},{24,20... | collective-permute-start | bytes 884744 | tf_op jit(solution)/shard_map/ppermute | solution.py:580
  27.6 3.7 %collective-permute-done.1.refs_1_ = bf16[256,512]{1,0:T(8,128)(2,1)S(1)} collective-permute-done((bf16[256,512]{1,0:T(8,128)(2,1)S(1)}, bf16[256,512]{1,0:T(8,128)(2,1)S(1)}, u32[]{:S(2)}, u32[]{:S(2)}) %collective-permute-start.1) | collective-permute-done | bytes 262176 | tf_op jit(solution)/shard_map/ppermute | solution.py:581
  31.3 2.5 %collective-permute-start.2 = (bf16[256,512]{1,0:T(8,128)(2,1)S(1)}, bf16[256,512]{1,0:T(8,128)(2,1)S(1)}, u32[]{:S(2)}, u32[]{:S(2)}) collective-permute-start(bf16[256,512]{1,0:T(8,128)(2,1)S(1)} %collective-permute-done.1.refs_1_), channel_id=1, source_target_pairs={{0,4},{4,12},{12,8},{8,0},{1,5},{5,13},{13,9},{9,1},{2,6},{6,14},{... | collective-permute-start | bytes 786440 | tf_op jit(solution)/shard_map/ppermute | solution.py:581
  33.8 0.0 collective-permute-done.7.got_ref.refs_1_
  33.8 1.4 %collective-permute-start.8 = (bf16[144,1024]{1,0:T(8,128)(2,1)S(1)}, bf16[144,1024]{1,0:T(8,128)(2,1)S(1)}, u32[]{:S(2)}, u32[]{:S(2)}) collective-permute-start(bf16[144,1024]{1,0:T(8,128)(2,1)S(1)} %chain.7), channel_id=1, source_target_pairs={{8,12},{4,0},{9,13},{5,1},{10,14},{6,2},{11,15},{7,3},{24,28},{20,... | collective-permute-start | bytes 884744 | tf_op jit(solution)/shard_map/ppermute | solution.py:580
  35.2 0.0 collective-permute-done.4.got_ref.refs_1_
  35.2 1.5 %collective-permute-start.5 = (bf16[144,1024]{1,0:T(8,128)(2,1)S(1)}, bf16[144,1024]{1,0:T(8,128)(2,1)S(1)}, u32[]{:S(2)}, u32[]{:S(2)}) collective-permute-start(bf16[144,1024]{1,0:T(8,128)(2,1)S(1)} %chain.5), channel_id=1, source_target_pairs={{8,12},{4,0},{9,13},{5,1},{10,14},{6,2},{11,15},{7,3},{24,28},{20,... | collective-permute-start | bytes 884744 | tf_op jit(solution)/shard_map/ppermute | solution.py:580
  36.7 6.6 %collective-permute-done.2.refs_2_ = bf16[256,512]{1,0:T(8,128)(2,1)S(1)} collective-permute-done((bf16[256,512]{1,0:T(8,128)(2,1)S(1)}, bf16[256,512]{1,0:T(8,128)(2,1)S(1)}, u32[]{:S(2)}, u32[]{:S(2)}) %collective-permute-start.2) | collective-permute-done | bytes 262176 | tf_op jit(solution)/shard_map/ppermute | solution.py:581
  43.3 0.0 copy-done.4
  43.3 0.0 copy-done.5
  43.3 0.0 copy-done.6
  43.3 4.9 %attention.2 = (bf16[256,2048]{1,0:T(8,128)(2,1)}, bf16[256,1024]{1,0:T(8,128)(2,1)S(1)}) custom-call(s32[1,1024]{1,0:T(1,128)S(1)} %copy-done.7, bf16[256,2048]{1,0:T(8,128)(2,1)S(1)} %bitcast.30, bf16[256,256]{1,0:T(8,128)(2,1)S(1)} %bitcast.33, bf16[256,256]{1,0:T(8,128)(2,1)S(1)} %bitcast.36, bf16[256,512]{1,0:T(8,128)(2,1)S(1)} %collective-permute-done.refs_0_, ...), custom_call_target="tpu_custom_call" | custom-call | flops 603979776 | bytes 2097152 | tf_op jit(solution)/shard_map/attention/pallas_call | solution.py:589
  48.2 4.9 %attention.3 = (bf16[256,2048]{1,0:T(8,128)(2,1)}, bf16[256,1024]{1,0:T(8,128)(2,1)S(1)}) custom-call(s32[1,1024]{1,0:T(1,128)S(1)} %copy-done.7, bf16[256,2048]{1,0:T(8,128)(2,1)S(1)} %bitcast.31, bf16[256,256]{1,0:T(8,128)(2,1)S(1)} %bitcast.34, bf16[256,256]{1,0:T(8,128)(2,1)S(1)} %bitcast.37, ...), custom_call_target="tpu_custom_call", output_to_operand_aliasing={{0}: (7, {})} | custom-call | flops 603979776 | bytes 2097152 | tf_op jit(solution)/shard_map/attention/pallas_call | solution.py:589
  53.1 0.0 collective-permute-done.8.refs_2_
  53.1 0.0 copy-done.8
  53.1 2.4 %final.2 = (bf16[256,2048]{1,0:T(8,128)(2,1)}, f32[3,1024]{1,0:T(4,128)S(1)}) custom-call(f32[256,1024]{1,0:T(8,128)S(1)} %get-tuple-element.62.pre_ref, f32[256,1024]{1,0:T(8,128)S(1)} %get-tuple-element.63.reach_ref, f32[256,1024]{1,0:T(8,128)S(1)} %get-tuple-element.64.sx_ref, bf16[256,256]{1,0:T(8,128)(2,1)S(1)} %bitcast.25, ...), custom_call_target="tpu_custom_call" | custom-call | flops 67108864 | bytes 5242880 | tf_op jit(solution)/shard_map/final/pallas_call | solution.py:625
  55.6 0.0 collective-permute-done.5.refs_2_
  55.6 2.4 %final.3 = (bf16[256,2048]{1,0:T(8,128)(2,1)}, f32[3,1024]{1,0:T(4,128)S(1)}) custom-call(f32[256,1024]{1,0:T(8,128)S(1)} %get-tuple-element.49.pre_ref, f32[256,1024]{1,0:T(8,128)S(1)} %get-tuple-element.50.reach_ref, f32[256,1024]{1,0:T(8,128)S(1)} %get-tuple-element.51.sx_ref, bf16[256,256]{1,0:T(8,128)(2,1)S(1)} %bitcast.26, ...), custom_call_target="tpu_custom_call", output_to_operand_aliasing={{0}: (12, {})} | custom-call | flops 67108864 | bytes 5242880 | tf_op jit(solution)/shard_map/final/pallas_call | solution.py:625
  58.0 0.6 collective-permute-start.11
  58.6 0.9 %collective-permute-start.10 = (f32[3,1024]{1,0:T(4,128)S(1)}, f32[3,1024]{1,0:T(4,128)S(1)}, u32[]{:S(2)}, u32[]{:S(2)}) collective-permute-start(f32[3,1024]{1,0:T(4,128)S(1)} %get-tuple-element.73), channel_id=1, source_target_pairs={{0,16},{4,20},{8,24},{12,28},{16,0},{20,4},{24,8},{28,12},{1,17},{... | collective-permute-start | bytes 36872 | tf_op jit(solution)/shard_map/ppermute | solution.py:460
  59.5 2.0 %collective-permute-start.9 = (f32[3,1024]{1,0:T(4,128)S(1)}, f32[3,1024]{1,0:T(4,128)S(1)}, u32[]{:S(2)}, u32[]{:S(2)}) collective-permute-start(f32[3,1024]{1,0:T(4,128)S(1)} %get-tuple-element.73), channel_id=1, source_target_pairs={{0,4},{4,0},{8,12},{12,8},{16,20},{20,16},{24,28},{28,24},{1,5},{5... | collective-permute-start | bytes 36872 | tf_op jit(solution)/shard_map/ppermute | solution.py:460
  61.5 1.1 %collective-permute-done.11 = f32[3,1024]{1,0:T(4,128)S(1)} collective-permute-done((f32[3,1024]{1,0:T(4,128)S(1)}, f32[3,1024]{1,0:T(4,128)S(1)}, u32[]{:S(2)}, u32[]{:S(2)}) %collective-permute-start.11) | collective-permute-done | bytes 12320 | tf_op jit(solution)/shard_map/ppermute | solution.py:460
  62.6 0.0 collective-permute-done.10
  62.6 0.6 collective-permute-done.9
  63.3 3.1 %collective-permute-start.12 = (f32[3,1024]{1,0:T(4,128)S(1)}, f32[3,1024]{1,0:T(4,128)S(1)}, u32[]{:S(2)}, u32[]{:S(2)}) collective-permute-start(f32[3,1024]{1,0:T(4,128)S(1)} %add_add_fusion.a_ref), channel_id=1, source_target_pairs={{0,8},{4,12},{8,0},{12,4},{16,24},{20,28},{24,16},{28,20},{1,9},{5... | collective-permute-start | bytes 36872 | tf_op jit(solution)/shard_map/ppermute | solution.py:460
  66.4 1.7 %collective-permute-done.12.b_ref = f32[3,1024]{1,0:T(4,128)S(1)} collective-permute-done((f32[3,1024]{1,0:T(4,128)S(1)}, f32[3,1024]{1,0:T(4,128)S(1)}, u32[]{:S(2)}, u32[]{:S(2)}) %collective-permute-start.12) | collective-permute-done | bytes 12320 | tf_op jit(solution)/shard_map/ppermute | solution.py:460
  68.1 0.6 closing.1
  (11 shorter events, 0.0 us)
Async XLA Ops:
  0.6 16.0 %copy-start = (bf16[1,256,2048]{2,1,0:T(8,128)(2,1)S(1)}, bf16[1,256,2048]{2,1,0:T(8,128)(2,1)}, u32[]{:S(2)}) copy-start(bf16[1,256,2048]{2,1,0:T(8,128)(2,1)} %param.17) | copy-start | bytes 3145732
  0.6 16.0 %copy-start.2 = (bf16[1,256,256]{2,1,0:T(8,128)(2,1)S(1)}, bf16[1,256,256]{2,1,0:T(8,128)(2,1)}, u32[]{:S(2)}) copy-start(bf16[1,256,256]{2,1,0:T(8,128)(2,1)} %param.20) | copy-start | bytes 393220
  0.7 16.0 %copy-start.3 = (bf16[1,256,256]{2,1,0:T(8,128)(2,1)S(1)}, bf16[1,256,256]{2,1,0:T(8,128)(2,1)}, u32[]{:S(2)}) copy-start(bf16[1,256,256]{2,1,0:T(8,128)(2,1)} %param.19) | copy-start | bytes 393220
  4.3 10.5 %collective-permute-start = (bf16[256,512]{1,0:T(8,128)(2,1)S(1)}, bf16[256,512]{1,0:T(8,128)(2,1)S(1)}, u32[]{:S(2)}, u32[]{:S(2)}) collective-permute-start(bf16[256,512]{1,0:T(8,128)(2,1)S(1)} %get-tuple-element.40), channel_id=1, source_target_pairs={{0,4},{4,12},{12,8},{8,0},{1,5},{5,13},{13,9},{9,1},{2,6},{6,14},{... | collective-permute-start | bytes 786440 | tf_op jit(solution)/shard_map/ppermute | solution.py:581
  7.5 13.0 %collective-permute-start.6 = (bf16[144,1024]{1,0:T(8,128)(2,1)S(1)}, bf16[144,1024]{1,0:T(8,128)(2,1)S(1)}, u32[]{:S(2)}, u32[]{:S(2)}) collective-permute-start(bf16[144,1024]{1,0:T(8,128)(2,1)S(1)} %get-tuple-element.57), channel_id=1, source_target_pairs={{0,4},{12,8},{1,5},{13,9},{2,6},{14,10},{3,7},{15,11},{16,20},{28,... | collective-permute-start | bytes 884744 | tf_op jit(solution)/shard_map/ppermute | solution.py:580
  12.0 14.8 %collective-permute-start.3 = (bf16[144,1024]{1,0:T(8,128)(2,1)S(1)}, bf16[144,1024]{1,0:T(8,128)(2,1)S(1)}, u32[]{:S(2)}, u32[]{:S(2)}) collective-permute-start(bf16[144,1024]{1,0:T(8,128)(2,1)S(1)} %get-tuple-element.43), channel_id=1, source_target_pairs={{0,4},{12,8},{1,5},{13,9},{2,6},{14,10},{3,7},{15,11},{16,20},{28,... | collective-permute-start | bytes 884744 | tf_op jit(solution)/shard_map/ppermute | solution.py:580
  14.8 16.5 %collective-permute-start.1 = (bf16[256,512]{1,0:T(8,128)(2,1)S(1)}, bf16[256,512]{1,0:T(8,128)(2,1)S(1)}, u32[]{:S(2)}, u32[]{:S(2)}) collective-permute-start(bf16[256,512]{1,0:T(8,128)(2,1)S(1)} %collective-permute-done.refs_0_), channel_id=1, source_target_pairs={{0,4},{4,12},{12,8},{8,0},{1,5},{5,13},{13,9},{9,1},{2,6},{6,14},{... | collective-permute-start | bytes 786440 | tf_op jit(solution)/shard_map/ppermute | solution.py:581
  16.6 0.7 copy-start.7
  16.6 0.7 %copy-start.9 = (f32[32]{0:T(128)S(1)}, f32[32]{0:T(128)}, u32[]{:S(2)}) copy-start(f32[32]{0:T(128)} %param.24) | copy-start | bytes 388
  17.3 1.2 %copy-start.1 = (bf16[1,256,2048]{2,1,0:T(8,128)(2,1)S(1)}, bf16[1,256,2048]{2,1,0:T(8,128)(2,1)}, u32[]{:S(2)}) copy-start(bf16[1,256,2048]{2,1,0:T(8,128)(2,1)} %param.18) | copy-start | bytes 3145732
  20.5 13.3 %collective-permute-start.7 = (bf16[144,1024]{1,0:T(8,128)(2,1)S(1)}, bf16[144,1024]{1,0:T(8,128)(2,1)S(1)}, u32[]{:S(2)}, u32[]{:S(2)}) collective-permute-start(bf16[144,1024]{1,0:T(8,128)(2,1)S(1)} %chain.6), channel_id=1, source_target_pairs={{4,8},{8,4},{5,9},{9,5},{6,10},{10,6},{7,11},{11,7},{20,24},{24,20... | collective-permute-start | bytes 884744 | tf_op jit(solution)/shard_map/ppermute | solution.py:580
  26.8 16.5 %copy-start.4 = (bf16[1,256,2048]{2,1,0:T(8,128)(2,1)S(1)}, bf16[1,256,2048]{2,1,0:T(8,128)(2,1)}, u32[]{:S(2)}) copy-start(bf16[1,256,2048]{2,1,0:T(8,128)(2,1)} %param.13) | copy-start | bytes 3145732
  26.8 8.4 %collective-permute-start.4 = (bf16[144,1024]{1,0:T(8,128)(2,1)S(1)}, bf16[144,1024]{1,0:T(8,128)(2,1)S(1)}, u32[]{:S(2)}, u32[]{:S(2)}) collective-permute-start(bf16[144,1024]{1,0:T(8,128)(2,1)S(1)} %chain.4), channel_id=1, source_target_pairs={{4,8},{8,4},{5,9},{9,5},{6,10},{10,6},{7,11},{11,7},{20,24},{24,20... | collective-permute-start | bytes 884744 | tf_op jit(solution)/shard_map/ppermute | solution.py:580
  31.3 12.0 %collective-permute-start.2 = (bf16[256,512]{1,0:T(8,128)(2,1)S(1)}, bf16[256,512]{1,0:T(8,128)(2,1)S(1)}, u32[]{:S(2)}, u32[]{:S(2)}) collective-permute-start(bf16[256,512]{1,0:T(8,128)(2,1)S(1)} %collective-permute-done.1.refs_1_), channel_id=1, source_target_pairs={{0,4},{4,12},{12,8},{8,0},{1,5},{5,13},{13,9},{9,1},{2,6},{6,14},{... | collective-permute-start | bytes 786440 | tf_op jit(solution)/shard_map/ppermute | solution.py:581
  33.8 9.5 %copy-start.5 = (bf16[1,256,256]{2,1,0:T(8,128)(2,1)S(1)}, bf16[1,256,256]{2,1,0:T(8,128)(2,1)}, u32[]{:S(2)}) copy-start(bf16[1,256,256]{2,1,0:T(8,128)(2,1)} %param.14) | copy-start | bytes 393220
  33.8 9.5 %copy-start.6 = (bf16[1,256,256]{2,1,0:T(8,128)(2,1)S(1)}, bf16[1,256,256]{2,1,0:T(8,128)(2,1)}, u32[]{:S(2)}) copy-start(bf16[1,256,256]{2,1,0:T(8,128)(2,1)} %param.15) | copy-start | bytes 393220
  33.8 19.4 %collective-permute-start.8 = (bf16[144,1024]{1,0:T(8,128)(2,1)S(1)}, bf16[144,1024]{1,0:T(8,128)(2,1)S(1)}, u32[]{:S(2)}, u32[]{:S(2)}) collective-permute-start(bf16[144,1024]{1,0:T(8,128)(2,1)S(1)} %chain.7), channel_id=1, source_target_pairs={{8,12},{4,0},{9,13},{5,1},{10,14},{6,2},{11,15},{7,3},{24,28},{20,... | collective-permute-start | bytes 884744 | tf_op jit(solution)/shard_map/ppermute | solution.py:580
  35.2 20.3 %collective-permute-start.5 = (bf16[144,1024]{1,0:T(8,128)(2,1)S(1)}, bf16[144,1024]{1,0:T(8,128)(2,1)S(1)}, u32[]{:S(2)}, u32[]{:S(2)}) collective-permute-start(bf16[144,1024]{1,0:T(8,128)(2,1)S(1)} %chain.5), channel_id=1, source_target_pairs={{8,12},{4,0},{9,13},{5,1},{10,14},{6,2},{11,15},{7,3},{24,28},{20,... | collective-permute-start | bytes 884744 | tf_op jit(solution)/shard_map/ppermute | solution.py:580
  48.2 4.9 %copy-start.8 = (f32[2048]{0:T(1024)S(1)}, f32[2048]{0:T(1024)}, u32[]{:S(2)}) copy-start(f32[2048]{0:T(1024)} %param.25) | copy-start | bytes 24580
  58.0 4.6 %collective-permute-start.11 = (f32[3,1024]{1,0:T(4,128)S(1)}, f32[3,1024]{1,0:T(4,128)S(1)}, u32[]{:S(2)}, u32[]{:S(2)}) collective-permute-start(f32[3,1024]{1,0:T(4,128)S(1)} %get-tuple-element.73), channel_id=1, source_target_pairs={{0,20},{4,16},{8,28},{12,24},{16,4},{20,0},{24,12},{28,8},{1,21},{... | collective-permute-start | bytes 36872 | tf_op jit(solution)/shard_map/ppermute | solution.py:460
  58.6 4.0 %collective-permute-start.10 = (f32[3,1024]{1,0:T(4,128)S(1)}, f32[3,1024]{1,0:T(4,128)S(1)}, u32[]{:S(2)}, u32[]{:S(2)}) collective-permute-start(f32[3,1024]{1,0:T(4,128)S(1)} %get-tuple-element.73), channel_id=1, source_target_pairs={{0,16},{4,20},{8,24},{12,28},{16,0},{20,4},{24,8},{28,12},{1,17},{... | collective-permute-start | bytes 36872 | tf_op jit(solution)/shard_map/ppermute | solution.py:460
  59.5 3.7 %collective-permute-start.9 = (f32[3,1024]{1,0:T(4,128)S(1)}, f32[3,1024]{1,0:T(4,128)S(1)}, u32[]{:S(2)}, u32[]{:S(2)}) collective-permute-start(f32[3,1024]{1,0:T(4,128)S(1)} %get-tuple-element.73), channel_id=1, source_target_pairs={{0,4},{4,0},{8,12},{12,8},{16,20},{20,16},{24,28},{28,24},{1,5},{5... | collective-permute-start | bytes 36872 | tf_op jit(solution)/shard_map/ppermute | solution.py:460
  63.3 4.9 %collective-permute-start.12 = (f32[3,1024]{1,0:T(4,128)S(1)}, f32[3,1024]{1,0:T(4,128)S(1)}, u32[]{:S(2)}, u32[]{:S(2)}) collective-permute-start(f32[3,1024]{1,0:T(4,128)S(1)} %add_add_fusion.a_ref), channel_id=1, source_target_pairs={{0,8},{4,12},{8,0},{12,4},{16,24},{20,28},{24,16},{28,20},{1,9},{5... | collective-permute-start | bytes 36872 | tf_op jit(solution)/shard_map/ppermute | solution.py:460

commit v4 on v3

--- a/solution.py
+++ b/solution.py
@@ -241,16 +241,40 @@
             reach_ref[at, :] = reached[here] * fade
 
 
+def pair_kernel(a_ref, b_ref, out_ref):
+    rows = a_ref.shape[0]
+    out_ref[:rows, :] = a_ref[...]
+    out_ref[rows:, :] = b_ref[...]
+
+
+def arrivals(index, count, rows, refs):
+    if count != 4:
+        return [(ring_source(index, count, r + 1), [(None, refs[r], 0)]) for r in range(count - 1)]
+    near, own_of_middle, next_of_middle, far = refs
+    middle = (index == 1) | (index == 2)
+    low = index < 2
+    return [
+        (index ^ 1, [(None, near, 0)]),
+        (
+            jnp.where(low, 2, 1),
+            [(middle, own_of_middle, 0), (jnp.logical_not(middle), far, 0)],
+        ),
+        (
+            jnp.where(low, 3, 0),
+            [(middle, next_of_middle, 0), (jnp.logical_not(middle), far, rows)],
+        ),
+    ]
+
+
 def attention_kernel(count, per, stack, g, docs_ref, q_ref, k_ref, v_ref, *refs):
     others = count - 1
-    got = refs[:others]
-    out_ref, copy_ref = refs[-11:-9]
-    kb, vb, ka, va, bias_b, bias_f, bias_a, bests, accs = refs[-9:]
+    sent = 4 if count == 4 else others
+    out_ref, copy_ref, kt, vt, bias_f, bias_b, bias_a = refs[-7:]
     rows = q_ref.shape[0]
     stretch = rows // 2
     index = lax.axis_index("ctx")
     last = 2 * count - 1
-    kv_width = got[0].shape[1] // 2
+    kv_width = refs[0].shape[1] // 2
     k_cols = slice(g * DH, (g + 1) * DH)
     v_cols = slice(kv_width + g * DH, kv_width + (g + 1) * DH)
     row_f = doc_row(docs_ref, index, stretch).astype(F32)
@@ -258,38 +282,51 @@
     col_f = as_column(row_f)
     col_b = as_column(row_b)
     triangle = lower_triangle(stretch)
+
+    def tile(k):
+        return slice(k * stretch, (k + 1) * stretch)
+
     bias_f[...] = jnp.where(triangle & (col_f == row_f), 0.0, MASKED)
-    bias_b[:, :stretch] = jnp.where(col_b == row_f, 0.0, MASKED)
-    bias_b[:, stretch:rows] = jnp.where(triangle & (col_b == row_b), 0.0, MASKED)
-    vb[:, DH:] = jnp.ones((vb.shape[0], DH), BF16)
-    va[:, DH:] = jnp.ones((va.shape[0], DH), BF16)
-    kb[:rows, :] = k_ref[...]
-    vb[:rows, :DH] = v_ref[...]
-    lower, at_a, picks = [], [], []
-    for r in range(others):
-        at_b = slice(rows + r * stretch, rows + (r + 1) * stretch)
-        at_a.append(slice(r * stretch, (r + 1) * stretch))
-        source = ring_source(index, count, r + 1)
+    bias_b[:, tile(0)] = jnp.where(col_b == row_f, 0.0, MASKED)
+    bias_b[:, tile(1)] = jnp.where(triangle & (col_b == row_b), 0.0, MASKED)
+    vt[:, DH:] = jnp.ones((vt.shape[0], DH), BF16)
+    kt[tile(0), :] = k_ref[:stretch, :]
+    vt[tile(0), :DH] = v_ref[:stretch, :]
+    kt[tile(count), :] = k_ref[stretch:, :]
+    vt[tile(count), :DH] = v_ref[stretch:, :]
+    lower = []
+    for r, (source, places) in enumerate(arrivals(index, count, rows, refs[:sent])):
         lower.append(source < index)
-        picks.append(jnp.where(lower[r], 0, 1))
-        own = pl.ds(pl.multiple_of(picks[r] * stretch, stretch), stretch)
-        kb[at_b, :] = got[r][:stretch, k_cols]
-        vb[at_b, :DH] = got[r][:stretch, v_cols]
-        ka[at_a[r], :] = got[r][own, k_cols]
-        va[at_a[r], :DH] = got[r][own, v_cols]
+        for condition, ref, first in places:
+
+            def fetch(ref=ref, first=first, r=r):
+                front = slice(first, first + stretch)
+                start = jnp.where(lower[r], first, first + stretch)
+                own = pl.ds(pl.multiple_of(start, stretch), stretch)
+                kt[tile(1 + r), :] = ref[own, k_cols]
+                vt[tile(1 + r), :DH] = ref[own, v_cols]
+                kt[tile(count + 1 + r), :] = ref[front, k_cols]
+                vt[tile(count + 1 + r), :DH] = ref[front, v_cols]
+
+            if condition is None:
+                fetch()
+            else:
+                pl.when(condition)(fetch)
         key_f = doc_row(docs_ref, source, stretch).astype(F32)
         key_a = doc_row(docs_ref, jnp.where(lower[r], source, last - source), stretch).astype(F32)
-        bias_b[:, at_b] = jnp.where(col_b == key_f, 0.0, MASKED)
-        bias_a[:, at_a[r]] = jnp.where(
-            jnp.where(lower[r], col_f, col_b) == key_a, 0.0, MASKED
-        )
+        bias_b[:, tile(2 + r)] = jnp.where(col_b == key_f, 0.0, MASKED)
+        bias_a[:, tile(r)] = jnp.where(jnp.where(lower[r], col_f, col_b) == key_a, 0.0, MASKED)
 
     factor = math.log2(math.e) / math.sqrt(DH)
     tall = stack * stretch
+    half_keys = count * stretch
 
     def stacked(first, base):
         return jnp.concatenate(
-            [q_ref[pl.ds(base, stretch), (first + j) * DH : (first + j + 1) * DH] for j in range(stack)],
+            [
+                q_ref[base : base + stretch, (first + j) * DH : (first + j + 1) * DH]
+                for j in range(stack)
+            ],
             axis=0,
         )
 
@@ -298,43 +335,42 @@
         return (score.reshape(stack, stretch, size) + bias[None]).reshape(tall, size)
 
     for first in range(0, per, stack):
-        best = bests.at[first // stack % 2]
-        acc = accs.at[first // stack % 2]
-        s_f = biased(dot_nt(stacked(first, 0), kb[:stretch, :]), bias_f[...])
-        s_b = biased(dot_nt(stacked(first, stretch), kb[...]), bias_b[...])
-        best[:tall, :] = s_f
-        top = s_b[:, :stretch]
+        s_f = dot_nt(stacked(first, 0), kt[:half_keys, :])
+        s_b = dot_nt(stacked(first, stretch), kt[...])
+        t_f = biased(s_f[:, tile(0)], bias_f[...])
+        t_b = [biased(s_b[:, tile(0)], bias_b[:, tile(0)])]
         for k in range(1, count + 1):
-            top = jnp.maximum(top, s_b[:, k * stretch : (k + 1) * stretch])
-        best[tall:, :] = top
-        s_a = []
-        places = []
+            t_b.append(biased(s_b[:, tile(count + k - 1)], bias_b[:, tile(k)]))
+        t_a = []
         for r in range(others):
-            base = pl.multiple_of(picks[r] * stretch, stretch)
-            place = pl.ds(pl.multiple_of(picks[r] * tall, tall), tall)
-            s_a.append(biased(dot_nt(stacked(first, base), ka[at_a[r], :]), bias_a[:, at_a[r]]))
-            best[place, :] = jnp.maximum(best[place, :], s_a[r])
-            places.append(place)
-        top_f = jnp.max(best[:tall, :], axis=1, keepdims=True)
-        top_b = jnp.max(best[tall:, :], axis=1, keepdims=True)
-        w_f = jnp.exp2((s_f - top_f) * factor).astype(BF16)
-        w_b = jnp.exp2((s_b - top_b) * factor).astype(BF16)
-        out_f = jnp.dot(w_f, vb[:stretch, :], preferred_element_type=F32)
-        out_b = jnp.dot(w_b, vb[...], preferred_element_type=F32)
-        acc[:tall, :] = out_f
-        acc[tall:, :] = out_b
+            score = jnp.where(lower[r], s_f[:, tile(1 + r)], s_b[:, tile(1 + r)])
+            t_a.append(biased(score, bias_a[:, tile(r)]))
+        best_f = t_f
+        best_b = functools.reduce(jnp.maximum, t_b)
+        for r in range(others):
+            best_f = jnp.maximum(best_f, jnp.where(lower[r], t_a[r], MASKED))
+            best_b = jnp.maximum(best_b, jnp.where(lower[r], MASKED, t_a[r]))
+        top_f = jnp.max(best_f, axis=1, keepdims=True)
+        top_b = jnp.max(best_b, axis=1, keepdims=True)
+        w_f = [jnp.exp2((t_f - top_f) * factor).astype(BF16)]
+        w_b = [jnp.exp2((t - top_b) * factor).astype(BF16) for t in t_b]
+        w_x = []
         for r in range(others):
             top = jnp.where(lower[r], top_f, top_b)
-            w = jnp.exp2((s_a[r] - top) * factor).astype(BF16)
-            acc[places[r], :] += jnp.dot(w, va[at_a[r], :], preferred_element_type=F32)
-        for half in range(2):
-            out = acc[half * tall : (half + 1) * tall, :]
+            w = jnp.exp2((t_a[r] - top) * factor)
+            w_f.append(jnp.where(lower[r], w, 0.0).astype(BF16))
+            w_x.append(jnp.where(lower[r], 0.0, w).astype(BF16))
+        w_b = w_b[:1] + w_x + w_b[1:]
+        out_f = jnp.dot(
+            jnp.concatenate(w_f, axis=1), vt[:half_keys, :], preferred_element_type=F32
+        )
+        out_b = jnp.dot(jnp.concatenate(w_b, axis=1), vt[...], preferred_element_type=F32)
+        for half, out in enumerate((out_f, out_b)):
             result = (out[:, :DH] / out[:, DH:]).astype(BF16)
-            sl = slice(half * stretch, (half + 1) * stretch)
             for j in range(stack):
                 cols = slice((first + j) * DH, (first + j + 1) * DH)
-                out_ref[sl, cols] = result[j * stretch : (j + 1) * stretch]
-                copy_ref[sl, cols] = result[j * stretch : (j + 1) * stretch]
+                out_ref[tile(half), cols] = result[tile(j)]
+                copy_ref[tile(half), cols] = result[tile(j)]
 
 
 def final_kernel(
@@ -558,10 +594,29 @@
 
     send = list(send)
     got = [[] for _ in range(groups)]
-    ring = ring_order(count)
-    ring_pairs = [(ring[d], ring[(d + 1) % count]) for d in range(count)]
-    moving = kv
-    kv_got = []
+    if count == 4:
+        across = [(1, 2), (2, 1)]
+        near = lax.ppermute(kv, "ctx", [(0, 1), (1, 0), (2, 3), (3, 2)])
+        middle = lax.ppermute(kv, "ctx", across)
+        beyond = lax.ppermute(near, "ctx", across)
+        both = pl.pallas_call(
+            pair_kernel,
+            out_shape=struct((2 * rows, kv.shape[1]), BF16),
+            in_specs=[VMEM] * 2,
+            out_specs=VMEM,
+            compiler_params=params(4),
+            cost_estimate=cost(0, 4 * kv.size),
+            name="pair",
+        )(middle, beyond)
+        far = lax.ppermute(both, "ctx", [(1, 0), (2, 3)])
+        kv_got = [near, middle, beyond, far]
+    else:
+        ring = ring_order(count)
+        ring_pairs = [(ring[d], ring[(d + 1) % count]) for d in range(count)]
+        kv_got = [kv]
+        for _ in range(others):
+            kv_got.append(lax.ppermute(kv_got[-1], "ctx", ring_pairs))
+        kv_got = kv_got[1:]
     for r in range(1, count):
         for g in range(groups):
             if r == 2:
@@ -578,8 +633,6 @@
                 )(got[g][-1], f_parts[g], b_parts[g], dec[g])
             pairs = [(r - 1, r), (count - r, count - r - 1)]
             got[g].append(lax.ppermute(send[g], "ctx", pairs))
-        moving = lax.ppermute(moving, "ctx", ring_pairs)
-        kv_got.append(moving)
 
     stack = 4 if per_kv % 4 == 0 and count <= 4 else 1
     teacher = None
@@ -595,22 +648,18 @@
                 chosen(per_kv * DH, g),
                 chosen(DH, g),
                 chosen(DH, g),
-                *[whole(rows, 2 * kv_dev * DH)] * others,
+                *[whole(*part.shape) for part in kv_got],
                 *[pl.BlockSpec(memory_space=pl.ANY)] * len(more),
             ],
             out_specs=(chosen(per_kv * DH, g), whole(rows, per_kv * DH)),
             scratch_shapes=[
-                pltpu.VMEM(((count + 1) * stretch, DH), BF16),
-                pltpu.VMEM(((count + 1) * stretch, 2 * DH), BF16),
-                pltpu.VMEM((others * stretch, DH), BF16),
-                pltpu.VMEM((others * stretch, 2 * DH), BF16),
+                pltpu.VMEM((2 * count * stretch, DH), BF16),
+                pltpu.VMEM((2 * count * stretch, 2 * DH), BF16),
+                pltpu.VMEM((stretch, stretch), F32),
                 pltpu.VMEM((stretch, (count + 1) * stretch), F32),
-                pltpu.VMEM((stretch, stretch), F32),
                 pltpu.VMEM((stretch, others * stretch), F32),
-                pltpu.VMEM((2, 2 * stack * stretch, stretch), F32),
-                pltpu.VMEM((2, 2 * stack * stretch, 2 * DH), F32),
             ],
-            input_output_aliases={4 + others: 0} if more else {},
+            input_output_aliases={4 + len(kv_got): 0} if more else {},
             compiler_params=params(24),
             cost_estimate=cost(
                 4 * (2 * count + 1) * stretch * stretch * per_kv * DH, 8 * rows * per_kv * DH

time: 69 us -> 67.6 us (0.980)
  Pallas kernels: 20.7 us -> 18.2 us
    ppermute x6, waiting for transfers between devices: 5.78 us -> 2.07 us  [body(): got[g].append(lax.ppermute(send[g], 'ctx', pairs))]
    ppermute x6, starting transfers between devices: 10.2 us -> 13.4 us  [body(): got[g].append(lax.ppermute(send[g], 'ctx', pairs))]
    ppermute x3 -> x4, waiting for transfers between devices: 11.7 us -> 14.9 us  [the longest x1 10.8 us: body(): far = lax.ppermute(both, 'ctx', [(1, 0), (2, 3)])]
    pallas_call x2, Pallas kernels: 9.81 us -> 7.24 us  [body(): pl.pallas_call(functools.partial(attention_kernel, count, per_kv, stack,...]
    ppermute x3 -> x4, starting transfers between devices: 7.51 us -> 5.81 us  [the longest x1 3.17 us: body(): near = lax.ppermute(kv, 'ctx', [(0, 1), (1, 0), (2, 3), (3, 2)])]
    ppermute x4, starting transfers between devices: 6.62 us -> 5.4 us  [exchange(): return lax.ppermute(part, axes, [(d, d ^ shift) for d in range(size)])]
    ppermute x4, waiting for transfers between devices: 3.48 us -> 4.57 us  [exchange(): return lax.ppermute(part, axes, [(d, d ^ shift) for d in range(size)])]
  transfers between devices with their start and end apart: 13 -> 14, of which waited for: 8 -> 6; matrix products, arithmetic and copies ran while one was open for 0% -> 0% of each run, Pallas kernels for 20% -> 17%
where the time goes in v4:
time: 67.6 us; the launch traced here: 67.2 us
  starting transfers between devices  24.6 us (36%)
  waiting for transfers between devices  21.6 us (32%)
  Pallas kernels  18.2 us (27%)
  local copies, waits for them, and re-layouts  1.91 us (3%)
  between operations  0.93 us (1%)
    ppermute x6, starting transfers between devices, body(): got[g].append(lax.ppermute(send[g], 'ctx', pairs))  13.4 us
    ppermute x1, waiting for transfers between devices, body(): far = lax.ppermute(both, 'ctx', [(1, 0), (2, 3)])  10.8 us
    pallas_call x2, Pallas kernels, body(): pl.pallas_call(functools.partial(attention_kernel, count, per_kv, stack,...  7.24 us
    ppermute x4, starting transfers between devices, exchange(): return lax.ppermute(part, axes, [(d, d ^ shift) for d in range(size)])  5.4 us
    pallas_call x2, Pallas kernels, body(): pl.pallas_call(functools.partial(final_kernel, count, g, groups, loss_sca...  4.85 us
    ppermute x4, waiting for transfers between devices, exchange(): return lax.ppermute(part, axes, [(d, d ^ shift) for d in range(size)])  4.57 us
    ppermute x1, waiting for transfers between devices, body(): near = lax.ppermute(kv, 'ctx', [(0, 1), (1, 0), (2, 3), (3, 2)])  4.09 us
    pallas_call x1, Pallas kernels, body(): pl.pallas_call(functools.partial(opening_kernel, count, groups), out_shap...  3.62 us
  transfers between devices with their start and end apart: 14, of which 6 were waited for; matrix products, arithmetic and copies ran while one was open for 0% of the time, Pallas kernels for 17%

profile of v4, /device:TPU:0, one launch (start us, length us, event | category | flops | bytes accessed | tf_op | source)
XLA Modules:
  0.0 67.2 jit_solution(7734427619293373228)
XLA Ops:
  0.6 0.0 copy-start
  0.6 0.0 copy-start.3
  0.7 0.0 copy-start.4
  0.7 3.6 %opening.1 = (bf16[256,512]{1,0:T(8,128)(2,1)S(1)}, f32[32,256]{1,0:T(8,128)S(1)}, bf16[256,1024]{1,0:T(8,128)(2,1)S(1)}, bf16[256,1024]{1,0:T(8,128)(2,1)S(1)},...) custom-call(s32[1,1024]{1,0:T(1,128)} %docs_ref.9, ...), custom_call_target="tpu_custom_call" | custom-call | flops 268435456 | bytes 4194304 | tf_op jit(solution)/shard_map/opening/pallas_call | solution.py:536
  4.3 3.2 %collective-permute-start = (bf16[256,512]{1,0:T(8,128)(2,1)S(1)}, bf16[256,512]{1,0:T(8,128)(2,1)S(1)}, u32[]{:S(2)}, u32[]{:S(2)}) collective-permute-start(bf16[256,512]{1,0:T(8,128)(2,1)S(1)} %get-tuple-element.40), channel_id=1, source_target_pairs={{0,4},{4,0},{8,12},{12,8},{1,5},{5,1},{9,13},{13,9},{2,6},{6,2},{1... | collective-permute-start | bytes 786440 | tf_op jit(solution)/shard_map/ppermute | solution.py:599
  7.5 1.9 %collective-permute-start.7 = (bf16[144,1024]{1,0:T(8,128)(2,1)S(1)}, bf16[144,1024]{1,0:T(8,128)(2,1)S(1)}, u32[]{:S(2)}, u32[]{:S(2)}) collective-permute-start(bf16[144,1024]{1,0:T(8,128)(2,1)S(1)} %get-tuple-element.57), channel_id=1, source_target_pairs={{0,4},{12,8},{1,5},{13,9},{2,6},{14,10},{3,7},{15,11},{16,20},{28,... | collective-permute-start | bytes 884744 | tf_op jit(solution)/shard_map/ppermute | solution.py:635
  9.4 0.7 %collective-permute-start.1 = (bf16[256,512]{1,0:T(8,128)(2,1)S(1)}, bf16[256,512]{1,0:T(8,128)(2,1)S(1)}, u32[]{:S(2)}, u32[]{:S(2)}) collective-permute-start(bf16[256,512]{1,0:T(8,128)(2,1)S(1)} %get-tuple-element.40), channel_id=1, source_target_pairs={{4,8},{8,4},{5,9},{9,5},{6,10},{10,6},{7,11},{11,7},{20,24},{24,20... | collective-permute-start | bytes 786440 | tf_op jit(solution)/shard_map/ppermute | solution.py:600
  10.1 4.1 %collective-permute-done.refs_0_ = bf16[256,512]{1,0:T(8,128)(2,1)S(1)} collective-permute-done((bf16[256,512]{1,0:T(8,128)(2,1)S(1)}, bf16[256,512]{1,0:T(8,128)(2,1)S(1)}, u32[]{:S(2)}, u32[]{:S(2)}) %collective-permute-start) | collective-permute-done | bytes 262176 | tf_op jit(solution)/shard_map/ppermute | solution.py:599
  14.2 0.7 collective-permute-start.2
  14.9 7.2 %collective-permute-start.4 = (bf16[144,1024]{1,0:T(8,128)(2,1)S(1)}, bf16[144,1024]{1,0:T(8,128)(2,1)S(1)}, u32[]{:S(2)}, u32[]{:S(2)}) collective-permute-start(bf16[144,1024]{1,0:T(8,128)(2,1)S(1)} %get-tuple-element.43), channel_id=1, source_target_pairs={{0,4},{12,8},{1,5},{13,9},{2,6},{14,10},{3,7},{15,11},{16,20},{28,... | collective-permute-start | bytes 884744 | tf_op jit(solution)/shard_map/ppermute | solution.py:635
  22.1 0.0 copy-start.7
  22.1 0.0 copy-start.9
  22.1 0.6 copy-done.7
  22.8 1.2 %copy-done.1 = bf16[1,256,2048]{2,1,0:T(8,128)(2,1)S(1)} copy-done((bf16[1,256,2048]{2,1,0:T(8,128)(2,1)S(1)}, bf16[1,256,2048]{2,1,0:T(8,128)(2,1)}, u32[]{:S(2)}) %copy-start.1) | copy-done | bytes 1048600
  24.0 0.9 %local.3 = (f32[256,1024]{1,0:T(8,128)S(1)}, f32[256,1024]{1,0:T(8,128)S(1)}, f32[256,1024]{1,0:T(8,128)S(1)}) custom-call(s32[1,1024]{1,0:T(1,128)S(1)} %copy-done.7, bf16[256,2048]{1,0:T(8,128)(2,1)S(1)} %bitcast.19, bf16[256,2048]{1,0:T(8,128)(2,1)S(1)} %bitcast.21, bf16[256,256]{1,0:T(8,128)(2,1)S(1)} %bitcast.30, bf16[256,256]{1,0:T(8,128)(2,1)S(1)} %bitcast.25, ...), custom_call_target="tpu_custom_call" | custom-call | flops 67108864 | bytes 4194304 | tf_op jit(solution)/shard_map/local/pallas_call | solution.py:574
  24.9 0.0 collective-permute-done.7.got_ref.refs_0_
  24.9 0.7 %collective-permute-start.8 = (bf16[144,1024]{1,0:T(8,128)(2,1)S(1)}, bf16[144,1024]{1,0:T(8,128)(2,1)S(1)}, u32[]{:S(2)}, u32[]{:S(2)}) collective-permute-start(bf16[144,1024]{1,0:T(8,128)(2,1)S(1)} %chain.6), channel_id=1, source_target_pairs={{4,8},{8,4},{5,9},{9,5},{6,10},{10,6},{7,11},{11,7},{20,24},{24,20... | collective-permute-start | bytes 884744 | tf_op jit(solution)/shard_map/ppermute | solution.py:635
  25.6 0.0 collective-permute-done.1.a_ref.refs_1_
  25.6 0.0 collective-permute-done.2.b_ref.refs_2_
  25.7 1.3 %collective-permute-start.3 = (bf16[512,512]{1,0:T(8,128)(2,1)S(1)}, bf16[512,512]{1,0:T(8,128)(2,1)S(1)}, u32[]{:S(2)}, u32[]{:S(2)}) collective-permute-start(bf16[512,512]{1,0:T(8,128)(2,1)S(1)} %pair.1), channel_id=1, source_target_pairs={{4,0},{8,12},{5,1},{9,13},{6,2},{10,14},{7,3},{11,15},{20,16},{24,... | collective-permute-start | bytes 1572872 | tf_op jit(solution)/shard_map/ppermute | solution.py:611
  27.0 0.9 %local.2 = (f32[256,1024]{1,0:T(8,128)S(1)}, f32[256,1024]{1,0:T(8,128)S(1)}, f32[256,1024]{1,0:T(8,128)S(1)}) custom-call(s32[1,1024]{1,0:T(1,128)S(1)} %copy-done.7, bf16[256,2048]{1,0:T(8,128)(2,1)S(1)} %bitcast.20, bf16[256,2048]{1,0:T(8,128)(2,1)S(1)} %bitcast.22, bf16[256,256]{1,0:T(8,128)(2,1)S(1)} %bitcast.31, bf16[256,256]{1,0:T(8,128)(2,1)S(1)} %bitcast.26, ...), custom_call_target="tpu_custom_call" | custom-call | flops 67108864 | bytes 4194304 | tf_op jit(solution)/shard_map/local/pallas_call | solution.py:574
  27.9 0.0 collective-permute-done.4.got_ref.refs_0_
  27.9 0.0 copy-start.2
  28.0 0.8 %collective-permute-start.5 = (bf16[144,1024]{1,0:T(8,128)(2,1)S(1)}, bf16[144,1024]{1,0:T(8,128)(2,1)S(1)}, u32[]{:S(2)}, u32[]{:S(2)}) collective-permute-start(bf16[144,1024]{1,0:T(8,128)(2,1)S(1)} %chain.4), channel_id=1, source_target_pairs={{4,8},{8,4},{5,9},{9,5},{6,10},{10,6},{7,11},{11,7},{20,24},{24,20... | collective-permute-start | bytes 884744 | tf_op jit(solution)/shard_map/ppermute | solution.py:635
  28.8 0.0 collective-permute-done.8.got_ref.refs_1_
  28.8 0.0 copy-start.5
  28.8 0.0 copy-start.6
  28.8 1.4 %collective-permute-start.9 = (bf16[144,1024]{1,0:T(8,128)(2,1)S(1)}, bf16[144,1024]{1,0:T(8,128)(2,1)S(1)}, u32[]{:S(2)}, u32[]{:S(2)}) collective-permute-start(bf16[144,1024]{1,0:T(8,128)(2,1)S(1)} %chain.7), channel_id=1, source_target_pairs={{8,12},{4,0},{9,13},{5,1},{10,14},{6,2},{11,15},{7,3},{24,28},{20,... | collective-permute-start | bytes 884744 | tf_op jit(solution)/shard_map/ppermute | solution.py:635
  30.3 0.0 collective-permute-done.5.got_ref.refs_1_
  30.3 1.3 %collective-permute-start.6 = (bf16[144,1024]{1,0:T(8,128)(2,1)S(1)}, bf16[144,1024]{1,0:T(8,128)(2,1)S(1)}, u32[]{:S(2)}, u32[]{:S(2)}) collective-permute-start(bf16[144,1024]{1,0:T(8,128)(2,1)S(1)} %chain.5), channel_id=1, source_target_pairs={{8,12},{4,0},{9,13},{5,1},{10,14},{6,2},{11,15},{7,3},{24,28},{20,... | collective-permute-start | bytes 884744 | tf_op jit(solution)/shard_map/ppermute | solution.py:635
  31.6 10.8 %collective-permute-done.3.refs_3_ = bf16[512,512]{1,0:T(8,128)(2,1)S(1)} collective-permute-done((bf16[512,512]{1,0:T(8,128)(2,1)S(1)}, bf16[512,512]{1,0:T(8,128)(2,1)S(1)}, u32[]{:S(2)}, u32[]{:S(2)}) %collective-permute-start.3) | collective-permute-done | bytes 524320 | tf_op jit(solution)/shard_map/ppermute | solution.py:611
  42.4 0.0 copy-done.6
  42.4 0.0 copy-start.8
  42.5 3.6 %attention.2 = (bf16[256,2048]{1,0:T(8,128)(2,1)}, bf16[256,1024]{1,0:T(8,128)(2,1)S(1)}) custom-call(s32[1,1024]{1,0:T(1,128)S(1)} %copy-done.7, bf16[256,2048]{1,0:T(8,128)(2,1)S(1)} %bitcast.23, bf16[256,256]{1,0:T(8,128)(2,1)S(1)} %bitcast.33, bf16[256,256]{1,0:T(8,128)(2,1)S(1)} %bitcast.36, bf16[256,512]{1,0:T(8,128)(2,1)S(1)} %collective-permute-done.refs_0_, ...), custom_call_target="tpu_custom_call" | custom-call | flops 603979776 | bytes 2097152 | tf_op jit(solution)/shard_map/attention/pallas_call | solution.py:642
  46.1 2.1 %collective-permute-done.9.refs_2_ = bf16[144,1024]{1,0:T(8,128)(2,1)S(1)} collective-permute-done((bf16[144,1024]{1,0:T(8,128)(2,1)S(1)}, bf16[144,1024]{1,0:T(8,128)(2,1)S(1)}, u32[]{:S(2)}, u32[]{:S(2)}) %collective-permute-start.9) | collective-permute-done | bytes 294944 | tf_op jit(solution)/shard_map/ppermute | solution.py:635
  48.1 2.4 %final.2 = (bf16[256,2048]{1,0:T(8,128)(2,1)}, f32[3,1024]{1,0:T(4,128)S(1)}) custom-call(f32[256,1024]{1,0:T(8,128)S(1)} %get-tuple-element.62.pre_ref, f32[256,1024]{1,0:T(8,128)S(1)} %get-tuple-element.63.reach_ref, f32[256,1024]{1,0:T(8,128)S(1)} %get-tuple-element.64.sx_ref, bf16[256,256]{1,0:T(8,128)(2,1)S(1)} %bitcast.27, ...), custom_call_target="tpu_custom_call" | custom-call | flops 67108864 | bytes 5242880 | tf_op jit(solution)/shard_map/final/pallas_call | solution.py:674
  50.6 3.6 %attention.3 = (bf16[256,2048]{1,0:T(8,128)(2,1)}, bf16[256,1024]{1,0:T(8,128)(2,1)S(1)}) custom-call(s32[1,1024]{1,0:T(1,128)S(1)} %copy-done.7, bf16[256,2048]{1,0:T(8,128)(2,1)S(1)} %bitcast.24, bf16[256,256]{1,0:T(8,128)(2,1)S(1)} %bitcast.34, bf16[256,256]{1,0:T(8,128)(2,1)S(1)} %bitcast.37, ...), custom_call_target="tpu_custom_call", output_to_operand_aliasing={{0}: (8, {})} | custom-call | flops 603979776 | bytes 2097152 | tf_op jit(solution)/shard_map/attention/pallas_call | solution.py:642
  54.2 0.0 collective-permute-done.6.refs_2_
  54.2 2.4 %final.3 = (bf16[256,2048]{1,0:T(8,128)(2,1)}, f32[3,1024]{1,0:T(4,128)S(1)}) custom-call(f32[256,1024]{1,0:T(8,128)S(1)} %get-tuple-element.49.pre_ref, f32[256,1024]{1,0:T(8,128)S(1)} %get-tuple-element.50.reach_ref, f32[256,1024]{1,0:T(8,128)S(1)} %get-tuple-element.51.sx_ref, bf16[256,256]{1,0:T(8,128)(2,1)S(1)} %bitcast.28, ...), custom_call_target="tpu_custom_call", output_to_operand_aliasing={{0}: (12, {})} | custom-call | flops 67108864 | bytes 5242880 | tf_op jit(solution)/shard_map/final/pallas_call | solution.py:674
  56.6 0.5 collective-permute-start.12
  57.1 1.0 %collective-permute-start.11 = (f32[3,1024]{1,0:T(4,128)S(1)}, f32[3,1024]{1,0:T(4,128)S(1)}, u32[]{:S(2)}, u32[]{:S(2)}) collective-permute-start(f32[3,1024]{1,0:T(4,128)S(1)} %get-tuple-element.73), channel_id=1, source_target_pairs={{0,16},{4,20},{8,24},{12,28},{16,0},{20,4},{24,8},{28,12},{1,17},{... | collective-permute-start | bytes 36872 | tf_op jit(solution)/shard_map/ppermute | solution.py:496
  58.1 2.0 %collective-permute-start.10 = (f32[3,1024]{1,0:T(4,128)S(1)}, f32[3,1024]{1,0:T(4,128)S(1)}, u32[]{:S(2)}, u32[]{:S(2)}) collective-permute-start(f32[3,1024]{1,0:T(4,128)S(1)} %get-tuple-element.73), channel_id=1, source_target_pairs={{0,4},{4,0},{8,12},{12,8},{16,20},{20,16},{24,28},{28,24},{1,5},{5... | collective-permute-start | bytes 36872 | tf_op jit(solution)/shard_map/ppermute | solution.py:496
  60.1 1.1 %collective-permute-done.12 = f32[3,1024]{1,0:T(4,128)S(1)} collective-permute-done((f32[3,1024]{1,0:T(4,128)S(1)}, f32[3,1024]{1,0:T(4,128)S(1)}, u32[]{:S(2)}, u32[]{:S(2)}) %collective-permute-start.12) | collective-permute-done | bytes 12320 | tf_op jit(solution)/shard_map/ppermute | solution.py:496
  61.2 0.0 collective-permute-done.11
  61.2 0.6 collective-permute-done.10
  61.9 1.9 %collective-permute-start.13 = (f32[3,1024]{1,0:T(4,128)S(1)}, f32[3,1024]{1,0:T(4,128)S(1)}, u32[]{:S(2)}, u32[]{:S(2)}) collective-permute-start(f32[3,1024]{1,0:T(4,128)S(1)} %add_add_fusion.a_ref), channel_id=1, source_target_pairs={{0,8},{4,12},{8,0},{12,4},{16,24},{20,28},{24,16},{28,20},{1,9},{5... | collective-permute-start | bytes 36872 | tf_op jit(solution)/shard_map/ppermute | solution.py:496
  63.8 2.8 %collective-permute-done.13.b_ref = f32[3,1024]{1,0:T(4,128)S(1)} collective-permute-done((f32[3,1024]{1,0:T(4,128)S(1)}, f32[3,1024]{1,0:T(4,128)S(1)}, u32[]{:S(2)}, u32[]{:S(2)}) %collective-permute-start.13) | collective-permute-done | bytes 12320 | tf_op jit(solution)/shard_map/ppermute | solution.py:496
  66.6 0.6 closing.1
  (14 shorter events, 0.1 us)
Async XLA Ops:
  0.6 21.5 %copy-start = (bf16[1,256,2048]{2,1,0:T(8,128)(2,1)S(1)}, bf16[1,256,2048]{2,1,0:T(8,128)(2,1)}, u32[]{:S(2)}) copy-start(bf16[1,256,2048]{2,1,0:T(8,128)(2,1)} %param.17) | copy-start | bytes 3145732
  0.6 21.5 %copy-start.3 = (bf16[1,256,256]{2,1,0:T(8,128)(2,1)S(1)}, bf16[1,256,256]{2,1,0:T(8,128)(2,1)}, u32[]{:S(2)}) copy-start(bf16[1,256,256]{2,1,0:T(8,128)(2,1)} %param.20) | copy-start | bytes 393220
  0.7 21.5 %copy-start.4 = (bf16[1,256,256]{2,1,0:T(8,128)(2,1)S(1)}, bf16[1,256,256]{2,1,0:T(8,128)(2,1)}, u32[]{:S(2)}) copy-start(bf16[1,256,256]{2,1,0:T(8,128)(2,1)} %param.19) | copy-start | bytes 393220
  4.3 9.9 %collective-permute-start = (bf16[256,512]{1,0:T(8,128)(2,1)S(1)}, bf16[256,512]{1,0:T(8,128)(2,1)S(1)}, u32[]{:S(2)}, u32[]{:S(2)}) collective-permute-start(bf16[256,512]{1,0:T(8,128)(2,1)S(1)} %get-tuple-element.40), channel_id=1, source_target_pairs={{0,4},{4,0},{8,12},{12,8},{1,5},{5,1},{9,13},{13,9},{2,6},{6,2},{1... | collective-permute-start | bytes 786440 | tf_op jit(solution)/shard_map/ppermute | solution.py:599
  7.5 17.4 %collective-permute-start.7 = (bf16[144,1024]{1,0:T(8,128)(2,1)S(1)}, bf16[144,1024]{1,0:T(8,128)(2,1)S(1)}, u32[]{:S(2)}, u32[]{:S(2)}) collective-permute-start(bf16[144,1024]{1,0:T(8,128)(2,1)S(1)} %get-tuple-element.57), channel_id=1, source_target_pairs={{0,4},{12,8},{1,5},{13,9},{2,6},{14,10},{3,7},{15,11},{16,20},{28,... | collective-permute-start | bytes 884744 | tf_op jit(solution)/shard_map/ppermute | solution.py:635
  9.4 16.2 %collective-permute-start.1 = (bf16[256,512]{1,0:T(8,128)(2,1)S(1)}, bf16[256,512]{1,0:T(8,128)(2,1)S(1)}, u32[]{:S(2)}, u32[]{:S(2)}) collective-permute-start(bf16[256,512]{1,0:T(8,128)(2,1)S(1)} %get-tuple-element.40), channel_id=1, source_target_pairs={{4,8},{8,4},{5,9},{9,5},{6,10},{10,6},{7,11},{11,7},{20,24},{24,20... | collective-permute-start | bytes 786440 | tf_op jit(solution)/shard_map/ppermute | solution.py:600
  14.2 11.4 %collective-permute-start.2 = (bf16[256,512]{1,0:T(8,128)(2,1)S(1)}, bf16[256,512]{1,0:T(8,128)(2,1)S(1)}, u32[]{:S(2)}, u32[]{:S(2)}) collective-permute-start(bf16[256,512]{1,0:T(8,128)(2,1)S(1)} %collective-permute-done.refs_0_), channel_id=1, source_target_pairs={{4,8},{8,4},{5,9},{9,5},{6,10},{10,6},{7,11},{11,7},{20,24},{24,20... | collective-permute-start | bytes 786440 | tf_op jit(solution)/shard_map/ppermute | solution.py:601
  14.9 13.1 %collective-permute-start.4 = (bf16[144,1024]{1,0:T(8,128)(2,1)S(1)}, bf16[144,1024]{1,0:T(8,128)(2,1)S(1)}, u32[]{:S(2)}, u32[]{:S(2)}) collective-permute-start(bf16[144,1024]{1,0:T(8,128)(2,1)S(1)} %get-tuple-element.43), channel_id=1, source_target_pairs={{0,4},{12,8},{1,5},{13,9},{2,6},{14,10},{3,7},{15,11},{16,20},{28,... | collective-permute-start | bytes 884744 | tf_op jit(solution)/shard_map/ppermute | solution.py:635
  22.1 0.7 %copy-start.7 = (s32[1,1024]{1,0:T(1,128)S(1)}, s32[1,1024]{1,0:T(1,128)}, u32[]{:S(2)}) copy-start(s32[1,1024]{1,0:T(1,128)} %docs_ref.9) | copy-start | bytes 12292
  22.1 0.7 %copy-start.9 = (f32[32]{0:T(128)S(1)}, f32[32]{0:T(128)}, u32[]{:S(2)}) copy-start(f32[32]{0:T(128)} %param.24) | copy-start | bytes 388
  22.8 1.2 %copy-start.1 = (bf16[1,256,2048]{2,1,0:T(8,128)(2,1)S(1)}, bf16[1,256,2048]{2,1,0:T(8,128)(2,1)}, u32[]{:S(2)}) copy-start(bf16[1,256,2048]{2,1,0:T(8,128)(2,1)} %param.18) | copy-start | bytes 3145732
  24.9 3.9 %collective-permute-start.8 = (bf16[144,1024]{1,0:T(8,128)(2,1)S(1)}, bf16[144,1024]{1,0:T(8,128)(2,1)S(1)}, u32[]{:S(2)}, u32[]{:S(2)}) collective-permute-start(bf16[144,1024]{1,0:T(8,128)(2,1)S(1)} %chain.6), channel_id=1, source_target_pairs={{4,8},{8,4},{5,9},{9,5},{6,10},{10,6},{7,11},{11,7},{20,24},{24,20... | collective-permute-start | bytes 884744 | tf_op jit(solution)/shard_map/ppermute | solution.py:635
  25.7 16.8 %collective-permute-start.3 = (bf16[512,512]{1,0:T(8,128)(2,1)S(1)}, bf16[512,512]{1,0:T(8,128)(2,1)S(1)}, u32[]{:S(2)}, u32[]{:S(2)}) collective-permute-start(bf16[512,512]{1,0:T(8,128)(2,1)S(1)} %pair.1), channel_id=1, source_target_pairs={{4,0},{8,12},{5,1},{9,13},{6,2},{10,14},{7,3},{11,15},{20,16},{24,... | collective-permute-start | bytes 1572872 | tf_op jit(solution)/shard_map/ppermute | solution.py:611
  27.9 14.5 %copy-start.2 = (bf16[1,256,2048]{2,1,0:T(8,128)(2,1)S(1)}, bf16[1,256,2048]{2,1,0:T(8,128)(2,1)}, u32[]{:S(2)}) copy-start(bf16[1,256,2048]{2,1,0:T(8,128)(2,1)} %param.13) | copy-start | bytes 3145732
  28.0 2.3 %collective-permute-start.5 = (bf16[144,1024]{1,0:T(8,128)(2,1)S(1)}, bf16[144,1024]{1,0:T(8,128)(2,1)S(1)}, u32[]{:S(2)}, u32[]{:S(2)}) collective-permute-start(bf16[144,1024]{1,0:T(8,128)(2,1)S(1)} %chain.4), channel_id=1, source_target_pairs={{4,8},{8,4},{5,9},{9,5},{6,10},{10,6},{7,11},{11,7},{20,24},{24,20... | collective-permute-start | bytes 884744 | tf_op jit(solution)/shard_map/ppermute | solution.py:635
  28.8 13.6 %copy-start.5 = (bf16[1,256,256]{2,1,0:T(8,128)(2,1)S(1)}, bf16[1,256,256]{2,1,0:T(8,128)(2,1)}, u32[]{:S(2)}) copy-start(bf16[1,256,256]{2,1,0:T(8,128)(2,1)} %param.14) | copy-start | bytes 393220
  28.8 13.6 %copy-start.6 = (bf16[1,256,256]{2,1,0:T(8,128)(2,1)S(1)}, bf16[1,256,256]{2,1,0:T(8,128)(2,1)}, u32[]{:S(2)}) copy-start(bf16[1,256,256]{2,1,0:T(8,128)(2,1)} %param.15) | copy-start | bytes 393220
  28.8 19.3 %collective-permute-start.9 = (bf16[144,1024]{1,0:T(8,128)(2,1)S(1)}, bf16[144,1024]{1,0:T(8,128)(2,1)S(1)}, u32[]{:S(2)}, u32[]{:S(2)}) collective-permute-start(bf16[144,1024]{1,0:T(8,128)(2,1)S(1)} %chain.7), channel_id=1, source_target_pairs={{8,12},{4,0},{9,13},{5,1},{10,14},{6,2},{11,15},{7,3},{24,28},{20,... | collective-permute-start | bytes 884744 | tf_op jit(solution)/shard_map/ppermute | solution.py:635
  30.3 23.9 %collective-permute-start.6 = (bf16[144,1024]{1,0:T(8,128)(2,1)S(1)}, bf16[144,1024]{1,0:T(8,128)(2,1)S(1)}, u32[]{:S(2)}, u32[]{:S(2)}) collective-permute-start(bf16[144,1024]{1,0:T(8,128)(2,1)S(1)} %chain.5), channel_id=1, source_target_pairs={{8,12},{4,0},{9,13},{5,1},{10,14},{6,2},{11,15},{7,3},{24,28},{20,... | collective-permute-start | bytes 884744 | tf_op jit(solution)/shard_map/ppermute | solution.py:635
  42.4 5.7 %copy-start.8 = (f32[2048]{0:T(1024)S(1)}, f32[2048]{0:T(1024)}, u32[]{:S(2)}) copy-start(f32[2048]{0:T(1024)} %param.25) | copy-start | bytes 24580
  56.6 4.6 %collective-permute-start.12 = (f32[3,1024]{1,0:T(4,128)S(1)}, f32[3,1024]{1,0:T(4,128)S(1)}, u32[]{:S(2)}, u32[]{:S(2)}) collective-permute-start(f32[3,1024]{1,0:T(4,128)S(1)} %get-tuple-element.73), channel_id=1, source_target_pairs={{0,20},{4,16},{8,28},{12,24},{16,4},{20,0},{24,12},{28,8},{1,21},{... | collective-permute-start | bytes 36872 | tf_op jit(solution)/shard_map/ppermute | solution.py:496
  57.1 4.1 %collective-permute-start.11 = (f32[3,1024]{1,0:T(4,128)S(1)}, f32[3,1024]{1,0:T(4,128)S(1)}, u32[]{:S(2)}, u32[]{:S(2)}) collective-permute-start(f32[3,1024]{1,0:T(4,128)S(1)} %get-tuple-element.73), channel_id=1, source_target_pairs={{0,16},{4,20},{8,24},{12,28},{16,0},{20,4},{24,8},{28,12},{1,17},{... | collective-permute-start | bytes 36872 | tf_op jit(solution)/shard_map/ppermute | solution.py:496
  58.1 3.7 %collective-permute-start.10 = (f32[3,1024]{1,0:T(4,128)S(1)}, f32[3,1024]{1,0:T(4,128)S(1)}, u32[]{:S(2)}, u32[]{:S(2)}) collective-permute-start(f32[3,1024]{1,0:T(4,128)S(1)} %get-tuple-element.73), channel_id=1, source_target_pairs={{0,4},{4,0},{8,12},{12,8},{16,20},{20,16},{24,28},{28,24},{1,5},{5... | collective-permute-start | bytes 36872 | tf_op jit(solution)/shard_map/ppermute | solution.py:496
  61.9 4.7 %collective-permute-start.13 = (f32[3,1024]{1,0:T(4,128)S(1)}, f32[3,1024]{1,0:T(4,128)S(1)}, u32[]{:S(2)}, u32[]{:S(2)}) collective-permute-start(f32[3,1024]{1,0:T(4,128)S(1)} %add_add_fusion.a_ref), channel_id=1, source_target_pairs={{0,8},{4,12},{8,0},{12,4},{16,24},{20,28},{24,16},{28,20},{1,9},{5... | collective-permute-start | bytes 36872 | tf_op jit(solution)/shard_map/ppermute | solution.py:496

commit v5 on v4

--- a/solution.py
+++ b/solution.py
@@ -241,34 +241,28 @@
             reach_ref[at, :] = reached[here] * fade
 
 
-def pair_kernel(a_ref, b_ref, out_ref):
-    rows = a_ref.shape[0]
-    out_ref[:rows, :] = a_ref[...]
-    out_ref[rows:, :] = b_ref[...]
-
-
-def arrivals(index, count, rows, refs):
+def arrivals(index, count, refs):
     if count != 4:
-        return [(ring_source(index, count, r + 1), [(None, refs[r], 0)]) for r in range(count - 1)]
-    near, own_of_middle, next_of_middle, far = refs
+        return [(ring_source(index, count, r + 1), [(None, refs[r])]) for r in range(count - 1)]
+    near, own_of_middle, next_of_middle, far, farther = refs
     middle = (index == 1) | (index == 2)
     low = index < 2
     return [
-        (index ^ 1, [(None, near, 0)]),
+        (index ^ 1, [(None, near)]),
         (
             jnp.where(low, 2, 1),
-            [(middle, own_of_middle, 0), (jnp.logical_not(middle), far, 0)],
+            [(middle, own_of_middle), (jnp.logical_not(middle), far)],
         ),
         (
             jnp.where(low, 3, 0),
-            [(middle, next_of_middle, 0), (jnp.logical_not(middle), far, rows)],
+            [(middle, next_of_middle), (jnp.logical_not(middle), farther)],
         ),
     ]
 
 
 def attention_kernel(count, per, stack, g, docs_ref, q_ref, k_ref, v_ref, *refs):
     others = count - 1
-    sent = 4 if count == 4 else others
+    sent = 5 if count == 4 else others
     out_ref, copy_ref, kt, vt, bias_f, bias_b, bias_a = refs[-7:]
     rows = q_ref.shape[0]
     stretch = rows // 2
@@ -295,13 +289,13 @@
     kt[tile(count), :] = k_ref[stretch:, :]
     vt[tile(count), :DH] = v_ref[stretch:, :]
     lower = []
-    for r, (source, places) in enumerate(arrivals(index, count, rows, refs[:sent])):
+    for r, (source, places) in enumerate(arrivals(index, count, refs[:sent])):
         lower.append(source < index)
-        for condition, ref, first in places:
-
-            def fetch(ref=ref, first=first, r=r):
-                front = slice(first, first + stretch)
-                start = jnp.where(lower[r], first, first + stretch)
+        for condition, ref in places:
+
+            def fetch(ref=ref, r=r):
+                front = slice(0, stretch)
+                start = jnp.where(lower[r], 0, stretch)
                 own = pl.ds(pl.multiple_of(start, stretch), stretch)
                 kt[tile(1 + r), :] = ref[own, k_cols]
                 vt[tile(1 + r), :DH] = ref[own, v_cols]
@@ -598,18 +592,12 @@
         across = [(1, 2), (2, 1)]
         near = lax.ppermute(kv, "ctx", [(0, 1), (1, 0), (2, 3), (3, 2)])
         middle = lax.ppermute(kv, "ctx", across)
+        near, local = lax.optimization_barrier((near, local))
         beyond = lax.ppermute(near, "ctx", across)
-        both = pl.pallas_call(
-            pair_kernel,
-            out_shape=struct((2 * rows, kv.shape[1]), BF16),
-            in_specs=[VMEM] * 2,
-            out_specs=VMEM,
-            compiler_params=params(4),
-            cost_estimate=cost(0, 4 * kv.size),
-            name="pair",
-        )(middle, beyond)
-        far = lax.ppermute(both, "ctx", [(1, 0), (2, 3)])
-        kv_got = [near, middle, beyond, far]
+        outward = [(1, 0), (2, 3)]
+        far = lax.ppermute(middle, "ctx", outward)
+        farther = lax.ppermute(beyond, "ctx", outward)
+        kv_got = [near, middle, beyond, far, farther]
     else:
         ring = ring_order(count)
         ring_pairs = [(ring[d], ring[(d + 1) % count]) for d in range(count)]
@@ -617,23 +605,6 @@
         for _ in range(others):
             kv_got.append(lax.ppermute(kv_got[-1], "ctx", ring_pairs))
         kv_got = kv_got[1:]
-    for r in range(1, count):
-        for g in range(groups):
-            if r == 2:
-                got[g][0], *local[g] = lax.optimization_barrier((got[g][0], *local[g]))
-            if r > 1:
-                send[g] = pl.pallas_call(
-                    functools.partial(chain_kernel, count, r - 1),
-                    out_shape=payload,
-                    in_specs=[VMEM] * 4,
-                    out_specs=VMEM,
-                    compiler_params=params(4),
-                    cost_estimate=cost(8 * N * width, 8 * N * width),
-                    name="chain",
-                )(got[g][-1], f_parts[g], b_parts[g], dec[g])
-            pairs = [(r - 1, r), (count - r, count - r - 1)]
-            got[g].append(lax.ppermute(send[g], "ctx", pairs))
-
     stack = 4 if per_kv % 4 == 0 and count <= 4 else 1
     teacher = None
     targets = []
@@ -667,6 +638,23 @@
             name="attention",
         )(doc_ids, queries[0], keys[0], values[0], *kv_got, *more)
         targets.append(target)
+
+    for r in range(1, count):
+        for g in range(groups):
+            if r == 3 and g == groups - 1:
+                got[g][-1], targets[0] = lax.optimization_barrier((got[g][-1], targets[0]))
+            if r > 1:
+                send[g] = pl.pallas_call(
+                    functools.partial(chain_kernel, count, r - 1),
+                    out_shape=payload,
+                    in_specs=[VMEM] * 4,
+                    out_specs=VMEM,
+                    compiler_params=params(4),
+                    cost_estimate=cost(8 * N * width, 8 * N * width),
+                    name="chain",
+                )(got[g][-1], f_parts[g], b_parts[g], dec[g])
+            pairs = [(r - 1, r), (count - r, count - r - 1)]
+            got[g].append(lax.ppermute(send[g], "ctx", pairs))
 
     student = grads = None
     for g in range(groups):

time: 67.6 us -> 66.8 us (0.988)
  starting transfers between devices: 24.6 us -> 23.2 us
  waiting for transfers between devices: 21.6 us -> 22.3 us
    ppermute x1, waiting for transfers between devices: 4.09 us -> 0.01 us  [body(): near = lax.ppermute(kv, 'ctx', [(0, 1), (1, 0), (2, 3), (3, 2)])]
    ppermute x4, waiting for transfers between devices: 4.57 us -> 6.86 us  [exchange(): return lax.ppermute(part, axes, [(d, d ^ shift) for d in range(size)])]
    ppermute x6, starting transfers between devices: 13.4 us -> 11.6 us  [body(): got[g].append(lax.ppermute(send[g], 'ctx', pairs))]
    ppermute x6, waiting for transfers between devices: 2.07 us -> 3.45 us  [body(): got[g].append(lax.ppermute(send[g], 'ctx', pairs))]
    ppermute x1 -> x2, starting transfers between devices: 1.29 us -> 2.58 us  [the longest x1 1.29 us: body(): far = lax.ppermute(middle, 'ctx', outward)]
    ppermute x1 -> x2, waiting for transfers between devices: 10.8 us -> 12 us  [the longest x1 6.89 us: body(): far = lax.ppermute(middle, 'ctx', outward)]
    ppermute x4, starting transfers between devices: 5.4 us -> 4.46 us  [exchange(): return lax.ppermute(part, axes, [(d, d ^ shift) for d in range(size)])]
  transfers between devices with their start and end apart: 14 -> 15, of which waited for: 6 -> 9; matrix products, arithmetic and copies ran while one was open for 0% -> 0% of each run, Pallas kernels for 17% -> 17%
where the time goes in v5:
time: 66.8 us; the launch traced here: 66.4 us
  starting transfers between devices  23.2 us (35%)
  waiting for transfers between devices  22.3 us (33%)
  Pallas kernels  18.1 us (27%)
  local copies, waits for them, and re-layouts  1.9 us (3%)
  between operations  0.87 us (1%)
    ppermute x6, starting transfers between devices, body(): got[g].append(lax.ppermute(send[g], 'ctx', pairs))  11.6 us
    pallas_call x2, Pallas kernels, body(): pl.pallas_call(functools.partial(attention_kernel, count, per_kv, stack,...  7.25 us
    ppermute x1, waiting for transfers between devices, body(): far = lax.ppermute(middle, 'ctx', outward)  6.89 us
    ppermute x4, waiting for transfers between devices, exchange(): return lax.ppermute(part, axes, [(d, d ^ shift) for d in range(size)])  6.86 us
    ppermute x1, waiting for transfers between devices, body(): farther = lax.ppermute(beyond, 'ctx', outward)  5.11 us
    pallas_call x2, Pallas kernels, body(): pl.pallas_call(functools.partial(final_kernel, count, g, groups, loss_sca...  4.85 us
    ppermute x4, starting transfers between devices, exchange(): return lax.ppermute(part, axes, [(d, d ^ shift) for d in range(size)])  4.46 us
    pallas_call x1, Pallas kernels, body(): pl.pallas_call(functools.partial(opening_kernel, count, groups), out_shap...  3.62 us
  transfers between devices with their start and end apart: 15, of which 9 were waited for; matrix products, arithmetic and copies ran while one was open for 0% of the time, Pallas kernels for 17%

profile of v5, /device:TPU:0, one launch (start us, length us, event | category | flops | bytes accessed | tf_op | source)
XLA Modules:
  0.0 66.4 jit_solution(7321704821976293984)
XLA Ops:
  0.6 0.0 copy-start
  0.6 0.0 copy-start.3
  0.7 0.0 copy-start.4
  0.7 3.6 %opening.1 = (bf16[256,512]{1,0:T(8,128)(2,1)S(1)}, f32[32,256]{1,0:T(8,128)S(1)}, bf16[256,1024]{1,0:T(8,128)(2,1)S(1)}, bf16[256,1024]{1,0:T(8,128)(2,1)S(1)},...) custom-call(s32[1,1024]{1,0:T(1,128)} %docs_ref.9, ...), custom_call_target="tpu_custom_call" | custom-call | flops 268435456 | bytes 4194304 | tf_op jit(solution)/shard_map/opening/pallas_call | solution.py:530
  4.3 3.2 %collective-permute-start = (bf16[256,512]{1,0:T(8,128)(2,1)S(1)}, bf16[256,512]{1,0:T(8,128)(2,1)S(1)}, u32[]{:S(2)}, u32[]{:S(2)}) collective-permute-start(bf16[256,512]{1,0:T(8,128)(2,1)S(1)} %get-tuple-element.41), channel_id=1, source_target_pairs={{0,4},{4,0},{8,12},{12,8},{1,5},{5,1},{9,13},{13,9},{2,6},{6,2},{1... | collective-permute-start | bytes 786440 | tf_op jit(solution)/shard_map/ppermute | solution.py:593
  7.5 1.9 %collective-permute-start.8 = (bf16[144,1024]{1,0:T(8,128)(2,1)S(1)}, bf16[144,1024]{1,0:T(8,128)(2,1)S(1)}, u32[]{:S(2)}, u32[]{:S(2)}) collective-permute-start(bf16[144,1024]{1,0:T(8,128)(2,1)S(1)} %get-tuple-element.70), channel_id=1, source_target_pairs={{0,4},{12,8},{1,5},{13,9},{2,6},{14,10},{3,7},{15,11},{16,20},{28,... | collective-permute-start | bytes 884744 | tf_op jit(solution)/shard_map/ppermute | solution.py:657
  9.4 0.7 %collective-permute-start.1 = (bf16[256,512]{1,0:T(8,128)(2,1)S(1)}, bf16[256,512]{1,0:T(8,128)(2,1)S(1)}, u32[]{:S(2)}, u32[]{:S(2)}) collective-permute-start(bf16[256,512]{1,0:T(8,128)(2,1)S(1)} %get-tuple-element.41), channel_id=1, source_target_pairs={{4,8},{8,4},{5,9},{9,5},{6,10},{10,6},{7,11},{11,7},{20,24},{24,20... | collective-permute-start | bytes 786440 | tf_op jit(solution)/shard_map/ppermute | solution.py:594
  10.1 5.7 %collective-permute-start.5 = (bf16[144,1024]{1,0:T(8,128)(2,1)S(1)}, bf16[144,1024]{1,0:T(8,128)(2,1)S(1)}, u32[]{:S(2)}, u32[]{:S(2)}) collective-permute-start(bf16[144,1024]{1,0:T(8,128)(2,1)S(1)} %get-tuple-element.60), channel_id=1, source_target_pairs={{0,4},{12,8},{1,5},{13,9},{2,6},{14,10},{3,7},{15,11},{16,20},{28,... | collective-permute-start | bytes 884744 | tf_op jit(solution)/shard_map/ppermute | solution.py:657
  15.8 0.0 copy-start.7
  15.8 0.0 copy-start.9
  15.8 0.0 copy-done
  15.8 0.6 copy-done.7
  16.5 0.0 copy-done.9
  16.5 1.2 %copy-done.1 = bf16[1,256,2048]{2,1,0:T(8,128)(2,1)S(1)} copy-done((bf16[1,256,2048]{2,1,0:T(8,128)(2,1)S(1)}, bf16[1,256,2048]{2,1,0:T(8,128)(2,1)}, u32[]{:S(2)}) %copy-start.1) | copy-done | bytes 1048600
  17.7 0.9 %local.2 = (f32[256,1024]{1,0:T(8,128)S(1)}, f32[256,1024]{1,0:T(8,128)S(1)}, f32[256,1024]{1,0:T(8,128)S(1)}) custom-call(s32[1,1024]{1,0:T(1,128)S(1)} %copy-done.7, bf16[256,2048]{1,0:T(8,128)(2,1)S(1)} %bitcast.19, bf16[256,2048]{1,0:T(8,128)(2,1)S(1)} %bitcast.21, bf16[256,256]{1,0:T(8,128)(2,1)S(1)} %bitcast.30, bf16[256,256]{1,0:T(8,128)(2,1)S(1)} %bitcast.25, ...), custom_call_target="tpu_custom_call" | custom-call | flops 67108864 | bytes 4194304 | tf_op jit(solution)/shard_map/local/pallas_call | solution.py:568
  18.6 0.9 %local.3 = (f32[256,1024]{1,0:T(8,128)S(1)}, f32[256,1024]{1,0:T(8,128)S(1)}, f32[256,1024]{1,0:T(8,128)S(1)}) custom-call(s32[1,1024]{1,0:T(1,128)S(1)} %copy-done.7, bf16[256,2048]{1,0:T(8,128)(2,1)S(1)} %bitcast.20, bf16[256,2048]{1,0:T(8,128)(2,1)S(1)} %bitcast.22, bf16[256,256]{1,0:T(8,128)(2,1)S(1)} %bitcast.31, bf16[256,256]{1,0:T(8,128)(2,1)S(1)} %bitcast.26, ...), custom_call_target="tpu_custom_call" | custom-call | flops 67108864 | bytes 4194304 | tf_op jit(solution)/shard_map/local/pallas_call | solution.py:568
  19.5 0.0 collective-permute-done.refs_0_
  19.5 0.7 %collective-permute-start.2 = (bf16[256,512]{1,0:T(8,128)(2,1)S(1)}, bf16[256,512]{1,0:T(8,128)(2,1)S(1)}, u32[]{:S(2)}, u32[]{:S(2)}) collective-permute-start(bf16[256,512]{1,0:T(8,128)(2,1)S(1)} %collective-permute-done.refs_0_), channel_id=1, source_target_pairs={{4,8},{8,4},{5,9},{9,5},{6,10},{10,6},{7,11},{11,7},{20,24},{24,20... | collective-permute-start | bytes 786440 | tf_op jit(solution)/shard_map/ppermute | solution.py:596
  20.2 0.3 collective-permute-done.8.got_ref.refs_0_
  20.5 0.7 %collective-permute-start.9 = (bf16[144,1024]{1,0:T(8,128)(2,1)S(1)}, bf16[144,1024]{1,0:T(8,128)(2,1)S(1)}, u32[]{:S(2)}, u32[]{:S(2)}) collective-permute-start(bf16[144,1024]{1,0:T(8,128)(2,1)S(1)} %chain.6), channel_id=1, source_target_pairs={{4,8},{8,4},{5,9},{9,5},{6,10},{10,6},{7,11},{11,7},{20,24},{24,20... | collective-permute-start | bytes 884744 | tf_op jit(solution)/shard_map/ppermute | solution.py:657
  21.2 0.0 collective-permute-done.1.refs_1_
  21.2 1.3 %collective-permute-start.3 = (bf16[256,512]{1,0:T(8,128)(2,1)S(1)}, bf16[256,512]{1,0:T(8,128)(2,1)S(1)}, u32[]{:S(2)}, u32[]{:S(2)}) collective-permute-start(bf16[256,512]{1,0:T(8,128)(2,1)S(1)} %collective-permute-done.1.refs_1_), channel_id=1, source_target_pairs={{4,0},{8,12},{5,1},{9,13},{6,2},{10,14},{7,3},{11,15},{20,16},{24,... | collective-permute-start | bytes 786440 | tf_op jit(solution)/shard_map/ppermute | solution.py:598
  22.5 0.0 collective-permute-done.2.refs_2_
  22.5 1.3 %collective-permute-start.4 = (bf16[256,512]{1,0:T(8,128)(2,1)S(1)}, bf16[256,512]{1,0:T(8,128)(2,1)S(1)}, u32[]{:S(2)}, u32[]{:S(2)}) collective-permute-start(bf16[256,512]{1,0:T(8,128)(2,1)S(1)} %collective-permute-done.2.refs_2_), channel_id=1, source_target_pairs={{4,0},{8,12},{5,1},{9,13},{6,2},{10,14},{7,3},{11,15},{20,16},{24,... | collective-permute-start | bytes 786440 | tf_op jit(solution)/shard_map/ppermute | solution.py:599
  23.8 1.9 %collective-permute-done.5.got_ref.refs_0_ = bf16[144,1024]{1,0:T(8,128)(2,1)S(1)} collective-permute-done((bf16[144,1024]{1,0:T(8,128)(2,1)S(1)}, bf16[144,1024]{1,0:T(8,128)(2,1)S(1)}, u32[]{:S(2)}, u32[]{:S(2)}) %collective-permute-start.5) | collective-permute-done | bytes 294944 | tf_op jit(solution)/shard_map/ppermute | solution.py:657
  25.7 0.8 %collective-permute-start.6 = (bf16[144,1024]{1,0:T(8,128)(2,1)S(1)}, bf16[144,1024]{1,0:T(8,128)(2,1)S(1)}, u32[]{:S(2)}, u32[]{:S(2)}) collective-permute-start(bf16[144,1024]{1,0:T(8,128)(2,1)S(1)} %chain.4), channel_id=1, source_target_pairs={{4,8},{8,4},{5,9},{9,5},{6,10},{10,6},{7,11},{11,7},{20,24},{24,20... | collective-permute-start | bytes 884744 | tf_op jit(solution)/shard_map/ppermute | solution.py:657
  26.5 0.0 collective-permute-done.9.got_ref.refs_1_
  26.5 1.3 %collective-permute-start.10 = (bf16[144,1024]{1,0:T(8,128)(2,1)S(1)}, bf16[144,1024]{1,0:T(8,128)(2,1)S(1)}, u32[]{:S(2)}, u32[]{:S(2)}) collective-permute-start(bf16[144,1024]{1,0:T(8,128)(2,1)S(1)} %chain.7), channel_id=1, source_target_pairs={{8,12},{4,0},{9,13},{5,1},{10,14},{6,2},{11,15},{7,3},{24,28},{20,... | collective-permute-start | bytes 884744 | tf_op jit(solution)/shard_map/ppermute | solution.py:657
  27.8 6.9 %collective-permute-done.3.refs_3_ = bf16[256,512]{1,0:T(8,128)(2,1)S(1)} collective-permute-done((bf16[256,512]{1,0:T(8,128)(2,1)S(1)}, bf16[256,512]{1,0:T(8,128)(2,1)S(1)}, u32[]{:S(2)}, u32[]{:S(2)}) %collective-permute-start.3) | collective-permute-done | bytes 262176 | tf_op jit(solution)/shard_map/ppermute | solution.py:598
  34.7 5.1 %collective-permute-done.4.refs_4_ = bf16[256,512]{1,0:T(8,128)(2,1)S(1)} collective-permute-done((bf16[256,512]{1,0:T(8,128)(2,1)S(1)}, bf16[256,512]{1,0:T(8,128)(2,1)S(1)}, u32[]{:S(2)}, u32[]{:S(2)}) %collective-permute-start.4) | collective-permute-done | bytes 262176 | tf_op jit(solution)/shard_map/ppermute | solution.py:599
  39.8 3.6 %attention.2 = (bf16[256,2048]{1,0:T(8,128)(2,1)}, bf16[256,1024]{1,0:T(8,128)(2,1)S(1)}) custom-call(s32[1,1024]{1,0:T(1,128)S(1)} %copy-done.7, bf16[256,2048]{1,0:T(8,128)(2,1)S(1)} %bitcast.23, bf16[256,256]{1,0:T(8,128)(2,1)S(1)} %bitcast.33, bf16[256,256]{1,0:T(8,128)(2,1)S(1)} %bitcast.36, bf16[256,512]{1,0:T(8,128)(2,1)S(1)} %collective-permute-done.refs_0_, ...), custom_call_target="tpu_custom_call" | custom-call | flops 603979776 | bytes 2097152 | tf_op jit(solution)/shard_map/attention/pallas_call | solution.py:613
  43.5 0.0 collective-permute-done.6.got_ref.refs_1_
  43.5 1.3 %collective-permute-start.7 = (bf16[144,1024]{1,0:T(8,128)(2,1)S(1)}, bf16[144,1024]{1,0:T(8,128)(2,1)S(1)}, u32[]{:S(2)}, u32[]{:S(2)}) collective-permute-start(bf16[144,1024]{1,0:T(8,128)(2,1)S(1)} %chain.5), channel_id=1, source_target_pairs={{8,12},{4,0},{9,13},{5,1},{10,14},{6,2},{11,15},{7,3},{24,28},{20,... | collective-permute-start | bytes 884744 | tf_op jit(solution)/shard_map/ppermute | solution.py:657
  44.8 0.0 copy-start.8
  44.8 3.6 %attention.3 = (bf16[256,2048]{1,0:T(8,128)(2,1)}, bf16[256,1024]{1,0:T(8,128)(2,1)S(1)}) custom-call(s32[1,1024]{1,0:T(1,128)S(1)} %copy-done.7, bf16[256,2048]{1,0:T(8,128)(2,1)S(1)} %bitcast.24, bf16[256,256]{1,0:T(8,128)(2,1)S(1)} %bitcast.34, bf16[256,256]{1,0:T(8,128)(2,1)S(1)} %bitcast.37, ...), custom_call_target="tpu_custom_call", output_to_operand_aliasing={{0}: (9, {})} | custom-call | flops 603979776 | bytes 2097152 | tf_op jit(solution)/shard_map/attention/pallas_call | solution.py:613
  48.4 0.0 collective-permute-done.10.refs_2_
  48.4 2.4 %final.2 = (bf16[256,2048]{1,0:T(8,128)(2,1)}, f32[3,1024]{1,0:T(4,128)S(1)}) custom-call(f32[256,1024]{1,0:T(8,128)S(1)} %get-tuple-element.64.pre_ref, f32[256,1024]{1,0:T(8,128)S(1)} %get-tuple-element.65.reach_ref, f32[256,1024]{1,0:T(8,128)S(1)} %get-tuple-element.66.sx_ref, bf16[256,256]{1,0:T(8,128)(2,1)S(1)} %bitcast.27, ...), custom_call_target="tpu_custom_call" | custom-call | flops 67108864 | bytes 5242880 | tf_op jit(solution)/shard_map/final/pallas_call | solution.py:662
  50.8 1.2 %collective-permute-done.7.refs_2_ = bf16[144,1024]{1,0:T(8,128)(2,1)S(1)} collective-permute-done((bf16[144,1024]{1,0:T(8,128)(2,1)S(1)}, bf16[144,1024]{1,0:T(8,128)(2,1)S(1)}, u32[]{:S(2)}, u32[]{:S(2)}) %collective-permute-start.7) | collective-permute-done | bytes 294944 | tf_op jit(solution)/shard_map/ppermute | solution.py:657
  52.1 2.4 %final.3 = (bf16[256,2048]{1,0:T(8,128)(2,1)}, f32[3,1024]{1,0:T(4,128)S(1)}) custom-call(f32[256,1024]{1,0:T(8,128)S(1)} %get-tuple-element.54.pre_ref, f32[256,1024]{1,0:T(8,128)S(1)} %get-tuple-element.55.reach_ref, f32[256,1024]{1,0:T(8,128)S(1)} %get-tuple-element.56.sx_ref, bf16[256,256]{1,0:T(8,128)(2,1)S(1)} %bitcast.28, ...), custom_call_target="tpu_custom_call", output_to_operand_aliasing={{0}: (12, {})} | custom-call | flops 67108864 | bytes 5242880 | tf_op jit(solution)/shard_map/final/pallas_call | solution.py:662
  54.5 1.5 %collective-permute-start.12 = (f32[3,1024]{1,0:T(4,128)S(1)}, f32[3,1024]{1,0:T(4,128)S(1)}, u32[]{:S(2)}, u32[]{:S(2)}) collective-permute-start(f32[3,1024]{1,0:T(4,128)S(1)} %get-tuple-element.75), channel_id=1, source_target_pairs={{0,16},{4,20},{8,24},{12,28},{16,0},{20,4},{24,8},{28,12},{1,17},{... | collective-permute-start | bytes 36872 | tf_op jit(solution)/shard_map/ppermute | solution.py:490
  56.0 1.3 %collective-permute-start.13 = (f32[3,1024]{1,0:T(4,128)S(1)}, f32[3,1024]{1,0:T(4,128)S(1)}, u32[]{:S(2)}, u32[]{:S(2)}) collective-permute-start(f32[3,1024]{1,0:T(4,128)S(1)} %get-tuple-element.75), channel_id=1, source_target_pairs={{0,20},{4,16},{8,28},{12,24},{16,4},{20,0},{24,12},{28,8},{1,21},{... | collective-permute-start | bytes 36872 | tf_op jit(solution)/shard_map/ppermute | solution.py:490
  57.4 0.6 collective-permute-start.11
  58.0 0.2 collective-permute-done.12
  58.2 2.4 %collective-permute-done.13 = f32[3,1024]{1,0:T(4,128)S(1)} collective-permute-done((f32[3,1024]{1,0:T(4,128)S(1)}, f32[3,1024]{1,0:T(4,128)S(1)}, u32[]{:S(2)}, u32[]{:S(2)}) %collective-permute-start.13) | collective-permute-done | bytes 12320 | tf_op jit(solution)/shard_map/ppermute | solution.py:490
  60.7 0.4 collective-permute-done.11
  61.1 1.0 %collective-permute-start.14 = (f32[3,1024]{1,0:T(4,128)S(1)}, f32[3,1024]{1,0:T(4,128)S(1)}, u32[]{:S(2)}, u32[]{:S(2)}) collective-permute-start(f32[3,1024]{1,0:T(4,128)S(1)} %add_add_fusion.a_ref), channel_id=1, source_target_pairs={{0,8},{4,12},{8,0},{12,4},{16,24},{20,28},{24,16},{28,20},{1,9},{5... | collective-permute-start | bytes 36872 | tf_op jit(solution)/shard_map/ppermute | solution.py:490
  62.1 3.7 %collective-permute-done.14.b_ref = f32[3,1024]{1,0:T(4,128)S(1)} collective-permute-done((f32[3,1024]{1,0:T(4,128)S(1)}, f32[3,1024]{1,0:T(4,128)S(1)}, u32[]{:S(2)}, u32[]{:S(2)}) %collective-permute-start.14) | collective-permute-done | bytes 12320 | tf_op jit(solution)/shard_map/ppermute | solution.py:490
  65.8 0.6 closing.1
  (15 shorter events, 0.1 us)
Async XLA Ops:
  0.6 15.2 %copy-start = (bf16[1,256,2048]{2,1,0:T(8,128)(2,1)S(1)}, bf16[1,256,2048]{2,1,0:T(8,128)(2,1)}, u32[]{:S(2)}) copy-start(bf16[1,256,2048]{2,1,0:T(8,128)(2,1)} %param.17) | copy-start | bytes 3145732
  0.6 15.2 %copy-start.3 = (bf16[1,256,256]{2,1,0:T(8,128)(2,1)S(1)}, bf16[1,256,256]{2,1,0:T(8,128)(2,1)}, u32[]{:S(2)}) copy-start(bf16[1,256,256]{2,1,0:T(8,128)(2,1)} %param.20) | copy-start | bytes 393220
  0.7 15.2 %copy-start.4 = (bf16[1,256,256]{2,1,0:T(8,128)(2,1)S(1)}, bf16[1,256,256]{2,1,0:T(8,128)(2,1)}, u32[]{:S(2)}) copy-start(bf16[1,256,256]{2,1,0:T(8,128)(2,1)} %param.19) | copy-start | bytes 393220
  4.3 15.2 %collective-permute-start = (bf16[256,512]{1,0:T(8,128)(2,1)S(1)}, bf16[256,512]{1,0:T(8,128)(2,1)S(1)}, u32[]{:S(2)}, u32[]{:S(2)}) collective-permute-start(bf16[256,512]{1,0:T(8,128)(2,1)S(1)} %get-tuple-element.41), channel_id=1, source_target_pairs={{0,4},{4,0},{8,12},{12,8},{1,5},{5,1},{9,13},{13,9},{2,6},{6,2},{1... | collective-permute-start | bytes 786440 | tf_op jit(solution)/shard_map/ppermute | solution.py:593
  7.5 13.0 %collective-permute-start.8 = (bf16[144,1024]{1,0:T(8,128)(2,1)S(1)}, bf16[144,1024]{1,0:T(8,128)(2,1)S(1)}, u32[]{:S(2)}, u32[]{:S(2)}) collective-permute-start(bf16[144,1024]{1,0:T(8,128)(2,1)S(1)} %get-tuple-element.70), channel_id=1, source_target_pairs={{0,4},{12,8},{1,5},{13,9},{2,6},{14,10},{3,7},{15,11},{16,20},{28,... | collective-permute-start | bytes 884744 | tf_op jit(solution)/shard_map/ppermute | solution.py:657
  9.4 11.8 %collective-permute-start.1 = (bf16[256,512]{1,0:T(8,128)(2,1)S(1)}, bf16[256,512]{1,0:T(8,128)(2,1)S(1)}, u32[]{:S(2)}, u32[]{:S(2)}) collective-permute-start(bf16[256,512]{1,0:T(8,128)(2,1)S(1)} %get-tuple-element.41), channel_id=1, source_target_pairs={{4,8},{8,4},{5,9},{9,5},{6,10},{10,6},{7,11},{11,7},{20,24},{24,20... | collective-permute-start | bytes 786440 | tf_op jit(solution)/shard_map/ppermute | solution.py:594
  10.1 15.6 %collective-permute-start.5 = (bf16[144,1024]{1,0:T(8,128)(2,1)S(1)}, bf16[144,1024]{1,0:T(8,128)(2,1)S(1)}, u32[]{:S(2)}, u32[]{:S(2)}) collective-permute-start(bf16[144,1024]{1,0:T(8,128)(2,1)S(1)} %get-tuple-element.60), channel_id=1, source_target_pairs={{0,4},{12,8},{1,5},{13,9},{2,6},{14,10},{3,7},{15,11},{16,20},{28,... | collective-permute-start | bytes 884744 | tf_op jit(solution)/shard_map/ppermute | solution.py:657
  15.8 0.7 %copy-start.7 = (s32[1,1024]{1,0:T(1,128)S(1)}, s32[1,1024]{1,0:T(1,128)}, u32[]{:S(2)}) copy-start(s32[1,1024]{1,0:T(1,128)} %docs_ref.9) | copy-start | bytes 12292
  15.8 0.7 %copy-start.9 = (f32[32]{0:T(128)S(1)}, f32[32]{0:T(128)}, u32[]{:S(2)}) copy-start(f32[32]{0:T(128)} %param.24) | copy-start | bytes 388
  16.5 1.2 %copy-start.1 = (bf16[1,256,2048]{2,1,0:T(8,128)(2,1)S(1)}, bf16[1,256,2048]{2,1,0:T(8,128)(2,1)}, u32[]{:S(2)}) copy-start(bf16[1,256,2048]{2,1,0:T(8,128)(2,1)} %param.18) | copy-start | bytes 3145732
  19.5 3.0 %collective-permute-start.2 = (bf16[256,512]{1,0:T(8,128)(2,1)S(1)}, bf16[256,512]{1,0:T(8,128)(2,1)S(1)}, u32[]{:S(2)}, u32[]{:S(2)}) collective-permute-start(bf16[256,512]{1,0:T(8,128)(2,1)S(1)} %collective-permute-done.refs_0_), channel_id=1, source_target_pairs={{4,8},{8,4},{5,9},{9,5},{6,10},{10,6},{7,11},{11,7},{20,24},{24,20... | collective-permute-start | bytes 786440 | tf_op jit(solution)/shard_map/ppermute | solution.py:596
  20.5 6.0 %collective-permute-start.9 = (bf16[144,1024]{1,0:T(8,128)(2,1)S(1)}, bf16[144,1024]{1,0:T(8,128)(2,1)S(1)}, u32[]{:S(2)}, u32[]{:S(2)}) collective-permute-start(bf16[144,1024]{1,0:T(8,128)(2,1)S(1)} %chain.6), channel_id=1, source_target_pairs={{4,8},{8,4},{5,9},{9,5},{6,10},{10,6},{7,11},{11,7},{20,24},{24,20... | collective-permute-start | bytes 884744 | tf_op jit(solution)/shard_map/ppermute | solution.py:657
  21.2 13.5 %collective-permute-start.3 = (bf16[256,512]{1,0:T(8,128)(2,1)S(1)}, bf16[256,512]{1,0:T(8,128)(2,1)S(1)}, u32[]{:S(2)}, u32[]{:S(2)}) collective-permute-start(bf16[256,512]{1,0:T(8,128)(2,1)S(1)} %collective-permute-done.1.refs_1_), channel_id=1, source_target_pairs={{4,0},{8,12},{5,1},{9,13},{6,2},{10,14},{7,3},{11,15},{20,16},{24,... | collective-permute-start | bytes 786440 | tf_op jit(solution)/shard_map/ppermute | solution.py:598
  22.5 17.3 %collective-permute-start.4 = (bf16[256,512]{1,0:T(8,128)(2,1)S(1)}, bf16[256,512]{1,0:T(8,128)(2,1)S(1)}, u32[]{:S(2)}, u32[]{:S(2)}) collective-permute-start(bf16[256,512]{1,0:T(8,128)(2,1)S(1)} %collective-permute-done.2.refs_2_), channel_id=1, source_target_pairs={{4,0},{8,12},{5,1},{9,13},{6,2},{10,14},{7,3},{11,15},{20,16},{24,... | collective-permute-start | bytes 786440 | tf_op jit(solution)/shard_map/ppermute | solution.py:599
  25.7 14.2 %copy-start.2 = (bf16[1,256,2048]{2,1,0:T(8,128)(2,1)S(1)}, bf16[1,256,2048]{2,1,0:T(8,128)(2,1)}, u32[]{:S(2)}) copy-start(bf16[1,256,2048]{2,1,0:T(8,128)(2,1)} %param.13) | copy-start | bytes 3145732
  25.7 14.2 %copy-start.5 = (bf16[1,256,256]{2,1,0:T(8,128)(2,1)S(1)}, bf16[1,256,256]{2,1,0:T(8,128)(2,1)}, u32[]{:S(2)}) copy-start(bf16[1,256,256]{2,1,0:T(8,128)(2,1)} %param.14) | copy-start | bytes 393220
  25.7 14.2 %copy-start.6 = (bf16[1,256,256]{2,1,0:T(8,128)(2,1)S(1)}, bf16[1,256,256]{2,1,0:T(8,128)(2,1)}, u32[]{:S(2)}) copy-start(bf16[1,256,256]{2,1,0:T(8,128)(2,1)} %param.15) | copy-start | bytes 393220
  25.7 17.8 %collective-permute-start.6 = (bf16[144,1024]{1,0:T(8,128)(2,1)S(1)}, bf16[144,1024]{1,0:T(8,128)(2,1)S(1)}, u32[]{:S(2)}, u32[]{:S(2)}) collective-permute-start(bf16[144,1024]{1,0:T(8,128)(2,1)S(1)} %chain.4), channel_id=1, source_target_pairs={{4,8},{8,4},{5,9},{9,5},{6,10},{10,6},{7,11},{11,7},{20,24},{24,20... | collective-permute-start | bytes 884744 | tf_op jit(solution)/shard_map/ppermute | solution.py:657
  26.5 21.9 %collective-permute-start.10 = (bf16[144,1024]{1,0:T(8,128)(2,1)S(1)}, bf16[144,1024]{1,0:T(8,128)(2,1)S(1)}, u32[]{:S(2)}, u32[]{:S(2)}) collective-permute-start(bf16[144,1024]{1,0:T(8,128)(2,1)S(1)} %chain.7), channel_id=1, source_target_pairs={{8,12},{4,0},{9,13},{5,1},{10,14},{6,2},{11,15},{7,3},{24,28},{20,... | collective-permute-start | bytes 884744 | tf_op jit(solution)/shard_map/ppermute | solution.py:657
  43.5 8.6 %collective-permute-start.7 = (bf16[144,1024]{1,0:T(8,128)(2,1)S(1)}, bf16[144,1024]{1,0:T(8,128)(2,1)S(1)}, u32[]{:S(2)}, u32[]{:S(2)}) collective-permute-start(bf16[144,1024]{1,0:T(8,128)(2,1)S(1)} %chain.5), channel_id=1, source_target_pairs={{8,12},{4,0},{9,13},{5,1},{10,14},{6,2},{11,15},{7,3},{24,28},{20,... | collective-permute-start | bytes 884744 | tf_op jit(solution)/shard_map/ppermute | solution.py:657
  44.8 3.7 %copy-start.8 = (f32[2048]{0:T(1024)S(1)}, f32[2048]{0:T(1024)}, u32[]{:S(2)}) copy-start(f32[2048]{0:T(1024)} %param.25) | copy-start | bytes 24580
  54.5 3.7 %collective-permute-start.12 = (f32[3,1024]{1,0:T(4,128)S(1)}, f32[3,1024]{1,0:T(4,128)S(1)}, u32[]{:S(2)}, u32[]{:S(2)}) collective-permute-start(f32[3,1024]{1,0:T(4,128)S(1)} %get-tuple-element.75), channel_id=1, source_target_pairs={{0,16},{4,20},{8,24},{12,28},{16,0},{20,4},{24,8},{28,12},{1,17},{... | collective-permute-start | bytes 36872 | tf_op jit(solution)/shard_map/ppermute | solution.py:490
  56.0 4.6 %collective-permute-start.13 = (f32[3,1024]{1,0:T(4,128)S(1)}, f32[3,1024]{1,0:T(4,128)S(1)}, u32[]{:S(2)}, u32[]{:S(2)}) collective-permute-start(f32[3,1024]{1,0:T(4,128)S(1)} %get-tuple-element.75), channel_id=1, source_target_pairs={{0,20},{4,16},{8,28},{12,24},{16,4},{20,0},{24,12},{28,8},{1,21},{... | collective-permute-start | bytes 36872 | tf_op jit(solution)/shard_map/ppermute | solution.py:490
  57.4 3.7 %collective-permute-start.11 = (f32[3,1024]{1,0:T(4,128)S(1)}, f32[3,1024]{1,0:T(4,128)S(1)}, u32[]{:S(2)}, u32[]{:S(2)}) collective-permute-start(f32[3,1024]{1,0:T(4,128)S(1)} %get-tuple-element.75), channel_id=1, source_target_pairs={{0,4},{4,0},{8,12},{12,8},{16,20},{20,16},{24,28},{28,24},{1,5},{5... | collective-permute-start | bytes 36872 | tf_op jit(solution)/shard_map/ppermute | solution.py:490
  61.1 4.7 %collective-permute-start.14 = (f32[3,1024]{1,0:T(4,128)S(1)}, f32[3,1024]{1,0:T(4,128)S(1)}, u32[]{:S(2)}, u32[]{:S(2)}) collective-permute-start(f32[3,1024]{1,0:T(4,128)S(1)} %add_add_fusion.a_ref), channel_id=1, source_target_pairs={{0,8},{4,12},{8,0},{12,4},{16,24},{20,28},{24,16},{28,20},{1,9},{5... | collective-permute-start | bytes 36872 | tf_op jit(solution)/shard_map/ppermute | solution.py:490

commit v6 on v5

--- a/solution.py
+++ b/solution.py
@@ -120,11 +120,20 @@
     xw_refs, dec_refs, f_refs, b_refs, send_refs = (
         outs[k * groups : (k + 1) * groups] for k in range(5)
     )
+    x_here, x_sem = outs[5 * groups :]
     heads, rows = dt_ref.shape
     stretch = rows // 2
     width = x_ref.shape[1] // groups
     kv_width = k_ref.shape[1]
     index = lax.axis_index("ctx")
+    loads_x = [
+        pltpu.make_async_copy(
+            x_ref.at[:, pl.ds(g * width, width)], x_here.at[g], x_sem.at[g]
+        )
+        for g in range(groups)
+    ]
+    for load in loads_x:
+        load.start()
     kv_ref[:, :kv_width] = k_ref[...]
     kv_ref[:, kv_width:] = v_ref[...]
     triangle = jnp.where(lower_triangle(stretch), 1.0, 0.0)
@@ -157,14 +166,14 @@
         same = jnp.where(as_column(row) == last.astype(F32), 1.0, 0.0)
         projs.append((b_ref[sl, :].astype(F32) * same).astype(BF16))
     for g in range(groups):
-        cols = slice(g * width, (g + 1) * width)
         matrix = spread_matrix(heads, width, g * (heads // groups))
         wide = spread(ends, matrix)
         dec_refs[g][...] = wide
         sums = []
+        loads_x[g].wait()
         for half in range(2):
             sl = slice(half * stretch, (half + 1) * stretch)
-            xw = (x_ref[sl, cols].astype(F32) * spread(loads[half], matrix)).astype(BF16)
+            xw = (x_here[g, sl, :].astype(F32) * spread(loads[half], matrix)).astype(BF16)
             xw_refs[g][sl, :] = xw
             sums.append(dot_tn(projs[half][:, g * N : (g + 1) * N], xw) * wide[2 + half : 3 + half])
         f_refs[g][...] = sums[0].astype(BF16)
@@ -196,49 +205,79 @@
 
 
 def local_kernel(
-    count,
-    first,
-    docs_ref,
-    x_ref,
-    gate_ref,
-    b_ref,
-    c_ref,
-    ec_ref,
-    skip_ref,
-    xw_ref,
-    pre_ref,
-    reach_ref,
-    sx_ref,
+    count, groups, docs_ref, x_ref, gate_ref, b_ref, c_ref, skip_ref, ec_ref, *refs
 ):
+    xw_refs, pre_refs, reach_refs, sx_refs = (
+        refs[k * groups : (k + 1) * groups] for k in range(4)
+    )
+    x_here, gate_here, sems = refs[4 * groups :]
     heads, rows = ec_ref.shape
     stretch = rows // 2
-    width = x_ref.shape[1]
+    width = x_ref.shape[1] // groups
     index = lax.axis_index("ctx")
-    matrix = spread_matrix(heads, width, first)
-    wide_skip = spread(as_column(skip_ref[...]), matrix)
+    moves = []
+    for g in range(groups):
+        cols = pl.ds(g * width, width)
+        moves.append(
+            [
+                pltpu.make_async_copy(x_ref.at[:, cols], x_here.at[g], sems.at[0, g]),
+                pltpu.make_async_copy(gate_ref.at[:, cols], gate_here.at[g], sems.at[1, g]),
+            ]
+        )
+        for move in moves[g]:
+            move.start()
     triangle = lower_triangle(stretch)
+    skip = as_column(skip_ref[...])
     step = 16
+    masks = []
     for half in range(2):
         block = own_block(index, count, half)
-        sl = slice(half * stretch, (half + 1) * stretch)
         row = doc_row(docs_ref, block, stretch)
         column = as_column(row)
-        gram = dot_nt(c_ref[sl, :], b_ref[sl, :])
-        gram = jnp.where(triangle & (column == row.astype(F32)), gram, 0.0).astype(BF16)
-        wide = spread(ec_ref[:, sl], matrix)
-        inner = jnp.dot(gram, xw_ref[sl, :], preferred_element_type=F32)
         reached = jnp.where(column == prior_doc(docs_ref, block, stretch).astype(F32), 1.0, 0.0)
-        for k in range(0, stretch, step):
-            at = slice(half * stretch + k, half * stretch + k + step)
-            here = slice(k, k + step)
-            x = x_ref[at, :].astype(F32)
-            gate = gate_ref[at, :].astype(F32)
-            silu = gate / (1.0 + jnp.exp(-gate))
-            fade = wide[here] * silu
-            sx = silu * x
-            sx_ref[at, :] = sx
-            pre_ref[at, :] = inner[here] * fade + wide_skip * sx
-            reach_ref[at, :] = reached[here] * fade
+        masks.append((triangle & (column == row.astype(F32)), reached))
+    for g in range(groups):
+        proj = slice(g * N, (g + 1) * N)
+        matrix = spread_matrix(heads, width, g * (heads // groups))
+        wide_skip = spread(skip, matrix)
+        for half in range(2):
+            sl = slice(half * stretch, (half + 1) * stretch)
+            near, reached = masks[half]
+            gram = dot_nt(c_ref[sl, proj], b_ref[sl, proj])
+            gram = jnp.where(near, gram, 0.0).astype(BF16)
+            wide = spread(ec_ref[:, sl], matrix)
+            inner = jnp.dot(gram, xw_refs[g][sl, :], preferred_element_type=F32)
+            if half == 0:
+                for move in moves[g]:
+                    move.wait()
+            for k in range(0, stretch, step):
+                at = slice(half * stretch + k, half * stretch + k + step)
+                here = slice(k, k + step)
+                x = x_here[g, at, :].astype(F32)
+                gate = gate_here[g, at, :].astype(F32)
+                silu = gate / (1.0 + jnp.exp(-gate))
+                fade = wide[here] * silu
+                sx = silu * x
+                sx_refs[g][at, :] = sx
+                pre_refs[g][at, :] = inner[here] * fade + wide_skip * sx
+                reach_refs[g][at, :] = reached[here] * fade
+
+
+def merge_kernel(count, state_ref, kv_ref, out_ref):
+    index = lax.axis_index("ctx")
+    outer = (index == 0) | (index == count - 1)
+    rows, wide = kv_ref.shape
+    stretch = rows // 2
+
+    @pl.when(outer)
+    def _():
+        out_ref[...] = state_ref[...]
+
+    @pl.when(jnp.logical_not(outer))
+    def _():
+        out_ref[:stretch, :wide] = kv_ref[:stretch, :]
+        out_ref[:stretch, wide:] = kv_ref[stretch:, :]
+        out_ref[stretch:, :] = jnp.zeros((out_ref.shape[0] - stretch, 2 * wide), BF16)
 
 
 def arrivals(index, count, refs):
@@ -263,14 +302,12 @@
 def attention_kernel(count, per, stack, g, docs_ref, q_ref, k_ref, v_ref, *refs):
     others = count - 1
     sent = 5 if count == 4 else others
-    out_ref, copy_ref, kt, vt, bias_f, bias_b, bias_a = refs[-7:]
+    out_ref, kt, vt, bias_f, bias_b, bias_a = refs[-6:]
     rows = q_ref.shape[0]
     stretch = rows // 2
     index = lax.axis_index("ctx")
     last = 2 * count - 1
     kv_width = refs[0].shape[1] // 2
-    k_cols = slice(g * DH, (g + 1) * DH)
-    v_cols = slice(kv_width + g * DH, kv_width + (g + 1) * DH)
     row_f = doc_row(docs_ref, index, stretch).astype(F32)
     row_b = doc_row(docs_ref, last - index, stretch).astype(F32)
     col_f = as_column(row_f)
@@ -284,23 +321,27 @@
     bias_b[:, tile(0)] = jnp.where(col_b == row_f, 0.0, MASKED)
     bias_b[:, tile(1)] = jnp.where(triangle & (col_b == row_b), 0.0, MASKED)
     vt[:, DH:] = jnp.ones((vt.shape[0], DH), BF16)
-    kt[tile(0), :] = k_ref[:stretch, :]
-    vt[tile(0), :DH] = v_ref[:stretch, :]
-    kt[tile(count), :] = k_ref[stretch:, :]
-    vt[tile(count), :DH] = v_ref[stretch:, :]
+    here = slice(g * DH, (g + 1) * DH)
+    kt[tile(0), :] = k_ref[:stretch, here]
+    vt[tile(0), :DH] = v_ref[:stretch, here]
+    kt[tile(count), :] = k_ref[stretch:, here]
+    vt[tile(count), :DH] = v_ref[stretch:, here]
     lower = []
     for r, (source, places) in enumerate(arrivals(index, count, refs[:sent])):
         lower.append(source < index)
         for condition, ref in places:
 
             def fetch(ref=ref, r=r):
-                front = slice(0, stretch)
-                start = jnp.where(lower[r], 0, stretch)
-                own = pl.ds(pl.multiple_of(start, stretch), stretch)
-                kt[tile(1 + r), :] = ref[own, k_cols]
-                vt[tile(1 + r), :DH] = ref[own, v_cols]
-                kt[tile(count + 1 + r), :] = ref[front, k_cols]
-                vt[tile(count + 1 + r), :DH] = ref[front, v_cols]
+                folded = ref.shape[1] > 2 * kv_width
+                gap = jnp.where(lower[r], 0, 2 * kv_width if folded else stretch)
+                for table, first in ((kt, g * DH), (vt, kv_width + g * DH)):
+                    front = ref[:stretch, first : first + DH]
+                    if folded:
+                        own = ref[:stretch, pl.ds(pl.multiple_of(first + gap, DH), DH)]
+                    else:
+                        own = ref[pl.ds(pl.multiple_of(gap, stretch), stretch), first : first + DH]
+                    table[tile(1 + r), :DH] = own
+                    table[tile(count + 1 + r), :DH] = front
 
             if condition is None:
                 fetch()
@@ -318,7 +359,7 @@
     def stacked(first, base):
         return jnp.concatenate(
             [
-                q_ref[base : base + stretch, (first + j) * DH : (first + j + 1) * DH]
+                q_ref[base : base + stretch, (g * per + first + j) * DH : (g * per + first + j + 1) * DH]
                 for j in range(stack)
             ],
             axis=0,
@@ -364,7 +405,6 @@
             for j in range(stack):
                 cols = slice((first + j) * DH, (first + j + 1) * DH)
                 out_ref[tile(half), cols] = result[tile(j)]
-                copy_ref[tile(half), cols] = result[tile(j)]
 
 
 def final_kernel(
@@ -385,6 +425,8 @@
     others = count - 1
     got = refs[:others]
     before = refs[others] if g else None
+    proj = slice(g * N, (g + 1) * N)
+    first_lane = g * pre_ref.shape[1]
     out_ref, grad_ref, front, back, flow, gated_ref, sums, gain_acc, skip_acc = refs[-9:]
     rows, width = pre_ref.shape
     stretch = rows // 2
@@ -416,8 +458,8 @@
     d_in = back[N : N + 1, :].astype(F32) + back[N + 1 : N + 2, :].astype(F32)
     through = dec_ref[0:1, :] * front[...].astype(F32) + f_ref[...].astype(F32)
     entering = (d_in * through + back[:N, :].astype(F32)).astype(BF16)
-    flow[:stretch, :] = jnp.dot(c_ref[:stretch, :], front[...], preferred_element_type=F32)
-    flow[stretch:, :] = jnp.dot(c_ref[stretch:, :], entering, preferred_element_type=F32)
+    flow[:stretch, :] = jnp.dot(c_ref[:stretch, proj], front[...], preferred_element_type=F32)
+    flow[stretch:, :] = jnp.dot(c_ref[stretch:, proj], entering, preferred_element_type=F32)
     gain_acc[...] = jnp.zeros_like(gain_acc)
     skip_acc[...] = jnp.zeros_like(skip_acc)
 
@@ -429,7 +471,7 @@
             cols = slice(j, j + tile)
             gated = pre_ref[sl, cols] + reach_ref[sl, cols] * flow[sl, cols]
             gated_ref[sl, cols] = gated
-            scaled = gated * gain_ref[:, cols]
+            scaled = gated * gain_ref[:, first_lane + j : first_lane + j + tile]
             totals[0] += gated * gated
             totals[1] += scaled * scaled
             totals[2] += scaled * teacher_ref[sl, cols].astype(F32)
@@ -453,7 +495,7 @@
         mean = sums[sl, tile : 2 * tile]
         for j in range(0, width, tile):
             cols = slice(j, j + tile)
-            gain = gain_ref[:, cols]
+            gain = gain_ref[:, first_lane + j : first_lane + j + tile]
             unit = gated_ref[sl, cols] * scale
             normed = unit * gain
             out_ref[sl, cols] = normed.astype(BF16)
@@ -474,6 +516,19 @@
         by_head += before[groups : groups + 1, :tile]
     grad_ref[g : g + 1, :] = jnp.sum(gain_acc[...], axis=0, keepdims=True)
     grad_ref[groups : groups + 1, :tile] = by_head
+
+
+def writing_kernel(*refs):
+    parts_in, out_ref, sems = refs[:-2], refs[-2], refs[-1]
+    width = parts_in[0].shape[1]
+    moves = [
+        pltpu.make_async_copy(part, out_ref.at[:, pl.ds(k * width, width)], sems.at[k])
+        for k, part in enumerate(parts_in)
+    ]
+    for move in moves:
+        move.start()
+    for move in moves:
+        move.wait()
 
 
 def closing_kernel(a_ref, b_ref, gain_ref, skip_ref):
@@ -519,11 +574,20 @@
     x, gate, bmat, cmat = inputs[0], gate_input[0], b_input[0], c_input[0]
     struct = jax.ShapeDtypeStruct
 
-    def whole(*shape):
-        return pl.BlockSpec(shape, lambda k: (0, 0))
-
-    def chosen(size, g):
-        return pl.BlockSpec((rows, size), lambda k: (0, g))
+    def in_hbm(*arrays):
+        return [pltpu.with_memory_space_constraint(array, pltpu.HBM) for array in arrays]
+
+    def write(*pieces):
+        return pl.pallas_call(
+            writing_kernel,
+            out_shape=struct((rows, features), BF16),
+            in_specs=[VMEM] * len(pieces),
+            out_specs=pl.BlockSpec(memory_space=pl.ANY),
+            scratch_shapes=[pltpu.SemaphoreType.DMA((len(pieces),))],
+            compiler_params=params(2),
+            cost_estimate=cost(0, 4 * rows * features),
+            name="writing",
+        )(*pieces)
 
     state = struct((N, width), BF16)
     payload = struct((N + EXTRA, width), BF16)
@@ -537,24 +601,25 @@
             *([state] * (2 * groups)),
             *([payload] * groups),
         ),
-        in_specs=[VMEM] * 8,
+        in_specs=[VMEM] * 3 + [pl.BlockSpec(memory_space=pl.ANY)] + [VMEM] * 4,
         out_specs=(VMEM,) * (2 + 5 * groups),
+        scratch_shapes=[
+            pltpu.VMEM((groups, rows, width), BF16),
+            pltpu.SemaphoreType.DMA((groups,)),
+        ],
         compiler_params=params(16),
         cost_estimate=cost(4 * rows * features * N, 8 * rows * features),
         name="opening",
     )(
-        *(
-            pltpu.with_memory_space_constraint(array, pltpu.HBM)
-            for array in (
-                doc_ids,
-                keys[0],
-                values[0],
-                x,
-                bmat,
-                dt_raw[0].T,
-                dt_bias.reshape(1, heads),
-                decay_log.reshape(1, heads),
-            )
+        *in_hbm(
+            doc_ids,
+            keys[0],
+            values[0],
+            x,
+            bmat,
+            dt_raw[0].T,
+            dt_bias.reshape(1, heads),
+            decay_log.reshape(1, heads),
         )
     )
     kv, ec = outs[:2]
@@ -562,40 +627,44 @@
         outs[2 + k * groups : 2 + (k + 1) * groups] for k in range(5)
     )
 
-    local = []
-    for g in range(groups):
-        local.append(
-            pl.pallas_call(
-                functools.partial(local_kernel, count, g * (heads // groups)),
-                out_shape=(struct((rows, width), F32),) * 3,
-                grid=(1,),
-                in_specs=[
-                    whole(1, length),
-                    chosen(width, g),
-                    chosen(width, g),
-                    chosen(N, g),
-                    chosen(N, g),
-                    whole(heads, rows),
-                    whole(1, heads),
-                    whole(rows, width),
-                ],
-                out_specs=(whole(rows, width),) * 3,
-                compiler_params=params(16),
-                cost_estimate=cost(2 * rows * width * N, 16 * rows * width),
-                name="local",
-            )(doc_ids, x, gate, bmat, cmat, ec, skip.reshape(1, heads), xw[g])
-        )
+    local = pl.pallas_call(
+        functools.partial(local_kernel, count, groups),
+        out_shape=(struct((rows, width), F32),) * (3 * groups),
+        in_specs=[
+            VMEM,
+            *[pl.BlockSpec(memory_space=pl.ANY)] * 2,
+            *[VMEM] * (4 + groups),
+        ],
+        out_specs=(VMEM,) * (3 * groups),
+        scratch_shapes=[
+            pltpu.VMEM((groups, rows, width), BF16),
+            pltpu.VMEM((groups, rows, width), BF16),
+            pltpu.SemaphoreType.DMA((2, groups)),
+        ],
+        compiler_params=params(16),
+        cost_estimate=cost(2 * rows * features * N, 16 * rows * features),
+        name="local",
+    )(*in_hbm(doc_ids, x, gate, bmat, cmat, skip.reshape(1, heads)), ec, *xw)
 
     send = list(send)
     got = [[] for _ in range(groups)]
     if count == 4:
-        across = [(1, 2), (2, 1)]
-        near = lax.ppermute(kv, "ctx", [(0, 1), (1, 0), (2, 3), (3, 2)])
+        inward, outward, across = [(0, 1), (3, 2)], [(1, 0), (2, 3)], [(1, 2), (2, 1)]
+        near = lax.ppermute(kv, "ctx", inward + outward)
         middle = lax.ppermute(kv, "ctx", across)
-        near, local = lax.optimization_barrier((near, local))
+        middle, *local = lax.optimization_barrier((middle, *local))
         beyond = lax.ppermute(near, "ctx", across)
-        outward = [(1, 0), (2, 3)]
-        far = lax.ppermute(middle, "ctx", outward)
+        send[-1] = pl.pallas_call(
+            functools.partial(merge_kernel, count),
+            out_shape=payload,
+            in_specs=[VMEM] * 2,
+            out_specs=VMEM,
+            compiler_params=params(4),
+            cost_estimate=cost(0, 4 * N * width),
+            name="merge",
+        )(send[-1], middle)
+        far = lax.ppermute(send[-1], "ctx", inward + outward)
+        got[-1].append(far)
         farther = lax.ppermute(beyond, "ctx", outward)
         kv_got = [near, middle, beyond, far, farther]
     else:
@@ -606,23 +675,12 @@
             kv_got.append(lax.ppermute(kv_got[-1], "ctx", ring_pairs))
         kv_got = kv_got[1:]
     stack = 4 if per_kv % 4 == 0 and count <= 4 else 1
-    teacher = None
-    targets = []
-    for g in range(kv_dev):
-        more = [] if teacher is None else [teacher]
-        teacher, target = pl.pallas_call(
+    targets = [
+        pl.pallas_call(
             functools.partial(attention_kernel, count, per_kv, stack, g),
-            out_shape=(struct((rows, features), BF16), struct((rows, per_kv * DH), BF16)),
-            grid=(1,),
-            in_specs=[
-                whole(1, length),
-                chosen(per_kv * DH, g),
-                chosen(DH, g),
-                chosen(DH, g),
-                *[whole(*part.shape) for part in kv_got],
-                *[pl.BlockSpec(memory_space=pl.ANY)] * len(more),
-            ],
-            out_specs=(chosen(per_kv * DH, g), whole(rows, per_kv * DH)),
+            out_shape=struct((rows, per_kv * DH), BF16),
+            in_specs=[VMEM] * (4 + len(kv_got)),
+            out_specs=VMEM,
             scratch_shapes=[
                 pltpu.VMEM((2 * count * stretch, DH), BF16),
                 pltpu.VMEM((2 * count * stretch, 2 * DH), BF16),
@@ -630,15 +688,14 @@
                 pltpu.VMEM((stretch, (count + 1) * stretch), F32),
                 pltpu.VMEM((stretch, others * stretch), F32),
             ],
-            input_output_aliases={4 + len(kv_got): 0} if more else {},
             compiler_params=params(24),
             cost_estimate=cost(
                 4 * (2 * count + 1) * stretch * stretch * per_kv * DH, 8 * rows * per_kv * DH
             ),
             name="attention",
-        )(doc_ids, queries[0], keys[0], values[0], *kv_got, *more)
-        targets.append(target)
-
+        )(doc_ids, queries[0], keys[0], values[0], *kv_got)
+        for g in range(kv_dev)
+    ]
     for r in range(1, count):
         for g in range(groups):
             if r == 3 and g == groups - 1:
@@ -653,27 +710,18 @@
                     cost_estimate=cost(8 * N * width, 8 * N * width),
                     name="chain",
                 )(got[g][-1], f_parts[g], b_parts[g], dec[g])
-            pairs = [(r - 1, r), (count - r, count - r - 1)]
-            got[g].append(lax.ppermute(send[g], "ctx", pairs))
-
-    student = grads = None
+            if len(got[g]) < r:
+                pairs = [(r - 1, r), (count - r, count - r - 1)]
+                got[g].append(lax.ppermute(send[g], "ctx", pairs))
+
+    normed, grads = [], None
     for g in range(groups):
-        more = [] if student is None else [grads, student]
-        student, grads = pl.pallas_call(
+        more = [] if grads is None else [grads]
+        made, grads = pl.pallas_call(
             functools.partial(final_kernel, count, g, groups, loss_scale),
-            out_shape=(struct((rows, features), BF16), struct((groups + 1, width), F32)),
-            grid=(1,),
-            in_specs=[
-                *[whole(rows, width)] * 3,
-                chosen(N, g),
-                whole(rows, width),
-                pl.BlockSpec((1, width), lambda k, g=g: (0, g)),
-                whole(N, width),
-                whole(8, width),
-                *[whole(N + EXTRA, width)] * others,
-                *([whole(groups + 1, width), pl.BlockSpec(memory_space=pl.ANY)] if more else []),
-            ],
-            out_specs=(chosen(width, g), whole(groups + 1, width)),
+            out_shape=(struct((rows, width), BF16), struct((groups + 1, width), F32)),
+            in_specs=[VMEM] * (8 + others + len(more)),
+            out_specs=(VMEM,) * 2,
             scratch_shapes=[
                 pltpu.VMEM((N, width), BF16),
                 pltpu.VMEM((N + EXTRA, width), BF16),
@@ -683,12 +731,11 @@
                 pltpu.VMEM((8, width), F32),
                 pltpu.VMEM((8, width), F32),
             ],
-            input_output_aliases={9 + others: 0} if more else {},
             compiler_params=params(16),
             cost_estimate=cost(2 * rows * width * N, 20 * rows * width),
             name="final",
         )(
-            *local[g],
+            *local[g::groups],
             cmat,
             targets[g],
             gain.reshape(1, features),
@@ -697,6 +744,8 @@
             *got[g],
             *more,
         )
+        normed.append(made)
+    teacher, student = write(*targets), write(*normed)
     partner = exchange(grads, 1)
     if lax.axis_size("dp") == 2:
         grads = (grads + partner) + (exchange(grads, count) + exchange(grads, count + 1))

time: 66.8 us -> 62.1 us (0.930)
  starting transfers between devices: 23.2 us -> 20.4 us
  waiting for transfers between devices: 22.3 us -> 20.2 us
  Pallas kernels: 18.1 us -> 20.2 us
  local copies, waits for them, and re-layouts: 1.9 us -> 0.03 us
    ppermute x6 -> x5, waiting for transfers between devices: 3.45 us -> 10.5 us  [body(): got[g].append(lax.ppermute(send[g], 'ctx', pairs))]
    ppermute x6 -> x5, starting transfers between devices: 11.6 us -> 6.12 us  [body(): got[g].append(lax.ppermute(send[g], 'ctx', pairs))]
    pallas_call x2 -> x4, Pallas kernels: 1.78 us -> 6.08 us  [the longest x1 4.08 us: body(): pl.pallas_call(functools.partial(local_kernel, count, groups), out_shape=...]
    ppermute x4, waiting for transfers between devices: 6.86 us -> 2.92 us  [exchange(): return lax.ppermute(part, axes, [(d, d ^ shift) for d in range(size)])]
    ppermute x2, waiting for transfers between devices: 6.89 us -> 3.15 us  [the longest x1 2.87 us: body(): far = lax.ppermute(send[-1], 'ctx', inward + outward)]
    ppermute x2, starting transfers between devices: 4.47 us -> 6.39 us  [the longest x1 6 us: body(): near = lax.ppermute(kv, 'ctx', inward + outward)]
    unnamed x20 -> x12, local copies, waits for them, and re-layouts: 1.9 us -> 0.03 us
    pallas_call x2, Pallas kernels: 7.25 us -> 5.58 us  [body(): pl.pallas_call(functools.partial(attention_kernel, count, per_kv, stack,...]
  transfers between devices with their start and end apart: 15 -> 14, of which waited for: 9 -> 8; matrix products, arithmetic and copies ran while one was open for 0% -> 0% of each run, Pallas kernels for 17% -> 22%
where the time goes in v6:
time: 62.1 us; the launch traced here: 61.7 us
  starting transfers between devices  20.4 us (33%)
  Pallas kernels  20.2 us (33%)
  waiting for transfers between devices  20.2 us (33%)
  between operations  0.87 us (1%)
    ppermute x5, waiting for transfers between devices, body(): got[g].append(lax.ppermute(send[g], 'ctx', pairs))  10.5 us
    ppermute x5, starting transfers between devices, body(): got[g].append(lax.ppermute(send[g], 'ctx', pairs))  6.12 us
    ppermute x1, starting transfers between devices, body(): near = lax.ppermute(kv, 'ctx', inward + outward)  6 us
    pallas_call x2, Pallas kernels, body(): pl.pallas_call(functools.partial(attention_kernel, count, per_kv, stack,...  5.58 us
    ppermute x4, starting transfers between devices, exchange(): return lax.ppermute(part, axes, [(d, d ^ shift) for d in range(size)])  5.24 us
    pallas_call x1, Pallas kernels, body(): pl.pallas_call(functools.partial(opening_kernel, count, groups), out_shap...  4.3 us
    pallas_call x1, Pallas kernels, body(): pl.pallas_call(functools.partial(local_kernel, count, groups), out_shape=...  4.08 us
    ppermute x1, waiting for transfers between devices, body(): farther = lax.ppermute(beyond, 'ctx', outward)  3.62 us
  transfers between devices with their start and end apart: 14, of which 8 were waited for; matrix products, arithmetic and copies ran while one was open for 0% of the time, Pallas kernels for 22%

profile of v6, /device:TPU:0, one launch (start us, length us, event | category | flops | bytes accessed | tf_op | source)
XLA Modules:
  0.0 61.7 jit_solution(5284974696469651939)
XLA Ops:
  0.6 4.3 %opening.1 = (bf16[256,512]{1,0:T(8,128)(2,1)S(1)}, f32[32,256]{1,0:T(8,128)S(1)}, bf16[256,1024]{1,0:T(8,128)(2,1)S(1)}, bf16[256,1024]{1,0:T(8,128)(2,1)S(1)},...) custom-call(s32[1,1024]{1,0:T(1,128)} %docs_ref.7, ...), custom_call_target="tpu_custom_call" | custom-call | flops 268435456 | bytes 4194304 | tf_op jit(solution)/shard_map/opening/pallas_call | solution.py:594
  4.9 0.7 %collective-permute-start = (bf16[256,512]{1,0:T(8,128)(2,1)S(1)}, bf16[256,512]{1,0:T(8,128)(2,1)S(1)}, u32[]{:S(2)}, u32[]{:S(2)}) collective-permute-start(bf16[256,512]{1,0:T(8,128)(2,1)S(1)} %get-tuple-element.38), channel_id=1, source_target_pairs={{4,8},{8,4},{5,9},{9,5},{6,10},{10,6},{7,11},{11,7},{20,24},{24,20... | collective-permute-start | bytes 786440 | tf_op jit(solution)/shard_map/ppermute | solution.py:654
  5.6 6.0 %collective-permute-start.3 = (bf16[256,512]{1,0:T(8,128)(2,1)S(1)}, bf16[256,512]{1,0:T(8,128)(2,1)S(1)}, u32[]{:S(2)}, u32[]{:S(2)}) collective-permute-start(bf16[256,512]{1,0:T(8,128)(2,1)S(1)} %get-tuple-element.38), channel_id=1, source_target_pairs={{0,4},{12,8},{4,0},{8,12},{1,5},{13,9},{5,1},{9,13},{2,6},{14,10},... | collective-permute-start | bytes 786440 | tf_op jit(solution)/shard_map/ppermute | solution.py:653
  11.6 1.9 %collective-permute-start.6 = (bf16[144,1024]{1,0:T(8,128)(2,1)S(1)}, bf16[144,1024]{1,0:T(8,128)(2,1)S(1)}, u32[]{:S(2)}, u32[]{:S(2)}) collective-permute-start(bf16[144,1024]{1,0:T(8,128)(2,1)S(1)} %get-tuple-element.58), channel_id=1, source_target_pairs={{0,4},{12,8},{1,5},{13,9},{2,6},{14,10},{3,7},{15,11},{16,20},{28,... | collective-permute-start | bytes 884744 | tf_op jit(solution)/shard_map/ppermute | solution.py:715
  13.6 4.1 %local.1 = (f32[256,1024]{1,0:T(8,128)S(1)}, f32[256,1024]{1,0:T(8,128)S(1)}, f32[256,1024]{1,0:T(8,128)S(1)}, f32[256,1024]{1,0:T(8,128)S(1)}, f32[256,1024]{1,0:T(8,128)S(1)}, /*index=5*/f32[256,1024]{1,0:T(8,128)S(1)}) custom-call(s32[1,1024]{1,0:T(1,128)} %docs_ref.7, bf16[256,2048]{1,0:T(8,128)(2,1)} %bitcast.32, bf16[256,2048]{1,0:T(8,128)(2,1)} %bitcast.33, ...), custom_call_target="tpu_custom_call" | custom-call | flops 134217728 | bytes 8388608 | tf_op jit(solution)/shard_map/local/pallas_call | solution.py:630
  17.7 0.0 collective-permute-done.kv_ref.refs_1_
  17.7 0.4 collective-permute-start.1
  18.1 0.3 collective-permute-done.3.refs_0_
  18.4 0.7 %collective-permute-start.4 = (bf16[256,512]{1,0:T(8,128)(2,1)S(1)}, bf16[256,512]{1,0:T(8,128)(2,1)S(1)}, u32[]{:S(2)}, u32[]{:S(2)}) collective-permute-start(bf16[256,512]{1,0:T(8,128)(2,1)S(1)} %collective-permute-done.3.refs_0_), channel_id=1, source_target_pairs={{4,8},{8,4},{5,9},{9,5},{6,10},{10,6},{7,11},{11,7},{20,24},{24,20... | collective-permute-start | bytes 786440 | tf_op jit(solution)/shard_map/ppermute | solution.py:656
  19.1 5.6 %collective-permute-done.6.got_ref.refs_0_ = bf16[144,1024]{1,0:T(8,128)(2,1)S(1)} collective-permute-done((bf16[144,1024]{1,0:T(8,128)(2,1)S(1)}, bf16[144,1024]{1,0:T(8,128)(2,1)S(1)}, u32[]{:S(2)}, u32[]{:S(2)}) %collective-permute-start.6) | collective-permute-done | bytes 294944 | tf_op jit(solution)/shard_map/ppermute | solution.py:715
  24.7 0.7 %collective-permute-start.7 = (bf16[144,1024]{1,0:T(8,128)(2,1)S(1)}, bf16[144,1024]{1,0:T(8,128)(2,1)S(1)}, u32[]{:S(2)}, u32[]{:S(2)}) collective-permute-start(bf16[144,1024]{1,0:T(8,128)(2,1)S(1)} %chain.5), channel_id=1, source_target_pairs={{4,8},{8,4},{5,9},{9,5},{6,10},{10,6},{7,11},{11,7},{20,24},{24,20... | collective-permute-start | bytes 884744 | tf_op jit(solution)/shard_map/ppermute | solution.py:715
  25.4 0.0 collective-permute-done.4.refs_2_
  25.4 1.3 %collective-permute-start.5 = (bf16[256,512]{1,0:T(8,128)(2,1)S(1)}, bf16[256,512]{1,0:T(8,128)(2,1)S(1)}, u32[]{:S(2)}, u32[]{:S(2)}) collective-permute-start(bf16[256,512]{1,0:T(8,128)(2,1)S(1)} %collective-permute-done.4.refs_2_), channel_id=1, source_target_pairs={{4,0},{8,12},{5,1},{9,13},{6,2},{10,14},{7,3},{11,15},{20,16},{24,... | collective-permute-start | bytes 786440 | tf_op jit(solution)/shard_map/ppermute | solution.py:668
  26.7 2.9 %collective-permute-done.1.got_ref.refs_3_.refs_0_ = bf16[144,1024]{1,0:T(8,128)(2,1)S(1)} collective-permute-done((bf16[144,1024]{1,0:T(8,128)(2,1)S(1)}, bf16[144,1024]{1,0:T(8,128)(2,1)S(1)}, u32[]{:S(2)}, u32[]{:S(2)}) %collective-permute-start.1) | collective-permute-done | bytes 294944 | tf_op jit(solution)/shard_map/ppermute | solution.py:666
  29.6 0.0 copy-start
  29.6 0.0 copy-start.1
  29.6 0.8 %collective-permute-start.2 = (bf16[144,1024]{1,0:T(8,128)(2,1)S(1)}, bf16[144,1024]{1,0:T(8,128)(2,1)S(1)}, u32[]{:S(2)}, u32[]{:S(2)}) collective-permute-start(bf16[144,1024]{1,0:T(8,128)(2,1)S(1)} %chain.4), channel_id=1, source_target_pairs={{4,8},{8,4},{5,9},{9,5},{6,10},{10,6},{7,11},{11,7},{20,24},{24,20... | collective-permute-start | bytes 884744 | tf_op jit(solution)/shard_map/ppermute | solution.py:715
  30.4 0.0 collective-permute-done.7.got_ref.refs_1_
  30.4 0.0 copy-start.4
  30.4 1.3 %collective-permute-start.8 = (bf16[144,1024]{1,0:T(8,128)(2,1)S(1)}, bf16[144,1024]{1,0:T(8,128)(2,1)S(1)}, u32[]{:S(2)}, u32[]{:S(2)}) collective-permute-start(bf16[144,1024]{1,0:T(8,128)(2,1)S(1)} %chain.6), channel_id=1, source_target_pairs={{8,12},{4,0},{9,13},{5,1},{10,14},{6,2},{11,15},{7,3},{24,28},{20,... | collective-permute-start | bytes 884744 | tf_op jit(solution)/shard_map/ppermute | solution.py:715
  31.7 3.6 %collective-permute-done.5.refs_4_ = bf16[256,512]{1,0:T(8,128)(2,1)S(1)} collective-permute-done((bf16[256,512]{1,0:T(8,128)(2,1)S(1)}, bf16[256,512]{1,0:T(8,128)(2,1)S(1)}, u32[]{:S(2)}, u32[]{:S(2)}) %collective-permute-start.5) | collective-permute-done | bytes 262176 | tf_op jit(solution)/shard_map/ppermute | solution.py:668
  35.3 0.0 copy-done
  35.4 0.0 copy-done.1
  35.4 0.0 copy-done.2
  35.4 0.0 copy-done.4
  35.4 2.8 %attention.2.refs_0_.teacher_ref = bf16[256,1024]{1,0:T(8,128)(2,1)S(1)} custom-call(s32[1,1024]{1,0:T(1,128)S(1)} %copy-done.4, bf16[256,2048]{1,0:T(8,128)(2,1)S(1)} %bitcast.18, bf16[256,256]{1,0:T(8,128)(2,1)S(1)} %bitcast.21, bf16[256,256]{1,0:T(8,128)(2,1)S(1)} %bitcast.24, bf16[256,512]{1,0:T(8,128)(2,1)S(1)} %collective-permute-done.3.refs_0_, ...), custom_call_target="tpu_custom_call" | custom-call | flops 603979776 | bytes 2097152 | tf_op jit(solution)/shard_map/attention/pallas_call | solution.py:679
  38.2 0.0 collective-permute-done.2.got_ref.refs_1_
  38.2 0.0 copy-start.3
  38.2 0.0 copy-start.5
  38.2 1.4 %collective-permute-start.9 = (bf16[144,1024]{1,0:T(8,128)(2,1)S(1)}, bf16[144,1024]{1,0:T(8,128)(2,1)S(1)}, u32[]{:S(2)}, u32[]{:S(2)}) collective-permute-start(bf16[144,1024]{1,0:T(8,128)(2,1)S(1)} %chain.7), channel_id=1, source_target_pairs={{8,12},{4,0},{9,13},{5,1},{10,14},{6,2},{11,15},{7,3},{24,28},{20,... | collective-permute-start | bytes 884744 | tf_op jit(solution)/shard_map/ppermute | solution.py:715
  39.7 2.8 %attention.3.refs_1_.teacher_ref = bf16[256,1024]{1,0:T(8,128)(2,1)S(1)} custom-call(s32[1,1024]{1,0:T(1,128)S(1)} %copy-done.4, bf16[256,2048]{1,0:T(8,128)(2,1)S(1)} %bitcast.19, bf16[256,256]{1,0:T(8,128)(2,1)S(1)} %bitcast.22, bf16[256,256]{1,0:T(8,128)(2,1)S(1)} %bitcast.25, bf16[256,512]{1,0:T(8,128)(2,1)S(1)} %collective-permute-done.3.refs_0_, ...), custom_call_target="tpu_custom_call" | custom-call | flops 603979776 | bytes 2097152 | tf_op jit(solution)/shard_map/attention/pallas_call | solution.py:679
  42.5 0.0 collective-permute-done.8.refs_2_
  42.5 0.0 copy-done.3
  42.5 0.0 copy-done.5
  42.5 1.8 %final.2 = (bf16[256,1024]{1,0:T(8,128)(2,1)S(1)}, f32[3,1024]{1,0:T(4,128)S(1)}) custom-call(f32[256,1024]{1,0:T(8,128)S(1)} %get-tuple-element.53.pre_ref, f32[256,1024]{1,0:T(8,128)S(1)} %get-tuple-element.54.reach_ref, f32[256,1024]{1,0:T(8,128)S(1)} %get-tuple-element.55.sx_ref, bf16[256,256]{1,0:T(8,128)(2,1)S(1)} %bitcast.27, ...), custom_call_target="tpu_custom_call" | custom-call | flops 67108864 | bytes 5242880 | tf_op jit(solution)/shard_map/final/pallas_call | solution.py:720
  44.3 4.9 %collective-permute-done.9.refs_2_ = bf16[144,1024]{1,0:T(8,128)(2,1)S(1)} collective-permute-done((bf16[144,1024]{1,0:T(8,128)(2,1)S(1)}, bf16[144,1024]{1,0:T(8,128)(2,1)S(1)}, u32[]{:S(2)}, u32[]{:S(2)}) %collective-permute-start.9) | collective-permute-done | bytes 294944 | tf_op jit(solution)/shard_map/ppermute | solution.py:715
  49.2 1.8 %final.3 = (bf16[256,1024]{1,0:T(8,128)(2,1)S(1)}, f32[3,1024]{1,0:T(4,128)S(1)}) custom-call(f32[256,1024]{1,0:T(8,128)S(1)} %get-tuple-element.61.pre_ref, f32[256,1024]{1,0:T(8,128)S(1)} %get-tuple-element.62.reach_ref, f32[256,1024]{1,0:T(8,128)S(1)} %get-tuple-element.63.sx_ref, bf16[256,256]{1,0:T(8,128)(2,1)S(1)} %bitcast.28, ...), custom_call_target="tpu_custom_call" | custom-call | flops 67108864 | bytes 5242880 | tf_op jit(solution)/shard_map/final/pallas_call | solution.py:720
  51.0 0.6 collective-permute-start.12
  51.5 1.1 %collective-permute-start.11 = (f32[3,1024]{1,0:T(4,128)S(1)}, f32[3,1024]{1,0:T(4,128)S(1)}, u32[]{:S(2)}, u32[]{:S(2)}) collective-permute-start(f32[3,1024]{1,0:T(4,128)S(1)} %get-tuple-element.67), channel_id=1, source_target_pairs={{0,16},{4,20},{8,24},{12,28},{16,0},{20,4},{24,8},{28,12},{1,17},{... | collective-permute-start | bytes 36872 | tf_op jit(solution)/shard_map/ppermute | solution.py:545
  52.6 1.9 %collective-permute-start.10 = (f32[3,1024]{1,0:T(4,128)S(1)}, f32[3,1024]{1,0:T(4,128)S(1)}, u32[]{:S(2)}, u32[]{:S(2)}) collective-permute-start(f32[3,1024]{1,0:T(4,128)S(1)} %get-tuple-element.67), channel_id=1, source_target_pairs={{0,4},{4,0},{8,12},{12,8},{16,20},{20,16},{24,28},{28,24},{1,5},{5... | collective-permute-start | bytes 36872 | tf_op jit(solution)/shard_map/ppermute | solution.py:545
  54.5 1.1 %collective-permute-done.12 = f32[3,1024]{1,0:T(4,128)S(1)} collective-permute-done((f32[3,1024]{1,0:T(4,128)S(1)}, f32[3,1024]{1,0:T(4,128)S(1)}, u32[]{:S(2)}, u32[]{:S(2)}) %collective-permute-start.12) | collective-permute-done | bytes 12320 | tf_op jit(solution)/shard_map/ppermute | solution.py:545
  55.7 0.0 collective-permute-done.11
  55.7 0.7 %collective-permute-done.10 = f32[3,1024]{1,0:T(4,128)S(1)} collective-permute-done((f32[3,1024]{1,0:T(4,128)S(1)}, f32[3,1024]{1,0:T(4,128)S(1)}, u32[]{:S(2)}, u32[]{:S(2)}) %collective-permute-start.10) | collective-permute-done | bytes 12320 | tf_op jit(solution)/shard_map/ppermute | solution.py:545
  56.4 1.7 %collective-permute-start.13 = (f32[3,1024]{1,0:T(4,128)S(1)}, f32[3,1024]{1,0:T(4,128)S(1)}, u32[]{:S(2)}, u32[]{:S(2)}) collective-permute-start(f32[3,1024]{1,0:T(4,128)S(1)} %add_add_fusion.a_ref), channel_id=1, source_target_pairs={{0,8},{4,12},{8,0},{12,4},{16,24},{20,28},{24,16},{28,20},{1,9},{5... | collective-permute-start | bytes 36872 | tf_op jit(solution)/shard_map/ppermute | solution.py:545
  58.1 1.0 %writing.2 = bf16[256,2048]{1,0:T(8,128)(2,1)} custom-call(bf16[256,1024]{1,0:T(8,128)(2,1)S(1)} %attention.2.refs_0_.teacher_ref, bf16[256,1024]{1,0:T(8,128)(2,1)S(1)} %attention.3.refs_1_.teacher_ref), custom_call_target="tpu_custom_call" | custom-call | bytes 2097152 | tf_op jit(solution)/shard_map/writing/pallas_call | solution.py:581
  59.1 1.0 %writing.3 = bf16[256,2048]{1,0:T(8,128)(2,1)} custom-call(bf16[256,1024]{1,0:T(8,128)(2,1)S(1)} %get-tuple-element.60.refs_0_, bf16[256,1024]{1,0:T(8,128)(2,1)S(1)} %get-tuple-element.66.refs_1_), custom_call_target="tpu_custom_call" | custom-call | bytes 2097152 | tf_op jit(solution)/shard_map/writing/pallas_call | solution.py:581
  60.1 1.0 %collective-permute-done.13.b_ref = f32[3,1024]{1,0:T(4,128)S(1)} collective-permute-done((f32[3,1024]{1,0:T(4,128)S(1)}, f32[3,1024]{1,0:T(4,128)S(1)}, u32[]{:S(2)}, u32[]{:S(2)}) %collective-permute-start.13) | collective-permute-done | bytes 12320 | tf_op jit(solution)/shard_map/ppermute | solution.py:545
  61.1 0.6 closing.1
  (7 shorter events, 0.1 us)
Async XLA Ops:
  4.9 12.7 %collective-permute-start = (bf16[256,512]{1,0:T(8,128)(2,1)S(1)}, bf16[256,512]{1,0:T(8,128)(2,1)S(1)}, u32[]{:S(2)}, u32[]{:S(2)}) collective-permute-start(bf16[256,512]{1,0:T(8,128)(2,1)S(1)} %get-tuple-element.38), channel_id=1, source_target_pairs={{4,8},{8,4},{5,9},{9,5},{6,10},{10,6},{7,11},{11,7},{20,24},{24,20... | collective-permute-start | bytes 786440 | tf_op jit(solution)/shard_map/ppermute | solution.py:654
  5.6 12.8 %collective-permute-start.3 = (bf16[256,512]{1,0:T(8,128)(2,1)S(1)}, bf16[256,512]{1,0:T(8,128)(2,1)S(1)}, u32[]{:S(2)}, u32[]{:S(2)}) collective-permute-start(bf16[256,512]{1,0:T(8,128)(2,1)S(1)} %get-tuple-element.38), channel_id=1, source_target_pairs={{0,4},{12,8},{4,0},{8,12},{1,5},{13,9},{5,1},{9,13},{2,6},{14,10},... | collective-permute-start | bytes 786440 | tf_op jit(solution)/shard_map/ppermute | solution.py:653
  11.6 13.1 %collective-permute-start.6 = (bf16[144,1024]{1,0:T(8,128)(2,1)S(1)}, bf16[144,1024]{1,0:T(8,128)(2,1)S(1)}, u32[]{:S(2)}, u32[]{:S(2)}) collective-permute-start(bf16[144,1024]{1,0:T(8,128)(2,1)S(1)} %get-tuple-element.58), channel_id=1, source_target_pairs={{0,4},{12,8},{1,5},{13,9},{2,6},{14,10},{3,7},{15,11},{16,20},{28,... | collective-permute-start | bytes 884744 | tf_op jit(solution)/shard_map/ppermute | solution.py:715
  17.7 11.8 %collective-permute-start.1 = (bf16[144,1024]{1,0:T(8,128)(2,1)S(1)}, bf16[144,1024]{1,0:T(8,128)(2,1)S(1)}, u32[]{:S(2)}, u32[]{:S(2)}) collective-permute-start(bf16[144,1024]{1,0:T(8,128)(2,1)S(1)} %merge.1), channel_id=1, source_target_pairs={{0,4},{12,8},{4,0},{8,12},{1,5},{13,9},{5,1},{9,13},{2,6},{14,10},... | collective-permute-start | bytes 884744 | tf_op jit(solution)/shard_map/ppermute | solution.py:666
  18.4 7.0 %collective-permute-start.4 = (bf16[256,512]{1,0:T(8,128)(2,1)S(1)}, bf16[256,512]{1,0:T(8,128)(2,1)S(1)}, u32[]{:S(2)}, u32[]{:S(2)}) collective-permute-start(bf16[256,512]{1,0:T(8,128)(2,1)S(1)} %collective-permute-done.3.refs_0_), channel_id=1, source_target_pairs={{4,8},{8,4},{5,9},{9,5},{6,10},{10,6},{7,11},{11,7},{20,24},{24,20... | collective-permute-start | bytes 786440 | tf_op jit(solution)/shard_map/ppermute | solution.py:656
  24.7 5.7 %collective-permute-start.7 = (bf16[144,1024]{1,0:T(8,128)(2,1)S(1)}, bf16[144,1024]{1,0:T(8,128)(2,1)S(1)}, u32[]{:S(2)}, u32[]{:S(2)}) collective-permute-start(bf16[144,1024]{1,0:T(8,128)(2,1)S(1)} %chain.5), channel_id=1, source_target_pairs={{4,8},{8,4},{5,9},{9,5},{6,10},{10,6},{7,11},{11,7},{20,24},{24,20... | collective-permute-start | bytes 884744 | tf_op jit(solution)/shard_map/ppermute | solution.py:715
  25.4 10.0 %collective-permute-start.5 = (bf16[256,512]{1,0:T(8,128)(2,1)S(1)}, bf16[256,512]{1,0:T(8,128)(2,1)S(1)}, u32[]{:S(2)}, u32[]{:S(2)}) collective-permute-start(bf16[256,512]{1,0:T(8,128)(2,1)S(1)} %collective-permute-done.4.refs_2_), channel_id=1, source_target_pairs={{4,0},{8,12},{5,1},{9,13},{6,2},{10,14},{7,3},{11,15},{20,16},{24,... | collective-permute-start | bytes 786440 | tf_op jit(solution)/shard_map/ppermute | solution.py:668
  29.6 5.8 %copy-start = (bf16[1,256,2048]{2,1,0:T(8,128)(2,1)S(1)}, bf16[1,256,2048]{2,1,0:T(8,128)(2,1)}, u32[]{:S(2)}) copy-start(bf16[1,256,2048]{2,1,0:T(8,128)(2,1)} %param.13) | copy-start | bytes 3145732
  29.6 5.8 %copy-start.1 = (bf16[1,256,256]{2,1,0:T(8,128)(2,1)S(1)}, bf16[1,256,256]{2,1,0:T(8,128)(2,1)}, u32[]{:S(2)}) copy-start(bf16[1,256,256]{2,1,0:T(8,128)(2,1)} %param.14) | copy-start | bytes 393220
  29.6 5.8 %copy-start.2 = (bf16[1,256,256]{2,1,0:T(8,128)(2,1)S(1)}, bf16[1,256,256]{2,1,0:T(8,128)(2,1)}, u32[]{:S(2)}) copy-start(bf16[1,256,256]{2,1,0:T(8,128)(2,1)} %param.15) | copy-start | bytes 393220
  29.6 8.6 %collective-permute-start.2 = (bf16[144,1024]{1,0:T(8,128)(2,1)S(1)}, bf16[144,1024]{1,0:T(8,128)(2,1)S(1)}, u32[]{:S(2)}, u32[]{:S(2)}) collective-permute-start(bf16[144,1024]{1,0:T(8,128)(2,1)S(1)} %chain.4), channel_id=1, source_target_pairs={{4,8},{8,4},{5,9},{9,5},{6,10},{10,6},{7,11},{11,7},{20,24},{24,20... | collective-permute-start | bytes 884744 | tf_op jit(solution)/shard_map/ppermute | solution.py:715
  30.4 5.0 %copy-start.4 = (s32[1,1024]{1,0:T(1,128)S(1)}, s32[1,1024]{1,0:T(1,128)}, u32[]{:S(2)}) copy-start(s32[1,1024]{1,0:T(1,128)} %docs_ref.7) | copy-start | bytes 12292
  30.4 12.0 %collective-permute-start.8 = (bf16[144,1024]{1,0:T(8,128)(2,1)S(1)}, bf16[144,1024]{1,0:T(8,128)(2,1)S(1)}, u32[]{:S(2)}, u32[]{:S(2)}) collective-permute-start(bf16[144,1024]{1,0:T(8,128)(2,1)S(1)} %chain.6), channel_id=1, source_target_pairs={{8,12},{4,0},{9,13},{5,1},{10,14},{6,2},{11,15},{7,3},{24,28},{20,... | collective-permute-start | bytes 884744 | tf_op jit(solution)/shard_map/ppermute | solution.py:715
  38.2 4.3 %copy-start.3 = (bf16[1,256,256]{2,1,0:T(8,128)(2,1)S(1)}, bf16[1,256,256]{2,1,0:T(8,128)(2,1)}, u32[]{:S(2)}) copy-start(bf16[1,256,256]{2,1,0:T(8,128)(2,1)} %param.20) | copy-start | bytes 393220
  38.2 4.3 %copy-start.5 = (f32[2048]{0:T(1024)S(1)}, f32[2048]{0:T(1024)}, u32[]{:S(2)}) copy-start(f32[2048]{0:T(1024)} %param.25) | copy-start | bytes 24580
  38.2 10.9 %collective-permute-start.9 = (bf16[144,1024]{1,0:T(8,128)(2,1)S(1)}, bf16[144,1024]{1,0:T(8,128)(2,1)S(1)}, u32[]{:S(2)}, u32[]{:S(2)}) collective-permute-start(bf16[144,1024]{1,0:T(8,128)(2,1)S(1)} %chain.7), channel_id=1, source_target_pairs={{8,12},{4,0},{9,13},{5,1},{10,14},{6,2},{11,15},{7,3},{24,28},{20,... | collective-permute-start | bytes 884744 | tf_op jit(solution)/shard_map/ppermute | solution.py:715
  51.0 4.7 %collective-permute-start.12 = (f32[3,1024]{1,0:T(4,128)S(1)}, f32[3,1024]{1,0:T(4,128)S(1)}, u32[]{:S(2)}, u32[]{:S(2)}) collective-permute-start(f32[3,1024]{1,0:T(4,128)S(1)} %get-tuple-element.67), channel_id=1, source_target_pairs={{0,20},{4,16},{8,28},{12,24},{16,4},{20,0},{24,12},{28,8},{1,21},{... | collective-permute-start | bytes 36872 | tf_op jit(solution)/shard_map/ppermute | solution.py:545
  51.5 4.2 %collective-permute-start.11 = (f32[3,1024]{1,0:T(4,128)S(1)}, f32[3,1024]{1,0:T(4,128)S(1)}, u32[]{:S(2)}, u32[]{:S(2)}) collective-permute-start(f32[3,1024]{1,0:T(4,128)S(1)} %get-tuple-element.67), channel_id=1, source_target_pairs={{0,16},{4,20},{8,24},{12,28},{16,0},{20,4},{24,8},{28,12},{1,17},{... | collective-permute-start | bytes 36872 | tf_op jit(solution)/shard_map/ppermute | solution.py:545
  52.6 3.8 %collective-permute-start.10 = (f32[3,1024]{1,0:T(4,128)S(1)}, f32[3,1024]{1,0:T(4,128)S(1)}, u32[]{:S(2)}, u32[]{:S(2)}) collective-permute-start(f32[3,1024]{1,0:T(4,128)S(1)} %get-tuple-element.67), channel_id=1, source_target_pairs={{0,4},{4,0},{8,12},{12,8},{16,20},{20,16},{24,28},{28,24},{1,5},{5... | collective-permute-start | bytes 36872 | tf_op jit(solution)/shard_map/ppermute | solution.py:545
  56.4 4.7 %collective-permute-start.13 = (f32[3,1024]{1,0:T(4,128)S(1)}, f32[3,1024]{1,0:T(4,128)S(1)}, u32[]{:S(2)}, u32[]{:S(2)}) collective-permute-start(f32[3,1024]{1,0:T(4,128)S(1)} %add_add_fusion.a_ref), channel_id=1, source_target_pairs={{0,8},{4,12},{8,0},{12,4},{16,24},{20,28},{24,16},{28,20},{1,9},{5... | collective-permute-start | bytes 36872 | tf_op jit(solution)/shard_map/ppermute | solution.py:545

commit v7 on v6

--- a/solution.py
+++ b/solution.py
@@ -47,8 +47,7 @@
 
 
 def spread(v, matrix):
-    hi, lo = parts(v)
-    return dot_tn(hi, matrix) + dot_tn(lo, matrix)
+    return dot_tn(jnp.concatenate(parts(v), axis=0), jnp.concatenate([matrix, matrix], axis=0))
 
 
 def doc_row(docs_ref, block, stretch):
@@ -106,36 +105,21 @@
     count,
     groups,
     docs_ref,
-    k_ref,
-    v_ref,
     x_ref,
     b_ref,
     dt_ref,
     bias_ref,
     log_ref,
-    kv_ref,
     ec_ref,
     *outs,
 ):
     xw_refs, dec_refs, f_refs, b_refs, send_refs = (
         outs[k * groups : (k + 1) * groups] for k in range(5)
     )
-    x_here, x_sem = outs[5 * groups :]
     heads, rows = dt_ref.shape
     stretch = rows // 2
     width = x_ref.shape[1] // groups
-    kv_width = k_ref.shape[1]
     index = lax.axis_index("ctx")
-    loads_x = [
-        pltpu.make_async_copy(
-            x_ref.at[:, pl.ds(g * width, width)], x_here.at[g], x_sem.at[g]
-        )
-        for g in range(groups)
-    ]
-    for load in loads_x:
-        load.start()
-    kv_ref[:, :kv_width] = k_ref[...]
-    kv_ref[:, kv_width:] = v_ref[...]
     triangle = jnp.where(lower_triangle(stretch), 1.0, 0.0)
     slope = jnp.exp(as_column(log_ref[...]))
     bias = as_column(bias_ref[...])
@@ -166,14 +150,14 @@
         same = jnp.where(as_column(row) == last.astype(F32), 1.0, 0.0)
         projs.append((b_ref[sl, :].astype(F32) * same).astype(BF16))
     for g in range(groups):
+        cols = slice(g * width, (g + 1) * width)
         matrix = spread_matrix(heads, width, g * (heads // groups))
         wide = spread(ends, matrix)
         dec_refs[g][...] = wide
         sums = []
-        loads_x[g].wait()
         for half in range(2):
             sl = slice(half * stretch, (half + 1) * stretch)
-            xw = (x_here[g, sl, :].astype(F32) * spread(loads[half], matrix)).astype(BF16)
+            xw = (x_ref[sl, cols].astype(F32) * spread(loads[half], matrix)).astype(BF16)
             xw_refs[g][sl, :] = xw
             sums.append(dot_tn(projs[half][:, g * N : (g + 1) * N], xw) * wide[2 + half : 3 + half])
         f_refs[g][...] = sums[0].astype(BF16)
@@ -186,6 +170,12 @@
         @pl.when(index != 0)
         def _():
             put_composite(send_refs[g], wide[1:2] * sums[0] + sums[1], wide[0:1] * wide[1:2])
+
+
+def pack_kernel(k_ref, v_ref, kv_ref):
+    width = k_ref.shape[1]
+    kv_ref[:, :width] = k_ref[...]
+    kv_ref[:, width:] = v_ref[...]
 
 
 def chain_kernel(count, stage, got_ref, f_ref, b_ref, dec_ref, send_ref):
@@ -510,12 +500,15 @@
     matrix = jnp.where(row == lane // P_SIZE + g * (width // P_SIZE), 1.0, 0.0).astype(BF16)
     hi, lo = parts(skip_acc[...])
     by_head = jnp.sum(dot_nt(hi, matrix) + dot_nt(lo, matrix), axis=0, keepdims=True)
-    grad_ref[...] = jnp.zeros_like(grad_ref)
+    by_lane = jnp.sum(gain_acc[...], axis=0, keepdims=True)
     if g:
-        grad_ref[:g, :] = before[:g, :]
-        by_head += before[groups : groups + 1, :tile]
-    grad_ref[g : g + 1, :] = jnp.sum(gain_acc[...], axis=0, keepdims=True)
-    grad_ref[groups : groups + 1, :tile] = by_head
+        by_head += before[0, groups : groups + 1, :tile]
+    for d in range(grad_ref.shape[0]):
+        if g:
+            grad_ref[d, :g, :] = before[0, :g, :]
+        grad_ref[d, g : g + 1, :] = by_lane
+        grad_ref[d, groups : groups + 1, :] = jnp.zeros((1, width), F32)
+        grad_ref[d, groups : groups + 1, :tile] = by_head
 
 
 def writing_kernel(*refs):
@@ -531,18 +524,14 @@
         move.wait()
 
 
-def closing_kernel(a_ref, b_ref, gain_ref, skip_ref):
-    total = a_ref[...] + b_ref[...]
+def closing_kernel(all_ref, gain_ref, skip_ref):
+    total = all_ref[0]
+    for d in range(1, all_ref.shape[0]):
+        total += all_ref[d]
     groups, width = total.shape[0] - 1, total.shape[1]
     for g in range(groups):
         gain_ref[:, g * width : (g + 1) * width] = total[g : g + 1, :]
     skip_ref[...] = total[groups : groups + 1, : skip_ref.shape[1]]
-
-
-def exchange(part, shift):
-    axes = ("dp", "ctx")
-    size = lax.axis_size(axes)
-    return lax.ppermute(part, axes, [(d, d ^ shift) for d in range(size)])
 
 
 def body(
@@ -570,6 +559,7 @@
     width = features // groups
     length = doc_ids.shape[1]
     others = count - 1
+    members = lax.axis_size("dp") * count
     loss_scale = 1.0 / (lax.axis_size("dp") * count * rows)
     x, gate, bmat, cmat = inputs[0], gate_input[0], b_input[0], c_input[0]
     struct = jax.ShapeDtypeStruct
@@ -594,27 +584,20 @@
     outs = pl.pallas_call(
         functools.partial(opening_kernel, count, groups),
         out_shape=(
-            struct((rows, 2 * kv_dev * DH), BF16),
             struct((heads, rows), F32),
             *([struct((rows, width), BF16)] * groups),
             *([struct((8, width), F32)] * groups),
             *([state] * (2 * groups)),
             *([payload] * groups),
         ),
-        in_specs=[VMEM] * 3 + [pl.BlockSpec(memory_space=pl.ANY)] + [VMEM] * 4,
-        out_specs=(VMEM,) * (2 + 5 * groups),
-        scratch_shapes=[
-            pltpu.VMEM((groups, rows, width), BF16),
-            pltpu.SemaphoreType.DMA((groups,)),
-        ],
+        in_specs=[VMEM] * 6,
+        out_specs=(VMEM,) * (1 + 5 * groups),
         compiler_params=params(16),
         cost_estimate=cost(4 * rows * features * N, 8 * rows * features),
         name="opening",
     )(
         *in_hbm(
             doc_ids,
-            keys[0],
-            values[0],
             x,
             bmat,
             dt_raw[0].T,
@@ -622,10 +605,20 @@
             decay_log.reshape(1, heads),
         )
     )
-    kv, ec = outs[:2]
+    ec = outs[0]
     xw, dec, f_parts, b_parts, send = (
-        outs[2 + k * groups : 2 + (k + 1) * groups] for k in range(5)
+        outs[1 + k * groups : 1 + (k + 1) * groups] for k in range(5)
     )
+    key_part, value_part, _ = lax.optimization_barrier((keys[0], values[0], ec))
+    kv = pl.pallas_call(
+        pack_kernel,
+        out_shape=struct((rows, 2 * kv_dev * DH), BF16),
+        in_specs=[VMEM] * 2,
+        out_specs=VMEM,
+        compiler_params=params(4),
+        cost_estimate=cost(0, 8 * keys.size),
+        name="pack",
+    )(key_part, value_part)
 
     local = pl.pallas_call(
         functools.partial(local_kernel, count, groups),
@@ -698,8 +691,6 @@
     ]
     for r in range(1, count):
         for g in range(groups):
-            if r == 3 and g == groups - 1:
-                got[g][-1], targets[0] = lax.optimization_barrier((got[g][-1], targets[0]))
             if r > 1:
                 send[g] = pl.pallas_call(
                     functools.partial(chain_kernel, count, r - 1),
@@ -707,7 +698,7 @@
                     in_specs=[VMEM] * 4,
                     out_specs=VMEM,
                     compiler_params=params(4),
-                    cost_estimate=cost(8 * N * width, 8 * N * width),
+                    cost_estimate=cost(16384 * N * width, 8 * N * width),
                     name="chain",
                 )(got[g][-1], f_parts[g], b_parts[g], dec[g])
             if len(got[g]) < r:
@@ -719,7 +710,10 @@
         more = [] if grads is None else [grads]
         made, grads = pl.pallas_call(
             functools.partial(final_kernel, count, g, groups, loss_scale),
-            out_shape=(struct((rows, width), BF16), struct((groups + 1, width), F32)),
+            out_shape=(
+                struct((rows, width), BF16),
+                struct((members if g == groups - 1 else 1, groups + 1, width), F32),
+            ),
             in_specs=[VMEM] * (8 + others + len(more)),
             out_specs=(VMEM,) * 2,
             scratch_shapes=[
@@ -746,22 +740,15 @@
         )
         normed.append(made)
     teacher, student = write(*targets), write(*normed)
-    partner = exchange(grads, 1)
-    if lax.axis_size("dp") == 2:
-        grads = (grads + partner) + (exchange(grads, count) + exchange(grads, count + 1))
-    else:
-        grads = grads + partner
-    shifts = [1 << k for k in range(1, count.bit_length() - 1)]
-    for shift in shifts[:-1]:
-        grads = grads + exchange(grads, shift)
+    gathered = lax.all_to_all(grads, ("dp", "ctx"), 0, 0)
     grad_gain, grad_skip = pl.pallas_call(
         closing_kernel,
         out_shape=(struct((1, features), F32), struct((1, heads), F32)),
-        in_specs=[VMEM] * 2,
+        in_specs=[VMEM],
         out_specs=(VMEM,) * 2,
-        compiler_params=params(2),
+        compiler_params=params(4),
         name="closing",
-    )(grads, exchange(grads, shifts[-1]))
+    )(gathered)
     return (teacher[None], student[None], grad_gain[0], grad_skip[0])
 
 

time: 62.1 us -> 71.7 us (1.15)
  waiting for transfers between devices: 20.2 us -> 29 us
  starting transfers between devices: 20.4 us -> 21.5 us
    ppermute x5, waiting for transfers between devices: 10.5 us -> 2.3 us  [body(): got[g].append(lax.ppermute(send[g], 'ctx', pairs))]
    ppermute x1, waiting for transfers between devices: 3.62 us -> 11 us  [body(): farther = lax.ppermute(beyond, 'ctx', outward)]
    ppermute x1, waiting for transfers between devices: 0.28 us -> 6.63 us  [body(): near = lax.ppermute(kv, 'ctx', inward + outward)]
    ppermute x1, starting transfers between devices: 6 us -> 0.07 us  [body(): near = lax.ppermute(kv, 'ctx', inward + outward)]
    ppermute x5, starting transfers between devices: 6.12 us -> 11.9 us  [body(): got[g].append(lax.ppermute(send[g], 'ctx', pairs))]
    all_to_all x0 -> x1, waiting for transfers between devices: none -> 5.54 us  [body(): gathered = lax.all_to_all(grads, ('dp', 'ctx'), 0, 0)]
    ppermute x4 -> x0, starting transfers between devices: 5.24 us -> none  [exchange(): return lax.ppermute(part, axes, [(d, d ^ shift) for d in range(size)])]
    all_to_all x0 -> x1, starting transfers between devices: none -> 4.84 us  [body(): gathered = lax.all_to_all(grads, ('dp', 'ctx'), 0, 0)]
  transfers between devices with their start and end apart: 14 -> 11, of which waited for: 8 -> 6; matrix products, arithmetic and copies ran while one was open for 0% -> 0% of each run, Pallas kernels for 22% -> 19%
where the time goes in v7:
time: 71.7 us; the launch traced here: 71.2 us
  waiting for transfers between devices  29 us (40%)
  starting transfers between devices  21.5 us (30%)
  Pallas kernels  19.8 us (28%)
  between operations  0.91 us (1%)
    ppermute x5, starting transfers between devices, body(): got[g].append(lax.ppermute(send[g], 'ctx', pairs))  11.9 us
    ppermute x1, waiting for transfers between devices, body(): farther = lax.ppermute(beyond, 'ctx', outward)  11 us
    ppermute x1, waiting for transfers between devices, body(): near = lax.ppermute(kv, 'ctx', inward + outward)  6.63 us
    pallas_call x2, Pallas kernels, body(): pl.pallas_call(functools.partial(attention_kernel, count, per_kv, stack,...  5.58 us
    all_to_all x1, waiting for transfers between devices, body(): gathered = lax.all_to_all(grads, ('dp', 'ctx'), 0, 0)  5.54 us
    all_to_all x1, starting transfers between devices, body(): gathered = lax.all_to_all(grads, ('dp', 'ctx'), 0, 0)  4.84 us
    pallas_call x2, Pallas kernels, body(): pl.pallas_call(functools.partial(final_kernel, count, g, groups, loss_sca...  4.21 us
    pallas_call x1, Pallas kernels, body(): pl.pallas_call(functools.partial(local_kernel, count, groups), out_shape=...  4.19 us
  transfers between devices with their start and end apart: 11, of which 6 were waited for; matrix products, arithmetic and copies ran while one was open for 0% of the time, Pallas kernels for 19%

profile of v7, /device:TPU:0, one launch (start us, length us, event | category | flops | bytes accessed | tf_op | source)
XLA Modules:
  0.0 71.2 jit_solution(5342855726397203921)
XLA Ops:
  0.6 0.0 copy-start.2
  0.6 0.0 copy-start.3
  0.7 3.1 %opening.1 = (f32[32,256]{1,0:T(8,128)S(1)}, bf16[256,1024]{1,0:T(8,128)(2,1)S(1)}, bf16[256,1024]{1,0:T(8,128)(2,1)S(1)}, f32[8,1024]{1,0:T(8,128)S(1)}, f32[8,...) custom-call(s32[1,1024]{1,0:T(1,128)} %docs_ref.7, ...), custom_call_target="tpu_custom_call" | custom-call | flops 268435456 | bytes 4194304 | tf_op jit(solution)/shard_map/opening/pallas_call | solution.py:584
  3.8 0.0 copy-done.2
  3.8 0.0 copy-done.3
  3.8 0.7 collective-permute-start.1
  4.5 7.9 %collective-permute-start.5 = (bf16[144,1024]{1,0:T(8,128)(2,1)S(1)}, bf16[144,1024]{1,0:T(8,128)(2,1)S(1)}, u32[]{:S(2)}, u32[]{:S(2)}) collective-permute-start(bf16[144,1024]{1,0:T(8,128)(2,1)S(1)} %get-tuple-element.54), channel_id=1, source_target_pairs={{0,4},{12,8},{1,5},{13,9},{2,6},{14,10},{3,7},{15,11},{16,20},{28,... | collective-permute-start | bytes 884744 | tf_op jit(solution)/shard_map/ppermute | solution.py:706
  12.4 0.1 collective-permute-start
  12.5 4.2 %local.1 = (f32[256,1024]{1,0:T(8,128)S(1)}, f32[256,1024]{1,0:T(8,128)S(1)}, f32[256,1024]{1,0:T(8,128)S(1)}, f32[256,1024]{1,0:T(8,128)S(1)}, f32[256,1024]{1,0:T(8,128)S(1)}, /*index=5*/f32[256,1024]{1,0:T(8,128)S(1)}) custom-call(s32[1,1024]{1,0:T(1,128)} %docs_ref.7, bf16[256,2048]{1,0:T(8,128)(2,1)} %bitcast.32, bf16[256,2048]{1,0:T(8,128)(2,1)} %bitcast.33, ...), custom_call_target="tpu_custom_call" | custom-call | flops 134217728 | bytes 8388608 | tf_op jit(solution)/shard_map/local/pallas_call | solution.py:623
  16.7 0.0 collective-permute-done.1.kv_ref.refs_1_
  16.7 2.1 %collective-permute-start.3 = (bf16[144,1024]{1,0:T(8,128)(2,1)S(1)}, bf16[144,1024]{1,0:T(8,128)(2,1)S(1)}, u32[]{:S(2)}, u32[]{:S(2)}) collective-permute-start(bf16[144,1024]{1,0:T(8,128)(2,1)S(1)} %merge.1), channel_id=1, source_target_pairs={{0,4},{12,8},{4,0},{8,12},{1,5},{13,9},{5,1},{9,13},{2,6},{14,10},... | collective-permute-start | bytes 884744 | tf_op jit(solution)/shard_map/ppermute | solution.py:659
  18.8 6.6 %collective-permute-done.refs_0_ = bf16[256,512]{1,0:T(8,128)(2,1)S(1)} collective-permute-done((bf16[256,512]{1,0:T(8,128)(2,1)S(1)}, bf16[256,512]{1,0:T(8,128)(2,1)S(1)}, u32[]{:S(2)}, u32[]{:S(2)}) %collective-permute-start) | collective-permute-done | bytes 262176 | tf_op jit(solution)/shard_map/ppermute | solution.py:646
  25.4 0.7 collective-permute-start.2
  26.1 0.0 collective-permute-done.5.got_ref.refs_0_
  26.1 0.7 collective-permute-start.6
  26.8 3.4 %collective-permute-done.3.refs_3_.got_ref.refs_0_ = bf16[144,1024]{1,0:T(8,128)(2,1)S(1)} collective-permute-done((bf16[144,1024]{1,0:T(8,128)(2,1)S(1)}, bf16[144,1024]{1,0:T(8,128)(2,1)S(1)}, u32[]{:S(2)}, u32[]{:S(2)}) %collective-permute-start.3) | collective-permute-done | bytes 294944 | tf_op jit(solution)/shard_map/ppermute | solution.py:659
  30.3 0.7 collective-permute-start.8
  30.9 0.0 collective-permute-done.2.refs_2_
  30.9 1.3 %collective-permute-start.4 = (bf16[256,512]{1,0:T(8,128)(2,1)S(1)}, bf16[256,512]{1,0:T(8,128)(2,1)S(1)}, u32[]{:S(2)}, u32[]{:S(2)}) collective-permute-start(bf16[256,512]{1,0:T(8,128)(2,1)S(1)} %collective-permute-done.2.refs_2_), channel_id=1, source_target_pairs={{4,0},{8,12},{5,1},{9,13},{6,2},{10,14},{7,3},{11,15},{20,16},{24,... | collective-permute-start | bytes 786440 | tf_op jit(solution)/shard_map/ppermute | solution.py:661
  32.2 0.0 collective-permute-done.6.got_ref.refs_1_
  32.3 0.0 copy-start
  32.3 1.4 %collective-permute-start.7 = (bf16[144,1024]{1,0:T(8,128)(2,1)S(1)}, bf16[144,1024]{1,0:T(8,128)(2,1)S(1)}, u32[]{:S(2)}, u32[]{:S(2)}) collective-permute-start(bf16[144,1024]{1,0:T(8,128)(2,1)S(1)} %chain.5), channel_id=1, source_target_pairs={{8,12},{4,0},{9,13},{5,1},{10,14},{6,2},{11,15},{7,3},{24,28},{20,... | collective-permute-start | bytes 884744 | tf_op jit(solution)/shard_map/ppermute | solution.py:706
  33.7 0.0 collective-permute-done.8.got_ref.refs_1_
  33.7 0.0 copy-start.4
  33.8 1.3 %collective-permute-start.9 = (bf16[144,1024]{1,0:T(8,128)(2,1)S(1)}, bf16[144,1024]{1,0:T(8,128)(2,1)S(1)}, u32[]{:S(2)}, u32[]{:S(2)}) collective-permute-start(bf16[144,1024]{1,0:T(8,128)(2,1)S(1)} %chain.7), channel_id=1, source_target_pairs={{8,12},{4,0},{9,13},{5,1},{10,14},{6,2},{11,15},{7,3},{24,28},{20,... | collective-permute-start | bytes 884744 | tf_op jit(solution)/shard_map/ppermute | solution.py:706
  35.1 11.0 %collective-permute-done.4.refs_4_ = bf16[256,512]{1,0:T(8,128)(2,1)S(1)} collective-permute-done((bf16[256,512]{1,0:T(8,128)(2,1)S(1)}, bf16[256,512]{1,0:T(8,128)(2,1)S(1)}, u32[]{:S(2)}, u32[]{:S(2)}) %collective-permute-start.4) | collective-permute-done | bytes 262176 | tf_op jit(solution)/shard_map/ppermute | solution.py:661
  46.1 0.0 copy-done
  46.1 0.0 copy-done.4
  46.1 2.8 %attention.3.refs_1_.teacher_ref = bf16[256,1024]{1,0:T(8,128)(2,1)S(1)} custom-call(s32[1,1024]{1,0:T(1,128)S(1)} %copy-done.4, bf16[256,2048]{1,0:T(8,128)(2,1)S(1)} %bitcast.18, bf16[256,256]{1,0:T(8,128)(2,1)S(1)} %bitcast.24, bf16[256,256]{1,0:T(8,128)(2,1)S(1)} %bitcast.27, bf16[256,512]{1,0:T(8,128)(2,1)S(1)} %collective-permute-done.refs_0_, ...), custom_call_target="tpu_custom_call" | custom-call | flops 603979776 | bytes 2097152 | tf_op jit(solution)/shard_map/attention/pallas_call | solution.py:672
  48.9 0.0 copy-start.1
  48.9 0.0 copy-start.5
  48.9 2.8 %attention.2.refs_0_.teacher_ref = bf16[256,1024]{1,0:T(8,128)(2,1)S(1)} custom-call(s32[1,1024]{1,0:T(1,128)S(1)} %copy-done.4, bf16[256,2048]{1,0:T(8,128)(2,1)S(1)} %bitcast.19, bf16[256,256]{1,0:T(8,128)(2,1)S(1)} %bitcast.25, bf16[256,256]{1,0:T(8,128)(2,1)S(1)} %bitcast.28, bf16[256,512]{1,0:T(8,128)(2,1)S(1)} %collective-permute-done.refs_0_, ...), custom_call_target="tpu_custom_call" | custom-call | flops 603979776 | bytes 2097152 | tf_op jit(solution)/shard_map/attention/pallas_call | solution.py:672
  51.7 0.9 %collective-permute-done.7.refs_2_ = bf16[144,1024]{1,0:T(8,128)(2,1)S(1)} collective-permute-done((bf16[144,1024]{1,0:T(8,128)(2,1)S(1)}, bf16[144,1024]{1,0:T(8,128)(2,1)S(1)}, u32[]{:S(2)}, u32[]{:S(2)}) %collective-permute-start.7) | collective-permute-done | bytes 294944 | tf_op jit(solution)/shard_map/ppermute | solution.py:706
  52.7 0.0 copy-done.1
  52.7 0.0 copy-done.5
  52.7 1.8 %final.2 = (bf16[256,1024]{1,0:T(8,128)(2,1)S(1)}, f32[1,3,1024]{2,1,0:T(4,128)S(1)}) custom-call(f32[256,1024]{1,0:T(8,128)S(1)} %get-tuple-element.49.pre_ref, f32[256,1024]{1,0:T(8,128)S(1)} %get-tuple-element.50.reach_ref, f32[256,1024]{1,0:T(8,128)S(1)} %get-tuple-element.51.sx_ref, bf16[256,256]{1,0:T(8,128)(2,1)S(1)} %bitcast.21, ...), custom_call_target="tpu_custom_call" | custom-call | flops 67108864 | bytes 5242880 | tf_op jit(solution)/shard_map/final/pallas_call | solution.py:711
  54.4 1.4 %collective-permute-done.9.refs_2_ = bf16[144,1024]{1,0:T(8,128)(2,1)S(1)} collective-permute-done((bf16[144,1024]{1,0:T(8,128)(2,1)S(1)}, bf16[144,1024]{1,0:T(8,128)(2,1)S(1)}, u32[]{:S(2)}, u32[]{:S(2)}) %collective-permute-start.9) | collective-permute-done | bytes 294944 | tf_op jit(solution)/shard_map/ppermute | solution.py:706
  55.8 2.5 %final.3 = (bf16[256,1024]{1,0:T(8,128)(2,1)S(1)}, f32[8,3,1024]{2,1,0:T(4,128)}) custom-call(f32[256,1024]{1,0:T(8,128)S(1)} %get-tuple-element.57.pre_ref, f32[256,1024]{1,0:T(8,128)S(1)} %get-tuple-element.58.reach_ref, f32[256,1024]{1,0:T(8,128)S(1)} %get-tuple-element.59.sx_ref, bf16[256,256]{1,0:T(8,128)(2,1)S(1)} %bitcast.22, ...), custom_call_target="tpu_custom_call" | custom-call | flops 67108864 | bytes 5242880 | tf_op jit(solution)/shard_map/final/pallas_call | solution.py:711
  58.3 4.8 %all-to-all-start = ((f32[8,3,1024]{2,1,0:T(4,128)}), f32[8,3,1024]{2,1,0:T(4,128)S(1)}, u32[]{:S(2)}, u32[]{:S(2)}) async-start(f32[8,3,1024]{2,1,0:T(4,128)} %get-tuple-element.65), calls=%async_computation | async-start | bytes 262144 | tf_op jit(solution)/shard_map/all_to_all | solution.py:743
  63.1 1.0 %writing.2 = bf16[256,2048]{1,0:T(8,128)(2,1)} custom-call(bf16[256,1024]{1,0:T(8,128)(2,1)S(1)} %attention.2.refs_0_.teacher_ref, bf16[256,1024]{1,0:T(8,128)(2,1)S(1)} %attention.3.refs_1_.teacher_ref), custom_call_target="tpu_custom_call" | custom-call | bytes 2097152 | tf_op jit(solution)/shard_map/writing/pallas_call | solution.py:571
  64.1 1.0 %writing.3 = bf16[256,2048]{1,0:T(8,128)(2,1)} custom-call(bf16[256,1024]{1,0:T(8,128)(2,1)S(1)} %get-tuple-element.56.refs_0_, bf16[256,1024]{1,0:T(8,128)(2,1)S(1)} %get-tuple-element.64.refs_1_), custom_call_target="tpu_custom_call" | custom-call | bytes 2097152 | tf_op jit(solution)/shard_map/writing/pallas_call | solution.py:571
  65.1 5.5 %all-to-all-done.all_ref = f32[8,3,1024]{2,1,0:T(4,128)S(1)} async-done(((f32[8,3,1024]{2,1,0:T(4,128)}), f32[8,3,1024]{2,1,0:T(4,128)S(1)}, u32[]{:S(2)}, u32[]{:S(2)}) %all-to-all-start) | async-done | bytes 98336 | tf_op jit(solution)/shard_map/all_to_all | solution.py:743
  70.6 0.6 closing.1
  (6 shorter events, 0.1 us)
Async XLA Ops:
  0.6 3.2 %copy-start.2 = (bf16[1,256,256]{2,1,0:T(8,128)(2,1)S(1)}, bf16[1,256,256]{2,1,0:T(8,128)(2,1)}, u32[]{:S(2)}) copy-start(bf16[1,256,256]{2,1,0:T(8,128)(2,1)} %param.14) | copy-start | bytes 393220
  0.6 3.2 %copy-start.3 = (bf16[1,256,256]{2,1,0:T(8,128)(2,1)S(1)}, bf16[1,256,256]{2,1,0:T(8,128)(2,1)}, u32[]{:S(2)}) copy-start(bf16[1,256,256]{2,1,0:T(8,128)(2,1)} %param.15) | copy-start | bytes 393220
  3.8 12.8 %collective-permute-start.1 = (bf16[256,512]{1,0:T(8,128)(2,1)S(1)}, bf16[256,512]{1,0:T(8,128)(2,1)S(1)}, u32[]{:S(2)}, u32[]{:S(2)}) collective-permute-start(bf16[256,512]{1,0:T(8,128)(2,1)S(1)} %pack.1), channel_id=1, source_target_pairs={{4,8},{8,4},{5,9},{9,5},{6,10},{10,6},{7,11},{11,7},{20,24},{24,20... | collective-permute-start | bytes 786440 | tf_op jit(solution)/shard_map/ppermute | solution.py:647
  4.5 21.6 %collective-permute-start.5 = (bf16[144,1024]{1,0:T(8,128)(2,1)S(1)}, bf16[144,1024]{1,0:T(8,128)(2,1)S(1)}, u32[]{:S(2)}, u32[]{:S(2)}) collective-permute-start(bf16[144,1024]{1,0:T(8,128)(2,1)S(1)} %get-tuple-element.54), channel_id=1, source_target_pairs={{0,4},{12,8},{1,5},{13,9},{2,6},{14,10},{3,7},{15,11},{16,20},{28,... | collective-permute-start | bytes 884744 | tf_op jit(solution)/shard_map/ppermute | solution.py:706
  12.4 13.0 %collective-permute-start = (bf16[256,512]{1,0:T(8,128)(2,1)S(1)}, bf16[256,512]{1,0:T(8,128)(2,1)S(1)}, u32[]{:S(2)}, u32[]{:S(2)}) collective-permute-start(bf16[256,512]{1,0:T(8,128)(2,1)S(1)} %pack.1), channel_id=1, source_target_pairs={{0,4},{12,8},{4,0},{8,12},{1,5},{13,9},{5,1},{9,13},{2,6},{14,10},... | collective-permute-start | bytes 786440 | tf_op jit(solution)/shard_map/ppermute | solution.py:646
  16.7 13.5 %collective-permute-start.3 = (bf16[144,1024]{1,0:T(8,128)(2,1)S(1)}, bf16[144,1024]{1,0:T(8,128)(2,1)S(1)}, u32[]{:S(2)}, u32[]{:S(2)}) collective-permute-start(bf16[144,1024]{1,0:T(8,128)(2,1)S(1)} %merge.1), channel_id=1, source_target_pairs={{0,4},{12,8},{4,0},{8,12},{1,5},{13,9},{5,1},{9,13},{2,6},{14,10},... | collective-permute-start | bytes 884744 | tf_op jit(solution)/shard_map/ppermute | solution.py:659
  25.4 5.5 %collective-permute-start.2 = (bf16[256,512]{1,0:T(8,128)(2,1)S(1)}, bf16[256,512]{1,0:T(8,128)(2,1)S(1)}, u32[]{:S(2)}, u32[]{:S(2)}) collective-permute-start(bf16[256,512]{1,0:T(8,128)(2,1)S(1)} %collective-permute-done.refs_0_), channel_id=1, source_target_pairs={{4,8},{8,4},{5,9},{9,5},{6,10},{10,6},{7,11},{11,7},{20,24},{24,20... | collective-permute-start | bytes 786440 | tf_op jit(solution)/shard_map/ppermute | solution.py:649
  26.1 6.1 %collective-permute-start.6 = (bf16[144,1024]{1,0:T(8,128)(2,1)S(1)}, bf16[144,1024]{1,0:T(8,128)(2,1)S(1)}, u32[]{:S(2)}, u32[]{:S(2)}) collective-permute-start(bf16[144,1024]{1,0:T(8,128)(2,1)S(1)} %chain.4), channel_id=1, source_target_pairs={{4,8},{8,4},{5,9},{9,5},{6,10},{10,6},{7,11},{11,7},{20,24},{24,20... | collective-permute-start | bytes 884744 | tf_op jit(solution)/shard_map/ppermute | solution.py:706
  30.3 3.5 %collective-permute-start.8 = (bf16[144,1024]{1,0:T(8,128)(2,1)S(1)}, bf16[144,1024]{1,0:T(8,128)(2,1)S(1)}, u32[]{:S(2)}, u32[]{:S(2)}) collective-permute-start(bf16[144,1024]{1,0:T(8,128)(2,1)S(1)} %chain.6), channel_id=1, source_target_pairs={{4,8},{8,4},{5,9},{9,5},{6,10},{10,6},{7,11},{11,7},{20,24},{24,20... | collective-permute-start | bytes 884744 | tf_op jit(solution)/shard_map/ppermute | solution.py:706
  30.9 15.2 %collective-permute-start.4 = (bf16[256,512]{1,0:T(8,128)(2,1)S(1)}, bf16[256,512]{1,0:T(8,128)(2,1)S(1)}, u32[]{:S(2)}, u32[]{:S(2)}) collective-permute-start(bf16[256,512]{1,0:T(8,128)(2,1)S(1)} %collective-permute-done.2.refs_2_), channel_id=1, source_target_pairs={{4,0},{8,12},{5,1},{9,13},{6,2},{10,14},{7,3},{11,15},{20,16},{24,... | collective-permute-start | bytes 786440 | tf_op jit(solution)/shard_map/ppermute | solution.py:661
  32.3 13.8 %copy-start = (bf16[1,256,2048]{2,1,0:T(8,128)(2,1)S(1)}, bf16[1,256,2048]{2,1,0:T(8,128)(2,1)}, u32[]{:S(2)}) copy-start(bf16[1,256,2048]{2,1,0:T(8,128)(2,1)} %param.13) | copy-start | bytes 3145732
  32.3 20.4 %collective-permute-start.7 = (bf16[144,1024]{1,0:T(8,128)(2,1)S(1)}, bf16[144,1024]{1,0:T(8,128)(2,1)S(1)}, u32[]{:S(2)}, u32[]{:S(2)}) collective-permute-start(bf16[144,1024]{1,0:T(8,128)(2,1)S(1)} %chain.5), channel_id=1, source_target_pairs={{8,12},{4,0},{9,13},{5,1},{10,14},{6,2},{11,15},{7,3},{24,28},{20,... | collective-permute-start | bytes 884744 | tf_op jit(solution)/shard_map/ppermute | solution.py:706
  33.7 12.4 %copy-start.4 = (s32[1,1024]{1,0:T(1,128)S(1)}, s32[1,1024]{1,0:T(1,128)}, u32[]{:S(2)}) copy-start(s32[1,1024]{1,0:T(1,128)} %docs_ref.7) | copy-start | bytes 12292
  33.8 22.0 %collective-permute-start.9 = (bf16[144,1024]{1,0:T(8,128)(2,1)S(1)}, bf16[144,1024]{1,0:T(8,128)(2,1)S(1)}, u32[]{:S(2)}, u32[]{:S(2)}) collective-permute-start(bf16[144,1024]{1,0:T(8,128)(2,1)S(1)} %chain.7), channel_id=1, source_target_pairs={{8,12},{4,0},{9,13},{5,1},{10,14},{6,2},{11,15},{7,3},{24,28},{20,... | collective-permute-start | bytes 884744 | tf_op jit(solution)/shard_map/ppermute | solution.py:706
  48.9 3.7 %copy-start.1 = (bf16[1,256,256]{2,1,0:T(8,128)(2,1)S(1)}, bf16[1,256,256]{2,1,0:T(8,128)(2,1)}, u32[]{:S(2)}) copy-start(bf16[1,256,256]{2,1,0:T(8,128)(2,1)} %param.20) | copy-start | bytes 393220
  48.9 3.7 %copy-start.5 = (f32[2048]{0:T(1024)S(1)}, f32[2048]{0:T(1024)}, u32[]{:S(2)}) copy-start(f32[2048]{0:T(1024)} %param.25) | copy-start | bytes 24580
  58.3 12.4 %all-to-all-start = ((f32[8,3,1024]{2,1,0:T(4,128)}), f32[8,3,1024]{2,1,0:T(4,128)S(1)}, u32[]{:S(2)}, u32[]{:S(2)}) async-start(f32[8,3,1024]{2,1,0:T(4,128)} %get-tuple-element.65), calls=%async_computation | async-start | bytes 262144 | tf_op jit(solution)/shard_map/all_to_all | solution.py:743

commit v8 on v7

--- a/solution.py
+++ b/solution.py
@@ -195,62 +195,64 @@
 
 
 def local_kernel(
-    count, groups, docs_ref, x_ref, gate_ref, b_ref, c_ref, skip_ref, ec_ref, *refs
+    count,
+    groups,
+    g,
+    docs_ref,
+    x_ref,
+    gate_ref,
+    b_ref,
+    c_ref,
+    skip_ref,
+    ec_ref,
+    xw_ref,
+    pre_ref,
+    reach_ref,
+    sx_ref,
+    x_here,
+    gate_here,
+    sems,
 ):
-    xw_refs, pre_refs, reach_refs, sx_refs = (
-        refs[k * groups : (k + 1) * groups] for k in range(4)
-    )
-    x_here, gate_here, sems = refs[4 * groups :]
     heads, rows = ec_ref.shape
     stretch = rows // 2
     width = x_ref.shape[1] // groups
     index = lax.axis_index("ctx")
-    moves = []
-    for g in range(groups):
-        cols = pl.ds(g * width, width)
-        moves.append(
-            [
-                pltpu.make_async_copy(x_ref.at[:, cols], x_here.at[g], sems.at[0, g]),
-                pltpu.make_async_copy(gate_ref.at[:, cols], gate_here.at[g], sems.at[1, g]),
-            ]
-        )
-        for move in moves[g]:
-            move.start()
+    cols = pl.ds(g * width, width)
+    moves = [
+        pltpu.make_async_copy(x_ref.at[:, cols], x_here, sems.at[0]),
+        pltpu.make_async_copy(gate_ref.at[:, cols], gate_here, sems.at[1]),
+    ]
+    for move in moves:
+        move.start()
     triangle = lower_triangle(stretch)
-    skip = as_column(skip_ref[...])
+    proj = slice(g * N, (g + 1) * N)
+    matrix = spread_matrix(heads, width, g * (heads // groups))
+    wide_skip = spread(as_column(skip_ref[...]), matrix)
     step = 16
-    masks = []
     for half in range(2):
         block = own_block(index, count, half)
+        sl = slice(half * stretch, (half + 1) * stretch)
         row = doc_row(docs_ref, block, stretch)
         column = as_column(row)
         reached = jnp.where(column == prior_doc(docs_ref, block, stretch).astype(F32), 1.0, 0.0)
-        masks.append((triangle & (column == row.astype(F32)), reached))
-    for g in range(groups):
-        proj = slice(g * N, (g + 1) * N)
-        matrix = spread_matrix(heads, width, g * (heads // groups))
-        wide_skip = spread(skip, matrix)
-        for half in range(2):
-            sl = slice(half * stretch, (half + 1) * stretch)
-            near, reached = masks[half]
-            gram = dot_nt(c_ref[sl, proj], b_ref[sl, proj])
-            gram = jnp.where(near, gram, 0.0).astype(BF16)
-            wide = spread(ec_ref[:, sl], matrix)
-            inner = jnp.dot(gram, xw_refs[g][sl, :], preferred_element_type=F32)
-            if half == 0:
-                for move in moves[g]:
-                    move.wait()
-            for k in range(0, stretch, step):
-                at = slice(half * stretch + k, half * stretch + k + step)
-                here = slice(k, k + step)
-                x = x_here[g, at, :].astype(F32)
-                gate = gate_here[g, at, :].astype(F32)
-                silu = gate / (1.0 + jnp.exp(-gate))
-                fade = wide[here] * silu
-                sx = silu * x
-                sx_refs[g][at, :] = sx
-                pre_refs[g][at, :] = inner[here] * fade + wide_skip * sx
-                reach_refs[g][at, :] = reached[here] * fade
+        gram = dot_nt(c_ref[sl, proj], b_ref[sl, proj])
+        gram = jnp.where(triangle & (column == row.astype(F32)), gram, 0.0).astype(BF16)
+        wide = spread(ec_ref[:, sl], matrix)
+        inner = jnp.dot(gram, xw_ref[sl, :], preferred_element_type=F32)
+        if half == 0:
+            for move in moves:
+                move.wait()
+        for k in range(0, stretch, step):
+            at = slice(half * stretch + k, half * stretch + k + step)
+            here = slice(k, k + step)
+            x = x_here[at, :].astype(F32)
+            gate = gate_here[at, :].astype(F32)
+            silu = gate / (1.0 + jnp.exp(-gate))
+            fade = wide[here] * silu
+            sx = silu * x
+            sx_ref[at, :] = sx
+            pre_ref[at, :] = inner[here] * fade + wide_skip * sx
+            reach_ref[at, :] = reached[here] * fade
 
 
 def merge_kernel(count, state_ref, kv_ref, out_ref):
@@ -500,15 +502,12 @@
     matrix = jnp.where(row == lane // P_SIZE + g * (width // P_SIZE), 1.0, 0.0).astype(BF16)
     hi, lo = parts(skip_acc[...])
     by_head = jnp.sum(dot_nt(hi, matrix) + dot_nt(lo, matrix), axis=0, keepdims=True)
-    by_lane = jnp.sum(gain_acc[...], axis=0, keepdims=True)
+    grad_ref[...] = jnp.zeros_like(grad_ref)
     if g:
-        by_head += before[0, groups : groups + 1, :tile]
-    for d in range(grad_ref.shape[0]):
-        if g:
-            grad_ref[d, :g, :] = before[0, :g, :]
-        grad_ref[d, g : g + 1, :] = by_lane
-        grad_ref[d, groups : groups + 1, :] = jnp.zeros((1, width), F32)
-        grad_ref[d, groups : groups + 1, :tile] = by_head
+        grad_ref[:g, :] = before[:g, :]
+        by_head += before[groups : groups + 1, :tile]
+    grad_ref[g : g + 1, :] = jnp.sum(gain_acc[...], axis=0, keepdims=True)
+    grad_ref[groups : groups + 1, :tile] = by_head
 
 
 def writing_kernel(*refs):
@@ -524,14 +523,18 @@
         move.wait()
 
 
-def closing_kernel(all_ref, gain_ref, skip_ref):
-    total = all_ref[0]
-    for d in range(1, all_ref.shape[0]):
-        total += all_ref[d]
+def closing_kernel(a_ref, b_ref, gain_ref, skip_ref):
+    total = a_ref[...] + b_ref[...]
     groups, width = total.shape[0] - 1, total.shape[1]
     for g in range(groups):
         gain_ref[:, g * width : (g + 1) * width] = total[g : g + 1, :]
     skip_ref[...] = total[groups : groups + 1, : skip_ref.shape[1]]
+
+
+def exchange(part, shift):
+    axes = ("dp", "ctx")
+    size = lax.axis_size(axes)
+    return lax.ppermute(part, axes, [(d, d ^ shift) for d in range(size)])
 
 
 def body(
@@ -559,7 +562,6 @@
     width = features // groups
     length = doc_ids.shape[1]
     others = count - 1
-    members = lax.axis_size("dp") * count
     loss_scale = 1.0 / (lax.axis_size("dp") * count * rows)
     x, gate, bmat, cmat = inputs[0], gate_input[0], b_input[0], c_input[0]
     struct = jax.ShapeDtypeStruct
@@ -620,32 +622,57 @@
         name="pack",
     )(key_part, value_part)
 
-    local = pl.pallas_call(
-        functools.partial(local_kernel, count, groups),
-        out_shape=(struct((rows, width), F32),) * (3 * groups),
-        in_specs=[
-            VMEM,
-            *[pl.BlockSpec(memory_space=pl.ANY)] * 2,
-            *[VMEM] * (4 + groups),
-        ],
-        out_specs=(VMEM,) * (3 * groups),
-        scratch_shapes=[
-            pltpu.VMEM((groups, rows, width), BF16),
-            pltpu.VMEM((groups, rows, width), BF16),
-            pltpu.SemaphoreType.DMA((2, groups)),
-        ],
-        compiler_params=params(16),
-        cost_estimate=cost(2 * rows * features * N, 16 * rows * features),
-        name="local",
-    )(*in_hbm(doc_ids, x, gate, bmat, cmat, skip.reshape(1, heads)), ec, *xw)
+    def local_terms(g, growth):
+        return pl.pallas_call(
+            functools.partial(local_kernel, count, groups, g),
+            out_shape=(struct((rows, width), F32),) * 3,
+            in_specs=[
+                VMEM,
+                *[pl.BlockSpec(memory_space=pl.ANY)] * 2,
+                *[VMEM] * 5,
+            ],
+            out_specs=(VMEM,) * 3,
+            scratch_shapes=[
+                pltpu.VMEM((rows, width), BF16),
+                pltpu.VMEM((rows, width), BF16),
+                pltpu.SemaphoreType.DMA((2,)),
+            ],
+            compiler_params=params(12),
+            cost_estimate=cost(2 * rows * width * N, 16 * rows * width),
+            name="local",
+        )(*in_hbm(doc_ids, x, gate, bmat, cmat, skip.reshape(1, heads)), growth, xw[g])
 
     send = list(send)
     got = [[] for _ in range(groups)]
+    local = []
+    def passed_on(g, stage):
+        return pl.pallas_call(
+            functools.partial(chain_kernel, count, stage),
+            out_shape=payload,
+            in_specs=[VMEM] * 4,
+            out_specs=VMEM,
+            compiler_params=params(4),
+            cost_estimate=pl.CostEstimate(flops=16384 * N * width, bytes_accessed=0, transcendentals=0),
+            name="chain",
+        )(got[g][-1], f_parts[g], b_parts[g], dec[g])
+
+    def stage_pairs(stage):
+        return [(stage - 1, stage), (count - stage, count - stage - 1)]
+
     if count == 4:
         inward, outward, across = [(0, 1), (3, 2)], [(1, 0), (2, 3)], [(1, 2), (2, 1)]
+        if groups > 1:
+            got[0].append(lax.ppermute(send[0], "ctx", stage_pairs(1)))
         near = lax.ppermute(kv, "ctx", inward + outward)
         middle = lax.ppermute(kv, "ctx", across)
-        middle, *local = lax.optimization_barrier((middle, *local))
+        if groups > 1:
+            local = [local_terms(0, ec)]
+            got[0][0], _ = lax.optimization_barrier((got[0][0], local[0][0]))
+            send[0] = passed_on(0, 1)
+            got[0].append(lax.ppermute(send[0], "ctx", stage_pairs(2)))
+            growth, _ = lax.optimization_barrier((ec, send[0]))
+            local += [local_terms(g, growth) for g in range(1, groups)]
+            middle, _ = lax.optimization_barrier((middle, local[-1][0]))
         beyond = lax.ppermute(near, "ctx", across)
         send[-1] = pl.pallas_call(
             functools.partial(merge_kernel, count),
@@ -667,6 +694,21 @@
         for _ in range(others):
             kv_got.append(lax.ppermute(kv_got[-1], "ctx", ring_pairs))
         kv_got = kv_got[1:]
+    if not local:
+        local = [local_terms(g, ec) for g in range(groups)]
+    ahead = None
+    for r in range(1, count):
+        for g in range(groups):
+            if len(got[g]) >= r:
+                continue
+            if r == 2 and 0 < g == groups - 1 and count == 4:
+                ahead = passed_on(0, 2)
+                got[g][0], _, _ = lax.optimization_barrier((got[g][0], ahead, beyond))
+            if r == 3 and g == 0 and ahead is not None:
+                send[g] = ahead
+            elif r > 1:
+                send[g] = passed_on(g, r - 1)
+            got[g].append(lax.ppermute(send[g], "ctx", stage_pairs(r)))
     stack = 4 if per_kv % 4 == 0 and count <= 4 else 1
     targets = [
         pl.pallas_call(
@@ -689,31 +731,12 @@
         )(doc_ids, queries[0], keys[0], values[0], *kv_got)
         for g in range(kv_dev)
     ]
-    for r in range(1, count):
-        for g in range(groups):
-            if r > 1:
-                send[g] = pl.pallas_call(
-                    functools.partial(chain_kernel, count, r - 1),
-                    out_shape=payload,
-                    in_specs=[VMEM] * 4,
-                    out_specs=VMEM,
-                    compiler_params=params(4),
-                    cost_estimate=cost(16384 * N * width, 8 * N * width),
-                    name="chain",
-                )(got[g][-1], f_parts[g], b_parts[g], dec[g])
-            if len(got[g]) < r:
-                pairs = [(r - 1, r), (count - r, count - r - 1)]
-                got[g].append(lax.ppermute(send[g], "ctx", pairs))
-
     normed, grads = [], None
     for g in range(groups):
         more = [] if grads is None else [grads]
         made, grads = pl.pallas_call(
             functools.partial(final_kernel, count, g, groups, loss_scale),
-            out_shape=(
-                struct((rows, width), BF16),
-                struct((members if g == groups - 1 else 1, groups + 1, width), F32),
-            ),
+            out_shape=(struct((rows, width), BF16), struct((groups + 1, width), F32)),
             in_specs=[VMEM] * (8 + others + len(more)),
             out_specs=(VMEM,) * 2,
             scratch_shapes=[
@@ -729,7 +752,7 @@
             cost_estimate=cost(2 * rows * width * N, 20 * rows * width),
             name="final",
         )(
-            *local[g::groups],
+            *local[g],
             cmat,
             targets[g],
             gain.reshape(1, features),
@@ -740,15 +763,22 @@
         )
         normed.append(made)
     teacher, student = write(*targets), write(*normed)
-    gathered = lax.all_to_all(grads, ("dp", "ctx"), 0, 0)
+    partner = exchange(grads, 1)
+    if lax.axis_size("dp") == 2:
+        grads = (grads + partner) + (exchange(grads, count) + exchange(grads, count + 1))
+    else:
+        grads = grads + partner
+    shifts = [1 << k for k in range(1, count.bit_length() - 1)]
+    for shift in shifts[:-1]:
+        grads = grads + exchange(grads, shift)
     grad_gain, grad_skip = pl.pallas_call(
         closing_kernel,
         out_shape=(struct((1, features), F32), struct((1, heads), F32)),
-        in_specs=[VMEM],
+        in_specs=[VMEM] * 2,
         out_specs=(VMEM,) * 2,
-        compiler_params=params(4),
+        compiler_params=params(2),
         name="closing",
-    )(gathered)
+    )(grads, exchange(grads, shifts[-1]))
     return (teacher[None], student[None], grad_gain[0], grad_skip[0])
 
 

time: 71.7 us -> 67.7 us (0.944)
  waiting for transfers between devices: 29 us -> 20.7 us
  starting transfers between devices: 21.5 us -> 24.7 us
  Pallas kernels: 19.8 us -> 20.9 us
    ppermute x1, waiting for transfers between devices: 6.63 us -> 0.01 us  [body(): near = lax.ppermute(kv, 'ctx', inward + outward)]
    all_to_all x1 -> x0, waiting for transfers between devices: 5.54 us -> none  [body(): gathered = lax.all_to_all(grads, ('dp', 'ctx'), 0, 0)]
    all_to_all x1 -> x0, starting transfers between devices: 4.84 us -> none  [body(): gathered = lax.all_to_all(grads, ('dp', 'ctx'), 0, 0)]
    ppermute x5 -> x9, waiting for transfers between devices: 2.3 us -> 6.25 us  [the longest x4 2.85 us: exchange(): return lax.ppermute(part, axes, [(d, d ^ shift) for d in range(size)])]
    ppermute x1, starting transfers between devices: 2.07 us -> 5.51 us  [body(): far = lax.ppermute(send[-1], 'ctx', inward + outward)]
    ppermute x5 -> x9, starting transfers between devices: 11.9 us -> 14.3 us  [the longest x4 5.25 us: exchange(): return lax.ppermute(part, axes, [(d, d ^ shift) for d in range(size)])]
    ppermute x1, starting transfers between devices: 0.07 us -> 2.24 us  [body(): near = lax.ppermute(kv, 'ctx', inward + outward)]
    pallas_call x5 -> x6, Pallas kernels: 4.26 us -> 6.05 us  [the longest x2 6 us: local_terms(): pl.pallas_call(functools.partial(local_kernel, count, groups, g), out_sha...]
  transfers between devices with their start and end apart: 11 -> 14, of which waited for: 6 -> 8; matrix products, arithmetic and copies ran while one was open for 0% -> 0% of each run, Pallas kernels for 19% -> 23%
where the time goes in v8:
time: 67.7 us; the launch traced here: 67.3 us
  starting transfers between devices  24.7 us (36%)
  Pallas kernels  20.9 us (31%)
  waiting for transfers between devices  20.7 us (31%)
  between operations  0.88 us (1%)
    ppermute x1, waiting for transfers between devices, body(): farther = lax.ppermute(beyond, 'ctx', outward)  10.5 us
    pallas_call x2, Pallas kernels, local_terms(): pl.pallas_call(functools.partial(local_kernel, count, groups, g), out_sha...  6 us
    pallas_call x2, Pallas kernels, body(): pl.pallas_call(functools.partial(attention_kernel, count, per_kv, stack,...  5.57 us
    ppermute x1, starting transfers between devices, body(): far = lax.ppermute(send[-1], 'ctx', inward + outward)  5.51 us
    ppermute x4, starting transfers between devices, exchange(): return lax.ppermute(part, axes, [(d, d ^ shift) for d in range(size)])  5.25 us
    ppermute x1, starting transfers between devices, body(): got[0].append(lax.ppermute(send[0], 'ctx', stage_pairs(1)))  5.04 us
    ppermute x1, waiting for transfers between devices, body(): far = lax.ppermute(send[-1], 'ctx', inward + outward)  3.99 us
    pallas_call x2, Pallas kernels, body(): pl.pallas_call(functools.partial(final_kernel, count, g, groups, loss_sca...  3.54 us
  transfers between devices with their start and end apart: 14, of which 8 were waited for; matrix products, arithmetic and copies ran while one was open for 0% of the time, Pallas kernels for 23%

profile of v8, /device:TPU:0, one launch (start us, length us, event | category | flops | bytes accessed | tf_op | source)
XLA Modules:
  0.0 67.3 jit_solution(17723058742416258205)
XLA Ops:
  0.6 0.0 copy-start.2
  0.6 0.0 copy-start.3
  0.7 3.1 %opening.1 = (f32[32,256]{1,0:T(8,128)S(1)}, bf16[256,1024]{1,0:T(8,128)(2,1)S(1)}, bf16[256,1024]{1,0:T(8,128)(2,1)S(1)}, f32[8,1024]{1,0:T(8,128)S(1)}, f32[8,...) custom-call(s32[1,1024]{1,0:T(1,128)} %docs_ref.9, ...), custom_call_target="tpu_custom_call" | custom-call | flops 268435456 | bytes 4194304 | tf_op jit(solution)/shard_map/opening/pallas_call | solution.py:586
  3.8 5.0 %collective-permute-start.2 = (bf16[144,1024]{1,0:T(8,128)(2,1)S(1)}, bf16[144,1024]{1,0:T(8,128)(2,1)S(1)}, u32[]{:S(2)}, u32[]{:S(2)}) collective-permute-start(bf16[144,1024]{1,0:T(8,128)(2,1)S(1)} %get-tuple-element.36), channel_id=1, source_target_pairs={{0,4},{12,8},{1,5},{13,9},{2,6},{14,10},{3,7},{15,11},{16,20},{28,... | collective-permute-start | bytes 884744 | tf_op jit(solution)/shard_map/ppermute | solution.py:665
  8.8 0.0 copy-done.2
  8.9 0.0 copy-done.3
  8.9 0.7 %collective-permute-start.1 = (bf16[256,512]{1,0:T(8,128)(2,1)S(1)}, bf16[256,512]{1,0:T(8,128)(2,1)S(1)}, u32[]{:S(2)}, u32[]{:S(2)}) collective-permute-start(bf16[256,512]{1,0:T(8,128)(2,1)S(1)} %pack.1), channel_id=1, source_target_pairs={{4,8},{8,4},{5,9},{9,5},{6,10},{10,6},{7,11},{11,7},{20,24},{24,20... | collective-permute-start | bytes 786440 | tf_op jit(solution)/shard_map/ppermute | solution.py:667
  9.6 2.2 %collective-permute-start = (bf16[256,512]{1,0:T(8,128)(2,1)S(1)}, bf16[256,512]{1,0:T(8,128)(2,1)S(1)}, u32[]{:S(2)}, u32[]{:S(2)}) collective-permute-start(bf16[256,512]{1,0:T(8,128)(2,1)S(1)} %pack.1), channel_id=1, source_target_pairs={{0,4},{12,8},{4,0},{8,12},{1,5},{13,9},{5,1},{9,13},{2,6},{14,10},... | collective-permute-start | bytes 786440 | tf_op jit(solution)/shard_map/ppermute | solution.py:666
  11.8 3.0 %local.2 = (f32[256,1024]{1,0:T(8,128)S(1)}, f32[256,1024]{1,0:T(8,128)S(1)}, f32[256,1024]{1,0:T(8,128)S(1)}) custom-call(s32[1,1024]{1,0:T(1,128)} %docs_ref.9, bf16[256,2048]{1,0:T(8,128)(2,1)} %bitcast.33, bf16[256,2048]{1,0:T(8,128)(2,1)} %bitcast.35, bf16[256,256]{1,0:T(8,128)(2,1)} %bitcast.38, bf16[256,256]{1,0:T(8,128)(2,1)} %bitcast.20, ...), custom_call_target="tpu_custom_call" | custom-call | flops 67108864 | bytes 4194304 | tf_op jit(solution)/shard_map/local/pallas_call | solution.py:626
  14.8 1.4 %collective-permute-done.2.got_ref.refs_0_ = bf16[144,1024]{1,0:T(8,128)(2,1)S(1)} collective-permute-done((bf16[144,1024]{1,0:T(8,128)(2,1)S(1)}, bf16[144,1024]{1,0:T(8,128)(2,1)S(1)}, u32[]{:S(2)}, u32[]{:S(2)}) %collective-permute-start.2) | collective-permute-done | bytes 294944 | tf_op jit(solution)/shard_map/ppermute | solution.py:665
  16.2 0.7 collective-permute-start.6
  16.9 3.0 %local.3 = (f32[256,1024]{1,0:T(8,128)S(1)}, f32[256,1024]{1,0:T(8,128)S(1)}, f32[256,1024]{1,0:T(8,128)S(1)}) custom-call(s32[1,1024]{1,0:T(1,128)} %docs_ref.9, bf16[256,2048]{1,0:T(8,128)(2,1)} %bitcast.34, bf16[256,2048]{1,0:T(8,128)(2,1)} %bitcast.36, bf16[256,256]{1,0:T(8,128)(2,1)} %bitcast.39, bf16[256,256]{1,0:T(8,128)(2,1)} %bitcast.21, ...), custom_call_target="tpu_custom_call" | custom-call | flops 67108864 | bytes 4194304 | tf_op jit(solution)/shard_map/local/pallas_call | solution.py:626
  19.9 0.0 collective-permute-done.1.kv_ref.refs_1_
  20.0 5.5 %collective-permute-start.4 = (bf16[144,1024]{1,0:T(8,128)(2,1)S(1)}, bf16[144,1024]{1,0:T(8,128)(2,1)S(1)}, u32[]{:S(2)}, u32[]{:S(2)}) collective-permute-start(bf16[144,1024]{1,0:T(8,128)(2,1)S(1)} %merge.1), channel_id=1, source_target_pairs={{0,4},{12,8},{4,0},{8,12},{1,5},{13,9},{5,1},{9,13},{2,6},{14,10},... | collective-permute-start | bytes 884744 | tf_op jit(solution)/shard_map/ppermute | solution.py:686
  25.5 0.0 collective-permute-done.refs_0_
  25.5 0.7 collective-permute-start.3
  26.2 0.0 collective-permute-done.6.got_ref.refs_1_
  26.2 0.0 collective-permute-done.3.refs_2_
  26.2 4.0 %collective-permute-done.4.refs_3_.got_ref.refs_0_ = bf16[144,1024]{1,0:T(8,128)(2,1)S(1)} collective-permute-done((bf16[144,1024]{1,0:T(8,128)(2,1)S(1)}, bf16[144,1024]{1,0:T(8,128)(2,1)S(1)}, u32[]{:S(2)}, u32[]{:S(2)}) %collective-permute-start.4) | collective-permute-done | bytes 294944 | tf_op jit(solution)/shard_map/ppermute | solution.py:686
  30.2 0.8 %collective-permute-start.8 = (bf16[144,1024]{1,0:T(8,128)(2,1)S(1)}, bf16[144,1024]{1,0:T(8,128)(2,1)S(1)}, u32[]{:S(2)}, u32[]{:S(2)}) collective-permute-start(bf16[144,1024]{1,0:T(8,128)(2,1)S(1)} %chain.6), channel_id=1, source_target_pairs={{4,8},{8,4},{5,9},{9,5},{6,10},{10,6},{7,11},{11,7},{20,24},{24,20... | collective-permute-start | bytes 884744 | tf_op jit(solution)/shard_map/ppermute | solution.py:711
  31.0 1.3 %collective-permute-start.5 = (bf16[256,512]{1,0:T(8,128)(2,1)S(1)}, bf16[256,512]{1,0:T(8,128)(2,1)S(1)}, u32[]{:S(2)}, u32[]{:S(2)}) collective-permute-start(bf16[256,512]{1,0:T(8,128)(2,1)S(1)} %collective-permute-done.3.refs_2_), channel_id=1, source_target_pairs={{4,0},{8,12},{5,1},{9,13},{6,2},{10,14},{7,3},{11,15},{20,16},{24,... | collective-permute-start | bytes 786440 | tf_op jit(solution)/shard_map/ppermute | solution.py:688
  32.3 1.3 %collective-permute-start.7 = (bf16[144,1024]{1,0:T(8,128)(2,1)S(1)}, bf16[144,1024]{1,0:T(8,128)(2,1)S(1)}, u32[]{:S(2)}, u32[]{:S(2)}) collective-permute-start(bf16[144,1024]{1,0:T(8,128)(2,1)S(1)} %chain.5), channel_id=1, source_target_pairs={{8,12},{4,0},{9,13},{5,1},{10,14},{6,2},{11,15},{7,3},{24,28},{20,... | collective-permute-start | bytes 884744 | tf_op jit(solution)/shard_map/ppermute | solution.py:711
  33.6 0.0 collective-permute-done.8.got_ref.refs_1_
  33.6 0.0 copy-start.4
  33.7 1.3 %collective-permute-start.9 = (bf16[144,1024]{1,0:T(8,128)(2,1)S(1)}, bf16[144,1024]{1,0:T(8,128)(2,1)S(1)}, u32[]{:S(2)}, u32[]{:S(2)}) collective-permute-start(bf16[144,1024]{1,0:T(8,128)(2,1)S(1)} %chain.7), channel_id=1, source_target_pairs={{8,12},{4,0},{9,13},{5,1},{10,14},{6,2},{11,15},{7,3},{24,28},{20,... | collective-permute-start | bytes 884744 | tf_op jit(solution)/shard_map/ppermute | solution.py:711
  35.0 10.5 %collective-permute-done.5.refs_4_ = bf16[256,512]{1,0:T(8,128)(2,1)S(1)} collective-permute-done((bf16[256,512]{1,0:T(8,128)(2,1)S(1)}, bf16[256,512]{1,0:T(8,128)(2,1)S(1)}, u32[]{:S(2)}, u32[]{:S(2)}) %collective-permute-start.5) | collective-permute-done | bytes 262176 | tf_op jit(solution)/shard_map/ppermute | solution.py:688
  45.4 0.0 copy-done
  45.4 0.0 copy-done.4
  45.4 2.8 %attention.3.refs_1_.teacher_ref = bf16[256,1024]{1,0:T(8,128)(2,1)S(1)} custom-call(s32[1,1024]{1,0:T(1,128)S(1)} %copy-done.4, bf16[256,2048]{1,0:T(8,128)(2,1)S(1)} %bitcast.18, bf16[256,256]{1,0:T(8,128)(2,1)S(1)} %bitcast.25, bf16[256,256]{1,0:T(8,128)(2,1)S(1)} %bitcast.28, bf16[256,512]{1,0:T(8,128)(2,1)S(1)} %collective-permute-done.refs_0_, ...), custom_call_target="tpu_custom_call" | custom-call | flops 603979776 | bytes 2097152 | tf_op jit(solution)/shard_map/attention/pallas_call | solution.py:714
  48.2 0.0 copy-start.1
  48.2 0.0 copy-start.5
  48.2 2.8 %attention.2.refs_0_.teacher_ref = bf16[256,1024]{1,0:T(8,128)(2,1)S(1)} custom-call(s32[1,1024]{1,0:T(1,128)S(1)} %copy-done.4, bf16[256,2048]{1,0:T(8,128)(2,1)S(1)} %bitcast.19, bf16[256,256]{1,0:T(8,128)(2,1)S(1)} %bitcast.26, bf16[256,256]{1,0:T(8,128)(2,1)S(1)} %bitcast.29, bf16[256,512]{1,0:T(8,128)(2,1)S(1)} %collective-permute-done.refs_0_, ...), custom_call_target="tpu_custom_call" | custom-call | flops 603979776 | bytes 2097152 | tf_op jit(solution)/shard_map/attention/pallas_call | solution.py:714
  51.0 0.6 collective-permute-done.7.refs_2_
  51.7 0.0 copy-done.5
  51.7 1.8 %final.2 = (bf16[256,1024]{1,0:T(8,128)(2,1)S(1)}, f32[3,1024]{1,0:T(4,128)S(1)}) custom-call(f32[256,1024]{1,0:T(8,128)S(1)} %get-tuple-element.38.pre_ref, f32[256,1024]{1,0:T(8,128)S(1)} %get-tuple-element.48.reach_ref, f32[256,1024]{1,0:T(8,128)S(1)} %get-tuple-element.49.sx_ref, bf16[256,256]{1,0:T(8,128)(2,1)S(1)} %bitcast.22, ...), custom_call_target="tpu_custom_call" | custom-call | flops 67108864 | bytes 5242880 | tf_op jit(solution)/shard_map/final/pallas_call | solution.py:737
  53.4 1.4 %collective-permute-done.9.refs_2_ = bf16[144,1024]{1,0:T(8,128)(2,1)S(1)} collective-permute-done((bf16[144,1024]{1,0:T(8,128)(2,1)S(1)}, bf16[144,1024]{1,0:T(8,128)(2,1)S(1)}, u32[]{:S(2)}, u32[]{:S(2)}) %collective-permute-start.9) | collective-permute-done | bytes 294944 | tf_op jit(solution)/shard_map/ppermute | solution.py:711
  54.8 1.8 %final.3 = (bf16[256,1024]{1,0:T(8,128)(2,1)S(1)}, f32[3,1024]{1,0:T(4,128)S(1)}) custom-call(f32[256,1024]{1,0:T(8,128)S(1)} %get-tuple-element.45.pre_ref, f32[256,1024]{1,0:T(8,128)S(1)} %get-tuple-element.51.reach_ref, f32[256,1024]{1,0:T(8,128)S(1)} %get-tuple-element.52.sx_ref, bf16[256,256]{1,0:T(8,128)(2,1)S(1)} %bitcast.23, ...), custom_call_target="tpu_custom_call" | custom-call | flops 67108864 | bytes 5242880 | tf_op jit(solution)/shard_map/final/pallas_call | solution.py:737
  56.6 0.5 collective-permute-start.12
  57.1 1.1 %collective-permute-start.11 = (f32[3,1024]{1,0:T(4,128)S(1)}, f32[3,1024]{1,0:T(4,128)S(1)}, u32[]{:S(2)}, u32[]{:S(2)}) collective-permute-start(f32[3,1024]{1,0:T(4,128)S(1)} %get-tuple-element.59), channel_id=1, source_target_pairs={{0,16},{4,20},{8,24},{12,28},{16,0},{20,4},{24,8},{28,12},{1,17},{... | collective-permute-start | bytes 36872 | tf_op jit(solution)/shard_map/ppermute | solution.py:537
  58.2 1.9 %collective-permute-start.10 = (f32[3,1024]{1,0:T(4,128)S(1)}, f32[3,1024]{1,0:T(4,128)S(1)}, u32[]{:S(2)}, u32[]{:S(2)}) collective-permute-start(f32[3,1024]{1,0:T(4,128)S(1)} %get-tuple-element.59), channel_id=1, source_target_pairs={{0,4},{4,0},{8,12},{12,8},{16,20},{20,16},{24,28},{28,24},{1,5},{5... | collective-permute-start | bytes 36872 | tf_op jit(solution)/shard_map/ppermute | solution.py:537
  60.1 1.1 %collective-permute-done.12 = f32[3,1024]{1,0:T(4,128)S(1)} collective-permute-done((f32[3,1024]{1,0:T(4,128)S(1)}, f32[3,1024]{1,0:T(4,128)S(1)}, u32[]{:S(2)}, u32[]{:S(2)}) %collective-permute-start.12) | collective-permute-done | bytes 12320 | tf_op jit(solution)/shard_map/ppermute | solution.py:537
  61.3 0.0 collective-permute-done.11
  61.3 0.7 %collective-permute-done.10 = f32[3,1024]{1,0:T(4,128)S(1)} collective-permute-done((f32[3,1024]{1,0:T(4,128)S(1)}, f32[3,1024]{1,0:T(4,128)S(1)}, u32[]{:S(2)}, u32[]{:S(2)}) %collective-permute-start.10) | collective-permute-done | bytes 12320 | tf_op jit(solution)/shard_map/ppermute | solution.py:537
  62.0 1.7 %collective-permute-start.13 = (f32[3,1024]{1,0:T(4,128)S(1)}, f32[3,1024]{1,0:T(4,128)S(1)}, u32[]{:S(2)}, u32[]{:S(2)}) collective-permute-start(f32[3,1024]{1,0:T(4,128)S(1)} %add_add_fusion.a_ref), channel_id=1, source_target_pairs={{0,8},{4,12},{8,0},{12,4},{16,24},{20,28},{24,16},{28,20},{1,9},{5... | collective-permute-start | bytes 36872 | tf_op jit(solution)/shard_map/ppermute | solution.py:537
  63.7 1.0 %writing.2 = bf16[256,2048]{1,0:T(8,128)(2,1)} custom-call(bf16[256,1024]{1,0:T(8,128)(2,1)S(1)} %attention.2.refs_0_.teacher_ref, bf16[256,1024]{1,0:T(8,128)(2,1)S(1)} %attention.3.refs_1_.teacher_ref), custom_call_target="tpu_custom_call" | custom-call | bytes 2097152 | tf_op jit(solution)/shard_map/writing/pallas_call | solution.py:573
  64.7 1.0 %writing.3 = bf16[256,2048]{1,0:T(8,128)(2,1)} custom-call(bf16[256,1024]{1,0:T(8,128)(2,1)S(1)} %get-tuple-element.50.refs_0_, bf16[256,1024]{1,0:T(8,128)(2,1)S(1)} %get-tuple-element.58.refs_1_), custom_call_target="tpu_custom_call" | custom-call | bytes 2097152 | tf_op jit(solution)/shard_map/writing/pallas_call | solution.py:573
  65.7 1.0 %collective-permute-done.13.b_ref = f32[3,1024]{1,0:T(4,128)S(1)} collective-permute-done((f32[3,1024]{1,0:T(4,128)S(1)}, f32[3,1024]{1,0:T(4,128)S(1)}, u32[]{:S(2)}, u32[]{:S(2)}) %collective-permute-start.13) | collective-permute-done | bytes 12320 | tf_op jit(solution)/shard_map/ppermute | solution.py:537
  66.7 0.6 closing.1
  (9 shorter events, 0.1 us)
Async XLA Ops:
  0.6 8.2 %copy-start.2 = (bf16[1,256,256]{2,1,0:T(8,128)(2,1)S(1)}, bf16[1,256,256]{2,1,0:T(8,128)(2,1)}, u32[]{:S(2)}) copy-start(bf16[1,256,256]{2,1,0:T(8,128)(2,1)} %param.14) | copy-start | bytes 393220
  0.6 8.2 %copy-start.3 = (bf16[1,256,256]{2,1,0:T(8,128)(2,1)S(1)}, bf16[1,256,256]{2,1,0:T(8,128)(2,1)}, u32[]{:S(2)}) copy-start(bf16[1,256,256]{2,1,0:T(8,128)(2,1)} %param.15) | copy-start | bytes 393220
  3.8 12.4 %collective-permute-start.2 = (bf16[144,1024]{1,0:T(8,128)(2,1)S(1)}, bf16[144,1024]{1,0:T(8,128)(2,1)S(1)}, u32[]{:S(2)}, u32[]{:S(2)}) collective-permute-start(bf16[144,1024]{1,0:T(8,128)(2,1)S(1)} %get-tuple-element.36), channel_id=1, source_target_pairs={{0,4},{12,8},{1,5},{13,9},{2,6},{14,10},{3,7},{15,11},{16,20},{28,... | collective-permute-start | bytes 884744 | tf_op jit(solution)/shard_map/ppermute | solution.py:665
  8.9 11.0 %collective-permute-start.1 = (bf16[256,512]{1,0:T(8,128)(2,1)S(1)}, bf16[256,512]{1,0:T(8,128)(2,1)S(1)}, u32[]{:S(2)}, u32[]{:S(2)}) collective-permute-start(bf16[256,512]{1,0:T(8,128)(2,1)S(1)} %pack.1), channel_id=1, source_target_pairs={{4,8},{8,4},{5,9},{9,5},{6,10},{10,6},{7,11},{11,7},{20,24},{24,20... | collective-permute-start | bytes 786440 | tf_op jit(solution)/shard_map/ppermute | solution.py:667
  9.6 15.9 %collective-permute-start = (bf16[256,512]{1,0:T(8,128)(2,1)S(1)}, bf16[256,512]{1,0:T(8,128)(2,1)S(1)}, u32[]{:S(2)}, u32[]{:S(2)}) collective-permute-start(bf16[256,512]{1,0:T(8,128)(2,1)S(1)} %pack.1), channel_id=1, source_target_pairs={{0,4},{12,8},{4,0},{8,12},{1,5},{13,9},{5,1},{9,13},{2,6},{14,10},... | collective-permute-start | bytes 786440 | tf_op jit(solution)/shard_map/ppermute | solution.py:666
  16.2 9.9 %collective-permute-start.6 = (bf16[144,1024]{1,0:T(8,128)(2,1)S(1)}, bf16[144,1024]{1,0:T(8,128)(2,1)S(1)}, u32[]{:S(2)}, u32[]{:S(2)}) collective-permute-start(bf16[144,1024]{1,0:T(8,128)(2,1)S(1)} %chain.4), channel_id=1, source_target_pairs={{4,8},{8,4},{5,9},{9,5},{6,10},{10,6},{7,11},{11,7},{20,24},{24,20... | collective-permute-start | bytes 884744 | tf_op jit(solution)/shard_map/ppermute | solution.py:672
  20.0 10.2 %collective-permute-start.4 = (bf16[144,1024]{1,0:T(8,128)(2,1)S(1)}, bf16[144,1024]{1,0:T(8,128)(2,1)S(1)}, u32[]{:S(2)}, u32[]{:S(2)}) collective-permute-start(bf16[144,1024]{1,0:T(8,128)(2,1)S(1)} %merge.1), channel_id=1, source_target_pairs={{0,4},{12,8},{4,0},{8,12},{1,5},{13,9},{5,1},{9,13},{2,6},{14,10},... | collective-permute-start | bytes 884744 | tf_op jit(solution)/shard_map/ppermute | solution.py:686
  25.5 0.7 %collective-permute-start.3 = (bf16[256,512]{1,0:T(8,128)(2,1)S(1)}, bf16[256,512]{1,0:T(8,128)(2,1)S(1)}, u32[]{:S(2)}, u32[]{:S(2)}) collective-permute-start(bf16[256,512]{1,0:T(8,128)(2,1)S(1)} %collective-permute-done.refs_0_), channel_id=1, source_target_pairs={{4,8},{8,4},{5,9},{9,5},{6,10},{10,6},{7,11},{11,7},{20,24},{24,20... | collective-permute-start | bytes 786440 | tf_op jit(solution)/shard_map/ppermute | solution.py:676
  30.2 15.2 %copy-start = (bf16[1,256,2048]{2,1,0:T(8,128)(2,1)S(1)}, bf16[1,256,2048]{2,1,0:T(8,128)(2,1)}, u32[]{:S(2)}) copy-start(bf16[1,256,2048]{2,1,0:T(8,128)(2,1)} %param.13) | copy-start | bytes 3145732
  30.2 3.4 %collective-permute-start.8 = (bf16[144,1024]{1,0:T(8,128)(2,1)S(1)}, bf16[144,1024]{1,0:T(8,128)(2,1)S(1)}, u32[]{:S(2)}, u32[]{:S(2)}) collective-permute-start(bf16[144,1024]{1,0:T(8,128)(2,1)S(1)} %chain.6), channel_id=1, source_target_pairs={{4,8},{8,4},{5,9},{9,5},{6,10},{10,6},{7,11},{11,7},{20,24},{24,20... | collective-permute-start | bytes 884744 | tf_op jit(solution)/shard_map/ppermute | solution.py:711
  31.0 14.4 %collective-permute-start.5 = (bf16[256,512]{1,0:T(8,128)(2,1)S(1)}, bf16[256,512]{1,0:T(8,128)(2,1)S(1)}, u32[]{:S(2)}, u32[]{:S(2)}) collective-permute-start(bf16[256,512]{1,0:T(8,128)(2,1)S(1)} %collective-permute-done.3.refs_2_), channel_id=1, source_target_pairs={{4,0},{8,12},{5,1},{9,13},{6,2},{10,14},{7,3},{11,15},{20,16},{24,... | collective-permute-start | bytes 786440 | tf_op jit(solution)/shard_map/ppermute | solution.py:688
  32.3 19.3 %collective-permute-start.7 = (bf16[144,1024]{1,0:T(8,128)(2,1)S(1)}, bf16[144,1024]{1,0:T(8,128)(2,1)S(1)}, u32[]{:S(2)}, u32[]{:S(2)}) collective-permute-start(bf16[144,1024]{1,0:T(8,128)(2,1)S(1)} %chain.5), channel_id=1, source_target_pairs={{8,12},{4,0},{9,13},{5,1},{10,14},{6,2},{11,15},{7,3},{24,28},{20,... | collective-permute-start | bytes 884744 | tf_op jit(solution)/shard_map/ppermute | solution.py:711
  33.6 11.8 %copy-start.4 = (s32[1,1024]{1,0:T(1,128)S(1)}, s32[1,1024]{1,0:T(1,128)}, u32[]{:S(2)}) copy-start(s32[1,1024]{1,0:T(1,128)} %docs_ref.9) | copy-start | bytes 12292
  33.7 21.2 %collective-permute-start.9 = (bf16[144,1024]{1,0:T(8,128)(2,1)S(1)}, bf16[144,1024]{1,0:T(8,128)(2,1)S(1)}, u32[]{:S(2)}, u32[]{:S(2)}) collective-permute-start(bf16[144,1024]{1,0:T(8,128)(2,1)S(1)} %chain.7), channel_id=1, source_target_pairs={{8,12},{4,0},{9,13},{5,1},{10,14},{6,2},{11,15},{7,3},{24,28},{20,... | collective-permute-start | bytes 884744 | tf_op jit(solution)/shard_map/ppermute | solution.py:711
  48.2 3.4 %copy-start.1 = (bf16[1,256,256]{2,1,0:T(8,128)(2,1)S(1)}, bf16[1,256,256]{2,1,0:T(8,128)(2,1)}, u32[]{:S(2)}) copy-start(bf16[1,256,256]{2,1,0:T(8,128)(2,1)} %param.20) | copy-start | bytes 393220
  48.2 3.4 %copy-start.5 = (f32[2048]{0:T(1024)S(1)}, f32[2048]{0:T(1024)}, u32[]{:S(2)}) copy-start(f32[2048]{0:T(1024)} %param.25) | copy-start | bytes 24580
  56.6 4.7 %collective-permute-start.12 = (f32[3,1024]{1,0:T(4,128)S(1)}, f32[3,1024]{1,0:T(4,128)S(1)}, u32[]{:S(2)}, u32[]{:S(2)}) collective-permute-start(f32[3,1024]{1,0:T(4,128)S(1)} %get-tuple-element.59), channel_id=1, source_target_pairs={{0,20},{4,16},{8,28},{12,24},{16,4},{20,0},{24,12},{28,8},{1,21},{... | collective-permute-start | bytes 36872 | tf_op jit(solution)/shard_map/ppermute | solution.py:537
  57.1 4.2 %collective-permute-start.11 = (f32[3,1024]{1,0:T(4,128)S(1)}, f32[3,1024]{1,0:T(4,128)S(1)}, u32[]{:S(2)}, u32[]{:S(2)}) collective-permute-start(f32[3,1024]{1,0:T(4,128)S(1)} %get-tuple-element.59), channel_id=1, source_target_pairs={{0,16},{4,20},{8,24},{12,28},{16,0},{20,4},{24,8},{28,12},{1,17},{... | collective-permute-start | bytes 36872 | tf_op jit(solution)/shard_map/ppermute | solution.py:537
  58.2 3.7 %collective-permute-start.10 = (f32[3,1024]{1,0:T(4,128)S(1)}, f32[3,1024]{1,0:T(4,128)S(1)}, u32[]{:S(2)}, u32[]{:S(2)}) collective-permute-start(f32[3,1024]{1,0:T(4,128)S(1)} %get-tuple-element.59), channel_id=1, source_target_pairs={{0,4},{4,0},{8,12},{12,8},{16,20},{20,16},{24,28},{28,24},{1,5},{5... | collective-permute-start | bytes 36872 | tf_op jit(solution)/shard_map/ppermute | solution.py:537
  62.0 4.7 %collective-permute-start.13 = (f32[3,1024]{1,0:T(4,128)S(1)}, f32[3,1024]{1,0:T(4,128)S(1)}, u32[]{:S(2)}, u32[]{:S(2)}) collective-permute-start(f32[3,1024]{1,0:T(4,128)S(1)} %add_add_fusion.a_ref), channel_id=1, source_target_pairs={{0,8},{4,12},{8,0},{12,4},{16,24},{20,28},{24,16},{28,20},{1,9},{5... | collective-permute-start | bytes 36872 | tf_op jit(solution)/shard_map/ppermute | solution.py:537

commit v9 on v7

--- a/solution.py
+++ b/solution.py
@@ -453,7 +453,7 @@
     gain_acc[...] = jnp.zeros_like(gain_acc)
     skip_acc[...] = jnp.zeros_like(skip_acc)
 
-    @pl.loop(0, rows // step, unroll=2)
+    @pl.loop(0, rows // step, unroll=4)
     def _(k):
         sl = pl.ds(pl.multiple_of(k * step, step), step)
         totals = [jnp.zeros((step, tile), F32)] * 3
@@ -478,7 +478,7 @@
     sums[:, :tile] = jnp.broadcast_to(scale, (rows, tile))
     sums[:, tile : 2 * tile] = jnp.broadcast_to(mean, (rows, tile))
 
-    @pl.loop(0, rows // step, unroll=2)
+    @pl.loop(0, rows // step, unroll=4)
     def _(k):
         sl = pl.ds(pl.multiple_of(k * step, step), step)
         scale = sums[sl, :tile]
@@ -500,15 +500,12 @@
     matrix = jnp.where(row == lane // P_SIZE + g * (width // P_SIZE), 1.0, 0.0).astype(BF16)
     hi, lo = parts(skip_acc[...])
     by_head = jnp.sum(dot_nt(hi, matrix) + dot_nt(lo, matrix), axis=0, keepdims=True)
-    by_lane = jnp.sum(gain_acc[...], axis=0, keepdims=True)
+    grad_ref[...] = jnp.zeros_like(grad_ref)
     if g:
-        by_head += before[0, groups : groups + 1, :tile]
-    for d in range(grad_ref.shape[0]):
-        if g:
-            grad_ref[d, :g, :] = before[0, :g, :]
-        grad_ref[d, g : g + 1, :] = by_lane
-        grad_ref[d, groups : groups + 1, :] = jnp.zeros((1, width), F32)
-        grad_ref[d, groups : groups + 1, :tile] = by_head
+        grad_ref[:g, :] = before[:g, :]
+        by_head += before[groups : groups + 1, :tile]
+    grad_ref[g : g + 1, :] = jnp.sum(gain_acc[...], axis=0, keepdims=True)
+    grad_ref[groups : groups + 1, :tile] = by_head
 
 
 def writing_kernel(*refs):
@@ -524,14 +521,18 @@
         move.wait()
 
 
-def closing_kernel(all_ref, gain_ref, skip_ref):
-    total = all_ref[0]
-    for d in range(1, all_ref.shape[0]):
-        total += all_ref[d]
+def closing_kernel(a_ref, b_ref, gain_ref, skip_ref):
+    total = a_ref[...] + b_ref[...]
     groups, width = total.shape[0] - 1, total.shape[1]
     for g in range(groups):
         gain_ref[:, g * width : (g + 1) * width] = total[g : g + 1, :]
     skip_ref[...] = total[groups : groups + 1, : skip_ref.shape[1]]
+
+
+def exchange(part, shift):
+    axes = ("dp", "ctx")
+    size = lax.axis_size(axes)
+    return lax.ppermute(part, axes, [(d, d ^ shift) for d in range(size)])
 
 
 def body(
@@ -559,7 +560,6 @@
     width = features // groups
     length = doc_ids.shape[1]
     others = count - 1
-    members = lax.axis_size("dp") * count
     loss_scale = 1.0 / (lax.axis_size("dp") * count * rows)
     x, gate, bmat, cmat = inputs[0], gate_input[0], b_input[0], c_input[0]
     struct = jax.ShapeDtypeStruct
@@ -641,6 +641,20 @@
 
     send = list(send)
     got = [[] for _ in range(groups)]
+    def passed_on(g, stage):
+        return pl.pallas_call(
+            functools.partial(chain_kernel, count, stage),
+            out_shape=payload,
+            in_specs=[VMEM] * 4,
+            out_specs=VMEM,
+            compiler_params=params(4),
+            cost_estimate=pl.CostEstimate(flops=16384 * N * width, bytes_accessed=0, transcendentals=0),
+            name="chain",
+        )(got[g][-1], f_parts[g], b_parts[g], dec[g])
+
+    def stage_pairs(stage):
+        return [(stage - 1, stage), (count - stage, count - stage - 1)]
+
     if count == 4:
         inward, outward, across = [(0, 1), (3, 2)], [(1, 0), (2, 3)], [(1, 2), (2, 1)]
         near = lax.ppermute(kv, "ctx", inward + outward)
@@ -667,7 +681,7 @@
         for _ in range(others):
             kv_got.append(lax.ppermute(kv_got[-1], "ctx", ring_pairs))
         kv_got = kv_got[1:]
-    stack = 4 if per_kv % 4 == 0 and count <= 4 else 1
+    stack = 2 if per_kv % 2 == 0 and count <= 4 else 1
     targets = [
         pl.pallas_call(
             functools.partial(attention_kernel, count, per_kv, stack, g),
@@ -683,7 +697,7 @@
             ],
             compiler_params=params(24),
             cost_estimate=cost(
-                4 * (2 * count + 1) * stretch * stretch * per_kv * DH, 8 * rows * per_kv * DH
+                32 * (2 * count + 1) * stretch * stretch * per_kv * DH, 8 * rows * per_kv * DH
             ),
             name="attention",
         )(doc_ids, queries[0], keys[0], values[0], *kv_got)
@@ -691,29 +705,19 @@
     ]
     for r in range(1, count):
         for g in range(groups):
+            if len(got[g]) >= r:
+                continue
+            if r == 3 and g == groups - 1:
+                got[g][-1], targets[0] = lax.optimization_barrier((got[g][-1], targets[0]))
             if r > 1:
-                send[g] = pl.pallas_call(
-                    functools.partial(chain_kernel, count, r - 1),
-                    out_shape=payload,
-                    in_specs=[VMEM] * 4,
-                    out_specs=VMEM,
-                    compiler_params=params(4),
-                    cost_estimate=cost(16384 * N * width, 8 * N * width),
-                    name="chain",
-                )(got[g][-1], f_parts[g], b_parts[g], dec[g])
-            if len(got[g]) < r:
-                pairs = [(r - 1, r), (count - r, count - r - 1)]
-                got[g].append(lax.ppermute(send[g], "ctx", pairs))
-
+                send[g] = passed_on(g, r - 1)
+            got[g].append(lax.ppermute(send[g], "ctx", stage_pairs(r)))
     normed, grads = [], None
     for g in range(groups):
         more = [] if grads is None else [grads]
         made, grads = pl.pallas_call(
             functools.partial(final_kernel, count, g, groups, loss_scale),
-            out_shape=(
-                struct((rows, width), BF16),
-                struct((members if g == groups - 1 else 1, groups + 1, width), F32),
-            ),
+            out_shape=(struct((rows, width), BF16), struct((groups + 1, width), F32)),
             in_specs=[VMEM] * (8 + others + len(more)),
             out_specs=(VMEM,) * 2,
             scratch_shapes=[
@@ -740,15 +744,22 @@
         )
         normed.append(made)
     teacher, student = write(*targets), write(*normed)
-    gathered = lax.all_to_all(grads, ("dp", "ctx"), 0, 0)
+    partner = exchange(grads, 1)
+    if lax.axis_size("dp") == 2:
+        grads = (grads + partner) + (exchange(grads, count) + exchange(grads, count + 1))
+    else:
+        grads = grads + partner
+    shifts = [1 << k for k in range(1, count.bit_length() - 1)]
+    for shift in shifts[:-1]:
+        grads = grads + exchange(grads, shift)
     grad_gain, grad_skip = pl.pallas_call(
         closing_kernel,
         out_shape=(struct((1, features), F32), struct((1, heads), F32)),
-        in_specs=[VMEM],
+        in_specs=[VMEM] * 2,
         out_specs=(VMEM,) * 2,
-        compiler_params=params(4),
+        compiler_params=params(2),
         name="closing",
-    )(gathered)
+    )(grads, exchange(grads, shifts[-1]))
     return (teacher[None], student[None], grad_gain[0], grad_skip[0])
 
 

time: 71.7 us -> 68.5 us (0.955)
  waiting for transfers between devices: 29 us -> 24.3 us
  starting transfers between devices: 21.5 us -> 23.4 us
    all_to_all x1 -> x0, waiting for transfers between devices: 5.54 us -> none  [body(): gathered = lax.all_to_all(grads, ('dp', 'ctx'), 0, 0)]
    all_to_all x1 -> x0, starting transfers between devices: 4.84 us -> none  [body(): gathered = lax.all_to_all(grads, ('dp', 'ctx'), 0, 0)]
    ppermute x5 -> x9, starting transfers between devices: 11.9 us -> 16.3 us  [the longest x5 9.24 us: body(): got[g].append(lax.ppermute(send[g], 'ctx', stage_pairs(r)))]
    ppermute x1, waiting for transfers between devices: 6.63 us -> 3.55 us  [body(): near = lax.ppermute(kv, 'ctx', inward + outward)]
    ppermute x1, waiting for transfers between devices: 11 us -> 13.9 us  [body(): farther = lax.ppermute(beyond, 'ctx', outward)]
    ppermute x1, starting transfers between devices: 0.07 us -> 2.24 us  [body(): near = lax.ppermute(kv, 'ctx', inward + outward)]
    ppermute x5 -> x9, waiting for transfers between devices: 2.3 us -> 4.45 us  [the longest x5 2.56 us: body(): got[g].append(lax.ppermute(send[g], 'ctx', stage_pairs(r)))]
    ppermute x1, waiting for transfers between devices: 3.45 us -> 2.46 us  [body(): far = lax.ppermute(send[-1], 'ctx', inward + outward)]
  transfers between devices with their start and end apart: 11 -> 14, of which waited for: 6 -> 8; matrix products, arithmetic and copies ran while one was open for 0% -> 0% of each run, Pallas kernels for 19% -> 21%
where the time goes in v9:
time: 68.5 us; the launch traced here: 68.2 us
  waiting for transfers between devices  24.3 us (35%)
  starting transfers between devices  23.4 us (34%)
  Pallas kernels  19.5 us (28%)
  between operations  0.89 us (1%)
    ppermute x1, waiting for transfers between devices, body(): farther = lax.ppermute(beyond, 'ctx', outward)  13.9 us
    ppermute x5, starting transfers between devices, body(): got[g].append(lax.ppermute(send[g], 'ctx', stage_pairs(r)))  9.24 us
    ppermute x4, starting transfers between devices, exchange(): return lax.ppermute(part, axes, [(d, d ^ shift) for d in range(size)])  7.07 us
    pallas_call x2, Pallas kernels, body(): pl.pallas_call(functools.partial(attention_kernel, count, per_kv, stack,...  5.97 us
    pallas_call x1, Pallas kernels, body(): pl.pallas_call(functools.partial(local_kernel, count, groups), out_shape=...  4.19 us
    ppermute x1, waiting for transfers between devices, body(): near = lax.ppermute(kv, 'ctx', inward + outward)  3.55 us
    pallas_call x2, Pallas kernels, body(): pl.pallas_call(functools.partial(final_kernel, count, g, groups, loss_sca...  3.53 us
    pallas_call x1, Pallas kernels, body(): pl.pallas_call(functools.partial(opening_kernel, count, groups), out_shap...  3.14 us
  transfers between devices with their start and end apart: 14, of which 8 were waited for; matrix products, arithmetic and copies ran while one was open for 0% of the time, Pallas kernels for 21%

profile of v9, /device:TPU:0, one launch (start us, length us, event | category | flops | bytes accessed | tf_op | source)
XLA Modules:
  0.0 68.2 jit_solution(6376998769572477459)
XLA Ops:
  0.6 0.0 copy-start.1
  0.6 0.0 copy-start.2
  0.7 3.1 %opening.1 = (f32[32,256]{1,0:T(8,128)S(1)}, bf16[256,1024]{1,0:T(8,128)(2,1)S(1)}, bf16[256,1024]{1,0:T(8,128)(2,1)S(1)}, f32[8,1024]{1,0:T(8,128)S(1)}, f32[8,...) custom-call(s32[1,1024]{1,0:T(1,128)} %docs_ref.7, ...), custom_call_target="tpu_custom_call" | custom-call | flops 268435456 | bytes 4194304 | tf_op jit(solution)/shard_map/opening/pallas_call | solution.py:584
  3.8 5.0 %collective-permute-start.6 = (bf16[144,1024]{1,0:T(8,128)(2,1)S(1)}, bf16[144,1024]{1,0:T(8,128)(2,1)S(1)}, u32[]{:S(2)}, u32[]{:S(2)}) collective-permute-start(bf16[144,1024]{1,0:T(8,128)(2,1)S(1)} %get-tuple-element.60), channel_id=1, source_target_pairs={{0,4},{12,8},{1,5},{13,9},{2,6},{14,10},{3,7},{15,11},{16,20},{28,... | collective-permute-start | bytes 884744 | tf_op jit(solution)/shard_map/ppermute | solution.py:714
  8.8 0.0 copy-done.1
  8.9 0.0 copy-done.2
  8.9 0.7 collective-permute-start
  9.6 2.2 %collective-permute-start.3 = (bf16[256,512]{1,0:T(8,128)(2,1)S(1)}, bf16[256,512]{1,0:T(8,128)(2,1)S(1)}, u32[]{:S(2)}, u32[]{:S(2)}) collective-permute-start(bf16[256,512]{1,0:T(8,128)(2,1)S(1)} %pack.1), channel_id=1, source_target_pairs={{0,4},{12,8},{4,0},{8,12},{1,5},{13,9},{5,1},{9,13},{2,6},{14,10},... | collective-permute-start | bytes 786440 | tf_op jit(solution)/shard_map/ppermute | solution.py:660
  11.8 4.2 %local.1 = (f32[256,1024]{1,0:T(8,128)S(1)}, f32[256,1024]{1,0:T(8,128)S(1)}, f32[256,1024]{1,0:T(8,128)S(1)}, f32[256,1024]{1,0:T(8,128)S(1)}, f32[256,1024]{1,0:T(8,128)S(1)}, /*index=5*/f32[256,1024]{1,0:T(8,128)S(1)}) custom-call(s32[1,1024]{1,0:T(1,128)} %docs_ref.7, bf16[256,2048]{1,0:T(8,128)(2,1)} %bitcast.32, bf16[256,2048]{1,0:T(8,128)(2,1)} %bitcast.33, ...), custom_call_target="tpu_custom_call" | custom-call | flops 134217728 | bytes 8388608 | tf_op jit(solution)/shard_map/local/pallas_call | solution.py:623
  16.0 0.0 collective-permute-done.kv_ref.refs_1_
  16.1 2.2 %collective-permute-start.1 = (bf16[144,1024]{1,0:T(8,128)(2,1)S(1)}, bf16[144,1024]{1,0:T(8,128)(2,1)S(1)}, u32[]{:S(2)}, u32[]{:S(2)}) collective-permute-start(bf16[144,1024]{1,0:T(8,128)(2,1)S(1)} %merge.1), channel_id=1, source_target_pairs={{0,4},{12,8},{4,0},{8,12},{1,5},{13,9},{5,1},{9,13},{2,6},{14,10},... | collective-permute-start | bytes 884744 | tf_op jit(solution)/shard_map/ppermute | solution.py:673
  18.3 3.6 %collective-permute-done.3.refs_0_ = bf16[256,512]{1,0:T(8,128)(2,1)S(1)} collective-permute-done((bf16[256,512]{1,0:T(8,128)(2,1)S(1)}, bf16[256,512]{1,0:T(8,128)(2,1)S(1)}, u32[]{:S(2)}, u32[]{:S(2)}) %collective-permute-start.3) | collective-permute-done | bytes 262176 | tf_op jit(solution)/shard_map/ppermute | solution.py:660
  21.9 0.7 collective-permute-start.4
  22.5 0.0 collective-permute-done.6.got_ref.refs_0_
  22.6 0.7 collective-permute-start.7
  23.3 0.0 collective-permute-done.4.refs_2_
  23.3 1.3 %collective-permute-start.5 = (bf16[256,512]{1,0:T(8,128)(2,1)S(1)}, bf16[256,512]{1,0:T(8,128)(2,1)S(1)}, u32[]{:S(2)}, u32[]{:S(2)}) collective-permute-start(bf16[256,512]{1,0:T(8,128)(2,1)S(1)} %collective-permute-done.4.refs_2_), channel_id=1, source_target_pairs={{4,0},{8,12},{5,1},{9,13},{6,2},{10,14},{7,3},{11,15},{20,16},{24,... | collective-permute-start | bytes 786440 | tf_op jit(solution)/shard_map/ppermute | solution.py:675
  24.6 2.5 %collective-permute-done.1.got_ref.refs_3_.refs_0_ = bf16[144,1024]{1,0:T(8,128)(2,1)S(1)} collective-permute-done((bf16[144,1024]{1,0:T(8,128)(2,1)S(1)}, bf16[144,1024]{1,0:T(8,128)(2,1)S(1)}, u32[]{:S(2)}, u32[]{:S(2)}) %collective-permute-start.1) | collective-permute-done | bytes 294944 | tf_op jit(solution)/shard_map/ppermute | solution.py:673
  27.0 0.0 copy-start.4
  27.0 0.8 %collective-permute-start.2 = (bf16[144,1024]{1,0:T(8,128)(2,1)S(1)}, bf16[144,1024]{1,0:T(8,128)(2,1)S(1)}, u32[]{:S(2)}, u32[]{:S(2)}) collective-permute-start(bf16[144,1024]{1,0:T(8,128)(2,1)S(1)} %chain.4), channel_id=1, source_target_pairs={{4,8},{8,4},{5,9},{9,5},{6,10},{10,6},{7,11},{11,7},{20,24},{24,20... | collective-permute-start | bytes 884744 | tf_op jit(solution)/shard_map/ppermute | solution.py:714
  27.8 0.0 collective-permute-done.7.got_ref.refs_1_
  27.9 1.3 %collective-permute-start.8 = (bf16[144,1024]{1,0:T(8,128)(2,1)S(1)}, bf16[144,1024]{1,0:T(8,128)(2,1)S(1)}, u32[]{:S(2)}, u32[]{:S(2)}) collective-permute-start(bf16[144,1024]{1,0:T(8,128)(2,1)S(1)} %chain.6), channel_id=1, source_target_pairs={{8,12},{4,0},{9,13},{5,1},{10,14},{6,2},{11,15},{7,3},{24,28},{20,... | collective-permute-start | bytes 884744 | tf_op jit(solution)/shard_map/ppermute | solution.py:714
  29.2 13.9 %collective-permute-done.5.refs_4_ = bf16[256,512]{1,0:T(8,128)(2,1)S(1)} collective-permute-done((bf16[256,512]{1,0:T(8,128)(2,1)S(1)}, bf16[256,512]{1,0:T(8,128)(2,1)S(1)}, u32[]{:S(2)}, u32[]{:S(2)}) %collective-permute-start.5) | collective-permute-done | bytes 262176 | tf_op jit(solution)/shard_map/ppermute | solution.py:675
  43.0 0.0 copy-done.4
  43.0 0.0 copy-done.5
  43.0 3.0 %attention.2.refs_0_.teacher_ref = bf16[256,1024]{1,0:T(8,128)(2,1)S(1)} custom-call(s32[1,1024]{1,0:T(1,128)S(1)} %copy-done.4, bf16[256,2048]{1,0:T(8,128)(2,1)S(1)} %bitcast.29, bf16[256,256]{1,0:T(8,128)(2,1)S(1)} %bitcast.22, bf16[256,256]{1,0:T(8,128)(2,1)S(1)} %bitcast.25, bf16[256,512]{1,0:T(8,128)(2,1)S(1)} %collective-permute-done.3.refs_0_, ...), custom_call_target="tpu_custom_call" | custom-call | flops 4831838208 | bytes 2097152 | tf_op jit(solution)/shard_map/attention/pallas_call | solution.py:686
  46.0 0.0 collective-permute-done.2.got_ref.refs_1_
  46.1 0.0 copy-start
  46.1 0.0 copy-start.3
  46.1 1.4 %collective-permute-start.9 = (bf16[144,1024]{1,0:T(8,128)(2,1)S(1)}, bf16[144,1024]{1,0:T(8,128)(2,1)S(1)}, u32[]{:S(2)}, u32[]{:S(2)}) collective-permute-start(bf16[144,1024]{1,0:T(8,128)(2,1)S(1)} %chain.7), channel_id=1, source_target_pairs={{8,12},{4,0},{9,13},{5,1},{10,14},{6,2},{11,15},{7,3},{24,28},{20,... | collective-permute-start | bytes 884744 | tf_op jit(solution)/shard_map/ppermute | solution.py:714
  47.5 3.0 %attention.3.refs_1_.teacher_ref = bf16[256,1024]{1,0:T(8,128)(2,1)S(1)} custom-call(s32[1,1024]{1,0:T(1,128)S(1)} %copy-done.4, bf16[256,2048]{1,0:T(8,128)(2,1)S(1)} %bitcast.30, bf16[256,256]{1,0:T(8,128)(2,1)S(1)} %bitcast.23, bf16[256,256]{1,0:T(8,128)(2,1)S(1)} %bitcast.26, bf16[256,512]{1,0:T(8,128)(2,1)S(1)} %collective-permute-done.3.refs_0_, ...), custom_call_target="tpu_custom_call" | custom-call | flops 4831838208 | bytes 2097152 | tf_op jit(solution)/shard_map/attention/pallas_call | solution.py:686
  50.5 0.1 collective-permute-done.8.refs_2_
  50.7 0.0 copy-done
  50.7 0.0 copy-done.3
  50.7 1.8 %final.2 = (bf16[256,1024]{1,0:T(8,128)(2,1)S(1)}, f32[3,1024]{1,0:T(4,128)S(1)}) custom-call(f32[256,1024]{1,0:T(8,128)S(1)} %get-tuple-element.55.pre_ref, f32[256,1024]{1,0:T(8,128)S(1)} %get-tuple-element.56.reach_ref, f32[256,1024]{1,0:T(8,128)S(1)} %get-tuple-element.57.sx_ref, bf16[256,256]{1,0:T(8,128)(2,1)S(1)} %bitcast.19, ...), custom_call_target="tpu_custom_call" | custom-call | flops 67108864 | bytes 5242880 | tf_op jit(solution)/shard_map/final/pallas_call | solution.py:718
  52.4 2.4 %collective-permute-done.9.refs_2_ = bf16[144,1024]{1,0:T(8,128)(2,1)S(1)} collective-permute-done((bf16[144,1024]{1,0:T(8,128)(2,1)S(1)}, bf16[144,1024]{1,0:T(8,128)(2,1)S(1)}, u32[]{:S(2)}, u32[]{:S(2)}) %collective-permute-start.9) | collective-permute-done | bytes 294944 | tf_op jit(solution)/shard_map/ppermute | solution.py:714
  54.8 1.8 %final.3 = (bf16[256,1024]{1,0:T(8,128)(2,1)S(1)}, f32[3,1024]{1,0:T(4,128)S(1)}) custom-call(f32[256,1024]{1,0:T(8,128)S(1)} %get-tuple-element.63.pre_ref, f32[256,1024]{1,0:T(8,128)S(1)} %get-tuple-element.64.reach_ref, f32[256,1024]{1,0:T(8,128)S(1)} %get-tuple-element.65.sx_ref, bf16[256,256]{1,0:T(8,128)(2,1)S(1)} %bitcast.20, ...), custom_call_target="tpu_custom_call" | custom-call | flops 67108864 | bytes 5242880 | tf_op jit(solution)/shard_map/final/pallas_call | solution.py:718
  56.6 1.2 %collective-permute-start.12 = (f32[3,1024]{1,0:T(4,128)S(1)}, f32[3,1024]{1,0:T(4,128)S(1)}, u32[]{:S(2)}, u32[]{:S(2)}) collective-permute-start(f32[3,1024]{1,0:T(4,128)S(1)} %get-tuple-element.69), channel_id=1, source_target_pairs={{0,20},{4,16},{8,28},{12,24},{16,4},{20,0},{24,12},{28,8},{1,21},{... | collective-permute-start | bytes 36872 | tf_op jit(solution)/shard_map/ppermute | solution.py:535
  57.8 0.5 collective-permute-start.11
  58.3 1.8 %collective-permute-start.10 = (f32[3,1024]{1,0:T(4,128)S(1)}, f32[3,1024]{1,0:T(4,128)S(1)}, u32[]{:S(2)}, u32[]{:S(2)}) collective-permute-start(f32[3,1024]{1,0:T(4,128)S(1)} %get-tuple-element.69), channel_id=1, source_target_pairs={{0,4},{4,0},{8,12},{12,8},{16,20},{20,16},{24,28},{28,24},{1,5},{5... | collective-permute-start | bytes 36872 | tf_op jit(solution)/shard_map/ppermute | solution.py:535
  60.2 1.1 %collective-permute-done.12 = f32[3,1024]{1,0:T(4,128)S(1)} collective-permute-done((f32[3,1024]{1,0:T(4,128)S(1)}, f32[3,1024]{1,0:T(4,128)S(1)}, u32[]{:S(2)}, u32[]{:S(2)}) %collective-permute-start.12) | collective-permute-done | bytes 12320 | tf_op jit(solution)/shard_map/ppermute | solution.py:535
  61.3 0.2 collective-permute-done.11
  61.6 0.5 collective-permute-done.10
  62.1 3.5 %collective-permute-start.13 = (f32[3,1024]{1,0:T(4,128)S(1)}, f32[3,1024]{1,0:T(4,128)S(1)}, u32[]{:S(2)}, u32[]{:S(2)}) collective-permute-start(f32[3,1024]{1,0:T(4,128)S(1)} %add_add_fusion.a_ref), channel_id=1, source_target_pairs={{0,8},{4,12},{8,0},{12,4},{16,24},{20,28},{24,16},{28,20},{1,9},{5... | collective-permute-start | bytes 36872 | tf_op jit(solution)/shard_map/ppermute | solution.py:535
  65.6 1.0 %writing.2 = bf16[256,2048]{1,0:T(8,128)(2,1)} custom-call(bf16[256,1024]{1,0:T(8,128)(2,1)S(1)} %attention.2.refs_0_.teacher_ref, bf16[256,1024]{1,0:T(8,128)(2,1)S(1)} %attention.3.refs_1_.teacher_ref), custom_call_target="tpu_custom_call" | custom-call | bytes 2097152 | tf_op jit(solution)/shard_map/writing/pallas_call | solution.py:571
  66.6 1.0 %writing.3 = bf16[256,2048]{1,0:T(8,128)(2,1)} custom-call(bf16[256,1024]{1,0:T(8,128)(2,1)S(1)} %get-tuple-element.62.refs_0_, bf16[256,1024]{1,0:T(8,128)(2,1)S(1)} %get-tuple-element.68.refs_1_), custom_call_target="tpu_custom_call" | custom-call | bytes 2097152 | tf_op jit(solution)/shard_map/writing/pallas_call | solution.py:571
  67.6 0.0 collective-permute-done.13.b_ref
  67.6 0.6 closing.1
  (8 shorter events, 0.1 us)
Async XLA Ops:
  0.6 8.2 %copy-start.1 = (bf16[1,256,256]{2,1,0:T(8,128)(2,1)S(1)}, bf16[1,256,256]{2,1,0:T(8,128)(2,1)}, u32[]{:S(2)}) copy-start(bf16[1,256,256]{2,1,0:T(8,128)(2,1)} %param.14) | copy-start | bytes 393220
  0.6 8.2 %copy-start.2 = (bf16[1,256,256]{2,1,0:T(8,128)(2,1)S(1)}, bf16[1,256,256]{2,1,0:T(8,128)(2,1)}, u32[]{:S(2)}) copy-start(bf16[1,256,256]{2,1,0:T(8,128)(2,1)} %param.15) | copy-start | bytes 393220
  3.8 18.7 %collective-permute-start.6 = (bf16[144,1024]{1,0:T(8,128)(2,1)S(1)}, bf16[144,1024]{1,0:T(8,128)(2,1)S(1)}, u32[]{:S(2)}, u32[]{:S(2)}) collective-permute-start(bf16[144,1024]{1,0:T(8,128)(2,1)S(1)} %get-tuple-element.60), channel_id=1, source_target_pairs={{0,4},{12,8},{1,5},{13,9},{2,6},{14,10},{3,7},{15,11},{16,20},{28,... | collective-permute-start | bytes 884744 | tf_op jit(solution)/shard_map/ppermute | solution.py:714
  8.9 7.1 %collective-permute-start = (bf16[256,512]{1,0:T(8,128)(2,1)S(1)}, bf16[256,512]{1,0:T(8,128)(2,1)S(1)}, u32[]{:S(2)}, u32[]{:S(2)}) collective-permute-start(bf16[256,512]{1,0:T(8,128)(2,1)S(1)} %pack.1), channel_id=1, source_target_pairs={{4,8},{8,4},{5,9},{9,5},{6,10},{10,6},{7,11},{11,7},{20,24},{24,20... | collective-permute-start | bytes 786440 | tf_op jit(solution)/shard_map/ppermute | solution.py:661
  9.6 12.3 %collective-permute-start.3 = (bf16[256,512]{1,0:T(8,128)(2,1)S(1)}, bf16[256,512]{1,0:T(8,128)(2,1)S(1)}, u32[]{:S(2)}, u32[]{:S(2)}) collective-permute-start(bf16[256,512]{1,0:T(8,128)(2,1)S(1)} %pack.1), channel_id=1, source_target_pairs={{0,4},{12,8},{4,0},{8,12},{1,5},{13,9},{5,1},{9,13},{2,6},{14,10},... | collective-permute-start | bytes 786440 | tf_op jit(solution)/shard_map/ppermute | solution.py:660
  16.1 10.9 %collective-permute-start.1 = (bf16[144,1024]{1,0:T(8,128)(2,1)S(1)}, bf16[144,1024]{1,0:T(8,128)(2,1)S(1)}, u32[]{:S(2)}, u32[]{:S(2)}) collective-permute-start(bf16[144,1024]{1,0:T(8,128)(2,1)S(1)} %merge.1), channel_id=1, source_target_pairs={{0,4},{12,8},{4,0},{8,12},{1,5},{13,9},{5,1},{9,13},{2,6},{14,10},... | collective-permute-start | bytes 884744 | tf_op jit(solution)/shard_map/ppermute | solution.py:673
  21.9 1.4 %collective-permute-start.4 = (bf16[256,512]{1,0:T(8,128)(2,1)S(1)}, bf16[256,512]{1,0:T(8,128)(2,1)S(1)}, u32[]{:S(2)}, u32[]{:S(2)}) collective-permute-start(bf16[256,512]{1,0:T(8,128)(2,1)S(1)} %collective-permute-done.3.refs_0_), channel_id=1, source_target_pairs={{4,8},{8,4},{5,9},{9,5},{6,10},{10,6},{7,11},{11,7},{20,24},{24,20... | collective-permute-start | bytes 786440 | tf_op jit(solution)/shard_map/ppermute | solution.py:663
  22.6 5.3 %collective-permute-start.7 = (bf16[144,1024]{1,0:T(8,128)(2,1)S(1)}, bf16[144,1024]{1,0:T(8,128)(2,1)S(1)}, u32[]{:S(2)}, u32[]{:S(2)}) collective-permute-start(bf16[144,1024]{1,0:T(8,128)(2,1)S(1)} %chain.5), channel_id=1, source_target_pairs={{4,8},{8,4},{5,9},{9,5},{6,10},{10,6},{7,11},{11,7},{20,24},{24,20... | collective-permute-start | bytes 884744 | tf_op jit(solution)/shard_map/ppermute | solution.py:714
  23.3 19.8 %collective-permute-start.5 = (bf16[256,512]{1,0:T(8,128)(2,1)S(1)}, bf16[256,512]{1,0:T(8,128)(2,1)S(1)}, u32[]{:S(2)}, u32[]{:S(2)}) collective-permute-start(bf16[256,512]{1,0:T(8,128)(2,1)S(1)} %collective-permute-done.4.refs_2_), channel_id=1, source_target_pairs={{4,0},{8,12},{5,1},{9,13},{6,2},{10,14},{7,3},{11,15},{20,16},{24,... | collective-permute-start | bytes 786440 | tf_op jit(solution)/shard_map/ppermute | solution.py:675
  27.0 16.0 %copy-start.4 = (s32[1,1024]{1,0:T(1,128)S(1)}, s32[1,1024]{1,0:T(1,128)}, u32[]{:S(2)}) copy-start(s32[1,1024]{1,0:T(1,128)} %docs_ref.7) | copy-start | bytes 12292
  27.0 16.0 %copy-start.5 = (bf16[1,256,2048]{2,1,0:T(8,128)(2,1)S(1)}, bf16[1,256,2048]{2,1,0:T(8,128)(2,1)}, u32[]{:S(2)}) copy-start(bf16[1,256,2048]{2,1,0:T(8,128)(2,1)} %param.13) | copy-start | bytes 3145732
  27.0 19.0 %collective-permute-start.2 = (bf16[144,1024]{1,0:T(8,128)(2,1)S(1)}, bf16[144,1024]{1,0:T(8,128)(2,1)S(1)}, u32[]{:S(2)}, u32[]{:S(2)}) collective-permute-start(bf16[144,1024]{1,0:T(8,128)(2,1)S(1)} %chain.4), channel_id=1, source_target_pairs={{4,8},{8,4},{5,9},{9,5},{6,10},{10,6},{7,11},{11,7},{20,24},{24,20... | collective-permute-start | bytes 884744 | tf_op jit(solution)/shard_map/ppermute | solution.py:714
  27.9 22.8 %collective-permute-start.8 = (bf16[144,1024]{1,0:T(8,128)(2,1)S(1)}, bf16[144,1024]{1,0:T(8,128)(2,1)S(1)}, u32[]{:S(2)}, u32[]{:S(2)}) collective-permute-start(bf16[144,1024]{1,0:T(8,128)(2,1)S(1)} %chain.6), channel_id=1, source_target_pairs={{8,12},{4,0},{9,13},{5,1},{10,14},{6,2},{11,15},{7,3},{24,28},{20,... | collective-permute-start | bytes 884744 | tf_op jit(solution)/shard_map/ppermute | solution.py:714
  46.1 4.6 %copy-start = (bf16[1,256,256]{2,1,0:T(8,128)(2,1)S(1)}, bf16[1,256,256]{2,1,0:T(8,128)(2,1)}, u32[]{:S(2)}) copy-start(bf16[1,256,256]{2,1,0:T(8,128)(2,1)} %param.20) | copy-start | bytes 393220
  46.1 4.6 %copy-start.3 = (f32[2048]{0:T(1024)S(1)}, f32[2048]{0:T(1024)}, u32[]{:S(2)}) copy-start(f32[2048]{0:T(1024)} %param.25) | copy-start | bytes 24580
  46.1 8.7 %collective-permute-start.9 = (bf16[144,1024]{1,0:T(8,128)(2,1)S(1)}, bf16[144,1024]{1,0:T(8,128)(2,1)S(1)}, u32[]{:S(2)}, u32[]{:S(2)}) collective-permute-start(bf16[144,1024]{1,0:T(8,128)(2,1)S(1)} %chain.7), channel_id=1, source_target_pairs={{8,12},{4,0},{9,13},{5,1},{10,14},{6,2},{11,15},{7,3},{24,28},{20,... | collective-permute-start | bytes 884744 | tf_op jit(solution)/shard_map/ppermute | solution.py:714
  56.6 4.7 %collective-permute-start.12 = (f32[3,1024]{1,0:T(4,128)S(1)}, f32[3,1024]{1,0:T(4,128)S(1)}, u32[]{:S(2)}, u32[]{:S(2)}) collective-permute-start(f32[3,1024]{1,0:T(4,128)S(1)} %get-tuple-element.69), channel_id=1, source_target_pairs={{0,20},{4,16},{8,28},{12,24},{16,4},{20,0},{24,12},{28,8},{1,21},{... | collective-permute-start | bytes 36872 | tf_op jit(solution)/shard_map/ppermute | solution.py:535
  57.8 3.7 %collective-permute-start.11 = (f32[3,1024]{1,0:T(4,128)S(1)}, f32[3,1024]{1,0:T(4,128)S(1)}, u32[]{:S(2)}, u32[]{:S(2)}) collective-permute-start(f32[3,1024]{1,0:T(4,128)S(1)} %get-tuple-element.69), channel_id=1, source_target_pairs={{0,16},{4,20},{8,24},{12,28},{16,0},{20,4},{24,8},{28,12},{1,17},{... | collective-permute-start | bytes 36872 | tf_op jit(solution)/shard_map/ppermute | solution.py:535
  58.3 3.7 %collective-permute-start.10 = (f32[3,1024]{1,0:T(4,128)S(1)}, f32[3,1024]{1,0:T(4,128)S(1)}, u32[]{:S(2)}, u32[]{:S(2)}) collective-permute-start(f32[3,1024]{1,0:T(4,128)S(1)} %get-tuple-element.69), channel_id=1, source_target_pairs={{0,4},{4,0},{8,12},{12,8},{16,20},{20,16},{24,28},{28,24},{1,5},{5... | collective-permute-start | bytes 36872 | tf_op jit(solution)/shard_map/ppermute | solution.py:535
  62.1 5.5 %collective-permute-start.13 = (f32[3,1024]{1,0:T(4,128)S(1)}, f32[3,1024]{1,0:T(4,128)S(1)}, u32[]{:S(2)}, u32[]{:S(2)}) collective-permute-start(f32[3,1024]{1,0:T(4,128)S(1)} %add_add_fusion.a_ref), channel_id=1, source_target_pairs={{0,8},{4,12},{8,0},{12,4},{16,24},{20,28},{24,16},{28,20},{1,9},{5... | collective-permute-start | bytes 36872 | tf_op jit(solution)/shard_map/ppermute | solution.py:535

commit v10 on v6

--- a/solution.py
+++ b/solution.py
@@ -47,8 +47,7 @@
 
 
 def spread(v, matrix):
-    hi, lo = parts(v)
-    return dot_tn(hi, matrix) + dot_tn(lo, matrix)
+    return dot_tn(jnp.concatenate(parts(v), axis=0), jnp.concatenate([matrix, matrix], axis=0))
 
 
 def doc_row(docs_ref, block, stretch):
@@ -120,20 +119,11 @@
     xw_refs, dec_refs, f_refs, b_refs, send_refs = (
         outs[k * groups : (k + 1) * groups] for k in range(5)
     )
-    x_here, x_sem = outs[5 * groups :]
     heads, rows = dt_ref.shape
     stretch = rows // 2
     width = x_ref.shape[1] // groups
     kv_width = k_ref.shape[1]
     index = lax.axis_index("ctx")
-    loads_x = [
-        pltpu.make_async_copy(
-            x_ref.at[:, pl.ds(g * width, width)], x_here.at[g], x_sem.at[g]
-        )
-        for g in range(groups)
-    ]
-    for load in loads_x:
-        load.start()
     kv_ref[:, :kv_width] = k_ref[...]
     kv_ref[:, kv_width:] = v_ref[...]
     triangle = jnp.where(lower_triangle(stretch), 1.0, 0.0)
@@ -166,14 +156,14 @@
         same = jnp.where(as_column(row) == last.astype(F32), 1.0, 0.0)
         projs.append((b_ref[sl, :].astype(F32) * same).astype(BF16))
     for g in range(groups):
+        cols = slice(g * width, (g + 1) * width)
         matrix = spread_matrix(heads, width, g * (heads // groups))
         wide = spread(ends, matrix)
         dec_refs[g][...] = wide
         sums = []
-        loads_x[g].wait()
         for half in range(2):
             sl = slice(half * stretch, (half + 1) * stretch)
-            xw = (x_here[g, sl, :].astype(F32) * spread(loads[half], matrix)).astype(BF16)
+            xw = (x_ref[sl, cols].astype(F32) * spread(loads[half], matrix)).astype(BF16)
             xw_refs[g][sl, :] = xw
             sums.append(dot_tn(projs[half][:, g * N : (g + 1) * N], xw) * wide[2 + half : 3 + half])
         f_refs[g][...] = sums[0].astype(BF16)
@@ -601,12 +591,8 @@
             *([state] * (2 * groups)),
             *([payload] * groups),
         ),
-        in_specs=[VMEM] * 3 + [pl.BlockSpec(memory_space=pl.ANY)] + [VMEM] * 4,
+        in_specs=[VMEM] * 8,
         out_specs=(VMEM,) * (2 + 5 * groups),
-        scratch_shapes=[
-            pltpu.VMEM((groups, rows, width), BF16),
-            pltpu.SemaphoreType.DMA((groups,)),
-        ],
         compiler_params=params(16),
         cost_estimate=cost(4 * rows * features * N, 8 * rows * features),
         name="opening",
@@ -652,7 +638,7 @@
         inward, outward, across = [(0, 1), (3, 2)], [(1, 0), (2, 3)], [(1, 2), (2, 1)]
         near = lax.ppermute(kv, "ctx", inward + outward)
         middle = lax.ppermute(kv, "ctx", across)
-        middle, *local = lax.optimization_barrier((middle, *local))
+        middle, near, *local = lax.optimization_barrier((middle, near, *local))
         beyond = lax.ppermute(near, "ctx", across)
         send[-1] = pl.pallas_call(
             functools.partial(merge_kernel, count),

time: 62.1 us -> 63.2 us (1.018)
  waiting for transfers between devices: 20.2 us -> 21.4 us
  starting transfers between devices: 20.4 us -> 21.3 us
  Pallas kernels: 20.2 us -> 19.3 us
    ppermute x1, waiting for transfers between devices: 3.62 us -> 10.1 us  [body(): farther = lax.ppermute(beyond, 'ctx', outward)]
    ppermute x5, waiting for transfers between devices: 10.5 us -> 5.19 us  [body(): got[g].append(lax.ppermute(send[g], 'ctx', pairs))]
    ppermute x5, starting transfers between devices: 6.12 us -> 10.5 us  [body(): got[g].append(lax.ppermute(send[g], 'ctx', pairs))]
    ppermute x1, starting transfers between devices: 6 us -> 3.18 us  [body(): near = lax.ppermute(kv, 'ctx', inward + outward)]
    pallas_call x1, Pallas kernels: 4.3 us -> 3.25 us  [body(): pl.pallas_call(functools.partial(opening_kernel, count, groups), out_shap...]
  transfers between devices with their start and end apart: 14 -> 14, of which waited for: 8 -> 9; matrix products, arithmetic and copies ran while one was open for 0% -> 0% of each run, Pallas kernels for 22% -> 22%
where the time goes in v10:
time: 63.2 us; the launch traced here: 62.9 us
  waiting for transfers between devices  21.4 us (34%)
  starting transfers between devices  21.3 us (34%)
  Pallas kernels  19.3 us (31%)
  between operations  0.86 us (1%)
    ppermute x5, starting transfers between devices, body(): got[g].append(lax.ppermute(send[g], 'ctx', pairs))  10.5 us
    ppermute x1, waiting for transfers between devices, body(): farther = lax.ppermute(beyond, 'ctx', outward)  10.1 us
    pallas_call x2, Pallas kernels, body(): pl.pallas_call(functools.partial(attention_kernel, count, per_kv, stack,...  5.58 us
    ppermute x5, waiting for transfers between devices, body(): got[g].append(lax.ppermute(send[g], 'ctx', pairs))  5.19 us
    ppermute x4, starting transfers between devices, exchange(): return lax.ppermute(part, axes, [(d, d ^ shift) for d in range(size)])  4.87 us
    pallas_call x1, Pallas kernels, body(): pl.pallas_call(functools.partial(local_kernel, count, groups), out_shape=...  4.2 us
    pallas_call x2, Pallas kernels, body(): pl.pallas_call(functools.partial(final_kernel, count, g, groups, loss_sca...  3.57 us
    ppermute x4, waiting for transfers between devices, exchange(): return lax.ppermute(part, axes, [(d, d ^ shift) for d in range(size)])  3.26 us
  transfers between devices with their start and end apart: 14, of which 9 were waited for; matrix products, arithmetic and copies ran while one was open for 0% of the time, Pallas kernels for 22%

profile of v10, /device:TPU:0, one launch (start us, length us, event | category | flops | bytes accessed | tf_op | source)
XLA Modules:
  0.0 62.9 jit_solution(2983763289548609821)
XLA Ops:
  0.6 3.2 %opening.1 = (bf16[256,512]{1,0:T(8,128)(2,1)S(1)}, f32[32,256]{1,0:T(8,128)S(1)}, bf16[256,1024]{1,0:T(8,128)(2,1)S(1)}, bf16[256,1024]{1,0:T(8,128)(2,1)S(1)},...) custom-call(s32[1,1024]{1,0:T(1,128)} %docs_ref.7, ...), custom_call_target="tpu_custom_call" | custom-call | flops 268435456 | bytes 4194304 | tf_op jit(solution)/shard_map/opening/pallas_call | solution.py:584
  3.9 3.2 %collective-permute-start.1 = (bf16[256,512]{1,0:T(8,128)(2,1)S(1)}, bf16[256,512]{1,0:T(8,128)(2,1)S(1)}, u32[]{:S(2)}, u32[]{:S(2)}) collective-permute-start(bf16[256,512]{1,0:T(8,128)(2,1)S(1)} %get-tuple-element.39), channel_id=1, source_target_pairs={{0,4},{12,8},{4,0},{8,12},{1,5},{13,9},{5,1},{9,13},{2,6},{14,10},... | collective-permute-start | bytes 786440 | tf_op jit(solution)/shard_map/ppermute | solution.py:639
  7.1 0.7 %collective-permute-start = (bf16[256,512]{1,0:T(8,128)(2,1)S(1)}, bf16[256,512]{1,0:T(8,128)(2,1)S(1)}, u32[]{:S(2)}, u32[]{:S(2)}) collective-permute-start(bf16[256,512]{1,0:T(8,128)(2,1)S(1)} %get-tuple-element.39), channel_id=1, source_target_pairs={{4,8},{8,4},{5,9},{9,5},{6,10},{10,6},{7,11},{11,7},{20,24},{24,20... | collective-permute-start | bytes 786440 | tf_op jit(solution)/shard_map/ppermute | solution.py:640
  7.7 6.3 %collective-permute-start.6 = (bf16[144,1024]{1,0:T(8,128)(2,1)S(1)}, bf16[144,1024]{1,0:T(8,128)(2,1)S(1)}, u32[]{:S(2)}, u32[]{:S(2)}) collective-permute-start(bf16[144,1024]{1,0:T(8,128)(2,1)S(1)} %get-tuple-element.60), channel_id=1, source_target_pairs={{0,4},{12,8},{1,5},{13,9},{2,6},{14,10},{3,7},{15,11},{16,20},{28,... | collective-permute-start | bytes 884744 | tf_op jit(solution)/shard_map/ppermute | solution.py:701
  14.1 4.2 %local.1 = (f32[256,1024]{1,0:T(8,128)S(1)}, f32[256,1024]{1,0:T(8,128)S(1)}, f32[256,1024]{1,0:T(8,128)S(1)}, f32[256,1024]{1,0:T(8,128)S(1)}, f32[256,1024]{1,0:T(8,128)S(1)}, /*index=5*/f32[256,1024]{1,0:T(8,128)S(1)}) custom-call(s32[1,1024]{1,0:T(1,128)} %docs_ref.7, bf16[256,2048]{1,0:T(8,128)(2,1)} %bitcast.32, bf16[256,2048]{1,0:T(8,128)(2,1)} %bitcast.33, ...), custom_call_target="tpu_custom_call" | custom-call | flops 134217728 | bytes 8388608 | tf_op jit(solution)/shard_map/local/pallas_call | solution.py:616
  18.3 0.0 collective-permute-done.1.refs_0_
  18.3 0.0 collective-permute-done.kv_ref.refs_1_
  18.3 0.1 collective-permute-start.2
  18.4 0.7 %collective-permute-start.4 = (bf16[256,512]{1,0:T(8,128)(2,1)S(1)}, bf16[256,512]{1,0:T(8,128)(2,1)S(1)}, u32[]{:S(2)}, u32[]{:S(2)}) collective-permute-start(bf16[256,512]{1,0:T(8,128)(2,1)S(1)} %collective-permute-done.1.refs_0_), channel_id=1, source_target_pairs={{4,8},{8,4},{5,9},{9,5},{6,10},{10,6},{7,11},{11,7},{20,24},{24,20... | collective-permute-start | bytes 786440 | tf_op jit(solution)/shard_map/ppermute | solution.py:642
  19.1 2.4 %collective-permute-done.6.got_ref.refs_0_ = bf16[144,1024]{1,0:T(8,128)(2,1)S(1)} collective-permute-done((bf16[144,1024]{1,0:T(8,128)(2,1)S(1)}, bf16[144,1024]{1,0:T(8,128)(2,1)S(1)}, u32[]{:S(2)}, u32[]{:S(2)}) %collective-permute-start.6) | collective-permute-done | bytes 294944 | tf_op jit(solution)/shard_map/ppermute | solution.py:701
  21.5 0.7 %collective-permute-start.7 = (bf16[144,1024]{1,0:T(8,128)(2,1)S(1)}, bf16[144,1024]{1,0:T(8,128)(2,1)S(1)}, u32[]{:S(2)}, u32[]{:S(2)}) collective-permute-start(bf16[144,1024]{1,0:T(8,128)(2,1)S(1)} %chain.5), channel_id=1, source_target_pairs={{4,8},{8,4},{5,9},{9,5},{6,10},{10,6},{7,11},{11,7},{20,24},{24,20... | collective-permute-start | bytes 884744 | tf_op jit(solution)/shard_map/ppermute | solution.py:701
  22.2 0.0 collective-permute-done.4.refs_2_
  22.2 1.3 %collective-permute-start.5 = (bf16[256,512]{1,0:T(8,128)(2,1)S(1)}, bf16[256,512]{1,0:T(8,128)(2,1)S(1)}, u32[]{:S(2)}, u32[]{:S(2)}) collective-permute-start(bf16[256,512]{1,0:T(8,128)(2,1)S(1)} %collective-permute-done.4.refs_2_), channel_id=1, source_target_pairs={{4,0},{8,12},{5,1},{9,13},{6,2},{10,14},{7,3},{11,15},{20,16},{24,... | collective-permute-start | bytes 786440 | tf_op jit(solution)/shard_map/ppermute | solution.py:654
  23.5 2.8 %collective-permute-done.2.got_ref.refs_3_.refs_0_ = bf16[144,1024]{1,0:T(8,128)(2,1)S(1)} collective-permute-done((bf16[144,1024]{1,0:T(8,128)(2,1)S(1)}, bf16[144,1024]{1,0:T(8,128)(2,1)S(1)}, u32[]{:S(2)}, u32[]{:S(2)}) %collective-permute-start.2) | collective-permute-done | bytes 294944 | tf_op jit(solution)/shard_map/ppermute | solution.py:652
  26.3 0.0 copy-start
  26.3 0.0 copy-start.1
  26.3 0.8 %collective-permute-start.3 = (bf16[144,1024]{1,0:T(8,128)(2,1)S(1)}, bf16[144,1024]{1,0:T(8,128)(2,1)S(1)}, u32[]{:S(2)}, u32[]{:S(2)}) collective-permute-start(bf16[144,1024]{1,0:T(8,128)(2,1)S(1)} %chain.4), channel_id=1, source_target_pairs={{4,8},{8,4},{5,9},{9,5},{6,10},{10,6},{7,11},{11,7},{20,24},{24,20... | collective-permute-start | bytes 884744 | tf_op jit(solution)/shard_map/ppermute | solution.py:701
  27.1 0.0 collective-permute-done.7.got_ref.refs_1_
  27.1 0.0 copy-start.4
  27.2 1.3 %collective-permute-start.8 = (bf16[144,1024]{1,0:T(8,128)(2,1)S(1)}, bf16[144,1024]{1,0:T(8,128)(2,1)S(1)}, u32[]{:S(2)}, u32[]{:S(2)}) collective-permute-start(bf16[144,1024]{1,0:T(8,128)(2,1)S(1)} %chain.6), channel_id=1, source_target_pairs={{8,12},{4,0},{9,13},{5,1},{10,14},{6,2},{11,15},{7,3},{24,28},{20,... | collective-permute-start | bytes 884744 | tf_op jit(solution)/shard_map/ppermute | solution.py:701
  28.5 10.1 %collective-permute-done.5.refs_4_ = bf16[256,512]{1,0:T(8,128)(2,1)S(1)} collective-permute-done((bf16[256,512]{1,0:T(8,128)(2,1)S(1)}, bf16[256,512]{1,0:T(8,128)(2,1)S(1)}, u32[]{:S(2)}, u32[]{:S(2)}) %collective-permute-start.5) | collective-permute-done | bytes 262176 | tf_op jit(solution)/shard_map/ppermute | solution.py:654
  38.6 0.0 copy-done
  38.6 0.0 copy-done.1
  38.6 0.0 copy-done.2
  38.6 0.0 copy-done.4
  38.7 2.8 %attention.2.refs_0_.teacher_ref = bf16[256,1024]{1,0:T(8,128)(2,1)S(1)} custom-call(s32[1,1024]{1,0:T(1,128)S(1)} %copy-done.4, bf16[256,2048]{1,0:T(8,128)(2,1)S(1)} %bitcast.18, bf16[256,256]{1,0:T(8,128)(2,1)S(1)} %bitcast.21, bf16[256,256]{1,0:T(8,128)(2,1)S(1)} %bitcast.24, bf16[256,512]{1,0:T(8,128)(2,1)S(1)} %collective-permute-done.1.refs_0_, ...), custom_call_target="tpu_custom_call" | custom-call | flops 603979776 | bytes 2097152 | tf_op jit(solution)/shard_map/attention/pallas_call | solution.py:665
  41.4 0.0 collective-permute-done.3.got_ref.refs_1_
  41.5 0.0 copy-start.3
  41.5 0.0 copy-start.5
  41.5 1.4 %collective-permute-start.9 = (bf16[144,1024]{1,0:T(8,128)(2,1)S(1)}, bf16[144,1024]{1,0:T(8,128)(2,1)S(1)}, u32[]{:S(2)}, u32[]{:S(2)}) collective-permute-start(bf16[144,1024]{1,0:T(8,128)(2,1)S(1)} %chain.7), channel_id=1, source_target_pairs={{8,12},{4,0},{9,13},{5,1},{10,14},{6,2},{11,15},{7,3},{24,28},{20,... | collective-permute-start | bytes 884744 | tf_op jit(solution)/shard_map/ppermute | solution.py:701
  42.9 2.8 %attention.3.refs_1_.teacher_ref = bf16[256,1024]{1,0:T(8,128)(2,1)S(1)} custom-call(s32[1,1024]{1,0:T(1,128)S(1)} %copy-done.4, bf16[256,2048]{1,0:T(8,128)(2,1)S(1)} %bitcast.19, bf16[256,256]{1,0:T(8,128)(2,1)S(1)} %bitcast.22, bf16[256,256]{1,0:T(8,128)(2,1)S(1)} %bitcast.25, bf16[256,512]{1,0:T(8,128)(2,1)S(1)} %collective-permute-done.1.refs_0_, ...), custom_call_target="tpu_custom_call" | custom-call | flops 603979776 | bytes 2097152 | tf_op jit(solution)/shard_map/attention/pallas_call | solution.py:665
  45.7 1.0 %collective-permute-done.8.refs_2_ = bf16[144,1024]{1,0:T(8,128)(2,1)S(1)} collective-permute-done((bf16[144,1024]{1,0:T(8,128)(2,1)S(1)}, bf16[144,1024]{1,0:T(8,128)(2,1)S(1)}, u32[]{:S(2)}, u32[]{:S(2)}) %collective-permute-start.8) | collective-permute-done | bytes 294944 | tf_op jit(solution)/shard_map/ppermute | solution.py:701
  46.8 0.0 copy-done.3
  46.8 0.0 copy-done.5
  46.8 1.8 %final.2 = (bf16[256,1024]{1,0:T(8,128)(2,1)S(1)}, f32[3,1024]{1,0:T(4,128)S(1)}) custom-call(f32[256,1024]{1,0:T(8,128)S(1)} %get-tuple-element.55.pre_ref, f32[256,1024]{1,0:T(8,128)S(1)} %get-tuple-element.56.reach_ref, f32[256,1024]{1,0:T(8,128)S(1)} %get-tuple-element.57.sx_ref, bf16[256,256]{1,0:T(8,128)(2,1)S(1)} %bitcast.27, ...), custom_call_target="tpu_custom_call" | custom-call | flops 67108864 | bytes 5242880 | tf_op jit(solution)/shard_map/final/pallas_call | solution.py:706
  48.6 1.8 %collective-permute-done.9.refs_2_ = bf16[144,1024]{1,0:T(8,128)(2,1)S(1)} collective-permute-done((bf16[144,1024]{1,0:T(8,128)(2,1)S(1)}, bf16[144,1024]{1,0:T(8,128)(2,1)S(1)}, u32[]{:S(2)}, u32[]{:S(2)}) %collective-permute-start.9) | collective-permute-done | bytes 294944 | tf_op jit(solution)/shard_map/ppermute | solution.py:701
  50.3 1.8 %final.3 = (bf16[256,1024]{1,0:T(8,128)(2,1)S(1)}, f32[3,1024]{1,0:T(4,128)S(1)}) custom-call(f32[256,1024]{1,0:T(8,128)S(1)} %get-tuple-element.63.pre_ref, f32[256,1024]{1,0:T(8,128)S(1)} %get-tuple-element.64.reach_ref, f32[256,1024]{1,0:T(8,128)S(1)} %get-tuple-element.65.sx_ref, bf16[256,256]{1,0:T(8,128)(2,1)S(1)} %bitcast.28, ...), custom_call_target="tpu_custom_call" | custom-call | flops 67108864 | bytes 5242880 | tf_op jit(solution)/shard_map/final/pallas_call | solution.py:706
  52.1 1.0 %collective-permute-start.12 = (f32[3,1024]{1,0:T(4,128)S(1)}, f32[3,1024]{1,0:T(4,128)S(1)}, u32[]{:S(2)}, u32[]{:S(2)}) collective-permute-start(f32[3,1024]{1,0:T(4,128)S(1)} %get-tuple-element.69), channel_id=1, source_target_pairs={{0,20},{4,16},{8,28},{12,24},{16,4},{20,0},{24,12},{28,8},{1,21},{... | collective-permute-start | bytes 36872 | tf_op jit(solution)/shard_map/ppermute | solution.py:535
  53.1 0.7 %collective-permute-start.11 = (f32[3,1024]{1,0:T(4,128)S(1)}, f32[3,1024]{1,0:T(4,128)S(1)}, u32[]{:S(2)}, u32[]{:S(2)}) collective-permute-start(f32[3,1024]{1,0:T(4,128)S(1)} %get-tuple-element.69), channel_id=1, source_target_pairs={{0,16},{4,20},{8,24},{12,28},{16,0},{20,4},{24,8},{28,12},{1,17},{... | collective-permute-start | bytes 36872 | tf_op jit(solution)/shard_map/ppermute | solution.py:535
  53.8 1.9 %collective-permute-start.10 = (f32[3,1024]{1,0:T(4,128)S(1)}, f32[3,1024]{1,0:T(4,128)S(1)}, u32[]{:S(2)}, u32[]{:S(2)}) collective-permute-start(f32[3,1024]{1,0:T(4,128)S(1)} %get-tuple-element.69), channel_id=1, source_target_pairs={{0,4},{4,0},{8,12},{12,8},{16,20},{20,16},{24,28},{28,24},{1,5},{5... | collective-permute-start | bytes 36872 | tf_op jit(solution)/shard_map/ppermute | solution.py:535
  55.7 1.2 %collective-permute-done.12 = f32[3,1024]{1,0:T(4,128)S(1)} collective-permute-done((f32[3,1024]{1,0:T(4,128)S(1)}, f32[3,1024]{1,0:T(4,128)S(1)}, u32[]{:S(2)}, u32[]{:S(2)}) %collective-permute-start.12) | collective-permute-done | bytes 12320 | tf_op jit(solution)/shard_map/ppermute | solution.py:535
  56.8 0.2 collective-permute-done.11
  57.0 0.5 collective-permute-done.10
  57.5 1.3 %collective-permute-start.13 = (f32[3,1024]{1,0:T(4,128)S(1)}, f32[3,1024]{1,0:T(4,128)S(1)}, u32[]{:S(2)}, u32[]{:S(2)}) collective-permute-start(f32[3,1024]{1,0:T(4,128)S(1)} %add_add_fusion.a_ref), channel_id=1, source_target_pairs={{0,8},{4,12},{8,0},{12,4},{16,24},{20,28},{24,16},{28,20},{1,9},{5... | collective-permute-start | bytes 36872 | tf_op jit(solution)/shard_map/ppermute | solution.py:535
  58.9 1.0 %writing.2 = bf16[256,2048]{1,0:T(8,128)(2,1)} custom-call(bf16[256,1024]{1,0:T(8,128)(2,1)S(1)} %attention.2.refs_0_.teacher_ref, bf16[256,1024]{1,0:T(8,128)(2,1)S(1)} %attention.3.refs_1_.teacher_ref), custom_call_target="tpu_custom_call" | custom-call | bytes 2097152 | tf_op jit(solution)/shard_map/writing/pallas_call | solution.py:571
  59.8 1.0 %writing.3 = bf16[256,2048]{1,0:T(8,128)(2,1)} custom-call(bf16[256,1024]{1,0:T(8,128)(2,1)S(1)} %get-tuple-element.62.refs_0_, bf16[256,1024]{1,0:T(8,128)(2,1)S(1)} %get-tuple-element.68.refs_1_), custom_call_target="tpu_custom_call" | custom-call | bytes 2097152 | tf_op jit(solution)/shard_map/writing/pallas_call | solution.py:571
  60.8 1.4 %collective-permute-done.13.b_ref = f32[3,1024]{1,0:T(4,128)S(1)} collective-permute-done((f32[3,1024]{1,0:T(4,128)S(1)}, f32[3,1024]{1,0:T(4,128)S(1)}, u32[]{:S(2)}, u32[]{:S(2)}) %collective-permute-start.13) | collective-permute-done | bytes 12320 | tf_op jit(solution)/shard_map/ppermute | solution.py:535
  62.2 0.6 closing.1
  (7 shorter events, 0.1 us)
Async XLA Ops:
  3.9 14.4 %collective-permute-start.1 = (bf16[256,512]{1,0:T(8,128)(2,1)S(1)}, bf16[256,512]{1,0:T(8,128)(2,1)S(1)}, u32[]{:S(2)}, u32[]{:S(2)}) collective-permute-start(bf16[256,512]{1,0:T(8,128)(2,1)S(1)} %get-tuple-element.39), channel_id=1, source_target_pairs={{0,4},{12,8},{4,0},{8,12},{1,5},{13,9},{5,1},{9,13},{2,6},{14,10},... | collective-permute-start | bytes 786440 | tf_op jit(solution)/shard_map/ppermute | solution.py:639
  7.1 11.2 %collective-permute-start = (bf16[256,512]{1,0:T(8,128)(2,1)S(1)}, bf16[256,512]{1,0:T(8,128)(2,1)S(1)}, u32[]{:S(2)}, u32[]{:S(2)}) collective-permute-start(bf16[256,512]{1,0:T(8,128)(2,1)S(1)} %get-tuple-element.39), channel_id=1, source_target_pairs={{4,8},{8,4},{5,9},{9,5},{6,10},{10,6},{7,11},{11,7},{20,24},{24,20... | collective-permute-start | bytes 786440 | tf_op jit(solution)/shard_map/ppermute | solution.py:640
  7.7 13.7 %collective-permute-start.6 = (bf16[144,1024]{1,0:T(8,128)(2,1)S(1)}, bf16[144,1024]{1,0:T(8,128)(2,1)S(1)}, u32[]{:S(2)}, u32[]{:S(2)}) collective-permute-start(bf16[144,1024]{1,0:T(8,128)(2,1)S(1)} %get-tuple-element.60), channel_id=1, source_target_pairs={{0,4},{12,8},{1,5},{13,9},{2,6},{14,10},{3,7},{15,11},{16,20},{28,... | collective-permute-start | bytes 884744 | tf_op jit(solution)/shard_map/ppermute | solution.py:701
  18.3 8.0 %collective-permute-start.2 = (bf16[144,1024]{1,0:T(8,128)(2,1)S(1)}, bf16[144,1024]{1,0:T(8,128)(2,1)S(1)}, u32[]{:S(2)}, u32[]{:S(2)}) collective-permute-start(bf16[144,1024]{1,0:T(8,128)(2,1)S(1)} %merge.1), channel_id=1, source_target_pairs={{0,4},{12,8},{4,0},{8,12},{1,5},{13,9},{5,1},{9,13},{2,6},{14,10},... | collective-permute-start | bytes 884744 | tf_op jit(solution)/shard_map/ppermute | solution.py:652
  18.4 3.8 %collective-permute-start.4 = (bf16[256,512]{1,0:T(8,128)(2,1)S(1)}, bf16[256,512]{1,0:T(8,128)(2,1)S(1)}, u32[]{:S(2)}, u32[]{:S(2)}) collective-permute-start(bf16[256,512]{1,0:T(8,128)(2,1)S(1)} %collective-permute-done.1.refs_0_), channel_id=1, source_target_pairs={{4,8},{8,4},{5,9},{9,5},{6,10},{10,6},{7,11},{11,7},{20,24},{24,20... | collective-permute-start | bytes 786440 | tf_op jit(solution)/shard_map/ppermute | solution.py:642
  21.5 5.6 %collective-permute-start.7 = (bf16[144,1024]{1,0:T(8,128)(2,1)S(1)}, bf16[144,1024]{1,0:T(8,128)(2,1)S(1)}, u32[]{:S(2)}, u32[]{:S(2)}) collective-permute-start(bf16[144,1024]{1,0:T(8,128)(2,1)S(1)} %chain.5), channel_id=1, source_target_pairs={{4,8},{8,4},{5,9},{9,5},{6,10},{10,6},{7,11},{11,7},{20,24},{24,20... | collective-permute-start | bytes 884744 | tf_op jit(solution)/shard_map/ppermute | solution.py:701
  22.2 16.5 %collective-permute-start.5 = (bf16[256,512]{1,0:T(8,128)(2,1)S(1)}, bf16[256,512]{1,0:T(8,128)(2,1)S(1)}, u32[]{:S(2)}, u32[]{:S(2)}) collective-permute-start(bf16[256,512]{1,0:T(8,128)(2,1)S(1)} %collective-permute-done.4.refs_2_), channel_id=1, source_target_pairs={{4,0},{8,12},{5,1},{9,13},{6,2},{10,14},{7,3},{11,15},{20,16},{24,... | collective-permute-start | bytes 786440 | tf_op jit(solution)/shard_map/ppermute | solution.py:654
  26.3 12.3 %copy-start = (bf16[1,256,2048]{2,1,0:T(8,128)(2,1)S(1)}, bf16[1,256,2048]{2,1,0:T(8,128)(2,1)}, u32[]{:S(2)}) copy-start(bf16[1,256,2048]{2,1,0:T(8,128)(2,1)} %param.13) | copy-start | bytes 3145732
  26.3 12.3 %copy-start.1 = (bf16[1,256,256]{2,1,0:T(8,128)(2,1)S(1)}, bf16[1,256,256]{2,1,0:T(8,128)(2,1)}, u32[]{:S(2)}) copy-start(bf16[1,256,256]{2,1,0:T(8,128)(2,1)} %param.14) | copy-start | bytes 393220
  26.3 12.3 %copy-start.2 = (bf16[1,256,256]{2,1,0:T(8,128)(2,1)S(1)}, bf16[1,256,256]{2,1,0:T(8,128)(2,1)}, u32[]{:S(2)}) copy-start(bf16[1,256,256]{2,1,0:T(8,128)(2,1)} %param.15) | copy-start | bytes 393220
  26.3 15.1 %collective-permute-start.3 = (bf16[144,1024]{1,0:T(8,128)(2,1)S(1)}, bf16[144,1024]{1,0:T(8,128)(2,1)S(1)}, u32[]{:S(2)}, u32[]{:S(2)}) collective-permute-start(bf16[144,1024]{1,0:T(8,128)(2,1)S(1)} %chain.4), channel_id=1, source_target_pairs={{4,8},{8,4},{5,9},{9,5},{6,10},{10,6},{7,11},{11,7},{20,24},{24,20... | collective-permute-start | bytes 884744 | tf_op jit(solution)/shard_map/ppermute | solution.py:701
  27.1 11.5 %copy-start.4 = (s32[1,1024]{1,0:T(1,128)S(1)}, s32[1,1024]{1,0:T(1,128)}, u32[]{:S(2)}) copy-start(s32[1,1024]{1,0:T(1,128)} %docs_ref.7) | copy-start | bytes 12292
  27.2 19.6 %collective-permute-start.8 = (bf16[144,1024]{1,0:T(8,128)(2,1)S(1)}, bf16[144,1024]{1,0:T(8,128)(2,1)S(1)}, u32[]{:S(2)}, u32[]{:S(2)}) collective-permute-start(bf16[144,1024]{1,0:T(8,128)(2,1)S(1)} %chain.6), channel_id=1, source_target_pairs={{8,12},{4,0},{9,13},{5,1},{10,14},{6,2},{11,15},{7,3},{24,28},{20,... | collective-permute-start | bytes 884744 | tf_op jit(solution)/shard_map/ppermute | solution.py:701
  41.5 5.3 %copy-start.3 = (bf16[1,256,256]{2,1,0:T(8,128)(2,1)S(1)}, bf16[1,256,256]{2,1,0:T(8,128)(2,1)}, u32[]{:S(2)}) copy-start(bf16[1,256,256]{2,1,0:T(8,128)(2,1)} %param.20) | copy-start | bytes 393220
  41.5 5.3 %copy-start.5 = (f32[2048]{0:T(1024)S(1)}, f32[2048]{0:T(1024)}, u32[]{:S(2)}) copy-start(f32[2048]{0:T(1024)} %param.25) | copy-start | bytes 24580
  41.5 8.8 %collective-permute-start.9 = (bf16[144,1024]{1,0:T(8,128)(2,1)S(1)}, bf16[144,1024]{1,0:T(8,128)(2,1)S(1)}, u32[]{:S(2)}, u32[]{:S(2)}) collective-permute-start(bf16[144,1024]{1,0:T(8,128)(2,1)S(1)} %chain.7), channel_id=1, source_target_pairs={{8,12},{4,0},{9,13},{5,1},{10,14},{6,2},{11,15},{7,3},{24,28},{20,... | collective-permute-start | bytes 884744 | tf_op jit(solution)/shard_map/ppermute | solution.py:701
  52.1 4.7 %collective-permute-start.12 = (f32[3,1024]{1,0:T(4,128)S(1)}, f32[3,1024]{1,0:T(4,128)S(1)}, u32[]{:S(2)}, u32[]{:S(2)}) collective-permute-start(f32[3,1024]{1,0:T(4,128)S(1)} %get-tuple-element.69), channel_id=1, source_target_pairs={{0,20},{4,16},{8,28},{12,24},{16,4},{20,0},{24,12},{28,8},{1,21},{... | collective-permute-start | bytes 36872 | tf_op jit(solution)/shard_map/ppermute | solution.py:535
  53.1 3.9 %collective-permute-start.11 = (f32[3,1024]{1,0:T(4,128)S(1)}, f32[3,1024]{1,0:T(4,128)S(1)}, u32[]{:S(2)}, u32[]{:S(2)}) collective-permute-start(f32[3,1024]{1,0:T(4,128)S(1)} %get-tuple-element.69), channel_id=1, source_target_pairs={{0,16},{4,20},{8,24},{12,28},{16,0},{20,4},{24,8},{28,12},{1,17},{... | collective-permute-start | bytes 36872 | tf_op jit(solution)/shard_map/ppermute | solution.py:535
  53.8 3.7 %collective-permute-start.10 = (f32[3,1024]{1,0:T(4,128)S(1)}, f32[3,1024]{1,0:T(4,128)S(1)}, u32[]{:S(2)}, u32[]{:S(2)}) collective-permute-start(f32[3,1024]{1,0:T(4,128)S(1)} %get-tuple-element.69), channel_id=1, source_target_pairs={{0,4},{4,0},{8,12},{12,8},{16,20},{20,16},{24,28},{28,24},{1,5},{5... | collective-permute-start | bytes 36872 | tf_op jit(solution)/shard_map/ppermute | solution.py:535
  57.5 4.7 %collective-permute-start.13 = (f32[3,1024]{1,0:T(4,128)S(1)}, f32[3,1024]{1,0:T(4,128)S(1)}, u32[]{:S(2)}, u32[]{:S(2)}) collective-permute-start(f32[3,1024]{1,0:T(4,128)S(1)} %add_add_fusion.a_ref), channel_id=1, source_target_pairs={{0,8},{4,12},{8,0},{12,4},{16,24},{20,28},{24,16},{28,20},{1,9},{5... | collective-permute-start | bytes 36872 | tf_op jit(solution)/shard_map/ppermute | solution.py:535

commit v11 on v10

--- a/solution.py
+++ b/solution.py
@@ -634,6 +634,20 @@
 
     send = list(send)
     got = [[] for _ in range(groups)]
+    def passed_on(g, stage):
+        return pl.pallas_call(
+            functools.partial(chain_kernel, count, stage),
+            out_shape=payload,
+            in_specs=[VMEM] * 4,
+            out_specs=VMEM,
+            compiler_params=params(4),
+            cost_estimate=pl.CostEstimate(flops=16384 * N * width, bytes_accessed=0, transcendentals=0),
+            name="chain",
+        )(got[g][-1], f_parts[g], b_parts[g], dec[g])
+
+    def stage_pairs(stage):
+        return [(stage - 1, stage), (count - stage, count - stage - 1)]
+
     if count == 4:
         inward, outward, across = [(0, 1), (3, 2)], [(1, 0), (2, 3)], [(1, 2), (2, 1)]
         near = lax.ppermute(kv, "ctx", inward + outward)
@@ -651,6 +665,9 @@
         )(send[-1], middle)
         far = lax.ppermute(send[-1], "ctx", inward + outward)
         got[-1].append(far)
+        send[-1] = passed_on(groups - 1, 1)
+        got[-1].append(lax.ppermute(send[-1], "ctx", stage_pairs(2)))
+        beyond, _ = lax.optimization_barrier((beyond, send[-1]))
         farther = lax.ppermute(beyond, "ctx", outward)
         kv_got = [near, middle, beyond, far, farther]
     else:
@@ -684,22 +701,11 @@
     ]
     for r in range(1, count):
         for g in range(groups):
-            if r == 3 and g == groups - 1:
-                got[g][-1], targets[0] = lax.optimization_barrier((got[g][-1], targets[0]))
+            if len(got[g]) >= r:
+                continue
             if r > 1:
-                send[g] = pl.pallas_call(
-                    functools.partial(chain_kernel, count, r - 1),
-                    out_shape=payload,
-                    in_specs=[VMEM] * 4,
-                    out_specs=VMEM,
-                    compiler_params=params(4),
-                    cost_estimate=cost(8 * N * width, 8 * N * width),
-                    name="chain",
-                )(got[g][-1], f_parts[g], b_parts[g], dec[g])
-            if len(got[g]) < r:
-                pairs = [(r - 1, r), (count - r, count - r - 1)]
-                got[g].append(lax.ppermute(send[g], "ctx", pairs))
-
+                send[g] = passed_on(g, r - 1)
+            got[g].append(lax.ppermute(send[g], "ctx", stage_pairs(r)))
     normed, grads = [], None
     for g in range(groups):
         more = [] if grads is None else [grads]

time: 63.2 us -> 63.7 us (level)
    ppermute x1, waiting for transfers between devices: 2.84 us -> 4.14 us  [body(): far = lax.ppermute(send[-1], 'ctx', inward + outward)]
    ppermute x1, waiting for transfers between devices: 10.1 us -> 8.89 us  [body(): farther = lax.ppermute(beyond, 'ctx', outward)]
  transfers between devices with their start and end apart: 14 -> 14, of which waited for: 9 -> 9; matrix products, arithmetic and copies ran while one was open for 0% -> 0% of each run, Pallas kernels for 22% -> 21%
where the time goes in v11:
time: 63.7 us; the launch traced here: 63.4 us
  waiting for transfers between devices  21.7 us (34%)
  starting transfers between devices  21.5 us (34%)
  Pallas kernels  19.3 us (30%)
  between operations  0.88 us (1%)
    ppermute x4, starting transfers between devices, body(): got[g].append(lax.ppermute(send[g], 'ctx', stage_pairs(r)))  9.69 us
    ppermute x1, waiting for transfers between devices, body(): farther = lax.ppermute(beyond, 'ctx', outward)  8.89 us
    ppermute x4, waiting for transfers between devices, body(): got[g].append(lax.ppermute(send[g], 'ctx', stage_pairs(r)))  5.61 us
    pallas_call x2, Pallas kernels, body(): pl.pallas_call(functools.partial(attention_kernel, count, per_kv, stack,...  5.58 us
    ppermute x4, starting transfers between devices, exchange(): return lax.ppermute(part, axes, [(d, d ^ shift) for d in range(size)])  5.22 us
    pallas_call x1, Pallas kernels, body(): pl.pallas_call(functools.partial(local_kernel, count, groups), out_shape=...  4.2 us
    ppermute x1, waiting for transfers between devices, body(): far = lax.ppermute(send[-1], 'ctx', inward + outward)  4.14 us
    pallas_call x2, Pallas kernels, body(): pl.pallas_call(functools.partial(final_kernel, count, g, groups, loss_sca...  3.57 us
  transfers between devices with their start and end apart: 14, of which 9 were waited for; matrix products, arithmetic and copies ran while one was open for 0% of the time, Pallas kernels for 21%

profile of v11, /device:TPU:0, one launch (start us, length us, event | category | flops | bytes accessed | tf_op | source)
XLA Modules:
  0.0 63.4 jit_solution(8104349616748614457)
XLA Ops:
  0.6 3.2 %opening.1 = (bf16[256,512]{1,0:T(8,128)(2,1)S(1)}, f32[32,256]{1,0:T(8,128)S(1)}, bf16[256,1024]{1,0:T(8,128)(2,1)S(1)}, bf16[256,1024]{1,0:T(8,128)(2,1)S(1)},...) custom-call(s32[1,1024]{1,0:T(1,128)} %docs_ref.7, ...), custom_call_target="tpu_custom_call" | custom-call | flops 268435456 | bytes 4194304 | tf_op jit(solution)/shard_map/opening/pallas_call | solution.py:584
  3.9 3.2 %collective-permute-start.1 = (bf16[256,512]{1,0:T(8,128)(2,1)S(1)}, bf16[256,512]{1,0:T(8,128)(2,1)S(1)}, u32[]{:S(2)}, u32[]{:S(2)}) collective-permute-start(bf16[256,512]{1,0:T(8,128)(2,1)S(1)} %get-tuple-element.37), channel_id=1, source_target_pairs={{0,4},{12,8},{4,0},{8,12},{1,5},{13,9},{5,1},{9,13},{2,6},{14,10},... | collective-permute-start | bytes 786440 | tf_op jit(solution)/shard_map/ppermute | solution.py:653
  7.1 0.7 %collective-permute-start = (bf16[256,512]{1,0:T(8,128)(2,1)S(1)}, bf16[256,512]{1,0:T(8,128)(2,1)S(1)}, u32[]{:S(2)}, u32[]{:S(2)}) collective-permute-start(bf16[256,512]{1,0:T(8,128)(2,1)S(1)} %get-tuple-element.37), channel_id=1, source_target_pairs={{4,8},{8,4},{5,9},{9,5},{6,10},{10,6},{7,11},{11,7},{20,24},{24,20... | collective-permute-start | bytes 786440 | tf_op jit(solution)/shard_map/ppermute | solution.py:654
  7.7 6.3 %collective-permute-start.5 = (bf16[144,1024]{1,0:T(8,128)(2,1)S(1)}, bf16[144,1024]{1,0:T(8,128)(2,1)S(1)}, u32[]{:S(2)}, u32[]{:S(2)}) collective-permute-start(bf16[144,1024]{1,0:T(8,128)(2,1)S(1)} %get-tuple-element.59), channel_id=1, source_target_pairs={{0,4},{12,8},{1,5},{13,9},{2,6},{14,10},{3,7},{15,11},{16,20},{28,... | collective-permute-start | bytes 884744 | tf_op jit(solution)/shard_map/ppermute | solution.py:708
  14.1 4.2 %local.1 = (f32[256,1024]{1,0:T(8,128)S(1)}, f32[256,1024]{1,0:T(8,128)S(1)}, f32[256,1024]{1,0:T(8,128)S(1)}, f32[256,1024]{1,0:T(8,128)S(1)}, f32[256,1024]{1,0:T(8,128)S(1)}, /*index=5*/f32[256,1024]{1,0:T(8,128)S(1)}) custom-call(s32[1,1024]{1,0:T(1,128)} %docs_ref.7, bf16[256,2048]{1,0:T(8,128)(2,1)} %bitcast.32, bf16[256,2048]{1,0:T(8,128)(2,1)} %bitcast.33, ...), custom_call_target="tpu_custom_call" | custom-call | flops 134217728 | bytes 8388608 | tf_op jit(solution)/shard_map/local/pallas_call | solution.py:616
  18.3 0.0 collective-permute-done.1.refs_0_
  18.3 0.0 collective-permute-done.kv_ref.refs_1_
  18.3 0.1 collective-permute-start.3
  18.4 0.7 %collective-permute-start.2 = (bf16[256,512]{1,0:T(8,128)(2,1)S(1)}, bf16[256,512]{1,0:T(8,128)(2,1)S(1)}, u32[]{:S(2)}, u32[]{:S(2)}) collective-permute-start(bf16[256,512]{1,0:T(8,128)(2,1)S(1)} %collective-permute-done.1.refs_0_), channel_id=1, source_target_pairs={{4,8},{8,4},{5,9},{9,5},{6,10},{10,6},{7,11},{11,7},{20,24},{24,20... | collective-permute-start | bytes 786440 | tf_op jit(solution)/shard_map/ppermute | solution.py:656
  19.1 2.4 %collective-permute-done.5.got_ref.refs_0_ = bf16[144,1024]{1,0:T(8,128)(2,1)S(1)} collective-permute-done((bf16[144,1024]{1,0:T(8,128)(2,1)S(1)}, bf16[144,1024]{1,0:T(8,128)(2,1)S(1)}, u32[]{:S(2)}, u32[]{:S(2)}) %collective-permute-start.5) | collective-permute-done | bytes 294944 | tf_op jit(solution)/shard_map/ppermute | solution.py:708
  21.5 0.7 %collective-permute-start.6 = (bf16[144,1024]{1,0:T(8,128)(2,1)S(1)}, bf16[144,1024]{1,0:T(8,128)(2,1)S(1)}, u32[]{:S(2)}, u32[]{:S(2)}) collective-permute-start(bf16[144,1024]{1,0:T(8,128)(2,1)S(1)} %chain.5), channel_id=1, source_target_pairs={{4,8},{8,4},{5,9},{9,5},{6,10},{10,6},{7,11},{11,7},{20,24},{24,20... | collective-permute-start | bytes 884744 | tf_op jit(solution)/shard_map/ppermute | solution.py:708
  22.2 4.1 %collective-permute-done.3.got_ref.refs_3_.refs_0_ = bf16[144,1024]{1,0:T(8,128)(2,1)S(1)} collective-permute-done((bf16[144,1024]{1,0:T(8,128)(2,1)S(1)}, bf16[144,1024]{1,0:T(8,128)(2,1)S(1)}, u32[]{:S(2)}, u32[]{:S(2)}) %collective-permute-start.3) | collective-permute-done | bytes 294944 | tf_op jit(solution)/shard_map/ppermute | solution.py:666
  26.3 0.7 %collective-permute-start.8 = (bf16[144,1024]{1,0:T(8,128)(2,1)S(1)}, bf16[144,1024]{1,0:T(8,128)(2,1)S(1)}, u32[]{:S(2)}, u32[]{:S(2)}) collective-permute-start(bf16[144,1024]{1,0:T(8,128)(2,1)S(1)} %chain.4), channel_id=1, source_target_pairs={{4,8},{8,4},{5,9},{9,5},{6,10},{10,6},{7,11},{11,7},{20,24},{24,20... | collective-permute-start | bytes 884744 | tf_op jit(solution)/shard_map/ppermute | solution.py:669
  27.0 0.0 collective-permute-done.2.refs_2_
  27.0 1.3 %collective-permute-start.4 = (bf16[256,512]{1,0:T(8,128)(2,1)S(1)}, bf16[256,512]{1,0:T(8,128)(2,1)S(1)}, u32[]{:S(2)}, u32[]{:S(2)}) collective-permute-start(bf16[256,512]{1,0:T(8,128)(2,1)S(1)} %collective-permute-done.2.refs_2_), channel_id=1, source_target_pairs={{4,0},{8,12},{5,1},{9,13},{6,2},{10,14},{7,3},{11,15},{20,16},{24,... | collective-permute-start | bytes 786440 | tf_op jit(solution)/shard_map/ppermute | solution.py:671
  28.3 0.0 collective-permute-done.6.got_ref.refs_1_
  28.3 0.0 copy-start
  28.3 0.0 copy-start.1
  28.4 0.0 copy-start.2
  28.4 1.4 %collective-permute-start.7 = (bf16[144,1024]{1,0:T(8,128)(2,1)S(1)}, bf16[144,1024]{1,0:T(8,128)(2,1)S(1)}, u32[]{:S(2)}, u32[]{:S(2)}) collective-permute-start(bf16[144,1024]{1,0:T(8,128)(2,1)S(1)} %chain.6), channel_id=1, source_target_pairs={{8,12},{4,0},{9,13},{5,1},{10,14},{6,2},{11,15},{7,3},{24,28},{20,... | collective-permute-start | bytes 884744 | tf_op jit(solution)/shard_map/ppermute | solution.py:708
  29.8 0.0 collective-permute-done.8.got_ref.refs_1_
  29.8 0.0 copy-start.4
  29.8 1.3 %collective-permute-start.9 = (bf16[144,1024]{1,0:T(8,128)(2,1)S(1)}, bf16[144,1024]{1,0:T(8,128)(2,1)S(1)}, u32[]{:S(2)}, u32[]{:S(2)}) collective-permute-start(bf16[144,1024]{1,0:T(8,128)(2,1)S(1)} %chain.7), channel_id=1, source_target_pairs={{8,12},{4,0},{9,13},{5,1},{10,14},{6,2},{11,15},{7,3},{24,28},{20,... | collective-permute-start | bytes 884744 | tf_op jit(solution)/shard_map/ppermute | solution.py:708
  31.1 8.9 %collective-permute-done.4.refs_4_ = bf16[256,512]{1,0:T(8,128)(2,1)S(1)} collective-permute-done((bf16[256,512]{1,0:T(8,128)(2,1)S(1)}, bf16[256,512]{1,0:T(8,128)(2,1)S(1)}, u32[]{:S(2)}, u32[]{:S(2)}) %collective-permute-start.4) | collective-permute-done | bytes 262176 | tf_op jit(solution)/shard_map/ppermute | solution.py:671
  40.0 0.0 copy-done
  40.0 0.0 copy-done.1
  40.0 0.0 copy-done.2
  40.0 0.0 copy-done.4
  40.1 2.8 %attention.3.refs_1_.teacher_ref = bf16[256,1024]{1,0:T(8,128)(2,1)S(1)} custom-call(s32[1,1024]{1,0:T(1,128)S(1)} %copy-done.4, bf16[256,2048]{1,0:T(8,128)(2,1)S(1)} %bitcast.18, bf16[256,256]{1,0:T(8,128)(2,1)S(1)} %bitcast.21, bf16[256,256]{1,0:T(8,128)(2,1)S(1)} %bitcast.24, bf16[256,512]{1,0:T(8,128)(2,1)S(1)} %collective-permute-done.1.refs_0_, ...), custom_call_target="tpu_custom_call" | custom-call | flops 603979776 | bytes 2097152 | tf_op jit(solution)/shard_map/attention/pallas_call | solution.py:682
  42.9 0.0 copy-start.3
  42.9 0.0 copy-start.5
  42.9 2.8 %attention.2.refs_0_.teacher_ref = bf16[256,1024]{1,0:T(8,128)(2,1)S(1)} custom-call(s32[1,1024]{1,0:T(1,128)S(1)} %copy-done.4, bf16[256,2048]{1,0:T(8,128)(2,1)S(1)} %bitcast.19, bf16[256,256]{1,0:T(8,128)(2,1)S(1)} %bitcast.22, bf16[256,256]{1,0:T(8,128)(2,1)S(1)} %bitcast.25, bf16[256,512]{1,0:T(8,128)(2,1)S(1)} %collective-permute-done.1.refs_0_, ...), custom_call_target="tpu_custom_call" | custom-call | flops 603979776 | bytes 2097152 | tf_op jit(solution)/shard_map/attention/pallas_call | solution.py:682
  45.7 1.1 %collective-permute-done.7.refs_2_ = bf16[144,1024]{1,0:T(8,128)(2,1)S(1)} collective-permute-done((bf16[144,1024]{1,0:T(8,128)(2,1)S(1)}, bf16[144,1024]{1,0:T(8,128)(2,1)S(1)}, u32[]{:S(2)}, u32[]{:S(2)}) %collective-permute-start.7) | collective-permute-done | bytes 294944 | tf_op jit(solution)/shard_map/ppermute | solution.py:708
  46.8 0.0 copy-done.3
  46.8 1.8 %final.2 = (bf16[256,1024]{1,0:T(8,128)(2,1)S(1)}, f32[3,1024]{1,0:T(4,128)S(1)}) custom-call(f32[256,1024]{1,0:T(8,128)S(1)} %get-tuple-element.54.pre_ref, f32[256,1024]{1,0:T(8,128)S(1)} %get-tuple-element.55.reach_ref, f32[256,1024]{1,0:T(8,128)S(1)} %get-tuple-element.56.sx_ref, bf16[256,256]{1,0:T(8,128)(2,1)S(1)} %bitcast.27, ...), custom_call_target="tpu_custom_call" | custom-call | flops 67108864 | bytes 5242880 | tf_op jit(solution)/shard_map/final/pallas_call | solution.py:712
  48.6 2.1 %collective-permute-done.9.refs_2_ = bf16[144,1024]{1,0:T(8,128)(2,1)S(1)} collective-permute-done((bf16[144,1024]{1,0:T(8,128)(2,1)S(1)}, bf16[144,1024]{1,0:T(8,128)(2,1)S(1)}, u32[]{:S(2)}, u32[]{:S(2)}) %collective-permute-start.9) | collective-permute-done | bytes 294944 | tf_op jit(solution)/shard_map/ppermute | solution.py:708
  50.7 1.8 %final.3 = (bf16[256,1024]{1,0:T(8,128)(2,1)S(1)}, f32[3,1024]{1,0:T(4,128)S(1)}) custom-call(f32[256,1024]{1,0:T(8,128)S(1)} %get-tuple-element.62.pre_ref, f32[256,1024]{1,0:T(8,128)S(1)} %get-tuple-element.63.reach_ref, f32[256,1024]{1,0:T(8,128)S(1)} %get-tuple-element.64.sx_ref, bf16[256,256]{1,0:T(8,128)(2,1)S(1)} %bitcast.28, ...), custom_call_target="tpu_custom_call" | custom-call | flops 67108864 | bytes 5242880 | tf_op jit(solution)/shard_map/final/pallas_call | solution.py:712
  52.5 1.2 %collective-permute-start.12 = (f32[3,1024]{1,0:T(4,128)S(1)}, f32[3,1024]{1,0:T(4,128)S(1)}, u32[]{:S(2)}, u32[]{:S(2)}) collective-permute-start(f32[3,1024]{1,0:T(4,128)S(1)} %get-tuple-element.67), channel_id=1, source_target_pairs={{0,20},{4,16},{8,28},{12,24},{16,4},{20,0},{24,12},{28,8},{1,21},{... | collective-permute-start | bytes 36872 | tf_op jit(solution)/shard_map/ppermute | solution.py:535
  53.7 0.5 collective-permute-start.11
  54.2 1.8 %collective-permute-start.10 = (f32[3,1024]{1,0:T(4,128)S(1)}, f32[3,1024]{1,0:T(4,128)S(1)}, u32[]{:S(2)}, u32[]{:S(2)}) collective-permute-start(f32[3,1024]{1,0:T(4,128)S(1)} %get-tuple-element.67), channel_id=1, source_target_pairs={{0,4},{4,0},{8,12},{12,8},{16,20},{20,16},{24,28},{28,24},{1,5},{5... | collective-permute-start | bytes 36872 | tf_op jit(solution)/shard_map/ppermute | solution.py:535
  56.0 1.1 %collective-permute-done.12 = f32[3,1024]{1,0:T(4,128)S(1)} collective-permute-done((f32[3,1024]{1,0:T(4,128)S(1)}, f32[3,1024]{1,0:T(4,128)S(1)}, u32[]{:S(2)}, u32[]{:S(2)}) %collective-permute-start.12) | collective-permute-done | bytes 12320 | tf_op jit(solution)/shard_map/ppermute | solution.py:535
  57.2 0.3 collective-permute-done.11
  57.4 0.6 collective-permute-done.10
  58.1 1.7 %collective-permute-start.13 = (f32[3,1024]{1,0:T(4,128)S(1)}, f32[3,1024]{1,0:T(4,128)S(1)}, u32[]{:S(2)}, u32[]{:S(2)}) collective-permute-start(f32[3,1024]{1,0:T(4,128)S(1)} %add_add_fusion.a_ref), channel_id=1, source_target_pairs={{0,8},{4,12},{8,0},{12,4},{16,24},{20,28},{24,16},{28,20},{1,9},{5... | collective-permute-start | bytes 36872 | tf_op jit(solution)/shard_map/ppermute | solution.py:535
  59.7 1.0 %writing.2 = bf16[256,2048]{1,0:T(8,128)(2,1)} custom-call(bf16[256,1024]{1,0:T(8,128)(2,1)S(1)} %attention.2.refs_0_.teacher_ref, bf16[256,1024]{1,0:T(8,128)(2,1)S(1)} %attention.3.refs_1_.teacher_ref), custom_call_target="tpu_custom_call" | custom-call | bytes 2097152 | tf_op jit(solution)/shard_map/writing/pallas_call | solution.py:571
  60.7 1.0 %writing.3 = bf16[256,2048]{1,0:T(8,128)(2,1)} custom-call(bf16[256,1024]{1,0:T(8,128)(2,1)S(1)} %get-tuple-element.61.refs_0_, bf16[256,1024]{1,0:T(8,128)(2,1)S(1)} %get-tuple-element.66.refs_1_), custom_call_target="tpu_custom_call" | custom-call | bytes 2097152 | tf_op jit(solution)/shard_map/writing/pallas_call | solution.py:571
  61.7 1.0 %collective-permute-done.13.b_ref = f32[3,1024]{1,0:T(4,128)S(1)} collective-permute-done((f32[3,1024]{1,0:T(4,128)S(1)}, f32[3,1024]{1,0:T(4,128)S(1)}, u32[]{:S(2)}, u32[]{:S(2)}) %collective-permute-start.13) | collective-permute-done | bytes 12320 | tf_op jit(solution)/shard_map/ppermute | solution.py:535
  62.8 0.6 closing.1
  (7 shorter events, 0.1 us)
Async XLA Ops:
  3.9 14.4 %collective-permute-start.1 = (bf16[256,512]{1,0:T(8,128)(2,1)S(1)}, bf16[256,512]{1,0:T(8,128)(2,1)S(1)}, u32[]{:S(2)}, u32[]{:S(2)}) collective-permute-start(bf16[256,512]{1,0:T(8,128)(2,1)S(1)} %get-tuple-element.37), channel_id=1, source_target_pairs={{0,4},{12,8},{4,0},{8,12},{1,5},{13,9},{5,1},{9,13},{2,6},{14,10},... | collective-permute-start | bytes 786440 | tf_op jit(solution)/shard_map/ppermute | solution.py:653
  7.1 11.2 %collective-permute-start = (bf16[256,512]{1,0:T(8,128)(2,1)S(1)}, bf16[256,512]{1,0:T(8,128)(2,1)S(1)}, u32[]{:S(2)}, u32[]{:S(2)}) collective-permute-start(bf16[256,512]{1,0:T(8,128)(2,1)S(1)} %get-tuple-element.37), channel_id=1, source_target_pairs={{4,8},{8,4},{5,9},{9,5},{6,10},{10,6},{7,11},{11,7},{20,24},{24,20... | collective-permute-start | bytes 786440 | tf_op jit(solution)/shard_map/ppermute | solution.py:654
  7.7 13.7 %collective-permute-start.5 = (bf16[144,1024]{1,0:T(8,128)(2,1)S(1)}, bf16[144,1024]{1,0:T(8,128)(2,1)S(1)}, u32[]{:S(2)}, u32[]{:S(2)}) collective-permute-start(bf16[144,1024]{1,0:T(8,128)(2,1)S(1)} %get-tuple-element.59), channel_id=1, source_target_pairs={{0,4},{12,8},{1,5},{13,9},{2,6},{14,10},{3,7},{15,11},{16,20},{28,... | collective-permute-start | bytes 884744 | tf_op jit(solution)/shard_map/ppermute | solution.py:708
  18.3 8.0 %collective-permute-start.3 = (bf16[144,1024]{1,0:T(8,128)(2,1)S(1)}, bf16[144,1024]{1,0:T(8,128)(2,1)S(1)}, u32[]{:S(2)}, u32[]{:S(2)}) collective-permute-start(bf16[144,1024]{1,0:T(8,128)(2,1)S(1)} %merge.1), channel_id=1, source_target_pairs={{0,4},{12,8},{4,0},{8,12},{1,5},{13,9},{5,1},{9,13},{2,6},{14,10},... | collective-permute-start | bytes 884744 | tf_op jit(solution)/shard_map/ppermute | solution.py:666
  18.4 8.6 %collective-permute-start.2 = (bf16[256,512]{1,0:T(8,128)(2,1)S(1)}, bf16[256,512]{1,0:T(8,128)(2,1)S(1)}, u32[]{:S(2)}, u32[]{:S(2)}) collective-permute-start(bf16[256,512]{1,0:T(8,128)(2,1)S(1)} %collective-permute-done.1.refs_0_), channel_id=1, source_target_pairs={{4,8},{8,4},{5,9},{9,5},{6,10},{10,6},{7,11},{11,7},{20,24},{24,20... | collective-permute-start | bytes 786440 | tf_op jit(solution)/shard_map/ppermute | solution.py:656
  21.5 6.8 %collective-permute-start.6 = (bf16[144,1024]{1,0:T(8,128)(2,1)S(1)}, bf16[144,1024]{1,0:T(8,128)(2,1)S(1)}, u32[]{:S(2)}, u32[]{:S(2)}) collective-permute-start(bf16[144,1024]{1,0:T(8,128)(2,1)S(1)} %chain.5), channel_id=1, source_target_pairs={{4,8},{8,4},{5,9},{9,5},{6,10},{10,6},{7,11},{11,7},{20,24},{24,20... | collective-permute-start | bytes 884744 | tf_op jit(solution)/shard_map/ppermute | solution.py:708
  26.3 3.5 %collective-permute-start.8 = (bf16[144,1024]{1,0:T(8,128)(2,1)S(1)}, bf16[144,1024]{1,0:T(8,128)(2,1)S(1)}, u32[]{:S(2)}, u32[]{:S(2)}) collective-permute-start(bf16[144,1024]{1,0:T(8,128)(2,1)S(1)} %chain.4), channel_id=1, source_target_pairs={{4,8},{8,4},{5,9},{9,5},{6,10},{10,6},{7,11},{11,7},{20,24},{24,20... | collective-permute-start | bytes 884744 | tf_op jit(solution)/shard_map/ppermute | solution.py:669
  27.0 13.0 %collective-permute-start.4 = (bf16[256,512]{1,0:T(8,128)(2,1)S(1)}, bf16[256,512]{1,0:T(8,128)(2,1)S(1)}, u32[]{:S(2)}, u32[]{:S(2)}) collective-permute-start(bf16[256,512]{1,0:T(8,128)(2,1)S(1)} %collective-permute-done.2.refs_2_), channel_id=1, source_target_pairs={{4,0},{8,12},{5,1},{9,13},{6,2},{10,14},{7,3},{11,15},{20,16},{24,... | collective-permute-start | bytes 786440 | tf_op jit(solution)/shard_map/ppermute | solution.py:671
  28.3 11.7 %copy-start = (bf16[1,256,2048]{2,1,0:T(8,128)(2,1)S(1)}, bf16[1,256,2048]{2,1,0:T(8,128)(2,1)}, u32[]{:S(2)}) copy-start(bf16[1,256,2048]{2,1,0:T(8,128)(2,1)} %param.13) | copy-start | bytes 3145732
  28.3 11.7 %copy-start.1 = (bf16[1,256,256]{2,1,0:T(8,128)(2,1)S(1)}, bf16[1,256,256]{2,1,0:T(8,128)(2,1)}, u32[]{:S(2)}) copy-start(bf16[1,256,256]{2,1,0:T(8,128)(2,1)} %param.14) | copy-start | bytes 393220
  28.4 11.7 %copy-start.2 = (bf16[1,256,256]{2,1,0:T(8,128)(2,1)S(1)}, bf16[1,256,256]{2,1,0:T(8,128)(2,1)}, u32[]{:S(2)}) copy-start(bf16[1,256,256]{2,1,0:T(8,128)(2,1)} %param.15) | copy-start | bytes 393220
  28.4 18.4 %collective-permute-start.7 = (bf16[144,1024]{1,0:T(8,128)(2,1)S(1)}, bf16[144,1024]{1,0:T(8,128)(2,1)S(1)}, u32[]{:S(2)}, u32[]{:S(2)}) collective-permute-start(bf16[144,1024]{1,0:T(8,128)(2,1)S(1)} %chain.6), channel_id=1, source_target_pairs={{8,12},{4,0},{9,13},{5,1},{10,14},{6,2},{11,15},{7,3},{24,28},{20,... | collective-permute-start | bytes 884744 | tf_op jit(solution)/shard_map/ppermute | solution.py:708
  29.8 10.2 %copy-start.4 = (s32[1,1024]{1,0:T(1,128)S(1)}, s32[1,1024]{1,0:T(1,128)}, u32[]{:S(2)}) copy-start(s32[1,1024]{1,0:T(1,128)} %docs_ref.7) | copy-start | bytes 12292
  29.8 20.8 %collective-permute-start.9 = (bf16[144,1024]{1,0:T(8,128)(2,1)S(1)}, bf16[144,1024]{1,0:T(8,128)(2,1)S(1)}, u32[]{:S(2)}, u32[]{:S(2)}) collective-permute-start(bf16[144,1024]{1,0:T(8,128)(2,1)S(1)} %chain.7), channel_id=1, source_target_pairs={{8,12},{4,0},{9,13},{5,1},{10,14},{6,2},{11,15},{7,3},{24,28},{20,... | collective-permute-start | bytes 884744 | tf_op jit(solution)/shard_map/ppermute | solution.py:708
  42.9 3.9 %copy-start.3 = (bf16[1,256,256]{2,1,0:T(8,128)(2,1)S(1)}, bf16[1,256,256]{2,1,0:T(8,128)(2,1)}, u32[]{:S(2)}) copy-start(bf16[1,256,256]{2,1,0:T(8,128)(2,1)} %param.20) | copy-start | bytes 393220
  42.9 3.9 %copy-start.5 = (f32[2048]{0:T(1024)S(1)}, f32[2048]{0:T(1024)}, u32[]{:S(2)}) copy-start(f32[2048]{0:T(1024)} %param.25) | copy-start | bytes 24580
  52.5 4.7 %collective-permute-start.12 = (f32[3,1024]{1,0:T(4,128)S(1)}, f32[3,1024]{1,0:T(4,128)S(1)}, u32[]{:S(2)}, u32[]{:S(2)}) collective-permute-start(f32[3,1024]{1,0:T(4,128)S(1)} %get-tuple-element.67), channel_id=1, source_target_pairs={{0,20},{4,16},{8,28},{12,24},{16,4},{20,0},{24,12},{28,8},{1,21},{... | collective-permute-start | bytes 36872 | tf_op jit(solution)/shard_map/ppermute | solution.py:535
  53.7 3.7 %collective-permute-start.11 = (f32[3,1024]{1,0:T(4,128)S(1)}, f32[3,1024]{1,0:T(4,128)S(1)}, u32[]{:S(2)}, u32[]{:S(2)}) collective-permute-start(f32[3,1024]{1,0:T(4,128)S(1)} %get-tuple-element.67), channel_id=1, source_target_pairs={{0,16},{4,20},{8,24},{12,28},{16,0},{20,4},{24,8},{28,12},{1,17},{... | collective-permute-start | bytes 36872 | tf_op jit(solution)/shard_map/ppermute | solution.py:535
  54.2 3.9 %collective-permute-start.10 = (f32[3,1024]{1,0:T(4,128)S(1)}, f32[3,1024]{1,0:T(4,128)S(1)}, u32[]{:S(2)}, u32[]{:S(2)}) collective-permute-start(f32[3,1024]{1,0:T(4,128)S(1)} %get-tuple-element.67), channel_id=1, source_target_pairs={{0,4},{4,0},{8,12},{12,8},{16,20},{20,16},{24,28},{28,24},{1,5},{5... | collective-permute-start | bytes 36872 | tf_op jit(solution)/shard_map/ppermute | solution.py:535
  58.1 4.7 %collective-permute-start.13 = (f32[3,1024]{1,0:T(4,128)S(1)}, f32[3,1024]{1,0:T(4,128)S(1)}, u32[]{:S(2)}, u32[]{:S(2)}) collective-permute-start(f32[3,1024]{1,0:T(4,128)S(1)} %add_add_fusion.a_ref), channel_id=1, source_target_pairs={{0,8},{4,12},{8,0},{12,4},{16,24},{20,28},{24,16},{28,20},{1,9},{5... | collective-permute-start | bytes 36872 | tf_op jit(solution)/shard_map/ppermute | solution.py:535

commit v12 on v11

--- a/solution.py
+++ b/solution.py
@@ -652,7 +652,8 @@
         inward, outward, across = [(0, 1), (3, 2)], [(1, 0), (2, 3)], [(1, 2), (2, 1)]
         near = lax.ppermute(kv, "ctx", inward + outward)
         middle = lax.ppermute(kv, "ctx", across)
-        middle, near, *local = lax.optimization_barrier((middle, near, *local))
+        near, *local = lax.optimization_barrier((near, *local))
+        middle, _ = lax.optimization_barrier((middle, near))
         beyond = lax.ppermute(near, "ctx", across)
         send[-1] = pl.pallas_call(
             functools.partial(merge_kernel, count),
@@ -665,10 +666,15 @@
         )(send[-1], middle)
         far = lax.ppermute(send[-1], "ctx", inward + outward)
         got[-1].append(far)
-        send[-1] = passed_on(groups - 1, 1)
-        got[-1].append(lax.ppermute(send[-1], "ctx", stage_pairs(2)))
-        beyond, _ = lax.optimization_barrier((beyond, send[-1]))
         farther = lax.ppermute(beyond, "ctx", outward)
+        if groups > 1:
+            got[0].append(lax.ppermute(send[0], "ctx", stage_pairs(1)))
+            got[0][0], _ = lax.optimization_barrier((got[0][0], beyond))
+            send[0] = passed_on(0, 1)
+            got[0].append(lax.ppermute(send[0], "ctx", stage_pairs(2)))
+            send[0] = passed_on(0, 2)
+            got[0].append(lax.ppermute(send[0], "ctx", stage_pairs(3)))
+            farther, _ = lax.optimization_barrier((farther, send[0]))
         kv_got = [near, middle, beyond, far, farther]
     else:
         ring = ring_order(count)
@@ -703,6 +709,8 @@
         for g in range(groups):
             if len(got[g]) >= r:
                 continue
+            if r == 3 and g == groups - 1:
+                got[g][-1], targets[0] = lax.optimization_barrier((got[g][-1], targets[0]))
             if r > 1:
                 send[g] = passed_on(g, r - 1)
             got[g].append(lax.ppermute(send[g], "ctx", stage_pairs(r)))

time: 63.7 us -> 64 us (level)
    ppermute x1 -> x3, starting transfers between devices: 0.67 us -> 8.27 us  [the longest x1 6.31 us: body(): got[0].append(lax.ppermute(send[0], 'ctx', stage_pairs(1)))]
    ppermute x4 -> x2, starting transfers between devices: 9.69 us -> 2.23 us  [body(): got[g].append(lax.ppermute(send[g], 'ctx', stage_pairs(r)))]
    ppermute x1 -> x3, waiting for transfers between devices: 0.01 us -> 4.82 us  [the longest x1 4.2 us: body(): got[0].append(lax.ppermute(send[0], 'ctx', stage_pairs(3)))]
    ppermute x4 -> x2, waiting for transfers between devices: 5.61 us -> 2.51 us  [body(): got[g].append(lax.ppermute(send[g], 'ctx', stage_pairs(r)))]
    ppermute x1, waiting for transfers between devices: 8.89 us -> 6.33 us  [body(): farther = lax.ppermute(beyond, 'ctx', outward)]
  transfers between devices with their start and end apart: 14 -> 14, of which waited for: 9 -> 8; matrix products, arithmetic and copies ran while one was open for 0% -> 0% of each run, Pallas kernels for 21% -> 21%
where the time goes in v12:
time: 64 us; the launch traced here: 63.6 us
  waiting for transfers between devices  21.8 us (34%)
  starting transfers between devices  21.7 us (34%)
  Pallas kernels  19.3 us (30%)
  between operations  0.85 us (1%)
    ppermute x1, waiting for transfers between devices, body(): farther = lax.ppermute(beyond, 'ctx', outward)  6.33 us
    ppermute x1, starting transfers between devices, body(): got[0].append(lax.ppermute(send[0], 'ctx', stage_pairs(1)))  6.31 us
    pallas_call x2, Pallas kernels, body(): pl.pallas_call(functools.partial(attention_kernel, count, per_kv, stack,...  5.58 us
    ppermute x4, starting transfers between devices, exchange(): return lax.ppermute(part, axes, [(d, d ^ shift) for d in range(size)])  4.69 us
    ppermute x1, waiting for transfers between devices, body(): far = lax.ppermute(send[-1], 'ctx', inward + outward)  4.69 us
    ppermute x1, waiting for transfers between devices, body(): got[0].append(lax.ppermute(send[0], 'ctx', stage_pairs(3)))  4.2 us
    pallas_call x1, Pallas kernels, body(): pl.pallas_call(functools.partial(local_kernel, count, groups), out_shape=...  4.2 us
    pallas_call x2, Pallas kernels, body(): pl.pallas_call(functools.partial(final_kernel, count, g, groups, loss_sca...  3.57 us
  transfers between devices with their start and end apart: 14, of which 8 were waited for; matrix products, arithmetic and copies ran while one was open for 0% of the time, Pallas kernels for 21%

profile of v12, /device:TPU:0, one launch (start us, length us, event | category | flops | bytes accessed | tf_op | source)
XLA Modules:
  0.0 63.6 jit_solution(7557041871270237021)
XLA Ops:
  0.6 3.2 %opening.1 = (bf16[256,512]{1,0:T(8,128)(2,1)S(1)}, f32[32,256]{1,0:T(8,128)S(1)}, bf16[256,1024]{1,0:T(8,128)(2,1)S(1)}, bf16[256,1024]{1,0:T(8,128)(2,1)S(1)},...) custom-call(s32[1,1024]{1,0:T(1,128)} %docs_ref.7, ...), custom_call_target="tpu_custom_call" | custom-call | flops 268435456 | bytes 4194304 | tf_op jit(solution)/shard_map/opening/pallas_call | solution.py:584
  3.9 3.2 %collective-permute-start.1 = (bf16[256,512]{1,0:T(8,128)(2,1)S(1)}, bf16[256,512]{1,0:T(8,128)(2,1)S(1)}, u32[]{:S(2)}, u32[]{:S(2)}) collective-permute-start(bf16[256,512]{1,0:T(8,128)(2,1)S(1)} %get-tuple-element.41), channel_id=1, source_target_pairs={{0,4},{12,8},{4,0},{8,12},{1,5},{13,9},{5,1},{9,13},{2,6},{14,10},... | collective-permute-start | bytes 786440 | tf_op jit(solution)/shard_map/ppermute | solution.py:653
  7.1 0.7 %collective-permute-start = (bf16[256,512]{1,0:T(8,128)(2,1)S(1)}, bf16[256,512]{1,0:T(8,128)(2,1)S(1)}, u32[]{:S(2)}, u32[]{:S(2)}) collective-permute-start(bf16[256,512]{1,0:T(8,128)(2,1)S(1)} %get-tuple-element.41), channel_id=1, source_target_pairs={{4,8},{8,4},{5,9},{9,5},{6,10},{10,6},{7,11},{11,7},{20,24},{24,20... | collective-permute-start | bytes 786440 | tf_op jit(solution)/shard_map/ppermute | solution.py:654
  7.7 6.3 %collective-permute-start.6 = (bf16[144,1024]{1,0:T(8,128)(2,1)S(1)}, bf16[144,1024]{1,0:T(8,128)(2,1)S(1)}, u32[]{:S(2)}, u32[]{:S(2)}) collective-permute-start(bf16[144,1024]{1,0:T(8,128)(2,1)S(1)} %get-tuple-element.56), channel_id=1, source_target_pairs={{0,4},{12,8},{1,5},{13,9},{2,6},{14,10},{3,7},{15,11},{16,20},{28,... | collective-permute-start | bytes 884744 | tf_op jit(solution)/shard_map/ppermute | solution.py:671
  14.1 4.2 %local.1 = (f32[256,1024]{1,0:T(8,128)S(1)}, f32[256,1024]{1,0:T(8,128)S(1)}, f32[256,1024]{1,0:T(8,128)S(1)}, f32[256,1024]{1,0:T(8,128)S(1)}, f32[256,1024]{1,0:T(8,128)S(1)}, /*index=5*/f32[256,1024]{1,0:T(8,128)S(1)}) custom-call(s32[1,1024]{1,0:T(1,128)} %docs_ref.7, bf16[256,2048]{1,0:T(8,128)(2,1)} %bitcast.32, bf16[256,2048]{1,0:T(8,128)(2,1)} %bitcast.33, ...), custom_call_target="tpu_custom_call" | custom-call | flops 134217728 | bytes 8388608 | tf_op jit(solution)/shard_map/local/pallas_call | solution.py:616
  18.3 0.0 collective-permute-done.1.refs_0_
  18.3 0.7 %collective-permute-start.4 = (bf16[256,512]{1,0:T(8,128)(2,1)S(1)}, bf16[256,512]{1,0:T(8,128)(2,1)S(1)}, u32[]{:S(2)}, u32[]{:S(2)}) collective-permute-start(bf16[256,512]{1,0:T(8,128)(2,1)S(1)} %collective-permute-done.1.refs_0_), channel_id=1, source_target_pairs={{4,8},{8,4},{5,9},{9,5},{6,10},{10,6},{7,11},{11,7},{20,24},{24,20... | collective-permute-start | bytes 786440 | tf_op jit(solution)/shard_map/ppermute | solution.py:657
  19.0 0.0 collective-permute-done.kv_ref.refs_1_
  19.0 0.7 %collective-permute-start.2 = (bf16[144,1024]{1,0:T(8,128)(2,1)S(1)}, bf16[144,1024]{1,0:T(8,128)(2,1)S(1)}, u32[]{:S(2)}, u32[]{:S(2)}) collective-permute-start(bf16[144,1024]{1,0:T(8,128)(2,1)S(1)} %merge.1), channel_id=1, source_target_pairs={{0,4},{12,8},{4,0},{8,12},{1,5},{13,9},{5,1},{9,13},{2,6},{14,10},... | collective-permute-start | bytes 884744 | tf_op jit(solution)/shard_map/ppermute | solution.py:667
  19.7 0.6 collective-permute-done.6.got_ref.refs_0_
  20.3 0.0 collective-permute-done.4.refs_2_
  20.3 0.7 %collective-permute-start.7 = (bf16[144,1024]{1,0:T(8,128)(2,1)S(1)}, bf16[144,1024]{1,0:T(8,128)(2,1)S(1)}, u32[]{:S(2)}, u32[]{:S(2)}) collective-permute-start(bf16[144,1024]{1,0:T(8,128)(2,1)S(1)} %chain.5), channel_id=1, source_target_pairs={{4,8},{8,4},{5,9},{9,5},{6,10},{10,6},{7,11},{11,7},{20,24},{24,20... | collective-permute-start | bytes 884744 | tf_op jit(solution)/shard_map/ppermute | solution.py:674
  21.0 1.3 %collective-permute-start.5 = (bf16[256,512]{1,0:T(8,128)(2,1)S(1)}, bf16[256,512]{1,0:T(8,128)(2,1)S(1)}, u32[]{:S(2)}, u32[]{:S(2)}) collective-permute-start(bf16[256,512]{1,0:T(8,128)(2,1)S(1)} %collective-permute-done.4.refs_2_), channel_id=1, source_target_pairs={{4,0},{8,12},{5,1},{9,13},{6,2},{10,14},{7,3},{11,15},{20,16},{24,... | collective-permute-start | bytes 786440 | tf_op jit(solution)/shard_map/ppermute | solution.py:669
  22.3 4.7 %collective-permute-done.2.got_ref.refs_3_.refs_0_ = bf16[144,1024]{1,0:T(8,128)(2,1)S(1)} collective-permute-done((bf16[144,1024]{1,0:T(8,128)(2,1)S(1)}, bf16[144,1024]{1,0:T(8,128)(2,1)S(1)}, u32[]{:S(2)}, u32[]{:S(2)}) %collective-permute-start.2) | collective-permute-done | bytes 294944 | tf_op jit(solution)/shard_map/ppermute | solution.py:667
  27.0 0.0 copy-start
  27.0 0.0 copy-start.1
  27.0 0.8 %collective-permute-start.3 = (bf16[144,1024]{1,0:T(8,128)(2,1)S(1)}, bf16[144,1024]{1,0:T(8,128)(2,1)S(1)}, u32[]{:S(2)}, u32[]{:S(2)}) collective-permute-start(bf16[144,1024]{1,0:T(8,128)(2,1)S(1)} %chain.4), channel_id=1, source_target_pairs={{4,8},{8,4},{5,9},{9,5},{6,10},{10,6},{7,11},{11,7},{20,24},{24,20... | collective-permute-start | bytes 884744 | tf_op jit(solution)/shard_map/ppermute | solution.py:716
  27.8 0.0 collective-permute-done.7.got_ref.refs_1_
  27.8 0.0 copy-start.4
  27.9 1.3 %collective-permute-start.8 = (bf16[144,1024]{1,0:T(8,128)(2,1)S(1)}, bf16[144,1024]{1,0:T(8,128)(2,1)S(1)}, u32[]{:S(2)}, u32[]{:S(2)}) collective-permute-start(bf16[144,1024]{1,0:T(8,128)(2,1)S(1)} %chain.6), channel_id=1, source_target_pairs={{8,12},{4,0},{9,13},{5,1},{10,14},{6,2},{11,15},{7,3},{24,28},{20,... | collective-permute-start | bytes 884744 | tf_op jit(solution)/shard_map/ppermute | solution.py:676
  29.2 6.3 %collective-permute-done.5.refs_4_ = bf16[256,512]{1,0:T(8,128)(2,1)S(1)} collective-permute-done((bf16[256,512]{1,0:T(8,128)(2,1)S(1)}, bf16[256,512]{1,0:T(8,128)(2,1)S(1)}, u32[]{:S(2)}, u32[]{:S(2)}) %collective-permute-start.5) | collective-permute-done | bytes 262176 | tf_op jit(solution)/shard_map/ppermute | solution.py:669
  35.5 0.0 copy-done
  35.5 0.0 copy-done.1
  35.5 0.0 copy-done.2
  35.5 0.0 copy-done.4
  35.5 2.8 %attention.2.refs_0_.teacher_ref = bf16[256,1024]{1,0:T(8,128)(2,1)S(1)} custom-call(s32[1,1024]{1,0:T(1,128)S(1)} %copy-done.4, bf16[256,2048]{1,0:T(8,128)(2,1)S(1)} %bitcast.18, bf16[256,256]{1,0:T(8,128)(2,1)S(1)} %bitcast.21, bf16[256,256]{1,0:T(8,128)(2,1)S(1)} %bitcast.24, bf16[256,512]{1,0:T(8,128)(2,1)S(1)} %collective-permute-done.1.refs_0_, ...), custom_call_target="tpu_custom_call" | custom-call | flops 603979776 | bytes 2097152 | tf_op jit(solution)/shard_map/attention/pallas_call | solution.py:688
  38.3 0.0 collective-permute-done.3.got_ref.refs_1_
  38.4 0.0 copy-start.3
  38.4 0.0 copy-start.5
  38.4 1.4 %collective-permute-start.9 = (bf16[144,1024]{1,0:T(8,128)(2,1)S(1)}, bf16[144,1024]{1,0:T(8,128)(2,1)S(1)}, u32[]{:S(2)}, u32[]{:S(2)}) collective-permute-start(bf16[144,1024]{1,0:T(8,128)(2,1)S(1)} %chain.7), channel_id=1, source_target_pairs={{8,12},{4,0},{9,13},{5,1},{10,14},{6,2},{11,15},{7,3},{24,28},{20,... | collective-permute-start | bytes 884744 | tf_op jit(solution)/shard_map/ppermute | solution.py:716
  39.8 2.8 %attention.3.refs_1_.teacher_ref = bf16[256,1024]{1,0:T(8,128)(2,1)S(1)} custom-call(s32[1,1024]{1,0:T(1,128)S(1)} %copy-done.4, bf16[256,2048]{1,0:T(8,128)(2,1)S(1)} %bitcast.19, bf16[256,256]{1,0:T(8,128)(2,1)S(1)} %bitcast.22, bf16[256,256]{1,0:T(8,128)(2,1)S(1)} %bitcast.25, bf16[256,512]{1,0:T(8,128)(2,1)S(1)} %collective-permute-done.1.refs_0_, ...), custom_call_target="tpu_custom_call" | custom-call | flops 603979776 | bytes 2097152 | tf_op jit(solution)/shard_map/attention/pallas_call | solution.py:688
  42.6 4.2 %collective-permute-done.8.refs_2_ = bf16[144,1024]{1,0:T(8,128)(2,1)S(1)} collective-permute-done((bf16[144,1024]{1,0:T(8,128)(2,1)S(1)}, bf16[144,1024]{1,0:T(8,128)(2,1)S(1)}, u32[]{:S(2)}, u32[]{:S(2)}) %collective-permute-start.8) | collective-permute-done | bytes 294944 | tf_op jit(solution)/shard_map/ppermute | solution.py:676
  46.8 0.0 copy-done.3
  46.8 0.0 copy-done.5
  46.8 1.8 %final.2 = (bf16[256,1024]{1,0:T(8,128)(2,1)S(1)}, f32[3,1024]{1,0:T(4,128)S(1)}) custom-call(f32[256,1024]{1,0:T(8,128)S(1)} %get-tuple-element.63.pre_ref, f32[256,1024]{1,0:T(8,128)S(1)} %get-tuple-element.64.reach_ref, f32[256,1024]{1,0:T(8,128)S(1)} %get-tuple-element.65.sx_ref, bf16[256,256]{1,0:T(8,128)(2,1)S(1)} %bitcast.27, ...), custom_call_target="tpu_custom_call" | custom-call | flops 67108864 | bytes 5242880 | tf_op jit(solution)/shard_map/final/pallas_call | solution.py:720
  48.6 2.5 %collective-permute-done.9.refs_2_ = bf16[144,1024]{1,0:T(8,128)(2,1)S(1)} collective-permute-done((bf16[144,1024]{1,0:T(8,128)(2,1)S(1)}, bf16[144,1024]{1,0:T(8,128)(2,1)S(1)}, u32[]{:S(2)}, u32[]{:S(2)}) %collective-permute-start.9) | collective-permute-done | bytes 294944 | tf_op jit(solution)/shard_map/ppermute | solution.py:716
  51.1 1.8 %final.3 = (bf16[256,1024]{1,0:T(8,128)(2,1)S(1)}, f32[3,1024]{1,0:T(4,128)S(1)}) custom-call(f32[256,1024]{1,0:T(8,128)S(1)} %get-tuple-element.67.pre_ref, f32[256,1024]{1,0:T(8,128)S(1)} %get-tuple-element.68.reach_ref, f32[256,1024]{1,0:T(8,128)S(1)} %get-tuple-element.69.sx_ref, bf16[256,256]{1,0:T(8,128)(2,1)S(1)} %bitcast.28, ...), custom_call_target="tpu_custom_call" | custom-call | flops 67108864 | bytes 5242880 | tf_op jit(solution)/shard_map/final/pallas_call | solution.py:720
  52.9 0.6 collective-permute-start.12
  53.5 1.1 %collective-permute-start.11 = (f32[3,1024]{1,0:T(4,128)S(1)}, f32[3,1024]{1,0:T(4,128)S(1)}, u32[]{:S(2)}, u32[]{:S(2)}) collective-permute-start(f32[3,1024]{1,0:T(4,128)S(1)} %get-tuple-element.73), channel_id=1, source_target_pairs={{0,16},{4,20},{8,24},{12,28},{16,0},{20,4},{24,8},{28,12},{1,17},{... | collective-permute-start | bytes 36872 | tf_op jit(solution)/shard_map/ppermute | solution.py:535
  54.6 1.9 %collective-permute-start.10 = (f32[3,1024]{1,0:T(4,128)S(1)}, f32[3,1024]{1,0:T(4,128)S(1)}, u32[]{:S(2)}, u32[]{:S(2)}) collective-permute-start(f32[3,1024]{1,0:T(4,128)S(1)} %get-tuple-element.73), channel_id=1, source_target_pairs={{0,4},{4,0},{8,12},{12,8},{16,20},{20,16},{24,28},{28,24},{1,5},{5... | collective-permute-start | bytes 36872 | tf_op jit(solution)/shard_map/ppermute | solution.py:535
  56.4 1.1 %collective-permute-done.12 = f32[3,1024]{1,0:T(4,128)S(1)} collective-permute-done((f32[3,1024]{1,0:T(4,128)S(1)}, f32[3,1024]{1,0:T(4,128)S(1)}, u32[]{:S(2)}, u32[]{:S(2)}) %collective-permute-start.12) | collective-permute-done | bytes 12320 | tf_op jit(solution)/shard_map/ppermute | solution.py:535
  57.6 0.0 collective-permute-done.11
  57.6 0.7 %collective-permute-done.10 = f32[3,1024]{1,0:T(4,128)S(1)} collective-permute-done((f32[3,1024]{1,0:T(4,128)S(1)}, f32[3,1024]{1,0:T(4,128)S(1)}, u32[]{:S(2)}, u32[]{:S(2)}) %collective-permute-start.10) | collective-permute-done | bytes 12320 | tf_op jit(solution)/shard_map/ppermute | solution.py:535
  58.3 1.1 %collective-permute-start.13 = (f32[3,1024]{1,0:T(4,128)S(1)}, f32[3,1024]{1,0:T(4,128)S(1)}, u32[]{:S(2)}, u32[]{:S(2)}) collective-permute-start(f32[3,1024]{1,0:T(4,128)S(1)} %add_add_fusion.a_ref), channel_id=1, source_target_pairs={{0,8},{4,12},{8,0},{12,4},{16,24},{20,28},{24,16},{28,20},{1,9},{5... | collective-permute-start | bytes 36872 | tf_op jit(solution)/shard_map/ppermute | solution.py:535
  59.5 1.0 %writing.2 = bf16[256,2048]{1,0:T(8,128)(2,1)} custom-call(bf16[256,1024]{1,0:T(8,128)(2,1)S(1)} %attention.2.refs_0_.teacher_ref, bf16[256,1024]{1,0:T(8,128)(2,1)S(1)} %attention.3.refs_1_.teacher_ref), custom_call_target="tpu_custom_call" | custom-call | bytes 2097152 | tf_op jit(solution)/shard_map/writing/pallas_call | solution.py:571
  60.5 1.0 %writing.3 = bf16[256,2048]{1,0:T(8,128)(2,1)} custom-call(bf16[256,1024]{1,0:T(8,128)(2,1)S(1)} %get-tuple-element.66.refs_0_, bf16[256,1024]{1,0:T(8,128)(2,1)S(1)} %get-tuple-element.72.refs_1_), custom_call_target="tpu_custom_call" | custom-call | bytes 2097152 | tf_op jit(solution)/shard_map/writing/pallas_call | solution.py:571
  61.5 1.6 %collective-permute-done.13.b_ref = f32[3,1024]{1,0:T(4,128)S(1)} collective-permute-done((f32[3,1024]{1,0:T(4,128)S(1)}, f32[3,1024]{1,0:T(4,128)S(1)}, u32[]{:S(2)}, u32[]{:S(2)}) %collective-permute-start.13) | collective-permute-done | bytes 12320 | tf_op jit(solution)/shard_map/ppermute | solution.py:535
  63.0 0.6 closing.1
  (7 shorter events, 0.1 us)
Async XLA Ops:
  3.9 14.4 %collective-permute-start.1 = (bf16[256,512]{1,0:T(8,128)(2,1)S(1)}, bf16[256,512]{1,0:T(8,128)(2,1)S(1)}, u32[]{:S(2)}, u32[]{:S(2)}) collective-permute-start(bf16[256,512]{1,0:T(8,128)(2,1)S(1)} %get-tuple-element.41), channel_id=1, source_target_pairs={{0,4},{12,8},{4,0},{8,12},{1,5},{13,9},{5,1},{9,13},{2,6},{14,10},... | collective-permute-start | bytes 786440 | tf_op jit(solution)/shard_map/ppermute | solution.py:653
  7.1 11.9 %collective-permute-start = (bf16[256,512]{1,0:T(8,128)(2,1)S(1)}, bf16[256,512]{1,0:T(8,128)(2,1)S(1)}, u32[]{:S(2)}, u32[]{:S(2)}) collective-permute-start(bf16[256,512]{1,0:T(8,128)(2,1)S(1)} %get-tuple-element.41), channel_id=1, source_target_pairs={{4,8},{8,4},{5,9},{9,5},{6,10},{10,6},{7,11},{11,7},{20,24},{24,20... | collective-permute-start | bytes 786440 | tf_op jit(solution)/shard_map/ppermute | solution.py:654
  7.7 12.6 %collective-permute-start.6 = (bf16[144,1024]{1,0:T(8,128)(2,1)S(1)}, bf16[144,1024]{1,0:T(8,128)(2,1)S(1)}, u32[]{:S(2)}, u32[]{:S(2)}) collective-permute-start(bf16[144,1024]{1,0:T(8,128)(2,1)S(1)} %get-tuple-element.56), channel_id=1, source_target_pairs={{0,4},{12,8},{1,5},{13,9},{2,6},{14,10},{3,7},{15,11},{16,20},{28,... | collective-permute-start | bytes 884744 | tf_op jit(solution)/shard_map/ppermute | solution.py:671
  18.3 2.0 %collective-permute-start.4 = (bf16[256,512]{1,0:T(8,128)(2,1)S(1)}, bf16[256,512]{1,0:T(8,128)(2,1)S(1)}, u32[]{:S(2)}, u32[]{:S(2)}) collective-permute-start(bf16[256,512]{1,0:T(8,128)(2,1)S(1)} %collective-permute-done.1.refs_0_), channel_id=1, source_target_pairs={{4,8},{8,4},{5,9},{9,5},{6,10},{10,6},{7,11},{11,7},{20,24},{24,20... | collective-permute-start | bytes 786440 | tf_op jit(solution)/shard_map/ppermute | solution.py:657
  19.0 8.0 %collective-permute-start.2 = (bf16[144,1024]{1,0:T(8,128)(2,1)S(1)}, bf16[144,1024]{1,0:T(8,128)(2,1)S(1)}, u32[]{:S(2)}, u32[]{:S(2)}) collective-permute-start(bf16[144,1024]{1,0:T(8,128)(2,1)S(1)} %merge.1), channel_id=1, source_target_pairs={{0,4},{12,8},{4,0},{8,12},{1,5},{13,9},{5,1},{9,13},{2,6},{14,10},... | collective-permute-start | bytes 884744 | tf_op jit(solution)/shard_map/ppermute | solution.py:667
  20.3 7.5 %collective-permute-start.7 = (bf16[144,1024]{1,0:T(8,128)(2,1)S(1)}, bf16[144,1024]{1,0:T(8,128)(2,1)S(1)}, u32[]{:S(2)}, u32[]{:S(2)}) collective-permute-start(bf16[144,1024]{1,0:T(8,128)(2,1)S(1)} %chain.5), channel_id=1, source_target_pairs={{4,8},{8,4},{5,9},{9,5},{6,10},{10,6},{7,11},{11,7},{20,24},{24,20... | collective-permute-start | bytes 884744 | tf_op jit(solution)/shard_map/ppermute | solution.py:674
  21.0 14.5 %collective-permute-start.5 = (bf16[256,512]{1,0:T(8,128)(2,1)S(1)}, bf16[256,512]{1,0:T(8,128)(2,1)S(1)}, u32[]{:S(2)}, u32[]{:S(2)}) collective-permute-start(bf16[256,512]{1,0:T(8,128)(2,1)S(1)} %collective-permute-done.4.refs_2_), channel_id=1, source_target_pairs={{4,0},{8,12},{5,1},{9,13},{6,2},{10,14},{7,3},{11,15},{20,16},{24,... | collective-permute-start | bytes 786440 | tf_op jit(solution)/shard_map/ppermute | solution.py:669
  27.0 8.5 %copy-start = (bf16[1,256,2048]{2,1,0:T(8,128)(2,1)S(1)}, bf16[1,256,2048]{2,1,0:T(8,128)(2,1)}, u32[]{:S(2)}) copy-start(bf16[1,256,2048]{2,1,0:T(8,128)(2,1)} %param.13) | copy-start | bytes 3145732
  27.0 8.5 %copy-start.1 = (bf16[1,256,256]{2,1,0:T(8,128)(2,1)S(1)}, bf16[1,256,256]{2,1,0:T(8,128)(2,1)}, u32[]{:S(2)}) copy-start(bf16[1,256,256]{2,1,0:T(8,128)(2,1)} %param.14) | copy-start | bytes 393220
  27.0 8.5 %copy-start.2 = (bf16[1,256,256]{2,1,0:T(8,128)(2,1)S(1)}, bf16[1,256,256]{2,1,0:T(8,128)(2,1)}, u32[]{:S(2)}) copy-start(bf16[1,256,256]{2,1,0:T(8,128)(2,1)} %param.15) | copy-start | bytes 393220
  27.0 11.3 %collective-permute-start.3 = (bf16[144,1024]{1,0:T(8,128)(2,1)S(1)}, bf16[144,1024]{1,0:T(8,128)(2,1)S(1)}, u32[]{:S(2)}, u32[]{:S(2)}) collective-permute-start(bf16[144,1024]{1,0:T(8,128)(2,1)S(1)} %chain.4), channel_id=1, source_target_pairs={{4,8},{8,4},{5,9},{9,5},{6,10},{10,6},{7,11},{11,7},{20,24},{24,20... | collective-permute-start | bytes 884744 | tf_op jit(solution)/shard_map/ppermute | solution.py:716
  27.8 7.7 %copy-start.4 = (s32[1,1024]{1,0:T(1,128)S(1)}, s32[1,1024]{1,0:T(1,128)}, u32[]{:S(2)}) copy-start(s32[1,1024]{1,0:T(1,128)} %docs_ref.7) | copy-start | bytes 12292
  27.9 18.9 %collective-permute-start.8 = (bf16[144,1024]{1,0:T(8,128)(2,1)S(1)}, bf16[144,1024]{1,0:T(8,128)(2,1)S(1)}, u32[]{:S(2)}, u32[]{:S(2)}) collective-permute-start(bf16[144,1024]{1,0:T(8,128)(2,1)S(1)} %chain.6), channel_id=1, source_target_pairs={{8,12},{4,0},{9,13},{5,1},{10,14},{6,2},{11,15},{7,3},{24,28},{20,... | collective-permute-start | bytes 884744 | tf_op jit(solution)/shard_map/ppermute | solution.py:676
  38.4 8.5 %copy-start.3 = (bf16[1,256,256]{2,1,0:T(8,128)(2,1)S(1)}, bf16[1,256,256]{2,1,0:T(8,128)(2,1)}, u32[]{:S(2)}) copy-start(bf16[1,256,256]{2,1,0:T(8,128)(2,1)} %param.20) | copy-start | bytes 393220
  38.4 8.4 %copy-start.5 = (f32[2048]{0:T(1024)S(1)}, f32[2048]{0:T(1024)}, u32[]{:S(2)}) copy-start(f32[2048]{0:T(1024)} %param.25) | copy-start | bytes 24580
  38.4 12.7 %collective-permute-start.9 = (bf16[144,1024]{1,0:T(8,128)(2,1)S(1)}, bf16[144,1024]{1,0:T(8,128)(2,1)S(1)}, u32[]{:S(2)}, u32[]{:S(2)}) collective-permute-start(bf16[144,1024]{1,0:T(8,128)(2,1)S(1)} %chain.7), channel_id=1, source_target_pairs={{8,12},{4,0},{9,13},{5,1},{10,14},{6,2},{11,15},{7,3},{24,28},{20,... | collective-permute-start | bytes 884744 | tf_op jit(solution)/shard_map/ppermute | solution.py:716
  52.9 4.7 %collective-permute-start.12 = (f32[3,1024]{1,0:T(4,128)S(1)}, f32[3,1024]{1,0:T(4,128)S(1)}, u32[]{:S(2)}, u32[]{:S(2)}) collective-permute-start(f32[3,1024]{1,0:T(4,128)S(1)} %get-tuple-element.73), channel_id=1, source_target_pairs={{0,20},{4,16},{8,28},{12,24},{16,4},{20,0},{24,12},{28,8},{1,21},{... | collective-permute-start | bytes 36872 | tf_op jit(solution)/shard_map/ppermute | solution.py:535
  53.5 4.1 %collective-permute-start.11 = (f32[3,1024]{1,0:T(4,128)S(1)}, f32[3,1024]{1,0:T(4,128)S(1)}, u32[]{:S(2)}, u32[]{:S(2)}) collective-permute-start(f32[3,1024]{1,0:T(4,128)S(1)} %get-tuple-element.73), channel_id=1, source_target_pairs={{0,16},{4,20},{8,24},{12,28},{16,0},{20,4},{24,8},{28,12},{1,17},{... | collective-permute-start | bytes 36872 | tf_op jit(solution)/shard_map/ppermute | solution.py:535
  54.6 3.7 %collective-permute-start.10 = (f32[3,1024]{1,0:T(4,128)S(1)}, f32[3,1024]{1,0:T(4,128)S(1)}, u32[]{:S(2)}, u32[]{:S(2)}) collective-permute-start(f32[3,1024]{1,0:T(4,128)S(1)} %get-tuple-element.73), channel_id=1, source_target_pairs={{0,4},{4,0},{8,12},{12,8},{16,20},{20,16},{24,28},{28,24},{1,5},{5... | collective-permute-start | bytes 36872 | tf_op jit(solution)/shard_map/ppermute | solution.py:535
  58.3 4.7 %collective-permute-start.13 = (f32[3,1024]{1,0:T(4,128)S(1)}, f32[3,1024]{1,0:T(4,128)S(1)}, u32[]{:S(2)}, u32[]{:S(2)}) collective-permute-start(f32[3,1024]{1,0:T(4,128)S(1)} %add_add_fusion.a_ref), channel_id=1, source_target_pairs={{0,8},{4,12},{8,0},{12,4},{16,24},{20,28},{24,16},{28,20},{1,9},{5... | collective-permute-start | bytes 36872 | tf_op jit(solution)/shard_map/ppermute | solution.py:535

commit v13 on v10

--- a/solution.py
+++ b/solution.py
@@ -508,12 +508,14 @@
     grad_ref[groups : groups + 1, :tile] = by_head
 
 
-def writing_kernel(*refs):
-    parts_in, out_ref, sems = refs[:-2], refs[-2], refs[-1]
-    width = parts_in[0].shape[1]
+def writing_kernel(count, first, *refs):
+    out_ref, sems = refs[-2:]
+    width = refs[0].shape[1]
     moves = [
-        pltpu.make_async_copy(part, out_ref.at[:, pl.ds(k * width, width)], sems.at[k])
-        for k, part in enumerate(parts_in)
+        pltpu.make_async_copy(
+            refs[k], out_ref.at[:, pl.ds((first + k) * width, width)], sems.at[k]
+        )
+        for k in range(count)
     ]
     for move in moves:
         move.start()
@@ -567,17 +569,19 @@
     def in_hbm(*arrays):
         return [pltpu.with_memory_space_constraint(array, pltpu.HBM) for array in arrays]
 
-    def write(*pieces):
+    def write(pieces, first=0, into=()):
+        anywhere = pl.BlockSpec(memory_space=pl.ANY)
         return pl.pallas_call(
-            writing_kernel,
+            functools.partial(writing_kernel, len(pieces), first),
             out_shape=struct((rows, features), BF16),
-            in_specs=[VMEM] * len(pieces),
-            out_specs=pl.BlockSpec(memory_space=pl.ANY),
+            in_specs=[VMEM] * len(pieces) + [anywhere] * len(into),
+            out_specs=anywhere,
             scratch_shapes=[pltpu.SemaphoreType.DMA((len(pieces),))],
+            input_output_aliases={len(pieces): 0} if into else {},
             compiler_params=params(2),
             cost_estimate=cost(0, 4 * rows * features),
             name="writing",
-        )(*pieces)
+        )(*pieces, *into)
 
     state = struct((N, width), BF16)
     payload = struct((N + EXTRA, width), BF16)
@@ -638,7 +642,7 @@
         inward, outward, across = [(0, 1), (3, 2)], [(1, 0), (2, 3)], [(1, 2), (2, 1)]
         near = lax.ppermute(kv, "ctx", inward + outward)
         middle = lax.ppermute(kv, "ctx", across)
-        middle, near, *local = lax.optimization_barrier((middle, near, *local))
+        middle, *local = lax.optimization_barrier((middle, *local))
         beyond = lax.ppermute(near, "ctx", across)
         send[-1] = pl.pallas_call(
             functools.partial(merge_kernel, count),
@@ -700,9 +704,14 @@
                 pairs = [(r - 1, r), (count - r, count - r - 1)]
                 got[g].append(lax.ppermute(send[g], "ctx", pairs))
 
-    normed, grads = [], None
+    teacher = write(targets)
+    student, grads = (), None
     for g in range(groups):
         more = [] if grads is None else [grads]
+        if g == groups - 1:
+            got[g][-1], teacher, *student = lax.optimization_barrier(
+                (got[g][-1], teacher, *student)
+            )
         made, grads = pl.pallas_call(
             functools.partial(final_kernel, count, g, groups, loss_scale),
             out_shape=(struct((rows, width), BF16), struct((groups + 1, width), F32)),
@@ -730,15 +739,15 @@
             *got[g],
             *more,
         )
-        normed.append(made)
-    teacher, student = write(*targets), write(*normed)
-    partner = exchange(grads, 1)
+        student = [write([made], g, student)]
+    student = student[0]
+    shifts = [1 << k for k in reversed(range(count.bit_length() - 1))]
+    partner = exchange(grads, shifts[0])
     if lax.axis_size("dp") == 2:
-        grads = (grads + partner) + (exchange(grads, count) + exchange(grads, count + 1))
+        grads = (grads + partner) + (exchange(grads, count) + exchange(grads, count + shifts[0]))
     else:
         grads = grads + partner
-    shifts = [1 << k for k in range(1, count.bit_length() - 1)]
-    for shift in shifts[:-1]:
+    for shift in shifts[1:-1]:
         grads = grads + exchange(grads, shift)
     grad_gain, grad_skip = pl.pallas_call(
         closing_kernel,

time: 63.2 us -> 61.7 us (0.976)
  starting transfers between devices: 21.3 us -> 20.2 us
  waiting for transfers between devices: 21.4 us -> 20.3 us
    ppermute x1, waiting for transfers between devices: 10.1 us -> 3.63 us  [body(): farther = lax.ppermute(beyond, 'ctx', outward)]
    ppermute x5, starting transfers between devices: 10.5 us -> 5.99 us  [body(): got[g].append(lax.ppermute(send[g], 'ctx', pairs))]
    ppermute x5, waiting for transfers between devices: 5.19 us -> 8.69 us  [body(): got[g].append(lax.ppermute(send[g], 'ctx', pairs))]
    ppermute x1, starting transfers between devices: 3.18 us -> 5.99 us  [body(): near = lax.ppermute(kv, 'ctx', inward + outward)]
    ppermute x4, waiting for transfers between devices: 3.26 us -> 4.85 us  [exchange(): return lax.ppermute(part, axes, [(d, d ^ shift) for d in range(size)])]
    pallas_call x2 -> x3, Pallas kernels: 1.97 us -> 2.61 us  [write(): pl.pallas_call(functools.partial(writing_kernel, len(pieces), first), out...]
  transfers between devices with their start and end apart: 14 -> 14, of which waited for: 9 -> 9; matrix products, arithmetic and copies ran while one was open for 0% -> 0% of each run, Pallas kernels for 22% -> 23%
where the time goes in v13:
time: 61.7 us; the launch traced here: 61.4 us
  waiting for transfers between devices  20.3 us (33%)
  starting transfers between devices  20.2 us (33%)
  Pallas kernels  19.9 us (32%)
  between operations  0.88 us (1%)
    ppermute x5, waiting for transfers between devices, body(): got[g].append(lax.ppermute(send[g], 'ctx', pairs))  8.69 us
    ppermute x1, starting transfers between devices, body(): near = lax.ppermute(kv, 'ctx', inward + outward)  5.99 us
    ppermute x5, starting transfers between devices, body(): got[g].append(lax.ppermute(send[g], 'ctx', pairs))  5.99 us
    pallas_call x2, Pallas kernels, body(): pl.pallas_call(functools.partial(attention_kernel, count, per_kv, stack,...  5.58 us
    ppermute x4, starting transfers between devices, exchange(): return lax.ppermute(part, axes, [(d, d ^ shift) for d in range(size)])  5.37 us
    ppermute x4, waiting for transfers between devices, exchange(): return lax.ppermute(part, axes, [(d, d ^ shift) for d in range(size)])  4.85 us
    pallas_call x1, Pallas kernels, body(): pl.pallas_call(functools.partial(local_kernel, count, groups), out_shape=...  4.2 us
    ppermute x1, waiting for transfers between devices, body(): farther = lax.ppermute(beyond, 'ctx', outward)  3.63 us
  transfers between devices with their start and end apart: 14, of which 9 were waited for; matrix products, arithmetic and copies ran while one was open for 0% of the time, Pallas kernels for 23%

profile of v13, /device:TPU:0, one launch (start us, length us, event | category | flops | bytes accessed | tf_op | source)
XLA Modules:
  0.0 61.4 jit_solution(2944505579867662683)
XLA Ops:
  0.6 3.2 %opening.1 = (bf16[256,512]{1,0:T(8,128)(2,1)S(1)}, f32[32,256]{1,0:T(8,128)S(1)}, bf16[256,1024]{1,0:T(8,128)(2,1)S(1)}, bf16[256,1024]{1,0:T(8,128)(2,1)S(1)},...) custom-call(s32[1,1024]{1,0:T(1,128)} %docs_ref.7, ...), custom_call_target="tpu_custom_call" | custom-call | flops 268435456 | bytes 4194304 | tf_op jit(solution)/shard_map/opening/pallas_call | solution.py:588
  3.9 0.7 %collective-permute-start = (bf16[256,512]{1,0:T(8,128)(2,1)S(1)}, bf16[256,512]{1,0:T(8,128)(2,1)S(1)}, u32[]{:S(2)}, u32[]{:S(2)}) collective-permute-start(bf16[256,512]{1,0:T(8,128)(2,1)S(1)} %get-tuple-element.41), channel_id=1, source_target_pairs={{4,8},{8,4},{5,9},{9,5},{6,10},{10,6},{7,11},{11,7},{20,24},{24,20... | collective-permute-start | bytes 786440 | tf_op jit(solution)/shard_map/ppermute | solution.py:644
  4.6 6.0 %collective-permute-start.3 = (bf16[256,512]{1,0:T(8,128)(2,1)S(1)}, bf16[256,512]{1,0:T(8,128)(2,1)S(1)}, u32[]{:S(2)}, u32[]{:S(2)}) collective-permute-start(bf16[256,512]{1,0:T(8,128)(2,1)S(1)} %get-tuple-element.41), channel_id=1, source_target_pairs={{0,4},{12,8},{4,0},{8,12},{1,5},{13,9},{5,1},{9,13},{2,6},{14,10},... | collective-permute-start | bytes 786440 | tf_op jit(solution)/shard_map/ppermute | solution.py:643
  10.6 1.9 %collective-permute-start.7 = (bf16[144,1024]{1,0:T(8,128)(2,1)S(1)}, bf16[144,1024]{1,0:T(8,128)(2,1)S(1)}, u32[]{:S(2)}, u32[]{:S(2)}) collective-permute-start(bf16[144,1024]{1,0:T(8,128)(2,1)S(1)} %get-tuple-element.62), channel_id=1, source_target_pairs={{0,4},{12,8},{1,5},{13,9},{2,6},{14,10},{3,7},{15,11},{16,20},{28,... | collective-permute-start | bytes 884744 | tf_op jit(solution)/shard_map/ppermute | solution.py:705
  12.5 4.2 %local.1 = (f32[256,1024]{1,0:T(8,128)S(1)}, f32[256,1024]{1,0:T(8,128)S(1)}, f32[256,1024]{1,0:T(8,128)S(1)}, f32[256,1024]{1,0:T(8,128)S(1)}, f32[256,1024]{1,0:T(8,128)S(1)}, /*index=5*/f32[256,1024]{1,0:T(8,128)S(1)}) custom-call(s32[1,1024]{1,0:T(1,128)} %docs_ref.7, bf16[256,2048]{1,0:T(8,128)(2,1)} %bitcast.32, bf16[256,2048]{1,0:T(8,128)(2,1)} %bitcast.34, ...), custom_call_target="tpu_custom_call" | custom-call | flops 134217728 | bytes 8388608 | tf_op jit(solution)/shard_map/local/pallas_call | solution.py:620
  16.7 0.0 collective-permute-done.kv_ref.refs_1_
  16.8 0.3 collective-permute-start.1
  17.0 0.3 collective-permute-done.3.refs_0_
  17.3 0.7 %collective-permute-start.4 = (bf16[256,512]{1,0:T(8,128)(2,1)S(1)}, bf16[256,512]{1,0:T(8,128)(2,1)S(1)}, u32[]{:S(2)}, u32[]{:S(2)}) collective-permute-start(bf16[256,512]{1,0:T(8,128)(2,1)S(1)} %collective-permute-done.3.refs_0_), channel_id=1, source_target_pairs={{4,8},{8,4},{5,9},{9,5},{6,10},{10,6},{7,11},{11,7},{20,24},{24,20... | collective-permute-start | bytes 786440 | tf_op jit(solution)/shard_map/ppermute | solution.py:646
  18.0 5.6 %collective-permute-done.7.got_ref.refs_0_ = bf16[144,1024]{1,0:T(8,128)(2,1)S(1)} collective-permute-done((bf16[144,1024]{1,0:T(8,128)(2,1)S(1)}, bf16[144,1024]{1,0:T(8,128)(2,1)S(1)}, u32[]{:S(2)}, u32[]{:S(2)}) %collective-permute-start.7) | collective-permute-done | bytes 294944 | tf_op jit(solution)/shard_map/ppermute | solution.py:705
  23.6 0.7 %collective-permute-start.8 = (bf16[144,1024]{1,0:T(8,128)(2,1)S(1)}, bf16[144,1024]{1,0:T(8,128)(2,1)S(1)}, u32[]{:S(2)}, u32[]{:S(2)}) collective-permute-start(bf16[144,1024]{1,0:T(8,128)(2,1)S(1)} %chain.6), channel_id=1, source_target_pairs={{4,8},{8,4},{5,9},{9,5},{6,10},{10,6},{7,11},{11,7},{20,24},{24,20... | collective-permute-start | bytes 884744 | tf_op jit(solution)/shard_map/ppermute | solution.py:705
  24.3 0.0 collective-permute-done.4.refs_2_
  24.3 1.3 %collective-permute-start.5 = (bf16[256,512]{1,0:T(8,128)(2,1)S(1)}, bf16[256,512]{1,0:T(8,128)(2,1)S(1)}, u32[]{:S(2)}, u32[]{:S(2)}) collective-permute-start(bf16[256,512]{1,0:T(8,128)(2,1)S(1)} %collective-permute-done.4.refs_2_), channel_id=1, source_target_pairs={{4,0},{8,12},{5,1},{9,13},{6,2},{10,14},{7,3},{11,15},{20,16},{24,... | collective-permute-start | bytes 786440 | tf_op jit(solution)/shard_map/ppermute | solution.py:658
  25.6 2.9 %collective-permute-done.1.got_ref.refs_3_.refs_0_ = bf16[144,1024]{1,0:T(8,128)(2,1)S(1)} collective-permute-done((bf16[144,1024]{1,0:T(8,128)(2,1)S(1)}, bf16[144,1024]{1,0:T(8,128)(2,1)S(1)}, u32[]{:S(2)}, u32[]{:S(2)}) %collective-permute-start.1) | collective-permute-done | bytes 294944 | tf_op jit(solution)/shard_map/ppermute | solution.py:656
  28.5 0.0 copy-start
  28.5 0.8 %collective-permute-start.2 = (bf16[144,1024]{1,0:T(8,128)(2,1)S(1)}, bf16[144,1024]{1,0:T(8,128)(2,1)S(1)}, u32[]{:S(2)}, u32[]{:S(2)}) collective-permute-start(bf16[144,1024]{1,0:T(8,128)(2,1)S(1)} %chain.4), channel_id=1, source_target_pairs={{4,8},{8,4},{5,9},{9,5},{6,10},{10,6},{7,11},{11,7},{20,24},{24,20... | collective-permute-start | bytes 884744 | tf_op jit(solution)/shard_map/ppermute | solution.py:705
  29.3 0.0 collective-permute-done.8.got_ref.refs_1_
  29.3 0.0 copy-start.4
  29.4 1.3 %collective-permute-start.9 = (bf16[144,1024]{1,0:T(8,128)(2,1)S(1)}, bf16[144,1024]{1,0:T(8,128)(2,1)S(1)}, u32[]{:S(2)}, u32[]{:S(2)}) collective-permute-start(bf16[144,1024]{1,0:T(8,128)(2,1)S(1)} %chain.7), channel_id=1, source_target_pairs={{8,12},{4,0},{9,13},{5,1},{10,14},{6,2},{11,15},{7,3},{24,28},{20,... | collective-permute-start | bytes 884744 | tf_op jit(solution)/shard_map/ppermute | solution.py:705
  30.7 3.6 %collective-permute-done.5.refs_4_ = bf16[256,512]{1,0:T(8,128)(2,1)S(1)} collective-permute-done((bf16[256,512]{1,0:T(8,128)(2,1)S(1)}, bf16[256,512]{1,0:T(8,128)(2,1)S(1)}, u32[]{:S(2)}, u32[]{:S(2)}) %collective-permute-start.5) | collective-permute-done | bytes 262176 | tf_op jit(solution)/shard_map/ppermute | solution.py:658
  34.3 0.0 copy-done
  34.3 0.0 copy-done.1
  34.3 0.0 copy-done.2
  34.3 0.0 copy-done.4
  34.3 2.8 %attention.2.refs_0_.teacher_ref = bf16[256,1024]{1,0:T(8,128)(2,1)S(1)} custom-call(s32[1,1024]{1,0:T(1,128)S(1)} %copy-done.4, bf16[256,2048]{1,0:T(8,128)(2,1)S(1)} %bitcast.18, bf16[256,256]{1,0:T(8,128)(2,1)S(1)} %bitcast.21, bf16[256,256]{1,0:T(8,128)(2,1)S(1)} %bitcast.24, bf16[256,512]{1,0:T(8,128)(2,1)S(1)} %collective-permute-done.3.refs_0_, ...), custom_call_target="tpu_custom_call" | custom-call | flops 603979776 | bytes 2097152 | tf_op jit(solution)/shard_map/attention/pallas_call | solution.py:669
  37.1 0.0 collective-permute-done.2.got_ref.refs_1_
  37.1 1.3 %collective-permute-start.6 = (bf16[144,1024]{1,0:T(8,128)(2,1)S(1)}, bf16[144,1024]{1,0:T(8,128)(2,1)S(1)}, u32[]{:S(2)}, u32[]{:S(2)}) collective-permute-start(bf16[144,1024]{1,0:T(8,128)(2,1)S(1)} %chain.5), channel_id=1, source_target_pairs={{8,12},{4,0},{9,13},{5,1},{10,14},{6,2},{11,15},{7,3},{24,28},{20,... | collective-permute-start | bytes 884744 | tf_op jit(solution)/shard_map/ppermute | solution.py:705
  38.4 2.8 %attention.3.refs_1_.teacher_ref = bf16[256,1024]{1,0:T(8,128)(2,1)S(1)} custom-call(s32[1,1024]{1,0:T(1,128)S(1)} %copy-done.4, bf16[256,2048]{1,0:T(8,128)(2,1)S(1)} %bitcast.19, bf16[256,256]{1,0:T(8,128)(2,1)S(1)} %bitcast.22, bf16[256,256]{1,0:T(8,128)(2,1)S(1)} %bitcast.25, bf16[256,512]{1,0:T(8,128)(2,1)S(1)} %collective-permute-done.3.refs_0_, ...), custom_call_target="tpu_custom_call" | custom-call | flops 603979776 | bytes 2097152 | tf_op jit(solution)/shard_map/attention/pallas_call | solution.py:669
  41.2 0.0 copy-start.3
  41.2 0.0 copy-start.5
  41.3 1.0 %writing.3 = bf16[256,2048]{1,0:T(8,128)(2,1)} custom-call(bf16[256,1024]{1,0:T(8,128)(2,1)S(1)} %attention.2.refs_0_.teacher_ref, bf16[256,1024]{1,0:T(8,128)(2,1)S(1)} %attention.3.refs_1_.teacher_ref), custom_call_target="tpu_custom_call" | custom-call | bytes 2097152 | tf_op jit(solution)/shard_map/writing/pallas_call | solution.py:574
  42.3 0.0 collective-permute-done.9.refs_2_
  42.3 0.0 copy-done.3
  42.3 0.0 copy-done.5
  42.3 1.8 %final.2 = (bf16[256,1024]{1,0:T(8,128)(2,1)S(1)}, f32[3,1024]{1,0:T(4,128)S(1)}) custom-call(f32[256,1024]{1,0:T(8,128)S(1)} %get-tuple-element.57.pre_ref, f32[256,1024]{1,0:T(8,128)S(1)} %get-tuple-element.58.reach_ref, f32[256,1024]{1,0:T(8,128)S(1)} %get-tuple-element.59.sx_ref, bf16[256,256]{1,0:T(8,128)(2,1)S(1)} %bitcast.27, ...), custom_call_target="tpu_custom_call" | custom-call | flops 67108864 | bytes 5242880 | tf_op jit(solution)/shard_map/final/pallas_call | solution.py:715
  44.1 0.8 %writing.4.refs_1_ = bf16[256,2048]{1,0:T(8,128)(2,1)} custom-call(bf16[256,1024]{1,0:T(8,128)(2,1)S(1)} %get-tuple-element.64.refs_0_), custom_call_target="tpu_custom_call" | custom-call | bytes 2097152 | tf_op jit(solution)/shard_map/writing/pallas_call | solution.py:574
  44.9 3.0 %collective-permute-done.6.refs_2_ = bf16[144,1024]{1,0:T(8,128)(2,1)S(1)} collective-permute-done((bf16[144,1024]{1,0:T(8,128)(2,1)S(1)}, bf16[144,1024]{1,0:T(8,128)(2,1)S(1)}, u32[]{:S(2)}, u32[]{:S(2)}) %collective-permute-start.6) | collective-permute-done | bytes 294944 | tf_op jit(solution)/shard_map/ppermute | solution.py:705
  48.0 1.8 %final.3 = (bf16[256,1024]{1,0:T(8,128)(2,1)S(1)}, f32[3,1024]{1,0:T(4,128)S(1)}) custom-call(f32[256,1024]{1,0:T(8,128)S(1)} %get-tuple-element.66.pre_ref, f32[256,1024]{1,0:T(8,128)S(1)} %get-tuple-element.67.reach_ref, f32[256,1024]{1,0:T(8,128)S(1)} %get-tuple-element.68.sx_ref, bf16[256,256]{1,0:T(8,128)(2,1)S(1)} %bitcast.28, ...), custom_call_target="tpu_custom_call" | custom-call | flops 67108864 | bytes 5242880 | tf_op jit(solution)/shard_map/final/pallas_call | solution.py:715
  49.7 2.1 %collective-permute-start.12 = (f32[3,1024]{1,0:T(4,128)S(1)}, f32[3,1024]{1,0:T(4,128)S(1)}, u32[]{:S(2)}, u32[]{:S(2)}) collective-permute-start(f32[3,1024]{1,0:T(4,128)S(1)} %get-tuple-element.73), channel_id=1, source_target_pairs={{0,24},{4,28},{8,16},{12,20},{16,8},{20,12},{24,0},{28,4},{1,25},{... | collective-permute-start | bytes 36872 | tf_op jit(solution)/shard_map/ppermute | solution.py:537
  51.8 0.5 collective-permute-start.11
  52.3 1.9 %collective-permute-start.10 = (f32[3,1024]{1,0:T(4,128)S(1)}, f32[3,1024]{1,0:T(4,128)S(1)}, u32[]{:S(2)}, u32[]{:S(2)}) collective-permute-start(f32[3,1024]{1,0:T(4,128)S(1)} %get-tuple-element.73), channel_id=1, source_target_pairs={{0,8},{4,12},{8,0},{12,4},{16,24},{20,28},{24,16},{28,20},{1,9},{5... | collective-permute-start | bytes 36872 | tf_op jit(solution)/shard_map/ppermute | solution.py:537
  54.2 1.1 %collective-permute-done.12 = f32[3,1024]{1,0:T(4,128)S(1)} collective-permute-done((f32[3,1024]{1,0:T(4,128)S(1)}, f32[3,1024]{1,0:T(4,128)S(1)}, u32[]{:S(2)}, u32[]{:S(2)}) %collective-permute-start.12) | collective-permute-done | bytes 12320 | tf_op jit(solution)/shard_map/ppermute | solution.py:537
  55.3 0.2 collective-permute-done.11
  55.5 1.4 %collective-permute-done.10 = f32[3,1024]{1,0:T(4,128)S(1)} collective-permute-done((f32[3,1024]{1,0:T(4,128)S(1)}, f32[3,1024]{1,0:T(4,128)S(1)}, u32[]{:S(2)}, u32[]{:S(2)}) %collective-permute-start.10) | collective-permute-done | bytes 12320 | tf_op jit(solution)/shard_map/ppermute | solution.py:537
  57.0 0.9 %collective-permute-start.13 = (f32[3,1024]{1,0:T(4,128)S(1)}, f32[3,1024]{1,0:T(4,128)S(1)}, u32[]{:S(2)}, u32[]{:S(2)}) collective-permute-start(f32[3,1024]{1,0:T(4,128)S(1)} %add_add_fusion.a_ref), channel_id=1, source_target_pairs={{0,4},{4,0},{8,12},{12,8},{16,20},{20,16},{24,28},{28,24},{1,5},{5... | collective-permute-start | bytes 36872 | tf_op jit(solution)/shard_map/ppermute | solution.py:537
  57.9 0.8 %writing.5 = bf16[256,2048]{1,0:T(8,128)(2,1)} custom-call(bf16[256,1024]{1,0:T(8,128)(2,1)S(1)} %get-tuple-element.71.refs_0_, bf16[256,2048]{1,0:T(8,128)(2,1)} %writing.4.refs_1_), custom_call_target="tpu_custom_call", output_to_operand_aliasing={{}: (1, {})} | custom-call | bytes 2097152 | tf_op jit(solution)/shard_map/writing/pallas_call | solution.py:574
  58.7 2.1 %collective-permute-done.13.b_ref = f32[3,1024]{1,0:T(4,128)S(1)} collective-permute-done((f32[3,1024]{1,0:T(4,128)S(1)}, f32[3,1024]{1,0:T(4,128)S(1)}, u32[]{:S(2)}, u32[]{:S(2)}) %collective-permute-start.13) | collective-permute-done | bytes 12320 | tf_op jit(solution)/shard_map/ppermute | solution.py:537
  60.8 0.6 closing.1
  (8 shorter events, 0.1 us)
Async XLA Ops:
  3.9 12.8 %collective-permute-start = (bf16[256,512]{1,0:T(8,128)(2,1)S(1)}, bf16[256,512]{1,0:T(8,128)(2,1)S(1)}, u32[]{:S(2)}, u32[]{:S(2)}) collective-permute-start(bf16[256,512]{1,0:T(8,128)(2,1)S(1)} %get-tuple-element.41), channel_id=1, source_target_pairs={{4,8},{8,4},{5,9},{9,5},{6,10},{10,6},{7,11},{11,7},{20,24},{24,20... | collective-permute-start | bytes 786440 | tf_op jit(solution)/shard_map/ppermute | solution.py:644
  4.6 12.7 %collective-permute-start.3 = (bf16[256,512]{1,0:T(8,128)(2,1)S(1)}, bf16[256,512]{1,0:T(8,128)(2,1)S(1)}, u32[]{:S(2)}, u32[]{:S(2)}) collective-permute-start(bf16[256,512]{1,0:T(8,128)(2,1)S(1)} %get-tuple-element.41), channel_id=1, source_target_pairs={{0,4},{12,8},{4,0},{8,12},{1,5},{13,9},{5,1},{9,13},{2,6},{14,10},... | collective-permute-start | bytes 786440 | tf_op jit(solution)/shard_map/ppermute | solution.py:643
  10.6 13.1 %collective-permute-start.7 = (bf16[144,1024]{1,0:T(8,128)(2,1)S(1)}, bf16[144,1024]{1,0:T(8,128)(2,1)S(1)}, u32[]{:S(2)}, u32[]{:S(2)}) collective-permute-start(bf16[144,1024]{1,0:T(8,128)(2,1)S(1)} %get-tuple-element.62), channel_id=1, source_target_pairs={{0,4},{12,8},{1,5},{13,9},{2,6},{14,10},{3,7},{15,11},{16,20},{28,... | collective-permute-start | bytes 884744 | tf_op jit(solution)/shard_map/ppermute | solution.py:705
  16.8 11.7 %collective-permute-start.1 = (bf16[144,1024]{1,0:T(8,128)(2,1)S(1)}, bf16[144,1024]{1,0:T(8,128)(2,1)S(1)}, u32[]{:S(2)}, u32[]{:S(2)}) collective-permute-start(bf16[144,1024]{1,0:T(8,128)(2,1)S(1)} %merge.1), channel_id=1, source_target_pairs={{0,4},{12,8},{4,0},{8,12},{1,5},{13,9},{5,1},{9,13},{2,6},{14,10},... | collective-permute-start | bytes 884744 | tf_op jit(solution)/shard_map/ppermute | solution.py:656
  17.3 7.0 %collective-permute-start.4 = (bf16[256,512]{1,0:T(8,128)(2,1)S(1)}, bf16[256,512]{1,0:T(8,128)(2,1)S(1)}, u32[]{:S(2)}, u32[]{:S(2)}) collective-permute-start(bf16[256,512]{1,0:T(8,128)(2,1)S(1)} %collective-permute-done.3.refs_0_), channel_id=1, source_target_pairs={{4,8},{8,4},{5,9},{9,5},{6,10},{10,6},{7,11},{11,7},{20,24},{24,20... | collective-permute-start | bytes 786440 | tf_op jit(solution)/shard_map/ppermute | solution.py:646
  23.6 5.7 %collective-permute-start.8 = (bf16[144,1024]{1,0:T(8,128)(2,1)S(1)}, bf16[144,1024]{1,0:T(8,128)(2,1)S(1)}, u32[]{:S(2)}, u32[]{:S(2)}) collective-permute-start(bf16[144,1024]{1,0:T(8,128)(2,1)S(1)} %chain.6), channel_id=1, source_target_pairs={{4,8},{8,4},{5,9},{9,5},{6,10},{10,6},{7,11},{11,7},{20,24},{24,20... | collective-permute-start | bytes 884744 | tf_op jit(solution)/shard_map/ppermute | solution.py:705
  24.3 10.0 %collective-permute-start.5 = (bf16[256,512]{1,0:T(8,128)(2,1)S(1)}, bf16[256,512]{1,0:T(8,128)(2,1)S(1)}, u32[]{:S(2)}, u32[]{:S(2)}) collective-permute-start(bf16[256,512]{1,0:T(8,128)(2,1)S(1)} %collective-permute-done.4.refs_2_), channel_id=1, source_target_pairs={{4,0},{8,12},{5,1},{9,13},{6,2},{10,14},{7,3},{11,15},{20,16},{24,... | collective-permute-start | bytes 786440 | tf_op jit(solution)/shard_map/ppermute | solution.py:658
  28.5 5.8 %copy-start = (bf16[1,256,2048]{2,1,0:T(8,128)(2,1)S(1)}, bf16[1,256,2048]{2,1,0:T(8,128)(2,1)}, u32[]{:S(2)}) copy-start(bf16[1,256,2048]{2,1,0:T(8,128)(2,1)} %param.13) | copy-start | bytes 3145732
  28.5 5.8 %copy-start.1 = (bf16[1,256,256]{2,1,0:T(8,128)(2,1)S(1)}, bf16[1,256,256]{2,1,0:T(8,128)(2,1)}, u32[]{:S(2)}) copy-start(bf16[1,256,256]{2,1,0:T(8,128)(2,1)} %param.14) | copy-start | bytes 393220
  28.5 5.8 %copy-start.2 = (bf16[1,256,256]{2,1,0:T(8,128)(2,1)S(1)}, bf16[1,256,256]{2,1,0:T(8,128)(2,1)}, u32[]{:S(2)}) copy-start(bf16[1,256,256]{2,1,0:T(8,128)(2,1)} %param.15) | copy-start | bytes 393220
  28.5 8.6 %collective-permute-start.2 = (bf16[144,1024]{1,0:T(8,128)(2,1)S(1)}, bf16[144,1024]{1,0:T(8,128)(2,1)S(1)}, u32[]{:S(2)}, u32[]{:S(2)}) collective-permute-start(bf16[144,1024]{1,0:T(8,128)(2,1)S(1)} %chain.4), channel_id=1, source_target_pairs={{4,8},{8,4},{5,9},{9,5},{6,10},{10,6},{7,11},{11,7},{20,24},{24,20... | collective-permute-start | bytes 884744 | tf_op jit(solution)/shard_map/ppermute | solution.py:705
  29.3 5.0 %copy-start.4 = (s32[1,1024]{1,0:T(1,128)S(1)}, s32[1,1024]{1,0:T(1,128)}, u32[]{:S(2)}) copy-start(s32[1,1024]{1,0:T(1,128)} %docs_ref.7) | copy-start | bytes 12292
  29.4 12.9 %collective-permute-start.9 = (bf16[144,1024]{1,0:T(8,128)(2,1)S(1)}, bf16[144,1024]{1,0:T(8,128)(2,1)S(1)}, u32[]{:S(2)}, u32[]{:S(2)}) collective-permute-start(bf16[144,1024]{1,0:T(8,128)(2,1)S(1)} %chain.7), channel_id=1, source_target_pairs={{8,12},{4,0},{9,13},{5,1},{10,14},{6,2},{11,15},{7,3},{24,28},{20,... | collective-permute-start | bytes 884744 | tf_op jit(solution)/shard_map/ppermute | solution.py:705
  37.1 10.8 %collective-permute-start.6 = (bf16[144,1024]{1,0:T(8,128)(2,1)S(1)}, bf16[144,1024]{1,0:T(8,128)(2,1)S(1)}, u32[]{:S(2)}, u32[]{:S(2)}) collective-permute-start(bf16[144,1024]{1,0:T(8,128)(2,1)S(1)} %chain.5), channel_id=1, source_target_pairs={{8,12},{4,0},{9,13},{5,1},{10,14},{6,2},{11,15},{7,3},{24,28},{20,... | collective-permute-start | bytes 884744 | tf_op jit(solution)/shard_map/ppermute | solution.py:705
  41.2 1.0 %copy-start.3 = (bf16[1,256,256]{2,1,0:T(8,128)(2,1)S(1)}, bf16[1,256,256]{2,1,0:T(8,128)(2,1)}, u32[]{:S(2)}) copy-start(bf16[1,256,256]{2,1,0:T(8,128)(2,1)} %param.20) | copy-start | bytes 393220
  41.2 1.0 %copy-start.5 = (f32[2048]{0:T(1024)S(1)}, f32[2048]{0:T(1024)}, u32[]{:S(2)}) copy-start(f32[2048]{0:T(1024)} %param.25) | copy-start | bytes 24580
  49.7 5.6 %collective-permute-start.12 = (f32[3,1024]{1,0:T(4,128)S(1)}, f32[3,1024]{1,0:T(4,128)S(1)}, u32[]{:S(2)}, u32[]{:S(2)}) collective-permute-start(f32[3,1024]{1,0:T(4,128)S(1)} %get-tuple-element.73), channel_id=1, source_target_pairs={{0,24},{4,28},{8,16},{12,20},{16,8},{20,12},{24,0},{28,4},{1,25},{... | collective-permute-start | bytes 36872 | tf_op jit(solution)/shard_map/ppermute | solution.py:537
  51.8 3.7 %collective-permute-start.11 = (f32[3,1024]{1,0:T(4,128)S(1)}, f32[3,1024]{1,0:T(4,128)S(1)}, u32[]{:S(2)}, u32[]{:S(2)}) collective-permute-start(f32[3,1024]{1,0:T(4,128)S(1)} %get-tuple-element.73), channel_id=1, source_target_pairs={{0,16},{4,20},{8,24},{12,28},{16,0},{20,4},{24,8},{28,12},{1,17},{... | collective-permute-start | bytes 36872 | tf_op jit(solution)/shard_map/ppermute | solution.py:537
  52.3 4.6 %collective-permute-start.10 = (f32[3,1024]{1,0:T(4,128)S(1)}, f32[3,1024]{1,0:T(4,128)S(1)}, u32[]{:S(2)}, u32[]{:S(2)}) collective-permute-start(f32[3,1024]{1,0:T(4,128)S(1)} %get-tuple-element.73), channel_id=1, source_target_pairs={{0,8},{4,12},{8,0},{12,4},{16,24},{20,28},{24,16},{28,20},{1,9},{5... | collective-permute-start | bytes 36872 | tf_op jit(solution)/shard_map/ppermute | solution.py:537
  57.0 3.8 %collective-permute-start.13 = (f32[3,1024]{1,0:T(4,128)S(1)}, f32[3,1024]{1,0:T(4,128)S(1)}, u32[]{:S(2)}, u32[]{:S(2)}) collective-permute-start(f32[3,1024]{1,0:T(4,128)S(1)} %add_add_fusion.a_ref), channel_id=1, source_target_pairs={{0,4},{4,0},{8,12},{12,8},{16,20},{20,16},{24,28},{28,24},{1,5},{5... | collective-permute-start | bytes 36872 | tf_op jit(solution)/shard_map/ppermute | solution.py:537

commit v14 on v10

--- a/solution.py
+++ b/solution.py
@@ -567,7 +567,7 @@
     def in_hbm(*arrays):
         return [pltpu.with_memory_space_constraint(array, pltpu.HBM) for array in arrays]
 
-    def write(*pieces):
+    def write(pieces):
         return pl.pallas_call(
             writing_kernel,
             out_shape=struct((rows, features), BF16),
@@ -638,7 +638,7 @@
         inward, outward, across = [(0, 1), (3, 2)], [(1, 0), (2, 3)], [(1, 2), (2, 1)]
         near = lax.ppermute(kv, "ctx", inward + outward)
         middle = lax.ppermute(kv, "ctx", across)
-        middle, near, *local = lax.optimization_barrier((middle, near, *local))
+        middle, *local = lax.optimization_barrier((middle, *local))
         beyond = lax.ppermute(near, "ctx", across)
         send[-1] = pl.pallas_call(
             functools.partial(merge_kernel, count),
@@ -731,14 +731,17 @@
             *more,
         )
         normed.append(made)
-    teacher, student = write(*targets), write(*normed)
-    partner = exchange(grads, 1)
+    shifts = [1 << k for k in reversed(range(count.bit_length() - 1))]
+    partner = exchange(grads, shifts[0])
+    *targets, _ = lax.optimization_barrier((*targets, grads))
+    teacher = write(targets)
+    partner, teacher = lax.optimization_barrier((partner, teacher))
+    student = write(normed)
     if lax.axis_size("dp") == 2:
-        grads = (grads + partner) + (exchange(grads, count) + exchange(grads, count + 1))
+        grads = (grads + partner) + (exchange(grads, count) + exchange(grads, count + shifts[0]))
     else:
         grads = grads + partner
-    shifts = [1 << k for k in range(1, count.bit_length() - 1)]
-    for shift in shifts[:-1]:
+    for shift in shifts[1:-1]:
         grads = grads + exchange(grads, shift)
     grad_gain, grad_skip = pl.pallas_call(
         closing_kernel,

time: 63.2 us -> 61.9 us (0.979)
  waiting for transfers between devices: 21.4 us -> 20.1 us
    ppermute x1, waiting for transfers between devices: 10.1 us -> 3.63 us  [body(): farther = lax.ppermute(beyond, 'ctx', outward)]
    ppermute x5, waiting for transfers between devices: 5.19 us -> 10.5 us  [body(): got[g].append(lax.ppermute(send[g], 'ctx', pairs))]
    ppermute x5, starting transfers between devices: 10.5 us -> 6.12 us  [body(): got[g].append(lax.ppermute(send[g], 'ctx', pairs))]
    ppermute x1, starting transfers between devices: 3.18 us -> 5.99 us  [body(): near = lax.ppermute(kv, 'ctx', inward + outward)]
    ppermute x4, starting transfers between devices: 4.87 us -> 6.27 us  [exchange(): return lax.ppermute(part, axes, [(d, d ^ shift) for d in range(size)])]
  transfers between devices with their start and end apart: 14 -> 14, of which waited for: 9 -> 7; matrix products, arithmetic and copies ran while one was open for 0% -> 0% of each run, Pallas kernels for 22% -> 22%
where the time goes in v14:
time: 61.9 us; the launch traced here: 61.5 us
  starting transfers between devices  21.3 us (34%)
  waiting for transfers between devices  20.1 us (32%)
  Pallas kernels  19.3 us (31%)
  between operations  0.89 us (1%)
    ppermute x5, waiting for transfers between devices, body(): got[g].append(lax.ppermute(send[g], 'ctx', pairs))  10.5 us
    ppermute x4, starting transfers between devices, exchange(): return lax.ppermute(part, axes, [(d, d ^ shift) for d in range(size)])  6.27 us
    ppermute x5, starting transfers between devices, body(): got[g].append(lax.ppermute(send[g], 'ctx', pairs))  6.12 us
    ppermute x1, starting transfers between devices, body(): near = lax.ppermute(kv, 'ctx', inward + outward)  5.99 us
    pallas_call x2, Pallas kernels, body(): pl.pallas_call(functools.partial(attention_kernel, count, per_kv, stack,...  5.58 us
    pallas_call x1, Pallas kernels, body(): pl.pallas_call(functools.partial(local_kernel, count, groups), out_shape=...  4.2 us
    ppermute x1, waiting for transfers between devices, body(): farther = lax.ppermute(beyond, 'ctx', outward)  3.63 us
    pallas_call x2, Pallas kernels, body(): pl.pallas_call(functools.partial(final_kernel, count, g, groups, loss_sca...  3.59 us
  transfers between devices with their start and end apart: 14, of which 7 were waited for; matrix products, arithmetic and copies ran while one was open for 0% of the time, Pallas kernels for 22%

profile of v14, /device:TPU:0, one launch (start us, length us, event | category | flops | bytes accessed | tf_op | source)
XLA Modules:
  0.0 61.5 jit_solution(3599074049239647673)
XLA Ops:
  0.6 3.2 %opening.1 = (bf16[256,512]{1,0:T(8,128)(2,1)S(1)}, f32[32,256]{1,0:T(8,128)S(1)}, bf16[256,1024]{1,0:T(8,128)(2,1)S(1)}, bf16[256,1024]{1,0:T(8,128)(2,1)S(1)},...) custom-call(s32[1,1024]{1,0:T(1,128)} %docs_ref.7, ...), custom_call_target="tpu_custom_call" | custom-call | flops 268435456 | bytes 4194304 | tf_op jit(solution)/shard_map/opening/pallas_call | solution.py:584
  3.9 0.7 %collective-permute-start = (bf16[256,512]{1,0:T(8,128)(2,1)S(1)}, bf16[256,512]{1,0:T(8,128)(2,1)S(1)}, u32[]{:S(2)}, u32[]{:S(2)}) collective-permute-start(bf16[256,512]{1,0:T(8,128)(2,1)S(1)} %get-tuple-element.41), channel_id=1, source_target_pairs={{4,8},{8,4},{5,9},{9,5},{6,10},{10,6},{7,11},{11,7},{20,24},{24,20... | collective-permute-start | bytes 786440 | tf_op jit(solution)/shard_map/ppermute | solution.py:640
  4.6 6.0 %collective-permute-start.1 = (bf16[256,512]{1,0:T(8,128)(2,1)S(1)}, bf16[256,512]{1,0:T(8,128)(2,1)S(1)}, u32[]{:S(2)}, u32[]{:S(2)}) collective-permute-start(bf16[256,512]{1,0:T(8,128)(2,1)S(1)} %get-tuple-element.41), channel_id=1, source_target_pairs={{0,4},{12,8},{4,0},{8,12},{1,5},{13,9},{5,1},{9,13},{2,6},{14,10},... | collective-permute-start | bytes 786440 | tf_op jit(solution)/shard_map/ppermute | solution.py:639
  10.6 1.9 %collective-permute-start.7 = (bf16[144,1024]{1,0:T(8,128)(2,1)S(1)}, bf16[144,1024]{1,0:T(8,128)(2,1)S(1)}, u32[]{:S(2)}, u32[]{:S(2)}) collective-permute-start(bf16[144,1024]{1,0:T(8,128)(2,1)S(1)} %get-tuple-element.66), channel_id=1, source_target_pairs={{0,4},{12,8},{1,5},{13,9},{2,6},{14,10},{3,7},{15,11},{16,20},{28,... | collective-permute-start | bytes 884744 | tf_op jit(solution)/shard_map/ppermute | solution.py:701
  12.5 4.2 %local.1 = (f32[256,1024]{1,0:T(8,128)S(1)}, f32[256,1024]{1,0:T(8,128)S(1)}, f32[256,1024]{1,0:T(8,128)S(1)}, f32[256,1024]{1,0:T(8,128)S(1)}, f32[256,1024]{1,0:T(8,128)S(1)}, /*index=5*/f32[256,1024]{1,0:T(8,128)S(1)}) custom-call(s32[1,1024]{1,0:T(1,128)} %docs_ref.7, bf16[256,2048]{1,0:T(8,128)(2,1)} %bitcast.32, bf16[256,2048]{1,0:T(8,128)(2,1)} %bitcast.33, ...), custom_call_target="tpu_custom_call" | custom-call | flops 134217728 | bytes 8388608 | tf_op jit(solution)/shard_map/local/pallas_call | solution.py:616
  16.7 0.0 collective-permute-done.kv_ref.refs_1_
  16.8 0.3 collective-permute-start.3
  17.0 0.3 collective-permute-done.1.refs_0_
  17.3 0.7 %collective-permute-start.2 = (bf16[256,512]{1,0:T(8,128)(2,1)S(1)}, bf16[256,512]{1,0:T(8,128)(2,1)S(1)}, u32[]{:S(2)}, u32[]{:S(2)}) collective-permute-start(bf16[256,512]{1,0:T(8,128)(2,1)S(1)} %collective-permute-done.1.refs_0_), channel_id=1, source_target_pairs={{4,8},{8,4},{5,9},{9,5},{6,10},{10,6},{7,11},{11,7},{20,24},{24,20... | collective-permute-start | bytes 786440 | tf_op jit(solution)/shard_map/ppermute | solution.py:642
  18.0 5.6 %collective-permute-done.7.got_ref.refs_0_ = bf16[144,1024]{1,0:T(8,128)(2,1)S(1)} collective-permute-done((bf16[144,1024]{1,0:T(8,128)(2,1)S(1)}, bf16[144,1024]{1,0:T(8,128)(2,1)S(1)}, u32[]{:S(2)}, u32[]{:S(2)}) %collective-permute-start.7) | collective-permute-done | bytes 294944 | tf_op jit(solution)/shard_map/ppermute | solution.py:701
  23.6 0.7 %collective-permute-start.8 = (bf16[144,1024]{1,0:T(8,128)(2,1)S(1)}, bf16[144,1024]{1,0:T(8,128)(2,1)S(1)}, u32[]{:S(2)}, u32[]{:S(2)}) collective-permute-start(bf16[144,1024]{1,0:T(8,128)(2,1)S(1)} %chain.6), channel_id=1, source_target_pairs={{4,8},{8,4},{5,9},{9,5},{6,10},{10,6},{7,11},{11,7},{20,24},{24,20... | collective-permute-start | bytes 884744 | tf_op jit(solution)/shard_map/ppermute | solution.py:701
  24.3 0.0 collective-permute-done.2.refs_2_
  24.3 1.3 %collective-permute-start.4 = (bf16[256,512]{1,0:T(8,128)(2,1)S(1)}, bf16[256,512]{1,0:T(8,128)(2,1)S(1)}, u32[]{:S(2)}, u32[]{:S(2)}) collective-permute-start(bf16[256,512]{1,0:T(8,128)(2,1)S(1)} %collective-permute-done.2.refs_2_), channel_id=1, source_target_pairs={{4,0},{8,12},{5,1},{9,13},{6,2},{10,14},{7,3},{11,15},{20,16},{24,... | collective-permute-start | bytes 786440 | tf_op jit(solution)/shard_map/ppermute | solution.py:654
  25.6 2.9 %collective-permute-done.3.refs_3_.got_ref.refs_0_ = bf16[144,1024]{1,0:T(8,128)(2,1)S(1)} collective-permute-done((bf16[144,1024]{1,0:T(8,128)(2,1)S(1)}, bf16[144,1024]{1,0:T(8,128)(2,1)S(1)}, u32[]{:S(2)}, u32[]{:S(2)}) %collective-permute-start.3) | collective-permute-done | bytes 294944 | tf_op jit(solution)/shard_map/ppermute | solution.py:652
  28.5 0.0 copy-start
  28.5 0.0 copy-start.1
  28.5 0.8 %collective-permute-start.5 = (bf16[144,1024]{1,0:T(8,128)(2,1)S(1)}, bf16[144,1024]{1,0:T(8,128)(2,1)S(1)}, u32[]{:S(2)}, u32[]{:S(2)}) collective-permute-start(bf16[144,1024]{1,0:T(8,128)(2,1)S(1)} %chain.4), channel_id=1, source_target_pairs={{4,8},{8,4},{5,9},{9,5},{6,10},{10,6},{7,11},{11,7},{20,24},{24,20... | collective-permute-start | bytes 884744 | tf_op jit(solution)/shard_map/ppermute | solution.py:701
  29.3 0.0 collective-permute-done.8.got_ref.refs_1_
  29.3 0.0 copy-start.4
  29.4 1.3 %collective-permute-start.9 = (bf16[144,1024]{1,0:T(8,128)(2,1)S(1)}, bf16[144,1024]{1,0:T(8,128)(2,1)S(1)}, u32[]{:S(2)}, u32[]{:S(2)}) collective-permute-start(bf16[144,1024]{1,0:T(8,128)(2,1)S(1)} %chain.7), channel_id=1, source_target_pairs={{8,12},{4,0},{9,13},{5,1},{10,14},{6,2},{11,15},{7,3},{24,28},{20,... | collective-permute-start | bytes 884744 | tf_op jit(solution)/shard_map/ppermute | solution.py:701
  30.7 3.6 %collective-permute-done.4.refs_4_ = bf16[256,512]{1,0:T(8,128)(2,1)S(1)} collective-permute-done((bf16[256,512]{1,0:T(8,128)(2,1)S(1)}, bf16[256,512]{1,0:T(8,128)(2,1)S(1)}, u32[]{:S(2)}, u32[]{:S(2)}) %collective-permute-start.4) | collective-permute-done | bytes 262176 | tf_op jit(solution)/shard_map/ppermute | solution.py:654
  34.3 0.0 copy-done
  34.3 0.0 copy-done.1
  34.3 0.0 copy-done.2
  34.3 0.0 copy-done.4
  34.3 2.8 %attention.3.teacher_ref.refs_0_ = bf16[256,1024]{1,0:T(8,128)(2,1)S(1)} custom-call(s32[1,1024]{1,0:T(1,128)S(1)} %copy-done.4, bf16[256,2048]{1,0:T(8,128)(2,1)S(1)} %bitcast.18, bf16[256,256]{1,0:T(8,128)(2,1)S(1)} %bitcast.21, bf16[256,256]{1,0:T(8,128)(2,1)S(1)} %bitcast.24, bf16[256,512]{1,0:T(8,128)(2,1)S(1)} %collective-permute-done.1.refs_0_, ...), custom_call_target="tpu_custom_call" | custom-call | flops 603979776 | bytes 2097152 | tf_op jit(solution)/shard_map/attention/pallas_call | solution.py:665
  37.1 0.0 collective-permute-done.5.got_ref.refs_1_
  37.1 0.0 copy-start.3
  37.2 0.0 copy-start.5
  37.2 1.4 %collective-permute-start.6 = (bf16[144,1024]{1,0:T(8,128)(2,1)S(1)}, bf16[144,1024]{1,0:T(8,128)(2,1)S(1)}, u32[]{:S(2)}, u32[]{:S(2)}) collective-permute-start(bf16[144,1024]{1,0:T(8,128)(2,1)S(1)} %chain.5), channel_id=1, source_target_pairs={{8,12},{4,0},{9,13},{5,1},{10,14},{6,2},{11,15},{7,3},{24,28},{20,... | collective-permute-start | bytes 884744 | tf_op jit(solution)/shard_map/ppermute | solution.py:701
  38.6 2.8 %attention.2.teacher_ref.refs_1_ = bf16[256,1024]{1,0:T(8,128)(2,1)S(1)} custom-call(s32[1,1024]{1,0:T(1,128)S(1)} %copy-done.4, bf16[256,2048]{1,0:T(8,128)(2,1)S(1)} %bitcast.19, bf16[256,256]{1,0:T(8,128)(2,1)S(1)} %bitcast.22, bf16[256,256]{1,0:T(8,128)(2,1)S(1)} %bitcast.25, bf16[256,512]{1,0:T(8,128)(2,1)S(1)} %collective-permute-done.1.refs_0_, ...), custom_call_target="tpu_custom_call" | custom-call | flops 603979776 | bytes 2097152 | tf_op jit(solution)/shard_map/attention/pallas_call | solution.py:665
  41.4 0.0 collective-permute-done.9.refs_2_
  41.4 0.0 copy-done.3
  41.4 0.0 copy-done.5
  41.4 1.8 %final.2 = (bf16[256,1024]{1,0:T(8,128)(2,1)S(1)}, f32[3,1024]{1,0:T(4,128)S(1)}) custom-call(f32[256,1024]{1,0:T(8,128)S(1)} %get-tuple-element.60.pre_ref, f32[256,1024]{1,0:T(8,128)S(1)} %get-tuple-element.61.reach_ref, f32[256,1024]{1,0:T(8,128)S(1)} %get-tuple-element.62.sx_ref, bf16[256,256]{1,0:T(8,128)(2,1)S(1)} %bitcast.27, ...), custom_call_target="tpu_custom_call" | custom-call | flops 67108864 | bytes 5242880 | tf_op jit(solution)/shard_map/final/pallas_call | solution.py:706
  43.2 4.9 %collective-permute-done.6.refs_2_ = bf16[144,1024]{1,0:T(8,128)(2,1)S(1)} collective-permute-done((bf16[144,1024]{1,0:T(8,128)(2,1)S(1)}, bf16[144,1024]{1,0:T(8,128)(2,1)S(1)}, u32[]{:S(2)}, u32[]{:S(2)}) %collective-permute-start.6) | collective-permute-done | bytes 294944 | tf_op jit(solution)/shard_map/ppermute | solution.py:701
  48.1 1.8 %final.3 = (bf16[256,1024]{1,0:T(8,128)(2,1)S(1)}, f32[3,1024]{1,0:T(4,128)S(1)}) custom-call(f32[256,1024]{1,0:T(8,128)S(1)} %get-tuple-element.51.pre_ref, f32[256,1024]{1,0:T(8,128)S(1)} %get-tuple-element.52.reach_ref, f32[256,1024]{1,0:T(8,128)S(1)} %get-tuple-element.53.sx_ref, bf16[256,256]{1,0:T(8,128)(2,1)S(1)} %bitcast.28, ...), custom_call_target="tpu_custom_call" | custom-call | flops 67108864 | bytes 5242880 | tf_op jit(solution)/shard_map/final/pallas_call | solution.py:706
  49.9 0.1 collective-permute-start.10
  50.0 1.6 %collective-permute-start.11 = (f32[3,1024]{1,0:T(4,128)S(1)}, f32[3,1024]{1,0:T(4,128)S(1)}, u32[]{:S(2)}, u32[]{:S(2)}) collective-permute-start(f32[3,1024]{1,0:T(4,128)S(1)} %get-tuple-element.69), channel_id=1, source_target_pairs={{0,16},{4,20},{8,24},{12,28},{16,0},{20,4},{24,8},{28,12},{1,17},{... | collective-permute-start | bytes 36872 | tf_op jit(solution)/shard_map/ppermute | solution.py:535
  51.6 2.8 %collective-permute-start.12 = (f32[3,1024]{1,0:T(4,128)S(1)}, f32[3,1024]{1,0:T(4,128)S(1)}, u32[]{:S(2)}, u32[]{:S(2)}) collective-permute-start(f32[3,1024]{1,0:T(4,128)S(1)} %get-tuple-element.69), channel_id=1, source_target_pairs={{0,24},{4,28},{8,16},{12,20},{16,8},{20,12},{24,0},{28,4},{1,25},{... | collective-permute-start | bytes 36872 | tf_op jit(solution)/shard_map/ppermute | solution.py:535
  54.3 1.0 %writing.2 = bf16[256,2048]{1,0:T(8,128)(2,1)} custom-call(bf16[256,1024]{1,0:T(8,128)(2,1)S(1)} %attention.3.teacher_ref.refs_0_, bf16[256,1024]{1,0:T(8,128)(2,1)S(1)} %attention.2.teacher_ref.refs_1_), custom_call_target="tpu_custom_call" | custom-call | bytes 2097152 | tf_op jit(solution)/shard_map/writing/pallas_call | solution.py:571
  55.3 0.0 collective-permute-done.10
  55.3 0.0 collective-permute-done.11
  55.4 1.7 %collective-permute-done.12 = f32[3,1024]{1,0:T(4,128)S(1)} collective-permute-done((f32[3,1024]{1,0:T(4,128)S(1)}, f32[3,1024]{1,0:T(4,128)S(1)}, u32[]{:S(2)}, u32[]{:S(2)}) %collective-permute-start.12) | collective-permute-done | bytes 12320 | tf_op jit(solution)/shard_map/ppermute | solution.py:535
  57.1 1.8 %collective-permute-start.13 = (f32[3,1024]{1,0:T(4,128)S(1)}, f32[3,1024]{1,0:T(4,128)S(1)}, u32[]{:S(2)}, u32[]{:S(2)}) collective-permute-start(f32[3,1024]{1,0:T(4,128)S(1)} %add_add_fusion.a_ref), channel_id=1, source_target_pairs={{0,4},{4,0},{8,12},{12,8},{16,20},{20,16},{24,28},{28,24},{1,5},{5... | collective-permute-start | bytes 36872 | tf_op jit(solution)/shard_map/ppermute | solution.py:535
  58.9 1.0 %writing.3 = bf16[256,2048]{1,0:T(8,128)(2,1)} custom-call(bf16[256,1024]{1,0:T(8,128)(2,1)S(1)} %get-tuple-element.73.refs_0_, bf16[256,1024]{1,0:T(8,128)(2,1)S(1)} %get-tuple-element.74.refs_1_), custom_call_target="tpu_custom_call" | custom-call | bytes 2097152 | tf_op jit(solution)/shard_map/writing/pallas_call | solution.py:571
  59.9 1.0 %collective-permute-done.13.b_ref = f32[3,1024]{1,0:T(4,128)S(1)} collective-permute-done((f32[3,1024]{1,0:T(4,128)S(1)}, f32[3,1024]{1,0:T(4,128)S(1)}, u32[]{:S(2)}, u32[]{:S(2)}) %collective-permute-start.13) | collective-permute-done | bytes 12320 | tf_op jit(solution)/shard_map/ppermute | solution.py:535
  60.9 0.6 closing.1
  (7 shorter events, 0.1 us)
Async XLA Ops:
  3.9 12.8 %collective-permute-start = (bf16[256,512]{1,0:T(8,128)(2,1)S(1)}, bf16[256,512]{1,0:T(8,128)(2,1)S(1)}, u32[]{:S(2)}, u32[]{:S(2)}) collective-permute-start(bf16[256,512]{1,0:T(8,128)(2,1)S(1)} %get-tuple-element.41), channel_id=1, source_target_pairs={{4,8},{8,4},{5,9},{9,5},{6,10},{10,6},{7,11},{11,7},{20,24},{24,20... | collective-permute-start | bytes 786440 | tf_op jit(solution)/shard_map/ppermute | solution.py:640
  4.6 12.7 %collective-permute-start.1 = (bf16[256,512]{1,0:T(8,128)(2,1)S(1)}, bf16[256,512]{1,0:T(8,128)(2,1)S(1)}, u32[]{:S(2)}, u32[]{:S(2)}) collective-permute-start(bf16[256,512]{1,0:T(8,128)(2,1)S(1)} %get-tuple-element.41), channel_id=1, source_target_pairs={{0,4},{12,8},{4,0},{8,12},{1,5},{13,9},{5,1},{9,13},{2,6},{14,10},... | collective-permute-start | bytes 786440 | tf_op jit(solution)/shard_map/ppermute | solution.py:639
  10.6 13.1 %collective-permute-start.7 = (bf16[144,1024]{1,0:T(8,128)(2,1)S(1)}, bf16[144,1024]{1,0:T(8,128)(2,1)S(1)}, u32[]{:S(2)}, u32[]{:S(2)}) collective-permute-start(bf16[144,1024]{1,0:T(8,128)(2,1)S(1)} %get-tuple-element.66), channel_id=1, source_target_pairs={{0,4},{12,8},{1,5},{13,9},{2,6},{14,10},{3,7},{15,11},{16,20},{28,... | collective-permute-start | bytes 884744 | tf_op jit(solution)/shard_map/ppermute | solution.py:701
  16.8 11.7 %collective-permute-start.3 = (bf16[144,1024]{1,0:T(8,128)(2,1)S(1)}, bf16[144,1024]{1,0:T(8,128)(2,1)S(1)}, u32[]{:S(2)}, u32[]{:S(2)}) collective-permute-start(bf16[144,1024]{1,0:T(8,128)(2,1)S(1)} %merge.1), channel_id=1, source_target_pairs={{0,4},{12,8},{4,0},{8,12},{1,5},{13,9},{5,1},{9,13},{2,6},{14,10},... | collective-permute-start | bytes 884744 | tf_op jit(solution)/shard_map/ppermute | solution.py:652
  17.3 7.0 %collective-permute-start.2 = (bf16[256,512]{1,0:T(8,128)(2,1)S(1)}, bf16[256,512]{1,0:T(8,128)(2,1)S(1)}, u32[]{:S(2)}, u32[]{:S(2)}) collective-permute-start(bf16[256,512]{1,0:T(8,128)(2,1)S(1)} %collective-permute-done.1.refs_0_), channel_id=1, source_target_pairs={{4,8},{8,4},{5,9},{9,5},{6,10},{10,6},{7,11},{11,7},{20,24},{24,20... | collective-permute-start | bytes 786440 | tf_op jit(solution)/shard_map/ppermute | solution.py:642
  23.6 5.7 %collective-permute-start.8 = (bf16[144,1024]{1,0:T(8,128)(2,1)S(1)}, bf16[144,1024]{1,0:T(8,128)(2,1)S(1)}, u32[]{:S(2)}, u32[]{:S(2)}) collective-permute-start(bf16[144,1024]{1,0:T(8,128)(2,1)S(1)} %chain.6), channel_id=1, source_target_pairs={{4,8},{8,4},{5,9},{9,5},{6,10},{10,6},{7,11},{11,7},{20,24},{24,20... | collective-permute-start | bytes 884744 | tf_op jit(solution)/shard_map/ppermute | solution.py:701
  24.3 10.0 %collective-permute-start.4 = (bf16[256,512]{1,0:T(8,128)(2,1)S(1)}, bf16[256,512]{1,0:T(8,128)(2,1)S(1)}, u32[]{:S(2)}, u32[]{:S(2)}) collective-permute-start(bf16[256,512]{1,0:T(8,128)(2,1)S(1)} %collective-permute-done.2.refs_2_), channel_id=1, source_target_pairs={{4,0},{8,12},{5,1},{9,13},{6,2},{10,14},{7,3},{11,15},{20,16},{24,... | collective-permute-start | bytes 786440 | tf_op jit(solution)/shard_map/ppermute | solution.py:654
  28.5 5.8 %copy-start = (bf16[1,256,2048]{2,1,0:T(8,128)(2,1)S(1)}, bf16[1,256,2048]{2,1,0:T(8,128)(2,1)}, u32[]{:S(2)}) copy-start(bf16[1,256,2048]{2,1,0:T(8,128)(2,1)} %param.13) | copy-start | bytes 3145732
  28.5 5.8 %copy-start.1 = (bf16[1,256,256]{2,1,0:T(8,128)(2,1)S(1)}, bf16[1,256,256]{2,1,0:T(8,128)(2,1)}, u32[]{:S(2)}) copy-start(bf16[1,256,256]{2,1,0:T(8,128)(2,1)} %param.14) | copy-start | bytes 393220
  28.5 5.8 %copy-start.2 = (bf16[1,256,256]{2,1,0:T(8,128)(2,1)S(1)}, bf16[1,256,256]{2,1,0:T(8,128)(2,1)}, u32[]{:S(2)}) copy-start(bf16[1,256,256]{2,1,0:T(8,128)(2,1)} %param.15) | copy-start | bytes 393220
  28.5 8.6 %collective-permute-start.5 = (bf16[144,1024]{1,0:T(8,128)(2,1)S(1)}, bf16[144,1024]{1,0:T(8,128)(2,1)S(1)}, u32[]{:S(2)}, u32[]{:S(2)}) collective-permute-start(bf16[144,1024]{1,0:T(8,128)(2,1)S(1)} %chain.4), channel_id=1, source_target_pairs={{4,8},{8,4},{5,9},{9,5},{6,10},{10,6},{7,11},{11,7},{20,24},{24,20... | collective-permute-start | bytes 884744 | tf_op jit(solution)/shard_map/ppermute | solution.py:701
  29.3 5.0 %copy-start.4 = (s32[1,1024]{1,0:T(1,128)S(1)}, s32[1,1024]{1,0:T(1,128)}, u32[]{:S(2)}) copy-start(s32[1,1024]{1,0:T(1,128)} %docs_ref.7) | copy-start | bytes 12292
  29.4 12.0 %collective-permute-start.9 = (bf16[144,1024]{1,0:T(8,128)(2,1)S(1)}, bf16[144,1024]{1,0:T(8,128)(2,1)S(1)}, u32[]{:S(2)}, u32[]{:S(2)}) collective-permute-start(bf16[144,1024]{1,0:T(8,128)(2,1)S(1)} %chain.7), channel_id=1, source_target_pairs={{8,12},{4,0},{9,13},{5,1},{10,14},{6,2},{11,15},{7,3},{24,28},{20,... | collective-permute-start | bytes 884744 | tf_op jit(solution)/shard_map/ppermute | solution.py:701
  37.1 4.3 %copy-start.3 = (bf16[1,256,256]{2,1,0:T(8,128)(2,1)S(1)}, bf16[1,256,256]{2,1,0:T(8,128)(2,1)}, u32[]{:S(2)}) copy-start(bf16[1,256,256]{2,1,0:T(8,128)(2,1)} %param.20) | copy-start | bytes 393220
  37.2 4.3 %copy-start.5 = (f32[2048]{0:T(1024)S(1)}, f32[2048]{0:T(1024)}, u32[]{:S(2)}) copy-start(f32[2048]{0:T(1024)} %param.25) | copy-start | bytes 24580
  37.2 11.0 %collective-permute-start.6 = (bf16[144,1024]{1,0:T(8,128)(2,1)S(1)}, bf16[144,1024]{1,0:T(8,128)(2,1)S(1)}, u32[]{:S(2)}, u32[]{:S(2)}) collective-permute-start(bf16[144,1024]{1,0:T(8,128)(2,1)S(1)} %chain.5), channel_id=1, source_target_pairs={{8,12},{4,0},{9,13},{5,1},{10,14},{6,2},{11,15},{7,3},{24,28},{20,... | collective-permute-start | bytes 884744 | tf_op jit(solution)/shard_map/ppermute | solution.py:701
  49.9 5.4 %collective-permute-start.10 = (f32[3,1024]{1,0:T(4,128)S(1)}, f32[3,1024]{1,0:T(4,128)S(1)}, u32[]{:S(2)}, u32[]{:S(2)}) collective-permute-start(f32[3,1024]{1,0:T(4,128)S(1)} %get-tuple-element.69), channel_id=1, source_target_pairs={{0,8},{4,12},{8,0},{12,4},{16,24},{20,28},{24,16},{28,20},{1,9},{5... | collective-permute-start | bytes 36872 | tf_op jit(solution)/shard_map/ppermute | solution.py:535
  50.0 5.4 %collective-permute-start.11 = (f32[3,1024]{1,0:T(4,128)S(1)}, f32[3,1024]{1,0:T(4,128)S(1)}, u32[]{:S(2)}, u32[]{:S(2)}) collective-permute-start(f32[3,1024]{1,0:T(4,128)S(1)} %get-tuple-element.69), channel_id=1, source_target_pairs={{0,16},{4,20},{8,24},{12,28},{16,0},{20,4},{24,8},{28,12},{1,17},{... | collective-permute-start | bytes 36872 | tf_op jit(solution)/shard_map/ppermute | solution.py:535
  51.6 5.5 %collective-permute-start.12 = (f32[3,1024]{1,0:T(4,128)S(1)}, f32[3,1024]{1,0:T(4,128)S(1)}, u32[]{:S(2)}, u32[]{:S(2)}) collective-permute-start(f32[3,1024]{1,0:T(4,128)S(1)} %get-tuple-element.69), channel_id=1, source_target_pairs={{0,24},{4,28},{8,16},{12,20},{16,8},{20,12},{24,0},{28,4},{1,25},{... | collective-permute-start | bytes 36872 | tf_op jit(solution)/shard_map/ppermute | solution.py:535
  57.1 3.8 %collective-permute-start.13 = (f32[3,1024]{1,0:T(4,128)S(1)}, f32[3,1024]{1,0:T(4,128)S(1)}, u32[]{:S(2)}, u32[]{:S(2)}) collective-permute-start(f32[3,1024]{1,0:T(4,128)S(1)} %add_add_fusion.a_ref), channel_id=1, source_target_pairs={{0,4},{4,0},{8,12},{12,8},{16,20},{20,16},{24,28},{28,24},{1,5},{5... | collective-permute-start | bytes 36872 | tf_op jit(solution)/shard_map/ppermute | solution.py:535

commit v15 on v14

--- a/solution.py
+++ b/solution.py
@@ -88,17 +88,10 @@
     return source
 
 
-def put_state(ref, state):
-    ref[:N, :] = state.astype(BF16)
-    ref[N:, :] = jnp.zeros((EXTRA, ref.shape[1]), BF16)
-
-
-def put_composite(ref, state, decay):
-    hi, lo = parts(decay)
-    ref[:N, :] = state.astype(BF16)
-    ref[N:, :] = jnp.concatenate(
-        [hi, lo, jnp.zeros((EXTRA - 2, ref.shape[1]), BF16)], axis=0
-    )
+def passed_decay(ref, first, heads, width, g):
+    matrix = spread_matrix(heads, width, g * (width // P_SIZE))
+    wide = jnp.dot(ref[first : first + EXTRA, :heads], matrix, preferred_element_type=F32)
+    return wide[0:1] + wide[1:2]
 
 
 def opening_kernel(
@@ -124,8 +117,9 @@
     width = x_ref.shape[1] // groups
     kv_width = k_ref.shape[1]
     index = lax.axis_index("ctx")
-    kv_ref[:, :kv_width] = k_ref[...]
-    kv_ref[:, kv_width:] = v_ref[...]
+    kv_ref[:rows, :kv_width] = k_ref[...]
+    kv_ref[:rows, kv_width:] = v_ref[...]
+    kv_ref[rows:, :] = jnp.zeros((EXTRA, 2 * kv_width), BF16)
     triangle = jnp.where(lower_triangle(stretch), 1.0, 0.0)
     slope = jnp.exp(as_column(log_ref[...]))
     bias = as_column(bias_ref[...])
@@ -155,6 +149,13 @@
         ends = jnp.where(lane == 2 + half, final, ends)
         same = jnp.where(as_column(row) == last.astype(F32), 1.0, 0.0)
         projs.append((b_ref[sl, :].astype(F32) * same).astype(BF16))
+    both = ends[:, 0:1] * ends[:, 1:2]
+    r = lax.broadcasted_iota(jnp.int32, (heads, heads), 0)
+    c = lax.broadcasted_iota(jnp.int32, (heads, heads), 1)
+    hi, lo = parts(jnp.sum(jnp.where(r == c, both, 0.0), axis=0, keepdims=True))
+    kv_ref[rows:, :heads] = jnp.concatenate(
+        [hi, lo, jnp.zeros((EXTRA - 2, heads), BF16)], axis=0
+    )
     for g in range(groups):
         cols = slice(g * width, (g + 1) * width)
         matrix = spread_matrix(heads, width, g * (heads // groups))
@@ -171,27 +172,33 @@
 
         @pl.when(index == 0)
         def _():
-            put_state(send_refs[g], sums[0])
+            send_refs[g][...] = sums[0].astype(BF16)
 
         @pl.when(index != 0)
         def _():
-            put_composite(send_refs[g], wide[1:2] * sums[0] + sums[1], wide[0:1] * wide[1:2])
-
-
-def chain_kernel(count, stage, got_ref, f_ref, b_ref, dec_ref, send_ref):
+            send_refs[g][...] = (wide[1:2] * sums[0] + sums[1]).astype(BF16)
+
+
+def chain_kernel(count, stage, g, heads, got_ref, f_ref, b_ref, dec_ref, *refs):
+    send_ref = refs[-1]
+    width = f_ref.shape[1]
     index = lax.axis_index("ctx")
 
     @pl.when(index == stage)
     def _():
         state = dec_ref[0:1, :] * got_ref[:N, :].astype(F32) + f_ref[...].astype(F32)
-        put_state(send_ref, state)
+        send_ref[...] = state.astype(BF16)
 
     @pl.when(index == count - 1 - stage)
     def _():
-        decay = got_ref[N : N + 1, :].astype(F32) + got_ref[N + 1 : N + 2, :].astype(F32)
+        decay = jnp.ones((1, width), F32)
+        for r, ref in enumerate(refs[:-1]):
+            one = passed_decay(ref, ref.shape[0] - EXTRA, heads, width, g)
+            if count != 4:
+                one = jnp.where(ring_source(index, count, r + 1) > index, one, 1.0)
+            decay = decay * one
         inner = decay * f_ref[...].astype(F32) + got_ref[:N, :].astype(F32)
-        state = dec_ref[1:2, :] * inner + b_ref[...].astype(F32)
-        put_composite(send_ref, state, dec_ref[1:2, :] * decay * dec_ref[0:1, :])
+        send_ref[...] = (dec_ref[1:2, :] * inner + b_ref[...].astype(F32)).astype(BF16)
 
 
 def local_kernel(
@@ -256,18 +263,21 @@
 def merge_kernel(count, state_ref, kv_ref, out_ref):
     index = lax.axis_index("ctx")
     outer = (index == 0) | (index == count - 1)
-    rows, wide = kv_ref.shape
+    wide = kv_ref.shape[1]
+    rows = kv_ref.shape[0] - EXTRA
     stretch = rows // 2
 
     @pl.when(outer)
     def _():
-        out_ref[...] = state_ref[...]
+        out_ref[:N, :] = state_ref[...]
+        out_ref[N:, :] = jnp.zeros((EXTRA, out_ref.shape[1]), BF16)
 
     @pl.when(jnp.logical_not(outer))
     def _():
         out_ref[:stretch, :wide] = kv_ref[:stretch, :]
-        out_ref[:stretch, wide:] = kv_ref[stretch:, :]
-        out_ref[stretch:, :] = jnp.zeros((out_ref.shape[0] - stretch, 2 * wide), BF16)
+        out_ref[:stretch, wide:] = kv_ref[stretch:rows, :]
+        out_ref[stretch:, :wide] = kv_ref[rows:, :]
+        out_ref[stretch:, wide:] = jnp.zeros((EXTRA, wide), BF16)
 
 
 def arrivals(index, count, refs):
@@ -402,6 +412,7 @@
     g,
     groups,
     loss_scale,
+    heads,
     pre_ref,
     reach_ref,
     sx_ref,
@@ -414,7 +425,9 @@
 ):
     others = count - 1
     got = refs[:others]
-    before = refs[others] if g else None
+    sent = 5 if count == 4 else others
+    kv_refs = refs[others : others + sent]
+    before = refs[others + sent] if g else None
     proj = slice(g * N, (g + 1) * N)
     first_lane = g * pre_ref.shape[1]
     out_ref, grad_ref, front, back, flow, gated_ref, sums, gain_acc, skip_acc = refs[-9:]
@@ -430,10 +443,7 @@
 
     @pl.when(index == count - 1)
     def _():
-        back[:N, :] = jnp.zeros((N, width), BF16)
-        back[N:, :] = jnp.where(
-            lax.broadcasted_iota(jnp.int32, (EXTRA, width), 0) == 0, 1.0, 0.0
-        ).astype(BF16)
+        back[...] = jnp.zeros_like(back)
 
     for r in range(1, count):
 
@@ -443,11 +453,18 @@
 
         @pl.when(index == count - 1 - r)
         def _():
-            back[...] = got[r - 1][...]
-
-    d_in = back[N : N + 1, :].astype(F32) + back[N + 1 : N + 2, :].astype(F32)
+            back[...] = got[r - 1][:N, :]
+
+    d_in = jnp.ones((1, width), F32)
+    for source, places in arrivals(index, count, kv_refs):
+        for condition, ref in places:
+            used = source > index
+            if condition is not None:
+                used = used & condition
+            one = passed_decay(ref, ref.shape[0] - EXTRA, heads, width, g)
+            d_in = d_in * jnp.where(used, one, 1.0)
     through = dec_ref[0:1, :] * front[...].astype(F32) + f_ref[...].astype(F32)
-    entering = (d_in * through + back[:N, :].astype(F32)).astype(BF16)
+    entering = (d_in * through + back[...].astype(F32)).astype(BF16)
     flow[:stretch, :] = jnp.dot(c_ref[:stretch, proj], front[...], preferred_element_type=F32)
     flow[stretch:, :] = jnp.dot(c_ref[stretch:, proj], entering, preferred_element_type=F32)
     gain_acc[...] = jnp.zeros_like(gain_acc)
@@ -567,7 +584,7 @@
     def in_hbm(*arrays):
         return [pltpu.with_memory_space_constraint(array, pltpu.HBM) for array in arrays]
 
-    def write(pieces):
+    def write(*pieces):
         return pl.pallas_call(
             writing_kernel,
             out_shape=struct((rows, features), BF16),
@@ -584,12 +601,12 @@
     outs = pl.pallas_call(
         functools.partial(opening_kernel, count, groups),
         out_shape=(
-            struct((rows, 2 * kv_dev * DH), BF16),
+            struct((rows + EXTRA, 2 * kv_dev * DH), BF16),
             struct((heads, rows), F32),
             *([struct((rows, width), BF16)] * groups),
             *([struct((8, width), F32)] * groups),
             *([state] * (2 * groups)),
-            *([payload] * groups),
+            *([state] * groups),
         ),
         in_specs=[VMEM] * 8,
         out_specs=(VMEM,) * (2 + 5 * groups),
@@ -634,6 +651,17 @@
 
     send = list(send)
     got = [[] for _ in range(groups)]
+    def passed_on(g, stage, needed):
+        return pl.pallas_call(
+            functools.partial(chain_kernel, count, stage, g, heads),
+            out_shape=state,
+            in_specs=[VMEM] * (4 + len(needed)),
+            out_specs=VMEM,
+            compiler_params=params(6),
+            cost_estimate=cost(16384 * N * width, 8 * N * width),
+            name="chain",
+        )(got[g][-1], f_parts[g], b_parts[g], dec[g], *needed)
+
     if count == 4:
         inward, outward, across = [(0, 1), (3, 2)], [(1, 0), (2, 3)], [(1, 2), (2, 1)]
         near = lax.ppermute(kv, "ctx", inward + outward)
@@ -651,6 +679,11 @@
         )(send[-1], middle)
         far = lax.ppermute(send[-1], "ctx", inward + outward)
         got[-1].append(far)
+        if groups > 1:
+            got[0].append(lax.ppermute(send[0], "ctx", [(0, 1), (3, 2)]))
+            send[0] = passed_on(0, 1, [near])
+            beyond, _ = lax.optimization_barrier((beyond, send[0]))
+            got[0].append(lax.ppermute(send[0], "ctx", across))
         farther = lax.ppermute(beyond, "ctx", outward)
         kv_got = [near, middle, beyond, far, farther]
     else:
@@ -684,33 +717,31 @@
     ]
     for r in range(1, count):
         for g in range(groups):
+            if len(got[g]) >= r:
+                continue
             if r == 3 and g == groups - 1:
                 got[g][-1], targets[0] = lax.optimization_barrier((got[g][-1], targets[0]))
             if r > 1:
-                send[g] = pl.pallas_call(
-                    functools.partial(chain_kernel, count, r - 1),
-                    out_shape=payload,
-                    in_specs=[VMEM] * 4,
-                    out_specs=VMEM,
-                    compiler_params=params(4),
-                    cost_estimate=cost(8 * N * width, 8 * N * width),
-                    name="chain",
-                )(got[g][-1], f_parts[g], b_parts[g], dec[g])
-            if len(got[g]) < r:
-                pairs = [(r - 1, r), (count - r, count - r - 1)]
-                got[g].append(lax.ppermute(send[g], "ctx", pairs))
-
+                if count == 4:
+                    needed = [near] if r == 2 else [middle, beyond]
+                else:
+                    needed = kv_got
+                send[g] = passed_on(g, r - 1, needed)
+            pairs = [(r - 1, r), (count - r, count - r - 1)]
+            got[g].append(lax.ppermute(send[g], "ctx", pairs))
+
+    got[0][-1], *targets = lax.optimization_barrier((got[0][-1], *targets))
     normed, grads = [], None
     for g in range(groups):
         more = [] if grads is None else [grads]
         made, grads = pl.pallas_call(
-            functools.partial(final_kernel, count, g, groups, loss_scale),
+            functools.partial(final_kernel, count, g, groups, loss_scale, heads),
             out_shape=(struct((rows, width), BF16), struct((groups + 1, width), F32)),
-            in_specs=[VMEM] * (8 + others + len(more)),
+            in_specs=[VMEM] * (8 + others + len(kv_got) + len(more)),
             out_specs=(VMEM,) * 2,
             scratch_shapes=[
                 pltpu.VMEM((N, width), BF16),
-                pltpu.VMEM((N + EXTRA, width), BF16),
+                pltpu.VMEM((N, width), BF16),
                 pltpu.VMEM((rows, width), F32),
                 pltpu.VMEM((rows, width), F32),
                 pltpu.VMEM((rows, 3 * 128), F32),
@@ -728,15 +759,13 @@
             f_parts[g],
             dec[g],
             *got[g],
+            *kv_got,
             *more,
         )
         normed.append(made)
+    teacher, student = write(*targets), write(*normed)
     shifts = [1 << k for k in reversed(range(count.bit_length() - 1))]
     partner = exchange(grads, shifts[0])
-    *targets, _ = lax.optimization_barrier((*targets, grads))
-    teacher = write(targets)
-    partner, teacher = lax.optimization_barrier((partner, teacher))
-    student = write(normed)
     if lax.axis_size("dp") == 2:
         grads = (grads + partner) + (exchange(grads, count) + exchange(grads, count + shifts[0]))
     else:

time: 61.9 us -> 60.6 us (0.979)
  waiting for transfers between devices: 20.1 us -> 19.3 us
  starting transfers between devices: 21.3 us -> 20.6 us
    ppermute x5 -> x3, waiting for transfers between devices: 10.5 us -> 2.26 us  [body(): got[g].append(lax.ppermute(send[g], 'ctx', pairs))]
    ppermute x0 -> x2, waiting for transfers between devices: none -> 4.95 us  [the longest x1 4.94 us: body(): got[0].append(lax.ppermute(send[0], 'ctx', [(0, 1), (3, 2)]))]
    ppermute x5 -> x3, starting transfers between devices: 6.12 us -> 3.51 us  [body(): got[g].append(lax.ppermute(send[g], 'ctx', pairs))]
    ppermute x0 -> x2, starting transfers between devices: none -> 2.6 us  [the longest x1 1.93 us: body(): got[0].append(lax.ppermute(send[0], 'ctx', [(0, 1), (3, 2)]))]
    ppermute x1, waiting for transfers between devices: 3.63 us -> 6.1 us  [body(): farther = lax.ppermute(beyond, 'ctx', outward)]
    ppermute x4, starting transfers between devices: 6.27 us -> 5.24 us  [exchange(): return lax.ppermute(part, axes, [(d, d ^ shift) for d in range(size)])]
  transfers between devices with their start and end apart: 14 -> 14, of which waited for: 7 -> 8; matrix products, arithmetic and copies ran while one was open for 0% -> 0% of each run, Pallas kernels for 22% -> 23%
where the time goes in v15:
time: 60.6 us; the launch traced here: 60.3 us
  starting transfers between devices  20.6 us (34%)
  Pallas kernels  19.4 us (32%)
  waiting for transfers between devices  19.3 us (32%)
  between operations  0.87 us (1%)
    ppermute x1, waiting for transfers between devices, body(): farther = lax.ppermute(beyond, 'ctx', outward)  6.1 us
    ppermute x1, starting transfers between devices, body(): near = lax.ppermute(kv, 'ctx', inward + outward)  5.97 us
    pallas_call x2, Pallas kernels, body(): pl.pallas_call(functools.partial(attention_kernel, count, per_kv, stack,...  5.58 us
    ppermute x4, starting transfers between devices, exchange(): return lax.ppermute(part, axes, [(d, d ^ shift) for d in range(size)])  5.24 us
    ppermute x1, waiting for transfers between devices, body(): got[0].append(lax.ppermute(send[0], 'ctx', [(0, 1), (3, 2)]))  4.94 us
    pallas_call x1, Pallas kernels, body(): pl.pallas_call(functools.partial(local_kernel, count, groups), out_shape=...  4.19 us
    pallas_call x2, Pallas kernels, body(): pl.pallas_call(functools.partial(final_kernel, count, g, groups, loss_sca...  3.77 us
    ppermute x3, starting transfers between devices, body(): got[g].append(lax.ppermute(send[g], 'ctx', pairs))  3.51 us
  transfers between devices with their start and end apart: 14, of which 8 were waited for; matrix products, arithmetic and copies ran while one was open for 0% of the time, Pallas kernels for 23%

profile of v15, /device:TPU:0, one launch (start us, length us, event | category | flops | bytes accessed | tf_op | source)
XLA Modules:
  0.0 60.3 jit_solution(5889779811540501693)
XLA Ops:
  0.6 3.2 %opening.1 = (bf16[272,512]{1,0:T(8,128)(2,1)S(1)}, f32[32,256]{1,0:T(8,128)S(1)}, bf16[256,1024]{1,0:T(8,128)(2,1)S(1)}, bf16[256,1024]{1,0:T(8,128)(2,1)S(1)},...) custom-call(s32[1,1024]{1,0:T(1,128)} %docs_ref.7, ...), custom_call_target="tpu_custom_call" | custom-call | flops 268435456 | bytes 4194304 | tf_op jit(solution)/shard_map/opening/pallas_call | solution.py:601
  3.9 0.7 %collective-permute-start.3 = (bf16[272,512]{1,0:T(8,128)(2,1)S(1)}, bf16[272,512]{1,0:T(8,128)(2,1)S(1)}, u32[]{:S(2)}, u32[]{:S(2)}) collective-permute-start(bf16[272,512]{1,0:T(8,128)(2,1)S(1)} %get-tuple-element.45), channel_id=1, source_target_pairs={{4,8},{8,4},{5,9},{9,5},{6,10},{10,6},{7,11},{11,7},{20,24},{24,20... | collective-permute-start | bytes 835592 | tf_op jit(solution)/shard_map/ppermute | solution.py:668
  4.6 6.0 %collective-permute-start.1 = (bf16[272,512]{1,0:T(8,128)(2,1)S(1)}, bf16[272,512]{1,0:T(8,128)(2,1)S(1)}, u32[]{:S(2)}, u32[]{:S(2)}) collective-permute-start(bf16[272,512]{1,0:T(8,128)(2,1)S(1)} %get-tuple-element.45), channel_id=1, source_target_pairs={{0,4},{12,8},{4,0},{8,12},{1,5},{13,9},{5,1},{9,13},{2,6},{14,10},... | collective-permute-start | bytes 835592 | tf_op jit(solution)/shard_map/ppermute | solution.py:667
  10.5 1.9 %collective-permute-start = (bf16[128,1024]{1,0:T(8,128)(2,1)S(1)}, bf16[128,1024]{1,0:T(8,128)(2,1)S(1)}, u32[]{:S(2)}, u32[]{:S(2)}) collective-permute-start(bf16[128,1024]{1,0:T(8,128)(2,1)S(1)} %get-tuple-element.41), channel_id=1, source_target_pairs={{0,4},{12,8},{1,5},{13,9},{2,6},{14,10},{3,7},{15,11},{16,20},{28,... | collective-permute-start | bytes 786440 | tf_op jit(solution)/shard_map/ppermute | solution.py:683
  12.5 4.2 %local.1 = (f32[256,1024]{1,0:T(8,128)S(1)}, f32[256,1024]{1,0:T(8,128)S(1)}, f32[256,1024]{1,0:T(8,128)S(1)}, f32[256,1024]{1,0:T(8,128)S(1)}, f32[256,1024]{1,0:T(8,128)S(1)}, /*index=5*/f32[256,1024]{1,0:T(8,128)S(1)}) custom-call(s32[1,1024]{1,0:T(1,128)} %docs_ref.7, bf16[256,2048]{1,0:T(8,128)(2,1)} %bitcast.32, bf16[256,2048]{1,0:T(8,128)(2,1)} %bitcast.33, ...), custom_call_target="tpu_custom_call" | custom-call | flops 134217728 | bytes 8388608 | tf_op jit(solution)/shard_map/local/pallas_call | solution.py:633
  16.7 0.0 collective-permute-done.3.refs_0_.kv_ref.refs_1_.refs_4_
  16.7 0.6 %collective-permute-start.6 = (bf16[144,1024]{1,0:T(8,128)(2,1)S(1)}, bf16[144,1024]{1,0:T(8,128)(2,1)S(1)}, u32[]{:S(2)}, u32[]{:S(2)}) collective-permute-start(bf16[144,1024]{1,0:T(8,128)(2,1)S(1)} %merge.1), channel_id=1, source_target_pairs={{0,4},{12,8},{4,0},{8,12},{1,5},{13,9},{5,1},{9,13},{2,6},{14,10},... | collective-permute-start | bytes 884744 | tf_op jit(solution)/shard_map/ppermute | solution.py:680
  17.4 0.3 collective-permute-done.1.refs_0_.refs_3_
  17.6 0.7 %collective-permute-start.4 = (bf16[272,512]{1,0:T(8,128)(2,1)S(1)}, bf16[272,512]{1,0:T(8,128)(2,1)S(1)}, u32[]{:S(2)}, u32[]{:S(2)}) collective-permute-start(bf16[272,512]{1,0:T(8,128)(2,1)S(1)} %collective-permute-done.1.refs_0_.refs_3_), channel_id=1, source_target_pairs={{4,8},{8,4},{5,9},{9,5},{6,10},{10,6},{7,11},{11,7},{20,24},{24,20... | collective-permute-start | bytes 835592 | tf_op jit(solution)/shard_map/ppermute | solution.py:670
  18.3 4.9 %collective-permute-done.got_ref.refs_0_ = bf16[128,1024]{1,0:T(8,128)(2,1)S(1)} collective-permute-done((bf16[128,1024]{1,0:T(8,128)(2,1)S(1)}, bf16[128,1024]{1,0:T(8,128)(2,1)S(1)}, u32[]{:S(2)}, u32[]{:S(2)}) %collective-permute-start) | collective-permute-done | bytes 262176 | tf_op jit(solution)/shard_map/ppermute | solution.py:683
  23.3 0.7 %collective-permute-start.2 = (bf16[128,1024]{1,0:T(8,128)(2,1)S(1)}, bf16[128,1024]{1,0:T(8,128)(2,1)S(1)}, u32[]{:S(2)}, u32[]{:S(2)}) collective-permute-start(bf16[128,1024]{1,0:T(8,128)(2,1)S(1)} %chain.4), channel_id=1, source_target_pairs={{4,8},{8,4},{5,9},{9,5},{6,10},{10,6},{7,11},{11,7},{20,24},{24,20... | collective-permute-start | bytes 786440 | tf_op jit(solution)/shard_map/ppermute | solution.py:686
  23.9 0.0 collective-permute-done.4.refs_1_.refs_2_.refs_5_
  23.9 1.3 %collective-permute-start.8 = (bf16[272,512]{1,0:T(8,128)(2,1)S(1)}, bf16[272,512]{1,0:T(8,128)(2,1)S(1)}, u32[]{:S(2)}, u32[]{:S(2)}) collective-permute-start(bf16[272,512]{1,0:T(8,128)(2,1)S(1)} %collective-permute-done.4.refs_1_.refs_2_.refs_5_), channel_id=1, source_target_pairs={{4,0},{8,12},{5,1},{9,13},{6,2},{10,14},{7,3},{11,15},{20,16},{24,... | collective-permute-start | bytes 835592 | tf_op jit(solution)/shard_map/ppermute | solution.py:687
  25.2 2.9 %collective-permute-done.6.got_ref.refs_3_.refs_6_.refs_0_ = bf16[144,1024]{1,0:T(8,128)(2,1)S(1)} collective-permute-done((bf16[144,1024]{1,0:T(8,128)(2,1)S(1)}, bf16[144,1024]{1,0:T(8,128)(2,1)S(1)}, u32[]{:S(2)}, u32[]{:S(2)}) %collective-permute-start.6) | collective-permute-done | bytes 294944 | tf_op jit(solution)/shard_map/ppermute | solution.py:680
  28.1 0.0 copy-start
  28.1 0.0 copy-start.1
  28.1 0.8 %collective-permute-start.7 = (bf16[128,1024]{1,0:T(8,128)(2,1)S(1)}, bf16[128,1024]{1,0:T(8,128)(2,1)S(1)}, u32[]{:S(2)}, u32[]{:S(2)}) collective-permute-start(bf16[128,1024]{1,0:T(8,128)(2,1)S(1)} %chain.6), channel_id=1, source_target_pairs={{4,8},{8,4},{5,9},{9,5},{6,10},{10,6},{7,11},{11,7},{20,24},{24,20... | collective-permute-start | bytes 786440 | tf_op jit(solution)/shard_map/ppermute | solution.py:731
  28.9 0.0 collective-permute-done.2.got_ref.refs_1_
  28.9 0.0 copy-start.4
  29.0 1.3 %collective-permute-start.5 = (bf16[128,1024]{1,0:T(8,128)(2,1)S(1)}, bf16[128,1024]{1,0:T(8,128)(2,1)S(1)}, u32[]{:S(2)}, u32[]{:S(2)}) collective-permute-start(bf16[128,1024]{1,0:T(8,128)(2,1)S(1)} %chain.5), channel_id=1, source_target_pairs={{8,12},{4,0},{9,13},{5,1},{10,14},{6,2},{11,15},{7,3},{24,28},{20,... | collective-permute-start | bytes 786440 | tf_op jit(solution)/shard_map/ppermute | solution.py:731
  30.3 6.1 %collective-permute-done.8.refs_4_.refs_7_ = bf16[272,512]{1,0:T(8,128)(2,1)S(1)} collective-permute-done((bf16[272,512]{1,0:T(8,128)(2,1)S(1)}, bf16[272,512]{1,0:T(8,128)(2,1)S(1)}, u32[]{:S(2)}, u32[]{:S(2)}) %collective-permute-start.8) | collective-permute-done | bytes 278560 | tf_op jit(solution)/shard_map/ppermute | solution.py:687
  36.4 0.0 copy-done
  36.4 0.0 copy-done.1
  36.4 0.0 copy-done.2
  36.4 0.0 copy-done.4
  36.4 2.8 %attention.2.refs_0_.teacher_ref = bf16[256,1024]{1,0:T(8,128)(2,1)S(1)} custom-call(s32[1,1024]{1,0:T(1,128)S(1)} %copy-done.4, bf16[256,2048]{1,0:T(8,128)(2,1)S(1)} %bitcast.18, bf16[256,256]{1,0:T(8,128)(2,1)S(1)} %bitcast.21, bf16[256,256]{1,0:T(8,128)(2,1)S(1)} %bitcast.24, bf16[272,512]{1,0:T(8,128)(2,1)S(1)} %collective-permute-done.1.refs_0_.refs_3_, ...), custom_call_target="tpu_custom_call" | custom-call | flops 603979776 | bytes 2097152 | tf_op jit(solution)/shard_map/attention/pallas_call | solution.py:698
  39.2 0.0 collective-permute-done.7.got_ref.refs_1_
  39.2 0.0 copy-start.3
  39.3 0.0 copy-start.5
  39.3 1.4 %collective-permute-start.9 = (bf16[128,1024]{1,0:T(8,128)(2,1)S(1)}, bf16[128,1024]{1,0:T(8,128)(2,1)S(1)}, u32[]{:S(2)}, u32[]{:S(2)}) collective-permute-start(bf16[128,1024]{1,0:T(8,128)(2,1)S(1)} %chain.7), channel_id=1, source_target_pairs={{8,12},{4,0},{9,13},{5,1},{10,14},{6,2},{11,15},{7,3},{24,28},{20,... | collective-permute-start | bytes 786440 | tf_op jit(solution)/shard_map/ppermute | solution.py:731
  40.7 2.8 %attention.3.refs_1_.teacher_ref = bf16[256,1024]{1,0:T(8,128)(2,1)S(1)} custom-call(s32[1,1024]{1,0:T(1,128)S(1)} %copy-done.4, bf16[256,2048]{1,0:T(8,128)(2,1)S(1)} %bitcast.19, bf16[256,256]{1,0:T(8,128)(2,1)S(1)} %bitcast.22, bf16[256,256]{1,0:T(8,128)(2,1)S(1)} %bitcast.25, bf16[272,512]{1,0:T(8,128)(2,1)S(1)} %collective-permute-done.1.refs_0_.refs_3_, ...), custom_call_target="tpu_custom_call" | custom-call | flops 603979776 | bytes 2097152 | tf_op jit(solution)/shard_map/attention/pallas_call | solution.py:698
  43.5 0.0 collective-permute-done.5.refs_2_
  43.5 0.0 copy-done.3
  43.5 0.0 copy-done.5
  43.5 1.9 %final.2 = (bf16[256,1024]{1,0:T(8,128)(2,1)S(1)}, f32[3,1024]{1,0:T(4,128)S(1)}) custom-call(f32[256,1024]{1,0:T(8,128)S(1)} %get-tuple-element.64.pre_ref, f32[256,1024]{1,0:T(8,128)S(1)} %get-tuple-element.65.reach_ref, f32[256,1024]{1,0:T(8,128)S(1)} %get-tuple-element.66.sx_ref, bf16[256,256]{1,0:T(8,128)(2,1)S(1)} %bitcast.27, ...), custom_call_target="tpu_custom_call" | custom-call | flops 67108864 | bytes 5242880 | tf_op jit(solution)/shard_map/final/pallas_call | solution.py:737
  45.4 2.3 %collective-permute-done.9.refs_2_ = bf16[128,1024]{1,0:T(8,128)(2,1)S(1)} collective-permute-done((bf16[128,1024]{1,0:T(8,128)(2,1)S(1)}, bf16[128,1024]{1,0:T(8,128)(2,1)S(1)}, u32[]{:S(2)}, u32[]{:S(2)}) %collective-permute-start.9) | collective-permute-done | bytes 262176 | tf_op jit(solution)/shard_map/ppermute | solution.py:731
  47.7 1.9 %final.3 = (bf16[256,1024]{1,0:T(8,128)(2,1)S(1)}, f32[3,1024]{1,0:T(4,128)S(1)}) custom-call(f32[256,1024]{1,0:T(8,128)S(1)} %get-tuple-element.69.pre_ref, f32[256,1024]{1,0:T(8,128)S(1)} %get-tuple-element.70.reach_ref, f32[256,1024]{1,0:T(8,128)S(1)} %get-tuple-element.71.sx_ref, bf16[256,256]{1,0:T(8,128)(2,1)S(1)} %bitcast.28, ...), custom_call_target="tpu_custom_call" | custom-call | flops 67108864 | bytes 5242880 | tf_op jit(solution)/shard_map/final/pallas_call | solution.py:737
  49.5 0.2 collective-permute-start.12
  49.7 1.4 %collective-permute-start.11 = (f32[3,1024]{1,0:T(4,128)S(1)}, f32[3,1024]{1,0:T(4,128)S(1)}, u32[]{:S(2)}, u32[]{:S(2)}) collective-permute-start(f32[3,1024]{1,0:T(4,128)S(1)} %get-tuple-element.75), channel_id=1, source_target_pairs={{0,16},{4,20},{8,24},{12,28},{16,0},{20,4},{24,8},{28,12},{1,17},{... | collective-permute-start | bytes 36872 | tf_op jit(solution)/shard_map/ppermute | solution.py:552
  51.2 2.8 %collective-permute-start.10 = (f32[3,1024]{1,0:T(4,128)S(1)}, f32[3,1024]{1,0:T(4,128)S(1)}, u32[]{:S(2)}, u32[]{:S(2)}) collective-permute-start(f32[3,1024]{1,0:T(4,128)S(1)} %get-tuple-element.75), channel_id=1, source_target_pairs={{0,8},{4,12},{8,0},{12,4},{16,24},{20,28},{24,16},{28,20},{1,9},{5... | collective-permute-start | bytes 36872 | tf_op jit(solution)/shard_map/ppermute | solution.py:552
  54.0 1.2 %collective-permute-done.12 = f32[3,1024]{1,0:T(4,128)S(1)} collective-permute-done((f32[3,1024]{1,0:T(4,128)S(1)}, f32[3,1024]{1,0:T(4,128)S(1)}, u32[]{:S(2)}, u32[]{:S(2)}) %collective-permute-start.12) | collective-permute-done | bytes 12320 | tf_op jit(solution)/shard_map/ppermute | solution.py:552
  55.2 0.0 collective-permute-done.11
  55.2 0.6 %collective-permute-done.10 = f32[3,1024]{1,0:T(4,128)S(1)} collective-permute-done((f32[3,1024]{1,0:T(4,128)S(1)}, f32[3,1024]{1,0:T(4,128)S(1)}, u32[]{:S(2)}, u32[]{:S(2)}) %collective-permute-start.10) | collective-permute-done | bytes 12320 | tf_op jit(solution)/shard_map/ppermute | solution.py:552
  55.8 0.8 %collective-permute-start.13 = (f32[3,1024]{1,0:T(4,128)S(1)}, f32[3,1024]{1,0:T(4,128)S(1)}, u32[]{:S(2)}, u32[]{:S(2)}) collective-permute-start(f32[3,1024]{1,0:T(4,128)S(1)} %add_add_fusion.a_ref), channel_id=1, source_target_pairs={{0,4},{4,0},{8,12},{12,8},{16,20},{20,16},{24,28},{28,24},{1,5},{5... | collective-permute-start | bytes 36872 | tf_op jit(solution)/shard_map/ppermute | solution.py:552
  56.6 1.0 %writing.2 = bf16[256,2048]{1,0:T(8,128)(2,1)} custom-call(bf16[256,1024]{1,0:T(8,128)(2,1)S(1)} %attention.2.refs_0_.teacher_ref, bf16[256,1024]{1,0:T(8,128)(2,1)S(1)} %attention.3.refs_1_.teacher_ref), custom_call_target="tpu_custom_call" | custom-call | bytes 2097152 | tf_op jit(solution)/shard_map/writing/pallas_call | solution.py:588
  57.6 1.0 %writing.3 = bf16[256,2048]{1,0:T(8,128)(2,1)} custom-call(bf16[256,1024]{1,0:T(8,128)(2,1)S(1)} %get-tuple-element.68.refs_0_, bf16[256,1024]{1,0:T(8,128)(2,1)S(1)} %get-tuple-element.74.refs_1_), custom_call_target="tpu_custom_call" | custom-call | bytes 2097152 | tf_op jit(solution)/shard_map/writing/pallas_call | solution.py:588
  58.6 1.0 %collective-permute-done.13.b_ref = f32[3,1024]{1,0:T(4,128)S(1)} collective-permute-done((f32[3,1024]{1,0:T(4,128)S(1)}, f32[3,1024]{1,0:T(4,128)S(1)}, u32[]{:S(2)}, u32[]{:S(2)}) %collective-permute-start.13) | collective-permute-done | bytes 12320 | tf_op jit(solution)/shard_map/ppermute | solution.py:552
  59.6 0.6 %closing.1 = (f32[1,2048]{1,0:T(1,128)}, f32[1,32]{1,0:T(1,128)}) custom-call(f32[3,1024]{1,0:T(4,128)S(1)} %add_add_fusion.a_ref, f32[3,1024]{1,0:T(4,128)S(1)} %collective-permute-done.13.b_ref), custom_call_target="tpu_custom_call" | custom-call | tf_op jit(solution)/shard_map/closing/pallas_call | solution.py:775
  (7 shorter events, 0.1 us)
Async XLA Ops:
  3.9 12.8 %collective-permute-start.3 = (bf16[272,512]{1,0:T(8,128)(2,1)S(1)}, bf16[272,512]{1,0:T(8,128)(2,1)S(1)}, u32[]{:S(2)}, u32[]{:S(2)}) collective-permute-start(bf16[272,512]{1,0:T(8,128)(2,1)S(1)} %get-tuple-element.45), channel_id=1, source_target_pairs={{4,8},{8,4},{5,9},{9,5},{6,10},{10,6},{7,11},{11,7},{20,24},{24,20... | collective-permute-start | bytes 835592 | tf_op jit(solution)/shard_map/ppermute | solution.py:668
  4.6 13.1 %collective-permute-start.1 = (bf16[272,512]{1,0:T(8,128)(2,1)S(1)}, bf16[272,512]{1,0:T(8,128)(2,1)S(1)}, u32[]{:S(2)}, u32[]{:S(2)}) collective-permute-start(bf16[272,512]{1,0:T(8,128)(2,1)S(1)} %get-tuple-element.45), channel_id=1, source_target_pairs={{0,4},{12,8},{4,0},{8,12},{1,5},{13,9},{5,1},{9,13},{2,6},{14,10},... | collective-permute-start | bytes 835592 | tf_op jit(solution)/shard_map/ppermute | solution.py:667
  10.5 12.7 %collective-permute-start = (bf16[128,1024]{1,0:T(8,128)(2,1)S(1)}, bf16[128,1024]{1,0:T(8,128)(2,1)S(1)}, u32[]{:S(2)}, u32[]{:S(2)}) collective-permute-start(bf16[128,1024]{1,0:T(8,128)(2,1)S(1)} %get-tuple-element.41), channel_id=1, source_target_pairs={{0,4},{12,8},{1,5},{13,9},{2,6},{14,10},{3,7},{15,11},{16,20},{28,... | collective-permute-start | bytes 786440 | tf_op jit(solution)/shard_map/ppermute | solution.py:683
  16.7 11.4 %collective-permute-start.6 = (bf16[144,1024]{1,0:T(8,128)(2,1)S(1)}, bf16[144,1024]{1,0:T(8,128)(2,1)S(1)}, u32[]{:S(2)}, u32[]{:S(2)}) collective-permute-start(bf16[144,1024]{1,0:T(8,128)(2,1)S(1)} %merge.1), channel_id=1, source_target_pairs={{0,4},{12,8},{4,0},{8,12},{1,5},{13,9},{5,1},{9,13},{2,6},{14,10},... | collective-permute-start | bytes 884744 | tf_op jit(solution)/shard_map/ppermute | solution.py:680
  17.6 6.3 %collective-permute-start.4 = (bf16[272,512]{1,0:T(8,128)(2,1)S(1)}, bf16[272,512]{1,0:T(8,128)(2,1)S(1)}, u32[]{:S(2)}, u32[]{:S(2)}) collective-permute-start(bf16[272,512]{1,0:T(8,128)(2,1)S(1)} %collective-permute-done.1.refs_0_.refs_3_), channel_id=1, source_target_pairs={{4,8},{8,4},{5,9},{9,5},{6,10},{10,6},{7,11},{11,7},{20,24},{24,20... | collective-permute-start | bytes 835592 | tf_op jit(solution)/shard_map/ppermute | solution.py:670
  23.3 5.7 %collective-permute-start.2 = (bf16[128,1024]{1,0:T(8,128)(2,1)S(1)}, bf16[128,1024]{1,0:T(8,128)(2,1)S(1)}, u32[]{:S(2)}, u32[]{:S(2)}) collective-permute-start(bf16[128,1024]{1,0:T(8,128)(2,1)S(1)} %chain.4), channel_id=1, source_target_pairs={{4,8},{8,4},{5,9},{9,5},{6,10},{10,6},{7,11},{11,7},{20,24},{24,20... | collective-permute-start | bytes 786440 | tf_op jit(solution)/shard_map/ppermute | solution.py:686
  23.9 12.4 %collective-permute-start.8 = (bf16[272,512]{1,0:T(8,128)(2,1)S(1)}, bf16[272,512]{1,0:T(8,128)(2,1)S(1)}, u32[]{:S(2)}, u32[]{:S(2)}) collective-permute-start(bf16[272,512]{1,0:T(8,128)(2,1)S(1)} %collective-permute-done.4.refs_1_.refs_2_.refs_5_), channel_id=1, source_target_pairs={{4,0},{8,12},{5,1},{9,13},{6,2},{10,14},{7,3},{11,15},{20,16},{24,... | collective-permute-start | bytes 835592 | tf_op jit(solution)/shard_map/ppermute | solution.py:687
  28.1 8.3 %copy-start = (bf16[1,256,2048]{2,1,0:T(8,128)(2,1)S(1)}, bf16[1,256,2048]{2,1,0:T(8,128)(2,1)}, u32[]{:S(2)}) copy-start(bf16[1,256,2048]{2,1,0:T(8,128)(2,1)} %param.13) | copy-start | bytes 3145732
  28.1 8.3 %copy-start.1 = (bf16[1,256,256]{2,1,0:T(8,128)(2,1)S(1)}, bf16[1,256,256]{2,1,0:T(8,128)(2,1)}, u32[]{:S(2)}) copy-start(bf16[1,256,256]{2,1,0:T(8,128)(2,1)} %param.14) | copy-start | bytes 393220
  28.1 8.3 %copy-start.2 = (bf16[1,256,256]{2,1,0:T(8,128)(2,1)S(1)}, bf16[1,256,256]{2,1,0:T(8,128)(2,1)}, u32[]{:S(2)}) copy-start(bf16[1,256,256]{2,1,0:T(8,128)(2,1)} %param.15) | copy-start | bytes 393220
  28.1 11.1 %collective-permute-start.7 = (bf16[128,1024]{1,0:T(8,128)(2,1)S(1)}, bf16[128,1024]{1,0:T(8,128)(2,1)S(1)}, u32[]{:S(2)}, u32[]{:S(2)}) collective-permute-start(bf16[128,1024]{1,0:T(8,128)(2,1)S(1)} %chain.6), channel_id=1, source_target_pairs={{4,8},{8,4},{5,9},{9,5},{6,10},{10,6},{7,11},{11,7},{20,24},{24,20... | collective-permute-start | bytes 786440 | tf_op jit(solution)/shard_map/ppermute | solution.py:731
  28.9 7.5 %copy-start.4 = (s32[1,1024]{1,0:T(1,128)S(1)}, s32[1,1024]{1,0:T(1,128)}, u32[]{:S(2)}) copy-start(s32[1,1024]{1,0:T(1,128)} %docs_ref.7) | copy-start | bytes 12292
  29.0 14.5 %collective-permute-start.5 = (bf16[128,1024]{1,0:T(8,128)(2,1)S(1)}, bf16[128,1024]{1,0:T(8,128)(2,1)S(1)}, u32[]{:S(2)}, u32[]{:S(2)}) collective-permute-start(bf16[128,1024]{1,0:T(8,128)(2,1)S(1)} %chain.5), channel_id=1, source_target_pairs={{8,12},{4,0},{9,13},{5,1},{10,14},{6,2},{11,15},{7,3},{24,28},{20,... | collective-permute-start | bytes 786440 | tf_op jit(solution)/shard_map/ppermute | solution.py:731
  39.2 4.3 %copy-start.3 = (bf16[1,256,256]{2,1,0:T(8,128)(2,1)S(1)}, bf16[1,256,256]{2,1,0:T(8,128)(2,1)}, u32[]{:S(2)}) copy-start(bf16[1,256,256]{2,1,0:T(8,128)(2,1)} %param.20) | copy-start | bytes 393220
  39.3 4.3 %copy-start.5 = (f32[2048]{0:T(1024)S(1)}, f32[2048]{0:T(1024)}, u32[]{:S(2)}) copy-start(f32[2048]{0:T(1024)} %param.25) | copy-start | bytes 24580
  39.3 8.4 %collective-permute-start.9 = (bf16[128,1024]{1,0:T(8,128)(2,1)S(1)}, bf16[128,1024]{1,0:T(8,128)(2,1)S(1)}, u32[]{:S(2)}, u32[]{:S(2)}) collective-permute-start(bf16[128,1024]{1,0:T(8,128)(2,1)S(1)} %chain.7), channel_id=1, source_target_pairs={{8,12},{4,0},{9,13},{5,1},{10,14},{6,2},{11,15},{7,3},{24,28},{20,... | collective-permute-start | bytes 786440 | tf_op jit(solution)/shard_map/ppermute | solution.py:731
  49.5 5.6 %collective-permute-start.12 = (f32[3,1024]{1,0:T(4,128)S(1)}, f32[3,1024]{1,0:T(4,128)S(1)}, u32[]{:S(2)}, u32[]{:S(2)}) collective-permute-start(f32[3,1024]{1,0:T(4,128)S(1)} %get-tuple-element.75), channel_id=1, source_target_pairs={{0,24},{4,28},{8,16},{12,20},{16,8},{20,12},{24,0},{28,4},{1,25},{... | collective-permute-start | bytes 36872 | tf_op jit(solution)/shard_map/ppermute | solution.py:552
  49.7 5.4 %collective-permute-start.11 = (f32[3,1024]{1,0:T(4,128)S(1)}, f32[3,1024]{1,0:T(4,128)S(1)}, u32[]{:S(2)}, u32[]{:S(2)}) collective-permute-start(f32[3,1024]{1,0:T(4,128)S(1)} %get-tuple-element.75), channel_id=1, source_target_pairs={{0,16},{4,20},{8,24},{12,28},{16,0},{20,4},{24,8},{28,12},{1,17},{... | collective-permute-start | bytes 36872 | tf_op jit(solution)/shard_map/ppermute | solution.py:552
  51.2 4.6 %collective-permute-start.10 = (f32[3,1024]{1,0:T(4,128)S(1)}, f32[3,1024]{1,0:T(4,128)S(1)}, u32[]{:S(2)}, u32[]{:S(2)}) collective-permute-start(f32[3,1024]{1,0:T(4,128)S(1)} %get-tuple-element.75), channel_id=1, source_target_pairs={{0,8},{4,12},{8,0},{12,4},{16,24},{20,28},{24,16},{28,20},{1,9},{5... | collective-permute-start | bytes 36872 | tf_op jit(solution)/shard_map/ppermute | solution.py:552
  55.8 3.8 %collective-permute-start.13 = (f32[3,1024]{1,0:T(4,128)S(1)}, f32[3,1024]{1,0:T(4,128)S(1)}, u32[]{:S(2)}, u32[]{:S(2)}) collective-permute-start(f32[3,1024]{1,0:T(4,128)S(1)} %add_add_fusion.a_ref), channel_id=1, source_target_pairs={{0,4},{4,0},{8,12},{12,8},{16,20},{20,16},{24,28},{28,24},{1,5},{5... | collective-permute-start | bytes 36872 | tf_op jit(solution)/shard_map/ppermute | solution.py:552

commit v16 on v15

--- a/solution.py
+++ b/solution.py
@@ -455,14 +455,21 @@
         def _():
             back[...] = got[r - 1][:N, :]
 
+    sources, rows_in = [], []
+    for source, places in arrivals(index, count, kv_refs):
+        found = [ref[ref.shape[0] - EXTRA :, :heads].astype(F32) for _, ref in places]
+        if len(found) == 2:
+            found = [jnp.where(places[0][0], found[0], found[1])]
+        sources.append(source)
+        rows_in.append(found[0])
+    spread_rows = spread_matrix(heads, width, g * (width // P_SIZE))
+    wide = jnp.dot(
+        jnp.concatenate(rows_in, axis=0).astype(BF16), spread_rows, preferred_element_type=F32
+    )
     d_in = jnp.ones((1, width), F32)
-    for source, places in arrivals(index, count, kv_refs):
-        for condition, ref in places:
-            used = source > index
-            if condition is not None:
-                used = used & condition
-            one = passed_decay(ref, ref.shape[0] - EXTRA, heads, width, g)
-            d_in = d_in * jnp.where(used, one, 1.0)
+    for r, source in enumerate(sources):
+        one = wide[r * EXTRA : r * EXTRA + 1] + wide[r * EXTRA + 1 : r * EXTRA + 2]
+        d_in = d_in * jnp.where(source > index, one, 1.0)
     through = dec_ref[0:1, :] * front[...].astype(F32) + f_ref[...].astype(F32)
     entering = (d_in * through + back[...].astype(F32)).astype(BF16)
     flow[:stretch, :] = jnp.dot(c_ref[:stretch, proj], front[...], preferred_element_type=F32)
@@ -764,7 +771,7 @@
         )
         normed.append(made)
     teacher, student = write(*targets), write(*normed)
-    shifts = [1 << k for k in reversed(range(count.bit_length() - 1))]
+    shifts = [1 << k for k in range(count.bit_length() - 1)]
     partner = exchange(grads, shifts[0])
     if lax.axis_size("dp") == 2:
         grads = (grads + partner) + (exchange(grads, count) + exchange(grads, count + shifts[0]))

time: 60.6 us -> 60.9 us (level)
  waiting for transfers between devices: 19.3 us -> 20.9 us
  starting transfers between devices: 20.6 us -> 19.3 us
    ppermute x4, waiting for transfers between devices: 2.86 us -> 4.43 us  [exchange(): return lax.ppermute(part, axes, [(d, d ^ shift) for d in range(size)])]
    ppermute x4, starting transfers between devices: 5.24 us -> 3.97 us  [exchange(): return lax.ppermute(part, axes, [(d, d ^ shift) for d in range(size)])]
  transfers between devices with their start and end apart: 14 -> 14, of which waited for: 8 -> 9; matrix products, arithmetic and copies ran while one was open for 0% -> 0% of each run, Pallas kernels for 23% -> 23%
where the time goes in v16:
time: 60.9 us; the launch traced here: 60.5 us
  waiting for transfers between devices  20.9 us (34%)
  Pallas kernels  19.4 us (32%)
  starting transfers between devices  19.3 us (32%)
  between operations  0.87 us (1%)
    ppermute x1, waiting for transfers between devices, body(): farther = lax.ppermute(beyond, 'ctx', outward)  6.1 us
    ppermute x1, starting transfers between devices, body(): near = lax.ppermute(kv, 'ctx', inward + outward)  5.97 us
    pallas_call x2, Pallas kernels, body(): pl.pallas_call(functools.partial(attention_kernel, count, per_kv, stack,...  5.58 us
    ppermute x1, waiting for transfers between devices, body(): got[0].append(lax.ppermute(send[0], 'ctx', [(0, 1), (3, 2)]))  4.94 us
    ppermute x4, waiting for transfers between devices, exchange(): return lax.ppermute(part, axes, [(d, d ^ shift) for d in range(size)])  4.43 us
    pallas_call x1, Pallas kernels, body(): pl.pallas_call(functools.partial(local_kernel, count, groups), out_shape=...  4.19 us
    ppermute x4, starting transfers between devices, exchange(): return lax.ppermute(part, axes, [(d, d ^ shift) for d in range(size)])  3.97 us
    pallas_call x2, Pallas kernels, body(): pl.pallas_call(functools.partial(final_kernel, count, g, groups, loss_sca...  3.72 us
  transfers between devices with their start and end apart: 14, of which 9 were waited for; matrix products, arithmetic and copies ran while one was open for 0% of the time, Pallas kernels for 23%

profile of v16, /device:TPU:0, one launch (start us, length us, event | category | flops | bytes accessed | tf_op | source)
XLA Modules:
  0.0 60.5 jit_solution(17659304002833516336)
XLA Ops:
  0.6 3.2 %opening.1 = (bf16[272,512]{1,0:T(8,128)(2,1)S(1)}, f32[32,256]{1,0:T(8,128)S(1)}, bf16[256,1024]{1,0:T(8,128)(2,1)S(1)}, bf16[256,1024]{1,0:T(8,128)(2,1)S(1)},...) custom-call(s32[1,1024]{1,0:T(1,128)} %docs_ref.7, ...), custom_call_target="tpu_custom_call" | custom-call | flops 268435456 | bytes 4194304 | tf_op jit(solution)/shard_map/opening/pallas_call | solution.py:608
  3.9 0.7 %collective-permute-start.3 = (bf16[272,512]{1,0:T(8,128)(2,1)S(1)}, bf16[272,512]{1,0:T(8,128)(2,1)S(1)}, u32[]{:S(2)}, u32[]{:S(2)}) collective-permute-start(bf16[272,512]{1,0:T(8,128)(2,1)S(1)} %get-tuple-element.45), channel_id=1, source_target_pairs={{4,8},{8,4},{5,9},{9,5},{6,10},{10,6},{7,11},{11,7},{20,24},{24,20... | collective-permute-start | bytes 835592 | tf_op jit(solution)/shard_map/ppermute | solution.py:675
  4.6 6.0 %collective-permute-start.1 = (bf16[272,512]{1,0:T(8,128)(2,1)S(1)}, bf16[272,512]{1,0:T(8,128)(2,1)S(1)}, u32[]{:S(2)}, u32[]{:S(2)}) collective-permute-start(bf16[272,512]{1,0:T(8,128)(2,1)S(1)} %get-tuple-element.45), channel_id=1, source_target_pairs={{0,4},{12,8},{4,0},{8,12},{1,5},{13,9},{5,1},{9,13},{2,6},{14,10},... | collective-permute-start | bytes 835592 | tf_op jit(solution)/shard_map/ppermute | solution.py:674
  10.5 1.9 %collective-permute-start = (bf16[128,1024]{1,0:T(8,128)(2,1)S(1)}, bf16[128,1024]{1,0:T(8,128)(2,1)S(1)}, u32[]{:S(2)}, u32[]{:S(2)}) collective-permute-start(bf16[128,1024]{1,0:T(8,128)(2,1)S(1)} %get-tuple-element.41), channel_id=1, source_target_pairs={{0,4},{12,8},{1,5},{13,9},{2,6},{14,10},{3,7},{15,11},{16,20},{28,... | collective-permute-start | bytes 786440 | tf_op jit(solution)/shard_map/ppermute | solution.py:690
  12.5 4.2 %local.1 = (f32[256,1024]{1,0:T(8,128)S(1)}, f32[256,1024]{1,0:T(8,128)S(1)}, f32[256,1024]{1,0:T(8,128)S(1)}, f32[256,1024]{1,0:T(8,128)S(1)}, f32[256,1024]{1,0:T(8,128)S(1)}, /*index=5*/f32[256,1024]{1,0:T(8,128)S(1)}) custom-call(s32[1,1024]{1,0:T(1,128)} %docs_ref.7, bf16[256,2048]{1,0:T(8,128)(2,1)} %bitcast.32, bf16[256,2048]{1,0:T(8,128)(2,1)} %bitcast.33, ...), custom_call_target="tpu_custom_call" | custom-call | flops 134217728 | bytes 8388608 | tf_op jit(solution)/shard_map/local/pallas_call | solution.py:640
  16.7 0.0 collective-permute-done.3.refs_0_.kv_ref.refs_1_.refs_4_
  16.7 0.6 %collective-permute-start.6 = (bf16[144,1024]{1,0:T(8,128)(2,1)S(1)}, bf16[144,1024]{1,0:T(8,128)(2,1)S(1)}, u32[]{:S(2)}, u32[]{:S(2)}) collective-permute-start(bf16[144,1024]{1,0:T(8,128)(2,1)S(1)} %merge.1), channel_id=1, source_target_pairs={{0,4},{12,8},{4,0},{8,12},{1,5},{13,9},{5,1},{9,13},{2,6},{14,10},... | collective-permute-start | bytes 884744 | tf_op jit(solution)/shard_map/ppermute | solution.py:687
  17.4 0.3 collective-permute-done.1.refs_0_.refs_3_
  17.6 0.7 %collective-permute-start.4 = (bf16[272,512]{1,0:T(8,128)(2,1)S(1)}, bf16[272,512]{1,0:T(8,128)(2,1)S(1)}, u32[]{:S(2)}, u32[]{:S(2)}) collective-permute-start(bf16[272,512]{1,0:T(8,128)(2,1)S(1)} %collective-permute-done.1.refs_0_.refs_3_), channel_id=1, source_target_pairs={{4,8},{8,4},{5,9},{9,5},{6,10},{10,6},{7,11},{11,7},{20,24},{24,20... | collective-permute-start | bytes 835592 | tf_op jit(solution)/shard_map/ppermute | solution.py:677
  18.3 4.9 %collective-permute-done.got_ref.refs_0_ = bf16[128,1024]{1,0:T(8,128)(2,1)S(1)} collective-permute-done((bf16[128,1024]{1,0:T(8,128)(2,1)S(1)}, bf16[128,1024]{1,0:T(8,128)(2,1)S(1)}, u32[]{:S(2)}, u32[]{:S(2)}) %collective-permute-start) | collective-permute-done | bytes 262176 | tf_op jit(solution)/shard_map/ppermute | solution.py:690
  23.3 0.7 %collective-permute-start.2 = (bf16[128,1024]{1,0:T(8,128)(2,1)S(1)}, bf16[128,1024]{1,0:T(8,128)(2,1)S(1)}, u32[]{:S(2)}, u32[]{:S(2)}) collective-permute-start(bf16[128,1024]{1,0:T(8,128)(2,1)S(1)} %chain.4), channel_id=1, source_target_pairs={{4,8},{8,4},{5,9},{9,5},{6,10},{10,6},{7,11},{11,7},{20,24},{24,20... | collective-permute-start | bytes 786440 | tf_op jit(solution)/shard_map/ppermute | solution.py:693
  23.9 0.0 collective-permute-done.4.refs_1_.refs_2_.refs_5_
  23.9 1.3 %collective-permute-start.8 = (bf16[272,512]{1,0:T(8,128)(2,1)S(1)}, bf16[272,512]{1,0:T(8,128)(2,1)S(1)}, u32[]{:S(2)}, u32[]{:S(2)}) collective-permute-start(bf16[272,512]{1,0:T(8,128)(2,1)S(1)} %collective-permute-done.4.refs_1_.refs_2_.refs_5_), channel_id=1, source_target_pairs={{4,0},{8,12},{5,1},{9,13},{6,2},{10,14},{7,3},{11,15},{20,16},{24,... | collective-permute-start | bytes 835592 | tf_op jit(solution)/shard_map/ppermute | solution.py:694
  25.2 2.9 %collective-permute-done.6.got_ref.refs_3_.refs_6_.refs_0_ = bf16[144,1024]{1,0:T(8,128)(2,1)S(1)} collective-permute-done((bf16[144,1024]{1,0:T(8,128)(2,1)S(1)}, bf16[144,1024]{1,0:T(8,128)(2,1)S(1)}, u32[]{:S(2)}, u32[]{:S(2)}) %collective-permute-start.6) | collective-permute-done | bytes 294944 | tf_op jit(solution)/shard_map/ppermute | solution.py:687
  28.1 0.0 copy-start
  28.1 0.0 copy-start.1
  28.1 0.8 %collective-permute-start.7 = (bf16[128,1024]{1,0:T(8,128)(2,1)S(1)}, bf16[128,1024]{1,0:T(8,128)(2,1)S(1)}, u32[]{:S(2)}, u32[]{:S(2)}) collective-permute-start(bf16[128,1024]{1,0:T(8,128)(2,1)S(1)} %chain.6), channel_id=1, source_target_pairs={{4,8},{8,4},{5,9},{9,5},{6,10},{10,6},{7,11},{11,7},{20,24},{24,20... | collective-permute-start | bytes 786440 | tf_op jit(solution)/shard_map/ppermute | solution.py:738
  28.9 0.0 collective-permute-done.2.got_ref.refs_1_
  28.9 0.0 copy-start.4
  29.0 1.3 %collective-permute-start.5 = (bf16[128,1024]{1,0:T(8,128)(2,1)S(1)}, bf16[128,1024]{1,0:T(8,128)(2,1)S(1)}, u32[]{:S(2)}, u32[]{:S(2)}) collective-permute-start(bf16[128,1024]{1,0:T(8,128)(2,1)S(1)} %chain.5), channel_id=1, source_target_pairs={{8,12},{4,0},{9,13},{5,1},{10,14},{6,2},{11,15},{7,3},{24,28},{20,... | collective-permute-start | bytes 786440 | tf_op jit(solution)/shard_map/ppermute | solution.py:738
  30.3 6.1 %collective-permute-done.8.refs_4_.refs_7_ = bf16[272,512]{1,0:T(8,128)(2,1)S(1)} collective-permute-done((bf16[272,512]{1,0:T(8,128)(2,1)S(1)}, bf16[272,512]{1,0:T(8,128)(2,1)S(1)}, u32[]{:S(2)}, u32[]{:S(2)}) %collective-permute-start.8) | collective-permute-done | bytes 278560 | tf_op jit(solution)/shard_map/ppermute | solution.py:694
  36.4 0.0 copy-done
  36.4 0.0 copy-done.1
  36.4 0.0 copy-done.2
  36.4 0.0 copy-done.4
  36.4 2.8 %attention.2.refs_0_.teacher_ref = bf16[256,1024]{1,0:T(8,128)(2,1)S(1)} custom-call(s32[1,1024]{1,0:T(1,128)S(1)} %copy-done.4, bf16[256,2048]{1,0:T(8,128)(2,1)S(1)} %bitcast.18, bf16[256,256]{1,0:T(8,128)(2,1)S(1)} %bitcast.21, bf16[256,256]{1,0:T(8,128)(2,1)S(1)} %bitcast.24, bf16[272,512]{1,0:T(8,128)(2,1)S(1)} %collective-permute-done.1.refs_0_.refs_3_, ...), custom_call_target="tpu_custom_call" | custom-call | flops 603979776 | bytes 2097152 | tf_op jit(solution)/shard_map/attention/pallas_call | solution.py:705
  39.2 0.0 collective-permute-done.7.got_ref.refs_1_
  39.2 0.0 copy-start.3
  39.3 0.0 copy-start.5
  39.3 1.4 %collective-permute-start.9 = (bf16[128,1024]{1,0:T(8,128)(2,1)S(1)}, bf16[128,1024]{1,0:T(8,128)(2,1)S(1)}, u32[]{:S(2)}, u32[]{:S(2)}) collective-permute-start(bf16[128,1024]{1,0:T(8,128)(2,1)S(1)} %chain.7), channel_id=1, source_target_pairs={{8,12},{4,0},{9,13},{5,1},{10,14},{6,2},{11,15},{7,3},{24,28},{20,... | collective-permute-start | bytes 786440 | tf_op jit(solution)/shard_map/ppermute | solution.py:738
  40.7 2.8 %attention.3.refs_1_.teacher_ref = bf16[256,1024]{1,0:T(8,128)(2,1)S(1)} custom-call(s32[1,1024]{1,0:T(1,128)S(1)} %copy-done.4, bf16[256,2048]{1,0:T(8,128)(2,1)S(1)} %bitcast.19, bf16[256,256]{1,0:T(8,128)(2,1)S(1)} %bitcast.22, bf16[256,256]{1,0:T(8,128)(2,1)S(1)} %bitcast.25, bf16[272,512]{1,0:T(8,128)(2,1)S(1)} %collective-permute-done.1.refs_0_.refs_3_, ...), custom_call_target="tpu_custom_call" | custom-call | flops 603979776 | bytes 2097152 | tf_op jit(solution)/shard_map/attention/pallas_call | solution.py:705
  43.5 0.0 collective-permute-done.5.refs_2_
  43.5 0.0 copy-done.3
  43.5 0.0 copy-done.5
  43.5 1.9 %final.2 = (bf16[256,1024]{1,0:T(8,128)(2,1)S(1)}, f32[3,1024]{1,0:T(4,128)S(1)}) custom-call(f32[256,1024]{1,0:T(8,128)S(1)} %get-tuple-element.64.pre_ref, f32[256,1024]{1,0:T(8,128)S(1)} %get-tuple-element.65.reach_ref, f32[256,1024]{1,0:T(8,128)S(1)} %get-tuple-element.66.sx_ref, bf16[256,256]{1,0:T(8,128)(2,1)S(1)} %bitcast.27, ...), custom_call_target="tpu_custom_call" | custom-call | flops 67108864 | bytes 5242880 | tf_op jit(solution)/shard_map/final/pallas_call | solution.py:744
  45.4 2.3 %collective-permute-done.9.refs_2_ = bf16[128,1024]{1,0:T(8,128)(2,1)S(1)} collective-permute-done((bf16[128,1024]{1,0:T(8,128)(2,1)S(1)}, bf16[128,1024]{1,0:T(8,128)(2,1)S(1)}, u32[]{:S(2)}, u32[]{:S(2)}) %collective-permute-start.9) | collective-permute-done | bytes 262176 | tf_op jit(solution)/shard_map/ppermute | solution.py:738
  47.7 1.9 %final.3 = (bf16[256,1024]{1,0:T(8,128)(2,1)S(1)}, f32[3,1024]{1,0:T(4,128)S(1)}) custom-call(f32[256,1024]{1,0:T(8,128)S(1)} %get-tuple-element.69.pre_ref, f32[256,1024]{1,0:T(8,128)S(1)} %get-tuple-element.70.reach_ref, f32[256,1024]{1,0:T(8,128)S(1)} %get-tuple-element.71.sx_ref, bf16[256,256]{1,0:T(8,128)(2,1)S(1)} %bitcast.28, ...), custom_call_target="tpu_custom_call" | custom-call | flops 67108864 | bytes 5242880 | tf_op jit(solution)/shard_map/final/pallas_call | solution.py:744
  49.5 1.4 %collective-permute-start.12 = (f32[3,1024]{1,0:T(4,128)S(1)}, f32[3,1024]{1,0:T(4,128)S(1)}, u32[]{:S(2)}, u32[]{:S(2)}) collective-permute-start(f32[3,1024]{1,0:T(4,128)S(1)} %get-tuple-element.75), channel_id=1, source_target_pairs={{0,20},{4,16},{8,28},{12,24},{16,4},{20,0},{24,12},{28,8},{1,21},{... | collective-permute-start | bytes 36872 | tf_op jit(solution)/shard_map/ppermute | solution.py:559
  50.9 0.5 collective-permute-start.11
  51.5 1.6 %collective-permute-start.10 = (f32[3,1024]{1,0:T(4,128)S(1)}, f32[3,1024]{1,0:T(4,128)S(1)}, u32[]{:S(2)}, u32[]{:S(2)}) collective-permute-start(f32[3,1024]{1,0:T(4,128)S(1)} %get-tuple-element.75), channel_id=1, source_target_pairs={{0,4},{4,0},{8,12},{12,8},{16,20},{20,16},{24,28},{28,24},{1,5},{5... | collective-permute-start | bytes 36872 | tf_op jit(solution)/shard_map/ppermute | solution.py:559
  53.1 1.1 %collective-permute-done.12 = f32[3,1024]{1,0:T(4,128)S(1)} collective-permute-done((f32[3,1024]{1,0:T(4,128)S(1)}, f32[3,1024]{1,0:T(4,128)S(1)}, u32[]{:S(2)}, u32[]{:S(2)}) %collective-permute-start.12) | collective-permute-done | bytes 12320 | tf_op jit(solution)/shard_map/ppermute | solution.py:559
  54.2 0.4 collective-permute-done.11
  54.7 0.5 collective-permute-done.10
  55.2 0.4 collective-permute-start.13
  55.6 1.0 %writing.2 = bf16[256,2048]{1,0:T(8,128)(2,1)} custom-call(bf16[256,1024]{1,0:T(8,128)(2,1)S(1)} %attention.2.refs_0_.teacher_ref, bf16[256,1024]{1,0:T(8,128)(2,1)S(1)} %attention.3.refs_1_.teacher_ref), custom_call_target="tpu_custom_call" | custom-call | bytes 2097152 | tf_op jit(solution)/shard_map/writing/pallas_call | solution.py:595
  56.6 1.0 %writing.3 = bf16[256,2048]{1,0:T(8,128)(2,1)} custom-call(bf16[256,1024]{1,0:T(8,128)(2,1)S(1)} %get-tuple-element.68.refs_0_, bf16[256,1024]{1,0:T(8,128)(2,1)S(1)} %get-tuple-element.74.refs_1_), custom_call_target="tpu_custom_call" | custom-call | bytes 2097152 | tf_op jit(solution)/shard_map/writing/pallas_call | solution.py:595
  57.6 2.3 %collective-permute-done.13.b_ref = f32[3,1024]{1,0:T(4,128)S(1)} collective-permute-done((f32[3,1024]{1,0:T(4,128)S(1)}, f32[3,1024]{1,0:T(4,128)S(1)}, u32[]{:S(2)}, u32[]{:S(2)}) %collective-permute-start.13) | collective-permute-done | bytes 12320 | tf_op jit(solution)/shard_map/ppermute | solution.py:559
  59.9 0.6 %closing.1 = (f32[1,2048]{1,0:T(1,128)}, f32[1,32]{1,0:T(1,128)}) custom-call(f32[3,1024]{1,0:T(4,128)S(1)} %add_add_fusion.a_ref, f32[3,1024]{1,0:T(4,128)S(1)} %collective-permute-done.13.b_ref), custom_call_target="tpu_custom_call" | custom-call | tf_op jit(solution)/shard_map/closing/pallas_call | solution.py:782
  (7 shorter events, 0.1 us)
Async XLA Ops:
  3.9 12.8 %collective-permute-start.3 = (bf16[272,512]{1,0:T(8,128)(2,1)S(1)}, bf16[272,512]{1,0:T(8,128)(2,1)S(1)}, u32[]{:S(2)}, u32[]{:S(2)}) collective-permute-start(bf16[272,512]{1,0:T(8,128)(2,1)S(1)} %get-tuple-element.45), channel_id=1, source_target_pairs={{4,8},{8,4},{5,9},{9,5},{6,10},{10,6},{7,11},{11,7},{20,24},{24,20... | collective-permute-start | bytes 835592 | tf_op jit(solution)/shard_map/ppermute | solution.py:675
  4.6 13.1 %collective-permute-start.1 = (bf16[272,512]{1,0:T(8,128)(2,1)S(1)}, bf16[272,512]{1,0:T(8,128)(2,1)S(1)}, u32[]{:S(2)}, u32[]{:S(2)}) collective-permute-start(bf16[272,512]{1,0:T(8,128)(2,1)S(1)} %get-tuple-element.45), channel_id=1, source_target_pairs={{0,4},{12,8},{4,0},{8,12},{1,5},{13,9},{5,1},{9,13},{2,6},{14,10},... | collective-permute-start | bytes 835592 | tf_op jit(solution)/shard_map/ppermute | solution.py:674
  10.5 12.7 %collective-permute-start = (bf16[128,1024]{1,0:T(8,128)(2,1)S(1)}, bf16[128,1024]{1,0:T(8,128)(2,1)S(1)}, u32[]{:S(2)}, u32[]{:S(2)}) collective-permute-start(bf16[128,1024]{1,0:T(8,128)(2,1)S(1)} %get-tuple-element.41), channel_id=1, source_target_pairs={{0,4},{12,8},{1,5},{13,9},{2,6},{14,10},{3,7},{15,11},{16,20},{28,... | collective-permute-start | bytes 786440 | tf_op jit(solution)/shard_map/ppermute | solution.py:690
  16.7 11.4 %collective-permute-start.6 = (bf16[144,1024]{1,0:T(8,128)(2,1)S(1)}, bf16[144,1024]{1,0:T(8,128)(2,1)S(1)}, u32[]{:S(2)}, u32[]{:S(2)}) collective-permute-start(bf16[144,1024]{1,0:T(8,128)(2,1)S(1)} %merge.1), channel_id=1, source_target_pairs={{0,4},{12,8},{4,0},{8,12},{1,5},{13,9},{5,1},{9,13},{2,6},{14,10},... | collective-permute-start | bytes 884744 | tf_op jit(solution)/shard_map/ppermute | solution.py:687
  17.6 6.3 %collective-permute-start.4 = (bf16[272,512]{1,0:T(8,128)(2,1)S(1)}, bf16[272,512]{1,0:T(8,128)(2,1)S(1)}, u32[]{:S(2)}, u32[]{:S(2)}) collective-permute-start(bf16[272,512]{1,0:T(8,128)(2,1)S(1)} %collective-permute-done.1.refs_0_.refs_3_), channel_id=1, source_target_pairs={{4,8},{8,4},{5,9},{9,5},{6,10},{10,6},{7,11},{11,7},{20,24},{24,20... | collective-permute-start | bytes 835592 | tf_op jit(solution)/shard_map/ppermute | solution.py:677
  23.3 5.7 %collective-permute-start.2 = (bf16[128,1024]{1,0:T(8,128)(2,1)S(1)}, bf16[128,1024]{1,0:T(8,128)(2,1)S(1)}, u32[]{:S(2)}, u32[]{:S(2)}) collective-permute-start(bf16[128,1024]{1,0:T(8,128)(2,1)S(1)} %chain.4), channel_id=1, source_target_pairs={{4,8},{8,4},{5,9},{9,5},{6,10},{10,6},{7,11},{11,7},{20,24},{24,20... | collective-permute-start | bytes 786440 | tf_op jit(solution)/shard_map/ppermute | solution.py:693
  23.9 12.4 %collective-permute-start.8 = (bf16[272,512]{1,0:T(8,128)(2,1)S(1)}, bf16[272,512]{1,0:T(8,128)(2,1)S(1)}, u32[]{:S(2)}, u32[]{:S(2)}) collective-permute-start(bf16[272,512]{1,0:T(8,128)(2,1)S(1)} %collective-permute-done.4.refs_1_.refs_2_.refs_5_), channel_id=1, source_target_pairs={{4,0},{8,12},{5,1},{9,13},{6,2},{10,14},{7,3},{11,15},{20,16},{24,... | collective-permute-start | bytes 835592 | tf_op jit(solution)/shard_map/ppermute | solution.py:694
  28.1 8.3 %copy-start = (bf16[1,256,2048]{2,1,0:T(8,128)(2,1)S(1)}, bf16[1,256,2048]{2,1,0:T(8,128)(2,1)}, u32[]{:S(2)}) copy-start(bf16[1,256,2048]{2,1,0:T(8,128)(2,1)} %param.13) | copy-start | bytes 3145732
  28.1 8.3 %copy-start.1 = (bf16[1,256,256]{2,1,0:T(8,128)(2,1)S(1)}, bf16[1,256,256]{2,1,0:T(8,128)(2,1)}, u32[]{:S(2)}) copy-start(bf16[1,256,256]{2,1,0:T(8,128)(2,1)} %param.14) | copy-start | bytes 393220
  28.1 8.3 %copy-start.2 = (bf16[1,256,256]{2,1,0:T(8,128)(2,1)S(1)}, bf16[1,256,256]{2,1,0:T(8,128)(2,1)}, u32[]{:S(2)}) copy-start(bf16[1,256,256]{2,1,0:T(8,128)(2,1)} %param.15) | copy-start | bytes 393220
  28.1 11.1 %collective-permute-start.7 = (bf16[128,1024]{1,0:T(8,128)(2,1)S(1)}, bf16[128,1024]{1,0:T(8,128)(2,1)S(1)}, u32[]{:S(2)}, u32[]{:S(2)}) collective-permute-start(bf16[128,1024]{1,0:T(8,128)(2,1)S(1)} %chain.6), channel_id=1, source_target_pairs={{4,8},{8,4},{5,9},{9,5},{6,10},{10,6},{7,11},{11,7},{20,24},{24,20... | collective-permute-start | bytes 786440 | tf_op jit(solution)/shard_map/ppermute | solution.py:738
  28.9 7.5 %copy-start.4 = (s32[1,1024]{1,0:T(1,128)S(1)}, s32[1,1024]{1,0:T(1,128)}, u32[]{:S(2)}) copy-start(s32[1,1024]{1,0:T(1,128)} %docs_ref.7) | copy-start | bytes 12292
  29.0 14.5 %collective-permute-start.5 = (bf16[128,1024]{1,0:T(8,128)(2,1)S(1)}, bf16[128,1024]{1,0:T(8,128)(2,1)S(1)}, u32[]{:S(2)}, u32[]{:S(2)}) collective-permute-start(bf16[128,1024]{1,0:T(8,128)(2,1)S(1)} %chain.5), channel_id=1, source_target_pairs={{8,12},{4,0},{9,13},{5,1},{10,14},{6,2},{11,15},{7,3},{24,28},{20,... | collective-permute-start | bytes 786440 | tf_op jit(solution)/shard_map/ppermute | solution.py:738
  39.2 4.3 %copy-start.3 = (bf16[1,256,256]{2,1,0:T(8,128)(2,1)S(1)}, bf16[1,256,256]{2,1,0:T(8,128)(2,1)}, u32[]{:S(2)}) copy-start(bf16[1,256,256]{2,1,0:T(8,128)(2,1)} %param.20) | copy-start | bytes 393220
  39.3 4.3 %copy-start.5 = (f32[2048]{0:T(1024)S(1)}, f32[2048]{0:T(1024)}, u32[]{:S(2)}) copy-start(f32[2048]{0:T(1024)} %param.25) | copy-start | bytes 24580
  39.3 8.4 %collective-permute-start.9 = (bf16[128,1024]{1,0:T(8,128)(2,1)S(1)}, bf16[128,1024]{1,0:T(8,128)(2,1)S(1)}, u32[]{:S(2)}, u32[]{:S(2)}) collective-permute-start(bf16[128,1024]{1,0:T(8,128)(2,1)S(1)} %chain.7), channel_id=1, source_target_pairs={{8,12},{4,0},{9,13},{5,1},{10,14},{6,2},{11,15},{7,3},{24,28},{20,... | collective-permute-start | bytes 786440 | tf_op jit(solution)/shard_map/ppermute | solution.py:738
  49.5 4.7 %collective-permute-start.12 = (f32[3,1024]{1,0:T(4,128)S(1)}, f32[3,1024]{1,0:T(4,128)S(1)}, u32[]{:S(2)}, u32[]{:S(2)}) collective-permute-start(f32[3,1024]{1,0:T(4,128)S(1)} %get-tuple-element.75), channel_id=1, source_target_pairs={{0,20},{4,16},{8,28},{12,24},{16,4},{20,0},{24,12},{28,8},{1,21},{... | collective-permute-start | bytes 36872 | tf_op jit(solution)/shard_map/ppermute | solution.py:559
  50.9 3.7 %collective-permute-start.11 = (f32[3,1024]{1,0:T(4,128)S(1)}, f32[3,1024]{1,0:T(4,128)S(1)}, u32[]{:S(2)}, u32[]{:S(2)}) collective-permute-start(f32[3,1024]{1,0:T(4,128)S(1)} %get-tuple-element.75), channel_id=1, source_target_pairs={{0,16},{4,20},{8,24},{12,28},{16,0},{20,4},{24,8},{28,12},{1,17},{... | collective-permute-start | bytes 36872 | tf_op jit(solution)/shard_map/ppermute | solution.py:559
  51.5 3.7 %collective-permute-start.10 = (f32[3,1024]{1,0:T(4,128)S(1)}, f32[3,1024]{1,0:T(4,128)S(1)}, u32[]{:S(2)}, u32[]{:S(2)}) collective-permute-start(f32[3,1024]{1,0:T(4,128)S(1)} %get-tuple-element.75), channel_id=1, source_target_pairs={{0,4},{4,0},{8,12},{12,8},{16,20},{20,16},{24,28},{28,24},{1,5},{5... | collective-permute-start | bytes 36872 | tf_op jit(solution)/shard_map/ppermute | solution.py:559
  55.2 4.7 %collective-permute-start.13 = (f32[3,1024]{1,0:T(4,128)S(1)}, f32[3,1024]{1,0:T(4,128)S(1)}, u32[]{:S(2)}, u32[]{:S(2)}) collective-permute-start(f32[3,1024]{1,0:T(4,128)S(1)} %add_add_fusion.a_ref), channel_id=1, source_target_pairs={{0,8},{4,12},{8,0},{12,4},{16,24},{20,28},{24,16},{28,20},{1,9},{5... | collective-permute-start | bytes 36872 | tf_op jit(solution)/shard_map/ppermute | solution.py:559

commit v17 on v16

--- a/solution.py
+++ b/solution.py
@@ -771,13 +771,11 @@
         )
         normed.append(made)
     teacher, student = write(*targets), write(*normed)
-    shifts = [1 << k for k in range(count.bit_length() - 1)]
-    partner = exchange(grads, shifts[0])
-    if lax.axis_size("dp") == 2:
-        grads = (grads + partner) + (exchange(grads, count) + exchange(grads, count + shifts[0]))
-    else:
-        grads = grads + partner
-    for shift in shifts[1:-1]:
+    shifts = [1 << k for k in range((lax.axis_size("dp") * count).bit_length() - 1)]
+    if count >= 4:
+        grads = (grads + exchange(grads, 1)) + (exchange(grads, 2) + exchange(grads, 3))
+        shifts = shifts[2:]
+    for shift in shifts[:-1]:
         grads = grads + exchange(grads, shift)
     grad_gain, grad_skip = pl.pallas_call(
         closing_kernel,

time: 60.9 us -> 60.5 us (level)
  waiting for transfers between devices: 20.9 us -> 18.5 us
  starting transfers between devices: 19.3 us -> 21.3 us
    ppermute x4, waiting for transfers between devices: 4.43 us -> 1.98 us  [exchange(): return lax.ppermute(part, axes, [(d, d ^ shift) for d in range(size)])]
    ppermute x4, starting transfers between devices: 3.97 us -> 6 us  [exchange(): return lax.ppermute(part, axes, [(d, d ^ shift) for d in range(size)])]
  transfers between devices with their start and end apart: 14 -> 14, of which waited for: 9 -> 8; matrix products, arithmetic and copies ran while one was open for 0% -> 0% of each run, Pallas kernels for 23% -> 23%
where the time goes in v17:
time: 60.5 us; the launch traced here: 60.1 us
  starting transfers between devices  21.3 us (35%)
  Pallas kernels  19.4 us (32%)
  waiting for transfers between devices  18.5 us (31%)
  between operations  0.87 us (1%)
    ppermute x1, waiting for transfers between devices, body(): farther = lax.ppermute(beyond, 'ctx', outward)  6.1 us
    ppermute x4, starting transfers between devices, exchange(): return lax.ppermute(part, axes, [(d, d ^ shift) for d in range(size)])  6 us
    ppermute x1, starting transfers between devices, body(): near = lax.ppermute(kv, 'ctx', inward + outward)  5.97 us
    pallas_call x2, Pallas kernels, body(): pl.pallas_call(functools.partial(attention_kernel, count, per_kv, stack,...  5.58 us
    ppermute x1, waiting for transfers between devices, body(): got[0].append(lax.ppermute(send[0], 'ctx', [(0, 1), (3, 2)]))  4.94 us
    pallas_call x1, Pallas kernels, body(): pl.pallas_call(functools.partial(local_kernel, count, groups), out_shape=...  4.19 us
    pallas_call x2, Pallas kernels, body(): pl.pallas_call(functools.partial(final_kernel, count, g, groups, loss_sca...  3.72 us
    ppermute x3, starting transfers between devices, body(): got[g].append(lax.ppermute(send[g], 'ctx', pairs))  3.51 us
  transfers between devices with their start and end apart: 14, of which 8 were waited for; matrix products, arithmetic and copies ran while one was open for 0% of the time, Pallas kernels for 23%

profile of v17, /device:TPU:0, one launch (start us, length us, event | category | flops | bytes accessed | tf_op | source)
XLA Modules:
  0.0 60.1 jit_solution(1374932110238606502)
XLA Ops:
  0.6 3.2 %opening.1 = (bf16[272,512]{1,0:T(8,128)(2,1)S(1)}, f32[32,256]{1,0:T(8,128)S(1)}, bf16[256,1024]{1,0:T(8,128)(2,1)S(1)}, bf16[256,1024]{1,0:T(8,128)(2,1)S(1)},...) custom-call(s32[1,1024]{1,0:T(1,128)} %docs_ref.7, ...), custom_call_target="tpu_custom_call" | custom-call | flops 268435456 | bytes 4194304 | tf_op jit(solution)/shard_map/opening/pallas_call | solution.py:608
  3.9 0.7 %collective-permute-start.3 = (bf16[272,512]{1,0:T(8,128)(2,1)S(1)}, bf16[272,512]{1,0:T(8,128)(2,1)S(1)}, u32[]{:S(2)}, u32[]{:S(2)}) collective-permute-start(bf16[272,512]{1,0:T(8,128)(2,1)S(1)} %get-tuple-element.45), channel_id=1, source_target_pairs={{4,8},{8,4},{5,9},{9,5},{6,10},{10,6},{7,11},{11,7},{20,24},{24,20... | collective-permute-start | bytes 835592 | tf_op jit(solution)/shard_map/ppermute | solution.py:675
  4.6 6.0 %collective-permute-start.1 = (bf16[272,512]{1,0:T(8,128)(2,1)S(1)}, bf16[272,512]{1,0:T(8,128)(2,1)S(1)}, u32[]{:S(2)}, u32[]{:S(2)}) collective-permute-start(bf16[272,512]{1,0:T(8,128)(2,1)S(1)} %get-tuple-element.45), channel_id=1, source_target_pairs={{0,4},{12,8},{4,0},{8,12},{1,5},{13,9},{5,1},{9,13},{2,6},{14,10},... | collective-permute-start | bytes 835592 | tf_op jit(solution)/shard_map/ppermute | solution.py:674
  10.5 1.9 %collective-permute-start = (bf16[128,1024]{1,0:T(8,128)(2,1)S(1)}, bf16[128,1024]{1,0:T(8,128)(2,1)S(1)}, u32[]{:S(2)}, u32[]{:S(2)}) collective-permute-start(bf16[128,1024]{1,0:T(8,128)(2,1)S(1)} %get-tuple-element.41), channel_id=1, source_target_pairs={{0,4},{12,8},{1,5},{13,9},{2,6},{14,10},{3,7},{15,11},{16,20},{28,... | collective-permute-start | bytes 786440 | tf_op jit(solution)/shard_map/ppermute | solution.py:690
  12.5 4.2 %local.1 = (f32[256,1024]{1,0:T(8,128)S(1)}, f32[256,1024]{1,0:T(8,128)S(1)}, f32[256,1024]{1,0:T(8,128)S(1)}, f32[256,1024]{1,0:T(8,128)S(1)}, f32[256,1024]{1,0:T(8,128)S(1)}, /*index=5*/f32[256,1024]{1,0:T(8,128)S(1)}) custom-call(s32[1,1024]{1,0:T(1,128)} %docs_ref.7, bf16[256,2048]{1,0:T(8,128)(2,1)} %bitcast.32, bf16[256,2048]{1,0:T(8,128)(2,1)} %bitcast.33, ...), custom_call_target="tpu_custom_call" | custom-call | flops 134217728 | bytes 8388608 | tf_op jit(solution)/shard_map/local/pallas_call | solution.py:640
  16.7 0.0 collective-permute-done.3.refs_0_.kv_ref.refs_1_.refs_4_
  16.7 0.6 %collective-permute-start.6 = (bf16[144,1024]{1,0:T(8,128)(2,1)S(1)}, bf16[144,1024]{1,0:T(8,128)(2,1)S(1)}, u32[]{:S(2)}, u32[]{:S(2)}) collective-permute-start(bf16[144,1024]{1,0:T(8,128)(2,1)S(1)} %merge.1), channel_id=1, source_target_pairs={{0,4},{12,8},{4,0},{8,12},{1,5},{13,9},{5,1},{9,13},{2,6},{14,10},... | collective-permute-start | bytes 884744 | tf_op jit(solution)/shard_map/ppermute | solution.py:687
  17.4 0.3 collective-permute-done.1.refs_0_.refs_3_
  17.6 0.7 %collective-permute-start.4 = (bf16[272,512]{1,0:T(8,128)(2,1)S(1)}, bf16[272,512]{1,0:T(8,128)(2,1)S(1)}, u32[]{:S(2)}, u32[]{:S(2)}) collective-permute-start(bf16[272,512]{1,0:T(8,128)(2,1)S(1)} %collective-permute-done.1.refs_0_.refs_3_), channel_id=1, source_target_pairs={{4,8},{8,4},{5,9},{9,5},{6,10},{10,6},{7,11},{11,7},{20,24},{24,20... | collective-permute-start | bytes 835592 | tf_op jit(solution)/shard_map/ppermute | solution.py:677
  18.3 4.9 %collective-permute-done.got_ref.refs_0_ = bf16[128,1024]{1,0:T(8,128)(2,1)S(1)} collective-permute-done((bf16[128,1024]{1,0:T(8,128)(2,1)S(1)}, bf16[128,1024]{1,0:T(8,128)(2,1)S(1)}, u32[]{:S(2)}, u32[]{:S(2)}) %collective-permute-start) | collective-permute-done | bytes 262176 | tf_op jit(solution)/shard_map/ppermute | solution.py:690
  23.3 0.7 %collective-permute-start.2 = (bf16[128,1024]{1,0:T(8,128)(2,1)S(1)}, bf16[128,1024]{1,0:T(8,128)(2,1)S(1)}, u32[]{:S(2)}, u32[]{:S(2)}) collective-permute-start(bf16[128,1024]{1,0:T(8,128)(2,1)S(1)} %chain.4), channel_id=1, source_target_pairs={{4,8},{8,4},{5,9},{9,5},{6,10},{10,6},{7,11},{11,7},{20,24},{24,20... | collective-permute-start | bytes 786440 | tf_op jit(solution)/shard_map/ppermute | solution.py:693
  23.9 0.0 collective-permute-done.4.refs_1_.refs_2_.refs_5_
  23.9 1.3 %collective-permute-start.8 = (bf16[272,512]{1,0:T(8,128)(2,1)S(1)}, bf16[272,512]{1,0:T(8,128)(2,1)S(1)}, u32[]{:S(2)}, u32[]{:S(2)}) collective-permute-start(bf16[272,512]{1,0:T(8,128)(2,1)S(1)} %collective-permute-done.4.refs_1_.refs_2_.refs_5_), channel_id=1, source_target_pairs={{4,0},{8,12},{5,1},{9,13},{6,2},{10,14},{7,3},{11,15},{20,16},{24,... | collective-permute-start | bytes 835592 | tf_op jit(solution)/shard_map/ppermute | solution.py:694
  25.2 2.9 %collective-permute-done.6.got_ref.refs_3_.refs_6_.refs_0_ = bf16[144,1024]{1,0:T(8,128)(2,1)S(1)} collective-permute-done((bf16[144,1024]{1,0:T(8,128)(2,1)S(1)}, bf16[144,1024]{1,0:T(8,128)(2,1)S(1)}, u32[]{:S(2)}, u32[]{:S(2)}) %collective-permute-start.6) | collective-permute-done | bytes 294944 | tf_op jit(solution)/shard_map/ppermute | solution.py:687
  28.1 0.0 copy-start
  28.1 0.0 copy-start.1
  28.1 0.8 %collective-permute-start.7 = (bf16[128,1024]{1,0:T(8,128)(2,1)S(1)}, bf16[128,1024]{1,0:T(8,128)(2,1)S(1)}, u32[]{:S(2)}, u32[]{:S(2)}) collective-permute-start(bf16[128,1024]{1,0:T(8,128)(2,1)S(1)} %chain.6), channel_id=1, source_target_pairs={{4,8},{8,4},{5,9},{9,5},{6,10},{10,6},{7,11},{11,7},{20,24},{24,20... | collective-permute-start | bytes 786440 | tf_op jit(solution)/shard_map/ppermute | solution.py:738
  28.9 0.0 collective-permute-done.2.got_ref.refs_1_
  28.9 0.0 copy-start.4
  29.0 1.3 %collective-permute-start.5 = (bf16[128,1024]{1,0:T(8,128)(2,1)S(1)}, bf16[128,1024]{1,0:T(8,128)(2,1)S(1)}, u32[]{:S(2)}, u32[]{:S(2)}) collective-permute-start(bf16[128,1024]{1,0:T(8,128)(2,1)S(1)} %chain.5), channel_id=1, source_target_pairs={{8,12},{4,0},{9,13},{5,1},{10,14},{6,2},{11,15},{7,3},{24,28},{20,... | collective-permute-start | bytes 786440 | tf_op jit(solution)/shard_map/ppermute | solution.py:738
  30.3 6.1 %collective-permute-done.8.refs_4_.refs_7_ = bf16[272,512]{1,0:T(8,128)(2,1)S(1)} collective-permute-done((bf16[272,512]{1,0:T(8,128)(2,1)S(1)}, bf16[272,512]{1,0:T(8,128)(2,1)S(1)}, u32[]{:S(2)}, u32[]{:S(2)}) %collective-permute-start.8) | collective-permute-done | bytes 278560 | tf_op jit(solution)/shard_map/ppermute | solution.py:694
  36.4 0.0 copy-done
  36.4 0.0 copy-done.1
  36.4 0.0 copy-done.2
  36.4 0.0 copy-done.4
  36.4 2.8 %attention.2.refs_0_.teacher_ref = bf16[256,1024]{1,0:T(8,128)(2,1)S(1)} custom-call(s32[1,1024]{1,0:T(1,128)S(1)} %copy-done.4, bf16[256,2048]{1,0:T(8,128)(2,1)S(1)} %bitcast.18, bf16[256,256]{1,0:T(8,128)(2,1)S(1)} %bitcast.21, bf16[256,256]{1,0:T(8,128)(2,1)S(1)} %bitcast.24, bf16[272,512]{1,0:T(8,128)(2,1)S(1)} %collective-permute-done.1.refs_0_.refs_3_, ...), custom_call_target="tpu_custom_call" | custom-call | flops 603979776 | bytes 2097152 | tf_op jit(solution)/shard_map/attention/pallas_call | solution.py:705
  39.2 0.0 collective-permute-done.7.got_ref.refs_1_
  39.2 0.0 copy-start.3
  39.3 0.0 copy-start.5
  39.3 1.4 %collective-permute-start.9 = (bf16[128,1024]{1,0:T(8,128)(2,1)S(1)}, bf16[128,1024]{1,0:T(8,128)(2,1)S(1)}, u32[]{:S(2)}, u32[]{:S(2)}) collective-permute-start(bf16[128,1024]{1,0:T(8,128)(2,1)S(1)} %chain.7), channel_id=1, source_target_pairs={{8,12},{4,0},{9,13},{5,1},{10,14},{6,2},{11,15},{7,3},{24,28},{20,... | collective-permute-start | bytes 786440 | tf_op jit(solution)/shard_map/ppermute | solution.py:738
  40.7 2.8 %attention.3.refs_1_.teacher_ref = bf16[256,1024]{1,0:T(8,128)(2,1)S(1)} custom-call(s32[1,1024]{1,0:T(1,128)S(1)} %copy-done.4, bf16[256,2048]{1,0:T(8,128)(2,1)S(1)} %bitcast.19, bf16[256,256]{1,0:T(8,128)(2,1)S(1)} %bitcast.22, bf16[256,256]{1,0:T(8,128)(2,1)S(1)} %bitcast.25, bf16[272,512]{1,0:T(8,128)(2,1)S(1)} %collective-permute-done.1.refs_0_.refs_3_, ...), custom_call_target="tpu_custom_call" | custom-call | flops 603979776 | bytes 2097152 | tf_op jit(solution)/shard_map/attention/pallas_call | solution.py:705
  43.5 0.0 collective-permute-done.5.refs_2_
  43.5 0.0 copy-done.3
  43.5 0.0 copy-done.5
  43.5 1.9 %final.2 = (bf16[256,1024]{1,0:T(8,128)(2,1)S(1)}, f32[3,1024]{1,0:T(4,128)S(1)}) custom-call(f32[256,1024]{1,0:T(8,128)S(1)} %get-tuple-element.64.pre_ref, f32[256,1024]{1,0:T(8,128)S(1)} %get-tuple-element.65.reach_ref, f32[256,1024]{1,0:T(8,128)S(1)} %get-tuple-element.66.sx_ref, bf16[256,256]{1,0:T(8,128)(2,1)S(1)} %bitcast.27, ...), custom_call_target="tpu_custom_call" | custom-call | flops 67108864 | bytes 5242880 | tf_op jit(solution)/shard_map/final/pallas_call | solution.py:744
  45.4 2.3 %collective-permute-done.9.refs_2_ = bf16[128,1024]{1,0:T(8,128)(2,1)S(1)} collective-permute-done((bf16[128,1024]{1,0:T(8,128)(2,1)S(1)}, bf16[128,1024]{1,0:T(8,128)(2,1)S(1)}, u32[]{:S(2)}, u32[]{:S(2)}) %collective-permute-start.9) | collective-permute-done | bytes 262176 | tf_op jit(solution)/shard_map/ppermute | solution.py:738
  47.7 1.9 %final.3 = (bf16[256,1024]{1,0:T(8,128)(2,1)S(1)}, f32[3,1024]{1,0:T(4,128)S(1)}) custom-call(f32[256,1024]{1,0:T(8,128)S(1)} %get-tuple-element.69.pre_ref, f32[256,1024]{1,0:T(8,128)S(1)} %get-tuple-element.70.reach_ref, f32[256,1024]{1,0:T(8,128)S(1)} %get-tuple-element.71.sx_ref, bf16[256,256]{1,0:T(8,128)(2,1)S(1)} %bitcast.28, ...), custom_call_target="tpu_custom_call" | custom-call | flops 67108864 | bytes 5242880 | tf_op jit(solution)/shard_map/final/pallas_call | solution.py:744
  49.5 0.3 collective-permute-start.12
  49.8 1.7 %collective-permute-start.11 = (f32[3,1024]{1,0:T(4,128)S(1)}, f32[3,1024]{1,0:T(4,128)S(1)}, u32[]{:S(2)}, u32[]{:S(2)}) collective-permute-start(f32[3,1024]{1,0:T(4,128)S(1)} %get-tuple-element.75), channel_id=1, source_target_pairs={{0,8},{4,12},{8,0},{12,4},{16,24},{20,28},{24,16},{28,20},{1,9},{5... | collective-permute-start | bytes 36872 | tf_op jit(solution)/shard_map/ppermute | solution.py:559
  51.5 2.5 %collective-permute-start.10 = (f32[3,1024]{1,0:T(4,128)S(1)}, f32[3,1024]{1,0:T(4,128)S(1)}, u32[]{:S(2)}, u32[]{:S(2)}) collective-permute-start(f32[3,1024]{1,0:T(4,128)S(1)} %get-tuple-element.75), channel_id=1, source_target_pairs={{0,4},{4,0},{8,12},{12,8},{16,20},{20,16},{24,28},{28,24},{1,5},{5... | collective-permute-start | bytes 36872 | tf_op jit(solution)/shard_map/ppermute | solution.py:559
  54.0 1.1 %collective-permute-done.12 = f32[3,1024]{1,0:T(4,128)S(1)} collective-permute-done((f32[3,1024]{1,0:T(4,128)S(1)}, f32[3,1024]{1,0:T(4,128)S(1)}, u32[]{:S(2)}, u32[]{:S(2)}) %collective-permute-start.12) | collective-permute-done | bytes 12320 | tf_op jit(solution)/shard_map/ppermute | solution.py:559
  55.1 0.0 collective-permute-done.11
  55.1 0.6 collective-permute-done.10
  55.7 1.6 %collective-permute-start.13 = (f32[3,1024]{1,0:T(4,128)S(1)}, f32[3,1024]{1,0:T(4,128)S(1)}, u32[]{:S(2)}, u32[]{:S(2)}) collective-permute-start(f32[3,1024]{1,0:T(4,128)S(1)} %add_add_fusion.a_ref), channel_id=1, source_target_pairs={{0,16},{4,20},{8,24},{12,28},{16,0},{20,4},{24,8},{28,12},{1,17},{... | collective-permute-start | bytes 36872 | tf_op jit(solution)/shard_map/ppermute | solution.py:559
  57.3 1.0 %writing.2 = bf16[256,2048]{1,0:T(8,128)(2,1)} custom-call(bf16[256,1024]{1,0:T(8,128)(2,1)S(1)} %attention.2.refs_0_.teacher_ref, bf16[256,1024]{1,0:T(8,128)(2,1)S(1)} %attention.3.refs_1_.teacher_ref), custom_call_target="tpu_custom_call" | custom-call | bytes 2097152 | tf_op jit(solution)/shard_map/writing/pallas_call | solution.py:595
  58.2 1.0 %writing.3 = bf16[256,2048]{1,0:T(8,128)(2,1)} custom-call(bf16[256,1024]{1,0:T(8,128)(2,1)S(1)} %get-tuple-element.68.refs_0_, bf16[256,1024]{1,0:T(8,128)(2,1)S(1)} %get-tuple-element.74.refs_1_), custom_call_target="tpu_custom_call" | custom-call | bytes 2097152 | tf_op jit(solution)/shard_map/writing/pallas_call | solution.py:595
  59.2 0.3 collective-permute-done.13.b_ref
  59.5 0.6 %closing.1 = (f32[1,2048]{1,0:T(1,128)}, f32[1,32]{1,0:T(1,128)}) custom-call(f32[3,1024]{1,0:T(4,128)S(1)} %add_add_fusion.a_ref, f32[3,1024]{1,0:T(4,128)S(1)} %collective-permute-done.13.b_ref), custom_call_target="tpu_custom_call" | custom-call | tf_op jit(solution)/shard_map/closing/pallas_call | solution.py:780
  (7 shorter events, 0.1 us)
Async XLA Ops:
  3.9 12.8 %collective-permute-start.3 = (bf16[272,512]{1,0:T(8,128)(2,1)S(1)}, bf16[272,512]{1,0:T(8,128)(2,1)S(1)}, u32[]{:S(2)}, u32[]{:S(2)}) collective-permute-start(bf16[272,512]{1,0:T(8,128)(2,1)S(1)} %get-tuple-element.45), channel_id=1, source_target_pairs={{4,8},{8,4},{5,9},{9,5},{6,10},{10,6},{7,11},{11,7},{20,24},{24,20... | collective-permute-start | bytes 835592 | tf_op jit(solution)/shard_map/ppermute | solution.py:675
  4.6 13.1 %collective-permute-start.1 = (bf16[272,512]{1,0:T(8,128)(2,1)S(1)}, bf16[272,512]{1,0:T(8,128)(2,1)S(1)}, u32[]{:S(2)}, u32[]{:S(2)}) collective-permute-start(bf16[272,512]{1,0:T(8,128)(2,1)S(1)} %get-tuple-element.45), channel_id=1, source_target_pairs={{0,4},{12,8},{4,0},{8,12},{1,5},{13,9},{5,1},{9,13},{2,6},{14,10},... | collective-permute-start | bytes 835592 | tf_op jit(solution)/shard_map/ppermute | solution.py:674
  10.5 12.7 %collective-permute-start = (bf16[128,1024]{1,0:T(8,128)(2,1)S(1)}, bf16[128,1024]{1,0:T(8,128)(2,1)S(1)}, u32[]{:S(2)}, u32[]{:S(2)}) collective-permute-start(bf16[128,1024]{1,0:T(8,128)(2,1)S(1)} %get-tuple-element.41), channel_id=1, source_target_pairs={{0,4},{12,8},{1,5},{13,9},{2,6},{14,10},{3,7},{15,11},{16,20},{28,... | collective-permute-start | bytes 786440 | tf_op jit(solution)/shard_map/ppermute | solution.py:690
  16.7 11.4 %collective-permute-start.6 = (bf16[144,1024]{1,0:T(8,128)(2,1)S(1)}, bf16[144,1024]{1,0:T(8,128)(2,1)S(1)}, u32[]{:S(2)}, u32[]{:S(2)}) collective-permute-start(bf16[144,1024]{1,0:T(8,128)(2,1)S(1)} %merge.1), channel_id=1, source_target_pairs={{0,4},{12,8},{4,0},{8,12},{1,5},{13,9},{5,1},{9,13},{2,6},{14,10},... | collective-permute-start | bytes 884744 | tf_op jit(solution)/shard_map/ppermute | solution.py:687
  17.6 6.3 %collective-permute-start.4 = (bf16[272,512]{1,0:T(8,128)(2,1)S(1)}, bf16[272,512]{1,0:T(8,128)(2,1)S(1)}, u32[]{:S(2)}, u32[]{:S(2)}) collective-permute-start(bf16[272,512]{1,0:T(8,128)(2,1)S(1)} %collective-permute-done.1.refs_0_.refs_3_), channel_id=1, source_target_pairs={{4,8},{8,4},{5,9},{9,5},{6,10},{10,6},{7,11},{11,7},{20,24},{24,20... | collective-permute-start | bytes 835592 | tf_op jit(solution)/shard_map/ppermute | solution.py:677
  23.3 5.7 %collective-permute-start.2 = (bf16[128,1024]{1,0:T(8,128)(2,1)S(1)}, bf16[128,1024]{1,0:T(8,128)(2,1)S(1)}, u32[]{:S(2)}, u32[]{:S(2)}) collective-permute-start(bf16[128,1024]{1,0:T(8,128)(2,1)S(1)} %chain.4), channel_id=1, source_target_pairs={{4,8},{8,4},{5,9},{9,5},{6,10},{10,6},{7,11},{11,7},{20,24},{24,20... | collective-permute-start | bytes 786440 | tf_op jit(solution)/shard_map/ppermute | solution.py:693
  23.9 12.4 %collective-permute-start.8 = (bf16[272,512]{1,0:T(8,128)(2,1)S(1)}, bf16[272,512]{1,0:T(8,128)(2,1)S(1)}, u32[]{:S(2)}, u32[]{:S(2)}) collective-permute-start(bf16[272,512]{1,0:T(8,128)(2,1)S(1)} %collective-permute-done.4.refs_1_.refs_2_.refs_5_), channel_id=1, source_target_pairs={{4,0},{8,12},{5,1},{9,13},{6,2},{10,14},{7,3},{11,15},{20,16},{24,... | collective-permute-start | bytes 835592 | tf_op jit(solution)/shard_map/ppermute | solution.py:694
  28.1 8.3 %copy-start = (bf16[1,256,2048]{2,1,0:T(8,128)(2,1)S(1)}, bf16[1,256,2048]{2,1,0:T(8,128)(2,1)}, u32[]{:S(2)}) copy-start(bf16[1,256,2048]{2,1,0:T(8,128)(2,1)} %param.13) | copy-start | bytes 3145732
  28.1 8.3 %copy-start.1 = (bf16[1,256,256]{2,1,0:T(8,128)(2,1)S(1)}, bf16[1,256,256]{2,1,0:T(8,128)(2,1)}, u32[]{:S(2)}) copy-start(bf16[1,256,256]{2,1,0:T(8,128)(2,1)} %param.14) | copy-start | bytes 393220
  28.1 8.3 %copy-start.2 = (bf16[1,256,256]{2,1,0:T(8,128)(2,1)S(1)}, bf16[1,256,256]{2,1,0:T(8,128)(2,1)}, u32[]{:S(2)}) copy-start(bf16[1,256,256]{2,1,0:T(8,128)(2,1)} %param.15) | copy-start | bytes 393220
  28.1 11.1 %collective-permute-start.7 = (bf16[128,1024]{1,0:T(8,128)(2,1)S(1)}, bf16[128,1024]{1,0:T(8,128)(2,1)S(1)}, u32[]{:S(2)}, u32[]{:S(2)}) collective-permute-start(bf16[128,1024]{1,0:T(8,128)(2,1)S(1)} %chain.6), channel_id=1, source_target_pairs={{4,8},{8,4},{5,9},{9,5},{6,10},{10,6},{7,11},{11,7},{20,24},{24,20... | collective-permute-start | bytes 786440 | tf_op jit(solution)/shard_map/ppermute | solution.py:738
  28.9 7.5 %copy-start.4 = (s32[1,1024]{1,0:T(1,128)S(1)}, s32[1,1024]{1,0:T(1,128)}, u32[]{:S(2)}) copy-start(s32[1,1024]{1,0:T(1,128)} %docs_ref.7) | copy-start | bytes 12292
  29.0 14.5 %collective-permute-start.5 = (bf16[128,1024]{1,0:T(8,128)(2,1)S(1)}, bf16[128,1024]{1,0:T(8,128)(2,1)S(1)}, u32[]{:S(2)}, u32[]{:S(2)}) collective-permute-start(bf16[128,1024]{1,0:T(8,128)(2,1)S(1)} %chain.5), channel_id=1, source_target_pairs={{8,12},{4,0},{9,13},{5,1},{10,14},{6,2},{11,15},{7,3},{24,28},{20,... | collective-permute-start | bytes 786440 | tf_op jit(solution)/shard_map/ppermute | solution.py:738
  39.2 4.3 %copy-start.3 = (bf16[1,256,256]{2,1,0:T(8,128)(2,1)S(1)}, bf16[1,256,256]{2,1,0:T(8,128)(2,1)}, u32[]{:S(2)}) copy-start(bf16[1,256,256]{2,1,0:T(8,128)(2,1)} %param.20) | copy-start | bytes 393220
  39.3 4.3 %copy-start.5 = (f32[2048]{0:T(1024)S(1)}, f32[2048]{0:T(1024)}, u32[]{:S(2)}) copy-start(f32[2048]{0:T(1024)} %param.25) | copy-start | bytes 24580
  39.3 8.4 %collective-permute-start.9 = (bf16[128,1024]{1,0:T(8,128)(2,1)S(1)}, bf16[128,1024]{1,0:T(8,128)(2,1)S(1)}, u32[]{:S(2)}, u32[]{:S(2)}) collective-permute-start(bf16[128,1024]{1,0:T(8,128)(2,1)S(1)} %chain.7), channel_id=1, source_target_pairs={{8,12},{4,0},{9,13},{5,1},{10,14},{6,2},{11,15},{7,3},{24,28},{20,... | collective-permute-start | bytes 786440 | tf_op jit(solution)/shard_map/ppermute | solution.py:738
  49.5 5.6 %collective-permute-start.12 = (f32[3,1024]{1,0:T(4,128)S(1)}, f32[3,1024]{1,0:T(4,128)S(1)}, u32[]{:S(2)}, u32[]{:S(2)}) collective-permute-start(f32[3,1024]{1,0:T(4,128)S(1)} %get-tuple-element.75), channel_id=1, source_target_pairs={{0,12},{4,8},{8,4},{12,0},{16,28},{20,24},{24,20},{28,16},{1,13},{... | collective-permute-start | bytes 36872 | tf_op jit(solution)/shard_map/ppermute | solution.py:559
  49.8 5.3 %collective-permute-start.11 = (f32[3,1024]{1,0:T(4,128)S(1)}, f32[3,1024]{1,0:T(4,128)S(1)}, u32[]{:S(2)}, u32[]{:S(2)}) collective-permute-start(f32[3,1024]{1,0:T(4,128)S(1)} %get-tuple-element.75), channel_id=1, source_target_pairs={{0,8},{4,12},{8,0},{12,4},{16,24},{20,28},{24,16},{28,20},{1,9},{5... | collective-permute-start | bytes 36872 | tf_op jit(solution)/shard_map/ppermute | solution.py:559
  51.5 4.2 %collective-permute-start.10 = (f32[3,1024]{1,0:T(4,128)S(1)}, f32[3,1024]{1,0:T(4,128)S(1)}, u32[]{:S(2)}, u32[]{:S(2)}) collective-permute-start(f32[3,1024]{1,0:T(4,128)S(1)} %get-tuple-element.75), channel_id=1, source_target_pairs={{0,4},{4,0},{8,12},{12,8},{16,20},{20,16},{24,28},{28,24},{1,5},{5... | collective-permute-start | bytes 36872 | tf_op jit(solution)/shard_map/ppermute | solution.py:559
  55.7 3.8 %collective-permute-start.13 = (f32[3,1024]{1,0:T(4,128)S(1)}, f32[3,1024]{1,0:T(4,128)S(1)}, u32[]{:S(2)}, u32[]{:S(2)}) collective-permute-start(f32[3,1024]{1,0:T(4,128)S(1)} %add_add_fusion.a_ref), channel_id=1, source_target_pairs={{0,16},{4,20},{8,24},{12,28},{16,0},{20,4},{24,8},{28,12},{1,17},{... | collective-permute-start | bytes 36872 | tf_op jit(solution)/shard_map/ppermute | solution.py:559

commit v18 on v17

--- a/solution.py
+++ b/solution.py
@@ -738,9 +738,12 @@
             got[g].append(lax.ppermute(send[g], "ctx", pairs))
 
     got[0][-1], *targets = lax.optimization_barrier((got[0][-1], *targets))
+    teacher = write(*targets)
     normed, grads = [], None
     for g in range(groups):
         more = [] if grads is None else [grads]
+        if g == groups - 1:
+            got[g][-1], teacher = lax.optimization_barrier((got[g][-1], teacher))
         made, grads = pl.pallas_call(
             functools.partial(final_kernel, count, g, groups, loss_scale, heads),
             out_shape=(struct((rows, width), BF16), struct((groups + 1, width), F32)),
@@ -770,7 +773,7 @@
             *more,
         )
         normed.append(made)
-    teacher, student = write(*targets), write(*normed)
+    student = write(*normed)
     shifts = [1 << k for k in range((lax.axis_size("dp") * count).bit_length() - 1)]
     if count >= 4:
         grads = (grads + exchange(grads, 1)) + (exchange(grads, 2) + exchange(grads, 3))

time: 60.5 us -> 60.8 us (level)
    ppermute x4, waiting for transfers between devices: 1.98 us -> 3.5 us  [exchange(): return lax.ppermute(part, axes, [(d, d ^ shift) for d in range(size)])]
    ppermute x3, waiting for transfers between devices: 2.27 us -> 1.26 us  [body(): got[g].append(lax.ppermute(send[g], 'ctx', pairs))]
where the time goes in v18:
time: 60.8 us; the launch traced here: 60.5 us
  starting transfers between devices  21.2 us (35%)
  Pallas kernels  19.4 us (32%)
  waiting for transfers between devices  19 us (31%)
  between operations  0.87 us (1%)
    ppermute x1, waiting for transfers between devices, body(): farther = lax.ppermute(beyond, 'ctx', outward)  6.1 us
    ppermute x4, starting transfers between devices, exchange(): return lax.ppermute(part, axes, [(d, d ^ shift) for d in range(size)])  6 us
    ppermute x1, starting transfers between devices, body(): near = lax.ppermute(kv, 'ctx', inward + outward)  5.97 us
    pallas_call x2, Pallas kernels, body(): pl.pallas_call(functools.partial(attention_kernel, count, per_kv, stack,...  5.58 us
    ppermute x1, waiting for transfers between devices, body(): got[0].append(lax.ppermute(send[0], 'ctx', [(0, 1), (3, 2)]))  4.94 us
    pallas_call x1, Pallas kernels, body(): pl.pallas_call(functools.partial(local_kernel, count, groups), out_shape=...  4.19 us
    pallas_call x2, Pallas kernels, body(): pl.pallas_call(functools.partial(final_kernel, count, g, groups, loss_sca...  3.72 us
    ppermute x4, waiting for transfers between devices, exchange(): return lax.ppermute(part, axes, [(d, d ^ shift) for d in range(size)])  3.5 us
  transfers between devices with their start and end apart: 14, of which 8 were waited for; matrix products, arithmetic and copies ran while one was open for 0% of the time, Pallas kernels for 23%

profile of v18, /device:TPU:0, one launch (start us, length us, event | category | flops | bytes accessed | tf_op | source)
XLA Modules:
  0.0 60.5 jit_solution(2869891175880566457)
XLA Ops:
  0.6 3.2 %opening.1 = (bf16[272,512]{1,0:T(8,128)(2,1)S(1)}, f32[32,256]{1,0:T(8,128)S(1)}, bf16[256,1024]{1,0:T(8,128)(2,1)S(1)}, bf16[256,1024]{1,0:T(8,128)(2,1)S(1)},...) custom-call(s32[1,1024]{1,0:T(1,128)} %docs_ref.7, ...), custom_call_target="tpu_custom_call" | custom-call | flops 268435456 | bytes 4194304 | tf_op jit(solution)/shard_map/opening/pallas_call | solution.py:608
  3.9 0.7 %collective-permute-start = (bf16[272,512]{1,0:T(8,128)(2,1)S(1)}, bf16[272,512]{1,0:T(8,128)(2,1)S(1)}, u32[]{:S(2)}, u32[]{:S(2)}) collective-permute-start(bf16[272,512]{1,0:T(8,128)(2,1)S(1)} %get-tuple-element.44), channel_id=1, source_target_pairs={{4,8},{8,4},{5,9},{9,5},{6,10},{10,6},{7,11},{11,7},{20,24},{24,20... | collective-permute-start | bytes 835592 | tf_op jit(solution)/shard_map/ppermute | solution.py:675
  4.6 6.0 %collective-permute-start.2 = (bf16[272,512]{1,0:T(8,128)(2,1)S(1)}, bf16[272,512]{1,0:T(8,128)(2,1)S(1)}, u32[]{:S(2)}, u32[]{:S(2)}) collective-permute-start(bf16[272,512]{1,0:T(8,128)(2,1)S(1)} %get-tuple-element.44), channel_id=1, source_target_pairs={{0,4},{12,8},{4,0},{8,12},{1,5},{13,9},{5,1},{9,13},{2,6},{14,10},... | collective-permute-start | bytes 835592 | tf_op jit(solution)/shard_map/ppermute | solution.py:674
  10.5 1.9 %collective-permute-start.5 = (bf16[128,1024]{1,0:T(8,128)(2,1)S(1)}, bf16[128,1024]{1,0:T(8,128)(2,1)S(1)}, u32[]{:S(2)}, u32[]{:S(2)}) collective-permute-start(bf16[128,1024]{1,0:T(8,128)(2,1)S(1)} %get-tuple-element.58), channel_id=1, source_target_pairs={{0,4},{12,8},{1,5},{13,9},{2,6},{14,10},{3,7},{15,11},{16,20},{28,... | collective-permute-start | bytes 786440 | tf_op jit(solution)/shard_map/ppermute | solution.py:690
  12.5 4.2 %local.1 = (f32[256,1024]{1,0:T(8,128)S(1)}, f32[256,1024]{1,0:T(8,128)S(1)}, f32[256,1024]{1,0:T(8,128)S(1)}, f32[256,1024]{1,0:T(8,128)S(1)}, f32[256,1024]{1,0:T(8,128)S(1)}, /*index=5*/f32[256,1024]{1,0:T(8,128)S(1)}) custom-call(s32[1,1024]{1,0:T(1,128)} %docs_ref.7, bf16[256,2048]{1,0:T(8,128)(2,1)} %bitcast.32, bf16[256,2048]{1,0:T(8,128)(2,1)} %bitcast.33, ...), custom_call_target="tpu_custom_call" | custom-call | flops 134217728 | bytes 8388608 | tf_op jit(solution)/shard_map/local/pallas_call | solution.py:640
  16.7 0.0 collective-permute-done.kv_ref.refs_1_.refs_0_.refs_4_
  16.7 0.6 %collective-permute-start.1 = (bf16[144,1024]{1,0:T(8,128)(2,1)S(1)}, bf16[144,1024]{1,0:T(8,128)(2,1)S(1)}, u32[]{:S(2)}, u32[]{:S(2)}) collective-permute-start(bf16[144,1024]{1,0:T(8,128)(2,1)S(1)} %merge.1), channel_id=1, source_target_pairs={{0,4},{12,8},{4,0},{8,12},{1,5},{13,9},{5,1},{9,13},{2,6},{14,10},... | collective-permute-start | bytes 884744 | tf_op jit(solution)/shard_map/ppermute | solution.py:687
  17.4 0.3 collective-permute-done.2.refs_0_.refs_3_
  17.6 0.7 %collective-permute-start.4 = (bf16[272,512]{1,0:T(8,128)(2,1)S(1)}, bf16[272,512]{1,0:T(8,128)(2,1)S(1)}, u32[]{:S(2)}, u32[]{:S(2)}) collective-permute-start(bf16[272,512]{1,0:T(8,128)(2,1)S(1)} %collective-permute-done.2.refs_0_.refs_3_), channel_id=1, source_target_pairs={{4,8},{8,4},{5,9},{9,5},{6,10},{10,6},{7,11},{11,7},{20,24},{24,20... | collective-permute-start | bytes 835592 | tf_op jit(solution)/shard_map/ppermute | solution.py:677
  18.3 4.9 %collective-permute-done.5.got_ref.refs_0_ = bf16[128,1024]{1,0:T(8,128)(2,1)S(1)} collective-permute-done((bf16[128,1024]{1,0:T(8,128)(2,1)S(1)}, bf16[128,1024]{1,0:T(8,128)(2,1)S(1)}, u32[]{:S(2)}, u32[]{:S(2)}) %collective-permute-start.5) | collective-permute-done | bytes 262176 | tf_op jit(solution)/shard_map/ppermute | solution.py:690
  23.3 0.7 %collective-permute-start.8 = (bf16[128,1024]{1,0:T(8,128)(2,1)S(1)}, bf16[128,1024]{1,0:T(8,128)(2,1)S(1)}, u32[]{:S(2)}, u32[]{:S(2)}) collective-permute-start(bf16[128,1024]{1,0:T(8,128)(2,1)S(1)} %chain.5), channel_id=1, source_target_pairs={{4,8},{8,4},{5,9},{9,5},{6,10},{10,6},{7,11},{11,7},{20,24},{24,20... | collective-permute-start | bytes 786440 | tf_op jit(solution)/shard_map/ppermute | solution.py:693
  23.9 0.0 collective-permute-done.4.refs_2_.refs_1_.refs_5_
  23.9 1.3 %collective-permute-start.6 = (bf16[272,512]{1,0:T(8,128)(2,1)S(1)}, bf16[272,512]{1,0:T(8,128)(2,1)S(1)}, u32[]{:S(2)}, u32[]{:S(2)}) collective-permute-start(bf16[272,512]{1,0:T(8,128)(2,1)S(1)} %collective-permute-done.4.refs_2_.refs_1_.refs_5_), channel_id=1, source_target_pairs={{4,0},{8,12},{5,1},{9,13},{6,2},{10,14},{7,3},{11,15},{20,16},{24,... | collective-permute-start | bytes 835592 | tf_op jit(solution)/shard_map/ppermute | solution.py:694
  25.2 2.9 %collective-permute-done.1.got_ref.refs_3_.refs_6_.refs_0_ = bf16[144,1024]{1,0:T(8,128)(2,1)S(1)} collective-permute-done((bf16[144,1024]{1,0:T(8,128)(2,1)S(1)}, bf16[144,1024]{1,0:T(8,128)(2,1)S(1)}, u32[]{:S(2)}, u32[]{:S(2)}) %collective-permute-start.1) | collective-permute-done | bytes 294944 | tf_op jit(solution)/shard_map/ppermute | solution.py:687
  28.1 0.0 copy-start
  28.1 0.0 copy-start.1
  28.1 0.8 %collective-permute-start.3 = (bf16[128,1024]{1,0:T(8,128)(2,1)S(1)}, bf16[128,1024]{1,0:T(8,128)(2,1)S(1)}, u32[]{:S(2)}, u32[]{:S(2)}) collective-permute-start(bf16[128,1024]{1,0:T(8,128)(2,1)S(1)} %chain.4), channel_id=1, source_target_pairs={{4,8},{8,4},{5,9},{9,5},{6,10},{10,6},{7,11},{11,7},{20,24},{24,20... | collective-permute-start | bytes 786440 | tf_op jit(solution)/shard_map/ppermute | solution.py:738
  28.9 0.0 collective-permute-done.8.got_ref.refs_1_
  28.9 0.0 copy-start.4
  29.0 1.3 %collective-permute-start.9 = (bf16[128,1024]{1,0:T(8,128)(2,1)S(1)}, bf16[128,1024]{1,0:T(8,128)(2,1)S(1)}, u32[]{:S(2)}, u32[]{:S(2)}) collective-permute-start(bf16[128,1024]{1,0:T(8,128)(2,1)S(1)} %chain.7), channel_id=1, source_target_pairs={{8,12},{4,0},{9,13},{5,1},{10,14},{6,2},{11,15},{7,3},{24,28},{20,... | collective-permute-start | bytes 786440 | tf_op jit(solution)/shard_map/ppermute | solution.py:738
  30.3 6.1 %collective-permute-done.6.refs_4_.refs_7_ = bf16[272,512]{1,0:T(8,128)(2,1)S(1)} collective-permute-done((bf16[272,512]{1,0:T(8,128)(2,1)S(1)}, bf16[272,512]{1,0:T(8,128)(2,1)S(1)}, u32[]{:S(2)}, u32[]{:S(2)}) %collective-permute-start.6) | collective-permute-done | bytes 278560 | tf_op jit(solution)/shard_map/ppermute | solution.py:694
  36.4 0.0 copy-done
  36.4 0.0 copy-done.1
  36.4 0.0 copy-done.2
  36.4 0.0 copy-done.4
  36.4 2.8 %attention.2.refs_0_.teacher_ref = bf16[256,1024]{1,0:T(8,128)(2,1)S(1)} custom-call(s32[1,1024]{1,0:T(1,128)S(1)} %copy-done.4, bf16[256,2048]{1,0:T(8,128)(2,1)S(1)} %bitcast.18, bf16[256,256]{1,0:T(8,128)(2,1)S(1)} %bitcast.21, bf16[256,256]{1,0:T(8,128)(2,1)S(1)} %bitcast.24, bf16[272,512]{1,0:T(8,128)(2,1)S(1)} %collective-permute-done.2.refs_0_.refs_3_, ...), custom_call_target="tpu_custom_call" | custom-call | flops 603979776 | bytes 2097152 | tf_op jit(solution)/shard_map/attention/pallas_call | solution.py:705
  39.2 0.0 collective-permute-done.3.got_ref.refs_1_
  39.2 1.3 %collective-permute-start.7 = (bf16[128,1024]{1,0:T(8,128)(2,1)S(1)}, bf16[128,1024]{1,0:T(8,128)(2,1)S(1)}, u32[]{:S(2)}, u32[]{:S(2)}) collective-permute-start(bf16[128,1024]{1,0:T(8,128)(2,1)S(1)} %chain.6), channel_id=1, source_target_pairs={{8,12},{4,0},{9,13},{5,1},{10,14},{6,2},{11,15},{7,3},{24,28},{20,... | collective-permute-start | bytes 786440 | tf_op jit(solution)/shard_map/ppermute | solution.py:738
  40.5 2.8 %attention.3.refs_1_.teacher_ref = bf16[256,1024]{1,0:T(8,128)(2,1)S(1)} custom-call(s32[1,1024]{1,0:T(1,128)S(1)} %copy-done.4, bf16[256,2048]{1,0:T(8,128)(2,1)S(1)} %bitcast.19, bf16[256,256]{1,0:T(8,128)(2,1)S(1)} %bitcast.22, bf16[256,256]{1,0:T(8,128)(2,1)S(1)} %bitcast.25, bf16[272,512]{1,0:T(8,128)(2,1)S(1)} %collective-permute-done.2.refs_0_.refs_3_, ...), custom_call_target="tpu_custom_call" | custom-call | flops 603979776 | bytes 2097152 | tf_op jit(solution)/shard_map/attention/pallas_call | solution.py:705
  43.3 0.0 copy-start.3
  43.3 0.0 copy-start.5
  43.4 0.0 collective-permute-done.9.refs_2_
  43.4 1.0 %writing.2 = bf16[256,2048]{1,0:T(8,128)(2,1)} custom-call(bf16[256,1024]{1,0:T(8,128)(2,1)S(1)} %attention.2.refs_0_.teacher_ref, bf16[256,1024]{1,0:T(8,128)(2,1)S(1)} %attention.3.refs_1_.teacher_ref), custom_call_target="tpu_custom_call" | custom-call | bytes 2097152 | tf_op jit(solution)/shard_map/writing/pallas_call | solution.py:595
  44.4 0.0 copy-done.3
  44.4 0.0 copy-done.5
  44.4 1.9 %final.2 = (bf16[256,1024]{1,0:T(8,128)(2,1)S(1)}, f32[3,1024]{1,0:T(4,128)S(1)}) custom-call(f32[256,1024]{1,0:T(8,128)S(1)} %get-tuple-element.68.pre_ref, f32[256,1024]{1,0:T(8,128)S(1)} %get-tuple-element.69.reach_ref, f32[256,1024]{1,0:T(8,128)S(1)} %get-tuple-element.70.sx_ref, bf16[256,256]{1,0:T(8,128)(2,1)S(1)} %bitcast.27, ...), custom_call_target="tpu_custom_call" | custom-call | flops 67108864 | bytes 5242880 | tf_op jit(solution)/shard_map/final/pallas_call | solution.py:747
  46.2 1.3 %collective-permute-done.7.refs_2_ = bf16[128,1024]{1,0:T(8,128)(2,1)S(1)} collective-permute-done((bf16[128,1024]{1,0:T(8,128)(2,1)S(1)}, bf16[128,1024]{1,0:T(8,128)(2,1)S(1)}, u32[]{:S(2)}, u32[]{:S(2)}) %collective-permute-start.7) | collective-permute-done | bytes 262176 | tf_op jit(solution)/shard_map/ppermute | solution.py:738
  47.5 1.9 %final.3 = (bf16[256,1024]{1,0:T(8,128)(2,1)S(1)}, f32[3,1024]{1,0:T(4,128)S(1)}) custom-call(f32[256,1024]{1,0:T(8,128)S(1)} %get-tuple-element.73.pre_ref, f32[256,1024]{1,0:T(8,128)S(1)} %get-tuple-element.74.reach_ref, f32[256,1024]{1,0:T(8,128)S(1)} %get-tuple-element.75.sx_ref, bf16[256,256]{1,0:T(8,128)(2,1)S(1)} %bitcast.28, ...), custom_call_target="tpu_custom_call" | custom-call | flops 67108864 | bytes 5242880 | tf_op jit(solution)/shard_map/final/pallas_call | solution.py:747
  49.4 0.3 collective-permute-start.12
  49.6 2.7 %collective-permute-start.11 = (f32[3,1024]{1,0:T(4,128)S(1)}, f32[3,1024]{1,0:T(4,128)S(1)}, u32[]{:S(2)}, u32[]{:S(2)}) collective-permute-start(f32[3,1024]{1,0:T(4,128)S(1)} %get-tuple-element.79), channel_id=1, source_target_pairs={{0,8},{4,12},{8,0},{12,4},{16,24},{20,28},{24,16},{28,20},{1,9},{5... | collective-permute-start | bytes 36872 | tf_op jit(solution)/shard_map/ppermute | solution.py:559
  52.3 1.5 %collective-permute-start.10 = (f32[3,1024]{1,0:T(4,128)S(1)}, f32[3,1024]{1,0:T(4,128)S(1)}, u32[]{:S(2)}, u32[]{:S(2)}) collective-permute-start(f32[3,1024]{1,0:T(4,128)S(1)} %get-tuple-element.79), channel_id=1, source_target_pairs={{0,4},{4,0},{8,12},{12,8},{16,20},{20,16},{24,28},{28,24},{1,5},{5... | collective-permute-start | bytes 36872 | tf_op jit(solution)/shard_map/ppermute | solution.py:559
  53.8 1.1 %collective-permute-done.12 = f32[3,1024]{1,0:T(4,128)S(1)} collective-permute-done((f32[3,1024]{1,0:T(4,128)S(1)}, f32[3,1024]{1,0:T(4,128)S(1)}, u32[]{:S(2)}, u32[]{:S(2)}) %collective-permute-start.12) | collective-permute-done | bytes 12320 | tf_op jit(solution)/shard_map/ppermute | solution.py:559
  55.0 0.0 collective-permute-done.11
  55.0 1.1 %collective-permute-done.10 = f32[3,1024]{1,0:T(4,128)S(1)} collective-permute-done((f32[3,1024]{1,0:T(4,128)S(1)}, f32[3,1024]{1,0:T(4,128)S(1)}, u32[]{:S(2)}, u32[]{:S(2)}) %collective-permute-start.10) | collective-permute-done | bytes 12320 | tf_op jit(solution)/shard_map/ppermute | solution.py:559
  56.1 1.6 %collective-permute-start.13 = (f32[3,1024]{1,0:T(4,128)S(1)}, f32[3,1024]{1,0:T(4,128)S(1)}, u32[]{:S(2)}, u32[]{:S(2)}) collective-permute-start(f32[3,1024]{1,0:T(4,128)S(1)} %add_add_fusion.a_ref), channel_id=1, source_target_pairs={{0,16},{4,20},{8,24},{12,28},{16,0},{20,4},{24,8},{28,12},{1,17},{... | collective-permute-start | bytes 36872 | tf_op jit(solution)/shard_map/ppermute | solution.py:559
  57.6 1.0 %writing.3 = bf16[256,2048]{1,0:T(8,128)(2,1)} custom-call(bf16[256,1024]{1,0:T(8,128)(2,1)S(1)} %get-tuple-element.72.refs_0_, bf16[256,1024]{1,0:T(8,128)(2,1)S(1)} %get-tuple-element.78.refs_1_), custom_call_target="tpu_custom_call" | custom-call | bytes 2097152 | tf_op jit(solution)/shard_map/writing/pallas_call | solution.py:595
  58.6 1.3 %collective-permute-done.13.b_ref = f32[3,1024]{1,0:T(4,128)S(1)} collective-permute-done((f32[3,1024]{1,0:T(4,128)S(1)}, f32[3,1024]{1,0:T(4,128)S(1)}, u32[]{:S(2)}, u32[]{:S(2)}) %collective-permute-start.13) | collective-permute-done | bytes 12320 | tf_op jit(solution)/shard_map/ppermute | solution.py:559
  59.9 0.6 %closing.1 = (f32[1,2048]{1,0:T(1,128)}, f32[1,32]{1,0:T(1,128)}) custom-call(f32[3,1024]{1,0:T(4,128)S(1)} %add_add_fusion.a_ref, f32[3,1024]{1,0:T(4,128)S(1)} %collective-permute-done.13.b_ref), custom_call_target="tpu_custom_call" | custom-call | tf_op jit(solution)/shard_map/closing/pallas_call | solution.py:783
  (7 shorter events, 0.1 us)
Async XLA Ops:
  3.9 12.8 %collective-permute-start = (bf16[272,512]{1,0:T(8,128)(2,1)S(1)}, bf16[272,512]{1,0:T(8,128)(2,1)S(1)}, u32[]{:S(2)}, u32[]{:S(2)}) collective-permute-start(bf16[272,512]{1,0:T(8,128)(2,1)S(1)} %get-tuple-element.44), channel_id=1, source_target_pairs={{4,8},{8,4},{5,9},{9,5},{6,10},{10,6},{7,11},{11,7},{20,24},{24,20... | collective-permute-start | bytes 835592 | tf_op jit(solution)/shard_map/ppermute | solution.py:675
  4.6 13.1 %collective-permute-start.2 = (bf16[272,512]{1,0:T(8,128)(2,1)S(1)}, bf16[272,512]{1,0:T(8,128)(2,1)S(1)}, u32[]{:S(2)}, u32[]{:S(2)}) collective-permute-start(bf16[272,512]{1,0:T(8,128)(2,1)S(1)} %get-tuple-element.44), channel_id=1, source_target_pairs={{0,4},{12,8},{4,0},{8,12},{1,5},{13,9},{5,1},{9,13},{2,6},{14,10},... | collective-permute-start | bytes 835592 | tf_op jit(solution)/shard_map/ppermute | solution.py:674
  10.5 12.7 %collective-permute-start.5 = (bf16[128,1024]{1,0:T(8,128)(2,1)S(1)}, bf16[128,1024]{1,0:T(8,128)(2,1)S(1)}, u32[]{:S(2)}, u32[]{:S(2)}) collective-permute-start(bf16[128,1024]{1,0:T(8,128)(2,1)S(1)} %get-tuple-element.58), channel_id=1, source_target_pairs={{0,4},{12,8},{1,5},{13,9},{2,6},{14,10},{3,7},{15,11},{16,20},{28,... | collective-permute-start | bytes 786440 | tf_op jit(solution)/shard_map/ppermute | solution.py:690
  16.7 11.4 %collective-permute-start.1 = (bf16[144,1024]{1,0:T(8,128)(2,1)S(1)}, bf16[144,1024]{1,0:T(8,128)(2,1)S(1)}, u32[]{:S(2)}, u32[]{:S(2)}) collective-permute-start(bf16[144,1024]{1,0:T(8,128)(2,1)S(1)} %merge.1), channel_id=1, source_target_pairs={{0,4},{12,8},{4,0},{8,12},{1,5},{13,9},{5,1},{9,13},{2,6},{14,10},... | collective-permute-start | bytes 884744 | tf_op jit(solution)/shard_map/ppermute | solution.py:687
  17.6 6.3 %collective-permute-start.4 = (bf16[272,512]{1,0:T(8,128)(2,1)S(1)}, bf16[272,512]{1,0:T(8,128)(2,1)S(1)}, u32[]{:S(2)}, u32[]{:S(2)}) collective-permute-start(bf16[272,512]{1,0:T(8,128)(2,1)S(1)} %collective-permute-done.2.refs_0_.refs_3_), channel_id=1, source_target_pairs={{4,8},{8,4},{5,9},{9,5},{6,10},{10,6},{7,11},{11,7},{20,24},{24,20... | collective-permute-start | bytes 835592 | tf_op jit(solution)/shard_map/ppermute | solution.py:677
  23.3 5.7 %collective-permute-start.8 = (bf16[128,1024]{1,0:T(8,128)(2,1)S(1)}, bf16[128,1024]{1,0:T(8,128)(2,1)S(1)}, u32[]{:S(2)}, u32[]{:S(2)}) collective-permute-start(bf16[128,1024]{1,0:T(8,128)(2,1)S(1)} %chain.5), channel_id=1, source_target_pairs={{4,8},{8,4},{5,9},{9,5},{6,10},{10,6},{7,11},{11,7},{20,24},{24,20... | collective-permute-start | bytes 786440 | tf_op jit(solution)/shard_map/ppermute | solution.py:693
  23.9 12.4 %collective-permute-start.6 = (bf16[272,512]{1,0:T(8,128)(2,1)S(1)}, bf16[272,512]{1,0:T(8,128)(2,1)S(1)}, u32[]{:S(2)}, u32[]{:S(2)}) collective-permute-start(bf16[272,512]{1,0:T(8,128)(2,1)S(1)} %collective-permute-done.4.refs_2_.refs_1_.refs_5_), channel_id=1, source_target_pairs={{4,0},{8,12},{5,1},{9,13},{6,2},{10,14},{7,3},{11,15},{20,16},{24,... | collective-permute-start | bytes 835592 | tf_op jit(solution)/shard_map/ppermute | solution.py:694
  28.1 8.3 %copy-start = (bf16[1,256,2048]{2,1,0:T(8,128)(2,1)S(1)}, bf16[1,256,2048]{2,1,0:T(8,128)(2,1)}, u32[]{:S(2)}) copy-start(bf16[1,256,2048]{2,1,0:T(8,128)(2,1)} %param.13) | copy-start | bytes 3145732
  28.1 8.3 %copy-start.1 = (bf16[1,256,256]{2,1,0:T(8,128)(2,1)S(1)}, bf16[1,256,256]{2,1,0:T(8,128)(2,1)}, u32[]{:S(2)}) copy-start(bf16[1,256,256]{2,1,0:T(8,128)(2,1)} %param.14) | copy-start | bytes 393220
  28.1 8.3 %copy-start.2 = (bf16[1,256,256]{2,1,0:T(8,128)(2,1)S(1)}, bf16[1,256,256]{2,1,0:T(8,128)(2,1)}, u32[]{:S(2)}) copy-start(bf16[1,256,256]{2,1,0:T(8,128)(2,1)} %param.15) | copy-start | bytes 393220
  28.1 11.1 %collective-permute-start.3 = (bf16[128,1024]{1,0:T(8,128)(2,1)S(1)}, bf16[128,1024]{1,0:T(8,128)(2,1)S(1)}, u32[]{:S(2)}, u32[]{:S(2)}) collective-permute-start(bf16[128,1024]{1,0:T(8,128)(2,1)S(1)} %chain.4), channel_id=1, source_target_pairs={{4,8},{8,4},{5,9},{9,5},{6,10},{10,6},{7,11},{11,7},{20,24},{24,20... | collective-permute-start | bytes 786440 | tf_op jit(solution)/shard_map/ppermute | solution.py:738
  28.9 7.5 %copy-start.4 = (s32[1,1024]{1,0:T(1,128)S(1)}, s32[1,1024]{1,0:T(1,128)}, u32[]{:S(2)}) copy-start(s32[1,1024]{1,0:T(1,128)} %docs_ref.7) | copy-start | bytes 12292
  29.0 14.4 %collective-permute-start.9 = (bf16[128,1024]{1,0:T(8,128)(2,1)S(1)}, bf16[128,1024]{1,0:T(8,128)(2,1)S(1)}, u32[]{:S(2)}, u32[]{:S(2)}) collective-permute-start(bf16[128,1024]{1,0:T(8,128)(2,1)S(1)} %chain.7), channel_id=1, source_target_pairs={{8,12},{4,0},{9,13},{5,1},{10,14},{6,2},{11,15},{7,3},{24,28},{20,... | collective-permute-start | bytes 786440 | tf_op jit(solution)/shard_map/ppermute | solution.py:738
  39.2 8.3 %collective-permute-start.7 = (bf16[128,1024]{1,0:T(8,128)(2,1)S(1)}, bf16[128,1024]{1,0:T(8,128)(2,1)S(1)}, u32[]{:S(2)}, u32[]{:S(2)}) collective-permute-start(bf16[128,1024]{1,0:T(8,128)(2,1)S(1)} %chain.6), channel_id=1, source_target_pairs={{8,12},{4,0},{9,13},{5,1},{10,14},{6,2},{11,15},{7,3},{24,28},{20,... | collective-permute-start | bytes 786440 | tf_op jit(solution)/shard_map/ppermute | solution.py:738
  43.3 1.0 %copy-start.3 = (bf16[1,256,256]{2,1,0:T(8,128)(2,1)S(1)}, bf16[1,256,256]{2,1,0:T(8,128)(2,1)}, u32[]{:S(2)}) copy-start(bf16[1,256,256]{2,1,0:T(8,128)(2,1)} %param.20) | copy-start | bytes 393220
  43.3 1.0 %copy-start.5 = (f32[2048]{0:T(1024)S(1)}, f32[2048]{0:T(1024)}, u32[]{:S(2)}) copy-start(f32[2048]{0:T(1024)} %param.25) | copy-start | bytes 24580
  49.4 5.6 %collective-permute-start.12 = (f32[3,1024]{1,0:T(4,128)S(1)}, f32[3,1024]{1,0:T(4,128)S(1)}, u32[]{:S(2)}, u32[]{:S(2)}) collective-permute-start(f32[3,1024]{1,0:T(4,128)S(1)} %get-tuple-element.79), channel_id=1, source_target_pairs={{0,12},{4,8},{8,4},{12,0},{16,28},{20,24},{24,20},{28,16},{1,13},{... | collective-permute-start | bytes 36872 | tf_op jit(solution)/shard_map/ppermute | solution.py:559
  49.6 5.3 %collective-permute-start.11 = (f32[3,1024]{1,0:T(4,128)S(1)}, f32[3,1024]{1,0:T(4,128)S(1)}, u32[]{:S(2)}, u32[]{:S(2)}) collective-permute-start(f32[3,1024]{1,0:T(4,128)S(1)} %get-tuple-element.79), channel_id=1, source_target_pairs={{0,8},{4,12},{8,0},{12,4},{16,24},{20,28},{24,16},{28,20},{1,9},{5... | collective-permute-start | bytes 36872 | tf_op jit(solution)/shard_map/ppermute | solution.py:559
  52.3 3.7 %collective-permute-start.10 = (f32[3,1024]{1,0:T(4,128)S(1)}, f32[3,1024]{1,0:T(4,128)S(1)}, u32[]{:S(2)}, u32[]{:S(2)}) collective-permute-start(f32[3,1024]{1,0:T(4,128)S(1)} %get-tuple-element.79), channel_id=1, source_target_pairs={{0,4},{4,0},{8,12},{12,8},{16,20},{20,16},{24,28},{28,24},{1,5},{5... | collective-permute-start | bytes 36872 | tf_op jit(solution)/shard_map/ppermute | solution.py:559
  56.1 3.8 %collective-permute-start.13 = (f32[3,1024]{1,0:T(4,128)S(1)}, f32[3,1024]{1,0:T(4,128)S(1)}, u32[]{:S(2)}, u32[]{:S(2)}) collective-permute-start(f32[3,1024]{1,0:T(4,128)S(1)} %add_add_fusion.a_ref), channel_id=1, source_target_pairs={{0,16},{4,20},{8,24},{12,28},{16,0},{20,4},{24,8},{28,12},{1,17},{... | collective-permute-start | bytes 36872 | tf_op jit(solution)/shard_map/ppermute | solution.py:559

commit v19 on v17

--- a/solution.py
+++ b/solution.py
@@ -120,28 +120,30 @@
     kv_ref[:rows, :kv_width] = k_ref[...]
     kv_ref[:rows, kv_width:] = v_ref[...]
     kv_ref[rows:, :] = jnp.zeros((EXTRA, 2 * kv_width), BF16)
-    triangle = jnp.where(lower_triangle(stretch), 1.0, 0.0)
     slope = jnp.exp(as_column(log_ref[...]))
     bias = as_column(bias_ref[...])
     lane = lax.broadcasted_iota(jnp.int32, (heads, 8), 1)
     ends = jnp.zeros((heads, 8), F32)
     loads = []
     projs = []
+    raw = jnp.concatenate([dt_ref[:, :stretch] + bias, dt_ref[:, stretch:] + bias], axis=0)
+    dt_both = jnp.maximum(raw, 0.0) + jnp.log1p(jnp.exp(-jnp.abs(raw)))
+    rate = -dt_both * jnp.concatenate([slope, slope], axis=0)
+    hi, lo = parts(rate)
+    rest = (rate - hi.astype(F32) - lo.astype(F32)).astype(BF16)
+    triangle = jnp.where(lower_triangle(stretch), 1.0, 0.0).astype(BF16)
+    cum_both = dot_nt(
+        jnp.concatenate([hi, lo, rest], axis=1), jnp.concatenate([triangle] * 3, axis=1)
+    )
+    grown = jnp.exp(cum_both)
+    load_both = jnp.exp(-cum_both) * dt_both
     for half in range(2):
         block = own_block(index, count, half)
         sl = slice(half * stretch, (half + 1) * stretch)
-        raw = dt_ref[:, sl] + bias
-        dt = jnp.maximum(raw, 0.0) + jnp.log1p(jnp.exp(-jnp.abs(raw)))
-        cum = lax.dot_general(
-            -dt * slope,
-            triangle,
-            (((1,), (1,)), ((), ())),
-            precision=lax.Precision.HIGHEST,
-            preferred_element_type=F32,
-        )
-        ec_ref[:, sl] = jnp.exp(cum)
-        loads.append(jnp.exp(-cum) * dt)
-        final = jnp.exp(cum[:, stretch - 1 :])
+        here = slice(half * heads, (half + 1) * heads)
+        ec_ref[:, sl] = grown[here]
+        loads.append(load_both[here])
+        final = grown[here, stretch - 1 :]
         row = doc_row(docs_ref, block, stretch)
         last = row[:, stretch - 1 :]
         kept = jnp.where(last == prior_doc(docs_ref, block, stretch), 1.0, 0.0)

time: 60.5 us -> 60.3 us (level)
  no operation moved by 1% of the time
where the time goes in v19:
time: 60.3 us; the launch traced here: 60 us
  starting transfers between devices  21.4 us (35%)
  Pallas kernels  19.3 us (32%)
  waiting for transfers between devices  18.4 us (31%)
  between operations  0.87 us (1%)
    ppermute x1, waiting for transfers between devices, body(): farther = lax.ppermute(beyond, 'ctx', outward)  6.07 us
    ppermute x4, starting transfers between devices, exchange(): return lax.ppermute(part, axes, [(d, d ^ shift) for d in range(size)])  6.04 us
    ppermute x1, starting transfers between devices, body(): near = lax.ppermute(kv, 'ctx', inward + outward)  5.96 us
    pallas_call x2, Pallas kernels, body(): pl.pallas_call(functools.partial(attention_kernel, count, per_kv, stack,...  5.58 us
    ppermute x1, waiting for transfers between devices, body(): got[0].append(lax.ppermute(send[0], 'ctx', [(0, 1), (3, 2)]))  4.94 us
    pallas_call x1, Pallas kernels, body(): pl.pallas_call(functools.partial(local_kernel, count, groups), out_shape=...  4.19 us
    pallas_call x2, Pallas kernels, body(): pl.pallas_call(functools.partial(final_kernel, count, g, groups, loss_sca...  3.72 us
    ppermute x3, starting transfers between devices, body(): got[g].append(lax.ppermute(send[g], 'ctx', pairs))  3.51 us
  transfers between devices with their start and end apart: 14, of which 8 were waited for; matrix products, arithmetic and copies ran while one was open for 0% of the time, Pallas kernels for 23%

profile of v19, /device:TPU:0, one launch (start us, length us, event | category | flops | bytes accessed | tf_op | source)
XLA Modules:
  0.0 60.0 jit_solution(1712099125987131271)
XLA Ops:
  0.6 3.1 %opening.1 = (bf16[272,512]{1,0:T(8,128)(2,1)S(1)}, f32[32,256]{1,0:T(8,128)S(1)}, bf16[256,1024]{1,0:T(8,128)(2,1)S(1)}, bf16[256,1024]{1,0:T(8,128)(2,1)S(1)},...) custom-call(s32[1,1024]{1,0:T(1,128)} %docs_ref.7, ...), custom_call_target="tpu_custom_call" | custom-call | flops 268435456 | bytes 4194304 | tf_op jit(solution)/shard_map/opening/pallas_call | solution.py:610
  3.8 0.7 %collective-permute-start.3 = (bf16[272,512]{1,0:T(8,128)(2,1)S(1)}, bf16[272,512]{1,0:T(8,128)(2,1)S(1)}, u32[]{:S(2)}, u32[]{:S(2)}) collective-permute-start(bf16[272,512]{1,0:T(8,128)(2,1)S(1)} %get-tuple-element.45), channel_id=1, source_target_pairs={{4,8},{8,4},{5,9},{9,5},{6,10},{10,6},{7,11},{11,7},{20,24},{24,20... | collective-permute-start | bytes 835592 | tf_op jit(solution)/shard_map/ppermute | solution.py:677
  4.5 6.0 %collective-permute-start.1 = (bf16[272,512]{1,0:T(8,128)(2,1)S(1)}, bf16[272,512]{1,0:T(8,128)(2,1)S(1)}, u32[]{:S(2)}, u32[]{:S(2)}) collective-permute-start(bf16[272,512]{1,0:T(8,128)(2,1)S(1)} %get-tuple-element.45), channel_id=1, source_target_pairs={{0,4},{12,8},{4,0},{8,12},{1,5},{13,9},{5,1},{9,13},{2,6},{14,10},... | collective-permute-start | bytes 835592 | tf_op jit(solution)/shard_map/ppermute | solution.py:676
  10.4 1.9 %collective-permute-start = (bf16[128,1024]{1,0:T(8,128)(2,1)S(1)}, bf16[128,1024]{1,0:T(8,128)(2,1)S(1)}, u32[]{:S(2)}, u32[]{:S(2)}) collective-permute-start(bf16[128,1024]{1,0:T(8,128)(2,1)S(1)} %get-tuple-element.41), channel_id=1, source_target_pairs={{0,4},{12,8},{1,5},{13,9},{2,6},{14,10},{3,7},{15,11},{16,20},{28,... | collective-permute-start | bytes 786440 | tf_op jit(solution)/shard_map/ppermute | solution.py:692
  12.4 4.2 %local.1 = (f32[256,1024]{1,0:T(8,128)S(1)}, f32[256,1024]{1,0:T(8,128)S(1)}, f32[256,1024]{1,0:T(8,128)S(1)}, f32[256,1024]{1,0:T(8,128)S(1)}, f32[256,1024]{1,0:T(8,128)S(1)}, /*index=5*/f32[256,1024]{1,0:T(8,128)S(1)}) custom-call(s32[1,1024]{1,0:T(1,128)} %docs_ref.7, bf16[256,2048]{1,0:T(8,128)(2,1)} %bitcast.32, bf16[256,2048]{1,0:T(8,128)(2,1)} %bitcast.33, ...), custom_call_target="tpu_custom_call" | custom-call | flops 134217728 | bytes 8388608 | tf_op jit(solution)/shard_map/local/pallas_call | solution.py:642
  16.6 0.0 collective-permute-done.3.refs_0_.kv_ref.refs_1_.refs_4_
  16.6 0.6 %collective-permute-start.6 = (bf16[144,1024]{1,0:T(8,128)(2,1)S(1)}, bf16[144,1024]{1,0:T(8,128)(2,1)S(1)}, u32[]{:S(2)}, u32[]{:S(2)}) collective-permute-start(bf16[144,1024]{1,0:T(8,128)(2,1)S(1)} %merge.1), channel_id=1, source_target_pairs={{0,4},{12,8},{4,0},{8,12},{1,5},{13,9},{5,1},{9,13},{2,6},{14,10},... | collective-permute-start | bytes 884744 | tf_op jit(solution)/shard_map/ppermute | solution.py:689
  17.2 0.3 collective-permute-done.1.refs_0_.refs_3_
  17.5 0.7 %collective-permute-start.4 = (bf16[272,512]{1,0:T(8,128)(2,1)S(1)}, bf16[272,512]{1,0:T(8,128)(2,1)S(1)}, u32[]{:S(2)}, u32[]{:S(2)}) collective-permute-start(bf16[272,512]{1,0:T(8,128)(2,1)S(1)} %collective-permute-done.1.refs_0_.refs_3_), channel_id=1, source_target_pairs={{4,8},{8,4},{5,9},{9,5},{6,10},{10,6},{7,11},{11,7},{20,24},{24,20... | collective-permute-start | bytes 835592 | tf_op jit(solution)/shard_map/ppermute | solution.py:679
  18.2 4.9 %collective-permute-done.got_ref.refs_0_ = bf16[128,1024]{1,0:T(8,128)(2,1)S(1)} collective-permute-done((bf16[128,1024]{1,0:T(8,128)(2,1)S(1)}, bf16[128,1024]{1,0:T(8,128)(2,1)S(1)}, u32[]{:S(2)}, u32[]{:S(2)}) %collective-permute-start) | collective-permute-done | bytes 262176 | tf_op jit(solution)/shard_map/ppermute | solution.py:692
  23.1 0.7 %collective-permute-start.2 = (bf16[128,1024]{1,0:T(8,128)(2,1)S(1)}, bf16[128,1024]{1,0:T(8,128)(2,1)S(1)}, u32[]{:S(2)}, u32[]{:S(2)}) collective-permute-start(bf16[128,1024]{1,0:T(8,128)(2,1)S(1)} %chain.4), channel_id=1, source_target_pairs={{4,8},{8,4},{5,9},{9,5},{6,10},{10,6},{7,11},{11,7},{20,24},{24,20... | collective-permute-start | bytes 786440 | tf_op jit(solution)/shard_map/ppermute | solution.py:695
  23.8 0.0 collective-permute-done.4.refs_1_.refs_2_.refs_5_
  23.8 1.3 %collective-permute-start.8 = (bf16[272,512]{1,0:T(8,128)(2,1)S(1)}, bf16[272,512]{1,0:T(8,128)(2,1)S(1)}, u32[]{:S(2)}, u32[]{:S(2)}) collective-permute-start(bf16[272,512]{1,0:T(8,128)(2,1)S(1)} %collective-permute-done.4.refs_1_.refs_2_.refs_5_), channel_id=1, source_target_pairs={{4,0},{8,12},{5,1},{9,13},{6,2},{10,14},{7,3},{11,15},{20,16},{24,... | collective-permute-start | bytes 835592 | tf_op jit(solution)/shard_map/ppermute | solution.py:696
  25.1 2.9 %collective-permute-done.6.got_ref.refs_3_.refs_6_.refs_0_ = bf16[144,1024]{1,0:T(8,128)(2,1)S(1)} collective-permute-done((bf16[144,1024]{1,0:T(8,128)(2,1)S(1)}, bf16[144,1024]{1,0:T(8,128)(2,1)S(1)}, u32[]{:S(2)}, u32[]{:S(2)}) %collective-permute-start.6) | collective-permute-done | bytes 294944 | tf_op jit(solution)/shard_map/ppermute | solution.py:689
  28.0 0.0 copy-start
  28.0 0.0 copy-start.1
  28.0 0.8 %collective-permute-start.7 = (bf16[128,1024]{1,0:T(8,128)(2,1)S(1)}, bf16[128,1024]{1,0:T(8,128)(2,1)S(1)}, u32[]{:S(2)}, u32[]{:S(2)}) collective-permute-start(bf16[128,1024]{1,0:T(8,128)(2,1)S(1)} %chain.6), channel_id=1, source_target_pairs={{4,8},{8,4},{5,9},{9,5},{6,10},{10,6},{7,11},{11,7},{20,24},{24,20... | collective-permute-start | bytes 786440 | tf_op jit(solution)/shard_map/ppermute | solution.py:740
  28.8 0.0 collective-permute-done.2.got_ref.refs_1_
  28.8 0.0 copy-start.4
  28.9 1.3 %collective-permute-start.5 = (bf16[128,1024]{1,0:T(8,128)(2,1)S(1)}, bf16[128,1024]{1,0:T(8,128)(2,1)S(1)}, u32[]{:S(2)}, u32[]{:S(2)}) collective-permute-start(bf16[128,1024]{1,0:T(8,128)(2,1)S(1)} %chain.5), channel_id=1, source_target_pairs={{8,12},{4,0},{9,13},{5,1},{10,14},{6,2},{11,15},{7,3},{24,28},{20,... | collective-permute-start | bytes 786440 | tf_op jit(solution)/shard_map/ppermute | solution.py:740
  30.2 6.1 %collective-permute-done.8.refs_4_.refs_7_ = bf16[272,512]{1,0:T(8,128)(2,1)S(1)} collective-permute-done((bf16[272,512]{1,0:T(8,128)(2,1)S(1)}, bf16[272,512]{1,0:T(8,128)(2,1)S(1)}, u32[]{:S(2)}, u32[]{:S(2)}) %collective-permute-start.8) | collective-permute-done | bytes 278560 | tf_op jit(solution)/shard_map/ppermute | solution.py:696
  36.2 0.0 copy-done
  36.2 0.0 copy-done.1
  36.2 0.0 copy-done.2
  36.2 0.0 copy-done.4
  36.3 2.8 %attention.2.refs_0_.teacher_ref = bf16[256,1024]{1,0:T(8,128)(2,1)S(1)} custom-call(s32[1,1024]{1,0:T(1,128)S(1)} %copy-done.4, bf16[256,2048]{1,0:T(8,128)(2,1)S(1)} %bitcast.18, bf16[256,256]{1,0:T(8,128)(2,1)S(1)} %bitcast.21, bf16[256,256]{1,0:T(8,128)(2,1)S(1)} %bitcast.24, bf16[272,512]{1,0:T(8,128)(2,1)S(1)} %collective-permute-done.1.refs_0_.refs_3_, ...), custom_call_target="tpu_custom_call" | custom-call | flops 603979776 | bytes 2097152 | tf_op jit(solution)/shard_map/attention/pallas_call | solution.py:707
  39.0 0.0 collective-permute-done.7.got_ref.refs_1_
  39.1 0.0 copy-start.3
  39.1 0.0 copy-start.5
  39.1 1.4 %collective-permute-start.9 = (bf16[128,1024]{1,0:T(8,128)(2,1)S(1)}, bf16[128,1024]{1,0:T(8,128)(2,1)S(1)}, u32[]{:S(2)}, u32[]{:S(2)}) collective-permute-start(bf16[128,1024]{1,0:T(8,128)(2,1)S(1)} %chain.7), channel_id=1, source_target_pairs={{8,12},{4,0},{9,13},{5,1},{10,14},{6,2},{11,15},{7,3},{24,28},{20,... | collective-permute-start | bytes 786440 | tf_op jit(solution)/shard_map/ppermute | solution.py:740
  40.5 2.8 %attention.3.refs_1_.teacher_ref = bf16[256,1024]{1,0:T(8,128)(2,1)S(1)} custom-call(s32[1,1024]{1,0:T(1,128)S(1)} %copy-done.4, bf16[256,2048]{1,0:T(8,128)(2,1)S(1)} %bitcast.19, bf16[256,256]{1,0:T(8,128)(2,1)S(1)} %bitcast.22, bf16[256,256]{1,0:T(8,128)(2,1)S(1)} %bitcast.25, bf16[272,512]{1,0:T(8,128)(2,1)S(1)} %collective-permute-done.1.refs_0_.refs_3_, ...), custom_call_target="tpu_custom_call" | custom-call | flops 603979776 | bytes 2097152 | tf_op jit(solution)/shard_map/attention/pallas_call | solution.py:707
  43.3 0.0 collective-permute-done.5.refs_2_
  43.4 0.0 copy-done.3
  43.4 0.0 copy-done.5
  43.4 1.9 %final.2 = (bf16[256,1024]{1,0:T(8,128)(2,1)S(1)}, f32[3,1024]{1,0:T(4,128)S(1)}) custom-call(f32[256,1024]{1,0:T(8,128)S(1)} %get-tuple-element.64.pre_ref, f32[256,1024]{1,0:T(8,128)S(1)} %get-tuple-element.65.reach_ref, f32[256,1024]{1,0:T(8,128)S(1)} %get-tuple-element.66.sx_ref, bf16[256,256]{1,0:T(8,128)(2,1)S(1)} %bitcast.27, ...), custom_call_target="tpu_custom_call" | custom-call | flops 67108864 | bytes 5242880 | tf_op jit(solution)/shard_map/final/pallas_call | solution.py:746
  45.2 2.3 %collective-permute-done.9.refs_2_ = bf16[128,1024]{1,0:T(8,128)(2,1)S(1)} collective-permute-done((bf16[128,1024]{1,0:T(8,128)(2,1)S(1)}, bf16[128,1024]{1,0:T(8,128)(2,1)S(1)}, u32[]{:S(2)}, u32[]{:S(2)}) %collective-permute-start.9) | collective-permute-done | bytes 262176 | tf_op jit(solution)/shard_map/ppermute | solution.py:740
  47.5 1.9 %final.3 = (bf16[256,1024]{1,0:T(8,128)(2,1)S(1)}, f32[3,1024]{1,0:T(4,128)S(1)}) custom-call(f32[256,1024]{1,0:T(8,128)S(1)} %get-tuple-element.69.pre_ref, f32[256,1024]{1,0:T(8,128)S(1)} %get-tuple-element.70.reach_ref, f32[256,1024]{1,0:T(8,128)S(1)} %get-tuple-element.71.sx_ref, bf16[256,256]{1,0:T(8,128)(2,1)S(1)} %bitcast.28, ...), custom_call_target="tpu_custom_call" | custom-call | flops 67108864 | bytes 5242880 | tf_op jit(solution)/shard_map/final/pallas_call | solution.py:746
  49.4 0.3 collective-permute-start.12
  49.7 1.7 %collective-permute-start.11 = (f32[3,1024]{1,0:T(4,128)S(1)}, f32[3,1024]{1,0:T(4,128)S(1)}, u32[]{:S(2)}, u32[]{:S(2)}) collective-permute-start(f32[3,1024]{1,0:T(4,128)S(1)} %get-tuple-element.75), channel_id=1, source_target_pairs={{0,8},{4,12},{8,0},{12,4},{16,24},{20,28},{24,16},{28,20},{1,9},{5... | collective-permute-start | bytes 36872 | tf_op jit(solution)/shard_map/ppermute | solution.py:561
  51.3 2.5 %collective-permute-start.10 = (f32[3,1024]{1,0:T(4,128)S(1)}, f32[3,1024]{1,0:T(4,128)S(1)}, u32[]{:S(2)}, u32[]{:S(2)}) collective-permute-start(f32[3,1024]{1,0:T(4,128)S(1)} %get-tuple-element.75), channel_id=1, source_target_pairs={{0,4},{4,0},{8,12},{12,8},{16,20},{20,16},{24,28},{28,24},{1,5},{5... | collective-permute-start | bytes 36872 | tf_op jit(solution)/shard_map/ppermute | solution.py:561
  53.8 1.1 %collective-permute-done.12 = f32[3,1024]{1,0:T(4,128)S(1)} collective-permute-done((f32[3,1024]{1,0:T(4,128)S(1)}, f32[3,1024]{1,0:T(4,128)S(1)}, u32[]{:S(2)}, u32[]{:S(2)}) %collective-permute-start.12) | collective-permute-done | bytes 12320 | tf_op jit(solution)/shard_map/ppermute | solution.py:561
  55.0 0.0 collective-permute-done.11
  55.0 0.6 collective-permute-done.10
  55.5 1.6 %collective-permute-start.13 = (f32[3,1024]{1,0:T(4,128)S(1)}, f32[3,1024]{1,0:T(4,128)S(1)}, u32[]{:S(2)}, u32[]{:S(2)}) collective-permute-start(f32[3,1024]{1,0:T(4,128)S(1)} %add_add_fusion.a_ref), channel_id=1, source_target_pairs={{0,16},{4,20},{8,24},{12,28},{16,0},{20,4},{24,8},{28,12},{1,17},{... | collective-permute-start | bytes 36872 | tf_op jit(solution)/shard_map/ppermute | solution.py:561
  57.1 1.0 %writing.2 = bf16[256,2048]{1,0:T(8,128)(2,1)} custom-call(bf16[256,1024]{1,0:T(8,128)(2,1)S(1)} %attention.2.refs_0_.teacher_ref, bf16[256,1024]{1,0:T(8,128)(2,1)S(1)} %attention.3.refs_1_.teacher_ref), custom_call_target="tpu_custom_call" | custom-call | bytes 2097152 | tf_op jit(solution)/shard_map/writing/pallas_call | solution.py:597
  58.1 1.0 %writing.3 = bf16[256,2048]{1,0:T(8,128)(2,1)} custom-call(bf16[256,1024]{1,0:T(8,128)(2,1)S(1)} %get-tuple-element.68.refs_0_, bf16[256,1024]{1,0:T(8,128)(2,1)S(1)} %get-tuple-element.74.refs_1_), custom_call_target="tpu_custom_call" | custom-call | bytes 2097152 | tf_op jit(solution)/shard_map/writing/pallas_call | solution.py:597
  59.1 0.2 collective-permute-done.13.b_ref
  59.3 0.6 %closing.1 = (f32[1,2048]{1,0:T(1,128)}, f32[1,32]{1,0:T(1,128)}) custom-call(f32[3,1024]{1,0:T(4,128)S(1)} %add_add_fusion.a_ref, f32[3,1024]{1,0:T(4,128)S(1)} %collective-permute-done.13.b_ref), custom_call_target="tpu_custom_call" | custom-call | tf_op jit(solution)/shard_map/closing/pallas_call | solution.py:782
  (7 shorter events, 0.1 us)
Async XLA Ops:
  3.8 12.8 %collective-permute-start.3 = (bf16[272,512]{1,0:T(8,128)(2,1)S(1)}, bf16[272,512]{1,0:T(8,128)(2,1)S(1)}, u32[]{:S(2)}, u32[]{:S(2)}) collective-permute-start(bf16[272,512]{1,0:T(8,128)(2,1)S(1)} %get-tuple-element.45), channel_id=1, source_target_pairs={{4,8},{8,4},{5,9},{9,5},{6,10},{10,6},{7,11},{11,7},{20,24},{24,20... | collective-permute-start | bytes 835592 | tf_op jit(solution)/shard_map/ppermute | solution.py:677
  4.5 13.1 %collective-permute-start.1 = (bf16[272,512]{1,0:T(8,128)(2,1)S(1)}, bf16[272,512]{1,0:T(8,128)(2,1)S(1)}, u32[]{:S(2)}, u32[]{:S(2)}) collective-permute-start(bf16[272,512]{1,0:T(8,128)(2,1)S(1)} %get-tuple-element.45), channel_id=1, source_target_pairs={{0,4},{12,8},{4,0},{8,12},{1,5},{13,9},{5,1},{9,13},{2,6},{14,10},... | collective-permute-start | bytes 835592 | tf_op jit(solution)/shard_map/ppermute | solution.py:676
  10.4 12.7 %collective-permute-start = (bf16[128,1024]{1,0:T(8,128)(2,1)S(1)}, bf16[128,1024]{1,0:T(8,128)(2,1)S(1)}, u32[]{:S(2)}, u32[]{:S(2)}) collective-permute-start(bf16[128,1024]{1,0:T(8,128)(2,1)S(1)} %get-tuple-element.41), channel_id=1, source_target_pairs={{0,4},{12,8},{1,5},{13,9},{2,6},{14,10},{3,7},{15,11},{16,20},{28,... | collective-permute-start | bytes 786440 | tf_op jit(solution)/shard_map/ppermute | solution.py:692
  16.6 11.4 %collective-permute-start.6 = (bf16[144,1024]{1,0:T(8,128)(2,1)S(1)}, bf16[144,1024]{1,0:T(8,128)(2,1)S(1)}, u32[]{:S(2)}, u32[]{:S(2)}) collective-permute-start(bf16[144,1024]{1,0:T(8,128)(2,1)S(1)} %merge.1), channel_id=1, source_target_pairs={{0,4},{12,8},{4,0},{8,12},{1,5},{13,9},{5,1},{9,13},{2,6},{14,10},... | collective-permute-start | bytes 884744 | tf_op jit(solution)/shard_map/ppermute | solution.py:689
  17.5 6.3 %collective-permute-start.4 = (bf16[272,512]{1,0:T(8,128)(2,1)S(1)}, bf16[272,512]{1,0:T(8,128)(2,1)S(1)}, u32[]{:S(2)}, u32[]{:S(2)}) collective-permute-start(bf16[272,512]{1,0:T(8,128)(2,1)S(1)} %collective-permute-done.1.refs_0_.refs_3_), channel_id=1, source_target_pairs={{4,8},{8,4},{5,9},{9,5},{6,10},{10,6},{7,11},{11,7},{20,24},{24,20... | collective-permute-start | bytes 835592 | tf_op jit(solution)/shard_map/ppermute | solution.py:679
  23.1 5.7 %collective-permute-start.2 = (bf16[128,1024]{1,0:T(8,128)(2,1)S(1)}, bf16[128,1024]{1,0:T(8,128)(2,1)S(1)}, u32[]{:S(2)}, u32[]{:S(2)}) collective-permute-start(bf16[128,1024]{1,0:T(8,128)(2,1)S(1)} %chain.4), channel_id=1, source_target_pairs={{4,8},{8,4},{5,9},{9,5},{6,10},{10,6},{7,11},{11,7},{20,24},{24,20... | collective-permute-start | bytes 786440 | tf_op jit(solution)/shard_map/ppermute | solution.py:695
  23.8 12.4 %collective-permute-start.8 = (bf16[272,512]{1,0:T(8,128)(2,1)S(1)}, bf16[272,512]{1,0:T(8,128)(2,1)S(1)}, u32[]{:S(2)}, u32[]{:S(2)}) collective-permute-start(bf16[272,512]{1,0:T(8,128)(2,1)S(1)} %collective-permute-done.4.refs_1_.refs_2_.refs_5_), channel_id=1, source_target_pairs={{4,0},{8,12},{5,1},{9,13},{6,2},{10,14},{7,3},{11,15},{20,16},{24,... | collective-permute-start | bytes 835592 | tf_op jit(solution)/shard_map/ppermute | solution.py:696
  28.0 8.2 %copy-start = (bf16[1,256,2048]{2,1,0:T(8,128)(2,1)S(1)}, bf16[1,256,2048]{2,1,0:T(8,128)(2,1)}, u32[]{:S(2)}) copy-start(bf16[1,256,2048]{2,1,0:T(8,128)(2,1)} %param.13) | copy-start | bytes 3145732
  28.0 8.2 %copy-start.1 = (bf16[1,256,256]{2,1,0:T(8,128)(2,1)S(1)}, bf16[1,256,256]{2,1,0:T(8,128)(2,1)}, u32[]{:S(2)}) copy-start(bf16[1,256,256]{2,1,0:T(8,128)(2,1)} %param.14) | copy-start | bytes 393220
  28.0 8.2 %copy-start.2 = (bf16[1,256,256]{2,1,0:T(8,128)(2,1)S(1)}, bf16[1,256,256]{2,1,0:T(8,128)(2,1)}, u32[]{:S(2)}) copy-start(bf16[1,256,256]{2,1,0:T(8,128)(2,1)} %param.15) | copy-start | bytes 393220
  28.0 11.0 %collective-permute-start.7 = (bf16[128,1024]{1,0:T(8,128)(2,1)S(1)}, bf16[128,1024]{1,0:T(8,128)(2,1)S(1)}, u32[]{:S(2)}, u32[]{:S(2)}) collective-permute-start(bf16[128,1024]{1,0:T(8,128)(2,1)S(1)} %chain.6), channel_id=1, source_target_pairs={{4,8},{8,4},{5,9},{9,5},{6,10},{10,6},{7,11},{11,7},{20,24},{24,20... | collective-permute-start | bytes 786440 | tf_op jit(solution)/shard_map/ppermute | solution.py:740
  28.8 7.4 %copy-start.4 = (s32[1,1024]{1,0:T(1,128)S(1)}, s32[1,1024]{1,0:T(1,128)}, u32[]{:S(2)}) copy-start(s32[1,1024]{1,0:T(1,128)} %docs_ref.7) | copy-start | bytes 12292
  28.9 14.5 %collective-permute-start.5 = (bf16[128,1024]{1,0:T(8,128)(2,1)S(1)}, bf16[128,1024]{1,0:T(8,128)(2,1)S(1)}, u32[]{:S(2)}, u32[]{:S(2)}) collective-permute-start(bf16[128,1024]{1,0:T(8,128)(2,1)S(1)} %chain.5), channel_id=1, source_target_pairs={{8,12},{4,0},{9,13},{5,1},{10,14},{6,2},{11,15},{7,3},{24,28},{20,... | collective-permute-start | bytes 786440 | tf_op jit(solution)/shard_map/ppermute | solution.py:740
  39.1 4.3 %copy-start.3 = (bf16[1,256,256]{2,1,0:T(8,128)(2,1)S(1)}, bf16[1,256,256]{2,1,0:T(8,128)(2,1)}, u32[]{:S(2)}) copy-start(bf16[1,256,256]{2,1,0:T(8,128)(2,1)} %param.20) | copy-start | bytes 393220
  39.1 4.3 %copy-start.5 = (f32[2048]{0:T(1024)S(1)}, f32[2048]{0:T(1024)}, u32[]{:S(2)}) copy-start(f32[2048]{0:T(1024)} %param.25) | copy-start | bytes 24580
  39.1 8.4 %collective-permute-start.9 = (bf16[128,1024]{1,0:T(8,128)(2,1)S(1)}, bf16[128,1024]{1,0:T(8,128)(2,1)S(1)}, u32[]{:S(2)}, u32[]{:S(2)}) collective-permute-start(bf16[128,1024]{1,0:T(8,128)(2,1)S(1)} %chain.7), channel_id=1, source_target_pairs={{8,12},{4,0},{9,13},{5,1},{10,14},{6,2},{11,15},{7,3},{24,28},{20,... | collective-permute-start | bytes 786440 | tf_op jit(solution)/shard_map/ppermute | solution.py:740
  49.4 5.6 %collective-permute-start.12 = (f32[3,1024]{1,0:T(4,128)S(1)}, f32[3,1024]{1,0:T(4,128)S(1)}, u32[]{:S(2)}, u32[]{:S(2)}) collective-permute-start(f32[3,1024]{1,0:T(4,128)S(1)} %get-tuple-element.75), channel_id=1, source_target_pairs={{0,12},{4,8},{8,4},{12,0},{16,28},{20,24},{24,20},{28,16},{1,13},{... | collective-permute-start | bytes 36872 | tf_op jit(solution)/shard_map/ppermute | solution.py:561
  49.7 5.3 %collective-permute-start.11 = (f32[3,1024]{1,0:T(4,128)S(1)}, f32[3,1024]{1,0:T(4,128)S(1)}, u32[]{:S(2)}, u32[]{:S(2)}) collective-permute-start(f32[3,1024]{1,0:T(4,128)S(1)} %get-tuple-element.75), channel_id=1, source_target_pairs={{0,8},{4,12},{8,0},{12,4},{16,24},{20,28},{24,16},{28,20},{1,9},{5... | collective-permute-start | bytes 36872 | tf_op jit(solution)/shard_map/ppermute | solution.py:561
  51.3 4.2 %collective-permute-start.10 = (f32[3,1024]{1,0:T(4,128)S(1)}, f32[3,1024]{1,0:T(4,128)S(1)}, u32[]{:S(2)}, u32[]{:S(2)}) collective-permute-start(f32[3,1024]{1,0:T(4,128)S(1)} %get-tuple-element.75), channel_id=1, source_target_pairs={{0,4},{4,0},{8,12},{12,8},{16,20},{20,16},{24,28},{28,24},{1,5},{5... | collective-permute-start | bytes 36872 | tf_op jit(solution)/shard_map/ppermute | solution.py:561
  55.5 3.8 %collective-permute-start.13 = (f32[3,1024]{1,0:T(4,128)S(1)}, f32[3,1024]{1,0:T(4,128)S(1)}, u32[]{:S(2)}, u32[]{:S(2)}) collective-permute-start(f32[3,1024]{1,0:T(4,128)S(1)} %add_add_fusion.a_ref), channel_id=1, source_target_pairs={{0,16},{4,20},{8,24},{12,28},{16,0},{20,4},{24,8},{28,12},{1,17},{... | collective-permute-start | bytes 36872 | tf_op jit(solution)/shard_map/ppermute | solution.py:561

commit v20 on v19

--- a/solution.py
+++ b/solution.py
@@ -304,7 +304,7 @@
 def attention_kernel(count, per, stack, g, docs_ref, q_ref, k_ref, v_ref, *refs):
     others = count - 1
     sent = 5 if count == 4 else others
-    out_ref, kt, vt, bias_f, bias_b, bias_a = refs[-6:]
+    out_ref, kt, vt, vf, bias_f, bias_b, bias_a = refs[-7:]
     rows = q_ref.shape[0]
     stretch = rows // 2
     index = lax.axis_index("ctx")
@@ -353,6 +353,17 @@
         key_a = doc_row(docs_ref, jnp.where(lower[r], source, last - source), stretch).astype(F32)
         bias_b[:, tile(2 + r)] = jnp.where(col_b == key_f, 0.0, MASKED)
         bias_a[:, tile(r)] = jnp.where(jnp.where(lower[r], col_f, col_b) == key_a, 0.0, MASKED)
+
+    vf[...] = vt[: count * stretch, :]
+    for r in range(others):
+
+        @pl.when(lower[r])
+        def _():
+            vt[tile(1 + r), :] = jnp.zeros((stretch, 2 * DH), BF16)
+
+        @pl.when(jnp.logical_not(lower[r]))
+        def _():
+            vf[tile(1 + r), :] = jnp.zeros((stretch, 2 * DH), BF16)
 
     factor = math.log2(math.e) / math.sqrt(DH)
     tall = stack * stretch
@@ -394,12 +405,12 @@
         w_x = []
         for r in range(others):
             top = jnp.where(lower[r], top_f, top_b)
-            w = jnp.exp2((t_a[r] - top) * factor)
-            w_f.append(jnp.where(lower[r], w, 0.0).astype(BF16))
-            w_x.append(jnp.where(lower[r], 0.0, w).astype(BF16))
+            w = jnp.exp2((t_a[r] - top) * factor).astype(BF16)
+            w_f.append(w)
+            w_x.append(w)
         w_b = w_b[:1] + w_x + w_b[1:]
         out_f = jnp.dot(
-            jnp.concatenate(w_f, axis=1), vt[:half_keys, :], preferred_element_type=F32
+            jnp.concatenate(w_f, axis=1), vf[...], preferred_element_type=F32
         )
         out_b = jnp.dot(jnp.concatenate(w_b, axis=1), vt[...], preferred_element_type=F32)
         for half, out in enumerate((out_f, out_b)):
@@ -712,6 +723,7 @@
             scratch_shapes=[
                 pltpu.VMEM((2 * count * stretch, DH), BF16),
                 pltpu.VMEM((2 * count * stretch, 2 * DH), BF16),
+                pltpu.VMEM((count * stretch, 2 * DH), BF16),
                 pltpu.VMEM((stretch, stretch), F32),
                 pltpu.VMEM((stretch, (count + 1) * stretch), F32),
                 pltpu.VMEM((stretch, others * stretch), F32),

time: 60.3 us -> 60.4 us (level)
  no operation moved by 1% of the time
where the time goes in v20:
time: 60.4 us; the launch traced here: 60 us
  starting transfers between devices  21.4 us (35%)
  Pallas kernels  19.4 us (32%)
  waiting for transfers between devices  18.3 us (30%)
  between operations  0.87 us (1%)
    ppermute x1, waiting for transfers between devices, body(): farther = lax.ppermute(beyond, 'ctx', outward)  6.07 us
    ppermute x4, starting transfers between devices, exchange(): return lax.ppermute(part, axes, [(d, d ^ shift) for d in range(size)])  6.04 us
    ppermute x1, starting transfers between devices, body(): near = lax.ppermute(kv, 'ctx', inward + outward)  5.96 us
    pallas_call x2, Pallas kernels, body(): pl.pallas_call(functools.partial(attention_kernel, count, per_kv, stack,...  5.72 us
    ppermute x1, waiting for transfers between devices, body(): got[0].append(lax.ppermute(send[0], 'ctx', [(0, 1), (3, 2)]))  4.94 us
    pallas_call x1, Pallas kernels, body(): pl.pallas_call(functools.partial(local_kernel, count, groups), out_shape=...  4.19 us
    pallas_call x2, Pallas kernels, body(): pl.pallas_call(functools.partial(final_kernel, count, g, groups, loss_sca...  3.72 us
    ppermute x3, starting transfers between devices, body(): got[g].append(lax.ppermute(send[g], 'ctx', pairs))  3.51 us
  transfers between devices with their start and end apart: 14, of which 8 were waited for; matrix products, arithmetic and copies ran while one was open for 0% of the time, Pallas kernels for 23%

profile of v20, /device:TPU:0, one launch (start us, length us, event | category | flops | bytes accessed | tf_op | source)
XLA Modules:
  0.0 60.0 jit_solution(1290621168380106853)
XLA Ops:
  0.6 3.1 %opening.1 = (bf16[272,512]{1,0:T(8,128)(2,1)S(1)}, f32[32,256]{1,0:T(8,128)S(1)}, bf16[256,1024]{1,0:T(8,128)(2,1)S(1)}, bf16[256,1024]{1,0:T(8,128)(2,1)S(1)},...) custom-call(s32[1,1024]{1,0:T(1,128)} %docs_ref.7, ...), custom_call_target="tpu_custom_call" | custom-call | flops 268435456 | bytes 4194304 | tf_op jit(solution)/shard_map/opening/pallas_call | solution.py:621
  3.8 0.7 %collective-permute-start.3 = (bf16[272,512]{1,0:T(8,128)(2,1)S(1)}, bf16[272,512]{1,0:T(8,128)(2,1)S(1)}, u32[]{:S(2)}, u32[]{:S(2)}) collective-permute-start(bf16[272,512]{1,0:T(8,128)(2,1)S(1)} %get-tuple-element.45), channel_id=1, source_target_pairs={{4,8},{8,4},{5,9},{9,5},{6,10},{10,6},{7,11},{11,7},{20,24},{24,20... | collective-permute-start | bytes 835592 | tf_op jit(solution)/shard_map/ppermute | solution.py:688
  4.5 6.0 %collective-permute-start.1 = (bf16[272,512]{1,0:T(8,128)(2,1)S(1)}, bf16[272,512]{1,0:T(8,128)(2,1)S(1)}, u32[]{:S(2)}, u32[]{:S(2)}) collective-permute-start(bf16[272,512]{1,0:T(8,128)(2,1)S(1)} %get-tuple-element.45), channel_id=1, source_target_pairs={{0,4},{12,8},{4,0},{8,12},{1,5},{13,9},{5,1},{9,13},{2,6},{14,10},... | collective-permute-start | bytes 835592 | tf_op jit(solution)/shard_map/ppermute | solution.py:687
  10.4 1.9 %collective-permute-start = (bf16[128,1024]{1,0:T(8,128)(2,1)S(1)}, bf16[128,1024]{1,0:T(8,128)(2,1)S(1)}, u32[]{:S(2)}, u32[]{:S(2)}) collective-permute-start(bf16[128,1024]{1,0:T(8,128)(2,1)S(1)} %get-tuple-element.41), channel_id=1, source_target_pairs={{0,4},{12,8},{1,5},{13,9},{2,6},{14,10},{3,7},{15,11},{16,20},{28,... | collective-permute-start | bytes 786440 | tf_op jit(solution)/shard_map/ppermute | solution.py:703
  12.4 4.2 %local.1 = (f32[256,1024]{1,0:T(8,128)S(1)}, f32[256,1024]{1,0:T(8,128)S(1)}, f32[256,1024]{1,0:T(8,128)S(1)}, f32[256,1024]{1,0:T(8,128)S(1)}, f32[256,1024]{1,0:T(8,128)S(1)}, /*index=5*/f32[256,1024]{1,0:T(8,128)S(1)}) custom-call(s32[1,1024]{1,0:T(1,128)} %docs_ref.7, bf16[256,2048]{1,0:T(8,128)(2,1)} %bitcast.32, bf16[256,2048]{1,0:T(8,128)(2,1)} %bitcast.33, ...), custom_call_target="tpu_custom_call" | custom-call | flops 134217728 | bytes 8388608 | tf_op jit(solution)/shard_map/local/pallas_call | solution.py:653
  16.6 0.0 collective-permute-done.3.refs_0_.kv_ref.refs_1_.refs_4_
  16.6 0.6 %collective-permute-start.6 = (bf16[144,1024]{1,0:T(8,128)(2,1)S(1)}, bf16[144,1024]{1,0:T(8,128)(2,1)S(1)}, u32[]{:S(2)}, u32[]{:S(2)}) collective-permute-start(bf16[144,1024]{1,0:T(8,128)(2,1)S(1)} %merge.1), channel_id=1, source_target_pairs={{0,4},{12,8},{4,0},{8,12},{1,5},{13,9},{5,1},{9,13},{2,6},{14,10},... | collective-permute-start | bytes 884744 | tf_op jit(solution)/shard_map/ppermute | solution.py:700
  17.2 0.3 collective-permute-done.1.refs_0_.refs_3_
  17.5 0.7 %collective-permute-start.4 = (bf16[272,512]{1,0:T(8,128)(2,1)S(1)}, bf16[272,512]{1,0:T(8,128)(2,1)S(1)}, u32[]{:S(2)}, u32[]{:S(2)}) collective-permute-start(bf16[272,512]{1,0:T(8,128)(2,1)S(1)} %collective-permute-done.1.refs_0_.refs_3_), channel_id=1, source_target_pairs={{4,8},{8,4},{5,9},{9,5},{6,10},{10,6},{7,11},{11,7},{20,24},{24,20... | collective-permute-start | bytes 835592 | tf_op jit(solution)/shard_map/ppermute | solution.py:690
  18.2 4.9 %collective-permute-done.got_ref.refs_0_ = bf16[128,1024]{1,0:T(8,128)(2,1)S(1)} collective-permute-done((bf16[128,1024]{1,0:T(8,128)(2,1)S(1)}, bf16[128,1024]{1,0:T(8,128)(2,1)S(1)}, u32[]{:S(2)}, u32[]{:S(2)}) %collective-permute-start) | collective-permute-done | bytes 262176 | tf_op jit(solution)/shard_map/ppermute | solution.py:703
  23.1 0.7 %collective-permute-start.2 = (bf16[128,1024]{1,0:T(8,128)(2,1)S(1)}, bf16[128,1024]{1,0:T(8,128)(2,1)S(1)}, u32[]{:S(2)}, u32[]{:S(2)}) collective-permute-start(bf16[128,1024]{1,0:T(8,128)(2,1)S(1)} %chain.4), channel_id=1, source_target_pairs={{4,8},{8,4},{5,9},{9,5},{6,10},{10,6},{7,11},{11,7},{20,24},{24,20... | collective-permute-start | bytes 786440 | tf_op jit(solution)/shard_map/ppermute | solution.py:706
  23.8 0.0 collective-permute-done.4.refs_1_.refs_2_.refs_5_
  23.8 1.3 %collective-permute-start.8 = (bf16[272,512]{1,0:T(8,128)(2,1)S(1)}, bf16[272,512]{1,0:T(8,128)(2,1)S(1)}, u32[]{:S(2)}, u32[]{:S(2)}) collective-permute-start(bf16[272,512]{1,0:T(8,128)(2,1)S(1)} %collective-permute-done.4.refs_1_.refs_2_.refs_5_), channel_id=1, source_target_pairs={{4,0},{8,12},{5,1},{9,13},{6,2},{10,14},{7,3},{11,15},{20,16},{24,... | collective-permute-start | bytes 835592 | tf_op jit(solution)/shard_map/ppermute | solution.py:707
  25.1 2.9 %collective-permute-done.6.got_ref.refs_3_.refs_6_.refs_0_ = bf16[144,1024]{1,0:T(8,128)(2,1)S(1)} collective-permute-done((bf16[144,1024]{1,0:T(8,128)(2,1)S(1)}, bf16[144,1024]{1,0:T(8,128)(2,1)S(1)}, u32[]{:S(2)}, u32[]{:S(2)}) %collective-permute-start.6) | collective-permute-done | bytes 294944 | tf_op jit(solution)/shard_map/ppermute | solution.py:700
  28.0 0.0 copy-start
  28.0 0.0 copy-start.2
  28.0 0.8 %collective-permute-start.7 = (bf16[128,1024]{1,0:T(8,128)(2,1)S(1)}, bf16[128,1024]{1,0:T(8,128)(2,1)S(1)}, u32[]{:S(2)}, u32[]{:S(2)}) collective-permute-start(bf16[128,1024]{1,0:T(8,128)(2,1)S(1)} %chain.6), channel_id=1, source_target_pairs={{4,8},{8,4},{5,9},{9,5},{6,10},{10,6},{7,11},{11,7},{20,24},{24,20... | collective-permute-start | bytes 786440 | tf_op jit(solution)/shard_map/ppermute | solution.py:752
  28.8 0.0 collective-permute-done.2.got_ref.refs_1_
  28.8 0.0 copy-start.4
  28.9 1.3 %collective-permute-start.5 = (bf16[128,1024]{1,0:T(8,128)(2,1)S(1)}, bf16[128,1024]{1,0:T(8,128)(2,1)S(1)}, u32[]{:S(2)}, u32[]{:S(2)}) collective-permute-start(bf16[128,1024]{1,0:T(8,128)(2,1)S(1)} %chain.5), channel_id=1, source_target_pairs={{8,12},{4,0},{9,13},{5,1},{10,14},{6,2},{11,15},{7,3},{24,28},{20,... | collective-permute-start | bytes 786440 | tf_op jit(solution)/shard_map/ppermute | solution.py:752
  30.2 6.1 %collective-permute-done.8.refs_4_.refs_7_ = bf16[272,512]{1,0:T(8,128)(2,1)S(1)} collective-permute-done((bf16[272,512]{1,0:T(8,128)(2,1)S(1)}, bf16[272,512]{1,0:T(8,128)(2,1)S(1)}, u32[]{:S(2)}, u32[]{:S(2)}) %collective-permute-start.8) | collective-permute-done | bytes 278560 | tf_op jit(solution)/shard_map/ppermute | solution.py:707
  36.2 0.0 copy-done
  36.2 0.0 copy-done.1
  36.2 0.0 copy-done.2
  36.2 0.0 copy-done.4
  36.3 2.9 %attention.2.refs_0_.teacher_ref = bf16[256,1024]{1,0:T(8,128)(2,1)S(1)} custom-call(s32[1,1024]{1,0:T(1,128)S(1)} %copy-done.4, bf16[256,2048]{1,0:T(8,128)(2,1)S(1)} %bitcast.18, bf16[256,256]{1,0:T(8,128)(2,1)S(1)} %bitcast.21, bf16[256,256]{1,0:T(8,128)(2,1)S(1)} %bitcast.24, bf16[272,512]{1,0:T(8,128)(2,1)S(1)} %collective-permute-done.1.refs_0_.refs_3_, ...), custom_call_target="tpu_custom_call" | custom-call | flops 603979776 | bytes 2097152 | tf_op jit(solution)/shard_map/attention/pallas_call | solution.py:718
  39.1 0.0 collective-permute-done.7.got_ref.refs_1_
  39.2 0.0 copy-start.3
  39.2 0.0 copy-start.5
  39.2 1.4 %collective-permute-start.9 = (bf16[128,1024]{1,0:T(8,128)(2,1)S(1)}, bf16[128,1024]{1,0:T(8,128)(2,1)S(1)}, u32[]{:S(2)}, u32[]{:S(2)}) collective-permute-start(bf16[128,1024]{1,0:T(8,128)(2,1)S(1)} %chain.7), channel_id=1, source_target_pairs={{8,12},{4,0},{9,13},{5,1},{10,14},{6,2},{11,15},{7,3},{24,28},{20,... | collective-permute-start | bytes 786440 | tf_op jit(solution)/shard_map/ppermute | solution.py:752
  40.6 2.9 %attention.3.refs_1_.teacher_ref = bf16[256,1024]{1,0:T(8,128)(2,1)S(1)} custom-call(s32[1,1024]{1,0:T(1,128)S(1)} %copy-done.4, bf16[256,2048]{1,0:T(8,128)(2,1)S(1)} %bitcast.19, bf16[256,256]{1,0:T(8,128)(2,1)S(1)} %bitcast.22, bf16[256,256]{1,0:T(8,128)(2,1)S(1)} %bitcast.25, bf16[272,512]{1,0:T(8,128)(2,1)S(1)} %collective-permute-done.1.refs_0_.refs_3_, ...), custom_call_target="tpu_custom_call" | custom-call | flops 603979776 | bytes 2097152 | tf_op jit(solution)/shard_map/attention/pallas_call | solution.py:718
  43.5 0.0 collective-permute-done.5.refs_2_
  43.5 0.0 copy-done.3
  43.5 0.0 copy-done.5
  43.5 1.9 %final.2 = (bf16[256,1024]{1,0:T(8,128)(2,1)S(1)}, f32[3,1024]{1,0:T(4,128)S(1)}) custom-call(f32[256,1024]{1,0:T(8,128)S(1)} %get-tuple-element.64.pre_ref, f32[256,1024]{1,0:T(8,128)S(1)} %get-tuple-element.65.reach_ref, f32[256,1024]{1,0:T(8,128)S(1)} %get-tuple-element.66.sx_ref, bf16[256,256]{1,0:T(8,128)(2,1)S(1)} %bitcast.27, ...), custom_call_target="tpu_custom_call" | custom-call | flops 67108864 | bytes 5242880 | tf_op jit(solution)/shard_map/final/pallas_call | solution.py:758
  45.4 2.2 %collective-permute-done.9.refs_2_ = bf16[128,1024]{1,0:T(8,128)(2,1)S(1)} collective-permute-done((bf16[128,1024]{1,0:T(8,128)(2,1)S(1)}, bf16[128,1024]{1,0:T(8,128)(2,1)S(1)}, u32[]{:S(2)}, u32[]{:S(2)}) %collective-permute-start.9) | collective-permute-done | bytes 262176 | tf_op jit(solution)/shard_map/ppermute | solution.py:752
  47.6 1.9 %final.3 = (bf16[256,1024]{1,0:T(8,128)(2,1)S(1)}, f32[3,1024]{1,0:T(4,128)S(1)}) custom-call(f32[256,1024]{1,0:T(8,128)S(1)} %get-tuple-element.69.pre_ref, f32[256,1024]{1,0:T(8,128)S(1)} %get-tuple-element.70.reach_ref, f32[256,1024]{1,0:T(8,128)S(1)} %get-tuple-element.71.sx_ref, bf16[256,256]{1,0:T(8,128)(2,1)S(1)} %bitcast.28, ...), custom_call_target="tpu_custom_call" | custom-call | flops 67108864 | bytes 5242880 | tf_op jit(solution)/shard_map/final/pallas_call | solution.py:758
  49.4 0.3 collective-permute-start.12
  49.7 1.7 %collective-permute-start.11 = (f32[3,1024]{1,0:T(4,128)S(1)}, f32[3,1024]{1,0:T(4,128)S(1)}, u32[]{:S(2)}, u32[]{:S(2)}) collective-permute-start(f32[3,1024]{1,0:T(4,128)S(1)} %get-tuple-element.75), channel_id=1, source_target_pairs={{0,8},{4,12},{8,0},{12,4},{16,24},{20,28},{24,16},{28,20},{1,9},{5... | collective-permute-start | bytes 36872 | tf_op jit(solution)/shard_map/ppermute | solution.py:572
  51.5 2.4 %collective-permute-start.10 = (f32[3,1024]{1,0:T(4,128)S(1)}, f32[3,1024]{1,0:T(4,128)S(1)}, u32[]{:S(2)}, u32[]{:S(2)}) collective-permute-start(f32[3,1024]{1,0:T(4,128)S(1)} %get-tuple-element.75), channel_id=1, source_target_pairs={{0,4},{4,0},{8,12},{12,8},{16,20},{20,16},{24,28},{28,24},{1,5},{5... | collective-permute-start | bytes 36872 | tf_op jit(solution)/shard_map/ppermute | solution.py:572
  53.9 1.1 %collective-permute-done.12 = f32[3,1024]{1,0:T(4,128)S(1)} collective-permute-done((f32[3,1024]{1,0:T(4,128)S(1)}, f32[3,1024]{1,0:T(4,128)S(1)}, u32[]{:S(2)}, u32[]{:S(2)}) %collective-permute-start.12) | collective-permute-done | bytes 12320 | tf_op jit(solution)/shard_map/ppermute | solution.py:572
  55.0 0.0 collective-permute-done.11
  55.0 0.6 collective-permute-done.10
  55.6 1.6 %collective-permute-start.13 = (f32[3,1024]{1,0:T(4,128)S(1)}, f32[3,1024]{1,0:T(4,128)S(1)}, u32[]{:S(2)}, u32[]{:S(2)}) collective-permute-start(f32[3,1024]{1,0:T(4,128)S(1)} %add_add_fusion.a_ref), channel_id=1, source_target_pairs={{0,16},{4,20},{8,24},{12,28},{16,0},{20,4},{24,8},{28,12},{1,17},{... | collective-permute-start | bytes 36872 | tf_op jit(solution)/shard_map/ppermute | solution.py:572
  57.2 1.0 %writing.2 = bf16[256,2048]{1,0:T(8,128)(2,1)} custom-call(bf16[256,1024]{1,0:T(8,128)(2,1)S(1)} %attention.2.refs_0_.teacher_ref, bf16[256,1024]{1,0:T(8,128)(2,1)S(1)} %attention.3.refs_1_.teacher_ref), custom_call_target="tpu_custom_call" | custom-call | bytes 2097152 | tf_op jit(solution)/shard_map/writing/pallas_call | solution.py:608
  58.2 1.0 %writing.3 = bf16[256,2048]{1,0:T(8,128)(2,1)} custom-call(bf16[256,1024]{1,0:T(8,128)(2,1)S(1)} %get-tuple-element.68.refs_0_, bf16[256,1024]{1,0:T(8,128)(2,1)S(1)} %get-tuple-element.74.refs_1_), custom_call_target="tpu_custom_call" | custom-call | bytes 2097152 | tf_op jit(solution)/shard_map/writing/pallas_call | solution.py:608
  59.2 0.2 collective-permute-done.13.b_ref
  59.4 0.6 %closing.1 = (f32[1,2048]{1,0:T(1,128)}, f32[1,32]{1,0:T(1,128)}) custom-call(f32[3,1024]{1,0:T(4,128)S(1)} %add_add_fusion.a_ref, f32[3,1024]{1,0:T(4,128)S(1)} %collective-permute-done.13.b_ref), custom_call_target="tpu_custom_call" | custom-call | tf_op jit(solution)/shard_map/closing/pallas_call | solution.py:794
  (7 shorter events, 0.1 us)
Async XLA Ops:
  3.8 12.8 %collective-permute-start.3 = (bf16[272,512]{1,0:T(8,128)(2,1)S(1)}, bf16[272,512]{1,0:T(8,128)(2,1)S(1)}, u32[]{:S(2)}, u32[]{:S(2)}) collective-permute-start(bf16[272,512]{1,0:T(8,128)(2,1)S(1)} %get-tuple-element.45), channel_id=1, source_target_pairs={{4,8},{8,4},{5,9},{9,5},{6,10},{10,6},{7,11},{11,7},{20,24},{24,20... | collective-permute-start | bytes 835592 | tf_op jit(solution)/shard_map/ppermute | solution.py:688
  4.5 13.1 %collective-permute-start.1 = (bf16[272,512]{1,0:T(8,128)(2,1)S(1)}, bf16[272,512]{1,0:T(8,128)(2,1)S(1)}, u32[]{:S(2)}, u32[]{:S(2)}) collective-permute-start(bf16[272,512]{1,0:T(8,128)(2,1)S(1)} %get-tuple-element.45), channel_id=1, source_target_pairs={{0,4},{12,8},{4,0},{8,12},{1,5},{13,9},{5,1},{9,13},{2,6},{14,10},... | collective-permute-start | bytes 835592 | tf_op jit(solution)/shard_map/ppermute | solution.py:687
  10.4 12.7 %collective-permute-start = (bf16[128,1024]{1,0:T(8,128)(2,1)S(1)}, bf16[128,1024]{1,0:T(8,128)(2,1)S(1)}, u32[]{:S(2)}, u32[]{:S(2)}) collective-permute-start(bf16[128,1024]{1,0:T(8,128)(2,1)S(1)} %get-tuple-element.41), channel_id=1, source_target_pairs={{0,4},{12,8},{1,5},{13,9},{2,6},{14,10},{3,7},{15,11},{16,20},{28,... | collective-permute-start | bytes 786440 | tf_op jit(solution)/shard_map/ppermute | solution.py:703
  16.6 11.4 %collective-permute-start.6 = (bf16[144,1024]{1,0:T(8,128)(2,1)S(1)}, bf16[144,1024]{1,0:T(8,128)(2,1)S(1)}, u32[]{:S(2)}, u32[]{:S(2)}) collective-permute-start(bf16[144,1024]{1,0:T(8,128)(2,1)S(1)} %merge.1), channel_id=1, source_target_pairs={{0,4},{12,8},{4,0},{8,12},{1,5},{13,9},{5,1},{9,13},{2,6},{14,10},... | collective-permute-start | bytes 884744 | tf_op jit(solution)/shard_map/ppermute | solution.py:700
  17.5 6.3 %collective-permute-start.4 = (bf16[272,512]{1,0:T(8,128)(2,1)S(1)}, bf16[272,512]{1,0:T(8,128)(2,1)S(1)}, u32[]{:S(2)}, u32[]{:S(2)}) collective-permute-start(bf16[272,512]{1,0:T(8,128)(2,1)S(1)} %collective-permute-done.1.refs_0_.refs_3_), channel_id=1, source_target_pairs={{4,8},{8,4},{5,9},{9,5},{6,10},{10,6},{7,11},{11,7},{20,24},{24,20... | collective-permute-start | bytes 835592 | tf_op jit(solution)/shard_map/ppermute | solution.py:690
  23.1 5.7 %collective-permute-start.2 = (bf16[128,1024]{1,0:T(8,128)(2,1)S(1)}, bf16[128,1024]{1,0:T(8,128)(2,1)S(1)}, u32[]{:S(2)}, u32[]{:S(2)}) collective-permute-start(bf16[128,1024]{1,0:T(8,128)(2,1)S(1)} %chain.4), channel_id=1, source_target_pairs={{4,8},{8,4},{5,9},{9,5},{6,10},{10,6},{7,11},{11,7},{20,24},{24,20... | collective-permute-start | bytes 786440 | tf_op jit(solution)/shard_map/ppermute | solution.py:706
  23.8 12.4 %collective-permute-start.8 = (bf16[272,512]{1,0:T(8,128)(2,1)S(1)}, bf16[272,512]{1,0:T(8,128)(2,1)S(1)}, u32[]{:S(2)}, u32[]{:S(2)}) collective-permute-start(bf16[272,512]{1,0:T(8,128)(2,1)S(1)} %collective-permute-done.4.refs_1_.refs_2_.refs_5_), channel_id=1, source_target_pairs={{4,0},{8,12},{5,1},{9,13},{6,2},{10,14},{7,3},{11,15},{20,16},{24,... | collective-permute-start | bytes 835592 | tf_op jit(solution)/shard_map/ppermute | solution.py:707
  28.0 8.2 %copy-start = (bf16[1,256,2048]{2,1,0:T(8,128)(2,1)S(1)}, bf16[1,256,2048]{2,1,0:T(8,128)(2,1)}, u32[]{:S(2)}) copy-start(bf16[1,256,2048]{2,1,0:T(8,128)(2,1)} %param.13) | copy-start | bytes 3145732
  28.0 8.2 %copy-start.1 = (bf16[1,256,256]{2,1,0:T(8,128)(2,1)S(1)}, bf16[1,256,256]{2,1,0:T(8,128)(2,1)}, u32[]{:S(2)}) copy-start(bf16[1,256,256]{2,1,0:T(8,128)(2,1)} %param.14) | copy-start | bytes 393220
  28.0 8.2 %copy-start.2 = (bf16[1,256,256]{2,1,0:T(8,128)(2,1)S(1)}, bf16[1,256,256]{2,1,0:T(8,128)(2,1)}, u32[]{:S(2)}) copy-start(bf16[1,256,256]{2,1,0:T(8,128)(2,1)} %param.15) | copy-start | bytes 393220
  28.0 11.1 %collective-permute-start.7 = (bf16[128,1024]{1,0:T(8,128)(2,1)S(1)}, bf16[128,1024]{1,0:T(8,128)(2,1)S(1)}, u32[]{:S(2)}, u32[]{:S(2)}) collective-permute-start(bf16[128,1024]{1,0:T(8,128)(2,1)S(1)} %chain.6), channel_id=1, source_target_pairs={{4,8},{8,4},{5,9},{9,5},{6,10},{10,6},{7,11},{11,7},{20,24},{24,20... | collective-permute-start | bytes 786440 | tf_op jit(solution)/shard_map/ppermute | solution.py:752
  28.8 7.4 %copy-start.4 = (s32[1,1024]{1,0:T(1,128)S(1)}, s32[1,1024]{1,0:T(1,128)}, u32[]{:S(2)}) copy-start(s32[1,1024]{1,0:T(1,128)} %docs_ref.7) | copy-start | bytes 12292
  28.9 14.6 %collective-permute-start.5 = (bf16[128,1024]{1,0:T(8,128)(2,1)S(1)}, bf16[128,1024]{1,0:T(8,128)(2,1)S(1)}, u32[]{:S(2)}, u32[]{:S(2)}) collective-permute-start(bf16[128,1024]{1,0:T(8,128)(2,1)S(1)} %chain.5), channel_id=1, source_target_pairs={{8,12},{4,0},{9,13},{5,1},{10,14},{6,2},{11,15},{7,3},{24,28},{20,... | collective-permute-start | bytes 786440 | tf_op jit(solution)/shard_map/ppermute | solution.py:752
  39.2 4.3 %copy-start.3 = (bf16[1,256,256]{2,1,0:T(8,128)(2,1)S(1)}, bf16[1,256,256]{2,1,0:T(8,128)(2,1)}, u32[]{:S(2)}) copy-start(bf16[1,256,256]{2,1,0:T(8,128)(2,1)} %param.20) | copy-start | bytes 393220
  39.2 4.3 %copy-start.5 = (f32[2048]{0:T(1024)S(1)}, f32[2048]{0:T(1024)}, u32[]{:S(2)}) copy-start(f32[2048]{0:T(1024)} %param.25) | copy-start | bytes 24580
  39.2 8.4 %collective-permute-start.9 = (bf16[128,1024]{1,0:T(8,128)(2,1)S(1)}, bf16[128,1024]{1,0:T(8,128)(2,1)S(1)}, u32[]{:S(2)}, u32[]{:S(2)}) collective-permute-start(bf16[128,1024]{1,0:T(8,128)(2,1)S(1)} %chain.7), channel_id=1, source_target_pairs={{8,12},{4,0},{9,13},{5,1},{10,14},{6,2},{11,15},{7,3},{24,28},{20,... | collective-permute-start | bytes 786440 | tf_op jit(solution)/shard_map/ppermute | solution.py:752
  49.4 5.6 %collective-permute-start.12 = (f32[3,1024]{1,0:T(4,128)S(1)}, f32[3,1024]{1,0:T(4,128)S(1)}, u32[]{:S(2)}, u32[]{:S(2)}) collective-permute-start(f32[3,1024]{1,0:T(4,128)S(1)} %get-tuple-element.75), channel_id=1, source_target_pairs={{0,12},{4,8},{8,4},{12,0},{16,28},{20,24},{24,20},{28,16},{1,13},{... | collective-permute-start | bytes 36872 | tf_op jit(solution)/shard_map/ppermute | solution.py:572
  49.7 5.3 %collective-permute-start.11 = (f32[3,1024]{1,0:T(4,128)S(1)}, f32[3,1024]{1,0:T(4,128)S(1)}, u32[]{:S(2)}, u32[]{:S(2)}) collective-permute-start(f32[3,1024]{1,0:T(4,128)S(1)} %get-tuple-element.75), channel_id=1, source_target_pairs={{0,8},{4,12},{8,0},{12,4},{16,24},{20,28},{24,16},{28,20},{1,9},{5... | collective-permute-start | bytes 36872 | tf_op jit(solution)/shard_map/ppermute | solution.py:572
  51.5 4.1 %collective-permute-start.10 = (f32[3,1024]{1,0:T(4,128)S(1)}, f32[3,1024]{1,0:T(4,128)S(1)}, u32[]{:S(2)}, u32[]{:S(2)}) collective-permute-start(f32[3,1024]{1,0:T(4,128)S(1)} %get-tuple-element.75), channel_id=1, source_target_pairs={{0,4},{4,0},{8,12},{12,8},{16,20},{20,16},{24,28},{28,24},{1,5},{5... | collective-permute-start | bytes 36872 | tf_op jit(solution)/shard_map/ppermute | solution.py:572
  55.6 3.8 %collective-permute-start.13 = (f32[3,1024]{1,0:T(4,128)S(1)}, f32[3,1024]{1,0:T(4,128)S(1)}, u32[]{:S(2)}, u32[]{:S(2)}) collective-permute-start(f32[3,1024]{1,0:T(4,128)S(1)} %add_add_fusion.a_ref), channel_id=1, source_target_pairs={{0,16},{4,20},{8,24},{12,28},{16,0},{20,4},{24,8},{28,12},{1,17},{... | collective-permute-start | bytes 36872 | tf_op jit(solution)/shard_map/ppermute | solution.py:572
